TPU v7x, 32 devices: a whole 2x2x4 slice. The times are simulated.
32 devices in a mesh: head: 4 (over y, core), seq: 8 (over z, x).
Axes of the slice: x: 2, y: 2, z: 4, core: 2. Of those that a mesh axis runs over, the one named last changes fastest.
Arguments:
- queries: bfloat16 [4, 1024, 256], P('head', 'seq'), may hold values from -6 to 6
- key_rows: bfloat16 [4, 1024, 256], P('head', 'seq'), may hold values from -6 to 6
- value_rows: bfloat16 [4, 1024, 256], P('head', 'seq'), may hold values from -6 to 6
- out_grad: bfloat16 [4, 1024, 256], P('head', 'seq'), may hold values from -6 to 6
- step_sizes: float32 [4, 1024], P('head', 'seq'), may hold values from 0.0001 to 0.0004
- norm_gain: float32 [4, 256], P('head'), may hold values from 0.1 to 1.9
- gate_init: bfloat16 [4, 256, 768], P('head', 'seq'), may hold values from -0.90625 to 0.90625
- up_init: bfloat16 [4, 256, 768], P('head', 'seq'), may hold values from -0.90625 to 0.90625
- down_init: bfloat16 [4, 256, 768], P('head', 'seq'), may hold values from -0.90625 to 0.90625
- gate_saved: bfloat16 [4, 256, 768], P('head', 'seq'), may hold values from -0.90625 to 0.90625
- up_saved: bfloat16 [4, 256, 768], P('head', 'seq'), may hold values from -0.90625 to 0.90625
- down_saved: bfloat16 [4, 256, 768], P('head', 'seq'), may hold values from -0.90625 to 0.90625
Outputs:
- grad_queries: bfloat16 [4, 1024, 256], P('head', 'seq')
- grad_keys: bfloat16 [4, 1024, 256], P('head', 'seq')
- grad_values: bfloat16 [4, 1024, 256], P('head', 'seq')
- grad_gate: float32 [4, 256, 768], P('head', 'seq')
- grad_up: float32 [4, 256, 768], P('head', 'seq')
- grad_down: float32 [4, 256, 768], P('head', 'seq')
All inputs are finite; a program needn't handle non-finite values.
Results may differ from a plain program's by a relative error of at most 0.0085.
The roundings to bfloat16 on the way count: a program that leaves them out, or rounds other values in their place, can miss the bound.
Values may be sent and summed in bfloat16 or wider, within the bound.
No kernel may reach another device: no remote copies, remote signals or barrier semaphores. Data moves between devices by JAX's collectives and lax.ppermute only.
A program may use at most 64 MiB of HBM per device.

v0:
```python
import functools

import jax
import jax.numpy as jnp
from jax import lax
from jax.experimental import pallas as pl
from jax.experimental.pallas import tpu as pltpu
from jax.sharding import PartitionSpec as P

EPS_COL = 1e-06
EPS_ROOT = 1e-05
BF = jnp.bfloat16
F32 = jnp.float32
VMEM = pl.BlockSpec(memory_space=pltpu.VMEM)
SMEM = pl.BlockSpec(memory_space=pltpu.SMEM)


def silu_parts(pre_act):
    sigmoid_val = jax.nn.sigmoid(pre_act)
    silu_val = pre_act * sigmoid_val
    silu_slope = sigmoid_val * (1.0 + pre_act * (1.0 - sigmoid_val))
    silu_bend = sigmoid_val * (1.0 - sigmoid_val) * (2.0 + pre_act * (1.0 - 2.0 * sigmoid_val))
    return (silu_val, silu_slope, silu_bend)


def mm(left_op, right_op):
    return jnp.dot(left_op, right_op, preferred_element_type=F32)


def mm_nt(left_op, right_op):
    return lax.dot_general(left_op, right_op, (((1,), (1,)), ((), ())), preferred_element_type=F32)


def mm_tn(left_op, right_op):
    return lax.dot_general(left_op, right_op, (((0,), (0,)), ((), ())), preferred_element_type=F32)


def column_norm(weight):
    return jnp.sqrt(jnp.sum(weight * weight, axis=0, keepdims=True) + EPS_COL)


def flat(x):
    return x.reshape(-1, x.shape[-1])


def call(kernel, outs, args, flops, mib, smem=0):
    moved = sum(x.size * x.dtype.itemsize for x in (*args, *outs))
    return pl.pallas_call(
        kernel,
        out_shape=outs,
        in_specs=[SMEM] * smem + [VMEM] * (len(args) - smem),
        out_specs=[VMEM] * len(outs),
        compiler_params=pltpu.CompilerParams(vmem_limit_bytes=mib << 20),
        cost_estimate=pl.CostEstimate(flops=flops, bytes_accessed=moved, transcendentals=0),
    )(*args)


def copying_call(kernel, outs, args, buffers):
    return pl.pallas_call(
        kernel,
        out_shape=outs,
        in_specs=[pl.BlockSpec(memory_space=pl.ANY)] * len(args),
        out_specs=[VMEM] * len(outs),
        scratch_shapes=[*buffers, pltpu.SemaphoreType.DMA((len(args),))],
        compiler_params=pltpu.CompilerParams(vmem_limit_bytes=16 << 20),
    )(*args)


def arr(shape, dtype):
    return jax.ShapeDtypeStruct(shape, dtype)


def fetch(sources, buffers, sems):
    copies = [pltpu.make_async_copy(s, b, sems.at[i]) for i, (s, b) in enumerate(zip(sources, buffers))]
    for copy in copies:
        copy.start()
    for copy in copies:
        copy.wait()


def pack_kernel(group, slab, gs, us, ds, gi, ui, di, w_out, buf, sems):
    fetch((gs, us, ds, gi, ui, di), [buf.at[pl.ds(i, 1)] for i in range(6)], sems)
    for j in range(group):
        cols = pl.ds(j * slab, slab)
        block = jnp.concatenate([buf[i, :, cols] for i in range(6)], axis=1)
        for p in range(j, w_out.shape[0], group):
            w_out[p] = block


def tokens_in_kernel(k, v, og, rates, gains, kv_out, gg_out, kb, vb, ob, rb, gb, sems):
    fetch((k, v, og, rates, gains), (kb, vb, ob, rb, gb), sems)
    tokens, feat = gg_out.shape
    rate = jnp.broadcast_to(rb[...], (feat, tokens)).T
    kv_out[:, 0:feat] = kb[0]
    kv_out[:, feat : 2 * feat] = (rate * vb[0].astype(F32)).astype(BF)
    gg_out[...] = gb[...] * ob[0].astype(F32)


def normalized(w, slab):
    parts = [w[:, pl.ds(i * slab, slab)].astype(F32) for i in range(6)]
    saved, init = parts[:3], parts[3:]
    norm_init = [column_norm(x) for x in init]
    norm_saved = [column_norm(x) for x in saved]
    ratio = [norm_init[i] / norm_saved[i] for i in range(3)]
    normed = [(saved[i] * ratio[i]).astype(BF) for i in range(3)]
    return saved, init, norm_init, norm_saved, ratio, normed


def forward_kernel(slab, w, q, out):
    normed = normalized(w, slab)[-1]
    rows = flat(q[...])
    hidden = (silu_parts(mm(rows, normed[0]))[0] * mm(rows, normed[1])).astype(BF)
    out[...] = mm_nt(hidden, normed[2]).astype(BF).reshape(out.shape)


def delta_kernel(width, sums, apply_out, gg, out):
    tokens, feat = apply_out.shape
    square = jnp.broadcast_to(sums[0:1, :], (feat, tokens)).T
    gain = jnp.broadcast_to(sums[1:2, :], (feat, tokens)).T
    root = jnp.sqrt(square / width + EPS_ROOT)
    delta = (gg[...] / root - apply_out[...] * (gain / width) / (root * root * root)).astype(BF)
    for p in range(out.shape[0]):
        out[p] = delta


def backward_kernel(slab, group, place, w, q, kv, od, *rest):
    outs, (inner_out, tok, ag, au, ad) = rest[:group], rest[group:]
    mine, rank = place[0], place[1]
    saved, init, norm_init, norm_saved, ratio, normed = normalized(w, slab)
    feat = q.shape[-1]

    def query_side(rows, delta):
        q_gate = mm(rows, normed[0])
        q_up = mm(rows, normed[1])
        act, slope, _ = silu_parts(q_gate)
        hidden = (act * q_up).astype(BF)
        delta_hidden = mm(delta, normed[2])
        delta_gate = (delta_hidden * q_up * slope).astype(BF)
        delta_up = (delta_hidden * act).astype(BF)
        grads = (mm_tn(rows, delta_gate), mm_tn(rows, delta_up), mm_tn(delta, hidden))
        return delta_gate, delta_up, grads

    def take(ref, e):
        return flat(ref[pl.ds((mine ^ e) * group, group)])

    delta_gate, delta_up, grads = query_side(take(q, 0), take(od, 0))
    grad_q = mm_nt(delta_gate, normed[0]) + mm_nt(delta_up, normed[1])
    tok[:, :, 0:feat] = grad_q.astype(BF).reshape(group, -1, feat)
    ag[...], au[...], ad[...] = grads

    def other(e, carry):
        more = query_side(take(q, e), take(od, e))[2]
        ag[...] += more[0]
        au[...] += more[1]
        ad[...] += more[2]
        return carry

    lax.fori_loop(1, od.shape[0] // group, other, 0)

    apply_grad = (ag[...], au[...], ad[...])
    cots, direct = [], []
    share = jnp.where(mine == 0, 1.0, 0.0)
    for i in range(3):
        col_dot = jnp.sum(saved[i] * apply_grad[i], axis=0, keepdims=True)
        cot = apply_grad[i] * ratio[i] - saved[i] * (
            col_dot * norm_init[i] / (norm_saved[i] * norm_saved[i] * norm_saved[i])
        )
        cots.append(cot.astype(BF))
        direct.append((cot + init[i] * (col_dot / (norm_init[i] * norm_saved[i]))) * share)

    init_bf = [w[:, pl.ds((3 + i) * slab, slab)] for i in range(3)]
    keys = flat(kv[:, :, 0:feat])
    values = flat(kv[:, :, feat : 2 * feat])
    k_gate = mm(keys, init_bf[0])
    k_up = mm(keys, init_bf[1])
    k_proj = mm(values, init_bf[2])
    k_act, k_slope, k_bend = silu_parts(k_gate)
    k_hidden = (k_act * k_up).astype(BF)
    rise_gate = (k_proj * k_up * k_slope).astype(BF)
    rise_up = (k_proj * k_act).astype(BF)
    back_gate = mm(keys, cots[0])
    back_up = mm(keys, cots[1])
    back_hidden = mm(values, cots[2])
    back_proj = (back_gate * k_up * k_slope + back_up * k_act).astype(BF)
    back_kup = (back_gate * k_proj * k_slope + back_hidden * k_act).astype(BF)
    back_kgate = (
        back_gate * k_proj * k_up * k_bend + (back_up * k_proj + back_hidden * k_up) * k_slope
    ).astype(BF)
    grad_k = (
        mm_nt(rise_gate, cots[0])
        + mm_nt(rise_up, cots[1])
        + mm_nt(back_kgate, init_bf[0])
        + mm_nt(back_kup, init_bf[1])
    )
    grad_v = mm_nt(k_hidden, cots[2]) + mm_nt(back_proj, init_bf[2])
    tok[:, :, feat : 2 * feat] = grad_k.astype(BF).reshape(group, -1, feat)
    tok[:, :, 2 * feat : 3 * feat] = grad_v.astype(BF).reshape(group, -1, feat)
    inner = (mm_tn(keys, back_kgate), mm_tn(keys, back_kup), mm_tn(values, back_proj))
    inner_out[...] = jnp.concatenate([inner[i] + direct[i] for i in range(3)], axis=1).astype(BF)
    for d in range(group):
        outs[d][...] = tok[rank ^ d]


def tokens_kernel(rates, *refs):
    got, (gq, gk, gv) = refs[:-3], refs[-3:]
    tokens, feat = gq.shape[1:]
    total = got[0][...].astype(F32)
    for block in got[1:]:
        total += block[...].astype(F32)
    gq[0] = total[:, 0:feat].astype(BF)
    gk[0] = total[:, feat : 2 * feat].astype(BF)
    rate = jnp.broadcast_to(rates[...], (feat, tokens)).T
    gv[0] = (rate * total[:, 2 * feat : 3 * feat]).astype(BF)


def weights_kernel(group, slab, got, *outs):
    cols = []
    for j in range(group):
        total = got[j].astype(F32)
        for p in range(j + group, got.shape[0], group):
            total += got[p].astype(F32)
        cols.append(total)
    for i in range(3):
        outs[i][0] = jnp.concatenate([c[:, i * slab : (i + 1) * slab] for c in cols], axis=1)


def make_local(seq_n, head_n, group):
    tok_groups = seq_n // group
    groups = [[t * group + j for j in range(group)] for t in range(tok_groups)]

    def swap(blocks, axis_groups=None):
        return lax.all_to_all(blocks, "seq", 0, 0, axis_index_groups=axis_groups, tiled=True)

    def local(q, k, v, og, rates, gains, gi, ui, di, gs, us, ds):
        _, rows, hidden = gi.shape
        _, own, feat = q.shape
        slab = hidden // group
        near = group * own
        me = lax.axis_index("seq")
        place = jnp.stack((lax.div(me, group), lax.rem(me, group))).astype(jnp.int32)

        queries = lax.all_gather(q[0], "seq", axis_index_groups=groups)
        (packed,) = copying_call(
            functools.partial(pack_kernel, group, slab),
            (arr((seq_n, rows, 6 * slab), BF),),
            (gs, us, ds, gi, ui, di),
            [pltpu.VMEM((6, rows, hidden), BF)],
        )
        kv, gg = copying_call(
            tokens_in_kernel,
            (arr((own, 2 * feat), BF), arr((own, feat), F32)),
            (k, v, og, rates, gains),
            [pltpu.VMEM(x.shape, x.dtype) for x in (k, v, og, rates, gains)],
        )
        wall = swap(packed).reshape(seq_n * rows, 6 * slab)
        kv = lax.all_gather(kv, "seq", axis_index_groups=groups)
        q_all = lax.all_gather(q[0], "seq")

        (part,) = call(
            functools.partial(forward_kernel, slab),
            (arr((group, own, feat), BF),),
            (wall, queries),
            6 * near * feat * slab,
            24,
        )
        apply_out = jnp.sum(swap(part, groups).astype(F32), axis=0)
        sums = lax.psum(
            jnp.stack((jnp.sum(apply_out * apply_out, axis=1), jnp.sum(apply_out * gg, axis=1))), "head"
        )
        (od,) = call(
            functools.partial(delta_kernel, head_n * feat),
            (arr((seq_n, own, feat), BF),),
            (sums, apply_out, gg),
            0,
            16,
        )
        od = swap(od)

        *tok, inner = pl.pallas_call(
            functools.partial(backward_kernel, slab, group),
            out_shape=(*[arr((own, 3 * feat), BF)] * group, arr((seq_n * rows, 3 * slab), BF)),
            in_specs=[SMEM, VMEM, VMEM, VMEM, VMEM],
            out_specs=[VMEM] * (group + 1),
            scratch_shapes=[
                pltpu.VMEM((group, own, 3 * feat), BF),
                *[pltpu.VMEM((seq_n * rows, slab), F32)] * 3,
            ],
            compiler_params=pltpu.CompilerParams(vmem_limit_bytes=40 << 20),
            cost_estimate=pl.CostEstimate(
                flops=66 * near * feat * slab, bytes_accessed=8 * near * feat, transcendentals=0
            ),
        )(place, wall, q_all, kv, od)
        inner = swap(inner.reshape(seq_n, rows, 3 * slab))
        tok = [tok[0]] + [
            lax.ppermute(tok[d], "seq", [(i, i ^ d) for i in range(seq_n)]) for d in range(1, group)
        ]
        out_tok = arr((1, own, feat), BF)
        grads_t = call(tokens_kernel, (out_tok, out_tok, out_tok), (rates, *tok), 0, 16)
        grad_w = arr((1, rows, hidden), F32)
        grads_w = call(
            functools.partial(weights_kernel, group, slab), (grad_w, grad_w, grad_w), (inner,), 0, 16
        )
        return (*grads_t, *grads_w)

    return local


def solution(mesh):
    seq_n = mesh.shape["seq"]
    head_n = mesh.shape["head"]
    group = min(4, seq_n)
    tok = P("head", "seq", None)
    return jax.shard_map(
        make_local(seq_n, head_n, group),
        mesh=mesh,
        in_specs=(tok, tok, tok, tok, P("head", "seq"), P("head", None), tok, tok, tok, tok, tok, tok),
        out_specs=(tok, tok, tok, tok, tok, tok),
        check_vma=False,
    )
```

profile of v0, /device:TPU:0, one launch (start us, length us, event | category | flops | bytes accessed | tf_op | source)
XLA Modules:
  0.0 130.4 jit_solution(8344196437760697235)
XLA Ops:
  0.6 0.0 copy-start.3
  0.6 0.8 copy-done.3
  1.4 0.0 copy-start.4
  1.4 0.8 copy-done.4
  2.2 0.0 copy-start.5
  2.2 0.8 copy-done.5
  3.0 0.0 copy-start.6
  3.0 0.8 copy-done.6
  3.8 0.0 copy-start.7
  3.8 0.8 copy-done.7
  4.6 0.0 copy-start.8
  4.6 0.8 copy-done.8
  5.4 1.3 %shard_map.163 = bf16[8,32,1152]{2,1,0:T(8,128)(2,1)} custom-call(bf16[1,32,768]{2,1,0:T(8,128)(2,1)S(1)} %copy-done.3, bf16[1,32,768]{2,1,0:T(8,128)(2,1)S(1)} %copy-done.4, bf16[1,32,768]{2,1,0:T(8,128)(2,1)S(1)} %copy-done.5, bf16[1,32,768]{2,1,0:T(8,128)(2,1)S(1)} %copy-done.6, bf16[1,32,768]{2,1,0:T(8,128)(2,1)S(1)} %copy-done.7, ...), custom_call_target="tpu_custom_call" | custom-call | tf_op jit(solution)/shard_map/pallas_call | solution.py:59
  6.8 0.0 copy-start.11
  6.8 7.4 %all-to-all-start = ((bf16[8,32,1152]{2,1,0:T(8,128)(2,1)}), bf16[8,32,1152]{2,1,0:T(8,128)(2,1)S(1)}, u32[]{:S(2)}, u32[]{:S(2)}) async-start(bf16[8,32,1152]{2,1,0:T(8,128)(2,1)} %shard_map.163), calls=%async_computation | async-start | bytes 1179648 | tf_op jit(solution)/shard_map/all_to_all | solution.py:232
  14.2 0.0 copy-done.11
  14.2 19.7 %all_gather.15.q = bf16[4,128,256]{2,1,0:T(8,128)(2,1)S(1)} all-gather(bf16[1,128,256]{2,1,0:T(8,128)(2,1)S(1)} %copy-done.11), channel_id=1, replica_groups={{0,1,2,3},{4,5,6,7},{8,9,10,11},{12,13,14,15},{16,17,18,19},{20,21,22,2..., dimensions={0}, use_global_device_ids=true | all-gather | bytes 327680 | tf_op jit(solution)/shard_map/all_gather | solution.py:242
  33.9 0.0 all-to-all-done
  33.9 1.5 %shard_map.165 = bf16[4,128,256]{2,1,0:T(8,128)(2,1)} custom-call(bf16[256,1152]{1,0:T(8,128)(2,1)S(1)} %bitcast.7, bf16[4,128,256]{2,1,0:T(8,128)(2,1)S(1)} %all_gather.15.q), custom_call_target="tpu_custom_call" | custom-call | flops 150994944 | bytes 1114112 | tf_op jit(solution)/shard_map/pallas_call | solution.py:48
  35.3 0.0 copy-start
  35.3 0.0 copy-start.1
  35.3 0.0 copy-start.2
  35.3 0.0 copy-start.9
  35.3 0.0 copy-start.10
  35.3 3.5 %all-to-all-start.1 = ((bf16[4,128,256]{2,1,0:T(8,128)(2,1)}), bf16[4,128,256]{2,1,0:T(8,128)(2,1)S(1)}, u32[]{:S(2)}, u32[]{:S(2)}) async-start(bf16[4,128,256]{2,1,0:T(8,128)(2,1)} %shard_map.165), calls=%async_computation.1 | async-start | bytes 524288 | tf_op jit(solution)/shard_map/all_to_all | solution.py:232
  38.9 0.0 copy-done
  38.9 0.0 copy-done.1
  38.9 0.0 copy-done.2
  38.9 0.0 copy-done.9
  38.9 0.0 copy-done.10
  39.0 0.4 shard_map.164
  39.4 4.9 %all-to-all-done.1 = bf16[4,128,256]{2,1,0:T(8,128)(2,1)S(1)} async-done(((bf16[4,128,256]{2,1,0:T(8,128)(2,1)}), bf16[4,128,256]{2,1,0:T(8,128)(2,1)S(1)}, u32[]{:S(2)}, u32[]{:S(2)}) %all-to-all-start.1) | async-done | bytes 262176 | tf_op jit(solution)/shard_map/all_to_all | solution.py:232
  44.3 0.1 multiply_reduce_fusion.1
  44.4 5.7 %psum.7.sums = f32[2,128]{1,0:T(2,128)S(1)} all-reduce(f32[2,128]{1,0:T(2,128)S(1)} %pad_maximum_fusion), channel_id=1, replica_groups=mesh['head'=4,'seq'=8] {'head'}, use_global_device_ids=true, to_apply=%region_3.0 | all-reduce | flops 256 | bytes 2048 | tf_op jit(solution)/shard_map/psum | solution.py:267
  50.1 0.9 shard_map.166
  51.0 5.0 %all-to-all-start.2 = ((bf16[8,128,256]{2,1,0:T(8,128)(2,1)}), bf16[8,128,256]{2,1,0:T(8,128)(2,1)S(1)}, u32[]{:S(2)}, u32[]{:S(2)}) async-start(bf16[8,128,256]{2,1,0:T(8,128)(2,1)} %shard_map.166), calls=%async_computation.2 | async-start | bytes 1048576 | tf_op jit(solution)/shard_map/all_to_all | solution.py:232
  56.0 0.1 pad_add_fusion.place
  56.1 20.0 %all-gather = bf16[512,512]{1,0:T(8,128)(2,1)S(1)} all-gather(bf16[128,512]{1,0:T(8,128)(2,1)S(1)} %get-tuple-element.19), channel_id=2, replica_groups={{0,1,2,3},{4,5,6,7},{8,9,10,11},{12,13,14,15},{16,17,18,19},{20,21,22,2..., dimensions={0}, use_global_device_ids=true | all-gather | bytes 655360 | tf_op jit(solution)/shard_map/all_gather | solution.py:256
  76.1 31.4 %all_gather.12.q = bf16[8,128,256]{2,1,0:T(8,128)(2,1)S(1)} all-gather(bf16[1,128,256]{2,1,0:T(8,128)(2,1)S(1)} %copy-done.11), channel_id=1, replica_groups=mesh['head'=4,'seq'=8] {'seq'}, dimensions={0}, use_global_device_ids=true | all-gather | bytes 589824 | tf_op jit(solution)/shard_map/all_gather | solution.py:257
  107.5 0.0 all-to-all-done.2.od
  107.5 4.7 %shard_map.167 = (bf16[128,768]{1,0:T(8,128)(2,1)S(1)}, bf16[128,768]{1,0:T(8,128)(2,1)S(1)}, bf16[128,768]{1,0:T(8,128)(2,1)S(1)}, bf16[128,768]{1,0:T(8,128)(2,1)S(1)}, bf16[256,576]{1,0:T(8,128)(2,1)}) custom-call(s32[2]{0:T(128)S(1)} %pad_add_fusion.place, bf16[256,1152]{1,0:T(8,128)(2,1)S(1)} %bitcast.8, bf16[8,128,256]{2,1,0:T(8,128)(2,1)S(1)} %all_gather.12.q, ...), custom_call_target="tpu_custom_call" | custom-call | flops 1660944384 | bytes 1048576 | tf_op jit(solution)/shard_map/pallas_call | solution.py:279
  112.2 5.1 %all-to-all-start.3 = ((bf16[8,32,576]{2,1,0:T(8,128)(2,1)}), bf16[8,32,576]{2,1,0:T(8,128)(2,1)S(1)}, u32[]{:S(2)}, u32[]{:S(2)}) async-start(bf16[8,32,576]{2,1,0:T(8,128)(2,1)} %bitcast.6), calls=%async_computation.3 | async-start | bytes 655360 | tf_op jit(solution)/shard_map/all_to_all | solution.py:232
  117.3 2.0 %collective-permute-start = (bf16[128,768]{1,0:T(8,128)(2,1)S(1)}, bf16[128,768]{1,0:T(8,128)(2,1)S(1)}, u32[]{:S(2)}, u32[]{:S(2)}) collective-permute-start(bf16[128,768]{1,0:T(8,128)(2,1)S(1)} %get-tuple-element.22), channel_id=1, source_target_pairs={{0,1},{1,0},{2,3},{3,2},{4,5},{5,4},{6,7},{7,6},{8,9},{9,8},{10,11... | collective-permute-start | bytes 589832 | tf_op jit(solution)/shard_map/ppermute | solution.py:295
  119.3 1.5 %collective-permute-start.1 = (bf16[128,768]{1,0:T(8,128)(2,1)S(1)}, bf16[128,768]{1,0:T(8,128)(2,1)S(1)}, u32[]{:S(2)}, u32[]{:S(2)}) collective-permute-start(bf16[128,768]{1,0:T(8,128)(2,1)S(1)} %get-tuple-element.23), channel_id=1, source_target_pairs={{0,2},{1,3},{2,0},{3,1},{4,6},{5,7},{6,4},{7,5},{8,10},{9,11},{10,... | collective-permute-start | bytes 589832 | tf_op jit(solution)/shard_map/ppermute | solution.py:295
  120.8 0.0 collective-permute-start.2
  120.8 3.7 %collective-permute-done.refs_1_ = bf16[128,768]{1,0:T(8,128)(2,1)S(1)} collective-permute-done((bf16[128,768]{1,0:T(8,128)(2,1)S(1)}, bf16[128,768]{1,0:T(8,128)(2,1)S(1)}, u32[]{:S(2)}, u32[]{:S(2)}) %collective-permute-start) | collective-permute-done | bytes 196640 | tf_op jit(solution)/shard_map/ppermute | solution.py:295
  124.5 2.2 %collective-permute-done.1.refs_2_ = bf16[128,768]{1,0:T(8,128)(2,1)S(1)} collective-permute-done((bf16[128,768]{1,0:T(8,128)(2,1)S(1)}, bf16[128,768]{1,0:T(8,128)(2,1)S(1)}, u32[]{:S(2)}, u32[]{:S(2)}) %collective-permute-start.1) | collective-permute-done | bytes 196640 | tf_op jit(solution)/shard_map/ppermute | solution.py:295
  126.7 2.1 %collective-permute-done.2.refs_3_ = bf16[128,768]{1,0:T(8,128)(2,1)S(1)} collective-permute-done((bf16[128,768]{1,0:T(8,128)(2,1)S(1)}, bf16[128,768]{1,0:T(8,128)(2,1)S(1)}, u32[]{:S(2)}, u32[]{:S(2)}) %collective-permute-start.2) | collective-permute-done | bytes 196640 | tf_op jit(solution)/shard_map/ppermute | solution.py:295
  128.8 0.8 shard_map.168
  129.6 0.0 all-to-all-done.3.got
  129.6 0.8 shard_map.169
  (2 shorter events, 0.0 us)
Async XLA Ops:
  0.6 0.8 copy-start.3
  1.4 0.8 copy-start.4
  2.2 0.8 copy-start.5
  3.0 0.8 copy-start.6
  3.8 0.8 copy-start.7
  4.6 0.8 copy-start.8
  6.8 7.4 %copy-start.11 = (bf16[1,128,256]{2,1,0:T(8,128)(2,1)S(1)}, bf16[1,128,256]{2,1,0:T(8,128)(2,1)}, u32[]{:S(2)}) copy-start(bf16[1,128,256]{2,1,0:T(8,128)(2,1)} %param.12) | copy-start | bytes 196612
  6.8 27.1 %all-to-all-start = ((bf16[8,32,1152]{2,1,0:T(8,128)(2,1)}), bf16[8,32,1152]{2,1,0:T(8,128)(2,1)S(1)}, u32[]{:S(2)}, u32[]{:S(2)}) async-start(bf16[8,32,1152]{2,1,0:T(8,128)(2,1)} %shard_map.163), calls=%async_computation | async-start | bytes 1179648 | tf_op jit(solution)/shard_map/all_to_all | solution.py:232
  35.3 3.6 %copy-start = (bf16[1,128,256]{2,1,0:T(8,128)(2,1)S(1)}, bf16[1,128,256]{2,1,0:T(8,128)(2,1)}, u32[]{:S(2)}) copy-start(bf16[1,128,256]{2,1,0:T(8,128)(2,1)} %k.1) | copy-start | bytes 196612
  35.3 3.6 %copy-start.1 = (bf16[1,128,256]{2,1,0:T(8,128)(2,1)S(1)}, bf16[1,128,256]{2,1,0:T(8,128)(2,1)}, u32[]{:S(2)}) copy-start(bf16[1,128,256]{2,1,0:T(8,128)(2,1)} %v.1) | copy-start | bytes 196612
  35.3 3.6 %copy-start.2 = (bf16[1,128,256]{2,1,0:T(8,128)(2,1)S(1)}, bf16[1,128,256]{2,1,0:T(8,128)(2,1)}, u32[]{:S(2)}) copy-start(bf16[1,128,256]{2,1,0:T(8,128)(2,1)} %og.1) | copy-start | bytes 196612
  35.3 3.6 %copy-start.9 = (f32[1,128]{1,0:T(1,128)S(1)}, f32[1,128]{1,0:T(1,128)}, u32[]{:S(2)}) copy-start(f32[1,128]{1,0:T(1,128)} %rates.3) | copy-start | bytes 1540
  35.3 3.6 %copy-start.10 = (f32[1,256]{1,0:T(1,128)S(1)}, f32[1,256]{1,0:T(1,128)}, u32[]{:S(2)}) copy-start(f32[1,256]{1,0:T(1,128)} %gains.1) | copy-start | bytes 3076
  35.3 8.9 %all-to-all-start.1 = ((bf16[4,128,256]{2,1,0:T(8,128)(2,1)}), bf16[4,128,256]{2,1,0:T(8,128)(2,1)S(1)}, u32[]{:S(2)}, u32[]{:S(2)}) async-start(bf16[4,128,256]{2,1,0:T(8,128)(2,1)} %shard_map.165), calls=%async_computation.1 | async-start | bytes 524288 | tf_op jit(solution)/shard_map/all_to_all | solution.py:232
  51.0 56.5 %all-to-all-start.2 = ((bf16[8,128,256]{2,1,0:T(8,128)(2,1)}), bf16[8,128,256]{2,1,0:T(8,128)(2,1)S(1)}, u32[]{:S(2)}, u32[]{:S(2)}) async-start(bf16[8,128,256]{2,1,0:T(8,128)(2,1)} %shard_map.166), calls=%async_computation.2 | async-start | bytes 1048576 | tf_op jit(solution)/shard_map/all_to_all | solution.py:232
  112.2 17.4 %all-to-all-start.3 = ((bf16[8,32,576]{2,1,0:T(8,128)(2,1)}), bf16[8,32,576]{2,1,0:T(8,128)(2,1)S(1)}, u32[]{:S(2)}, u32[]{:S(2)}) async-start(bf16[8,32,576]{2,1,0:T(8,128)(2,1)} %bitcast.6), calls=%async_computation.3 | async-start | bytes 655360 | tf_op jit(solution)/shard_map/all_to_all | solution.py:232
  117.3 7.2 %collective-permute-start = (bf16[128,768]{1,0:T(8,128)(2,1)S(1)}, bf16[128,768]{1,0:T(8,128)(2,1)S(1)}, u32[]{:S(2)}, u32[]{:S(2)}) collective-permute-start(bf16[128,768]{1,0:T(8,128)(2,1)S(1)} %get-tuple-element.22), channel_id=1, source_target_pairs={{0,1},{1,0},{2,3},{3,2},{4,5},{5,4},{6,7},{7,6},{8,9},{9,8},{10,11... | collective-permute-start | bytes 589832 | tf_op jit(solution)/shard_map/ppermute | solution.py:295
  119.3 7.4 %collective-permute-start.1 = (bf16[128,768]{1,0:T(8,128)(2,1)S(1)}, bf16[128,768]{1,0:T(8,128)(2,1)S(1)}, u32[]{:S(2)}, u32[]{:S(2)}) collective-permute-start(bf16[128,768]{1,0:T(8,128)(2,1)S(1)} %get-tuple-element.23), channel_id=1, source_target_pairs={{0,2},{1,3},{2,0},{3,1},{4,6},{5,7},{6,4},{7,5},{8,10},{9,11},{10,... | collective-permute-start | bytes 589832 | tf_op jit(solution)/shard_map/ppermute | solution.py:295
  120.8 8.0 %collective-permute-start.2 = (bf16[128,768]{1,0:T(8,128)(2,1)S(1)}, bf16[128,768]{1,0:T(8,128)(2,1)S(1)}, u32[]{:S(2)}, u32[]{:S(2)}) collective-permute-start(bf16[128,768]{1,0:T(8,128)(2,1)S(1)} %get-tuple-element.24), channel_id=1, source_target_pairs={{0,3},{1,2},{2,1},{3,0},{4,7},{5,6},{6,5},{7,4},{8,11},{9,10},{10,... | collective-permute-start | bytes 589832 | tf_op jit(solution)/shard_map/ppermute | solution.py:295
where the time goes:
time: 131 us; the launch traced here: 130 us
  blocking collectives  76.8 us (59%)
  starting transfers between devices  24.6 us (19%)
  waiting for transfers between devices  12.9 us (10%)
  Pallas kernels  10.4 us (8%)
  local copies, waits for them, and re-layouts  4.81 us (4%)
    all_gather x1, blocking collectives, local(): q_all = lax.all_gather(q[0], 'seq')  31.4 us
    all_to_all x4, starting transfers between devices, swap(): lax.all_to_all(blocks, 'seq', 0, 0, axis_index_groups=axis_groups, tiled=...  21.1 us
    all_gather x1, blocking collectives, local(): kv = lax.all_gather(kv, 'seq', axis_index_groups=groups)  20 us
    all_gather x1, blocking collectives, local(): queries = lax.all_gather(q[0], 'seq', axis_index_groups=groups)  19.7 us
    ppermute x3, waiting for transfers between devices, local(): lax.ppermute(tok[d], 'seq', [(i, i ^ d) for i in range(seq_n)])  8 us
    psum x1, blocking collectives, local(): lax.psum(jnp.stack((jnp.sum(apply_out * apply_out, axis=1), jnp.sum(apply...  5.67 us
    all_to_all x4, waiting for transfers between devices, swap(): lax.all_to_all(blocks, 'seq', 0, 0, axis_index_groups=axis_groups, tiled=...  4.87 us
    unnamed x24, local copies, waits for them, and re-layouts  4.81 us
  transfers between devices with their start and end apart: 7, of which 4 were waited for; matrix products, arithmetic and copies ran while one was open for 0% of the time, Pallas kernels for 1%

commit v1 on v0

--- a/solution.py
+++ b/solution.py
@@ -59,7 +59,7 @@
     return pl.pallas_call(
         kernel,
         out_shape=outs,
-        in_specs=[pl.BlockSpec(memory_space=pl.ANY)] * len(args),
+        in_specs=[pl.BlockSpec(memory_space=pltpu.HBM)] * len(args),
         out_specs=[VMEM] * len(outs),
         scratch_shapes=[*buffers, pltpu.SemaphoreType.DMA((len(args),))],
         compiler_params=pltpu.CompilerParams(vmem_limit_bytes=16 << 20),
@@ -78,21 +78,20 @@
         copy.wait()
 
 
-def pack_kernel(group, slab, gs, us, ds, gi, ui, di, w_out, buf, sems):
-    fetch((gs, us, ds, gi, ui, di), [buf.at[pl.ds(i, 1)] for i in range(6)], sems)
+def pack_kernel(group, slab, *refs):
+    args, (w_out, tok_out, q_out, gg_out, buf, qb, kb, vb, ob, rb, gb, sems) = refs[:12], refs[12:]
+    fetch(args, [buf.at[pl.ds(i, 1)] for i in range(6)] + [qb, kb, vb, ob, rb, gb], sems)
     for j in range(group):
         cols = pl.ds(j * slab, slab)
         block = jnp.concatenate([buf[i, :, cols] for i in range(6)], axis=1)
         for p in range(j, w_out.shape[0], group):
             w_out[p] = block
-
-
-def tokens_in_kernel(k, v, og, rates, gains, kv_out, gg_out, kb, vb, ob, rb, gb, sems):
-    fetch((k, v, og, rates, gains), (kb, vb, ob, rb, gb), sems)
     tokens, feat = gg_out.shape
     rate = jnp.broadcast_to(rb[...], (feat, tokens)).T
-    kv_out[:, 0:feat] = kb[0]
-    kv_out[:, feat : 2 * feat] = (rate * vb[0].astype(F32)).astype(BF)
+    tok_out[:, 0:feat] = qb[0]
+    tok_out[:, feat : 2 * feat] = kb[0]
+    tok_out[:, 2 * feat : 3 * feat] = (rate * vb[0].astype(F32)).astype(BF)
+    q_out[...] = qb[0]
     gg_out[...] = gb[...] * ob[0].astype(F32)
 
 
@@ -106,11 +105,16 @@
     return saved, init, norm_init, norm_saved, ratio, normed
 
 
-def forward_kernel(slab, w, q, out):
+def forward_kernel(slab, group, place, w, *refs):
+    toks, (out, part) = refs[:group], refs[group:]
+    rank = place[1]
+    feat = out.shape[-1]
     normed = normalized(w, slab)[-1]
-    rows = flat(q[...])
+    rows = jnp.concatenate([t[:, 0:feat] for t in toks], axis=0)
     hidden = (silu_parts(mm(rows, normed[0]))[0] * mm(rows, normed[1])).astype(BF)
-    out[...] = mm_nt(hidden, normed[2]).astype(BF).reshape(out.shape)
+    part[...] = mm_nt(hidden, normed[2]).astype(BF).reshape(part.shape)
+    for d in range(group):
+        out[rank ^ d] = part[d]
 
 
 def delta_kernel(width, sums, apply_out, gg, out):
@@ -123,11 +127,18 @@
         out[p] = delta
 
 
-def backward_kernel(slab, group, place, w, q, kv, od, *rest):
-    outs, (inner_out, tok, ag, au, ad) = rest[:group], rest[group:]
+def backward_kernel(slab, group, tok_groups, place, w, *refs):
+    toks, refs = refs[:group], refs[group:]
+    far, refs = refs[: (tok_groups - 1) * group], refs[(tok_groups - 1) * group :]
+    od, *refs = refs
+    outs, (inner_out, q, tok, ag, au, ad) = refs[:group], refs[group:]
     mine, rank = place[0], place[1]
     saved, init, norm_init, norm_saved, ratio, normed = normalized(w, slab)
-    feat = q.shape[-1]
+    own, feat = od.shape[1:]
+    for d in range(group):
+        q[0, rank ^ d] = toks[d][:, 0:feat]
+        for e in range(1, tok_groups):
+            q[e, rank ^ d] = far[(e - 1) * group + d][...]
 
     def query_side(rows, delta):
         q_gate = mm(rows, normed[0])
@@ -140,16 +151,16 @@
         grads = (mm_tn(rows, delta_gate), mm_tn(rows, delta_up), mm_tn(delta, hidden))
         return delta_gate, delta_up, grads
 
-    def take(ref, e):
-        return flat(ref[pl.ds((mine ^ e) * group, group)])
-
-    delta_gate, delta_up, grads = query_side(take(q, 0), take(od, 0))
+    def take(e):
+        return flat(q[e]), flat(od[pl.ds((mine ^ e) * group, group)])
+
+    delta_gate, delta_up, grads = query_side(*take(0))
     grad_q = mm_nt(delta_gate, normed[0]) + mm_nt(delta_up, normed[1])
-    tok[:, :, 0:feat] = grad_q.astype(BF).reshape(group, -1, feat)
+    tok[...] = grad_q.astype(BF).reshape(tok.shape)
     ag[...], au[...], ad[...] = grads
 
     def other(e, carry):
-        more = query_side(take(q, e), take(od, e))[2]
+        more = query_side(*take(e))[2]
         ag[...] += more[0]
         au[...] += more[1]
         ad[...] += more[2]
@@ -169,8 +180,8 @@
         direct.append((cot + init[i] * (col_dot / (norm_init[i] * norm_saved[i]))) * share)
 
     init_bf = [w[:, pl.ds((3 + i) * slab, slab)] for i in range(3)]
-    keys = flat(kv[:, :, 0:feat])
-    values = flat(kv[:, :, feat : 2 * feat])
+    keys = jnp.concatenate([t[:, feat : 2 * feat] for t in toks], axis=0)
+    values = jnp.concatenate([t[:, 2 * feat : 3 * feat] for t in toks], axis=0)
     k_gate = mm(keys, init_bf[0])
     k_up = mm(keys, init_bf[1])
     k_proj = mm(values, init_bf[2])
@@ -193,12 +204,14 @@
         + mm_nt(back_kup, init_bf[1])
     )
     grad_v = mm_nt(k_hidden, cots[2]) + mm_nt(back_proj, init_bf[2])
-    tok[:, :, feat : 2 * feat] = grad_k.astype(BF).reshape(group, -1, feat)
-    tok[:, :, 2 * feat : 3 * feat] = grad_v.astype(BF).reshape(group, -1, feat)
+    grad_k = grad_k.astype(BF)
+    grad_v = grad_v.astype(BF)
+    for d in range(group):
+        outs[d][:, 0:feat] = tok[rank ^ d]
+        outs[d][:, feat : 2 * feat] = grad_k[d * own : (d + 1) * own]
+        outs[d][:, 2 * feat : 3 * feat] = grad_v[d * own : (d + 1) * own]
     inner = (mm_tn(keys, back_kgate), mm_tn(keys, back_kup), mm_tn(values, back_proj))
     inner_out[...] = jnp.concatenate([inner[i] + direct[i] for i in range(3)], axis=1).astype(BF)
-    for d in range(group):
-        outs[d][...] = tok[rank ^ d]
 
 
 def tokens_kernel(rates, *refs):
@@ -239,30 +252,39 @@
         me = lax.axis_index("seq")
         place = jnp.stack((lax.div(me, group), lax.rem(me, group))).astype(jnp.int32)
 
-        queries = lax.all_gather(q[0], "seq", axis_index_groups=groups)
-        (packed,) = copying_call(
+        def near_all(x):
+            return [x] + [lax.ppermute(x, "seq", [(i, i ^ d) for i in range(seq_n)]) for d in range(1, group)]
+
+        args = (gs, us, ds, gi, ui, di, q, k, v, og, rates, gains)
+        packed, tokens, queries, gg = copying_call(
             functools.partial(pack_kernel, group, slab),
-            (arr((seq_n, rows, 6 * slab), BF),),
-            (gs, us, ds, gi, ui, di),
-            [pltpu.VMEM((6, rows, hidden), BF)],
-        )
-        kv, gg = copying_call(
-            tokens_in_kernel,
-            (arr((own, 2 * feat), BF), arr((own, feat), F32)),
-            (k, v, og, rates, gains),
-            [pltpu.VMEM(x.shape, x.dtype) for x in (k, v, og, rates, gains)],
+            (
+                arr((seq_n, rows, 6 * slab), BF),
+                arr((own, 3 * feat), BF),
+                arr((own, feat), BF),
+                arr((own, feat), F32),
+            ),
+            args,
+            [pltpu.VMEM((6, rows, hidden), BF), *[pltpu.VMEM(x.shape, x.dtype) for x in args[6:]]],
         )
         wall = swap(packed).reshape(seq_n * rows, 6 * slab)
-        kv = lax.all_gather(kv, "seq", axis_index_groups=groups)
-        q_all = lax.all_gather(q[0], "seq")
-
-        (part,) = call(
-            functools.partial(forward_kernel, slab),
-            (arr((group, own, feat), BF),),
-            (wall, queries),
-            6 * near * feat * slab,
-            24,
-        )
+        tokens = near_all(tokens)
+        mirrored = [
+            lax.ppermute(queries, "seq", [(i, i ^ (e * group)) for i in range(seq_n)])
+            for e in range(1, tok_groups)
+        ]
+
+        (part,) = pl.pallas_call(
+            functools.partial(forward_kernel, slab, group),
+            out_shape=(arr((group, own, feat), BF),),
+            in_specs=[SMEM] + [VMEM] * (group + 1),
+            out_specs=[VMEM],
+            scratch_shapes=[pltpu.VMEM((group, own, feat), BF)],
+            compiler_params=pltpu.CompilerParams(vmem_limit_bytes=24 << 20),
+            cost_estimate=pl.CostEstimate(
+                flops=6 * near * feat * slab, bytes_accessed=4 * near * feat, transcendentals=0
+            ),
+        )(place, wall, *tokens)
         apply_out = jnp.sum(swap(part, groups).astype(F32), axis=0)
         sums = lax.psum(
             jnp.stack((jnp.sum(apply_out * apply_out, axis=1), jnp.sum(apply_out * gg, axis=1))), "head"
@@ -274,22 +296,25 @@
             0,
             16,
         )
+        od, *mirrored = lax.optimization_barrier((od, *mirrored))
         od = swap(od)
+        far = [block for m in mirrored for block in near_all(m)]
 
         *tok, inner = pl.pallas_call(
-            functools.partial(backward_kernel, slab, group),
+            functools.partial(backward_kernel, slab, group, tok_groups),
             out_shape=(*[arr((own, 3 * feat), BF)] * group, arr((seq_n * rows, 3 * slab), BF)),
-            in_specs=[SMEM, VMEM, VMEM, VMEM, VMEM],
+            in_specs=[SMEM] + [VMEM] * (2 + group * tok_groups),
             out_specs=[VMEM] * (group + 1),
             scratch_shapes=[
-                pltpu.VMEM((group, own, 3 * feat), BF),
+                pltpu.VMEM((tok_groups, group, own, feat), BF),
+                pltpu.VMEM((group, own, feat), BF),
                 *[pltpu.VMEM((seq_n * rows, slab), F32)] * 3,
             ],
             compiler_params=pltpu.CompilerParams(vmem_limit_bytes=40 << 20),
             cost_estimate=pl.CostEstimate(
                 flops=66 * near * feat * slab, bytes_accessed=8 * near * feat, transcendentals=0
             ),
-        )(place, wall, q_all, kv, od)
+        )(place, wall, *tokens, *far, od)
         inner = swap(inner.reshape(seq_n, rows, 3 * slab))
         tok = [tok[0]] + [
             lax.ppermute(tok[d], "seq", [(i, i ^ d) for i in range(seq_n)]) for d in range(1, group)

time: 131 us -> 105 us (0.80)
  blocking collectives: 76.8 us -> 5.67 us
  waiting for transfers between devices: 12.9 us -> 44.1 us
  starting transfers between devices: 24.6 us -> 32.4 us
  local copies, waits for them, and re-layouts: 4.81 us -> 9.47 us
    all_gather x3 -> x0, blocking collectives: 71.1 us -> none  [the longest x1 31.4 us: local(): q_all = lax.all_gather(q[0], 'seq')]
    ppermute x0 -> x7, waiting for transfers between devices: none -> 25.6 us  [the longest x6 25.6 us: near_all(): lax.ppermute(x, 'seq', [(i, i ^ d) for i in range(seq_n)])]
    ppermute x0 -> x7, starting transfers between devices: none -> 9.51 us  [the longest x6 7.03 us: near_all(): lax.ppermute(x, 'seq', [(i, i ^ d) for i in range(seq_n)])]
    ppermute x3, waiting for transfers between devices: 8 us -> 13.5 us  [local(): lax.ppermute(tok[d], 'seq', [(i, i ^ d) for i in range(seq_n)])]
    unnamed x24 -> x26, local copies, waits for them, and re-layouts: 4.81 us -> 9.47 us
    pallas_call x1 -> x2, Pallas kernels: 4.68 us -> 6.67 us  [the longest x1 4.65 us: local(): pl.pallas_call(functools.partial(backward_kernel, slab, group, tok_groups...]
    all_to_all x4, starting transfers between devices: 21.1 us -> 19.4 us  [swap(): lax.all_to_all(blocks, 'seq', 0, 0, axis_index_groups=axis_groups, tiled=...]
    pallas_call x4 -> x3, Pallas kernels: 3.96 us -> 2.52 us  [call(): pl.pallas_call(kernel, out_shape=outs, in_specs=[SMEM] * smem + [VMEM] *...]
  transfers between devices with their start and end apart: 7 -> 14, of which waited for: 4 -> 9; matrix products, arithmetic and copies ran while one was open for 0% -> 0% of each run, Pallas kernels for 1% -> 2%
where the time goes in v1:
time: 105 us; the launch traced here: 104 us
  waiting for transfers between devices  44.1 us (42%)
  starting transfers between devices  32.4 us (31%)
  Pallas kernels  11 us (10%)
  local copies, waits for them, and re-layouts  9.47 us (9%)
  blocking collectives  5.67 us (5%)
    ppermute x6, waiting for transfers between devices, near_all(): lax.ppermute(x, 'seq', [(i, i ^ d) for i in range(seq_n)])  25.6 us
    all_to_all x4, starting transfers between devices, swap(): lax.all_to_all(blocks, 'seq', 0, 0, axis_index_groups=axis_groups, tiled=...  19.4 us
    ppermute x3, waiting for transfers between devices, local(): lax.ppermute(tok[d], 'seq', [(i, i ^ d) for i in range(seq_n)])  13.5 us
    unnamed x26, local copies, waits for them, and re-layouts  9.47 us
    ppermute x6, starting transfers between devices, near_all(): lax.ppermute(x, 'seq', [(i, i ^ d) for i in range(seq_n)])  7.03 us
    psum x1, blocking collectives, local(): lax.psum(jnp.stack((jnp.sum(apply_out * apply_out, axis=1), jnp.sum(apply...  5.67 us
    all_to_all x4, waiting for transfers between devices, swap(): lax.all_to_all(blocks, 'seq', 0, 0, axis_index_groups=axis_groups, tiled=...  5.04 us
    pallas_call x1, Pallas kernels, local(): pl.pallas_call(functools.partial(backward_kernel, slab, group, tok_groups...  4.65 us
  transfers between devices with their start and end apart: 14, of which 9 were waited for; matrix products, arithmetic and copies ran while one was open for 0% of the time, Pallas kernels for 2%

profile of v1, /device:TPU:0, one launch (start us, length us, event | category | flops | bytes accessed | tf_op | source)
XLA Modules:
  0.0 103.6 jit_solution(13045245164198718233)
XLA Ops:
  0.6 0.0 copy-start
  0.6 0.8 copy-done
  1.5 0.0 copy-start.1
  1.5 0.8 copy-done.1
  2.3 0.0 copy-start.2
  2.3 0.8 copy-done.2
  3.2 0.0 copy-start.3
  3.2 0.8 copy-done.3
  4.0 0.0 copy-start.4
  4.0 0.8 copy-done.4
  4.8 0.0 copy-start.5
  4.8 0.8 copy-done.5
  5.6 0.0 copy-start.6
  5.6 0.8 copy-done.6
  6.4 0.0 copy-start.7
  6.4 0.8 copy-done.7
  7.2 0.0 copy-start.8
  7.2 0.8 copy-done.8
  8.0 0.0 copy-start.9
  8.0 0.8 copy-done.9
  8.8 0.0 copy-start.10
  8.8 0.7 copy-done.10
  9.4 0.0 copy-start.12
  9.4 0.7 copy-done.12
  10.1 1.8 %shard_map.163 = (bf16[8,32,1152]{2,1,0:T(8,128)(2,1)}, bf16[128,768]{1,0:T(8,128)(2,1)S(1)}, bf16[128,256]{1,0:T(8,128)(2,1)S(1)}, f32[128,256]{1,0:T(8,128)S(1)}) custom-call(bf16[1,32,768]{2,1,0:T(8,128)(2,1)S(1)} %copy-done.4, bf16[1,32,768]{2,1,0:T(8,128)(2,1)S(1)} %copy-done.5, bf16[1,32,768]{2,1,0:T(8,128)(2,1)S(1)} %copy-done.6, ...), custom_call_target="tpu_custom_call" | custom-call | tf_op jit(solution)/shard_map/pallas_call | solution.py:59
  11.9 7.3 %all-to-all-start = ((bf16[8,32,1152]{2,1,0:T(8,128)(2,1)}), bf16[8,32,1152]{2,1,0:T(8,128)(2,1)S(1)}, u32[]{:S(2)}, u32[]{:S(2)}) async-start(bf16[8,32,1152]{2,1,0:T(8,128)(2,1)} %get-tuple-element.23), calls=%async_computation | async-start | bytes 1179648 | tf_op jit(solution)/shard_map/all_to_all | solution.py:245
  19.2 2.9 %collective-permute-start.2 = (bf16[128,768]{1,0:T(8,128)(2,1)S(1)}, bf16[128,768]{1,0:T(8,128)(2,1)S(1)}, u32[]{:S(2)}, u32[]{:S(2)}) collective-permute-start(bf16[128,768]{1,0:T(8,128)(2,1)S(1)} %get-tuple-element.24.refs_0_), channel_id=1, source_target_pairs={{0,3},{1,2},{2,1},{3,0},{4,7},{5,6},{6,5},{7,4},{8,11},{9,10},{10,... | collective-permute-start | bytes 589832 | tf_op jit(solution)/shard_map/ppermute | solution.py:256
  22.1 0.6 collective-permute-start.1
  22.7 0.0 collective-permute-start
  22.7 0.1 pad_add_fusion.place
  22.8 14.4 %collective-permute-done.2.refs_3_ = bf16[128,768]{1,0:T(8,128)(2,1)S(1)} collective-permute-done((bf16[128,768]{1,0:T(8,128)(2,1)S(1)}, bf16[128,768]{1,0:T(8,128)(2,1)S(1)}, u32[]{:S(2)}, u32[]{:S(2)}) %collective-permute-start.2) | collective-permute-done | bytes 196640 | tf_op jit(solution)/shard_map/ppermute | solution.py:256
  37.2 2.3 %collective-permute-done.1.refs_2_ = bf16[128,768]{1,0:T(8,128)(2,1)S(1)} collective-permute-done((bf16[128,768]{1,0:T(8,128)(2,1)S(1)}, bf16[128,768]{1,0:T(8,128)(2,1)S(1)}, u32[]{:S(2)}, u32[]{:S(2)}) %collective-permute-start.1) | collective-permute-done | bytes 196640 | tf_op jit(solution)/shard_map/ppermute | solution.py:256
  39.5 0.0 collective-permute-done.refs_1_
  39.5 0.0 all-to-all-done
  39.5 2.0 %shard_map.164 = bf16[4,128,256]{2,1,0:T(8,128)(2,1)} custom-call(s32[2]{0:T(128)S(1)} %pad_add_fusion.place, bf16[256,1152]{1,0:T(8,128)(2,1)S(1)} %bitcast.6, bf16[128,768]{1,0:T(8,128)(2,1)S(1)} %get-tuple-element.24.refs_0_, bf16[128,768]{1,0:T(8,128)(2,1)S(1)} %collective-permute-done.refs_1_, bf16[128,768]{1,0:T(8,128)(2,1)S(1)} %collective-permute-done.1.refs_2_, ...), custom_call_target="tpu_custom_call" | custom-call | flops 150994944 | bytes 524288 | tf_op jit(solution)/shard_map/pallas_call | solution.py:277
  41.5 3.4 %all-to-all-start.1 = ((bf16[4,128,256]{2,1,0:T(8,128)(2,1)}), bf16[4,128,256]{2,1,0:T(8,128)(2,1)S(1)}, u32[]{:S(2)}, u32[]{:S(2)}) async-start(bf16[4,128,256]{2,1,0:T(8,128)(2,1)} %shard_map.164), calls=%async_computation.1 | async-start | bytes 524288 | tf_op jit(solution)/shard_map/all_to_all | solution.py:245
  44.9 2.5 %collective-permute-start.3 = (bf16[128,256]{1,0:T(8,128)(2,1)S(1)}, bf16[128,256]{1,0:T(8,128)(2,1)S(1)}, u32[]{:S(2)}, u32[]{:S(2)}) collective-permute-start(bf16[128,256]{1,0:T(8,128)(2,1)S(1)} %get-tuple-element.26), channel_id=1, source_target_pairs={{0,4},{1,5},{2,6},{3,7},{4,0},{5,1},{6,2},{7,3},{8,12},{9,13},{10,... | collective-permute-start | bytes 196616 | tf_op jit(solution)/shard_map/ppermute | solution.py:273
  47.4 2.9 %all-to-all-done.1 = bf16[4,128,256]{2,1,0:T(8,128)(2,1)S(1)} async-done(((bf16[4,128,256]{2,1,0:T(8,128)(2,1)}), bf16[4,128,256]{2,1,0:T(8,128)(2,1)S(1)}, u32[]{:S(2)}, u32[]{:S(2)}) %all-to-all-start.1) | async-done | bytes 262176 | tf_op jit(solution)/shard_map/all_to_all | solution.py:245
  50.3 0.1 multiply_reduce_fusion.1
  50.5 5.7 %psum.7.sums = f32[2,128]{1,0:T(2,128)S(1)} all-reduce(f32[2,128]{1,0:T(2,128)S(1)} %pad_maximum_fusion), channel_id=1, replica_groups=mesh['head'=4,'seq'=8] {'head'}, use_global_device_ids=true, to_apply=%region_3.0 | all-reduce | flops 256 | bytes 2048 | tf_op jit(solution)/shard_map/psum | solution.py:289
  56.1 0.9 shard_map.165
  57.1 0.0 collective-permute-done.3.refs_4_
  57.1 5.0 %all-to-all-start.2 = ((bf16[8,128,256]{2,1,0:T(8,128)(2,1)}), bf16[8,128,256]{2,1,0:T(8,128)(2,1)S(1)}, u32[]{:S(2)}, u32[]{:S(2)}) async-start(bf16[8,128,256]{2,1,0:T(8,128)(2,1)} %shard_map.165), calls=%async_computation.2 | async-start | bytes 1048576 | tf_op jit(solution)/shard_map/all_to_all | solution.py:245
  62.1 2.9 %collective-permute-start.6 = (bf16[128,256]{1,0:T(8,128)(2,1)S(1)}, bf16[128,256]{1,0:T(8,128)(2,1)S(1)}, u32[]{:S(2)}, u32[]{:S(2)}) collective-permute-start(bf16[128,256]{1,0:T(8,128)(2,1)S(1)} %collective-permute-done.3.refs_4_), channel_id=1, source_target_pairs={{0,3},{1,2},{2,1},{3,0},{4,7},{5,6},{6,5},{7,4},{8,11},{9,10},{10,... | collective-permute-start | bytes 196616 | tf_op jit(solution)/shard_map/ppermute | solution.py:256
  65.0 0.6 collective-permute-start.5
  65.5 0.0 collective-permute-start.4
  65.6 8.5 %collective-permute-done.6.refs_7_ = bf16[128,256]{1,0:T(8,128)(2,1)S(1)} collective-permute-done((bf16[128,256]{1,0:T(8,128)(2,1)S(1)}, bf16[128,256]{1,0:T(8,128)(2,1)S(1)}, u32[]{:S(2)}, u32[]{:S(2)}) %collective-permute-start.6) | collective-permute-done | bytes 65568 | tf_op jit(solution)/shard_map/ppermute | solution.py:256
  74.1 0.4 collective-permute-done.5.refs_6_
  74.4 0.0 collective-permute-done.4.refs_5_
  74.4 2.1 %all-to-all-done.2.refs_8_ = bf16[8,128,256]{2,1,0:T(8,128)(2,1)S(1)} async-done(((bf16[8,128,256]{2,1,0:T(8,128)(2,1)}), bf16[8,128,256]{2,1,0:T(8,128)(2,1)S(1)}, u32[]{:S(2)}, u32[]{:S(2)}) %all-to-all-start.2) | async-done | bytes 524320 | tf_op jit(solution)/shard_map/all_to_all | solution.py:245
  76.6 4.7 %shard_map.166 = (bf16[128,768]{1,0:T(8,128)(2,1)S(1)}, bf16[128,768]{1,0:T(8,128)(2,1)S(1)}, bf16[128,768]{1,0:T(8,128)(2,1)S(1)}, bf16[128,768]{1,0:T(8,128)(2,1)S(1)}, bf16[256,576]{1,0:T(8,128)(2,1)}) custom-call(s32[2]{0:T(128)S(1)} %pad_add_fusion.place, bf16[256,1152]{1,0:T(8,128)(2,1)S(1)} %bitcast.7, ...), custom_call_target="tpu_custom_call" | custom-call | flops 1660944384 | bytes 1048576 | tf_op jit(solution)/shard_map/pallas_call | solution.py:303
  81.2 3.7 %all-to-all-start.3 = ((bf16[8,32,576]{2,1,0:T(8,128)(2,1)}), bf16[8,32,576]{2,1,0:T(8,128)(2,1)S(1)}, u32[]{:S(2)}, u32[]{:S(2)}) async-start(bf16[8,32,576]{2,1,0:T(8,128)(2,1)} %bitcast.5), calls=%async_computation.3 | async-start | bytes 655360 | tf_op jit(solution)/shard_map/all_to_all | solution.py:245
  85.0 2.0 %collective-permute-start.7 = (bf16[128,768]{1,0:T(8,128)(2,1)S(1)}, bf16[128,768]{1,0:T(8,128)(2,1)S(1)}, u32[]{:S(2)}, u32[]{:S(2)}) collective-permute-start(bf16[128,768]{1,0:T(8,128)(2,1)S(1)} %get-tuple-element.30), channel_id=1, source_target_pairs={{0,1},{1,0},{2,3},{3,2},{4,5},{5,4},{6,7},{7,6},{8,9},{9,8},{10,11... | collective-permute-start | bytes 589832 | tf_op jit(solution)/shard_map/ppermute | solution.py:320
  87.0 1.5 %collective-permute-start.8 = (bf16[128,768]{1,0:T(8,128)(2,1)S(1)}, bf16[128,768]{1,0:T(8,128)(2,1)S(1)}, u32[]{:S(2)}, u32[]{:S(2)}) collective-permute-start(bf16[128,768]{1,0:T(8,128)(2,1)S(1)} %get-tuple-element.31), channel_id=1, source_target_pairs={{0,2},{1,3},{2,0},{3,1},{4,6},{5,7},{6,4},{7,5},{8,10},{9,11},{10,... | collective-permute-start | bytes 589832 | tf_op jit(solution)/shard_map/ppermute | solution.py:320
  88.5 0.0 copy-start.11
  88.5 0.0 collective-permute-start.9
  88.5 6.2 %collective-permute-done.7.refs_1_ = bf16[128,768]{1,0:T(8,128)(2,1)S(1)} collective-permute-done((bf16[128,768]{1,0:T(8,128)(2,1)S(1)}, bf16[128,768]{1,0:T(8,128)(2,1)S(1)}, u32[]{:S(2)}, u32[]{:S(2)}) %collective-permute-start.7) | collective-permute-done | bytes 196640 | tf_op jit(solution)/shard_map/ppermute | solution.py:320
  94.7 3.5 %collective-permute-done.8.refs_2_ = bf16[128,768]{1,0:T(8,128)(2,1)S(1)} collective-permute-done((bf16[128,768]{1,0:T(8,128)(2,1)S(1)}, bf16[128,768]{1,0:T(8,128)(2,1)S(1)}, u32[]{:S(2)}, u32[]{:S(2)}) %collective-permute-start.8) | collective-permute-done | bytes 196640 | tf_op jit(solution)/shard_map/ppermute | solution.py:320
  98.2 3.8 %collective-permute-done.9.refs_3_ = bf16[128,768]{1,0:T(8,128)(2,1)S(1)} collective-permute-done((bf16[128,768]{1,0:T(8,128)(2,1)S(1)}, bf16[128,768]{1,0:T(8,128)(2,1)S(1)}, u32[]{:S(2)}, u32[]{:S(2)}) %collective-permute-start.9) | collective-permute-done | bytes 196640 | tf_op jit(solution)/shard_map/ppermute | solution.py:320
  102.0 0.0 copy-done.11
  102.0 0.8 shard_map.167
  102.8 0.0 all-to-all-done.3.got
  102.8 0.8 shard_map.168
  (2 shorter events, 0.0 us)
Async XLA Ops:
  0.6 0.8 copy-start
  1.5 0.8 copy-start.1
  2.3 0.8 copy-start.2
  3.2 0.8 copy-start.3
  4.0 0.8 copy-start.4
  4.8 0.8 copy-start.5
  5.6 0.8 copy-start.6
  6.4 0.8 copy-start.7
  7.2 0.8 copy-start.8
  8.0 0.8 copy-start.9
  8.8 0.7 copy-start.10
  9.4 0.7 copy-start.12
  11.9 27.6 %all-to-all-start = ((bf16[8,32,1152]{2,1,0:T(8,128)(2,1)}), bf16[8,32,1152]{2,1,0:T(8,128)(2,1)S(1)}, u32[]{:S(2)}, u32[]{:S(2)}) async-start(bf16[8,32,1152]{2,1,0:T(8,128)(2,1)} %get-tuple-element.23), calls=%async_computation | async-start | bytes 1179648 | tf_op jit(solution)/shard_map/all_to_all | solution.py:245
  19.2 18.0 %collective-permute-start.2 = (bf16[128,768]{1,0:T(8,128)(2,1)S(1)}, bf16[128,768]{1,0:T(8,128)(2,1)S(1)}, u32[]{:S(2)}, u32[]{:S(2)}) collective-permute-start(bf16[128,768]{1,0:T(8,128)(2,1)S(1)} %get-tuple-element.24.refs_0_), channel_id=1, source_target_pairs={{0,3},{1,2},{2,1},{3,0},{4,7},{5,6},{6,5},{7,4},{8,11},{9,10},{10,... | collective-permute-start | bytes 589832 | tf_op jit(solution)/shard_map/ppermute | solution.py:256
  22.1 17.4 %collective-permute-start.1 = (bf16[128,768]{1,0:T(8,128)(2,1)S(1)}, bf16[128,768]{1,0:T(8,128)(2,1)S(1)}, u32[]{:S(2)}, u32[]{:S(2)}) collective-permute-start(bf16[128,768]{1,0:T(8,128)(2,1)S(1)} %get-tuple-element.24.refs_0_), channel_id=1, source_target_pairs={{0,2},{1,3},{2,0},{3,1},{4,6},{5,7},{6,4},{7,5},{8,10},{9,11},{10,... | collective-permute-start | bytes 589832 | tf_op jit(solution)/shard_map/ppermute | solution.py:256
  22.7 16.8 %collective-permute-start = (bf16[128,768]{1,0:T(8,128)(2,1)S(1)}, bf16[128,768]{1,0:T(8,128)(2,1)S(1)}, u32[]{:S(2)}, u32[]{:S(2)}) collective-permute-start(bf16[128,768]{1,0:T(8,128)(2,1)S(1)} %get-tuple-element.24.refs_0_), channel_id=1, source_target_pairs={{0,1},{1,0},{2,3},{3,2},{4,5},{5,4},{6,7},{7,6},{8,9},{9,8},{10,11... | collective-permute-start | bytes 589832 | tf_op jit(solution)/shard_map/ppermute | solution.py:256
  41.5 8.8 %all-to-all-start.1 = ((bf16[4,128,256]{2,1,0:T(8,128)(2,1)}), bf16[4,128,256]{2,1,0:T(8,128)(2,1)S(1)}, u32[]{:S(2)}, u32[]{:S(2)}) async-start(bf16[4,128,256]{2,1,0:T(8,128)(2,1)} %shard_map.164), calls=%async_computation.1 | async-start | bytes 524288 | tf_op jit(solution)/shard_map/all_to_all | solution.py:245
  44.9 12.2 %collective-permute-start.3 = (bf16[128,256]{1,0:T(8,128)(2,1)S(1)}, bf16[128,256]{1,0:T(8,128)(2,1)S(1)}, u32[]{:S(2)}, u32[]{:S(2)}) collective-permute-start(bf16[128,256]{1,0:T(8,128)(2,1)S(1)} %get-tuple-element.26), channel_id=1, source_target_pairs={{0,4},{1,5},{2,6},{3,7},{4,0},{5,1},{6,2},{7,3},{8,12},{9,13},{10,... | collective-permute-start | bytes 196616 | tf_op jit(solution)/shard_map/ppermute | solution.py:273
  57.1 19.5 %all-to-all-start.2 = ((bf16[8,128,256]{2,1,0:T(8,128)(2,1)}), bf16[8,128,256]{2,1,0:T(8,128)(2,1)S(1)}, u32[]{:S(2)}, u32[]{:S(2)}) async-start(bf16[8,128,256]{2,1,0:T(8,128)(2,1)} %shard_map.165), calls=%async_computation.2 | async-start | bytes 1048576 | tf_op jit(solution)/shard_map/all_to_all | solution.py:245
  62.1 12.0 %collective-permute-start.6 = (bf16[128,256]{1,0:T(8,128)(2,1)S(1)}, bf16[128,256]{1,0:T(8,128)(2,1)S(1)}, u32[]{:S(2)}, u32[]{:S(2)}) collective-permute-start(bf16[128,256]{1,0:T(8,128)(2,1)S(1)} %collective-permute-done.3.refs_4_), channel_id=1, source_target_pairs={{0,3},{1,2},{2,1},{3,0},{4,7},{5,6},{6,5},{7,4},{8,11},{9,10},{10,... | collective-permute-start | bytes 196616 | tf_op jit(solution)/shard_map/ppermute | solution.py:256
  65.0 9.5 %collective-permute-start.5 = (bf16[128,256]{1,0:T(8,128)(2,1)S(1)}, bf16[128,256]{1,0:T(8,128)(2,1)S(1)}, u32[]{:S(2)}, u32[]{:S(2)}) collective-permute-start(bf16[128,256]{1,0:T(8,128)(2,1)S(1)} %collective-permute-done.3.refs_4_), channel_id=1, source_target_pairs={{0,2},{1,3},{2,0},{3,1},{4,6},{5,7},{6,4},{7,5},{8,10},{9,11},{10,... | collective-permute-start | bytes 196616 | tf_op jit(solution)/shard_map/ppermute | solution.py:256
  65.5 8.9 %collective-permute-start.4 = (bf16[128,256]{1,0:T(8,128)(2,1)S(1)}, bf16[128,256]{1,0:T(8,128)(2,1)S(1)}, u32[]{:S(2)}, u32[]{:S(2)}) collective-permute-start(bf16[128,256]{1,0:T(8,128)(2,1)S(1)} %collective-permute-done.3.refs_4_), channel_id=1, source_target_pairs={{0,1},{1,0},{2,3},{3,2},{4,5},{5,4},{6,7},{7,6},{8,9},{9,8},{10,11... | collective-permute-start | bytes 196616 | tf_op jit(solution)/shard_map/ppermute | solution.py:256
  81.2 21.5 %all-to-all-start.3 = ((bf16[8,32,576]{2,1,0:T(8,128)(2,1)}), bf16[8,32,576]{2,1,0:T(8,128)(2,1)S(1)}, u32[]{:S(2)}, u32[]{:S(2)}) async-start(bf16[8,32,576]{2,1,0:T(8,128)(2,1)} %bitcast.5), calls=%async_computation.3 | async-start | bytes 655360 | tf_op jit(solution)/shard_map/all_to_all | solution.py:245
  85.0 9.7 %collective-permute-start.7 = (bf16[128,768]{1,0:T(8,128)(2,1)S(1)}, bf16[128,768]{1,0:T(8,128)(2,1)S(1)}, u32[]{:S(2)}, u32[]{:S(2)}) collective-permute-start(bf16[128,768]{1,0:T(8,128)(2,1)S(1)} %get-tuple-element.30), channel_id=1, source_target_pairs={{0,1},{1,0},{2,3},{3,2},{4,5},{5,4},{6,7},{7,6},{8,9},{9,8},{10,11... | collective-permute-start | bytes 589832 | tf_op jit(solution)/shard_map/ppermute | solution.py:320
  87.0 11.2 %collective-permute-start.8 = (bf16[128,768]{1,0:T(8,128)(2,1)S(1)}, bf16[128,768]{1,0:T(8,128)(2,1)S(1)}, u32[]{:S(2)}, u32[]{:S(2)}) collective-permute-start(bf16[128,768]{1,0:T(8,128)(2,1)S(1)} %get-tuple-element.31), channel_id=1, source_target_pairs={{0,2},{1,3},{2,0},{3,1},{4,6},{5,7},{6,4},{7,5},{8,10},{9,11},{10,... | collective-permute-start | bytes 589832 | tf_op jit(solution)/shard_map/ppermute | solution.py:320
  88.5 13.5 %copy-start.11 = (f32[1,128]{1,0:T(1,128)S(1)}, f32[1,128]{1,0:T(1,128)}, u32[]{:S(2)}) copy-start(f32[1,128]{1,0:T(1,128)} %rates.1) | copy-start | bytes 1540
  88.5 13.5 %collective-permute-start.9 = (bf16[128,768]{1,0:T(8,128)(2,1)S(1)}, bf16[128,768]{1,0:T(8,128)(2,1)S(1)}, u32[]{:S(2)}, u32[]{:S(2)}) collective-permute-start(bf16[128,768]{1,0:T(8,128)(2,1)S(1)} %get-tuple-element.32), channel_id=1, source_target_pairs={{0,3},{1,2},{2,1},{3,0},{4,7},{5,6},{6,5},{7,4},{8,11},{9,10},{10,... | collective-permute-start | bytes 589832 | tf_op jit(solution)/shard_map/ppermute | solution.py:320

commit v2 on v0

v2 whole, which is shorter than its diff:
```python
import functools

import jax
import jax.numpy as jnp
from jax import lax
from jax.experimental import pallas as pl
from jax.experimental.pallas import tpu as pltpu
from jax.sharding import PartitionSpec as P

EPS_COL = 1e-06
EPS_ROOT = 1e-05
BF = jnp.bfloat16
F32 = jnp.float32
VMEM = pl.BlockSpec(memory_space=pltpu.VMEM)
SMEM = pl.BlockSpec(memory_space=pltpu.SMEM)


def silu_parts(pre_act):
    sigmoid_val = jax.nn.sigmoid(pre_act)
    silu_val = pre_act * sigmoid_val
    silu_slope = sigmoid_val * (1.0 + pre_act * (1.0 - sigmoid_val))
    silu_bend = sigmoid_val * (1.0 - sigmoid_val) * (2.0 + pre_act * (1.0 - 2.0 * sigmoid_val))
    return (silu_val, silu_slope, silu_bend)


def mm(left_op, right_op):
    return jnp.dot(left_op, right_op, preferred_element_type=F32)


def mm_nt(left_op, right_op):
    return lax.dot_general(left_op, right_op, (((1,), (1,)), ((), ())), preferred_element_type=F32)


def mm_tn(left_op, right_op):
    return lax.dot_general(left_op, right_op, (((0,), (0,)), ((), ())), preferred_element_type=F32)


def column_norm(weight):
    return jnp.sqrt(jnp.sum(weight * weight, axis=0, keepdims=True) + EPS_COL)


def flat(x):
    return x.reshape(-1, x.shape[-1])


def call(kernel, outs, args, mib, smem=0, flops=0, scratch=()):
    moved = sum(x.size * x.dtype.itemsize for x in (*args, *outs))
    return pl.pallas_call(
        kernel,
        out_shape=outs,
        in_specs=[SMEM] * smem + [VMEM] * (len(args) - smem),
        out_specs=[VMEM] * len(outs),
        scratch_shapes=scratch,
        compiler_params=pltpu.CompilerParams(vmem_limit_bytes=mib << 20),
        cost_estimate=pl.CostEstimate(flops=flops, bytes_accessed=moved, transcendentals=0),
    )(*args)


def copying_call(kernel, outs, args, buffers):
    return pl.pallas_call(
        kernel,
        out_shape=outs,
        in_specs=[pl.BlockSpec(memory_space=pltpu.HBM)] * len(args),
        out_specs=[VMEM] * len(outs),
        scratch_shapes=[*buffers, pltpu.SemaphoreType.DMA((len(args),))],
        compiler_params=pltpu.CompilerParams(vmem_limit_bytes=56 << 20),
    )(*args)


def arr(shape, dtype):
    return jax.ShapeDtypeStruct(shape, dtype)


def fetch(sources, buffers, sems):
    copies = [pltpu.make_async_copy(s, b, sems.at[i]) for i, (s, b) in enumerate(zip(sources, buffers))]
    for copy in copies:
        copy.start()
    for copy in copies:
        copy.wait()


def token_pack_kernel(*refs):
    args, (tok_out, gg_out, qb, kb, vb, ob, rb, gb, sems) = refs[:6], refs[6:]
    fetch(args, (qb, kb, vb, ob, rb, gb), sems)
    tokens, feat = gg_out.shape
    rate = jnp.broadcast_to(rb[...], (feat, tokens)).T
    tok_out[:, 0:feat] = qb[0]
    tok_out[:, feat : 2 * feat] = kb[0]
    tok_out[:, 2 * feat : 3 * feat] = (rate * vb[0].astype(F32)).astype(BF)
    gg_out[...] = gb[...] * ob[0].astype(F32)


def weight_pack_kernel(group, slab, *refs):
    args, (w_out, buf, sems) = refs[:6], refs[6:]
    fetch(args, [buf.at[pl.ds(i, 1)] for i in range(6)], sems)
    for j in range(group):
        cols = pl.ds(j * slab, slab)
        block = jnp.concatenate([buf[i, :, cols] for i in range(6)], axis=1)
        for p in range(j, w_out.shape[0], group):
            w_out[p] = block


def normalized(w, slab):
    parts = [w[:, pl.ds(i * slab, slab)].astype(F32) for i in range(6)]
    saved, init = parts[:3], parts[3:]
    norm_init = [column_norm(x) for x in init]
    norm_saved = [column_norm(x) for x in saved]
    ratio = [norm_init[i] / norm_saved[i] for i in range(3)]
    normed = [(saved[i] * ratio[i]).astype(BF) for i in range(3)]
    return saved, init, norm_init, norm_saved, ratio, normed


def stack(refs, cols=slice(None)):
    return jnp.concatenate([r[:, cols] for r in refs], axis=0)


def forward_kernel(slab, group, w, *refs):
    tokens, mirrored, parts = refs[:group], refs[group:-group], refs[-group:]
    own, feat = parts[0].shape[0], parts[0].shape[1] // (1 + len(mirrored))
    normed = normalized(w, slab)[-1]
    rows = stack(tokens, slice(0, feat))
    hidden = (silu_parts(mm(rows, normed[0]))[0] * mm(rows, normed[1])).astype(BF)
    out = mm_nt(hidden, normed[2]).astype(BF)
    for d in range(group):
        parts[d][:, 0:feat] = out[d * own : (d + 1) * own]
        for e, queries in enumerate(mirrored):
            parts[d][:, (1 + e) * feat : (2 + e) * feat] = queries[...]


def reduce_kernel(gg, *refs):
    parts, (apply_out, sums) = refs[:-2], refs[-2:]
    feat = apply_out.shape[1]
    total = parts[0][:, 0:feat].astype(F32)
    for part in parts[1:]:
        total += part[:, 0:feat].astype(F32)
    apply_out[...] = total
    sums[0:1, :] = jnp.sum((total * total).T, axis=0, keepdims=True)
    sums[1:2, :] = jnp.sum((total * gg[...]).T, axis=0, keepdims=True)


def delta_kernel(width, apply_out, gg, *refs):
    sums, out = refs[:-1], refs[-1]
    tokens, feat = apply_out.shape
    total = sums[0][...]
    for more in sums[1:]:
        total += more[...]
    square = jnp.broadcast_to(total[0:1, :], (feat, tokens)).T
    gain = jnp.broadcast_to(total[1:2, :], (feat, tokens)).T
    root = jnp.sqrt(square / width + EPS_ROOT)
    out[...] = (gg[...] / root - apply_out[...] * (gain / width) / (root * root * root)).astype(BF)


def backward_kernel(slab, group, tok_groups, place, w, *refs):
    lists = []
    for count in (group, group, group, group * (tok_groups - 1), group, group * tok_groups):
        lists.append(refs[:count])
        refs = refs[count:]
    tokens, parts, od_near, od_far, outs, inner_outs = lists
    far_q, far_od, inner_all, ag, au, ad = refs
    mine, me = place[0], place[2]
    saved, init, norm_init, norm_saved, ratio, normed = normalized(w, slab)
    own, feat = od_near[0].shape
    for e in range(1, tok_groups):
        for d in range(group):
            far_q[e - 1, d] = parts[d][:, e * feat : (e + 1) * feat]
            far_od[e - 1, d] = od_far[(e - 1) * group + d][...]

    def query_side(rows, delta):
        q_gate = mm(rows, normed[0])
        q_up = mm(rows, normed[1])
        act, slope, _ = silu_parts(q_gate)
        hidden = (act * q_up).astype(BF)
        delta_hidden = mm(delta, normed[2])
        delta_gate = (delta_hidden * q_up * slope).astype(BF)
        delta_up = (delta_hidden * act).astype(BF)
        grads = (mm_tn(rows, delta_gate), mm_tn(rows, delta_up), mm_tn(delta, hidden))
        return delta_gate, delta_up, grads

    delta_gate, delta_up, grads = query_side(stack(tokens, slice(0, feat)), stack(od_near))
    grad_q = (mm_nt(delta_gate, normed[0]) + mm_nt(delta_up, normed[1])).astype(BF)
    ag[...], au[...], ad[...] = grads

    def other(e, carry):
        more = query_side(flat(far_q[e]), flat(far_od[e]))[2]
        ag[...] += more[0]
        au[...] += more[1]
        ad[...] += more[2]
        return carry

    lax.fori_loop(0, tok_groups - 1, other, 0)

    apply_grad = (ag[...], au[...], ad[...])
    cots, direct = [], []
    share = jnp.where(mine == 0, 1.0, 0.0)
    for i in range(3):
        col_dot = jnp.sum(saved[i] * apply_grad[i], axis=0, keepdims=True)
        cot = apply_grad[i] * ratio[i] - saved[i] * (
            col_dot * norm_init[i] / (norm_saved[i] * norm_saved[i] * norm_saved[i])
        )
        cots.append(cot.astype(BF))
        direct.append((cot + init[i] * (col_dot / (norm_init[i] * norm_saved[i]))) * share)

    init_bf = [w[:, pl.ds((3 + i) * slab, slab)] for i in range(3)]
    keys = stack(tokens, slice(feat, 2 * feat))
    values = stack(tokens, slice(2 * feat, 3 * feat))
    k_gate = mm(keys, init_bf[0])
    k_up = mm(keys, init_bf[1])
    k_proj = mm(values, init_bf[2])
    k_act, k_slope, k_bend = silu_parts(k_gate)
    k_hidden = (k_act * k_up).astype(BF)
    rise_gate = (k_proj * k_up * k_slope).astype(BF)
    rise_up = (k_proj * k_act).astype(BF)
    back_gate = mm(keys, cots[0])
    back_up = mm(keys, cots[1])
    back_hidden = mm(values, cots[2])
    back_proj = (back_gate * k_up * k_slope + back_up * k_act).astype(BF)
    back_kup = (back_gate * k_proj * k_slope + back_hidden * k_act).astype(BF)
    back_kgate = (
        back_gate * k_proj * k_up * k_bend + (back_up * k_proj + back_hidden * k_up) * k_slope
    ).astype(BF)
    grad_k = (
        mm_nt(rise_gate, cots[0])
        + mm_nt(rise_up, cots[1])
        + mm_nt(back_kgate, init_bf[0])
        + mm_nt(back_kup, init_bf[1])
    )
    grad_v = mm_nt(k_hidden, cots[2]) + mm_nt(back_proj, init_bf[2])
    grad_k = grad_k.astype(BF)
    grad_v = grad_v.astype(BF)
    for d in range(group):
        outs[d][:, 0:feat] = grad_q[d * own : (d + 1) * own]
        outs[d][:, feat : 2 * feat] = grad_k[d * own : (d + 1) * own]
        outs[d][:, 2 * feat : 3 * feat] = grad_v[d * own : (d + 1) * own]
    inner = (mm_tn(keys, back_kgate), mm_tn(keys, back_kup), mm_tn(values, back_proj))
    total = jnp.concatenate([inner[i] + direct[i] for i in range(3)], axis=1)
    rows = inner_all.shape[1]
    for p in range(inner_all.shape[0]):
        inner_all[p] = total[p * rows : (p + 1) * rows]
    for d, out in enumerate(inner_outs):
        out[...] = inner_all[me ^ d].astype(BF)


def tokens_kernel(rates, *refs):
    got, (gq, gk, gv) = refs[:-3], refs[-3:]
    tokens, feat = gq.shape[1:]
    total = got[0][...].astype(F32)
    for block in got[1:]:
        total += block[...].astype(F32)
    gq[0] = total[:, 0:feat].astype(BF)
    gk[0] = total[:, feat : 2 * feat].astype(BF)
    rate = jnp.broadcast_to(rates[...], (feat, tokens)).T
    gv[0] = (rate * total[:, 2 * feat : 3 * feat]).astype(BF)


def weights_kernel(group, slab, place, *refs):
    got, outs, total = refs[:-4], refs[-4:-1], refs[-1]
    for d in range(group):
        block = got[d][...].astype(F32)
        for more in got[d + group :: group]:
            block += more[...].astype(F32)
        total[d] = block
    cols = [total[place[1] ^ j] for j in range(group)]
    for i in range(3):
        outs[i][0] = jnp.concatenate([c[:, i * slab : (i + 1) * slab] for c in cols], axis=1)


def make_local(seq_n, head_n, group):
    tok_groups = seq_n // group

    def move(x, dist, axis="seq", size=seq_n):
        return lax.ppermute(x, axis, [(i, i ^ dist) for i in range(size)])

    def near_all(x):
        return [x] + [move(x, d) for d in range(1, group)]

    def mirror(x):
        return [move(x, e * group) for e in range(1, tok_groups)]

    def local(q, k, v, og, rates, gains, gi, ui, di, gs, us, ds):
        _, rows, hidden = gi.shape
        _, own, feat = q.shape
        slab = hidden // group
        near = group * own
        me = lax.axis_index("seq")
        place = jnp.stack((lax.div(me, group), lax.rem(me, group), me)).astype(jnp.int32)

        q_mirror = mirror(q[0])
        tok_args = (q, k, v, og, rates, gains)
        tokens, gg = copying_call(
            token_pack_kernel,
            (arr((own, 3 * feat), BF), arr((own, feat), F32)),
            tok_args,
            [pltpu.VMEM(x.shape, x.dtype) for x in tok_args],
        )
        tokens = near_all(tokens)
        (packed,) = copying_call(
            functools.partial(weight_pack_kernel, group, slab),
            (arr((seq_n, rows, 6 * slab), BF),),
            (gs, us, ds, gi, ui, di),
            [pltpu.VMEM((6, rows, hidden), BF)],
        )
        wall = lax.all_to_all(packed, "seq", 0, 0, tiled=True).reshape(seq_n * rows, 6 * slab)

        block = arr((own, feat), BF)
        parts = call(
            functools.partial(forward_kernel, slab, group),
            (arr((own, feat * tok_groups), BF),) * group,
            (wall, *tokens, *q_mirror),
            24,
            flops=6 * near * feat * slab,
        )
        parts = [parts[0]] + [move(parts[d], d) for d in range(1, group)]
        apply_out, sums = call(
            reduce_kernel, (arr((own, feat), F32), arr((2, own), F32)), (gg, *parts), 16
        )
        sums = [sums] + [move(sums, d, "head", head_n) for d in range(1, head_n)]
        (od,) = call(functools.partial(delta_kernel, head_n * feat), (block,), (apply_out, gg, *sums), 16)
        od_mirror = mirror(od)
        od_near = near_all(od)
        od_far = [x for m in od_mirror for x in near_all(m)]

        far = pltpu.VMEM((max(tok_groups - 1, 1), group, own, feat), BF)
        result = call(
            functools.partial(backward_kernel, slab, group, tok_groups),
            (arr((own, 3 * feat), BF),) * group + (arr((rows, 3 * slab), BF),) * seq_n,
            (place, wall, *tokens, *parts, *od_near, *od_far),
            40,
            smem=1,
            flops=66 * near * feat * slab,
            scratch=[
                far,
                far,
                pltpu.VMEM((seq_n, rows, 3 * slab), F32),
                *[pltpu.VMEM((seq_n * rows, slab), F32)] * 3,
            ],
        )
        tok, inner = result[:group], result[group:]
        tok = [tok[0]] + [move(tok[d], d) for d in range(1, group)]
        inner = [inner[0]] + [move(inner[d], d) for d in range(1, seq_n)]
        out_tok = arr((1, own, feat), BF)
        grad_w = arr((1, rows, hidden), F32)
        grads_t = call(tokens_kernel, (out_tok,) * 3, (rates, *tok), 16)
        grads_w = call(
            functools.partial(weights_kernel, group, slab),
            (grad_w,) * 3,
            (place, *inner),
            16,
            smem=1,
            scratch=[pltpu.VMEM((group, rows, 3 * slab), F32)],
        )
        return (*grads_t, *grads_w)

    return local


def solution(mesh):
    seq_n = mesh.shape["seq"]
    head_n = mesh.shape["head"]
    group = min(4, seq_n)
    tok = P("head", "seq", None)
    return jax.shard_map(
        make_local(seq_n, head_n, group),
        mesh=mesh,
        in_specs=(tok, tok, tok, tok, P("head", "seq"), P("head", None), tok, tok, tok, tok, tok, tok),
        out_specs=(tok, tok, tok, tok, tok, tok),
        check_vma=False,
    )
```

time: 131 us -> 94.6 us (0.72)
  blocking collectives: 76.8 us -> 0 us
  waiting for transfers between devices: 12.9 us -> 43 us
  starting transfers between devices: 24.6 us -> 38 us
  local copies, waits for them, and re-layouts: 4.81 us -> 1.57 us
    all_gather x3 -> x0, blocking collectives: 71.1 us -> none  [the longest x1 31.4 us: local(): q_all = lax.all_gather(q[0], 'seq')]
    ppermute x3 -> x27, waiting for transfers between devices: 8 us -> 43 us  [move(): return lax.ppermute(x, axis, [(i, i ^ dist) for i in range(size)])]
    ppermute x3 -> x27, starting transfers between devices: 3.51 us -> 30.7 us  [move(): return lax.ppermute(x, axis, [(i, i ^ dist) for i in range(size)])]
    all_to_all x4 -> x1, starting transfers between devices: 21.1 us -> 7.26 us  [local(): lax.all_to_all(packed, 'seq', 0, 0, tiled=True)]
    psum x1 -> x0, blocking collectives: 5.67 us -> none  [local(): lax.psum(jnp.stack((jnp.sum(apply_out * apply_out, axis=1), jnp.sum(apply...]
    all_to_all x4 -> x1, waiting for transfers between devices: 4.87 us -> 0.01 us  [local(): lax.all_to_all(packed, 'seq', 0, 0, tiled=True)]
    pallas_call x1 -> x0, Pallas kernels: 4.68 us -> none  [local(): pl.pallas_call(functools.partial(backward_kernel, slab, group), out_shape...]
    unnamed x24 -> x10, local copies, waits for them, and re-layouts: 4.81 us -> 1.57 us
  transfers between devices with their start and end apart: 7 -> 28, of which waited for: 4 -> 17; matrix products, arithmetic and copies ran while one was open for 0% -> 0% of each run, Pallas kernels for 1% -> 3%
where the time goes in v2:
time: 94.6 us; the launch traced here: 94.2 us
  waiting for transfers between devices  43 us (45%)
  starting transfers between devices  38 us (40%)
  Pallas kernels  10.8 us (11%)
  local copies, waits for them, and re-layouts  1.57 us (2%)
    ppermute x27, waiting for transfers between devices, move(): return lax.ppermute(x, axis, [(i, i ^ dist) for i in range(size)])  43 us
    ppermute x27, starting transfers between devices, move(): return lax.ppermute(x, axis, [(i, i ^ dist) for i in range(size)])  30.7 us
    all_to_all x1, starting transfers between devices, local(): lax.all_to_all(packed, 'seq', 0, 0, tiled=True)  7.26 us
    pallas_call x6, Pallas kernels, call(): pl.pallas_call(kernel, out_shape=outs, in_specs=[SMEM] * smem + [VMEM] *...  7.1 us
    pallas_call x2, Pallas kernels, copying_call(): pl.pallas_call(kernel, out_shape=outs, in_specs=[pl.BlockSpec(memory_spac...  3.7 us
  transfers between devices with their start and end apart: 28, of which 17 were waited for; matrix products, arithmetic and copies ran while one was open for 0% of the time, Pallas kernels for 3%

profile of v2, /device:TPU:0, one launch (start us, length us, event | category | flops | bytes accessed | tf_op | source)
XLA Modules:
  0.0 94.2 jit_solution(10983620158625725952)
XLA Ops:
  0.6 1.9 %shard_map.163 = bf16[8,32,1152]{2,1,0:T(8,128)(2,1)} custom-call(bf16[1,32,768]{2,1,0:T(8,128)(2,1)} %refs_0_.2, bf16[1,32,768]{2,1,0:T(8,128)(2,1)} %refs_1_.2, bf16[1,32,768]{2,1,0:T(8,128)(2,1)} %refs_2_.2, bf16[1,32,768]{2,1,0:T(8,128)(2,1)} %refs_3_.2, bf16[1,32,768]{2,1,0:T(8,128)(2,1)} %refs_4_.2, bf16[1,32,768]{2,1,0:T(8,128)(2,1)} %refs_5_.2), custom_call_target="tpu_custom_call" | custom-call | tf_op jit(solution)/shard_map/pallas_call | solution.py:60
  2.5 7.3 %all-to-all-start = ((bf16[8,32,1152]{2,1,0:T(8,128)(2,1)}), bf16[8,32,1152]{2,1,0:T(8,128)(2,1)S(1)}, u32[]{:S(2)}, u32[]{:S(2)}) async-start(bf16[8,32,1152]{2,1,0:T(8,128)(2,1)} %shard_map.163), calls=%async_computation | async-start | bytes 1179648 | tf_op jit(solution)/shard_map/all_to_all | solution.py:302
  9.8 1.8 %shard_map.164 = (bf16[128,768]{1,0:T(8,128)(2,1)}, f32[128,256]{1,0:T(8,128)}) custom-call(bf16[1,128,256]{2,1,0:T(8,128)(2,1)} %refs_0_.3, bf16[1,128,256]{2,1,0:T(8,128)(2,1)} %refs_1_.3, bf16[1,128,256]{2,1,0:T(8,128)(2,1)} %refs_2_.3, bf16[1,128,256]{2,1,0:T(8,128)(2,1)} %refs_3_.3, f32[1,128]{1,0:T(1,128)} %rates.1, f32[1,256]{1,0:T(1,128)} %refs_5_.3), custom_call_target="tpu_custom_call" | custom-call | tf_op jit(solution)/shard_map/pallas_call | solution.py:60
  11.6 3.0 %collective-permute-start.2 = (bf16[128,768]{1,0:T(8,128)(2,1)}, bf16[128,768]{1,0:T(8,128)(2,1)S(1)}, u32[]{:S(2)}, u32[]{:S(2)}) collective-permute-start(bf16[128,768]{1,0:T(8,128)(2,1)} %get-tuple-element.32.refs_0_), channel_id=1, source_target_pairs={{0,3},{1,2},{2,1},{3,0},{4,7},{5,6},{6,5},{7,4},{8,11},{9,10},{10,... | collective-permute-start | bytes 589832 | tf_op jit(solution)/shard_map/ppermute | solution.py:271
  14.6 0.6 collective-permute-start.1
  15.2 0.1 collective-permute-start
  15.2 2.8 %collective-permute-start.3 = (bf16[128,256]{1,0:T(8,128)(2,1)S(1)}, bf16[128,256]{1,0:T(8,128)(2,1)S(1)}, u32[]{:S(2)}, u32[]{:S(2)}) collective-permute-start(bf16[128,256]{1,0:T(8,128)(2,1)S(1)} %bitcast.7), channel_id=1, source_target_pairs={{0,4},{1,5},{2,6},{3,7},{4,0},{5,1},{6,2},{7,3},{8,12},{9,13},{10,... | collective-permute-start | bytes 196616 | tf_op jit(solution)/shard_map/ppermute | solution.py:271
  18.1 11.6 %collective-permute-done.3.refs_4_ = bf16[128,256]{1,0:T(8,128)(2,1)S(1)} collective-permute-done((bf16[128,256]{1,0:T(8,128)(2,1)S(1)}, bf16[128,256]{1,0:T(8,128)(2,1)S(1)}, u32[]{:S(2)}, u32[]{:S(2)}) %collective-permute-start.3) | collective-permute-done | bytes 65568 | tf_op jit(solution)/shard_map/ppermute | solution.py:271
  29.7 0.0 collective-permute-done.2.refs_3_
  29.7 1.8 %collective-permute-done.1.refs_2_ = bf16[128,768]{1,0:T(8,128)(2,1)S(1)} collective-permute-done((bf16[128,768]{1,0:T(8,128)(2,1)}, bf16[128,768]{1,0:T(8,128)(2,1)S(1)}, u32[]{:S(2)}, u32[]{:S(2)}) %collective-permute-start.1) | collective-permute-done | bytes 196640 | tf_op jit(solution)/shard_map/ppermute | solution.py:271
  31.5 0.0 collective-permute-done.refs_1_
  31.5 0.0 all-to-all-done
  31.5 0.9 copy-done.1
  32.4 0.8 shard_map.165
  33.2 1.6 %collective-permute-start.4 = (bf16[128,512]{1,0:T(8,128)(2,1)S(1)}, bf16[128,512]{1,0:T(8,128)(2,1)S(1)}, u32[]{:S(2)}, u32[]{:S(2)}) collective-permute-start(bf16[128,512]{1,0:T(8,128)(2,1)S(1)} %get-tuple-element.34), channel_id=1, source_target_pairs={{0,1},{1,0},{2,3},{3,2},{4,5},{5,4},{6,7},{7,6},{8,9},{9,8},{10,11... | collective-permute-start | bytes 393224 | tf_op jit(solution)/shard_map/ppermute | solution.py:271
  34.8 2.4 %collective-permute-start.5 = (bf16[128,512]{1,0:T(8,128)(2,1)S(1)}, bf16[128,512]{1,0:T(8,128)(2,1)S(1)}, u32[]{:S(2)}, u32[]{:S(2)}) collective-permute-start(bf16[128,512]{1,0:T(8,128)(2,1)S(1)} %get-tuple-element.35), channel_id=1, source_target_pairs={{0,2},{1,3},{2,0},{3,1},{4,6},{5,7},{6,4},{7,5},{8,10},{9,11},{10,... | collective-permute-start | bytes 393224 | tf_op jit(solution)/shard_map/ppermute | solution.py:271
  37.2 0.0 collective-permute-start.6
  37.2 1.5 %collective-permute-done.4.refs_1_.refs_5_ = bf16[128,512]{1,0:T(8,128)(2,1)S(1)} collective-permute-done((bf16[128,512]{1,0:T(8,128)(2,1)S(1)}, bf16[128,512]{1,0:T(8,128)(2,1)S(1)}, u32[]{:S(2)}, u32[]{:S(2)}) %collective-permute-start.4) | collective-permute-done | bytes 131104 | tf_op jit(solution)/shard_map/ppermute | solution.py:271
  38.7 1.7 %collective-permute-done.5.refs_2_.refs_6_ = bf16[128,512]{1,0:T(8,128)(2,1)S(1)} collective-permute-done((bf16[128,512]{1,0:T(8,128)(2,1)S(1)}, bf16[128,512]{1,0:T(8,128)(2,1)S(1)}, u32[]{:S(2)}, u32[]{:S(2)}) %collective-permute-start.5) | collective-permute-done | bytes 131104 | tf_op jit(solution)/shard_map/ppermute | solution.py:271
  40.4 2.6 %collective-permute-done.6.refs_3_.refs_7_ = bf16[128,512]{1,0:T(8,128)(2,1)S(1)} collective-permute-done((bf16[128,512]{1,0:T(8,128)(2,1)S(1)}, bf16[128,512]{1,0:T(8,128)(2,1)S(1)}, u32[]{:S(2)}, u32[]{:S(2)}) %collective-permute-start.6) | collective-permute-done | bytes 131104 | tf_op jit(solution)/shard_map/ppermute | solution.py:271
  43.0 0.1 shard_map.166
  43.2 0.1 collective-permute-start.9
  43.3 1.6 %collective-permute-start.8 = (f32[2,128]{1,0:T(2,128)S(1)}, f32[2,128]{1,0:T(2,128)S(1)}, u32[]{:S(2)}, u32[]{:S(2)}) collective-permute-start(f32[2,128]{1,0:T(2,128)S(1)} %get-tuple-element.39.refs_0_), channel_id=1, source_target_pairs={{0,16},{8,24},{16,0},{24,8},{1,17},{9,25},{17,1},{25,9},{2,18},{10... | collective-permute-start | bytes 3080 | tf_op jit(solution)/shard_map/ppermute | solution.py:271
  44.9 0.3 collective-permute-start.7
  45.1 1.1 %collective-permute-done.9.refs_3_ = f32[2,128]{1,0:T(2,128)S(1)} collective-permute-done((f32[2,128]{1,0:T(2,128)S(1)}, f32[2,128]{1,0:T(2,128)S(1)}, u32[]{:S(2)}, u32[]{:S(2)}) %collective-permute-start.9) | collective-permute-done | bytes 1056 | tf_op jit(solution)/shard_map/ppermute | solution.py:271
  46.3 0.7 collective-permute-done.8.refs_2_
  46.9 0.0 collective-permute-done.7.refs_1_
  46.9 0.1 shard_map.167.refs_8_
  47.1 1.0 %collective-permute-start.13 = (bf16[128,256]{1,0:T(8,128)(2,1)S(1)}, bf16[128,256]{1,0:T(8,128)(2,1)S(1)}, u32[]{:S(2)}, u32[]{:S(2)}) collective-permute-start(bf16[128,256]{1,0:T(8,128)(2,1)S(1)} %shard_map.167.refs_8_), channel_id=1, source_target_pairs={{0,4},{1,5},{2,6},{3,7},{4,0},{5,1},{6,2},{7,3},{8,12},{9,13},{10,... | collective-permute-start | bytes 196616 | tf_op jit(solution)/shard_map/ppermute | solution.py:271
  48.0 1.7 %collective-permute-start.12 = (bf16[128,256]{1,0:T(8,128)(2,1)S(1)}, bf16[128,256]{1,0:T(8,128)(2,1)S(1)}, u32[]{:S(2)}, u32[]{:S(2)}) collective-permute-start(bf16[128,256]{1,0:T(8,128)(2,1)S(1)} %shard_map.167.refs_8_), channel_id=1, source_target_pairs={{0,3},{1,2},{2,1},{3,0},{4,7},{5,6},{6,5},{7,4},{8,11},{9,10},{10,... | collective-permute-start | bytes 196616 | tf_op jit(solution)/shard_map/ppermute | solution.py:271
  49.7 0.4 collective-permute-start.11
  50.1 1.4 %collective-permute-start.10 = (bf16[128,256]{1,0:T(8,128)(2,1)S(1)}, bf16[128,256]{1,0:T(8,128)(2,1)S(1)}, u32[]{:S(2)}, u32[]{:S(2)}) collective-permute-start(bf16[128,256]{1,0:T(8,128)(2,1)S(1)} %shard_map.167.refs_8_), channel_id=1, source_target_pairs={{0,1},{1,0},{2,3},{3,2},{4,5},{5,4},{6,7},{7,6},{8,9},{9,8},{10,11... | collective-permute-start | bytes 196616 | tf_op jit(solution)/shard_map/ppermute | solution.py:271
  51.5 2.4 %collective-permute-done.13.refs_12_ = bf16[128,256]{1,0:T(8,128)(2,1)S(1)} collective-permute-done((bf16[128,256]{1,0:T(8,128)(2,1)S(1)}, bf16[128,256]{1,0:T(8,128)(2,1)S(1)}, u32[]{:S(2)}, u32[]{:S(2)}) %collective-permute-start.13) | collective-permute-done | bytes 65568 | tf_op jit(solution)/shard_map/ppermute | solution.py:271
  53.9 0.2 collective-permute-start.16
  54.2 1.8 %collective-permute-start.15 = (bf16[128,256]{1,0:T(8,128)(2,1)S(1)}, bf16[128,256]{1,0:T(8,128)(2,1)S(1)}, u32[]{:S(2)}, u32[]{:S(2)}) collective-permute-start(bf16[128,256]{1,0:T(8,128)(2,1)S(1)} %collective-permute-done.13.refs_12_), channel_id=1, source_target_pairs={{0,2},{1,3},{2,0},{3,1},{4,6},{5,7},{6,4},{7,5},{8,10},{9,11},{10,... | collective-permute-start | bytes 196616 | tf_op jit(solution)/shard_map/ppermute | solution.py:271
  56.0 0.0 collective-permute-done.12.refs_11_
  56.0 1.4 %collective-permute-start.14 = (bf16[128,256]{1,0:T(8,128)(2,1)S(1)}, bf16[128,256]{1,0:T(8,128)(2,1)S(1)}, u32[]{:S(2)}, u32[]{:S(2)}) collective-permute-start(bf16[128,256]{1,0:T(8,128)(2,1)S(1)} %collective-permute-done.13.refs_12_), channel_id=1, source_target_pairs={{0,1},{1,0},{2,3},{3,2},{4,5},{5,4},{6,7},{7,6},{8,9},{9,8},{10,11... | collective-permute-start | bytes 196616 | tf_op jit(solution)/shard_map/ppermute | solution.py:271
  57.4 0.1 pad_add_fusion.place
  57.5 0.0 collective-permute-done.11.refs_10_
  57.5 2.0 %collective-permute-done.16.refs_15_ = bf16[128,256]{1,0:T(8,128)(2,1)S(1)} collective-permute-done((bf16[128,256]{1,0:T(8,128)(2,1)S(1)}, bf16[128,256]{1,0:T(8,128)(2,1)S(1)}, u32[]{:S(2)}, u32[]{:S(2)}) %collective-permute-start.16) | collective-permute-done | bytes 65568 | tf_op jit(solution)/shard_map/ppermute | solution.py:271
  59.5 0.0 collective-permute-done.15.refs_14_
  59.5 0.7 collective-permute-done.14.refs_13_
  60.3 3.9 %shard_map.168 = (bf16[128,768]{1,0:T(8,128)(2,1)S(1)}, bf16[128,768]{1,0:T(8,128)(2,1)S(1)}, bf16[128,768]{1,0:T(8,128)(2,1)S(1)}, bf16[128,768]{1,0:T(8,128)(2...) custom-call(s32[3]{0:T(128)S(1)} %pad_add_fusion.place, ...), custom_call_target="tpu_custom_call" | custom-call | flops 1660944384 | bytes 3506188 | tf_op jit(solution)/shard_map/pallas_call | solution.py:48
  64.2 1.5 %collective-permute-start.17 = (bf16[128,768]{1,0:T(8,128)(2,1)S(1)}, bf16[128,768]{1,0:T(8,128)(2,1)S(1)}, u32[]{:S(2)}, u32[]{:S(2)}) collective-permute-start(bf16[128,768]{1,0:T(8,128)(2,1)S(1)} %get-tuple-element.41), channel_id=1, source_target_pairs={{0,1},{1,0},{2,3},{3,2},{4,5},{5,4},{6,7},{7,6},{8,9},{9,8},{10,11... | collective-permute-start | bytes 589832 | tf_op jit(solution)/shard_map/ppermute | solution.py:271
  65.7 0.0 collective-permute-start.18
  65.7 2.1 %collective-permute-start.19 = (bf16[128,768]{1,0:T(8,128)(2,1)S(1)}, bf16[128,768]{1,0:T(8,128)(2,1)S(1)}, u32[]{:S(2)}, u32[]{:S(2)}) collective-permute-start(bf16[128,768]{1,0:T(8,128)(2,1)S(1)} %get-tuple-element.43), channel_id=1, source_target_pairs={{0,3},{1,2},{2,1},{3,0},{4,7},{5,6},{6,5},{7,4},{8,11},{9,10},{10,... | collective-permute-start | bytes 589832 | tf_op jit(solution)/shard_map/ppermute | solution.py:271
  67.8 1.4 %collective-permute-start.20 = (bf16[32,576]{1,0:T(8,128)(2,1)S(1)}, bf16[32,576]{1,0:T(8,128)(2,1)S(1)}, u32[]{:S(2)}, u32[]{:S(2)}) collective-permute-start(bf16[32,576]{1,0:T(8,128)(2,1)S(1)} %get-tuple-element.48), channel_id=1, source_target_pairs={{0,1},{1,0},{2,3},{3,2},{4,5},{5,4},{6,7},{7,6},{8,9},{9,8},{10,11... | collective-permute-start | bytes 110600 | tf_op jit(solution)/shard_map/ppermute | solution.py:271
  69.2 0.0 collective-permute-start.21
  69.2 3.8 %collective-permute-done.20.refs_1_ = bf16[32,576]{1,0:T(8,128)(2,1)S(1)} collective-permute-done((bf16[32,576]{1,0:T(8,128)(2,1)S(1)}, bf16[32,576]{1,0:T(8,128)(2,1)S(1)}, u32[]{:S(2)}, u32[]{:S(2)}) %collective-permute-start.20) | collective-permute-done | bytes 36896 | tf_op jit(solution)/shard_map/ppermute | solution.py:271
  73.0 0.6 collective-permute-start.22
  73.6 3.0 %collective-permute-done.21.refs_2_ = bf16[32,576]{1,0:T(8,128)(2,1)S(1)} collective-permute-done((bf16[32,576]{1,0:T(8,128)(2,1)S(1)}, bf16[32,576]{1,0:T(8,128)(2,1)S(1)}, u32[]{:S(2)}, u32[]{:S(2)}) %collective-permute-start.21) | collective-permute-done | bytes 36896 | tf_op jit(solution)/shard_map/ppermute | solution.py:271
  76.6 0.1 collective-permute-start.23
  76.6 1.4 %collective-permute-done.22.refs_3_ = bf16[32,576]{1,0:T(8,128)(2,1)S(1)} collective-permute-done((bf16[32,576]{1,0:T(8,128)(2,1)S(1)}, bf16[32,576]{1,0:T(8,128)(2,1)S(1)}, u32[]{:S(2)}, u32[]{:S(2)}) %collective-permute-start.22) | collective-permute-done | bytes 36896 | tf_op jit(solution)/shard_map/ppermute | solution.py:271
  78.1 1.8 %collective-permute-start.24 = (bf16[32,576]{1,0:T(8,128)(2,1)S(1)}, bf16[32,576]{1,0:T(8,128)(2,1)S(1)}, u32[]{:S(2)}, u32[]{:S(2)}) collective-permute-start(bf16[32,576]{1,0:T(8,128)(2,1)S(1)} %get-tuple-element.52), channel_id=1, source_target_pairs={{0,5},{1,4},{2,7},{3,6},{4,1},{5,0},{6,3},{7,2},{8,13},{9,12},{10,... | collective-permute-start | bytes 110600 | tf_op jit(solution)/shard_map/ppermute | solution.py:271
  79.8 1.8 %collective-permute-done.23.refs_4_ = bf16[32,576]{1,0:T(8,128)(2,1)S(1)} collective-permute-done((bf16[32,576]{1,0:T(8,128)(2,1)S(1)}, bf16[32,576]{1,0:T(8,128)(2,1)S(1)}, u32[]{:S(2)}, u32[]{:S(2)}) %collective-permute-start.23) | collective-permute-done | bytes 36896 | tf_op jit(solution)/shard_map/ppermute | solution.py:271
  81.6 1.5 %collective-permute-start.25 = (bf16[32,576]{1,0:T(8,128)(2,1)S(1)}, bf16[32,576]{1,0:T(8,128)(2,1)S(1)}, u32[]{:S(2)}, u32[]{:S(2)}) collective-permute-start(bf16[32,576]{1,0:T(8,128)(2,1)S(1)} %get-tuple-element.53), channel_id=1, source_target_pairs={{0,6},{1,7},{2,4},{3,5},{4,2},{5,3},{6,0},{7,1},{8,14},{9,15},{10,... | collective-permute-start | bytes 110600 | tf_op jit(solution)/shard_map/ppermute | solution.py:271
  83.1 1.6 %collective-permute-done.24.refs_5_ = bf16[32,576]{1,0:T(8,128)(2,1)S(1)} collective-permute-done((bf16[32,576]{1,0:T(8,128)(2,1)S(1)}, bf16[32,576]{1,0:T(8,128)(2,1)S(1)}, u32[]{:S(2)}, u32[]{:S(2)}) %collective-permute-start.24) | collective-permute-done | bytes 36896 | tf_op jit(solution)/shard_map/ppermute | solution.py:271
  84.7 1.5 %collective-permute-start.26 = (bf16[32,576]{1,0:T(8,128)(2,1)S(1)}, bf16[32,576]{1,0:T(8,128)(2,1)S(1)}, u32[]{:S(2)}, u32[]{:S(2)}) collective-permute-start(bf16[32,576]{1,0:T(8,128)(2,1)S(1)} %get-tuple-element.54), channel_id=1, source_target_pairs={{0,7},{1,6},{2,5},{3,4},{4,3},{5,2},{6,1},{7,0},{8,15},{9,14},{10,... | collective-permute-start | bytes 110600 | tf_op jit(solution)/shard_map/ppermute | solution.py:271
  86.2 1.2 %collective-permute-done.25.refs_6_ = bf16[32,576]{1,0:T(8,128)(2,1)S(1)} collective-permute-done((bf16[32,576]{1,0:T(8,128)(2,1)S(1)}, bf16[32,576]{1,0:T(8,128)(2,1)S(1)}, u32[]{:S(2)}, u32[]{:S(2)}) %collective-permute-start.25) | collective-permute-done | bytes 36896 | tf_op jit(solution)/shard_map/ppermute | solution.py:271
  87.4 4.0 %collective-permute-done.26.refs_7_ = bf16[32,576]{1,0:T(8,128)(2,1)S(1)} collective-permute-done((bf16[32,576]{1,0:T(8,128)(2,1)S(1)}, bf16[32,576]{1,0:T(8,128)(2,1)S(1)}, u32[]{:S(2)}, u32[]{:S(2)}) %collective-permute-start.26) | collective-permute-done | bytes 36896 | tf_op jit(solution)/shard_map/ppermute | solution.py:271
  91.4 1.4 %shard_map.170 = (f32[1,32,768]{2,1,0:T(8,128)}, f32[1,32,768]{2,1,0:T(8,128)}, f32[1,32,768]{2,1,0:T(8,128)}) custom-call(s32[3]{0:T(128)S(1)} %pad_add_fusion.place, bf16[32,576]{1,0:T(8,128)(2,1)S(1)} %get-tuple-element.47.refs_0_, bf16[32,576]{1,0:T(8,128)(2,1)S(1)} %collective-permute-done.20.refs_1_, ...), custom_call_target="tpu_custom_call" | custom-call | bytes 589836 | tf_op jit(solution)/shard_map/pallas_call | solution.py:48
  92.8 0.0 collective-permute-done.19.refs_3_
  92.8 0.6 copy-done.3
  93.5 0.8 shard_map.169
  (11 shorter events, 0.0 us)
Async XLA Ops:
  2.5 28.9 %all-to-all-start = ((bf16[8,32,1152]{2,1,0:T(8,128)(2,1)}), bf16[8,32,1152]{2,1,0:T(8,128)(2,1)S(1)}, u32[]{:S(2)}, u32[]{:S(2)}) async-start(bf16[8,32,1152]{2,1,0:T(8,128)(2,1)} %shard_map.163), calls=%async_computation | async-start | bytes 1179648 | tf_op jit(solution)/shard_map/all_to_all | solution.py:302
  9.8 5.4 %copy-start.4 = (bf16[1,128,256]{2,1,0:T(8,128)(2,1)S(1)}, bf16[1,128,256]{2,1,0:T(8,128)(2,1)}, u32[]{:S(2)}) copy-start(bf16[1,128,256]{2,1,0:T(8,128)(2,1)} %refs_0_.3) | copy-start | bytes 196612
  11.6 18.1 %collective-permute-start.2 = (bf16[128,768]{1,0:T(8,128)(2,1)}, bf16[128,768]{1,0:T(8,128)(2,1)S(1)}, u32[]{:S(2)}, u32[]{:S(2)}) collective-permute-start(bf16[128,768]{1,0:T(8,128)(2,1)} %get-tuple-element.32.refs_0_), channel_id=1, source_target_pairs={{0,3},{1,2},{2,1},{3,0},{4,7},{5,6},{6,5},{7,4},{8,11},{9,10},{10,... | collective-permute-start | bytes 589832 | tf_op jit(solution)/shard_map/ppermute | solution.py:271
  14.6 16.9 %collective-permute-start.1 = (bf16[128,768]{1,0:T(8,128)(2,1)}, bf16[128,768]{1,0:T(8,128)(2,1)S(1)}, u32[]{:S(2)}, u32[]{:S(2)}) collective-permute-start(bf16[128,768]{1,0:T(8,128)(2,1)} %get-tuple-element.32.refs_0_), channel_id=1, source_target_pairs={{0,2},{1,3},{2,0},{3,1},{4,6},{5,7},{6,4},{7,5},{8,10},{9,11},{10,... | collective-permute-start | bytes 589832 | tf_op jit(solution)/shard_map/ppermute | solution.py:271
  15.2 16.3 %collective-permute-start = (bf16[128,768]{1,0:T(8,128)(2,1)}, bf16[128,768]{1,0:T(8,128)(2,1)S(1)}, u32[]{:S(2)}, u32[]{:S(2)}) collective-permute-start(bf16[128,768]{1,0:T(8,128)(2,1)} %get-tuple-element.32.refs_0_), channel_id=1, source_target_pairs={{0,1},{1,0},{2,3},{3,2},{4,5},{5,4},{6,7},{7,6},{8,9},{9,8},{10,11... | collective-permute-start | bytes 589832 | tf_op jit(solution)/shard_map/ppermute | solution.py:271
  15.2 14.5 %collective-permute-start.3 = (bf16[128,256]{1,0:T(8,128)(2,1)S(1)}, bf16[128,256]{1,0:T(8,128)(2,1)S(1)}, u32[]{:S(2)}, u32[]{:S(2)}) collective-permute-start(bf16[128,256]{1,0:T(8,128)(2,1)S(1)} %bitcast.7), channel_id=1, source_target_pairs={{0,4},{1,5},{2,6},{3,7},{4,0},{5,1},{6,2},{7,3},{8,12},{9,13},{10,... | collective-permute-start | bytes 196616 | tf_op jit(solution)/shard_map/ppermute | solution.py:271
  31.5 0.9 copy-start.1
  32.4 10.6 %copy-start = (f32[128,256]{1,0:T(8,128)S(1)}, f32[128,256]{1,0:T(8,128)}, u32[]{:S(2)}) copy-start(f32[128,256]{1,0:T(8,128)} %get-tuple-element.37.gg) | copy-start | bytes 393220
  33.2 5.5 %collective-permute-start.4 = (bf16[128,512]{1,0:T(8,128)(2,1)S(1)}, bf16[128,512]{1,0:T(8,128)(2,1)S(1)}, u32[]{:S(2)}, u32[]{:S(2)}) collective-permute-start(bf16[128,512]{1,0:T(8,128)(2,1)S(1)} %get-tuple-element.34), channel_id=1, source_target_pairs={{0,1},{1,0},{2,3},{3,2},{4,5},{5,4},{6,7},{7,6},{8,9},{9,8},{10,11... | collective-permute-start | bytes 393224 | tf_op jit(solution)/shard_map/ppermute | solution.py:271
  34.8 5.7 %collective-permute-start.5 = (bf16[128,512]{1,0:T(8,128)(2,1)S(1)}, bf16[128,512]{1,0:T(8,128)(2,1)S(1)}, u32[]{:S(2)}, u32[]{:S(2)}) collective-permute-start(bf16[128,512]{1,0:T(8,128)(2,1)S(1)} %get-tuple-element.35), channel_id=1, source_target_pairs={{0,2},{1,3},{2,0},{3,1},{4,6},{5,7},{6,4},{7,5},{8,10},{9,11},{10,... | collective-permute-start | bytes 393224 | tf_op jit(solution)/shard_map/ppermute | solution.py:271
  37.2 5.9 %collective-permute-start.6 = (bf16[128,512]{1,0:T(8,128)(2,1)S(1)}, bf16[128,512]{1,0:T(8,128)(2,1)S(1)}, u32[]{:S(2)}, u32[]{:S(2)}) collective-permute-start(bf16[128,512]{1,0:T(8,128)(2,1)S(1)} %get-tuple-element.36), channel_id=1, source_target_pairs={{0,3},{1,2},{2,1},{3,0},{4,7},{5,6},{6,5},{7,4},{8,11},{9,10},{10,... | collective-permute-start | bytes 393224 | tf_op jit(solution)/shard_map/ppermute | solution.py:271
  43.2 17.1 %copy-start.2 = (bf16[128,768]{1,0:T(8,128)(2,1)S(1)}, bf16[128,768]{1,0:T(8,128)(2,1)}, u32[]{:S(2)}) copy-start(bf16[128,768]{1,0:T(8,128)(2,1)} %get-tuple-element.32.refs_0_) | copy-start | bytes 589828
  43.2 3.1 %collective-permute-start.9 = (f32[2,128]{1,0:T(2,128)S(1)}, f32[2,128]{1,0:T(2,128)S(1)}, u32[]{:S(2)}, u32[]{:S(2)}) collective-permute-start(f32[2,128]{1,0:T(2,128)S(1)} %get-tuple-element.39.refs_0_), channel_id=1, source_target_pairs={{0,24},{8,16},{16,8},{24,0},{1,25},{9,17},{17,9},{25,1},{2,26},{10... | collective-permute-start | bytes 3080 | tf_op jit(solution)/shard_map/ppermute | solution.py:271
  43.3 3.6 %collective-permute-start.8 = (f32[2,128]{1,0:T(2,128)S(1)}, f32[2,128]{1,0:T(2,128)S(1)}, u32[]{:S(2)}, u32[]{:S(2)}) collective-permute-start(f32[2,128]{1,0:T(2,128)S(1)} %get-tuple-element.39.refs_0_), channel_id=1, source_target_pairs={{0,16},{8,24},{16,0},{24,8},{1,17},{9,25},{17,1},{25,9},{2,18},{10... | collective-permute-start | bytes 3080 | tf_op jit(solution)/shard_map/ppermute | solution.py:271
  44.9 2.1 %collective-permute-start.7 = (f32[2,128]{1,0:T(2,128)S(1)}, f32[2,128]{1,0:T(2,128)S(1)}, u32[]{:S(2)}, u32[]{:S(2)}) collective-permute-start(f32[2,128]{1,0:T(2,128)S(1)} %get-tuple-element.39.refs_0_), channel_id=1, source_target_pairs={{0,8},{8,0},{16,24},{24,16},{1,9},{9,1},{17,25},{25,17},{2,10},{10... | collective-permute-start | bytes 3080 | tf_op jit(solution)/shard_map/ppermute | solution.py:271
  47.1 6.8 %collective-permute-start.13 = (bf16[128,256]{1,0:T(8,128)(2,1)S(1)}, bf16[128,256]{1,0:T(8,128)(2,1)S(1)}, u32[]{:S(2)}, u32[]{:S(2)}) collective-permute-start(bf16[128,256]{1,0:T(8,128)(2,1)S(1)} %shard_map.167.refs_8_), channel_id=1, source_target_pairs={{0,4},{1,5},{2,6},{3,7},{4,0},{5,1},{6,2},{7,3},{8,12},{9,13},{10,... | collective-permute-start | bytes 196616 | tf_op jit(solution)/shard_map/ppermute | solution.py:271
  48.0 8.0 %collective-permute-start.12 = (bf16[128,256]{1,0:T(8,128)(2,1)S(1)}, bf16[128,256]{1,0:T(8,128)(2,1)S(1)}, u32[]{:S(2)}, u32[]{:S(2)}) collective-permute-start(bf16[128,256]{1,0:T(8,128)(2,1)S(1)} %shard_map.167.refs_8_), channel_id=1, source_target_pairs={{0,3},{1,2},{2,1},{3,0},{4,7},{5,6},{6,5},{7,4},{8,11},{9,10},{10,... | collective-permute-start | bytes 196616 | tf_op jit(solution)/shard_map/ppermute | solution.py:271
  49.7 7.8 %collective-permute-start.11 = (bf16[128,256]{1,0:T(8,128)(2,1)S(1)}, bf16[128,256]{1,0:T(8,128)(2,1)S(1)}, u32[]{:S(2)}, u32[]{:S(2)}) collective-permute-start(bf16[128,256]{1,0:T(8,128)(2,1)S(1)} %shard_map.167.refs_8_), channel_id=1, source_target_pairs={{0,2},{1,3},{2,0},{3,1},{4,6},{5,7},{6,4},{7,5},{8,10},{9,11},{10,... | collective-permute-start | bytes 196616 | tf_op jit(solution)/shard_map/ppermute | solution.py:271
  50.1 7.4 %collective-permute-start.10 = (bf16[128,256]{1,0:T(8,128)(2,1)S(1)}, bf16[128,256]{1,0:T(8,128)(2,1)S(1)}, u32[]{:S(2)}, u32[]{:S(2)}) collective-permute-start(bf16[128,256]{1,0:T(8,128)(2,1)S(1)} %shard_map.167.refs_8_), channel_id=1, source_target_pairs={{0,1},{1,0},{2,3},{3,2},{4,5},{5,4},{6,7},{7,6},{8,9},{9,8},{10,11... | collective-permute-start | bytes 196616 | tf_op jit(solution)/shard_map/ppermute | solution.py:271
  53.9 5.6 %collective-permute-start.16 = (bf16[128,256]{1,0:T(8,128)(2,1)S(1)}, bf16[128,256]{1,0:T(8,128)(2,1)S(1)}, u32[]{:S(2)}, u32[]{:S(2)}) collective-permute-start(bf16[128,256]{1,0:T(8,128)(2,1)S(1)} %collective-permute-done.13.refs_12_), channel_id=1, source_target_pairs={{0,3},{1,2},{2,1},{3,0},{4,7},{5,6},{6,5},{7,4},{8,11},{9,10},{10,... | collective-permute-start | bytes 196616 | tf_op jit(solution)/shard_map/ppermute | solution.py:271
  54.2 5.4 %collective-permute-start.15 = (bf16[128,256]{1,0:T(8,128)(2,1)S(1)}, bf16[128,256]{1,0:T(8,128)(2,1)S(1)}, u32[]{:S(2)}, u32[]{:S(2)}) collective-permute-start(bf16[128,256]{1,0:T(8,128)(2,1)S(1)} %collective-permute-done.13.refs_12_), channel_id=1, source_target_pairs={{0,2},{1,3},{2,0},{3,1},{4,6},{5,7},{6,4},{7,5},{8,10},{9,11},{10,... | collective-permute-start | bytes 196616 | tf_op jit(solution)/shard_map/ppermute | solution.py:271
  56.0 4.3 %collective-permute-start.14 = (bf16[128,256]{1,0:T(8,128)(2,1)S(1)}, bf16[128,256]{1,0:T(8,128)(2,1)S(1)}, u32[]{:S(2)}, u32[]{:S(2)}) collective-permute-start(bf16[128,256]{1,0:T(8,128)(2,1)S(1)} %collective-permute-done.13.refs_12_), channel_id=1, source_target_pairs={{0,1},{1,0},{2,3},{3,2},{4,5},{5,4},{6,7},{7,6},{8,9},{9,8},{10,11... | collective-permute-start | bytes 196616 | tf_op jit(solution)/shard_map/ppermute | solution.py:271
  64.2 28.6 %collective-permute-start.17 = (bf16[128,768]{1,0:T(8,128)(2,1)S(1)}, bf16[128,768]{1,0:T(8,128)(2,1)S(1)}, u32[]{:S(2)}, u32[]{:S(2)}) collective-permute-start(bf16[128,768]{1,0:T(8,128)(2,1)S(1)} %get-tuple-element.41), channel_id=1, source_target_pairs={{0,1},{1,0},{2,3},{3,2},{4,5},{5,4},{6,7},{7,6},{8,9},{9,8},{10,11... | collective-permute-start | bytes 589832 | tf_op jit(solution)/shard_map/ppermute | solution.py:271
  65.7 27.1 %collective-permute-start.18 = (bf16[128,768]{1,0:T(8,128)(2,1)S(1)}, bf16[128,768]{1,0:T(8,128)(2,1)S(1)}, u32[]{:S(2)}, u32[]{:S(2)}) collective-permute-start(bf16[128,768]{1,0:T(8,128)(2,1)S(1)} %get-tuple-element.42), channel_id=1, source_target_pairs={{0,2},{1,3},{2,0},{3,1},{4,6},{5,7},{6,4},{7,5},{8,10},{9,11},{10,... | collective-permute-start | bytes 589832 | tf_op jit(solution)/shard_map/ppermute | solution.py:271
  65.7 27.1 %collective-permute-start.19 = (bf16[128,768]{1,0:T(8,128)(2,1)S(1)}, bf16[128,768]{1,0:T(8,128)(2,1)S(1)}, u32[]{:S(2)}, u32[]{:S(2)}) collective-permute-start(bf16[128,768]{1,0:T(8,128)(2,1)S(1)} %get-tuple-element.43), channel_id=1, source_target_pairs={{0,3},{1,2},{2,1},{3,0},{4,7},{5,6},{6,5},{7,4},{8,11},{9,10},{10,... | collective-permute-start | bytes 589832 | tf_op jit(solution)/shard_map/ppermute | solution.py:271
  67.8 5.2 %collective-permute-start.20 = (bf16[32,576]{1,0:T(8,128)(2,1)S(1)}, bf16[32,576]{1,0:T(8,128)(2,1)S(1)}, u32[]{:S(2)}, u32[]{:S(2)}) collective-permute-start(bf16[32,576]{1,0:T(8,128)(2,1)S(1)} %get-tuple-element.48), channel_id=1, source_target_pairs={{0,1},{1,0},{2,3},{3,2},{4,5},{5,4},{6,7},{7,6},{8,9},{9,8},{10,11... | collective-permute-start | bytes 110600 | tf_op jit(solution)/shard_map/ppermute | solution.py:271
  69.2 7.4 %collective-permute-start.21 = (bf16[32,576]{1,0:T(8,128)(2,1)S(1)}, bf16[32,576]{1,0:T(8,128)(2,1)S(1)}, u32[]{:S(2)}, u32[]{:S(2)}) collective-permute-start(bf16[32,576]{1,0:T(8,128)(2,1)S(1)} %get-tuple-element.49), channel_id=1, source_target_pairs={{0,2},{1,3},{2,0},{3,1},{4,6},{5,7},{6,4},{7,5},{8,10},{9,11},{10,... | collective-permute-start | bytes 110600 | tf_op jit(solution)/shard_map/ppermute | solution.py:271
  73.0 5.1 %collective-permute-start.22 = (bf16[32,576]{1,0:T(8,128)(2,1)S(1)}, bf16[32,576]{1,0:T(8,128)(2,1)S(1)}, u32[]{:S(2)}, u32[]{:S(2)}) collective-permute-start(bf16[32,576]{1,0:T(8,128)(2,1)S(1)} %get-tuple-element.50), channel_id=1, source_target_pairs={{0,3},{1,2},{2,1},{3,0},{4,7},{5,6},{6,5},{7,4},{8,11},{9,10},{10,... | collective-permute-start | bytes 110600 | tf_op jit(solution)/shard_map/ppermute | solution.py:271
  76.6 5.1 %collective-permute-start.23 = (bf16[32,576]{1,0:T(8,128)(2,1)S(1)}, bf16[32,576]{1,0:T(8,128)(2,1)S(1)}, u32[]{:S(2)}, u32[]{:S(2)}) collective-permute-start(bf16[32,576]{1,0:T(8,128)(2,1)S(1)} %get-tuple-element.51), channel_id=1, source_target_pairs={{0,4},{1,5},{2,6},{3,7},{4,0},{5,1},{6,2},{7,3},{8,12},{9,13},{10,... | collective-permute-start | bytes 110600 | tf_op jit(solution)/shard_map/ppermute | solution.py:271
  78.1 6.6 %collective-permute-start.24 = (bf16[32,576]{1,0:T(8,128)(2,1)S(1)}, bf16[32,576]{1,0:T(8,128)(2,1)S(1)}, u32[]{:S(2)}, u32[]{:S(2)}) collective-permute-start(bf16[32,576]{1,0:T(8,128)(2,1)S(1)} %get-tuple-element.52), channel_id=1, source_target_pairs={{0,5},{1,4},{2,7},{3,6},{4,1},{5,0},{6,3},{7,2},{8,13},{9,12},{10,... | collective-permute-start | bytes 110600 | tf_op jit(solution)/shard_map/ppermute | solution.py:271
  81.6 5.8 %collective-permute-start.25 = (bf16[32,576]{1,0:T(8,128)(2,1)S(1)}, bf16[32,576]{1,0:T(8,128)(2,1)S(1)}, u32[]{:S(2)}, u32[]{:S(2)}) collective-permute-start(bf16[32,576]{1,0:T(8,128)(2,1)S(1)} %get-tuple-element.53), channel_id=1, source_target_pairs={{0,6},{1,7},{2,4},{3,5},{4,2},{5,3},{6,0},{7,1},{8,14},{9,15},{10,... | collective-permute-start | bytes 110600 | tf_op jit(solution)/shard_map/ppermute | solution.py:271
  84.7 6.7 %collective-permute-start.26 = (bf16[32,576]{1,0:T(8,128)(2,1)S(1)}, bf16[32,576]{1,0:T(8,128)(2,1)S(1)}, u32[]{:S(2)}, u32[]{:S(2)}) collective-permute-start(bf16[32,576]{1,0:T(8,128)(2,1)S(1)} %get-tuple-element.54), channel_id=1, source_target_pairs={{0,7},{1,6},{2,5},{3,4},{4,3},{5,2},{6,1},{7,0},{8,15},{9,14},{10,... | collective-permute-start | bytes 110600 | tf_op jit(solution)/shard_map/ppermute | solution.py:271
  92.8 0.7 copy-start.3

commit v3 on v2

--- a/solution.py
+++ b/solution.py
@@ -79,15 +79,13 @@
         copy.wait()
 
 
-def token_pack_kernel(*refs):
-    args, (tok_out, gg_out, qb, kb, vb, ob, rb, gb, sems) = refs[:6], refs[6:]
-    fetch(args, (qb, kb, vb, ob, rb, gb), sems)
+def token_pack_kernel(k, v, og, rates, gains, kv_out, gg_out, rate_out):
     tokens, feat = gg_out.shape
-    rate = jnp.broadcast_to(rb[...], (feat, tokens)).T
-    tok_out[:, 0:feat] = qb[0]
-    tok_out[:, feat : 2 * feat] = kb[0]
-    tok_out[:, 2 * feat : 3 * feat] = (rate * vb[0].astype(F32)).astype(BF)
-    gg_out[...] = gb[...] * ob[0].astype(F32)
+    rate = jnp.broadcast_to(rates[...], (feat, tokens)).T
+    kv_out[:, 0:feat] = k[0]
+    kv_out[:, feat : 2 * feat] = (rate * v[0].astype(F32)).astype(BF)
+    gg_out[...] = gains[...] * og[0].astype(F32)
+    rate_out[...] = rate
 
 
 def weight_pack_kernel(group, slab, *refs):
@@ -115,31 +113,28 @@
 
 
 def forward_kernel(slab, group, w, *refs):
-    tokens, mirrored, parts = refs[:group], refs[group:-group], refs[-group:]
-    own, feat = parts[0].shape[0], parts[0].shape[1] // (1 + len(mirrored))
+    queries, parts = refs[:group], refs[group:]
     normed = normalized(w, slab)[-1]
-    rows = stack(tokens, slice(0, feat))
+    rows = stack(queries)
     hidden = (silu_parts(mm(rows, normed[0]))[0] * mm(rows, normed[1])).astype(BF)
     out = mm_nt(hidden, normed[2]).astype(BF)
+    own = rows.shape[0] // group
     for d in range(group):
-        parts[d][:, 0:feat] = out[d * own : (d + 1) * own]
-        for e, queries in enumerate(mirrored):
-            parts[d][:, (1 + e) * feat : (2 + e) * feat] = queries[...]
+        parts[d][...] = out[d * own : (d + 1) * own]
 
 
 def reduce_kernel(gg, *refs):
     parts, (apply_out, sums) = refs[:-2], refs[-2:]
-    feat = apply_out.shape[1]
-    total = parts[0][:, 0:feat].astype(F32)
+    total = parts[0][...].astype(F32)
     for part in parts[1:]:
-        total += part[:, 0:feat].astype(F32)
+        total += part[...].astype(F32)
     apply_out[...] = total
     sums[0:1, :] = jnp.sum((total * total).T, axis=0, keepdims=True)
     sums[1:2, :] = jnp.sum((total * gg[...]).T, axis=0, keepdims=True)
 
 
-def delta_kernel(width, apply_out, gg, *refs):
-    sums, out = refs[:-1], refs[-1]
+def delta_kernel(width, apply_out, gg, kv, *refs):
+    sums, (od_out, out) = refs[:-2], refs[-2:]
     tokens, feat = apply_out.shape
     total = sums[0][...]
     for more in sums[1:]:
@@ -147,23 +142,26 @@
     square = jnp.broadcast_to(total[0:1, :], (feat, tokens)).T
     gain = jnp.broadcast_to(total[1:2, :], (feat, tokens)).T
     root = jnp.sqrt(square / width + EPS_ROOT)
-    out[...] = (gg[...] / root - apply_out[...] * (gain / width) / (root * root * root)).astype(BF)
+    delta = (gg[...] / root - apply_out[...] * (gain / width) / (root * root * root)).astype(BF)
+    od_out[...] = delta
+    out[:, 0:feat] = delta
+    out[:, feat : 3 * feat] = kv[...]
 
 
 def backward_kernel(slab, group, tok_groups, place, w, *refs):
+    far = group * (tok_groups - 1)
     lists = []
-    for count in (group, group, group, group * (tok_groups - 1), group, group * tok_groups):
+    for count in (group, far, group, far, group, tok_groups):
         lists.append(refs[:count])
         refs = refs[count:]
-    tokens, parts, od_near, od_far, outs, inner_outs = lists
-    far_q, far_od, inner_all, ag, au, ad = refs
-    mine, me = place[0], place[2]
+    q_near, q_far, tokens, od_far, outs, homes = lists
+    far_q, far_od, home, ag, au, ad = refs
+    mine = place[0]
     saved, init, norm_init, norm_saved, ratio, normed = normalized(w, slab)
-    own, feat = od_near[0].shape
-    for e in range(1, tok_groups):
-        for d in range(group):
-            far_q[e - 1, d] = parts[d][:, e * feat : (e + 1) * feat]
-            far_od[e - 1, d] = od_far[(e - 1) * group + d][...]
+    own, feat = q_near[0].shape
+    for i in range(far):
+        far_q[i // group, i % group] = q_far[i][...]
+        far_od[i // group, i % group] = od_far[i][...]
 
     def query_side(rows, delta):
         q_gate = mm(rows, normed[0])
@@ -176,7 +174,7 @@
         grads = (mm_tn(rows, delta_gate), mm_tn(rows, delta_up), mm_tn(delta, hidden))
         return delta_gate, delta_up, grads
 
-    delta_gate, delta_up, grads = query_side(stack(tokens, slice(0, feat)), stack(od_near))
+    delta_gate, delta_up, grads = query_side(stack(q_near), stack(tokens, slice(0, feat)))
     grad_q = (mm_nt(delta_gate, normed[0]) + mm_nt(delta_up, normed[1])).astype(BF)
     ag[...], au[...], ad[...] = grads
 
@@ -233,32 +231,40 @@
         outs[d][:, 2 * feat : 3 * feat] = grad_v[d * own : (d + 1) * own]
     inner = (mm_tn(keys, back_kgate), mm_tn(keys, back_kup), mm_tn(values, back_proj))
     total = jnp.concatenate([inner[i] + direct[i] for i in range(3)], axis=1)
-    rows = inner_all.shape[1]
-    for p in range(inner_all.shape[0]):
-        inner_all[p] = total[p * rows : (p + 1) * rows]
-    for d, out in enumerate(inner_outs):
-        out[...] = inner_all[me ^ d].astype(BF)
-
-
-def tokens_kernel(rates, *refs):
+    rows = home.shape[1]
+    for t in range(tok_groups):
+        home[t] = total[t * rows : (t + 1) * rows]
+    for e, out in enumerate(homes):
+        out[...] = home[mine ^ e].astype(out.dtype)
+
+
+def home_kernel(group, place, *refs):
+    blocks, outs, total = refs[: -group - 1], refs[-group - 1 : -1], refs[-1]
+    whole = blocks[0][...]
+    for block in blocks[1:]:
+        whole += block[...].astype(F32)
+    rows = total.shape[1]
+    for j in range(group):
+        total[j] = whole[j * rows : (j + 1) * rows]
+    for d in range(group):
+        outs[d][...] = total[place[1] ^ d].astype(BF)
+
+
+def tokens_kernel(rate, *refs):
     got, (gq, gk, gv) = refs[:-3], refs[-3:]
-    tokens, feat = gq.shape[1:]
+    feat = gq.shape[2]
     total = got[0][...].astype(F32)
     for block in got[1:]:
         total += block[...].astype(F32)
     gq[0] = total[:, 0:feat].astype(BF)
     gk[0] = total[:, feat : 2 * feat].astype(BF)
-    rate = jnp.broadcast_to(rates[...], (feat, tokens)).T
-    gv[0] = (rate * total[:, 2 * feat : 3 * feat]).astype(BF)
+    gv[0] = (rate[...] * total[:, 2 * feat : 3 * feat]).astype(BF)
 
 
 def weights_kernel(group, slab, place, *refs):
     got, outs, total = refs[:-4], refs[-4:-1], refs[-1]
     for d in range(group):
-        block = got[d][...].astype(F32)
-        for more in got[d + group :: group]:
-            block += more[...].astype(F32)
-        total[d] = block
+        total[d] = got[d][...].astype(F32)
     cols = [total[place[1] ^ j] for j in range(group)]
     for i in range(3):
         outs[i][0] = jnp.concatenate([c[:, i * slab : (i + 1) * slab] for c in cols], axis=1)
@@ -284,28 +290,29 @@
         me = lax.axis_index("seq")
         place = jnp.stack((lax.div(me, group), lax.rem(me, group), me)).astype(jnp.int32)
 
-        q_mirror = mirror(q[0])
-        tok_args = (q, k, v, og, rates, gains)
-        tokens, gg = copying_call(
-            token_pack_kernel,
-            (arr((own, 3 * feat), BF), arr((own, feat), F32)),
-            tok_args,
-            [pltpu.VMEM(x.shape, x.dtype) for x in tok_args],
-        )
-        tokens = near_all(tokens)
         (packed,) = copying_call(
             functools.partial(weight_pack_kernel, group, slab),
             (arr((seq_n, rows, 6 * slab), BF),),
             (gs, us, ds, gi, ui, di),
             [pltpu.VMEM((6, rows, hidden), BF)],
         )
+        packed, queries = lax.optimization_barrier((packed, q[0]))
         wall = lax.all_to_all(packed, "seq", 0, 0, tiled=True).reshape(seq_n * rows, 6 * slab)
+        q_near = near_all(queries)
+        q_far = [x for m in mirror(queries) for x in near_all(m)]
+        kv, gg, rate = call(
+            token_pack_kernel,
+            (arr((own, 2 * feat), BF), arr((own, feat), F32), arr((own, feat), F32)),
+            (k, v, og, rates, gains),
+            8,
+        )
+        wall, kv, *q_far = lax.optimization_barrier((wall, kv, *q_far))
 
         block = arr((own, feat), BF)
         parts = call(
             functools.partial(forward_kernel, slab, group),
-            (arr((own, feat * tok_groups), BF),) * group,
-            (wall, *tokens, *q_mirror),
+            (block,) * group,
+            (wall, *q_near),
             24,
             flops=6 * near * feat * slab,
         )
@@ -314,32 +321,51 @@
             reduce_kernel, (arr((own, feat), F32), arr((2, own), F32)), (gg, *parts), 16
         )
         sums = [sums] + [move(sums, d, "head", head_n) for d in range(1, head_n)]
-        (od,) = call(functools.partial(delta_kernel, head_n * feat), (block,), (apply_out, gg, *sums), 16)
+        od, tokens = call(
+            functools.partial(delta_kernel, head_n * feat),
+            (block, arr((own, 3 * feat), BF)),
+            (apply_out, gg, kv, *sums),
+            16,
+        )
         od_mirror = mirror(od)
-        od_near = near_all(od)
+        tokens = near_all(tokens)
         od_far = [x for m in od_mirror for x in near_all(m)]
 
         far = pltpu.VMEM((max(tok_groups - 1, 1), group, own, feat), BF)
+        home = (group * rows, 3 * slab)
         result = call(
             functools.partial(backward_kernel, slab, group, tok_groups),
-            (arr((own, 3 * feat), BF),) * group + (arr((rows, 3 * slab), BF),) * seq_n,
-            (place, wall, *tokens, *parts, *od_near, *od_far),
+            (
+                *(arr((own, 3 * feat), BF),) * group,
+                arr(home, F32),
+                *(arr(home, BF),) * (tok_groups - 1),
+            ),
+            (place, wall, *q_near, *q_far, *tokens, *od_far),
             40,
             smem=1,
             flops=66 * near * feat * slab,
             scratch=[
                 far,
                 far,
-                pltpu.VMEM((seq_n, rows, 3 * slab), F32),
+                pltpu.VMEM((tok_groups, *home), F32),
                 *[pltpu.VMEM((seq_n * rows, slab), F32)] * 3,
             ],
         )
         tok, inner = result[:group], result[group:]
+        inner = [inner[0]] + [move(inner[e], e * group) for e in range(1, tok_groups)]
         tok = [tok[0]] + [move(tok[d], d) for d in range(1, group)]
-        inner = [inner[0]] + [move(inner[d], d) for d in range(1, seq_n)]
+        inner = call(
+            functools.partial(home_kernel, group),
+            (arr((rows, 3 * slab), BF),) * group,
+            (place, *inner),
+            16,
+            smem=1,
+            scratch=[pltpu.VMEM((group, rows, 3 * slab), F32)],
+        )
+        inner = [inner[0]] + [move(inner[d], d) for d in range(1, group)]
         out_tok = arr((1, own, feat), BF)
         grad_w = arr((1, rows, hidden), F32)
-        grads_t = call(tokens_kernel, (out_tok,) * 3, (rates, *tok), 16)
+        grads_t = call(tokens_kernel, (out_tok,) * 3, (rate, *tok), 16)
         grads_w = call(
             functools.partial(weights_kernel, group, slab),
             (grad_w,) * 3,

time: 94.6 us -> 96.4 us (1.019)
  waiting for transfers between devices: 43 us -> 47.2 us
  local copies, waits for them, and re-layouts: 1.57 us -> 0.04 us
  Pallas kernels: 10.8 us -> 9.7 us
    ppermute x27, waiting for transfers between devices: 43 us -> 47.2 us  [move(): return lax.ppermute(x, axis, [(i, i ^ dist) for i in range(size)])]
    pallas_call x2 -> x1, Pallas kernels: 3.7 us -> 1.92 us  [copying_call(): pl.pallas_call(kernel, out_shape=outs, in_specs=[pl.BlockSpec(memory_spac...]
    unnamed x10 -> x12, local copies, waits for them, and re-layouts: 1.57 us -> 0.04 us
    pallas_call x6 -> x8, Pallas kernels: 7.1 us -> 7.78 us  [call(): pl.pallas_call(kernel, out_shape=outs, in_specs=[SMEM] * smem + [VMEM] *...]
  transfers between devices with their start and end apart: 28 -> 28, of which waited for: 17 -> 17; matrix products, arithmetic and copies ran while one was open for 0% -> 0% of each run, Pallas kernels for 3% -> 2%
where the time goes in v3:
time: 96.4 us; the launch traced here: 96.1 us
  waiting for transfers between devices  47.2 us (49%)
  starting transfers between devices  38.3 us (40%)
  Pallas kernels  9.7 us (10%)
    ppermute x27, waiting for transfers between devices, move(): return lax.ppermute(x, axis, [(i, i ^ dist) for i in range(size)])  47.2 us
    ppermute x27, starting transfers between devices, move(): return lax.ppermute(x, axis, [(i, i ^ dist) for i in range(size)])  30.9 us
    pallas_call x8, Pallas kernels, call(): pl.pallas_call(kernel, out_shape=outs, in_specs=[SMEM] * smem + [VMEM] *...  7.78 us
    all_to_all x1, starting transfers between devices, local(): lax.all_to_all(packed, 'seq', 0, 0, tiled=True)  7.4 us
  transfers between devices with their start and end apart: 28, of which 17 were waited for; matrix products, arithmetic and copies ran while one was open for 0% of the time, Pallas kernels for 2%

profile of v3, /device:TPU:0, one launch (start us, length us, event | category | flops | bytes accessed | tf_op | source)
XLA Modules:
  0.0 96.1 jit_solution(15733909845654793213)
XLA Ops:
  0.6 1.9 %shard_map.164 = bf16[8,32,1152]{2,1,0:T(8,128)(2,1)} custom-call(bf16[1,32,768]{2,1,0:T(8,128)(2,1)} %refs_0_.1, bf16[1,32,768]{2,1,0:T(8,128)(2,1)} %refs_1_.1, bf16[1,32,768]{2,1,0:T(8,128)(2,1)} %refs_2_.1, bf16[1,32,768]{2,1,0:T(8,128)(2,1)} %refs_3_.1, bf16[1,32,768]{2,1,0:T(8,128)(2,1)} %refs_4_.1, bf16[1,32,768]{2,1,0:T(8,128)(2,1)} %refs_5_.1), custom_call_target="tpu_custom_call" | custom-call | tf_op jit(solution)/shard_map/pallas_call | solution.py:60
  2.6 0.0 copy-start.3
  2.6 0.0 copy-start
  2.6 0.0 copy-start.1
  2.6 0.0 copy-start.2
  2.6 0.0 copy-start.4
  2.6 0.0 copy-start.5
  2.6 7.4 %all-to-all-start = ((bf16[8,32,1152]{2,1,0:T(8,128)(2,1)}), bf16[8,32,1152]{2,1,0:T(8,128)(2,1)S(1)}, u32[]{:S(2)}, u32[]{:S(2)}) async-start(bf16[8,32,1152]{2,1,0:T(8,128)(2,1)} %shard_map.164), calls=%async_computation | async-start | bytes 1179648 | tf_op jit(solution)/shard_map/all_to_all | solution.py:300
  10.0 2.9 %collective-permute-start = (bf16[128,256]{1,0:T(8,128)(2,1)S(1)}, bf16[128,256]{1,0:T(8,128)(2,1)S(1)}, u32[]{:S(2)}, u32[]{:S(2)}) collective-permute-start(bf16[128,256]{1,0:T(8,128)(2,1)S(1)} %bitcast.7), channel_id=1, source_target_pairs={{0,4},{1,5},{2,6},{3,7},{4,0},{5,1},{6,2},{7,3},{8,12},{9,13},{10,... | collective-permute-start | bytes 196616 | tf_op jit(solution)/shard_map/ppermute | solution.py:277
  13.0 15.8 %collective-permute-done.refs_4_ = bf16[128,256]{1,0:T(8,128)(2,1)S(1)} collective-permute-done((bf16[128,256]{1,0:T(8,128)(2,1)S(1)}, bf16[128,256]{1,0:T(8,128)(2,1)S(1)}, u32[]{:S(2)}, u32[]{:S(2)}) %collective-permute-start) | collective-permute-done | bytes 65568 | tf_op jit(solution)/shard_map/ppermute | solution.py:277
  28.7 0.0 collective-permute-start.3
  28.7 2.9 %collective-permute-start.2 = (bf16[128,256]{1,0:T(8,128)(2,1)S(1)}, bf16[128,256]{1,0:T(8,128)(2,1)S(1)}, u32[]{:S(2)}, u32[]{:S(2)}) collective-permute-start(bf16[128,256]{1,0:T(8,128)(2,1)S(1)} %collective-permute-done.refs_4_), channel_id=1, source_target_pairs={{0,2},{1,3},{2,0},{3,1},{4,6},{5,7},{6,4},{7,5},{8,10},{9,11},{10,... | collective-permute-start | bytes 196616 | tf_op jit(solution)/shard_map/ppermute | solution.py:277
  31.7 0.6 collective-permute-start.1
  32.2 0.9 collective-permute-start.6
  33.1 2.0 %collective-permute-start.5 = (bf16[128,256]{1,0:T(8,128)(2,1)S(1)}, bf16[128,256]{1,0:T(8,128)(2,1)S(1)}, u32[]{:S(2)}, u32[]{:S(2)}) collective-permute-start(bf16[128,256]{1,0:T(8,128)(2,1)S(1)} %bitcast.9), channel_id=1, source_target_pairs={{0,2},{1,3},{2,0},{3,1},{4,6},{5,7},{6,4},{7,5},{8,10},{9,11},{10,... | collective-permute-start | bytes 196616 | tf_op jit(solution)/shard_map/ppermute | solution.py:277
  35.1 0.0 collective-permute-done.3.refs_7_
  35.1 0.6 collective-permute-start.4
  35.7 0.1 shard_map.163
  35.9 0.6 collective-permute-done.1.refs_5_
  36.4 0.9 collective-permute-done.6.refs_3_
  37.4 0.7 collective-permute-done.5.refs_2_
  38.1 1.3 %collective-permute-done.4.refs_1_ = bf16[128,256]{1,0:T(8,128)(2,1)S(1)} collective-permute-done((bf16[128,256]{1,0:T(8,128)(2,1)S(1)}, bf16[128,256]{1,0:T(8,128)(2,1)S(1)}, u32[]{:S(2)}, u32[]{:S(2)}) %collective-permute-start.4) | collective-permute-done | bytes 65568 | tf_op jit(solution)/shard_map/ppermute | solution.py:277
  39.4 0.8 shard_map.165
  40.2 0.6 collective-permute-start.7
  40.8 0.0 collective-permute-start.8
  40.8 2.9 %collective-permute-start.9 = (bf16[128,256]{1,0:T(8,128)(2,1)S(1)}, bf16[128,256]{1,0:T(8,128)(2,1)S(1)}, u32[]{:S(2)}, u32[]{:S(2)}) collective-permute-start(bf16[128,256]{1,0:T(8,128)(2,1)S(1)} %get-tuple-element.54), channel_id=1, source_target_pairs={{0,3},{1,2},{2,1},{3,0},{4,7},{5,6},{6,5},{7,4},{8,11},{9,10},{10,... | collective-permute-start | bytes 196616 | tf_op jit(solution)/shard_map/ppermute | solution.py:277
  43.7 0.8 collective-permute-done.7.refs_1_
  44.5 0.6 collective-permute-done.8.refs_2_
  45.1 1.6 %collective-permute-done.9.refs_3_ = bf16[128,256]{1,0:T(8,128)(2,1)S(1)} collective-permute-done((bf16[128,256]{1,0:T(8,128)(2,1)S(1)}, bf16[128,256]{1,0:T(8,128)(2,1)S(1)}, u32[]{:S(2)}, u32[]{:S(2)}) %collective-permute-start.9) | collective-permute-done | bytes 65568 | tf_op jit(solution)/shard_map/ppermute | solution.py:277
  46.7 0.1 shard_map.166
  46.8 0.1 collective-permute-start.12
  46.9 1.6 %collective-permute-start.11 = (f32[2,128]{1,0:T(2,128)S(1)}, f32[2,128]{1,0:T(2,128)S(1)}, u32[]{:S(2)}, u32[]{:S(2)}) collective-permute-start(f32[2,128]{1,0:T(2,128)S(1)} %get-tuple-element.57.refs_0_), channel_id=1, source_target_pairs={{0,16},{8,24},{16,0},{24,8},{1,17},{9,25},{17,1},{25,9},{2,18},{10... | collective-permute-start | bytes 3080 | tf_op jit(solution)/shard_map/ppermute | solution.py:277
  48.5 0.3 collective-permute-start.10
  48.8 1.1 %collective-permute-done.12.refs_3_ = f32[2,128]{1,0:T(2,128)S(1)} collective-permute-done((f32[2,128]{1,0:T(2,128)S(1)}, f32[2,128]{1,0:T(2,128)S(1)}, u32[]{:S(2)}, u32[]{:S(2)}) %collective-permute-start.12) | collective-permute-done | bytes 1056 | tf_op jit(solution)/shard_map/ppermute | solution.py:277
  49.9 0.7 collective-permute-done.11.refs_2_
  50.5 0.0 collective-permute-done.10.refs_1_
  50.5 0.1 shard_map.167
  50.7 1.5 %collective-permute-start.16 = (bf16[128,256]{1,0:T(8,128)(2,1)S(1)}, bf16[128,256]{1,0:T(8,128)(2,1)S(1)}, u32[]{:S(2)}, u32[]{:S(2)}) collective-permute-start(bf16[128,256]{1,0:T(8,128)(2,1)S(1)} %get-tuple-element.59), channel_id=1, source_target_pairs={{0,4},{1,5},{2,6},{3,7},{4,0},{5,1},{6,2},{7,3},{8,12},{9,13},{10,... | collective-permute-start | bytes 196616 | tf_op jit(solution)/shard_map/ppermute | solution.py:277
  52.2 0.9 collective-permute-start.15
  53.1 1.9 %collective-permute-start.14 = (bf16[128,768]{1,0:T(8,128)(2,1)S(1)}, bf16[128,768]{1,0:T(8,128)(2,1)S(1)}, u32[]{:S(2)}, u32[]{:S(2)}) collective-permute-start(bf16[128,768]{1,0:T(8,128)(2,1)S(1)} %get-tuple-element.58.refs_8_), channel_id=1, source_target_pairs={{0,2},{1,3},{2,0},{3,1},{4,6},{5,7},{6,4},{7,5},{8,10},{9,11},{10,... | collective-permute-start | bytes 589832 | tf_op jit(solution)/shard_map/ppermute | solution.py:277
  55.0 0.7 collective-permute-start.13
  55.7 1.9 %collective-permute-done.16.refs_12_ = bf16[128,256]{1,0:T(8,128)(2,1)S(1)} collective-permute-done((bf16[128,256]{1,0:T(8,128)(2,1)S(1)}, bf16[128,256]{1,0:T(8,128)(2,1)S(1)}, u32[]{:S(2)}, u32[]{:S(2)}) %collective-permute-start.16) | collective-permute-done | bytes 65568 | tf_op jit(solution)/shard_map/ppermute | solution.py:277
  57.6 1.2 %collective-permute-start.19 = (bf16[128,256]{1,0:T(8,128)(2,1)S(1)}, bf16[128,256]{1,0:T(8,128)(2,1)S(1)}, u32[]{:S(2)}, u32[]{:S(2)}) collective-permute-start(bf16[128,256]{1,0:T(8,128)(2,1)S(1)} %collective-permute-done.16.refs_12_), channel_id=1, source_target_pairs={{0,3},{1,2},{2,1},{3,0},{4,7},{5,6},{6,5},{7,4},{8,11},{9,10},{10,... | collective-permute-start | bytes 196616 | tf_op jit(solution)/shard_map/ppermute | solution.py:277
  58.8 0.0 collective-permute-start.18
  58.8 7.7 %collective-permute-done.19.refs_15_ = bf16[128,256]{1,0:T(8,128)(2,1)S(1)} collective-permute-done((bf16[128,256]{1,0:T(8,128)(2,1)S(1)}, bf16[128,256]{1,0:T(8,128)(2,1)S(1)}, u32[]{:S(2)}, u32[]{:S(2)}) %collective-permute-start.19) | collective-permute-done | bytes 65568 | tf_op jit(solution)/shard_map/ppermute | solution.py:277
  66.5 1.8 %collective-permute-start.17 = (bf16[128,256]{1,0:T(8,128)(2,1)S(1)}, bf16[128,256]{1,0:T(8,128)(2,1)S(1)}, u32[]{:S(2)}, u32[]{:S(2)}) collective-permute-start(bf16[128,256]{1,0:T(8,128)(2,1)S(1)} %collective-permute-done.16.refs_12_), channel_id=1, source_target_pairs={{0,1},{1,0},{2,3},{3,2},{4,5},{5,4},{6,7},{7,6},{8,9},{9,8},{10,11... | collective-permute-start | bytes 196616 | tf_op jit(solution)/shard_map/ppermute | solution.py:277
  68.3 0.1 pad_add_fusion.place
  68.3 0.0 collective-permute-done.18.refs_14_
  68.3 2.4 %collective-permute-done.17.refs_13_ = bf16[128,256]{1,0:T(8,128)(2,1)S(1)} collective-permute-done((bf16[128,256]{1,0:T(8,128)(2,1)S(1)}, bf16[128,256]{1,0:T(8,128)(2,1)S(1)}, u32[]{:S(2)}, u32[]{:S(2)}) %collective-permute-start.17) | collective-permute-done | bytes 65568 | tf_op jit(solution)/shard_map/ppermute | solution.py:277
  70.8 3.9 %shard_map.168 = (bf16[128,768]{1,0:T(8,128)(2,1)S(1)}, bf16[128,768]{1,0:T(8,128)(2,1)S(1)}, bf16[128,768]{1,0:T(8,128)(2,1)S(1)}, bf16[128,768]{1,0:T(8,128)(2...) custom-call(s32[3]{0:T(128)S(1)} %pad_add_fusion.place, bf16[256,1152]{1,0:T(8,128)(2,1)S(1)} %bitcast.6, ...), custom_call_target="tpu_custom_call" | custom-call | flops 1660944384 | bytes 3391500 | tf_op jit(solution)/shard_map/pallas_call | solution.py:48
  74.7 2.2 %collective-permute-start.23 = (bf16[128,576]{1,0:T(8,128)(2,1)S(1)}, bf16[128,576]{1,0:T(8,128)(2,1)S(1)}, u32[]{:S(2)}, u32[]{:S(2)}) collective-permute-start(bf16[128,576]{1,0:T(8,128)(2,1)S(1)} %get-tuple-element.68), channel_id=1, source_target_pairs={{0,4},{1,5},{2,6},{3,7},{4,0},{5,1},{6,2},{7,3},{8,12},{9,13},{10,... | collective-permute-start | bytes 442376 | tf_op jit(solution)/shard_map/ppermute | solution.py:277
  76.9 0.6 collective-permute-start.20
  77.5 1.6 %collective-permute-start.21 = (bf16[128,768]{1,0:T(8,128)(2,1)S(1)}, bf16[128,768]{1,0:T(8,128)(2,1)S(1)}, u32[]{:S(2)}, u32[]{:S(2)}) collective-permute-start(bf16[128,768]{1,0:T(8,128)(2,1)S(1)} %get-tuple-element.62), channel_id=1, source_target_pairs={{0,2},{1,3},{2,0},{3,1},{4,6},{5,7},{6,4},{7,5},{8,10},{9,11},{10,... | collective-permute-start | bytes 589832 | tf_op jit(solution)/shard_map/ppermute | solution.py:277
  79.1 1.4 %collective-permute-start.22 = (bf16[128,768]{1,0:T(8,128)(2,1)S(1)}, bf16[128,768]{1,0:T(8,128)(2,1)S(1)}, u32[]{:S(2)}, u32[]{:S(2)}) collective-permute-start(bf16[128,768]{1,0:T(8,128)(2,1)S(1)} %get-tuple-element.63), channel_id=1, source_target_pairs={{0,3},{1,2},{2,1},{3,0},{4,7},{5,6},{6,5},{7,4},{8,11},{9,10},{10,... | collective-permute-start | bytes 589832 | tf_op jit(solution)/shard_map/ppermute | solution.py:277
  80.4 3.2 %collective-permute-done.23.refs_1_ = bf16[128,576]{1,0:T(8,128)(2,1)S(1)} collective-permute-done((bf16[128,576]{1,0:T(8,128)(2,1)S(1)}, bf16[128,576]{1,0:T(8,128)(2,1)S(1)}, u32[]{:S(2)}, u32[]{:S(2)}) %collective-permute-start.23) | collective-permute-done | bytes 147488 | tf_op jit(solution)/shard_map/ppermute | solution.py:277
  83.6 0.6 shard_map.170
  84.2 0.8 collective-permute-start.24
  85.0 0.4 collective-permute-start.25
  85.4 3.7 %collective-permute-done.24.refs_1_ = bf16[32,576]{1,0:T(8,128)(2,1)S(1)} collective-permute-done((bf16[32,576]{1,0:T(8,128)(2,1)S(1)}, bf16[32,576]{1,0:T(8,128)(2,1)S(1)}, u32[]{:S(2)}, u32[]{:S(2)}) %collective-permute-start.24) | collective-permute-done | bytes 36896 | tf_op jit(solution)/shard_map/ppermute | solution.py:277
  89.1 0.8 collective-permute-start.26
  89.8 0.4 collective-permute-done.25.refs_2_
  90.3 3.7 %collective-permute-done.26.refs_3_ = bf16[32,576]{1,0:T(8,128)(2,1)S(1)} collective-permute-done((bf16[32,576]{1,0:T(8,128)(2,1)S(1)}, bf16[32,576]{1,0:T(8,128)(2,1)S(1)}, u32[]{:S(2)}, u32[]{:S(2)}) %collective-permute-start.26) | collective-permute-done | bytes 36896 | tf_op jit(solution)/shard_map/ppermute | solution.py:277
  94.0 1.4 %shard_map.171 = (f32[1,32,768]{2,1,0:T(8,128)}, f32[1,32,768]{2,1,0:T(8,128)}, f32[1,32,768]{2,1,0:T(8,128)}) custom-call(s32[3]{0:T(128)S(1)} %pad_add_fusion.place, bf16[32,576]{1,0:T(8,128)(2,1)S(1)} %get-tuple-element.69.refs_0_, bf16[32,576]{1,0:T(8,128)(2,1)S(1)} %collective-permute-done.24.refs_1_, ...), custom_call_target="tpu_custom_call" | custom-call | bytes 442380 | tf_op jit(solution)/shard_map/pallas_call | solution.py:48
  95.4 0.7 shard_map.169
  (14 shorter events, 0.0 us)
Async XLA Ops:
  2.6 7.5 %copy-start.3 = (bf16[1,128,256]{2,1,0:T(8,128)(2,1)S(1)}, bf16[1,128,256]{2,1,0:T(8,128)(2,1)}, u32[]{:S(2)}) copy-start(bf16[1,128,256]{2,1,0:T(8,128)(2,1)} %param.12) | copy-start | bytes 196612
  2.6 33.1 %copy-start = (bf16[1,128,256]{2,1,0:T(8,128)(2,1)S(1)}, bf16[1,128,256]{2,1,0:T(8,128)(2,1)}, u32[]{:S(2)}) copy-start(bf16[1,128,256]{2,1,0:T(8,128)(2,1)} %k.1) | copy-start | bytes 196612
  2.6 33.1 %copy-start.1 = (bf16[1,128,256]{2,1,0:T(8,128)(2,1)S(1)}, bf16[1,128,256]{2,1,0:T(8,128)(2,1)}, u32[]{:S(2)}) copy-start(bf16[1,128,256]{2,1,0:T(8,128)(2,1)} %v.1) | copy-start | bytes 196612
  2.6 33.1 %copy-start.2 = (bf16[1,128,256]{2,1,0:T(8,128)(2,1)S(1)}, bf16[1,128,256]{2,1,0:T(8,128)(2,1)}, u32[]{:S(2)}) copy-start(bf16[1,128,256]{2,1,0:T(8,128)(2,1)} %og.1) | copy-start | bytes 196612
  2.6 33.1 %copy-start.4 = (f32[1,256]{1,0:T(1,128)S(1)}, f32[1,256]{1,0:T(1,128)}, u32[]{:S(2)}) copy-start(f32[1,256]{1,0:T(1,128)} %gains.1) | copy-start | bytes 3076
  2.6 33.1 %copy-start.5 = (f32[1,128]{1,0:T(1,128)S(1)}, f32[1,128]{1,0:T(1,128)}, u32[]{:S(2)}) copy-start(f32[1,128]{1,0:T(1,128)} %rates.1) | copy-start | bytes 1540
  2.6 33.8 %all-to-all-start = ((bf16[8,32,1152]{2,1,0:T(8,128)(2,1)}), bf16[8,32,1152]{2,1,0:T(8,128)(2,1)S(1)}, u32[]{:S(2)}, u32[]{:S(2)}) async-start(bf16[8,32,1152]{2,1,0:T(8,128)(2,1)} %shard_map.164), calls=%async_computation | async-start | bytes 1179648 | tf_op jit(solution)/shard_map/all_to_all | solution.py:300
  10.0 18.7 %collective-permute-start = (bf16[128,256]{1,0:T(8,128)(2,1)S(1)}, bf16[128,256]{1,0:T(8,128)(2,1)S(1)}, u32[]{:S(2)}, u32[]{:S(2)}) collective-permute-start(bf16[128,256]{1,0:T(8,128)(2,1)S(1)} %bitcast.7), channel_id=1, source_target_pairs={{0,4},{1,5},{2,6},{3,7},{4,0},{5,1},{6,2},{7,3},{8,12},{9,13},{10,... | collective-permute-start | bytes 196616 | tf_op jit(solution)/shard_map/ppermute | solution.py:277
  28.7 6.4 %collective-permute-start.3 = (bf16[128,256]{1,0:T(8,128)(2,1)S(1)}, bf16[128,256]{1,0:T(8,128)(2,1)S(1)}, u32[]{:S(2)}, u32[]{:S(2)}) collective-permute-start(bf16[128,256]{1,0:T(8,128)(2,1)S(1)} %collective-permute-done.refs_4_), channel_id=1, source_target_pairs={{0,3},{1,2},{2,1},{3,0},{4,7},{5,6},{6,5},{7,4},{8,11},{9,10},{10,... | collective-permute-start | bytes 196616 | tf_op jit(solution)/shard_map/ppermute | solution.py:277
  28.7 7.1 %collective-permute-start.2 = (bf16[128,256]{1,0:T(8,128)(2,1)S(1)}, bf16[128,256]{1,0:T(8,128)(2,1)S(1)}, u32[]{:S(2)}, u32[]{:S(2)}) collective-permute-start(bf16[128,256]{1,0:T(8,128)(2,1)S(1)} %collective-permute-done.refs_4_), channel_id=1, source_target_pairs={{0,2},{1,3},{2,0},{3,1},{4,6},{5,7},{6,4},{7,5},{8,10},{9,11},{10,... | collective-permute-start | bytes 196616 | tf_op jit(solution)/shard_map/ppermute | solution.py:277
  31.7 4.8 %collective-permute-start.1 = (bf16[128,256]{1,0:T(8,128)(2,1)S(1)}, bf16[128,256]{1,0:T(8,128)(2,1)S(1)}, u32[]{:S(2)}, u32[]{:S(2)}) collective-permute-start(bf16[128,256]{1,0:T(8,128)(2,1)S(1)} %collective-permute-done.refs_4_), channel_id=1, source_target_pairs={{0,1},{1,0},{2,3},{3,2},{4,5},{5,4},{6,7},{7,6},{8,9},{9,8},{10,11... | collective-permute-start | bytes 196616 | tf_op jit(solution)/shard_map/ppermute | solution.py:277
  32.2 5.2 %collective-permute-start.6 = (bf16[128,256]{1,0:T(8,128)(2,1)S(1)}, bf16[128,256]{1,0:T(8,128)(2,1)S(1)}, u32[]{:S(2)}, u32[]{:S(2)}) collective-permute-start(bf16[128,256]{1,0:T(8,128)(2,1)S(1)} %bitcast.8), channel_id=1, source_target_pairs={{0,3},{1,2},{2,1},{3,0},{4,7},{5,6},{6,5},{7,4},{8,11},{9,10},{10,... | collective-permute-start | bytes 196616 | tf_op jit(solution)/shard_map/ppermute | solution.py:277
  33.1 5.0 %collective-permute-start.5 = (bf16[128,256]{1,0:T(8,128)(2,1)S(1)}, bf16[128,256]{1,0:T(8,128)(2,1)S(1)}, u32[]{:S(2)}, u32[]{:S(2)}) collective-permute-start(bf16[128,256]{1,0:T(8,128)(2,1)S(1)} %bitcast.9), channel_id=1, source_target_pairs={{0,2},{1,3},{2,0},{3,1},{4,6},{5,7},{6,4},{7,5},{8,10},{9,11},{10,... | collective-permute-start | bytes 196616 | tf_op jit(solution)/shard_map/ppermute | solution.py:277
  35.1 4.3 %collective-permute-start.4 = (bf16[128,256]{1,0:T(8,128)(2,1)S(1)}, bf16[128,256]{1,0:T(8,128)(2,1)S(1)}, u32[]{:S(2)}, u32[]{:S(2)}) collective-permute-start(bf16[128,256]{1,0:T(8,128)(2,1)S(1)} %bitcast.10), channel_id=1, source_target_pairs={{0,1},{1,0},{2,3},{3,2},{4,5},{5,4},{6,7},{7,6},{8,9},{9,8},{10,11... | collective-permute-start | bytes 196616 | tf_op jit(solution)/shard_map/ppermute | solution.py:277
  40.2 4.3 %collective-permute-start.7 = (bf16[128,256]{1,0:T(8,128)(2,1)S(1)}, bf16[128,256]{1,0:T(8,128)(2,1)S(1)}, u32[]{:S(2)}, u32[]{:S(2)}) collective-permute-start(bf16[128,256]{1,0:T(8,128)(2,1)S(1)} %get-tuple-element.52), channel_id=1, source_target_pairs={{0,1},{1,0},{2,3},{3,2},{4,5},{5,4},{6,7},{7,6},{8,9},{9,8},{10,11... | collective-permute-start | bytes 196616 | tf_op jit(solution)/shard_map/ppermute | solution.py:277
  40.8 4.3 %collective-permute-start.8 = (bf16[128,256]{1,0:T(8,128)(2,1)S(1)}, bf16[128,256]{1,0:T(8,128)(2,1)S(1)}, u32[]{:S(2)}, u32[]{:S(2)}) collective-permute-start(bf16[128,256]{1,0:T(8,128)(2,1)S(1)} %get-tuple-element.53), channel_id=1, source_target_pairs={{0,2},{1,3},{2,0},{3,1},{4,6},{5,7},{6,4},{7,5},{8,10},{9,11},{10,... | collective-permute-start | bytes 196616 | tf_op jit(solution)/shard_map/ppermute | solution.py:277
  40.8 5.9 %collective-permute-start.9 = (bf16[128,256]{1,0:T(8,128)(2,1)S(1)}, bf16[128,256]{1,0:T(8,128)(2,1)S(1)}, u32[]{:S(2)}, u32[]{:S(2)}) collective-permute-start(bf16[128,256]{1,0:T(8,128)(2,1)S(1)} %get-tuple-element.54), channel_id=1, source_target_pairs={{0,3},{1,2},{2,1},{3,0},{4,7},{5,6},{6,5},{7,4},{8,11},{9,10},{10,... | collective-permute-start | bytes 196616 | tf_op jit(solution)/shard_map/ppermute | solution.py:277
  46.8 3.1 %collective-permute-start.12 = (f32[2,128]{1,0:T(2,128)S(1)}, f32[2,128]{1,0:T(2,128)S(1)}, u32[]{:S(2)}, u32[]{:S(2)}) collective-permute-start(f32[2,128]{1,0:T(2,128)S(1)} %get-tuple-element.57.refs_0_), channel_id=1, source_target_pairs={{0,24},{8,16},{16,8},{24,0},{1,25},{9,17},{17,9},{25,1},{2,26},{10... | collective-permute-start | bytes 3080 | tf_op jit(solution)/shard_map/ppermute | solution.py:277
  46.9 3.6 %collective-permute-start.11 = (f32[2,128]{1,0:T(2,128)S(1)}, f32[2,128]{1,0:T(2,128)S(1)}, u32[]{:S(2)}, u32[]{:S(2)}) collective-permute-start(f32[2,128]{1,0:T(2,128)S(1)} %get-tuple-element.57.refs_0_), channel_id=1, source_target_pairs={{0,16},{8,24},{16,0},{24,8},{1,17},{9,25},{17,1},{25,9},{2,18},{10... | collective-permute-start | bytes 3080 | tf_op jit(solution)/shard_map/ppermute | solution.py:277
  48.5 2.1 %collective-permute-start.10 = (f32[2,128]{1,0:T(2,128)S(1)}, f32[2,128]{1,0:T(2,128)S(1)}, u32[]{:S(2)}, u32[]{:S(2)}) collective-permute-start(f32[2,128]{1,0:T(2,128)S(1)} %get-tuple-element.57.refs_0_), channel_id=1, source_target_pairs={{0,8},{8,0},{16,24},{24,16},{1,9},{9,1},{17,25},{25,17},{2,10},{10... | collective-permute-start | bytes 3080 | tf_op jit(solution)/shard_map/ppermute | solution.py:277
  50.7 6.9 %collective-permute-start.16 = (bf16[128,256]{1,0:T(8,128)(2,1)S(1)}, bf16[128,256]{1,0:T(8,128)(2,1)S(1)}, u32[]{:S(2)}, u32[]{:S(2)}) collective-permute-start(bf16[128,256]{1,0:T(8,128)(2,1)S(1)} %get-tuple-element.59), channel_id=1, source_target_pairs={{0,4},{1,5},{2,6},{3,7},{4,0},{5,1},{6,2},{7,3},{8,12},{9,13},{10,... | collective-permute-start | bytes 196616 | tf_op jit(solution)/shard_map/ppermute | solution.py:277
  52.2 18.6 %collective-permute-start.15 = (bf16[128,768]{1,0:T(8,128)(2,1)S(1)}, bf16[128,768]{1,0:T(8,128)(2,1)S(1)}, u32[]{:S(2)}, u32[]{:S(2)}) collective-permute-start(bf16[128,768]{1,0:T(8,128)(2,1)S(1)} %get-tuple-element.58.refs_8_), channel_id=1, source_target_pairs={{0,3},{1,2},{2,1},{3,0},{4,7},{5,6},{6,5},{7,4},{8,11},{9,10},{10,... | collective-permute-start | bytes 589832 | tf_op jit(solution)/shard_map/ppermute | solution.py:277
  53.1 17.7 %collective-permute-start.14 = (bf16[128,768]{1,0:T(8,128)(2,1)S(1)}, bf16[128,768]{1,0:T(8,128)(2,1)S(1)}, u32[]{:S(2)}, u32[]{:S(2)}) collective-permute-start(bf16[128,768]{1,0:T(8,128)(2,1)S(1)} %get-tuple-element.58.refs_8_), channel_id=1, source_target_pairs={{0,2},{1,3},{2,0},{3,1},{4,6},{5,7},{6,4},{7,5},{8,10},{9,11},{10,... | collective-permute-start | bytes 589832 | tf_op jit(solution)/shard_map/ppermute | solution.py:277
  55.0 15.8 %collective-permute-start.13 = (bf16[128,768]{1,0:T(8,128)(2,1)S(1)}, bf16[128,768]{1,0:T(8,128)(2,1)S(1)}, u32[]{:S(2)}, u32[]{:S(2)}) collective-permute-start(bf16[128,768]{1,0:T(8,128)(2,1)S(1)} %get-tuple-element.58.refs_8_), channel_id=1, source_target_pairs={{0,1},{1,0},{2,3},{3,2},{4,5},{5,4},{6,7},{7,6},{8,9},{9,8},{10,11... | collective-permute-start | bytes 589832 | tf_op jit(solution)/shard_map/ppermute | solution.py:277
  57.6 8.9 %collective-permute-start.19 = (bf16[128,256]{1,0:T(8,128)(2,1)S(1)}, bf16[128,256]{1,0:T(8,128)(2,1)S(1)}, u32[]{:S(2)}, u32[]{:S(2)}) collective-permute-start(bf16[128,256]{1,0:T(8,128)(2,1)S(1)} %collective-permute-done.16.refs_12_), channel_id=1, source_target_pairs={{0,3},{1,2},{2,1},{3,0},{4,7},{5,6},{6,5},{7,4},{8,11},{9,10},{10,... | collective-permute-start | bytes 196616 | tf_op jit(solution)/shard_map/ppermute | solution.py:277
  58.8 9.6 %collective-permute-start.18 = (bf16[128,256]{1,0:T(8,128)(2,1)S(1)}, bf16[128,256]{1,0:T(8,128)(2,1)S(1)}, u32[]{:S(2)}, u32[]{:S(2)}) collective-permute-start(bf16[128,256]{1,0:T(8,128)(2,1)S(1)} %collective-permute-done.16.refs_12_), channel_id=1, source_target_pairs={{0,2},{1,3},{2,0},{3,1},{4,6},{5,7},{6,4},{7,5},{8,10},{9,11},{10,... | collective-permute-start | bytes 196616 | tf_op jit(solution)/shard_map/ppermute | solution.py:277
  66.5 4.3 %collective-permute-start.17 = (bf16[128,256]{1,0:T(8,128)(2,1)S(1)}, bf16[128,256]{1,0:T(8,128)(2,1)S(1)}, u32[]{:S(2)}, u32[]{:S(2)}) collective-permute-start(bf16[128,256]{1,0:T(8,128)(2,1)S(1)} %collective-permute-done.16.refs_12_), channel_id=1, source_target_pairs={{0,1},{1,0},{2,3},{3,2},{4,5},{5,4},{6,7},{7,6},{8,9},{9,8},{10,11... | collective-permute-start | bytes 196616 | tf_op jit(solution)/shard_map/ppermute | solution.py:277
  74.7 8.9 %collective-permute-start.23 = (bf16[128,576]{1,0:T(8,128)(2,1)S(1)}, bf16[128,576]{1,0:T(8,128)(2,1)S(1)}, u32[]{:S(2)}, u32[]{:S(2)}) collective-permute-start(bf16[128,576]{1,0:T(8,128)(2,1)S(1)} %get-tuple-element.68), channel_id=1, source_target_pairs={{0,4},{1,5},{2,6},{3,7},{4,0},{5,1},{6,2},{7,3},{8,12},{9,13},{10,... | collective-permute-start | bytes 442376 | tf_op jit(solution)/shard_map/ppermute | solution.py:277
  76.9 18.4 %collective-permute-start.20 = (bf16[128,768]{1,0:T(8,128)(2,1)S(1)}, bf16[128,768]{1,0:T(8,128)(2,1)S(1)}, u32[]{:S(2)}, u32[]{:S(2)}) collective-permute-start(bf16[128,768]{1,0:T(8,128)(2,1)S(1)} %get-tuple-element.61), channel_id=1, source_target_pairs={{0,1},{1,0},{2,3},{3,2},{4,5},{5,4},{6,7},{7,6},{8,9},{9,8},{10,11... | collective-permute-start | bytes 589832 | tf_op jit(solution)/shard_map/ppermute | solution.py:277
  77.5 17.8 %collective-permute-start.21 = (bf16[128,768]{1,0:T(8,128)(2,1)S(1)}, bf16[128,768]{1,0:T(8,128)(2,1)S(1)}, u32[]{:S(2)}, u32[]{:S(2)}) collective-permute-start(bf16[128,768]{1,0:T(8,128)(2,1)S(1)} %get-tuple-element.62), channel_id=1, source_target_pairs={{0,2},{1,3},{2,0},{3,1},{4,6},{5,7},{6,4},{7,5},{8,10},{9,11},{10,... | collective-permute-start | bytes 589832 | tf_op jit(solution)/shard_map/ppermute | solution.py:277
  79.1 16.3 %collective-permute-start.22 = (bf16[128,768]{1,0:T(8,128)(2,1)S(1)}, bf16[128,768]{1,0:T(8,128)(2,1)S(1)}, u32[]{:S(2)}, u32[]{:S(2)}) collective-permute-start(bf16[128,768]{1,0:T(8,128)(2,1)S(1)} %get-tuple-element.63), channel_id=1, source_target_pairs={{0,3},{1,2},{2,1},{3,0},{4,7},{5,6},{6,5},{7,4},{8,11},{9,10},{10,... | collective-permute-start | bytes 589832 | tf_op jit(solution)/shard_map/ppermute | solution.py:277
  84.2 4.9 %collective-permute-start.24 = (bf16[32,576]{1,0:T(8,128)(2,1)S(1)}, bf16[32,576]{1,0:T(8,128)(2,1)S(1)}, u32[]{:S(2)}, u32[]{:S(2)}) collective-permute-start(bf16[32,576]{1,0:T(8,128)(2,1)S(1)} %get-tuple-element.70), channel_id=1, source_target_pairs={{0,1},{1,0},{2,3},{3,2},{4,5},{5,4},{6,7},{7,6},{8,9},{9,8},{10,11... | collective-permute-start | bytes 110600 | tf_op jit(solution)/shard_map/ppermute | solution.py:277
  85.0 5.2 %collective-permute-start.25 = (bf16[32,576]{1,0:T(8,128)(2,1)S(1)}, bf16[32,576]{1,0:T(8,128)(2,1)S(1)}, u32[]{:S(2)}, u32[]{:S(2)}) collective-permute-start(bf16[32,576]{1,0:T(8,128)(2,1)S(1)} %get-tuple-element.71), channel_id=1, source_target_pairs={{0,2},{1,3},{2,0},{3,1},{4,6},{5,7},{6,4},{7,5},{8,10},{9,11},{10,... | collective-permute-start | bytes 110600 | tf_op jit(solution)/shard_map/ppermute | solution.py:277
  89.1 4.9 %collective-permute-start.26 = (bf16[32,576]{1,0:T(8,128)(2,1)S(1)}, bf16[32,576]{1,0:T(8,128)(2,1)S(1)}, u32[]{:S(2)}, u32[]{:S(2)}) collective-permute-start(bf16[32,576]{1,0:T(8,128)(2,1)S(1)} %get-tuple-element.72), channel_id=1, source_target_pairs={{0,3},{1,2},{2,1},{3,0},{4,7},{5,6},{6,5},{7,4},{8,11},{9,10},{10,... | collective-permute-start | bytes 110600 | tf_op jit(solution)/shard_map/ppermute | solution.py:277

commit v4 on v3

--- a/solution.py
+++ b/solution.py
@@ -82,8 +82,10 @@
 def token_pack_kernel(k, v, og, rates, gains, kv_out, gg_out, rate_out):
     tokens, feat = gg_out.shape
     rate = jnp.broadcast_to(rates[...], (feat, tokens)).T
-    kv_out[:, 0:feat] = k[0]
-    kv_out[:, feat : 2 * feat] = (rate * v[0].astype(F32)).astype(BF)
+    values = (rate * v[0].astype(F32)).astype(BF)
+    for j in range(kv_out.shape[0]):
+        kv_out[j, :, 0:feat] = k[0]
+        kv_out[j, :, feat : 2 * feat] = values
     gg_out[...] = gains[...] * og[0].astype(F32)
     rate_out[...] = rate
 
@@ -133,8 +135,8 @@
     sums[1:2, :] = jnp.sum((total * gg[...]).T, axis=0, keepdims=True)
 
 
-def delta_kernel(width, apply_out, gg, kv, *refs):
-    sums, (od_out, out) = refs[:-2], refs[-2:]
+def delta_kernel(width, apply_out, gg, *refs):
+    sums, out = refs[:-1], refs[-1]
     tokens, feat = apply_out.shape
     total = sums[0][...]
     for more in sums[1:]:
@@ -142,26 +144,29 @@
     square = jnp.broadcast_to(total[0:1, :], (feat, tokens)).T
     gain = jnp.broadcast_to(total[1:2, :], (feat, tokens)).T
     root = jnp.sqrt(square / width + EPS_ROOT)
-    delta = (gg[...] / root - apply_out[...] * (gain / width) / (root * root * root)).astype(BF)
-    od_out[...] = delta
-    out[:, 0:feat] = delta
-    out[:, feat : 3 * feat] = kv[...]
-
-
-def backward_kernel(slab, group, tok_groups, place, w, *refs):
+    out[...] = (gg[...] / root - apply_out[...] * (gain / width) / (root * root * root)).astype(BF)
+
+
+def pair_kernel(left, right, out):
+    feat = left.shape[1]
+    out[:, 0:feat] = left[...]
+    out[:, feat : 2 * feat] = right[...]
+
+
+def backward_kernel(slab, group, tok_groups, place, w, kv, *refs):
     far = group * (tok_groups - 1)
     lists = []
-    for count in (group, far, group, far, group, tok_groups):
+    for count in (group, group, far, group, tok_groups):
         lists.append(refs[:count])
         refs = refs[count:]
-    q_near, q_far, tokens, od_far, outs, homes = lists
+    q_near, od_near, pairs, outs, homes = lists
     far_q, far_od, home, ag, au, ad = refs
     mine = place[0]
     saved, init, norm_init, norm_saved, ratio, normed = normalized(w, slab)
     own, feat = q_near[0].shape
     for i in range(far):
-        far_q[i // group, i % group] = q_far[i][...]
-        far_od[i // group, i % group] = od_far[i][...]
+        far_od[i // group, i % group] = pairs[i][:, 0:feat]
+        far_q[i // group, i % group] = pairs[i][:, feat : 2 * feat]
 
     def query_side(rows, delta):
         q_gate = mm(rows, normed[0])
@@ -174,7 +179,7 @@
         grads = (mm_tn(rows, delta_gate), mm_tn(rows, delta_up), mm_tn(delta, hidden))
         return delta_gate, delta_up, grads
 
-    delta_gate, delta_up, grads = query_side(stack(q_near), stack(tokens, slice(0, feat)))
+    delta_gate, delta_up, grads = query_side(stack(q_near), stack(od_near))
     grad_q = (mm_nt(delta_gate, normed[0]) + mm_nt(delta_up, normed[1])).astype(BF)
     ag[...], au[...], ad[...] = grads
 
@@ -199,8 +204,9 @@
         direct.append((cot + init[i] * (col_dot / (norm_init[i] * norm_saved[i]))) * share)
 
     init_bf = [w[:, pl.ds((3 + i) * slab, slab)] for i in range(3)]
-    keys = stack(tokens, slice(feat, 2 * feat))
-    values = stack(tokens, slice(2 * feat, 3 * feat))
+    rank = place[1]
+    keys = jnp.concatenate([kv[rank ^ d, :, 0:feat] for d in range(group)], axis=0)
+    values = jnp.concatenate([kv[rank ^ d, :, feat : 2 * feat] for d in range(group)], axis=0)
     k_gate = mm(keys, init_bf[0])
     k_up = mm(keys, init_bf[1])
     k_proj = mm(values, init_bf[2])
@@ -272,6 +278,7 @@
 
 def make_local(seq_n, head_n, group):
     tok_groups = seq_n // group
+    groups = [[t * group + j for j in range(group)] for t in range(tok_groups)]
 
     def move(x, dist, axis="seq", size=seq_n):
         return lax.ppermute(x, axis, [(i, i ^ dist) for i in range(size)])
@@ -299,14 +306,13 @@
         packed, queries = lax.optimization_barrier((packed, q[0]))
         wall = lax.all_to_all(packed, "seq", 0, 0, tiled=True).reshape(seq_n * rows, 6 * slab)
         q_near = near_all(queries)
-        q_far = [x for m in mirror(queries) for x in near_all(m)]
         kv, gg, rate = call(
             token_pack_kernel,
-            (arr((own, 2 * feat), BF), arr((own, feat), F32), arr((own, feat), F32)),
+            (arr((group, own, 2 * feat), BF), arr((own, feat), F32), arr((own, feat), F32)),
             (k, v, og, rates, gains),
             8,
         )
-        wall, kv, *q_far = lax.optimization_barrier((wall, kv, *q_far))
+        wall, kv = lax.optimization_barrier((wall, kv))
 
         block = arr((own, feat), BF)
         parts = call(
@@ -316,20 +322,23 @@
             24,
             flops=6 * near * feat * slab,
         )
+        *parts, queries = lax.optimization_barrier((*parts, queries))
         parts = [parts[0]] + [move(parts[d], d) for d in range(1, group)]
+        q_mirror = mirror(queries)
+        parts[1], kv = lax.optimization_barrier((parts[1], kv))
+        kv = lax.all_to_all(kv, "seq", 0, 0, axis_index_groups=groups, tiled=True)
         apply_out, sums = call(
             reduce_kernel, (arr((own, feat), F32), arr((2, own), F32)), (gg, *parts), 16
         )
         sums = [sums] + [move(sums, d, "head", head_n) for d in range(1, head_n)]
-        od, tokens = call(
-            functools.partial(delta_kernel, head_n * feat),
-            (block, arr((own, 3 * feat), BF)),
-            (apply_out, gg, kv, *sums),
-            16,
-        )
+        (od,) = call(functools.partial(delta_kernel, head_n * feat), (block,), (apply_out, gg, *sums), 16)
         od_mirror = mirror(od)
-        tokens = near_all(tokens)
-        od_far = [x for m in od_mirror for x in near_all(m)]
+        od_near = near_all(od)
+        kv, *od_mirror = lax.optimization_barrier((kv, *od_mirror))
+        pairs = [
+            call(pair_kernel, (arr((own, 2 * feat), BF),), pair, 16)[0] for pair in zip(od_mirror, q_mirror)
+        ]
+        pairs = [x for m in pairs for x in near_all(m)]
 
         far = pltpu.VMEM((max(tok_groups - 1, 1), group, own, feat), BF)
         home = (group * rows, 3 * slab)
@@ -340,7 +349,7 @@
                 arr(home, F32),
                 *(arr(home, BF),) * (tok_groups - 1),
             ),
-            (place, wall, *q_near, *q_far, *tokens, *od_far),
+            (place, wall, kv, *q_near, *od_near, *pairs),
             40,
             smem=1,
             flops=66 * near * feat * slab,
@@ -362,6 +371,7 @@
             smem=1,
             scratch=[pltpu.VMEM((group, rows, 3 * slab), F32)],
         )
+        *inner, tok[1] = lax.optimization_barrier((*inner, tok[1]))
         inner = [inner[0]] + [move(inner[d], d) for d in range(1, group)]
         out_tok = arr((1, own, feat), BF)
         grad_w = arr((1, rows, hidden), F32)

time: 96.4 us -> 95.9 us (level)
  starting transfers between devices: 38.3 us -> 36.4 us
    all_to_all x1, waiting for transfers between devices: 0.01 us -> 11.4 us  [local(): lax.all_to_all(packed, 'seq', 0, 0, tiled=True)]
    ppermute x27 -> x24, waiting for transfers between devices: 47.2 us -> 36.3 us  [move(): return lax.ppermute(x, axis, [(i, i ^ dist) for i in range(size)])]
    ppermute x27 -> x24, starting transfers between devices: 30.9 us -> 25.5 us  [move(): return lax.ppermute(x, axis, [(i, i ^ dist) for i in range(size)])]
    all_to_all x0 -> x1, starting transfers between devices: none -> 3.47 us  [local(): kv = lax.all_to_all(kv, 'seq', 0, 0, axis_index_groups=groups, tiled=True)]
    pallas_call x8 -> x9, Pallas kernels: 7.78 us -> 8.62 us  [call(): pl.pallas_call(kernel, out_shape=outs, in_specs=[SMEM] * smem + [VMEM] *...]
  transfers between devices with their start and end apart: 28 -> 26, of which waited for: 17 -> 13; matrix products, arithmetic and copies ran while one was open for 0% -> 0% of each run, Pallas kernels for 2% -> 3%
where the time goes in v4:
time: 95.9 us; the launch traced here: 95.5 us
  waiting for transfers between devices  47.7 us (50%)
  starting transfers between devices  36.4 us (38%)
  Pallas kernels  10.5 us (11%)
    ppermute x24, waiting for transfers between devices, move(): return lax.ppermute(x, axis, [(i, i ^ dist) for i in range(size)])  36.3 us
    ppermute x24, starting transfers between devices, move(): return lax.ppermute(x, axis, [(i, i ^ dist) for i in range(size)])  25.5 us
    all_to_all x1, waiting for transfers between devices, local(): lax.all_to_all(packed, 'seq', 0, 0, tiled=True)  11.4 us
    pallas_call x9, Pallas kernels, call(): pl.pallas_call(kernel, out_shape=outs, in_specs=[SMEM] * smem + [VMEM] *...  8.62 us
    all_to_all x1, starting transfers between devices, local(): lax.all_to_all(packed, 'seq', 0, 0, tiled=True)  7.4 us
    all_to_all x1, starting transfers between devices, local(): kv = lax.all_to_all(kv, 'seq', 0, 0, axis_index_groups=groups, tiled=True)  3.47 us
    pallas_call x1, Pallas kernels, copying_call(): pl.pallas_call(kernel, out_shape=outs, in_specs=[pl.BlockSpec(memory_spac...  1.92 us
  transfers between devices with their start and end apart: 26, of which 13 were waited for; matrix products, arithmetic and copies ran while one was open for 0% of the time, Pallas kernels for 3%

profile of v4, /device:TPU:0, one launch (start us, length us, event | category | flops | bytes accessed | tf_op | source)
XLA Modules:
  0.0 95.5 jit_solution(9245204075094288502)
XLA Ops:
  0.6 1.9 %shard_map.164 = bf16[8,32,1152]{2,1,0:T(8,128)(2,1)} custom-call(bf16[1,32,768]{2,1,0:T(8,128)(2,1)} %refs_0_.1, bf16[1,32,768]{2,1,0:T(8,128)(2,1)} %refs_1_.1, bf16[1,32,768]{2,1,0:T(8,128)(2,1)} %refs_2_.1, bf16[1,32,768]{2,1,0:T(8,128)(2,1)} %refs_3_.1, bf16[1,32,768]{2,1,0:T(8,128)(2,1)} %refs_4_.1, bf16[1,32,768]{2,1,0:T(8,128)(2,1)} %refs_5_.1), custom_call_target="tpu_custom_call" | custom-call | tf_op jit(solution)/shard_map/pallas_call | solution.py:60
  2.6 0.0 copy-start.3
  2.6 0.0 copy-start
  2.6 0.0 copy-start.1
  2.6 0.0 copy-start.2
  2.6 0.0 copy-start.4
  2.6 0.0 copy-start.5
  2.6 7.4 %all-to-all-start = ((bf16[8,32,1152]{2,1,0:T(8,128)(2,1)}), bf16[8,32,1152]{2,1,0:T(8,128)(2,1)S(1)}, u32[]{:S(2)}, u32[]{:S(2)}) async-start(bf16[8,32,1152]{2,1,0:T(8,128)(2,1)} %shard_map.164), calls=%async_computation | async-start | bytes 1179648 | tf_op jit(solution)/shard_map/all_to_all | solution.py:307
  10.0 2.9 %collective-permute-start.2 = (bf16[128,256]{1,0:T(8,128)(2,1)S(1)}, bf16[128,256]{1,0:T(8,128)(2,1)S(1)}, u32[]{:S(2)}, u32[]{:S(2)}) collective-permute-start(bf16[128,256]{1,0:T(8,128)(2,1)S(1)} %bitcast.7), channel_id=1, source_target_pairs={{0,3},{1,2},{2,1},{3,0},{4,7},{5,6},{6,5},{7,4},{8,11},{9,10},{10,... | collective-permute-start | bytes 196616 | tf_op jit(solution)/shard_map/ppermute | solution.py:284
  13.0 0.6 collective-permute-start.1
  13.5 0.1 collective-permute-start
  13.6 0.9 shard_map.163
  14.5 11.4 %all-to-all-done = bf16[8,32,1152]{2,1,0:T(8,128)(2,1)S(1)} async-done(((bf16[8,32,1152]{2,1,0:T(8,128)(2,1)}), bf16[8,32,1152]{2,1,0:T(8,128)(2,1)S(1)}, u32[]{:S(2)}, u32[]{:S(2)}) %all-to-all-start) | async-done | bytes 589856 | tf_op jit(solution)/shard_map/all_to_all | solution.py:307
  25.9 0.0 collective-permute-done.2.refs_3_
  25.9 0.0 collective-permute-done.1.refs_2_
  25.9 0.0 collective-permute-done.refs_1_
  25.9 0.8 shard_map.165
  26.7 1.5 %collective-permute-start.3 = (bf16[128,256]{1,0:T(8,128)(2,1)S(1)}, bf16[128,256]{1,0:T(8,128)(2,1)S(1)}, u32[]{:S(2)}, u32[]{:S(2)}) collective-permute-start(bf16[128,256]{1,0:T(8,128)(2,1)S(1)} %get-tuple-element.58), channel_id=1, source_target_pairs={{0,1},{1,0},{2,3},{3,2},{4,5},{5,4},{6,7},{7,6},{8,9},{9,8},{10,11... | collective-permute-start | bytes 196616 | tf_op jit(solution)/shard_map/ppermute | solution.py:284
  28.2 2.8 %collective-permute-done.3.refs_1_ = bf16[128,256]{1,0:T(8,128)(2,1)S(1)} collective-permute-done((bf16[128,256]{1,0:T(8,128)(2,1)S(1)}, bf16[128,256]{1,0:T(8,128)(2,1)S(1)}, u32[]{:S(2)}, u32[]{:S(2)}) %collective-permute-start.3) | collective-permute-done | bytes 65568 | tf_op jit(solution)/shard_map/ppermute | solution.py:284
  31.0 3.5 %all-to-all-start.1 = ((bf16[4,128,512]{2,1,0:T(8,128)(2,1)}), bf16[4,128,512]{2,1,0:T(8,128)(2,1)S(1)}, u32[]{:S(2)}, u32[]{:S(2)}) async-start(bf16[4,128,512]{2,1,0:T(8,128)(2,1)} %get-tuple-element.60), calls=%async_computation.1 | async-start | bytes 1048576 | tf_op jit(solution)/shard_map/all_to_all | solution.py:329
  34.5 2.0 %collective-permute-start.4 = (bf16[128,256]{1,0:T(8,128)(2,1)S(1)}, bf16[128,256]{1,0:T(8,128)(2,1)S(1)}, u32[]{:S(2)}, u32[]{:S(2)}) collective-permute-start(bf16[128,256]{1,0:T(8,128)(2,1)S(1)} %get-tuple-element.64), channel_id=1, source_target_pairs={{0,2},{1,3},{2,0},{3,1},{4,6},{5,7},{6,4},{7,5},{8,10},{9,11},{10,... | collective-permute-start | bytes 196616 | tf_op jit(solution)/shard_map/ppermute | solution.py:284
  36.5 1.5 %collective-permute-start.5 = (bf16[128,256]{1,0:T(8,128)(2,1)S(1)}, bf16[128,256]{1,0:T(8,128)(2,1)S(1)}, u32[]{:S(2)}, u32[]{:S(2)}) collective-permute-start(bf16[128,256]{1,0:T(8,128)(2,1)S(1)} %get-tuple-element.65), channel_id=1, source_target_pairs={{0,3},{1,2},{2,1},{3,0},{4,7},{5,6},{6,5},{7,4},{8,11},{9,10},{10,... | collective-permute-start | bytes 196616 | tf_op jit(solution)/shard_map/ppermute | solution.py:284
  38.0 4.4 %collective-permute-done.4.refs_2_ = bf16[128,256]{1,0:T(8,128)(2,1)S(1)} collective-permute-done((bf16[128,256]{1,0:T(8,128)(2,1)S(1)}, bf16[128,256]{1,0:T(8,128)(2,1)S(1)}, u32[]{:S(2)}, u32[]{:S(2)}) %collective-permute-start.4) | collective-permute-done | bytes 65568 | tf_op jit(solution)/shard_map/ppermute | solution.py:284
  42.4 1.6 %collective-permute-done.5.refs_3_ = bf16[128,256]{1,0:T(8,128)(2,1)S(1)} collective-permute-done((bf16[128,256]{1,0:T(8,128)(2,1)S(1)}, bf16[128,256]{1,0:T(8,128)(2,1)S(1)}, u32[]{:S(2)}, u32[]{:S(2)}) %collective-permute-start.5) | collective-permute-done | bytes 65568 | tf_op jit(solution)/shard_map/ppermute | solution.py:284
  44.0 0.1 shard_map.166
  44.1 0.1 collective-permute-start.8
  44.2 1.6 %collective-permute-start.7 = (f32[2,128]{1,0:T(2,128)S(1)}, f32[2,128]{1,0:T(2,128)S(1)}, u32[]{:S(2)}, u32[]{:S(2)}) collective-permute-start(f32[2,128]{1,0:T(2,128)S(1)} %get-tuple-element.67.refs_0_), channel_id=1, source_target_pairs={{0,16},{8,24},{16,0},{24,8},{1,17},{9,25},{17,1},{25,9},{2,18},{10... | collective-permute-start | bytes 3080 | tf_op jit(solution)/shard_map/ppermute | solution.py:284
  45.8 0.3 collective-permute-start.6
  46.0 1.1 %collective-permute-done.8.refs_3_ = f32[2,128]{1,0:T(2,128)S(1)} collective-permute-done((f32[2,128]{1,0:T(2,128)S(1)}, f32[2,128]{1,0:T(2,128)S(1)}, u32[]{:S(2)}, u32[]{:S(2)}) %collective-permute-start.8) | collective-permute-done | bytes 1056 | tf_op jit(solution)/shard_map/ppermute | solution.py:284
  47.2 0.7 collective-permute-done.7.refs_2_
  47.8 0.0 collective-permute-done.6.refs_1_
  47.8 0.1 shard_map.167.refs_4_
  48.0 2.1 %collective-permute-start.9 = (bf16[128,256]{1,0:T(8,128)(2,1)S(1)}, bf16[128,256]{1,0:T(8,128)(2,1)S(1)}, u32[]{:S(2)}, u32[]{:S(2)}) collective-permute-start(bf16[128,256]{1,0:T(8,128)(2,1)S(1)} %shard_map.167.refs_4_), channel_id=1, source_target_pairs={{0,4},{1,5},{2,6},{3,7},{4,0},{5,1},{6,2},{7,3},{8,12},{9,13},{10,... | collective-permute-start | bytes 196616 | tf_op jit(solution)/shard_map/ppermute | solution.py:284
  50.1 0.9 collective-permute-start.13
  51.0 0.2 collective-permute-start.12
  51.2 5.0 %collective-permute-done.9.left = bf16[128,256]{1,0:T(8,128)(2,1)S(1)} collective-permute-done((bf16[128,256]{1,0:T(8,128)(2,1)S(1)}, bf16[128,256]{1,0:T(8,128)(2,1)S(1)}, u32[]{:S(2)}, u32[]{:S(2)}) %collective-permute-start.9) | collective-permute-done | bytes 65568 | tf_op jit(solution)/shard_map/ppermute | solution.py:284
  56.2 0.0 all-to-all-done.1.kv
  56.2 1.4 %collective-permute-done.13.right = bf16[128,256]{1,0:T(8,128)(2,1)S(1)} collective-permute-done((bf16[128,256]{1,0:T(8,128)(2,1)S(1)}, bf16[128,256]{1,0:T(8,128)(2,1)S(1)}, u32[]{:S(2)}, u32[]{:S(2)}) %collective-permute-start.13) | collective-permute-done | bytes 65568 | tf_op jit(solution)/shard_map/ppermute | solution.py:284
  57.5 0.1 collective-permute-start.16
  57.6 1.8 %collective-permute-start.15 = (bf16[128,512]{1,0:T(8,128)(2,1)S(1)}, bf16[128,512]{1,0:T(8,128)(2,1)S(1)}, u32[]{:S(2)}, u32[]{:S(2)}) collective-permute-start(bf16[128,512]{1,0:T(8,128)(2,1)S(1)} %shard_map.168.refs_8_), channel_id=1, source_target_pairs={{0,2},{1,3},{2,0},{3,1},{4,6},{5,7},{6,4},{7,5},{8,10},{9,11},{10,... | collective-permute-start | bytes 393224 | tf_op jit(solution)/shard_map/ppermute | solution.py:284
  59.4 1.7 %collective-permute-start.14 = (bf16[128,512]{1,0:T(8,128)(2,1)S(1)}, bf16[128,512]{1,0:T(8,128)(2,1)S(1)}, u32[]{:S(2)}, u32[]{:S(2)}) collective-permute-start(bf16[128,512]{1,0:T(8,128)(2,1)S(1)} %shard_map.168.refs_8_), channel_id=1, source_target_pairs={{0,1},{1,0},{2,3},{3,2},{4,5},{5,4},{6,7},{7,6},{8,9},{9,8},{10,11... | collective-permute-start | bytes 393224 | tf_op jit(solution)/shard_map/ppermute | solution.py:284
  61.1 0.0 collective-permute-start.11
  61.1 0.0 collective-permute-done.12.refs_7_
  61.1 0.6 collective-permute-start.10
  61.7 0.1 pad_add_fusion.place
  61.8 5.2 %collective-permute-done.11.refs_6_ = bf16[128,256]{1,0:T(8,128)(2,1)S(1)} collective-permute-done((bf16[128,256]{1,0:T(8,128)(2,1)S(1)}, bf16[128,256]{1,0:T(8,128)(2,1)S(1)}, u32[]{:S(2)}, u32[]{:S(2)}) %collective-permute-start.11) | collective-permute-done | bytes 65568 | tf_op jit(solution)/shard_map/ppermute | solution.py:284
  67.0 1.1 %collective-permute-done.10.refs_5_ = bf16[128,256]{1,0:T(8,128)(2,1)S(1)} collective-permute-done((bf16[128,256]{1,0:T(8,128)(2,1)S(1)}, bf16[128,256]{1,0:T(8,128)(2,1)S(1)}, u32[]{:S(2)}, u32[]{:S(2)}) %collective-permute-start.10) | collective-permute-done | bytes 65568 | tf_op jit(solution)/shard_map/ppermute | solution.py:284
  68.2 0.0 collective-permute-done.16.refs_11_
  68.2 0.0 collective-permute-done.15.refs_10_
  68.2 0.0 collective-permute-done.14.refs_9_
  68.2 3.9 %shard_map.169 = (bf16[128,768]{1,0:T(8,128)(2,1)S(1)}, bf16[128,768]{1,0:T(8,128)(2,1)S(1)}, bf16[128,768]{1,0:T(8,128)(2,1)S(1)}, bf16[128,768]{1,0:T(8,128)(2...) custom-call(s32[3]{0:T(128)S(1)} %pad_add_fusion.place, bf16[256,1152]{1,0:T(8,128)(2,1)S(1)} %bitcast.6, ...), custom_call_target="tpu_custom_call" | custom-call | flops 1660944384 | bytes 3391500 | tf_op jit(solution)/shard_map/pallas_call | solution.py:48
  72.1 0.6 collective-permute-start.18
  72.8 0.3 collective-permute-start.19
  73.1 2.6 %collective-permute-start.20 = (bf16[128,768]{1,0:T(8,128)(2,1)S(1)}, bf16[128,768]{1,0:T(8,128)(2,1)S(1)}, u32[]{:S(2)}, u32[]{:S(2)}) collective-permute-start(bf16[128,768]{1,0:T(8,128)(2,1)S(1)} %get-tuple-element.81), channel_id=1, source_target_pairs={{0,3},{1,2},{2,1},{3,0},{4,7},{5,6},{6,5},{7,4},{8,11},{9,10},{10,... | collective-permute-start | bytes 589832 | tf_op jit(solution)/shard_map/ppermute | solution.py:284
  75.7 0.2 collective-permute-start.17
  75.9 8.8 %collective-permute-done.17.refs_1_ = bf16[128,576]{1,0:T(8,128)(2,1)S(1)} collective-permute-done((bf16[128,576]{1,0:T(8,128)(2,1)S(1)}, bf16[128,576]{1,0:T(8,128)(2,1)S(1)}, u32[]{:S(2)}, u32[]{:S(2)}) %collective-permute-start.17) | collective-permute-done | bytes 147488 | tf_op jit(solution)/shard_map/ppermute | solution.py:284
  84.7 0.6 shard_map.170
  85.3 1.6 %collective-permute-start.21 = (bf16[32,576]{1,0:T(8,128)(2,1)S(1)}, bf16[32,576]{1,0:T(8,128)(2,1)S(1)}, u32[]{:S(2)}, u32[]{:S(2)}) collective-permute-start(bf16[32,576]{1,0:T(8,128)(2,1)S(1)} %get-tuple-element.86), channel_id=1, source_target_pairs={{0,1},{1,0},{2,3},{3,2},{4,5},{5,4},{6,7},{7,6},{8,9},{9,8},{10,11... | collective-permute-start | bytes 110600 | tf_op jit(solution)/shard_map/ppermute | solution.py:284
  87.0 2.3 %collective-permute-start.22 = (bf16[32,576]{1,0:T(8,128)(2,1)S(1)}, bf16[32,576]{1,0:T(8,128)(2,1)S(1)}, u32[]{:S(2)}, u32[]{:S(2)}) collective-permute-start(bf16[32,576]{1,0:T(8,128)(2,1)S(1)} %get-tuple-element.87), channel_id=1, source_target_pairs={{0,2},{1,3},{2,0},{3,1},{4,6},{5,7},{6,4},{7,5},{8,10},{9,11},{10,... | collective-permute-start | bytes 110600 | tf_op jit(solution)/shard_map/ppermute | solution.py:284
  89.3 0.7 shard_map.171
  90.0 0.0 collective-permute-done.21.refs_1_
  90.0 1.2 %collective-permute-done.22.refs_2_ = bf16[32,576]{1,0:T(8,128)(2,1)S(1)} collective-permute-done((bf16[32,576]{1,0:T(8,128)(2,1)S(1)}, bf16[32,576]{1,0:T(8,128)(2,1)S(1)}, u32[]{:S(2)}, u32[]{:S(2)}) %collective-permute-start.22) | collective-permute-done | bytes 36896 | tf_op jit(solution)/shard_map/ppermute | solution.py:284
  91.2 2.9 %collective-permute-done.23.refs_3_ = bf16[32,576]{1,0:T(8,128)(2,1)S(1)} collective-permute-done((bf16[32,576]{1,0:T(8,128)(2,1)S(1)}, bf16[32,576]{1,0:T(8,128)(2,1)S(1)}, u32[]{:S(2)}, u32[]{:S(2)}) %collective-permute-start.23) | collective-permute-done | bytes 36896 | tf_op jit(solution)/shard_map/ppermute | solution.py:284
  94.2 1.4 %shard_map.172 = (f32[1,32,768]{2,1,0:T(8,128)}, f32[1,32,768]{2,1,0:T(8,128)}, f32[1,32,768]{2,1,0:T(8,128)}) custom-call(s32[3]{0:T(128)S(1)} %pad_add_fusion.place, bf16[32,576]{1,0:T(8,128)(2,1)S(1)} %get-tuple-element.85.refs_0_, bf16[32,576]{1,0:T(8,128)(2,1)S(1)} %collective-permute-done.21.refs_1_, ...), custom_call_target="tpu_custom_call" | custom-call | bytes 442380 | tf_op jit(solution)/shard_map/pallas_call | solution.py:48
  (11 shorter events, 0.0 us)
Async XLA Ops:
  2.6 7.5 %copy-start.3 = (bf16[1,128,256]{2,1,0:T(8,128)(2,1)S(1)}, bf16[1,128,256]{2,1,0:T(8,128)(2,1)}, u32[]{:S(2)}) copy-start(bf16[1,128,256]{2,1,0:T(8,128)(2,1)} %param.12) | copy-start | bytes 196612
  2.6 11.0 %copy-start = (bf16[1,128,256]{2,1,0:T(8,128)(2,1)S(1)}, bf16[1,128,256]{2,1,0:T(8,128)(2,1)}, u32[]{:S(2)}) copy-start(bf16[1,128,256]{2,1,0:T(8,128)(2,1)} %k.1) | copy-start | bytes 196612
  2.6 11.0 %copy-start.1 = (bf16[1,128,256]{2,1,0:T(8,128)(2,1)S(1)}, bf16[1,128,256]{2,1,0:T(8,128)(2,1)}, u32[]{:S(2)}) copy-start(bf16[1,128,256]{2,1,0:T(8,128)(2,1)} %v.1) | copy-start | bytes 196612
  2.6 11.0 %copy-start.2 = (bf16[1,128,256]{2,1,0:T(8,128)(2,1)S(1)}, bf16[1,128,256]{2,1,0:T(8,128)(2,1)}, u32[]{:S(2)}) copy-start(bf16[1,128,256]{2,1,0:T(8,128)(2,1)} %og.1) | copy-start | bytes 196612
  2.6 11.0 %copy-start.4 = (f32[1,256]{1,0:T(1,128)S(1)}, f32[1,256]{1,0:T(1,128)}, u32[]{:S(2)}) copy-start(f32[1,256]{1,0:T(1,128)} %gains.1) | copy-start | bytes 3076
  2.6 11.0 %copy-start.5 = (f32[1,128]{1,0:T(1,128)S(1)}, f32[1,128]{1,0:T(1,128)}, u32[]{:S(2)}) copy-start(f32[1,128]{1,0:T(1,128)} %rates.1) | copy-start | bytes 1540
  2.6 23.3 %all-to-all-start = ((bf16[8,32,1152]{2,1,0:T(8,128)(2,1)}), bf16[8,32,1152]{2,1,0:T(8,128)(2,1)S(1)}, u32[]{:S(2)}, u32[]{:S(2)}) async-start(bf16[8,32,1152]{2,1,0:T(8,128)(2,1)} %shard_map.164), calls=%async_computation | async-start | bytes 1179648 | tf_op jit(solution)/shard_map/all_to_all | solution.py:307
  10.0 15.9 %collective-permute-start.2 = (bf16[128,256]{1,0:T(8,128)(2,1)S(1)}, bf16[128,256]{1,0:T(8,128)(2,1)S(1)}, u32[]{:S(2)}, u32[]{:S(2)}) collective-permute-start(bf16[128,256]{1,0:T(8,128)(2,1)S(1)} %bitcast.7), channel_id=1, source_target_pairs={{0,3},{1,2},{2,1},{3,0},{4,7},{5,6},{6,5},{7,4},{8,11},{9,10},{10,... | collective-permute-start | bytes 196616 | tf_op jit(solution)/shard_map/ppermute | solution.py:284
  13.0 13.0 %collective-permute-start.1 = (bf16[128,256]{1,0:T(8,128)(2,1)S(1)}, bf16[128,256]{1,0:T(8,128)(2,1)S(1)}, u32[]{:S(2)}, u32[]{:S(2)}) collective-permute-start(bf16[128,256]{1,0:T(8,128)(2,1)S(1)} %bitcast.8), channel_id=1, source_target_pairs={{0,2},{1,3},{2,0},{3,1},{4,6},{5,7},{6,4},{7,5},{8,10},{9,11},{10,... | collective-permute-start | bytes 196616 | tf_op jit(solution)/shard_map/ppermute | solution.py:284
  13.5 12.4 %collective-permute-start = (bf16[128,256]{1,0:T(8,128)(2,1)S(1)}, bf16[128,256]{1,0:T(8,128)(2,1)S(1)}, u32[]{:S(2)}, u32[]{:S(2)}) collective-permute-start(bf16[128,256]{1,0:T(8,128)(2,1)S(1)} %bitcast.9), channel_id=1, source_target_pairs={{0,1},{1,0},{2,3},{3,2},{4,5},{5,4},{6,7},{7,6},{8,9},{9,8},{10,11... | collective-permute-start | bytes 196616 | tf_op jit(solution)/shard_map/ppermute | solution.py:284
  26.7 4.3 %collective-permute-start.3 = (bf16[128,256]{1,0:T(8,128)(2,1)S(1)}, bf16[128,256]{1,0:T(8,128)(2,1)S(1)}, u32[]{:S(2)}, u32[]{:S(2)}) collective-permute-start(bf16[128,256]{1,0:T(8,128)(2,1)S(1)} %get-tuple-element.58), channel_id=1, source_target_pairs={{0,1},{1,0},{2,3},{3,2},{4,5},{5,4},{6,7},{7,6},{8,9},{9,8},{10,11... | collective-permute-start | bytes 196616 | tf_op jit(solution)/shard_map/ppermute | solution.py:284
  31.0 25.1 %all-to-all-start.1 = ((bf16[4,128,512]{2,1,0:T(8,128)(2,1)}), bf16[4,128,512]{2,1,0:T(8,128)(2,1)S(1)}, u32[]{:S(2)}, u32[]{:S(2)}) async-start(bf16[4,128,512]{2,1,0:T(8,128)(2,1)} %get-tuple-element.60), calls=%async_computation.1 | async-start | bytes 1048576 | tf_op jit(solution)/shard_map/all_to_all | solution.py:329
  34.5 7.8 %collective-permute-start.4 = (bf16[128,256]{1,0:T(8,128)(2,1)S(1)}, bf16[128,256]{1,0:T(8,128)(2,1)S(1)}, u32[]{:S(2)}, u32[]{:S(2)}) collective-permute-start(bf16[128,256]{1,0:T(8,128)(2,1)S(1)} %get-tuple-element.64), channel_id=1, source_target_pairs={{0,2},{1,3},{2,0},{3,1},{4,6},{5,7},{6,4},{7,5},{8,10},{9,11},{10,... | collective-permute-start | bytes 196616 | tf_op jit(solution)/shard_map/ppermute | solution.py:284
  36.5 7.5 %collective-permute-start.5 = (bf16[128,256]{1,0:T(8,128)(2,1)S(1)}, bf16[128,256]{1,0:T(8,128)(2,1)S(1)}, u32[]{:S(2)}, u32[]{:S(2)}) collective-permute-start(bf16[128,256]{1,0:T(8,128)(2,1)S(1)} %get-tuple-element.65), channel_id=1, source_target_pairs={{0,3},{1,2},{2,1},{3,0},{4,7},{5,6},{6,5},{7,4},{8,11},{9,10},{10,... | collective-permute-start | bytes 196616 | tf_op jit(solution)/shard_map/ppermute | solution.py:284
  44.1 3.1 %collective-permute-start.8 = (f32[2,128]{1,0:T(2,128)S(1)}, f32[2,128]{1,0:T(2,128)S(1)}, u32[]{:S(2)}, u32[]{:S(2)}) collective-permute-start(f32[2,128]{1,0:T(2,128)S(1)} %get-tuple-element.67.refs_0_), channel_id=1, source_target_pairs={{0,24},{8,16},{16,8},{24,0},{1,25},{9,17},{17,9},{25,1},{2,26},{10... | collective-permute-start | bytes 3080 | tf_op jit(solution)/shard_map/ppermute | solution.py:284
  44.2 3.6 %collective-permute-start.7 = (f32[2,128]{1,0:T(2,128)S(1)}, f32[2,128]{1,0:T(2,128)S(1)}, u32[]{:S(2)}, u32[]{:S(2)}) collective-permute-start(f32[2,128]{1,0:T(2,128)S(1)} %get-tuple-element.67.refs_0_), channel_id=1, source_target_pairs={{0,16},{8,24},{16,0},{24,8},{1,17},{9,25},{17,1},{25,9},{2,18},{10... | collective-permute-start | bytes 3080 | tf_op jit(solution)/shard_map/ppermute | solution.py:284
  45.8 2.1 %collective-permute-start.6 = (f32[2,128]{1,0:T(2,128)S(1)}, f32[2,128]{1,0:T(2,128)S(1)}, u32[]{:S(2)}, u32[]{:S(2)}) collective-permute-start(f32[2,128]{1,0:T(2,128)S(1)} %get-tuple-element.67.refs_0_), channel_id=1, source_target_pairs={{0,8},{8,0},{16,24},{24,16},{1,9},{9,1},{17,25},{25,17},{2,10},{10... | collective-permute-start | bytes 3080 | tf_op jit(solution)/shard_map/ppermute | solution.py:284
  48.0 8.2 %collective-permute-start.9 = (bf16[128,256]{1,0:T(8,128)(2,1)S(1)}, bf16[128,256]{1,0:T(8,128)(2,1)S(1)}, u32[]{:S(2)}, u32[]{:S(2)}) collective-permute-start(bf16[128,256]{1,0:T(8,128)(2,1)S(1)} %shard_map.167.refs_4_), channel_id=1, source_target_pairs={{0,4},{1,5},{2,6},{3,7},{4,0},{5,1},{6,2},{7,3},{8,12},{9,13},{10,... | collective-permute-start | bytes 196616 | tf_op jit(solution)/shard_map/ppermute | solution.py:284
  50.1 7.5 %collective-permute-start.13 = (bf16[128,256]{1,0:T(8,128)(2,1)S(1)}, bf16[128,256]{1,0:T(8,128)(2,1)S(1)}, u32[]{:S(2)}, u32[]{:S(2)}) collective-permute-start(bf16[128,256]{1,0:T(8,128)(2,1)S(1)} %bitcast.11), channel_id=1, source_target_pairs={{0,4},{1,5},{2,6},{3,7},{4,0},{5,1},{6,2},{7,3},{8,12},{9,13},{10,... | collective-permute-start | bytes 196616 | tf_op jit(solution)/shard_map/ppermute | solution.py:284
  51.0 10.1 %collective-permute-start.12 = (bf16[128,256]{1,0:T(8,128)(2,1)S(1)}, bf16[128,256]{1,0:T(8,128)(2,1)S(1)}, u32[]{:S(2)}, u32[]{:S(2)}) collective-permute-start(bf16[128,256]{1,0:T(8,128)(2,1)S(1)} %shard_map.167.refs_4_), channel_id=1, source_target_pairs={{0,3},{1,2},{2,1},{3,0},{4,7},{5,6},{6,5},{7,4},{8,11},{9,10},{10,... | collective-permute-start | bytes 196616 | tf_op jit(solution)/shard_map/ppermute | solution.py:284
  57.5 10.6 %collective-permute-start.16 = (bf16[128,512]{1,0:T(8,128)(2,1)S(1)}, bf16[128,512]{1,0:T(8,128)(2,1)S(1)}, u32[]{:S(2)}, u32[]{:S(2)}) collective-permute-start(bf16[128,512]{1,0:T(8,128)(2,1)S(1)} %shard_map.168.refs_8_), channel_id=1, source_target_pairs={{0,3},{1,2},{2,1},{3,0},{4,7},{5,6},{6,5},{7,4},{8,11},{9,10},{10,... | collective-permute-start | bytes 393224 | tf_op jit(solution)/shard_map/ppermute | solution.py:284
  57.6 10.6 %collective-permute-start.15 = (bf16[128,512]{1,0:T(8,128)(2,1)S(1)}, bf16[128,512]{1,0:T(8,128)(2,1)S(1)}, u32[]{:S(2)}, u32[]{:S(2)}) collective-permute-start(bf16[128,512]{1,0:T(8,128)(2,1)S(1)} %shard_map.168.refs_8_), channel_id=1, source_target_pairs={{0,2},{1,3},{2,0},{3,1},{4,6},{5,7},{6,4},{7,5},{8,10},{9,11},{10,... | collective-permute-start | bytes 393224 | tf_op jit(solution)/shard_map/ppermute | solution.py:284
  59.4 8.8 %collective-permute-start.14 = (bf16[128,512]{1,0:T(8,128)(2,1)S(1)}, bf16[128,512]{1,0:T(8,128)(2,1)S(1)}, u32[]{:S(2)}, u32[]{:S(2)}) collective-permute-start(bf16[128,512]{1,0:T(8,128)(2,1)S(1)} %shard_map.168.refs_8_), channel_id=1, source_target_pairs={{0,1},{1,0},{2,3},{3,2},{4,5},{5,4},{6,7},{7,6},{8,9},{9,8},{10,11... | collective-permute-start | bytes 393224 | tf_op jit(solution)/shard_map/ppermute | solution.py:284
  61.1 5.9 %collective-permute-start.11 = (bf16[128,256]{1,0:T(8,128)(2,1)S(1)}, bf16[128,256]{1,0:T(8,128)(2,1)S(1)}, u32[]{:S(2)}, u32[]{:S(2)}) collective-permute-start(bf16[128,256]{1,0:T(8,128)(2,1)S(1)} %shard_map.167.refs_4_), channel_id=1, source_target_pairs={{0,2},{1,3},{2,0},{3,1},{4,6},{5,7},{6,4},{7,5},{8,10},{9,11},{10,... | collective-permute-start | bytes 196616 | tf_op jit(solution)/shard_map/ppermute | solution.py:284
  61.1 7.1 %collective-permute-start.10 = (bf16[128,256]{1,0:T(8,128)(2,1)S(1)}, bf16[128,256]{1,0:T(8,128)(2,1)S(1)}, u32[]{:S(2)}, u32[]{:S(2)}) collective-permute-start(bf16[128,256]{1,0:T(8,128)(2,1)S(1)} %shard_map.167.refs_4_), channel_id=1, source_target_pairs={{0,1},{1,0},{2,3},{3,2},{4,5},{5,4},{6,7},{7,6},{8,9},{9,8},{10,11... | collective-permute-start | bytes 196616 | tf_op jit(solution)/shard_map/ppermute | solution.py:284
  72.1 13.2 %collective-permute-start.18 = (bf16[128,768]{1,0:T(8,128)(2,1)S(1)}, bf16[128,768]{1,0:T(8,128)(2,1)S(1)}, u32[]{:S(2)}, u32[]{:S(2)}) collective-permute-start(bf16[128,768]{1,0:T(8,128)(2,1)S(1)} %get-tuple-element.78), channel_id=1, source_target_pairs={{0,1},{1,0},{2,3},{3,2},{4,5},{5,4},{6,7},{7,6},{8,9},{9,8},{10,11... | collective-permute-start | bytes 589832 | tf_op jit(solution)/shard_map/ppermute | solution.py:284
  72.8 16.5 %collective-permute-start.19 = (bf16[128,768]{1,0:T(8,128)(2,1)S(1)}, bf16[128,768]{1,0:T(8,128)(2,1)S(1)}, u32[]{:S(2)}, u32[]{:S(2)}) collective-permute-start(bf16[128,768]{1,0:T(8,128)(2,1)S(1)} %get-tuple-element.80), channel_id=1, source_target_pairs={{0,2},{1,3},{2,0},{3,1},{4,6},{5,7},{6,4},{7,5},{8,10},{9,11},{10,... | collective-permute-start | bytes 589832 | tf_op jit(solution)/shard_map/ppermute | solution.py:284
  73.1 16.2 %collective-permute-start.20 = (bf16[128,768]{1,0:T(8,128)(2,1)S(1)}, bf16[128,768]{1,0:T(8,128)(2,1)S(1)}, u32[]{:S(2)}, u32[]{:S(2)}) collective-permute-start(bf16[128,768]{1,0:T(8,128)(2,1)S(1)} %get-tuple-element.81), channel_id=1, source_target_pairs={{0,3},{1,2},{2,1},{3,0},{4,7},{5,6},{6,5},{7,4},{8,11},{9,10},{10,... | collective-permute-start | bytes 589832 | tf_op jit(solution)/shard_map/ppermute | solution.py:284
  75.7 9.0 %collective-permute-start.17 = (bf16[128,576]{1,0:T(8,128)(2,1)S(1)}, bf16[128,576]{1,0:T(8,128)(2,1)S(1)}, u32[]{:S(2)}, u32[]{:S(2)}) collective-permute-start(bf16[128,576]{1,0:T(8,128)(2,1)S(1)} %get-tuple-element.73), channel_id=1, source_target_pairs={{0,4},{1,5},{2,6},{3,7},{4,0},{5,1},{6,2},{7,3},{8,12},{9,13},{10,... | collective-permute-start | bytes 442376 | tf_op jit(solution)/shard_map/ppermute | solution.py:284
  85.3 4.7 %collective-permute-start.21 = (bf16[32,576]{1,0:T(8,128)(2,1)S(1)}, bf16[32,576]{1,0:T(8,128)(2,1)S(1)}, u32[]{:S(2)}, u32[]{:S(2)}) collective-permute-start(bf16[32,576]{1,0:T(8,128)(2,1)S(1)} %get-tuple-element.86), channel_id=1, source_target_pairs={{0,1},{1,0},{2,3},{3,2},{4,5},{5,4},{6,7},{7,6},{8,9},{9,8},{10,11... | collective-permute-start | bytes 110600 | tf_op jit(solution)/shard_map/ppermute | solution.py:284
  87.0 4.3 %collective-permute-start.22 = (bf16[32,576]{1,0:T(8,128)(2,1)S(1)}, bf16[32,576]{1,0:T(8,128)(2,1)S(1)}, u32[]{:S(2)}, u32[]{:S(2)}) collective-permute-start(bf16[32,576]{1,0:T(8,128)(2,1)S(1)} %get-tuple-element.87), channel_id=1, source_target_pairs={{0,2},{1,3},{2,0},{3,1},{4,6},{5,7},{6,4},{7,5},{8,10},{9,11},{10,... | collective-permute-start | bytes 110600 | tf_op jit(solution)/shard_map/ppermute | solution.py:284
  89.3 4.9 %collective-permute-start.23 = (bf16[32,576]{1,0:T(8,128)(2,1)S(1)}, bf16[32,576]{1,0:T(8,128)(2,1)S(1)}, u32[]{:S(2)}, u32[]{:S(2)}) collective-permute-start(bf16[32,576]{1,0:T(8,128)(2,1)S(1)} %get-tuple-element.88), channel_id=1, source_target_pairs={{0,3},{1,2},{2,1},{3,0},{4,7},{5,6},{6,5},{7,4},{8,11},{9,10},{10,... | collective-permute-start | bytes 110600 | tf_op jit(solution)/shard_map/ppermute | solution.py:284

commit v5 on v4

v5 whole, which is shorter than its diff:
```python
import functools

import jax
import jax.numpy as jnp
from jax import lax
from jax.experimental import pallas as pl
from jax.experimental.pallas import tpu as pltpu
from jax.sharding import PartitionSpec as P

EPS_COL = 1e-06
EPS_ROOT = 1e-05
BF = jnp.bfloat16
F32 = jnp.float32
VMEM = pl.BlockSpec(memory_space=pltpu.VMEM)
SMEM = pl.BlockSpec(memory_space=pltpu.SMEM)


def silu_parts(pre_act):
    sigmoid_val = jax.nn.sigmoid(pre_act)
    silu_val = pre_act * sigmoid_val
    silu_slope = sigmoid_val * (1.0 + pre_act * (1.0 - sigmoid_val))
    silu_bend = sigmoid_val * (1.0 - sigmoid_val) * (2.0 + pre_act * (1.0 - 2.0 * sigmoid_val))
    return (silu_val, silu_slope, silu_bend)


def mm(left_op, right_op):
    return jnp.dot(left_op, right_op, preferred_element_type=F32)


def mm_nt(left_op, right_op):
    return lax.dot_general(left_op, right_op, (((1,), (1,)), ((), ())), preferred_element_type=F32)


def mm_tn(left_op, right_op):
    return lax.dot_general(left_op, right_op, (((0,), (0,)), ((), ())), preferred_element_type=F32)


def column_norm(weight):
    return jnp.sqrt(jnp.sum(weight * weight, axis=0, keepdims=True) + EPS_COL)


def flat(x):
    return x.reshape(-1, x.shape[-1])


def call(kernel, outs, args, mib, smem=0, flops=0, scratch=()):
    moved = sum(x.size * x.dtype.itemsize for x in (*args, *outs))
    return pl.pallas_call(
        kernel,
        out_shape=outs,
        in_specs=[SMEM] * smem + [VMEM] * (len(args) - smem),
        out_specs=[VMEM] * len(outs),
        scratch_shapes=scratch,
        compiler_params=pltpu.CompilerParams(vmem_limit_bytes=mib << 20),
        cost_estimate=pl.CostEstimate(flops=flops, bytes_accessed=moved, transcendentals=0),
    )(*args)


def copying_call(kernel, outs, args, buffers):
    return pl.pallas_call(
        kernel,
        out_shape=outs,
        in_specs=[pl.BlockSpec(memory_space=pltpu.HBM)] * len(args),
        out_specs=[VMEM] * len(outs),
        scratch_shapes=[*buffers, pltpu.SemaphoreType.DMA((len(args),))],
        compiler_params=pltpu.CompilerParams(vmem_limit_bytes=56 << 20),
    )(*args)


def arr(shape, dtype):
    return jax.ShapeDtypeStruct(shape, dtype)


def fetch(sources, buffers, sems):
    copies = [pltpu.make_async_copy(s, b, sems.at[i]) for i, (s, b) in enumerate(zip(sources, buffers))]
    for copy in copies:
        copy.start()
    for copy in copies:
        copy.wait()


def token_pack_kernel(q, k, v, og, rates, gains, all_out, kv_out, gg_out, rate_out):
    tokens, feat = gg_out.shape
    rate = jnp.broadcast_to(rates[...], (feat, tokens)).T
    values = (rate * v[0].astype(F32)).astype(BF)
    all_out[:, 0:feat] = q[0]
    all_out[:, feat : 2 * feat] = k[0]
    all_out[:, 2 * feat : 3 * feat] = values
    kv_out[:, 0:feat] = k[0]
    kv_out[:, feat : 2 * feat] = values
    gg_out[...] = gains[...] * og[0].astype(F32)
    rate_out[...] = rate


def weight_pack_kernel(group, slab, *refs):
    args, (w_out, buf, sems) = refs[:6], refs[6:]
    fetch(args, [buf.at[pl.ds(i, 1)] for i in range(6)], sems)
    for j in range(group):
        cols = pl.ds(j * slab, slab)
        block = jnp.concatenate([buf[i, :, cols] for i in range(6)], axis=1)
        for p in range(j, w_out.shape[0], group):
            w_out[p] = block


def columns(w, slab):
    parts = [w[:, pl.ds(i * slab, slab)].astype(F32) for i in range(6)]
    saved, init = parts[:3], parts[3:]
    return saved, init, [column_norm(x) for x in init], [column_norm(x) for x in saved]


def stack(refs, cols=slice(None)):
    return jnp.concatenate([r[:, cols] for r in refs], axis=0)


def thirds(x, slab):
    return [x[:, pl.ds(i * slab, slab)] for i in range(3)]


def forward_kernel(slab, group, w, *refs):
    queries, parts, normed_out = refs[:group], refs[group:-1], refs[-1]
    own, feat = parts[0].shape
    saved, init, norm_init, norm_saved = columns(w, slab)
    normed = [(saved[i] * (norm_init[i] / norm_saved[i])).astype(BF) for i in range(3)]
    rows = stack(queries, slice(0, feat))
    hidden = (silu_parts(mm(rows, normed[0]))[0] * mm(rows, normed[1])).astype(BF)
    out = mm_nt(hidden, normed[2]).astype(BF)
    for d in range(group):
        parts[d][...] = out[d * own : (d + 1) * own]
    normed_out[...] = jnp.concatenate(normed, axis=1)


def reduce_kernel(gg, *refs):
    parts, (apply_out, sums) = refs[:-2], refs[-2:]
    total = total_of(parts)
    apply_out[...] = total
    sums[0:1, :] = jnp.sum((total * total).T, axis=0, keepdims=True)
    sums[1:2, :] = jnp.sum((total * gg[...]).T, axis=0, keepdims=True)


def delta_kernel(width, apply_out, gg, *refs):
    sums, out = refs[:-1], refs[-1]
    tokens, feat = apply_out.shape
    total = sums[0][...]
    for more in sums[1:]:
        total += more[...]
    square = jnp.broadcast_to(total[0:1, :], (feat, tokens)).T
    gain = jnp.broadcast_to(total[1:2, :], (feat, tokens)).T
    root = jnp.sqrt(square / width + EPS_ROOT)
    out[...] = (gg[...] / root - apply_out[...] * (gain / width) / (root * root * root)).astype(BF)


def pair_kernel(left, right, out):
    feat = left.shape[1]
    out[:, 0:feat] = left[...]
    out[:, feat : 2 * feat] = right[...]


def query_side(rows, delta, normed):
    q_gate = mm(rows, normed[0])
    q_up = mm(rows, normed[1])
    act, slope, _ = silu_parts(q_gate)
    hidden = (act * q_up).astype(BF)
    delta_hidden = mm(delta, normed[2])
    delta_gate = (delta_hidden * q_up * slope).astype(BF)
    delta_up = (delta_hidden * act).astype(BF)
    grads = (mm_tn(rows, delta_gate), mm_tn(rows, delta_up), mm_tn(delta, hidden))
    return delta_gate, delta_up, grads


def near_kernel(slab, group, normed_ref, *refs):
    q_near, od_near, outs, grads_out = refs[:group], refs[group : 2 * group], refs[2 * group : -1], refs[-1]
    own, feat = od_near[0].shape
    normed = thirds(normed_ref, slab)
    delta_gate, delta_up, grads = query_side(stack(q_near, slice(0, feat)), stack(od_near), normed)
    grad_q = (mm_nt(delta_gate, normed[0]) + mm_nt(delta_up, normed[1])).astype(BF)
    for d in range(group):
        outs[d][...] = grad_q[d * own : (d + 1) * own]
    for i in range(3):
        grads_out[i] = grads[i]


def key_kernel(slab, group, w, *refs):
    kvs, (factors, rises) = refs[:group], refs[group:]
    feat = w.shape[0]
    init = [w[:, pl.ds((3 + i) * slab, slab)] for i in range(3)]
    keys = stack(kvs, slice(-2 * feat, -feat))
    values = stack(kvs, slice(-feat, None))
    k_gate = mm(keys, init[0])
    k_up = mm(keys, init[1])
    k_proj = mm(values, init[2])
    k_act, k_slope, k_bend = silu_parts(k_gate)
    rises[0] = (k_act * k_up).astype(BF)
    rises[1] = (k_proj * k_up * k_slope).astype(BF)
    rises[2] = (k_proj * k_act).astype(BF)
    factors[0] = k_act
    factors[1] = k_up * k_slope
    factors[2] = k_proj * k_slope
    factors[3] = k_proj * k_up * k_bend


def backward_kernel(slab, group, tok_groups, place, w, normed_ref, grads, factors, rises, *refs):
    far = group * (tok_groups - 1)
    kvs, pairs, outs, refs = refs[:group], refs[group : group + far], refs[group + far : -4], refs[-4:]
    inner_out, far_od, far_q, sums = refs
    feat = w.shape[0]
    own = outs[0].shape[0]
    for i in range(far):
        far_od[i // group, i % group] = pairs[i][:, 0:feat]
        far_q[i // group, i % group] = pairs[i][:, feat : 2 * feat]
    normed = thirds(normed_ref, slab)
    sums[...] = grads[...]

    def other(e, carry):
        more = query_side(flat(far_q[e]), flat(far_od[e]), normed)[2]
        for i in range(3):
            sums[i] += more[i]
        return carry

    lax.fori_loop(0, tok_groups - 1, other, 0)

    saved, init, norm_init, norm_saved = columns(w, slab)
    cots, direct = [], []
    once = jnp.where(place[0] == 0, 1.0, 0.0)
    for i in range(3):
        apply_grad = sums[i]
        col_dot = jnp.sum(saved[i] * apply_grad, axis=0, keepdims=True)
        cot = apply_grad * (norm_init[i] / norm_saved[i]) - saved[i] * (
            col_dot * norm_init[i] / (norm_saved[i] * norm_saved[i] * norm_saved[i])
        )
        cots.append(cot.astype(BF))
        direct.append((cot + init[i] * (col_dot / (norm_init[i] * norm_saved[i]))) * once)

    init_bf = [w[:, pl.ds((3 + i) * slab, slab)] for i in range(3)]
    keys = stack(kvs, slice(-2 * feat, -feat))
    values = stack(kvs, slice(-feat, None))
    back_gate = mm(keys, cots[0])
    back_up = mm(keys, cots[1])
    back_hidden = mm(values, cots[2])
    back_proj = (back_gate * factors[1] + back_up * factors[0]).astype(BF)
    back_kup = (back_gate * factors[2] + back_hidden * factors[0]).astype(BF)
    back_kgate = (back_gate * factors[3] + (back_up * factors[2] + back_hidden * factors[1])).astype(BF)
    grad_k = (
        mm_nt(rises[1], cots[0])
        + mm_nt(rises[2], cots[1])
        + mm_nt(back_kgate, init_bf[0])
        + mm_nt(back_kup, init_bf[1])
    ).astype(BF)
    grad_v = (mm_nt(rises[0], cots[2]) + mm_nt(back_proj, init_bf[2])).astype(BF)
    for d in range(group):
        outs[d][:, 0:feat] = grad_k[d * own : (d + 1) * own]
        outs[d][:, feat : 2 * feat] = grad_v[d * own : (d + 1) * own]
    inner = (mm_tn(keys, back_kgate), mm_tn(keys, back_kup), mm_tn(values, back_proj))
    inner_out[...] = jnp.concatenate([inner[i] + direct[i] for i in range(3)], axis=1).astype(BF)


def total_of(refs):
    total = refs[0][...].astype(F32)
    for block in refs[1:]:
        total += block[...].astype(F32)
    return total


def tokens_kernel(group, rate, *refs):
    queries, got, (gq, gk, gv) = refs[:group], refs[group:-3], refs[-3:]
    feat = gq.shape[2]
    gq[0] = total_of(queries).astype(BF)
    total = total_of(got)
    gk[0] = total[:, 0:feat].astype(BF)
    gv[0] = (rate[...] * total[:, feat : 2 * feat]).astype(BF)


def weights_kernel(group, slab, got, *outs):
    cols = []
    for j in range(group):
        total = got[j].astype(F32)
        for p in range(j + group, got.shape[0], group):
            total += got[p].astype(F32)
        cols.append(total)
    for i in range(3):
        outs[i][0] = jnp.concatenate([c[:, i * slab : (i + 1) * slab] for c in cols], axis=1)


def make_local(seq_n, head_n, group):
    tok_groups = seq_n // group

    def move(x, dist, axis="seq", size=seq_n):
        return lax.ppermute(x, axis, [(i, i ^ dist) for i in range(size)])

    def near_all(x):
        return [x] + [move(x, d) for d in range(1, group)]

    def mirror(x):
        return [move(x, e * group) for e in range(1, tok_groups)]

    def local(q, k, v, og, rates, gains, gi, ui, di, gs, us, ds):
        _, rows, hidden = gi.shape
        _, own, feat = q.shape
        slab = hidden // group
        near = group * own
        me = lax.axis_index("seq")
        place = jnp.stack((lax.div(me, group), lax.rem(me, group), me)).astype(jnp.int32)

        (packed,) = copying_call(
            functools.partial(weight_pack_kernel, group, slab),
            (arr((seq_n, rows, 6 * slab), BF),),
            (gs, us, ds, gi, ui, di),
            [pltpu.VMEM((6, rows, hidden), BF)],
        )
        packed, queries = lax.optimization_barrier((packed, q[0]))
        wall = lax.all_to_all(packed, "seq", 0, 0, tiled=True).reshape(seq_n * rows, 6 * slab)
        tokens, kv, gg, rate = call(
            token_pack_kernel,
            (arr((own, 3 * feat), BF), arr((own, 2 * feat), BF), arr((own, feat), F32), arr((own, feat), F32)),
            (q, k, v, og, rates, gains),
            8,
        )
        beside = move(tokens, 1) if group > 1 else None
        rest = range(2, group)
        q_near = [queries, beside][:group] + [move(queries, d) for d in rest]
        kv_near = [kv, beside][:group] + [move(kv, d) for d in rest]

        block = arr((own, feat), BF)
        mflop = 2 * near * feat * slab
        *parts, normed = call(
            functools.partial(forward_kernel, slab, group),
            (*(block,) * group, arr((seq_n * rows, 3 * slab), BF)),
            (wall, *q_near),
            24,
            flops=3 * mflop,
        )
        parts = [parts[0]] + [move(parts[d], d) for d in range(1, group)]
        *parts, kv_near = lax.optimization_barrier((*parts, kv_near))
        apply_out, sums = call(
            reduce_kernel, (arr((own, feat), F32), arr((2, own), F32)), (gg, *parts), 16
        )
        sums, queries = lax.optimization_barrier((sums, queries))
        sums = [sums] + [move(sums, d, "head", head_n) for d in range(1, head_n)]
        q_mirror = mirror(queries)
        (od,) = call(functools.partial(delta_kernel, head_n * feat), (block,), (apply_out, gg, *sums), 16)
        od_mirror = mirror(od)
        od_near = near_all(od)
        factors, rises = call(
            functools.partial(key_kernel, slab, group),
            (arr((4, near, slab), F32), arr((3, near, slab), BF)),
            (wall, *kv_near),
            24,
            flops=12 * mflop,
        )
        pairs = [
            call(pair_kernel, (arr((own, 2 * feat), BF),), pair, 16)[0] for pair in zip(od_mirror, q_mirror)
        ]
        pairs = [x for m in pairs for x in near_all(m)]
        *grad_q, grads = call(
            functools.partial(near_kernel, slab, group),
            (*(block,) * group, arr((3, seq_n * rows, slab), F32)),
            (normed, *q_near, *od_near),
            24,
            flops=12 * mflop,
        )
        grad_q = [grad_q[0]] + [move(grad_q[d], d) for d in range(1, group)]

        far = pltpu.VMEM((max(tok_groups - 1, 1), group, own, feat), BF)
        *tok, inner = call(
            functools.partial(backward_kernel, slab, group, tok_groups),
            (*(arr((own, 2 * feat), BF),) * group, arr((seq_n * rows, 3 * slab), BF)),
            (place, wall, normed, grads, factors, rises, *kv_near, *pairs),
            32,
            smem=1,
            flops=24 * mflop,
            scratch=[far, far, pltpu.VMEM((3, seq_n * rows, slab), F32)],
        )
        inner = lax.all_to_all(inner.reshape(seq_n, rows, 3 * slab), "seq", 0, 0, tiled=True)
        tok = [tok[0]] + [move(tok[d], d) for d in range(1, group)]
        out_tok = arr((1, own, feat), BF)
        grad_w = arr((1, rows, hidden), F32)
        grads_t = call(
            functools.partial(tokens_kernel, group), (out_tok,) * 3, (rate, *grad_q, *tok), 16
        )
        grads_w = call(functools.partial(weights_kernel, group, slab), (grad_w,) * 3, (inner,), 16)
        return (*grads_t, *grads_w)

    return local


def solution(mesh):
    seq_n = mesh.shape["seq"]
    head_n = mesh.shape["head"]
    group = min(4, seq_n)
    tok = P("head", "seq", None)
    return jax.shard_map(
        make_local(seq_n, head_n, group),
        mesh=mesh,
        in_specs=(tok, tok, tok, tok, P("head", "seq"), P("head", None), tok, tok, tok, tok, tok, tok),
        out_specs=(tok, tok, tok, tok, tok, tok),
        check_vma=False,
    )
```

time: 95.9 us -> 81.9 us (0.85)
  waiting for transfers between devices: 47.7 us -> 26.5 us
  starting transfers between devices: 36.4 us -> 42.9 us
  local copies, waits for them, and re-layouts: 0.04 us -> 1.35 us
    all_to_all x1, waiting for transfers between devices: 11.4 us -> 0.01 us  [local(): lax.all_to_all(packed, 'seq', 0, 0, tiled=True)]
    ppermute x24 -> x25, waiting for transfers between devices: 36.3 us -> 26.5 us  [move(): return lax.ppermute(x, axis, [(i, i ^ dist) for i in range(size)])]
    ppermute x24 -> x25, starting transfers between devices: 25.5 us -> 31 us  [move(): return lax.ppermute(x, axis, [(i, i ^ dist) for i in range(size)])]
    unnamed x12, local copies, waits for them, and re-layouts: 0.04 us -> 1.35 us
    all_to_all x1, starting transfers between devices: 3.47 us -> 4.59 us  [local(): lax.all_to_all(inner.reshape(seq_n, rows, 3 * slab), 'seq', 0, 0, tiled=T...]
    pallas_call x9 -> x10, Pallas kernels: 8.62 us -> 7.95 us  [call(): pl.pallas_call(kernel, out_shape=outs, in_specs=[SMEM] * smem + [VMEM] *...]
  transfers between devices with their start and end apart: 26 -> 27, of which waited for: 13 -> 14; matrix products, arithmetic and copies ran while one was open for 0% -> 0% of each run, Pallas kernels for 3% -> 4%
where the time goes in v5:
time: 81.9 us; the launch traced here: 81.5 us
  starting transfers between devices  42.9 us (52%)
  waiting for transfers between devices  26.5 us (32%)
  Pallas kernels  9.92 us (12%)
  local copies, waits for them, and re-layouts  1.35 us (2%)
  between operations  0.82 us (1%)
    ppermute x25, starting transfers between devices, move(): return lax.ppermute(x, axis, [(i, i ^ dist) for i in range(size)])  31 us
    ppermute x25, waiting for transfers between devices, move(): return lax.ppermute(x, axis, [(i, i ^ dist) for i in range(size)])  26.5 us
    pallas_call x10, Pallas kernels, call(): pl.pallas_call(kernel, out_shape=outs, in_specs=[SMEM] * smem + [VMEM] *...  7.95 us
    all_to_all x1, starting transfers between devices, local(): lax.all_to_all(packed, 'seq', 0, 0, tiled=True)  7.26 us
    all_to_all x1, starting transfers between devices, local(): lax.all_to_all(inner.reshape(seq_n, rows, 3 * slab), 'seq', 0, 0, tiled=T...  4.59 us
    pallas_call x1, Pallas kernels, copying_call(): pl.pallas_call(kernel, out_shape=outs, in_specs=[pl.BlockSpec(memory_spac...  1.97 us
  transfers between devices with their start and end apart: 27, of which 14 were waited for; matrix products, arithmetic and copies ran while one was open for 0% of the time, Pallas kernels for 4%

profile of v5, /device:TPU:0, one launch (start us, length us, event | category | flops | bytes accessed | tf_op | source)
XLA Modules:
  0.0 81.5 jit_solution(11232656508423120778)
XLA Ops:
  0.7 2.0 %shard_map.164 = bf16[8,32,1152]{2,1,0:T(8,128)(2,1)} custom-call(bf16[1,32,768]{2,1,0:T(8,128)(2,1)} %refs_0_.1, bf16[1,32,768]{2,1,0:T(8,128)(2,1)} %refs_1_.1, bf16[1,32,768]{2,1,0:T(8,128)(2,1)} %refs_2_.1, bf16[1,32,768]{2,1,0:T(8,128)(2,1)} %refs_3_.1, bf16[1,32,768]{2,1,0:T(8,128)(2,1)} %refs_4_.1, bf16[1,32,768]{2,1,0:T(8,128)(2,1)} %refs_5_.1), custom_call_target="tpu_custom_call" | custom-call | tf_op jit(solution)/shard_map/pallas_call | solution.py:60
  2.7 7.3 %all-to-all-start = ((bf16[8,32,1152]{2,1,0:T(8,128)(2,1)}), bf16[8,32,1152]{2,1,0:T(8,128)(2,1)S(1)}, u32[]{:S(2)}, u32[]{:S(2)}) async-start(bf16[8,32,1152]{2,1,0:T(8,128)(2,1)} %shard_map.164), calls=%async_computation | async-start | bytes 1179648 | tf_op jit(solution)/shard_map/all_to_all | solution.py:310
  10.0 0.0 copy-start.4
  10.0 0.7 copy-done.4
  10.6 0.7 copy-done.5
  11.3 0.1 shard_map.163
  11.4 2.1 %collective-permute-start = (bf16[128,768]{1,0:T(8,128)(2,1)S(1)}, bf16[128,768]{1,0:T(8,128)(2,1)S(1)}, u32[]{:S(2)}, u32[]{:S(2)}) collective-permute-start(bf16[128,768]{1,0:T(8,128)(2,1)S(1)} %get-tuple-element.50), channel_id=1, source_target_pairs={{0,1},{1,0},{2,3},{3,2},{4,5},{5,4},{6,7},{7,6},{8,9},{9,8},{10,11... | collective-permute-start | bytes 589832 | tf_op jit(solution)/shard_map/ppermute | solution.py:287
  13.5 1.5 %collective-permute-start.2 = (bf16[128,256]{1,0:T(8,128)(2,1)S(1)}, bf16[128,256]{1,0:T(8,128)(2,1)S(1)}, u32[]{:S(2)}, u32[]{:S(2)}) collective-permute-start(bf16[128,256]{1,0:T(8,128)(2,1)S(1)} %bitcast.9), channel_id=1, source_target_pairs={{0,3},{1,2},{2,1},{3,0},{4,7},{5,6},{6,5},{7,4},{8,11},{9,10},{10,... | collective-permute-start | bytes 196616 | tf_op jit(solution)/shard_map/ppermute | solution.py:287
  14.9 0.1 collective-permute-start.1
  15.0 2.8 %collective-permute-start.7 = (bf16[128,512]{1,0:T(8,128)(2,1)S(1)}, bf16[128,512]{1,0:T(8,128)(2,1)S(1)}, u32[]{:S(2)}, u32[]{:S(2)}) collective-permute-start(bf16[128,512]{1,0:T(8,128)(2,1)S(1)} %get-tuple-element.70.refs_0_), channel_id=1, source_target_pairs={{0,3},{1,2},{2,1},{3,0},{4,7},{5,6},{6,5},{7,4},{8,11},{9,10},{10,... | collective-permute-start | bytes 393224 | tf_op jit(solution)/shard_map/ppermute | solution.py:287
  17.9 0.6 collective-permute-start.6
  18.4 4.8 %collective-permute-done.2.refs_3_ = bf16[128,256]{1,0:T(8,128)(2,1)S(1)} collective-permute-done((bf16[128,256]{1,0:T(8,128)(2,1)S(1)}, bf16[128,256]{1,0:T(8,128)(2,1)S(1)}, u32[]{:S(2)}, u32[]{:S(2)}) %collective-permute-start.2) | collective-permute-done | bytes 65568 | tf_op jit(solution)/shard_map/ppermute | solution.py:287
  23.3 0.4 collective-permute-done.1.refs_2_
  23.6 2.3 %collective-permute-done.refs_1_ = bf16[128,768]{1,0:T(8,128)(2,1)S(1)} collective-permute-done((bf16[128,768]{1,0:T(8,128)(2,1)S(1)}, bf16[128,768]{1,0:T(8,128)(2,1)S(1)}, u32[]{:S(2)}, u32[]{:S(2)}) %collective-permute-start) | collective-permute-done | bytes 196640 | tf_op jit(solution)/shard_map/ppermute | solution.py:287
  25.9 0.0 all-to-all-done
  25.9 0.8 shard_map.165
  26.7 1.5 %collective-permute-start.3 = (bf16[128,256]{1,0:T(8,128)(2,1)S(1)}, bf16[128,256]{1,0:T(8,128)(2,1)S(1)}, u32[]{:S(2)}, u32[]{:S(2)}) collective-permute-start(bf16[128,256]{1,0:T(8,128)(2,1)S(1)} %get-tuple-element.54), channel_id=1, source_target_pairs={{0,1},{1,0},{2,3},{3,2},{4,5},{5,4},{6,7},{7,6},{8,9},{9,8},{10,11... | collective-permute-start | bytes 196616 | tf_op jit(solution)/shard_map/ppermute | solution.py:287
  28.2 0.9 %collective-permute-start.4 = (bf16[128,256]{1,0:T(8,128)(2,1)S(1)}, bf16[128,256]{1,0:T(8,128)(2,1)S(1)}, u32[]{:S(2)}, u32[]{:S(2)}) collective-permute-start(bf16[128,256]{1,0:T(8,128)(2,1)S(1)} %get-tuple-element.55), channel_id=1, source_target_pairs={{0,2},{1,3},{2,0},{3,1},{4,6},{5,7},{6,4},{7,5},{8,10},{9,11},{10,... | collective-permute-start | bytes 196616 | tf_op jit(solution)/shard_map/ppermute | solution.py:287
  29.2 1.1 %collective-permute-start.5 = (bf16[128,256]{1,0:T(8,128)(2,1)S(1)}, bf16[128,256]{1,0:T(8,128)(2,1)S(1)}, u32[]{:S(2)}, u32[]{:S(2)}) collective-permute-start(bf16[128,256]{1,0:T(8,128)(2,1)S(1)} %get-tuple-element.56), channel_id=1, source_target_pairs={{0,3},{1,2},{2,1},{3,0},{4,7},{5,6},{6,5},{7,4},{8,11},{9,10},{10,... | collective-permute-start | bytes 196616 | tf_op jit(solution)/shard_map/ppermute | solution.py:287
  30.3 0.0 collective-permute-done.7.refs_3_
  30.3 0.5 collective-permute-done.6.refs_2_
  30.7 0.3 collective-permute-done.3.refs_1_
  31.0 1.5 %collective-permute-done.4.refs_2_ = bf16[128,256]{1,0:T(8,128)(2,1)S(1)} collective-permute-done((bf16[128,256]{1,0:T(8,128)(2,1)S(1)}, bf16[128,256]{1,0:T(8,128)(2,1)S(1)}, u32[]{:S(2)}, u32[]{:S(2)}) %collective-permute-start.4) | collective-permute-done | bytes 65568 | tf_op jit(solution)/shard_map/ppermute | solution.py:287
  32.5 1.8 %collective-permute-done.5.refs_3_ = bf16[128,256]{1,0:T(8,128)(2,1)S(1)} collective-permute-done((bf16[128,256]{1,0:T(8,128)(2,1)S(1)}, bf16[128,256]{1,0:T(8,128)(2,1)S(1)}, u32[]{:S(2)}, u32[]{:S(2)}) %collective-permute-start.5) | collective-permute-done | bytes 65568 | tf_op jit(solution)/shard_map/ppermute | solution.py:287
  34.3 0.1 shard_map.166
  34.5 0.1 collective-permute-start.10
  34.6 1.6 %collective-permute-start.9 = (f32[2,128]{1,0:T(2,128)S(1)}, f32[2,128]{1,0:T(2,128)S(1)}, u32[]{:S(2)}, u32[]{:S(2)}) collective-permute-start(f32[2,128]{1,0:T(2,128)S(1)} %get-tuple-element.64.refs_0_), channel_id=1, source_target_pairs={{0,16},{8,24},{16,0},{24,8},{1,17},{9,25},{17,1},{25,9},{2,18},{10... | collective-permute-start | bytes 3080 | tf_op jit(solution)/shard_map/ppermute | solution.py:287
  36.1 0.3 collective-permute-start.8
  36.4 2.0 %collective-permute-start.18 = (bf16[128,256]{1,0:T(8,128)(2,1)S(1)}, bf16[128,256]{1,0:T(8,128)(2,1)S(1)}, u32[]{:S(2)}, u32[]{:S(2)}) collective-permute-start(bf16[128,256]{1,0:T(8,128)(2,1)S(1)} %bitcast.12), channel_id=1, source_target_pairs={{0,4},{1,5},{2,6},{3,7},{4,0},{5,1},{6,2},{7,3},{8,12},{9,13},{10,... | collective-permute-start | bytes 196616 | tf_op jit(solution)/shard_map/ppermute | solution.py:287
  38.4 0.0 collective-permute-done.10.refs_3_
  38.4 0.0 collective-permute-done.9.refs_2_
  38.4 0.0 collective-permute-done.8.refs_1_
  38.4 0.1 shard_map.167.refs_4_
  38.6 1.8 %collective-permute-start.17 = (bf16[128,256]{1,0:T(8,128)(2,1)S(1)}, bf16[128,256]{1,0:T(8,128)(2,1)S(1)}, u32[]{:S(2)}, u32[]{:S(2)}) collective-permute-start(bf16[128,256]{1,0:T(8,128)(2,1)S(1)} %shard_map.167.refs_4_), channel_id=1, source_target_pairs={{0,4},{1,5},{2,6},{3,7},{4,0},{5,1},{6,2},{7,3},{8,12},{9,13},{10,... | collective-permute-start | bytes 196616 | tf_op jit(solution)/shard_map/ppermute | solution.py:287
  40.4 1.6 %collective-permute-start.13 = (bf16[128,256]{1,0:T(8,128)(2,1)S(1)}, bf16[128,256]{1,0:T(8,128)(2,1)S(1)}, u32[]{:S(2)}, u32[]{:S(2)}) collective-permute-start(bf16[128,256]{1,0:T(8,128)(2,1)S(1)} %shard_map.167.refs_4_), channel_id=1, source_target_pairs={{0,3},{1,2},{2,1},{3,0},{4,7},{5,6},{6,5},{7,4},{8,11},{9,10},{10,... | collective-permute-start | bytes 196616 | tf_op jit(solution)/shard_map/ppermute | solution.py:287
  42.0 1.0 %collective-permute-start.12 = (bf16[128,256]{1,0:T(8,128)(2,1)S(1)}, bf16[128,256]{1,0:T(8,128)(2,1)S(1)}, u32[]{:S(2)}, u32[]{:S(2)}) collective-permute-start(bf16[128,256]{1,0:T(8,128)(2,1)S(1)} %shard_map.167.refs_4_), channel_id=1, source_target_pairs={{0,2},{1,3},{2,0},{3,1},{4,6},{5,7},{6,4},{7,5},{8,10},{9,11},{10,... | collective-permute-start | bytes 196616 | tf_op jit(solution)/shard_map/ppermute | solution.py:287
  43.0 0.9 %collective-permute-start.11 = (bf16[128,256]{1,0:T(8,128)(2,1)S(1)}, bf16[128,256]{1,0:T(8,128)(2,1)S(1)}, u32[]{:S(2)}, u32[]{:S(2)}) collective-permute-start(bf16[128,256]{1,0:T(8,128)(2,1)S(1)} %shard_map.167.refs_4_), channel_id=1, source_target_pairs={{0,1},{1,0},{2,3},{3,2},{4,5},{5,4},{6,7},{7,6},{8,9},{9,8},{10,11... | collective-permute-start | bytes 196616 | tf_op jit(solution)/shard_map/ppermute | solution.py:287
  43.9 0.6 collective-permute-done.18.right
  44.5 1.3 %collective-permute-done.17.left = bf16[128,256]{1,0:T(8,128)(2,1)S(1)} collective-permute-done((bf16[128,256]{1,0:T(8,128)(2,1)S(1)}, bf16[128,256]{1,0:T(8,128)(2,1)S(1)}, u32[]{:S(2)}, u32[]{:S(2)}) %collective-permute-start.17) | collective-permute-done | bytes 65568 | tf_op jit(solution)/shard_map/ppermute | solution.py:287
  45.8 0.4 collective-permute-start.21
  46.1 2.3 %collective-permute-start.20 = (bf16[128,512]{1,0:T(8,128)(2,1)S(1)}, bf16[128,512]{1,0:T(8,128)(2,1)S(1)}, u32[]{:S(2)}, u32[]{:S(2)}) collective-permute-start(bf16[128,512]{1,0:T(8,128)(2,1)S(1)} %shard_map.170.refs_4_), channel_id=1, source_target_pairs={{0,2},{1,3},{2,0},{3,1},{4,6},{5,7},{6,4},{7,5},{8,10},{9,11},{10,... | collective-permute-start | bytes 393224 | tf_op jit(solution)/shard_map/ppermute | solution.py:287
  48.4 0.9 %collective-permute-start.19 = (bf16[128,512]{1,0:T(8,128)(2,1)S(1)}, bf16[128,512]{1,0:T(8,128)(2,1)S(1)}, u32[]{:S(2)}, u32[]{:S(2)}) collective-permute-start(bf16[128,512]{1,0:T(8,128)(2,1)S(1)} %shard_map.170.refs_4_), channel_id=1, source_target_pairs={{0,1},{1,0},{2,3},{3,2},{4,5},{5,4},{6,7},{7,6},{8,9},{9,8},{10,11... | collective-permute-start | bytes 393224 | tf_op jit(solution)/shard_map/ppermute | solution.py:287
  49.3 0.1 pad_add_fusion.place
  49.4 0.7 shard_map.169
  50.2 0.0 collective-permute-done.11.refs_5_
  50.2 0.8 %shard_map.168 = (bf16[128,256]{1,0:T(8,128)(2,1)S(1)}, bf16[128,256]{1,0:T(8,128)(2,1)S(1)}, bf16[128,256]{1,0:T(8,128)(2,1)S(1)}, bf16[128,256]{1,0:T(8,128)(2,1)S(1)}, f32[3,256,192]{2,1,0:T(8,128)S(1)}) custom-call(bf16[256,576]{1,0:T(8,128)(2,1)S(1)} %get-tuple-element.51.normed_ref, bf16[128,256]{1,0:T(8,128)(2,1)S(1)} %bitcast.13, ...), custom_call_target="tpu_custom_call" | custom-call | flops 603979776 | bytes 1802240 | tf_op jit(solution)/shard_map/pallas_call | solution.py:48
  51.0 1.9 %collective-permute-done.21.refs_7_ = bf16[128,512]{1,0:T(8,128)(2,1)S(1)} collective-permute-done((bf16[128,512]{1,0:T(8,128)(2,1)S(1)}, bf16[128,512]{1,0:T(8,128)(2,1)S(1)}, u32[]{:S(2)}, u32[]{:S(2)}) %collective-permute-start.21) | collective-permute-done | bytes 131104 | tf_op jit(solution)/shard_map/ppermute | solution.py:287
  52.9 1.7 %collective-permute-done.20.refs_6_ = bf16[128,512]{1,0:T(8,128)(2,1)S(1)} collective-permute-done((bf16[128,512]{1,0:T(8,128)(2,1)S(1)}, bf16[128,512]{1,0:T(8,128)(2,1)S(1)}, u32[]{:S(2)}, u32[]{:S(2)}) %collective-permute-start.20) | collective-permute-done | bytes 131104 | tf_op jit(solution)/shard_map/ppermute | solution.py:287
  54.6 0.0 collective-permute-done.19.refs_5_
  54.7 3.7 %shard_map.171 = (bf16[128,512]{1,0:T(8,128)(2,1)S(1)}, bf16[128,512]{1,0:T(8,128)(2,1)S(1)}, bf16[128,512]{1,0:T(8,128)(2,1)S(1)}, bf16[128,512]{1,0:T(8,128)(2,1)S(1)}, bf16[256,576]{1,0:T(8,128)(2,1)}) custom-call(s32[3]{0:T(128)S(1)} %pad_add_fusion.place, bf16[256,1152]{1,0:T(8,128)(2,1)S(1)} %bitcast.8, ...), custom_call_target="tpu_custom_call" | custom-call | flops 1207959552 | bytes 5570572 | tf_op jit(solution)/shard_map/pallas_call | solution.py:48
  58.3 4.6 %all-to-all-start.1 = ((bf16[8,32,576]{2,1,0:T(8,128)(2,1)}), bf16[8,32,576]{2,1,0:T(8,128)(2,1)S(1)}, u32[]{:S(2)}, u32[]{:S(2)}) async-start(bf16[8,32,576]{2,1,0:T(8,128)(2,1)} %bitcast.5), calls=%async_computation.1 | async-start | bytes 655360 | tf_op jit(solution)/shard_map/all_to_all | solution.py:372
  62.9 2.0 %collective-permute-start.14 = (bf16[128,256]{1,0:T(8,128)(2,1)S(1)}, bf16[128,256]{1,0:T(8,128)(2,1)S(1)}, u32[]{:S(2)}, u32[]{:S(2)}) collective-permute-start(bf16[128,256]{1,0:T(8,128)(2,1)S(1)} %get-tuple-element.66), channel_id=1, source_target_pairs={{0,1},{1,0},{2,3},{3,2},{4,5},{5,4},{6,7},{7,6},{8,9},{9,8},{10,11... | collective-permute-start | bytes 196616 | tf_op jit(solution)/shard_map/ppermute | solution.py:287
  64.9 0.0 collective-permute-start.22
  65.0 2.0 %collective-permute-start.23 = (bf16[128,512]{1,0:T(8,128)(2,1)S(1)}, bf16[128,512]{1,0:T(8,128)(2,1)S(1)}, u32[]{:S(2)}, u32[]{:S(2)}) collective-permute-start(bf16[128,512]{1,0:T(8,128)(2,1)S(1)} %get-tuple-element.79), channel_id=1, source_target_pairs={{0,2},{1,3},{2,0},{3,1},{4,6},{5,7},{6,4},{7,5},{8,10},{9,11},{10,... | collective-permute-start | bytes 393224 | tf_op jit(solution)/shard_map/ppermute | solution.py:287
  67.0 1.5 %collective-permute-start.24 = (bf16[128,512]{1,0:T(8,128)(2,1)S(1)}, bf16[128,512]{1,0:T(8,128)(2,1)S(1)}, u32[]{:S(2)}, u32[]{:S(2)}) collective-permute-start(bf16[128,512]{1,0:T(8,128)(2,1)S(1)} %get-tuple-element.80), channel_id=1, source_target_pairs={{0,3},{1,2},{2,1},{3,0},{4,7},{5,6},{6,5},{7,4},{8,11},{9,10},{10,... | collective-permute-start | bytes 393224 | tf_op jit(solution)/shard_map/ppermute | solution.py:287
  68.4 1.5 %collective-permute-start.15 = (bf16[128,256]{1,0:T(8,128)(2,1)S(1)}, bf16[128,256]{1,0:T(8,128)(2,1)S(1)}, u32[]{:S(2)}, u32[]{:S(2)}) collective-permute-start(bf16[128,256]{1,0:T(8,128)(2,1)S(1)} %get-tuple-element.67), channel_id=1, source_target_pairs={{0,2},{1,3},{2,0},{3,1},{4,6},{5,7},{6,4},{7,5},{8,10},{9,11},{10,... | collective-permute-start | bytes 196616 | tf_op jit(solution)/shard_map/ppermute | solution.py:287
  69.9 1.3 %collective-permute-done.14.refs_1_ = bf16[128,256]{1,0:T(8,128)(2,1)S(1)} collective-permute-done((bf16[128,256]{1,0:T(8,128)(2,1)S(1)}, bf16[128,256]{1,0:T(8,128)(2,1)S(1)}, u32[]{:S(2)}, u32[]{:S(2)}) %collective-permute-start.14) | collective-permute-done | bytes 65568 | tf_op jit(solution)/shard_map/ppermute | solution.py:287
  71.2 0.6 collective-permute-start.16
  71.8 7.0 %collective-permute-done.15.refs_2_ = bf16[128,256]{1,0:T(8,128)(2,1)S(1)} collective-permute-done((bf16[128,256]{1,0:T(8,128)(2,1)S(1)}, bf16[128,256]{1,0:T(8,128)(2,1)S(1)}, u32[]{:S(2)}, u32[]{:S(2)}) %collective-permute-start.15) | collective-permute-done | bytes 65568 | tf_op jit(solution)/shard_map/ppermute | solution.py:287
  78.8 1.2 %collective-permute-done.16.refs_3_ = bf16[128,256]{1,0:T(8,128)(2,1)S(1)} collective-permute-done((bf16[128,256]{1,0:T(8,128)(2,1)S(1)}, bf16[128,256]{1,0:T(8,128)(2,1)S(1)}, u32[]{:S(2)}, u32[]{:S(2)}) %collective-permute-start.16) | collective-permute-done | bytes 65568 | tf_op jit(solution)/shard_map/ppermute | solution.py:287
  80.0 0.0 collective-permute-done.22.refs_5_
  80.0 0.0 collective-permute-done.23.refs_6_
  80.0 0.7 shard_map.172
  80.7 0.8 shard_map.173
  (14 shorter events, 0.0 us)
Async XLA Ops:
  0.6 9.3 %copy-start = (bf16[1,128,256]{2,1,0:T(8,128)(2,1)S(1)}, bf16[1,128,256]{2,1,0:T(8,128)(2,1)}, u32[]{:S(2)}) copy-start(bf16[1,128,256]{2,1,0:T(8,128)(2,1)} %q.1) | copy-start | bytes 196612
  0.6 9.3 %copy-start.3 = (bf16[1,128,256]{2,1,0:T(8,128)(2,1)S(1)}, bf16[1,128,256]{2,1,0:T(8,128)(2,1)}, u32[]{:S(2)}) copy-start(bf16[1,128,256]{2,1,0:T(8,128)(2,1)} %og.1) | copy-start | bytes 196612
  0.7 9.3 %copy-start.2 = (bf16[1,128,256]{2,1,0:T(8,128)(2,1)S(1)}, bf16[1,128,256]{2,1,0:T(8,128)(2,1)}, u32[]{:S(2)}) copy-start(bf16[1,128,256]{2,1,0:T(8,128)(2,1)} %v.1) | copy-start | bytes 196612
  0.7 9.3 %copy-start.1 = (bf16[1,128,256]{2,1,0:T(8,128)(2,1)S(1)}, bf16[1,128,256]{2,1,0:T(8,128)(2,1)}, u32[]{:S(2)}) copy-start(bf16[1,128,256]{2,1,0:T(8,128)(2,1)} %k.1) | copy-start | bytes 196612
  2.7 23.3 %all-to-all-start = ((bf16[8,32,1152]{2,1,0:T(8,128)(2,1)}), bf16[8,32,1152]{2,1,0:T(8,128)(2,1)S(1)}, u32[]{:S(2)}, u32[]{:S(2)}) async-start(bf16[8,32,1152]{2,1,0:T(8,128)(2,1)} %shard_map.164), calls=%async_computation | async-start | bytes 1179648 | tf_op jit(solution)/shard_map/all_to_all | solution.py:310
  10.0 0.7 copy-start.4
  10.6 0.7 copy-start.5
  11.4 14.5 %collective-permute-start = (bf16[128,768]{1,0:T(8,128)(2,1)S(1)}, bf16[128,768]{1,0:T(8,128)(2,1)S(1)}, u32[]{:S(2)}, u32[]{:S(2)}) collective-permute-start(bf16[128,768]{1,0:T(8,128)(2,1)S(1)} %get-tuple-element.50), channel_id=1, source_target_pairs={{0,1},{1,0},{2,3},{3,2},{4,5},{5,4},{6,7},{7,6},{8,9},{9,8},{10,11... | collective-permute-start | bytes 589832 | tf_op jit(solution)/shard_map/ppermute | solution.py:287
  13.5 9.8 %collective-permute-start.2 = (bf16[128,256]{1,0:T(8,128)(2,1)S(1)}, bf16[128,256]{1,0:T(8,128)(2,1)S(1)}, u32[]{:S(2)}, u32[]{:S(2)}) collective-permute-start(bf16[128,256]{1,0:T(8,128)(2,1)S(1)} %bitcast.9), channel_id=1, source_target_pairs={{0,3},{1,2},{2,1},{3,0},{4,7},{5,6},{6,5},{7,4},{8,11},{9,10},{10,... | collective-permute-start | bytes 196616 | tf_op jit(solution)/shard_map/ppermute | solution.py:287
  14.9 8.7 %collective-permute-start.1 = (bf16[128,256]{1,0:T(8,128)(2,1)S(1)}, bf16[128,256]{1,0:T(8,128)(2,1)S(1)}, u32[]{:S(2)}, u32[]{:S(2)}) collective-permute-start(bf16[128,256]{1,0:T(8,128)(2,1)S(1)} %bitcast.10), channel_id=1, source_target_pairs={{0,2},{1,3},{2,0},{3,1},{4,6},{5,7},{6,4},{7,5},{8,10},{9,11},{10,... | collective-permute-start | bytes 196616 | tf_op jit(solution)/shard_map/ppermute | solution.py:287
  15.0 15.2 %collective-permute-start.7 = (bf16[128,512]{1,0:T(8,128)(2,1)S(1)}, bf16[128,512]{1,0:T(8,128)(2,1)S(1)}, u32[]{:S(2)}, u32[]{:S(2)}) collective-permute-start(bf16[128,512]{1,0:T(8,128)(2,1)S(1)} %get-tuple-element.70.refs_0_), channel_id=1, source_target_pairs={{0,3},{1,2},{2,1},{3,0},{4,7},{5,6},{6,5},{7,4},{8,11},{9,10},{10,... | collective-permute-start | bytes 393224 | tf_op jit(solution)/shard_map/ppermute | solution.py:287
  17.9 12.9 %collective-permute-start.6 = (bf16[128,512]{1,0:T(8,128)(2,1)S(1)}, bf16[128,512]{1,0:T(8,128)(2,1)S(1)}, u32[]{:S(2)}, u32[]{:S(2)}) collective-permute-start(bf16[128,512]{1,0:T(8,128)(2,1)S(1)} %get-tuple-element.70.refs_0_), channel_id=1, source_target_pairs={{0,2},{1,3},{2,0},{3,1},{4,6},{5,7},{6,4},{7,5},{8,10},{9,11},{10,... | collective-permute-start | bytes 393224 | tf_op jit(solution)/shard_map/ppermute | solution.py:287
  26.7 4.3 %collective-permute-start.3 = (bf16[128,256]{1,0:T(8,128)(2,1)S(1)}, bf16[128,256]{1,0:T(8,128)(2,1)S(1)}, u32[]{:S(2)}, u32[]{:S(2)}) collective-permute-start(bf16[128,256]{1,0:T(8,128)(2,1)S(1)} %get-tuple-element.54), channel_id=1, source_target_pairs={{0,1},{1,0},{2,3},{3,2},{4,5},{5,4},{6,7},{7,6},{8,9},{9,8},{10,11... | collective-permute-start | bytes 196616 | tf_op jit(solution)/shard_map/ppermute | solution.py:287
  28.2 4.3 %collective-permute-start.4 = (bf16[128,256]{1,0:T(8,128)(2,1)S(1)}, bf16[128,256]{1,0:T(8,128)(2,1)S(1)}, u32[]{:S(2)}, u32[]{:S(2)}) collective-permute-start(bf16[128,256]{1,0:T(8,128)(2,1)S(1)} %get-tuple-element.55), channel_id=1, source_target_pairs={{0,2},{1,3},{2,0},{3,1},{4,6},{5,7},{6,4},{7,5},{8,10},{9,11},{10,... | collective-permute-start | bytes 196616 | tf_op jit(solution)/shard_map/ppermute | solution.py:287
  29.2 5.2 %collective-permute-start.5 = (bf16[128,256]{1,0:T(8,128)(2,1)S(1)}, bf16[128,256]{1,0:T(8,128)(2,1)S(1)}, u32[]{:S(2)}, u32[]{:S(2)}) collective-permute-start(bf16[128,256]{1,0:T(8,128)(2,1)S(1)} %get-tuple-element.56), channel_id=1, source_target_pairs={{0,3},{1,2},{2,1},{3,0},{4,7},{5,6},{6,5},{7,4},{8,11},{9,10},{10,... | collective-permute-start | bytes 196616 | tf_op jit(solution)/shard_map/ppermute | solution.py:287
  34.5 4.0 %collective-permute-start.10 = (f32[2,128]{1,0:T(2,128)S(1)}, f32[2,128]{1,0:T(2,128)S(1)}, u32[]{:S(2)}, u32[]{:S(2)}) collective-permute-start(f32[2,128]{1,0:T(2,128)S(1)} %get-tuple-element.64.refs_0_), channel_id=1, source_target_pairs={{0,24},{8,16},{16,8},{24,0},{1,25},{9,17},{17,9},{25,1},{2,26},{10... | collective-permute-start | bytes 3080 | tf_op jit(solution)/shard_map/ppermute | solution.py:287
  34.6 3.9 %collective-permute-start.9 = (f32[2,128]{1,0:T(2,128)S(1)}, f32[2,128]{1,0:T(2,128)S(1)}, u32[]{:S(2)}, u32[]{:S(2)}) collective-permute-start(f32[2,128]{1,0:T(2,128)S(1)} %get-tuple-element.64.refs_0_), channel_id=1, source_target_pairs={{0,16},{8,24},{16,0},{24,8},{1,17},{9,25},{17,1},{25,9},{2,18},{10... | collective-permute-start | bytes 3080 | tf_op jit(solution)/shard_map/ppermute | solution.py:287
  36.1 2.3 %collective-permute-start.8 = (f32[2,128]{1,0:T(2,128)S(1)}, f32[2,128]{1,0:T(2,128)S(1)}, u32[]{:S(2)}, u32[]{:S(2)}) collective-permute-start(f32[2,128]{1,0:T(2,128)S(1)} %get-tuple-element.64.refs_0_), channel_id=1, source_target_pairs={{0,8},{8,0},{16,24},{24,16},{1,9},{9,1},{17,25},{25,17},{2,10},{10... | collective-permute-start | bytes 3080 | tf_op jit(solution)/shard_map/ppermute | solution.py:287
  36.4 8.1 %collective-permute-start.18 = (bf16[128,256]{1,0:T(8,128)(2,1)S(1)}, bf16[128,256]{1,0:T(8,128)(2,1)S(1)}, u32[]{:S(2)}, u32[]{:S(2)}) collective-permute-start(bf16[128,256]{1,0:T(8,128)(2,1)S(1)} %bitcast.12), channel_id=1, source_target_pairs={{0,4},{1,5},{2,6},{3,7},{4,0},{5,1},{6,2},{7,3},{8,12},{9,13},{10,... | collective-permute-start | bytes 196616 | tf_op jit(solution)/shard_map/ppermute | solution.py:287
  38.6 7.2 %collective-permute-start.17 = (bf16[128,256]{1,0:T(8,128)(2,1)S(1)}, bf16[128,256]{1,0:T(8,128)(2,1)S(1)}, u32[]{:S(2)}, u32[]{:S(2)}) collective-permute-start(bf16[128,256]{1,0:T(8,128)(2,1)S(1)} %shard_map.167.refs_4_), channel_id=1, source_target_pairs={{0,4},{1,5},{2,6},{3,7},{4,0},{5,1},{6,2},{7,3},{8,12},{9,13},{10,... | collective-permute-start | bytes 196616 | tf_op jit(solution)/shard_map/ppermute | solution.py:287
  40.4 8.0 %collective-permute-start.13 = (bf16[128,256]{1,0:T(8,128)(2,1)S(1)}, bf16[128,256]{1,0:T(8,128)(2,1)S(1)}, u32[]{:S(2)}, u32[]{:S(2)}) collective-permute-start(bf16[128,256]{1,0:T(8,128)(2,1)S(1)} %shard_map.167.refs_4_), channel_id=1, source_target_pairs={{0,3},{1,2},{2,1},{3,0},{4,7},{5,6},{6,5},{7,4},{8,11},{9,10},{10,... | collective-permute-start | bytes 196616 | tf_op jit(solution)/shard_map/ppermute | solution.py:287
  42.0 8.1 %collective-permute-start.12 = (bf16[128,256]{1,0:T(8,128)(2,1)S(1)}, bf16[128,256]{1,0:T(8,128)(2,1)S(1)}, u32[]{:S(2)}, u32[]{:S(2)}) collective-permute-start(bf16[128,256]{1,0:T(8,128)(2,1)S(1)} %shard_map.167.refs_4_), channel_id=1, source_target_pairs={{0,2},{1,3},{2,0},{3,1},{4,6},{5,7},{6,4},{7,5},{8,10},{9,11},{10,... | collective-permute-start | bytes 196616 | tf_op jit(solution)/shard_map/ppermute | solution.py:287
  43.0 7.2 %collective-permute-start.11 = (bf16[128,256]{1,0:T(8,128)(2,1)S(1)}, bf16[128,256]{1,0:T(8,128)(2,1)S(1)}, u32[]{:S(2)}, u32[]{:S(2)}) collective-permute-start(bf16[128,256]{1,0:T(8,128)(2,1)S(1)} %shard_map.167.refs_4_), channel_id=1, source_target_pairs={{0,1},{1,0},{2,3},{3,2},{4,5},{5,4},{6,7},{7,6},{8,9},{9,8},{10,11... | collective-permute-start | bytes 196616 | tf_op jit(solution)/shard_map/ppermute | solution.py:287
  45.8 7.1 %collective-permute-start.21 = (bf16[128,512]{1,0:T(8,128)(2,1)S(1)}, bf16[128,512]{1,0:T(8,128)(2,1)S(1)}, u32[]{:S(2)}, u32[]{:S(2)}) collective-permute-start(bf16[128,512]{1,0:T(8,128)(2,1)S(1)} %shard_map.170.refs_4_), channel_id=1, source_target_pairs={{0,3},{1,2},{2,1},{3,0},{4,7},{5,6},{6,5},{7,4},{8,11},{9,10},{10,... | collective-permute-start | bytes 393224 | tf_op jit(solution)/shard_map/ppermute | solution.py:287
  46.1 8.5 %collective-permute-start.20 = (bf16[128,512]{1,0:T(8,128)(2,1)S(1)}, bf16[128,512]{1,0:T(8,128)(2,1)S(1)}, u32[]{:S(2)}, u32[]{:S(2)}) collective-permute-start(bf16[128,512]{1,0:T(8,128)(2,1)S(1)} %shard_map.170.refs_4_), channel_id=1, source_target_pairs={{0,2},{1,3},{2,0},{3,1},{4,6},{5,7},{6,4},{7,5},{8,10},{9,11},{10,... | collective-permute-start | bytes 393224 | tf_op jit(solution)/shard_map/ppermute | solution.py:287
  48.4 6.2 %collective-permute-start.19 = (bf16[128,512]{1,0:T(8,128)(2,1)S(1)}, bf16[128,512]{1,0:T(8,128)(2,1)S(1)}, u32[]{:S(2)}, u32[]{:S(2)}) collective-permute-start(bf16[128,512]{1,0:T(8,128)(2,1)S(1)} %shard_map.170.refs_4_), channel_id=1, source_target_pairs={{0,1},{1,0},{2,3},{3,2},{4,5},{5,4},{6,7},{7,6},{8,9},{9,8},{10,11... | collective-permute-start | bytes 393224 | tf_op jit(solution)/shard_map/ppermute | solution.py:287
  58.3 22.4 %all-to-all-start.1 = ((bf16[8,32,576]{2,1,0:T(8,128)(2,1)}), bf16[8,32,576]{2,1,0:T(8,128)(2,1)S(1)}, u32[]{:S(2)}, u32[]{:S(2)}) async-start(bf16[8,32,576]{2,1,0:T(8,128)(2,1)} %bitcast.5), calls=%async_computation.1 | async-start | bytes 655360 | tf_op jit(solution)/shard_map/all_to_all | solution.py:372
  62.9 8.2 %collective-permute-start.14 = (bf16[128,256]{1,0:T(8,128)(2,1)S(1)}, bf16[128,256]{1,0:T(8,128)(2,1)S(1)}, u32[]{:S(2)}, u32[]{:S(2)}) collective-permute-start(bf16[128,256]{1,0:T(8,128)(2,1)S(1)} %get-tuple-element.66), channel_id=1, source_target_pairs={{0,1},{1,0},{2,3},{3,2},{4,5},{5,4},{6,7},{7,6},{8,9},{9,8},{10,11... | collective-permute-start | bytes 196616 | tf_op jit(solution)/shard_map/ppermute | solution.py:287
  64.9 15.0 %collective-permute-start.22 = (bf16[128,512]{1,0:T(8,128)(2,1)S(1)}, bf16[128,512]{1,0:T(8,128)(2,1)S(1)}, u32[]{:S(2)}, u32[]{:S(2)}) collective-permute-start(bf16[128,512]{1,0:T(8,128)(2,1)S(1)} %get-tuple-element.78), channel_id=1, source_target_pairs={{0,1},{1,0},{2,3},{3,2},{4,5},{5,4},{6,7},{7,6},{8,9},{9,8},{10,11... | collective-permute-start | bytes 393224 | tf_op jit(solution)/shard_map/ppermute | solution.py:287
  65.0 15.0 %collective-permute-start.23 = (bf16[128,512]{1,0:T(8,128)(2,1)S(1)}, bf16[128,512]{1,0:T(8,128)(2,1)S(1)}, u32[]{:S(2)}, u32[]{:S(2)}) collective-permute-start(bf16[128,512]{1,0:T(8,128)(2,1)S(1)} %get-tuple-element.79), channel_id=1, source_target_pairs={{0,2},{1,3},{2,0},{3,1},{4,6},{5,7},{6,4},{7,5},{8,10},{9,11},{10,... | collective-permute-start | bytes 393224 | tf_op jit(solution)/shard_map/ppermute | solution.py:287
  67.0 13.0 %collective-permute-start.24 = (bf16[128,512]{1,0:T(8,128)(2,1)S(1)}, bf16[128,512]{1,0:T(8,128)(2,1)S(1)}, u32[]{:S(2)}, u32[]{:S(2)}) collective-permute-start(bf16[128,512]{1,0:T(8,128)(2,1)S(1)} %get-tuple-element.80), channel_id=1, source_target_pairs={{0,3},{1,2},{2,1},{3,0},{4,7},{5,6},{6,5},{7,4},{8,11},{9,10},{10,... | collective-permute-start | bytes 393224 | tf_op jit(solution)/shard_map/ppermute | solution.py:287
  68.4 10.3 %collective-permute-start.15 = (bf16[128,256]{1,0:T(8,128)(2,1)S(1)}, bf16[128,256]{1,0:T(8,128)(2,1)S(1)}, u32[]{:S(2)}, u32[]{:S(2)}) collective-permute-start(bf16[128,256]{1,0:T(8,128)(2,1)S(1)} %get-tuple-element.67), channel_id=1, source_target_pairs={{0,2},{1,3},{2,0},{3,1},{4,6},{5,7},{6,4},{7,5},{8,10},{9,11},{10,... | collective-permute-start | bytes 196616 | tf_op jit(solution)/shard_map/ppermute | solution.py:287
  71.2 8.8 %collective-permute-start.16 = (bf16[128,256]{1,0:T(8,128)(2,1)S(1)}, bf16[128,256]{1,0:T(8,128)(2,1)S(1)}, u32[]{:S(2)}, u32[]{:S(2)}) collective-permute-start(bf16[128,256]{1,0:T(8,128)(2,1)S(1)} %get-tuple-element.68), channel_id=1, source_target_pairs={{0,3},{1,2},{2,1},{3,0},{4,7},{5,6},{6,5},{7,4},{8,11},{9,10},{10,... | collective-permute-start | bytes 196616 | tf_op jit(solution)/shard_map/ppermute | solution.py:287

commit v6 on v5

--- a/solution.py
+++ b/solution.py
@@ -11,6 +11,7 @@
 EPS_ROOT = 1e-05
 BF = jnp.bfloat16
 F32 = jnp.float32
+LANES = 128
 VMEM = pl.BlockSpec(memory_space=pltpu.VMEM)
 SMEM = pl.BlockSpec(memory_space=pltpu.SMEM)
 
@@ -56,15 +57,15 @@
     )(*args)
 
 
-def copying_call(kernel, outs, args, buffers):
+def copying_call(kernel, outs, place, args, buffers):
     return pl.pallas_call(
         kernel,
         out_shape=outs,
-        in_specs=[pl.BlockSpec(memory_space=pltpu.HBM)] * len(args),
+        in_specs=[SMEM] + [pl.BlockSpec(memory_space=pltpu.HBM)] * len(args),
         out_specs=[VMEM] * len(outs),
         scratch_shapes=[*buffers, pltpu.SemaphoreType.DMA((len(args),))],
         compiler_params=pltpu.CompilerParams(vmem_limit_bytes=56 << 20),
-    )(*args)
+    )(place, *args)
 
 
 def arr(shape, dtype):
@@ -79,27 +80,65 @@
         copy.wait()
 
 
-def token_pack_kernel(q, k, v, og, rates, gains, all_out, kv_out, gg_out, rate_out):
-    tokens, feat = gg_out.shape
-    rate = jnp.broadcast_to(rates[...], (feat, tokens)).T
-    values = (rate * v[0].astype(F32)).astype(BF)
-    all_out[:, 0:feat] = q[0]
-    all_out[:, feat : 2 * feat] = k[0]
-    all_out[:, 2 * feat : 3 * feat] = values
-    kv_out[:, 0:feat] = k[0]
-    kv_out[:, feat : 2 * feat] = values
-    gg_out[...] = gains[...] * og[0].astype(F32)
-    rate_out[...] = rate
-
-
-def weight_pack_kernel(group, slab, *refs):
-    args, (w_out, buf, sems) = refs[:6], refs[6:]
-    fetch(args, [buf.at[pl.ds(i, 1)] for i in range(6)], sems)
+def padded(rows):
+    return -(-rows // 16) * 16
+
+
+def tiles(cols):
+    return -(-cols // LANES)
+
+
+def put(out, at, value):
+    rows, cols = value.shape
+    for t in range(tiles(cols)):
+        wide = min(LANES, cols - t * LANES)
+        out[at : at + rows, 0:wide] = value[:, t * LANES : t * LANES + wide]
+        at += padded(rows)
+    return at
+
+
+def get(ref, at, rows, cols):
+    parts = []
+    for t in range(tiles(cols)):
+        wide = min(LANES, cols - t * LANES)
+        parts.append(ref[at : at + rows, 0:wide])
+        at += padded(rows)
+    return jnp.concatenate(parts, axis=1), at
+
+
+def message(*blocks):
+    return arr((sum(tiles(cols) * padded(rows) for rows, cols in blocks), LANES), BF)
+
+
+def pack_kernel(group, slab, place, *refs):
+    args, refs = refs[:12], refs[12:]
+    w_outs, near_outs, (kv_out, gg_out, rate_out), refs = (
+        refs[:group],
+        refs[group : 2 * group - 1],
+        refs[2 * group - 1 : 2 * group + 2],
+        refs[2 * group + 2 :],
+    )
+    buf, qb, kb, vb, ob, rb, gb, slabs, sems = refs
+    fetch(args, [buf.at[pl.ds(i, 1)] for i in range(6)] + [qb, kb, vb, ob, rb, gb], sems)
+    rank = place[1]
     for j in range(group):
         cols = pl.ds(j * slab, slab)
-        block = jnp.concatenate([buf[i, :, cols] for i in range(6)], axis=1)
-        for p in range(j, w_out.shape[0], group):
-            w_out[p] = block
+        slabs[j] = jnp.concatenate([buf[i, :, cols] for i in range(6)], axis=1)
+    tokens, feat = gg_out.shape
+    rate = jnp.broadcast_to(rb[...], (feat, tokens)).T
+    values = (rate * vb[0].astype(F32)).astype(BF)
+    for d in range(group):
+        block = slabs[rank ^ d]
+        w_outs[d][...] = block
+        if d:
+            out = near_outs[d - 1]
+            at = put(out, put(out, 0, block), qb[0])
+            if d == 1:
+                put(out, put(out, at, kb[0]), values)
+    kv_out[:, 0:feat] = kb[0]
+    kv_out[:, feat : 2 * feat] = values
+    gg_out[...] = gb[...] * ob[0].astype(F32)
+    rate_out[...] = rate
 
 
 def columns(w, slab):
@@ -116,12 +155,29 @@
     return [x[:, pl.ds(i * slab, slab)] for i in range(3)]
 
 
-def forward_kernel(slab, group, w, *refs):
-    queries, parts, normed_out = refs[:group], refs[group:-1], refs[-1]
+def forward_kernel(slab, group, place, q, *refs):
+    blocks, refs = refs[: -group - 4], refs[-group - 4 :]
+    parts, (normed_out, w, kv_out, buf) = refs[:group], refs[group:]
     own, feat = parts[0].shape
+    me, (_, rows, cols) = place[2], buf.shape
+    queries = [q[...]]
+    for d, block in enumerate(blocks):
+        if 0 < d < group:
+            value, at = get(block, 0, rows, cols)
+            tokens, at = get(block, at, own, feat)
+            queries.append(tokens)
+            if d == 1:
+                kv_out[...] = get(block, at, own, 2 * feat)[0]
+        else:
+            value = block[...]
+        buf[me ^ d] = value
+    if rows % 16:
+        w[...] = jnp.concatenate([buf[p].astype(F32) for p in range(buf.shape[0])], axis=0).astype(BF)
+    else:
+        w[...] = flat(buf[...])
     saved, init, norm_init, norm_saved = columns(w, slab)
     normed = [(saved[i] * (norm_init[i] / norm_saved[i])).astype(BF) for i in range(3)]
-    rows = stack(queries, slice(0, feat))
+    rows = jnp.concatenate(queries, axis=0)
     hidden = (silu_parts(mm(rows, normed[0]))[0] * mm(rows, normed[1])).astype(BF)
     out = mm_nt(hidden, normed[2]).astype(BF)
     for d in range(group):
@@ -167,11 +223,13 @@
     return delta_gate, delta_up, grads
 
 
-def near_kernel(slab, group, normed_ref, *refs):
-    q_near, od_near, outs, grads_out = refs[:group], refs[group : 2 * group], refs[2 * group : -1], refs[-1]
+def near_kernel(slab, group, rows_of_w, normed_ref, *refs):
+    msgs, od_near, outs, grads_out = refs[:group], refs[group : 2 * group], refs[2 * group : -1], refs[-1]
     own, feat = od_near[0].shape
     normed = thirds(normed_ref, slab)
-    delta_gate, delta_up, grads = query_side(stack(q_near, slice(0, feat)), stack(od_near), normed)
+    at = tiles(6 * slab) * padded(rows_of_w)
+    queries = [msgs[0][...]] + [get(m, at, own, feat)[0] for m in msgs[1:]]
+    delta_gate, delta_up, grads = query_side(jnp.concatenate(queries, axis=0), stack(od_near), normed)
     grad_q = (mm_nt(delta_gate, normed[0]) + mm_nt(delta_up, normed[1])).astype(BF)
     for d in range(group):
         outs[d][...] = grad_q[d * own : (d + 1) * own]
@@ -183,8 +241,8 @@
     kvs, (factors, rises) = refs[:group], refs[group:]
     feat = w.shape[0]
     init = [w[:, pl.ds((3 + i) * slab, slab)] for i in range(3)]
-    keys = stack(kvs, slice(-2 * feat, -feat))
-    values = stack(kvs, slice(-feat, None))
+    keys = stack(kvs, slice(0, feat))
+    values = stack(kvs, slice(feat, 2 * feat))
     k_gate = mm(keys, init[0])
     k_up = mm(keys, init[1])
     k_proj = mm(values, init[2])
@@ -200,29 +258,26 @@
 
 def backward_kernel(slab, group, tok_groups, place, w, normed_ref, grads, factors, rises, *refs):
     far = group * (tok_groups - 1)
-    kvs, pairs, outs, refs = refs[:group], refs[group : group + far], refs[group + far : -4], refs[-4:]
-    inner_out, far_od, far_q, sums = refs
+    kvs, pairs, outs, (inner_buf, sums) = refs[:group], refs[group : group + far], refs[group + far : -2], refs[-2:]
     feat = w.shape[0]
-    own = outs[0].shape[0]
-    for i in range(far):
-        far_od[i // group, i % group] = pairs[i][:, 0:feat]
-        far_q[i // group, i % group] = pairs[i][:, feat : 2 * feat]
+    tok_out, outs = outs[0], outs[1:]
+    own = tok_out.shape[0]
     normed = thirds(normed_ref, slab)
-    sums[...] = grads[...]
-
-    def other(e, carry):
-        more = query_side(flat(far_q[e]), flat(far_od[e]), normed)[2]
-        for i in range(3):
-            sums[i] += more[i]
-        return carry
-
-    lax.fori_loop(0, tok_groups - 1, other, 0)
+    total = [grads[i] for i in range(3)]
+    for e in range(tok_groups - 1):
+        these = pairs[e * group : (e + 1) * group]
+        more = query_side(stack(these, slice(feat, 2 * feat)), stack(these, slice(0, feat)), normed)[2]
+        total = [total[i] + more[i] for i in range(3)]
+        if tok_groups > 2:
+            for i in range(3):
+                sums[i] = total[i]
+            total = [sums[i] for i in range(3)]
 
     saved, init, norm_init, norm_saved = columns(w, slab)
     cots, direct = [], []
     once = jnp.where(place[0] == 0, 1.0, 0.0)
     for i in range(3):
-        apply_grad = sums[i]
+        apply_grad = total[i]
         col_dot = jnp.sum(saved[i] * apply_grad, axis=0, keepdims=True)
         cot = apply_grad * (norm_init[i] / norm_saved[i]) - saved[i] * (
             col_dot * norm_init[i] / (norm_saved[i] * norm_saved[i] * norm_saved[i])
@@ -231,8 +286,8 @@
         direct.append((cot + init[i] * (col_dot / (norm_init[i] * norm_saved[i]))) * once)
 
     init_bf = [w[:, pl.ds((3 + i) * slab, slab)] for i in range(3)]
-    keys = stack(kvs, slice(-2 * feat, -feat))
-    values = stack(kvs, slice(-feat, None))
+    keys = stack(kvs, slice(0, feat))
+    values = stack(kvs, slice(feat, 2 * feat))
     back_gate = mm(keys, cots[0])
     back_up = mm(keys, cots[1])
     back_hidden = mm(values, cots[2])
@@ -246,11 +301,21 @@
         + mm_nt(back_kup, init_bf[1])
     ).astype(BF)
     grad_v = (mm_nt(rises[0], cots[2]) + mm_nt(back_proj, init_bf[2])).astype(BF)
-    for d in range(group):
-        outs[d][:, 0:feat] = grad_k[d * own : (d + 1) * own]
-        outs[d][:, feat : 2 * feat] = grad_v[d * own : (d + 1) * own]
     inner = (mm_tn(keys, back_kgate), mm_tn(keys, back_kup), mm_tn(values, back_proj))
-    inner_out[...] = jnp.concatenate([inner[i] + direct[i] for i in range(3)], axis=1).astype(BF)
+    whole = jnp.concatenate([inner[i] + direct[i] for i in range(3)], axis=1)
+    rows = inner_buf.shape[1]
+    for p in range(inner_buf.shape[0]):
+        inner_buf[p] = whole[p * rows : (p + 1) * rows]
+    tok_out[:, 0:feat] = grad_k[0:own]
+    tok_out[:, feat : 2 * feat] = grad_v[0:own]
+    for d in range(inner_buf.shape[0]):
+        block = inner_buf[place[2] ^ d].astype(BF)
+        if 0 < d < group:
+            out = outs[d]
+            at = put(out, 0, grad_k[d * own : (d + 1) * own])
+            put(out, put(out, at, grad_v[d * own : (d + 1) * own]), block)
+        else:
+            outs[d][...] = block
 
 
 def total_of(refs):
@@ -260,24 +325,41 @@
     return total
 
 
-def tokens_kernel(group, rate, *refs):
-    queries, got, (gq, gk, gv) = refs[:group], refs[group:-3], refs[-3:]
-    feat = gq.shape[2]
+def final_kernel(group, slab, place, rate, tok, *refs):
+    queries, blocks, (gq, gk, gv, *outs, buf) = refs[:group], refs[group:-7], refs[-7:]
+    _, own, feat = gq.shape
+    rows = buf.shape[1]
     gq[0] = total_of(queries).astype(BF)
-    total = total_of(got)
-    gk[0] = total[:, 0:feat].astype(BF)
-    gv[0] = (rate[...] * total[:, feat : 2 * feat]).astype(BF)
-
-
-def weights_kernel(group, slab, got, *outs):
-    cols = []
-    for j in range(group):
-        total = got[j].astype(F32)
-        for p in range(j + group, got.shape[0], group):
-            total += got[p].astype(F32)
-        cols.append(total)
+    keys = tok[:, 0:feat].astype(F32)
+    values = tok[:, feat : 2 * feat].astype(F32)
+    for d in range(group):
+        if d:
+            more, at = get(blocks[d], 0, own, feat)
+            keys += more.astype(F32)
+            more, at = get(blocks[d], at, own, feat)
+            values += more.astype(F32)
+            block = get(blocks[d], at, rows, 3 * slab)[0]
+        else:
+            block = blocks[d][...]
+        buf[d] = block.astype(F32)
+        for other in blocks[d + group :: group]:
+            buf[d] += other[...].astype(F32)
+    gk[0] = keys.astype(BF)
+    gv[0] = (rate[...] * values).astype(BF)
+    cols = [buf[place[1] ^ j] for j in range(group)]
     for i in range(3):
         outs[i][0] = jnp.concatenate([c[:, i * slab : (i + 1) * slab] for c in cols], axis=1)
+
+
+def mixed(seq_n, group, lead):
+    near, far = list(range(1, group)), list(range(group, seq_n))
+    first, second = (far, near) if lead == 2 else (near, far)
+    order = first[:2]
+    first = first[2:]
+    while first or second:
+        order += second[:1] + first[:1]
+        first, second = first[1:], second[1:]
+    return order
 
 
 def make_local(seq_n, head_n, group):
@@ -300,34 +382,55 @@
         me = lax.axis_index("seq")
         place = jnp.stack((lax.div(me, group), lax.rem(me, group), me)).astype(jnp.int32)
 
-        (packed,) = copying_call(
-            functools.partial(weight_pack_kernel, group, slab),
-            (arr((seq_n, rows, 6 * slab), BF),),
-            (gs, us, ds, gi, ui, di),
-            [pltpu.VMEM((6, rows, hidden), BF)],
-        )
-        packed, queries = lax.optimization_barrier((packed, q[0]))
-        wall = lax.all_to_all(packed, "seq", 0, 0, tiled=True).reshape(seq_n * rows, 6 * slab)
-        tokens, kv, gg, rate = call(
-            token_pack_kernel,
-            (arr((own, 3 * feat), BF), arr((own, 2 * feat), BF), arr((own, feat), F32), arr((own, feat), F32)),
-            (q, k, v, og, rates, gains),
-            8,
-        )
-        beside = move(tokens, 1) if group > 1 else None
-        rest = range(2, group)
-        q_near = [queries, beside][:group] + [move(queries, d) for d in rest]
-        kv_near = [kv, beside][:group] + [move(kv, d) for d in rest]
-
-        block = arr((own, feat), BF)
+        w_block, q_block = (rows, 6 * slab), (own, feat)
+        near_msgs = [
+            message(w_block, q_block, *((q_block, q_block) if d == 1 else ())) for d in range(1, group)
+        ]
+        args = (gs, us, ds, gi, ui, di, q, k, v, og, rates, gains)
+        packed = copying_call(
+            functools.partial(pack_kernel, group, slab),
+            (
+                *(arr(w_block, BF),) * group,
+                *near_msgs,
+                arr((own, 2 * feat), BF),
+                arr(q_block, F32),
+                arr(q_block, F32),
+            ),
+            place,
+            args,
+            [
+                pltpu.VMEM((6, rows, hidden), BF),
+                *[pltpu.VMEM(x.shape, x.dtype) for x in args[6:]],
+                pltpu.VMEM((group, rows, 6 * slab), BF),
+            ],
+        )
+        w_blocks, near_blocks, (kv, gg, rate) = packed[:group], packed[group:-3], packed[-3:]
+        sends = {d: w_blocks[d % group] for d in range(group, seq_n)}
+        sends.update({d: near_blocks[d - 1] for d in range(1, group)})
+        got = {0: w_blocks[0]}
+        for d in mixed(seq_n, group, 2):
+            got[d] = move(sends[d], d)
+        kv_far = [move(kv, d) for d in range(2, group)]
+        queries = q[0]
+
+        block = arr(q_block, BF)
         mflop = 2 * near * feat * slab
-        *parts, normed = call(
+        *parts, normed, wall, kv_one = call(
             functools.partial(forward_kernel, slab, group),
-            (*(block,) * group, arr((seq_n * rows, 3 * slab), BF)),
-            (wall, *q_near),
+            (
+                *(block,) * group,
+                arr((seq_n * rows, 3 * slab), BF),
+                arr((seq_n * rows, 6 * slab), BF),
+                arr((own, 2 * feat), BF),
+            ),
+            (place, queries, *[got[d] for d in range(seq_n)]),
             24,
+            smem=1,
             flops=3 * mflop,
-        )
+            scratch=[pltpu.VMEM((seq_n, rows, 6 * slab), BF)],
+        )
+        kv_near = [kv, kv_one, *kv_far][:group]
+        q_near = [queries] + [got[d] for d in range(1, group)]
         parts = [parts[0]] + [move(parts[d], d) for d in range(1, group)]
         *parts, kv_near = lax.optimization_barrier((*parts, kv_near))
         apply_out, sums = call(
@@ -351,7 +454,7 @@
         ]
         pairs = [x for m in pairs for x in near_all(m)]
         *grad_q, grads = call(
-            functools.partial(near_kernel, slab, group),
+            functools.partial(near_kernel, slab, group, rows),
             (*(block,) * group, arr((3, seq_n * rows, slab), F32)),
             (normed, *q_near, *od_near),
             24,
@@ -359,25 +462,40 @@
         )
         grad_q = [grad_q[0]] + [move(grad_q[d], d) for d in range(1, group)]
 
-        far = pltpu.VMEM((max(tok_groups - 1, 1), group, own, feat), BF)
-        *tok, inner = call(
+        pairs = list(pairs)
+        *tok_inner, = call(
             functools.partial(backward_kernel, slab, group, tok_groups),
-            (*(arr((own, 2 * feat), BF),) * group, arr((seq_n * rows, 3 * slab), BF)),
+            (
+                arr((own, 2 * feat), BF),
+                *[
+                    message(q_block, q_block, (rows, 3 * slab)) if 0 < d < group else arr((rows, 3 * slab), BF)
+                    for d in range(seq_n)
+                ],
+            ),
             (place, wall, normed, grads, factors, rises, *kv_near, *pairs),
-            32,
+            40,
             smem=1,
             flops=24 * mflop,
-            scratch=[far, far, pltpu.VMEM((3, seq_n * rows, slab), F32)],
-        )
-        inner = lax.all_to_all(inner.reshape(seq_n, rows, 3 * slab), "seq", 0, 0, tiled=True)
-        tok = [tok[0]] + [move(tok[d], d) for d in range(1, group)]
+            scratch=[
+                pltpu.VMEM((seq_n, rows, 3 * slab), F32),
+                pltpu.VMEM((3, seq_n * rows, slab), F32),
+            ],
+        )
+        tok_inner, grad_q = lax.optimization_barrier((tok_inner, grad_q))
+        tok, sends = tok_inner[0], tok_inner[1:]
+        got = {0: sends[0]}
+        for d in mixed(seq_n, group, 1):
+            got[d] = move(sends[d], d)
         out_tok = arr((1, own, feat), BF)
         grad_w = arr((1, rows, hidden), F32)
-        grads_t = call(
-            functools.partial(tokens_kernel, group), (out_tok,) * 3, (rate, *grad_q, *tok), 16
-        )
-        grads_w = call(functools.partial(weights_kernel, group, slab), (grad_w,) * 3, (inner,), 16)
-        return (*grads_t, *grads_w)
+        return call(
+            functools.partial(final_kernel, group, slab),
+            (*(out_tok,) * 3, *(grad_w,) * 3),
+            (place, rate, tok, *grad_q, *[got[d] for d in range(seq_n)]),
+            16,
+            smem=1,
+            scratch=[pltpu.VMEM((group, rows, 3 * slab), F32)],
+        )
 
     return local
 

time: 81.9 us -> 88.9 us (1.085)
  waiting for transfers between devices: 26.5 us -> 29.5 us
  local copies, waits for them, and re-layouts: 1.35 us -> 4.15 us
    all_to_all x2 -> x0, starting transfers between devices: 11.9 us -> none  [the longest x1 7.26 us: local(): lax.all_to_all(packed, 'seq', 0, 0, tiled=True)]
    ppermute x25 -> x33, starting transfers between devices: 31 us -> 42.8 us  [move(): return lax.ppermute(x, axis, [(i, i ^ dist) for i in range(size)])]
    ppermute x25 -> x33, waiting for transfers between devices: 26.5 us -> 29.5 us  [move(): return lax.ppermute(x, axis, [(i, i ^ dist) for i in range(size)])]
    unnamed x12 -> x18, local copies, waits for them, and re-layouts: 1.35 us -> 4.15 us
    pallas_call x1, Pallas kernels: 1.97 us -> 3.04 us  [copying_call(): pl.pallas_call(kernel, out_shape=outs, in_specs=[SMEM] + [pl.BlockSpec(me...]
    pallas_call x10 -> x8, Pallas kernels: 7.95 us -> 7.66 us  [call(): pl.pallas_call(kernel, out_shape=outs, in_specs=[SMEM] * smem + [VMEM] *...]
  transfers between devices with their start and end apart: 27 -> 33, of which waited for: 14 -> 14; matrix products, arithmetic and copies ran while one was open for 0% -> 0% of each run, Pallas kernels for 4% -> 7%
where the time goes in v6:
time: 88.9 us; the launch traced here: 88.6 us
  starting transfers between devices  42.8 us (48%)
  waiting for transfers between devices  29.5 us (33%)
  Pallas kernels  10.7 us (12%)
  local copies, waits for them, and re-layouts  4.15 us (5%)
    ppermute x33, starting transfers between devices, move(): return lax.ppermute(x, axis, [(i, i ^ dist) for i in range(size)])  42.8 us
    ppermute x33, waiting for transfers between devices, move(): return lax.ppermute(x, axis, [(i, i ^ dist) for i in range(size)])  29.5 us
    pallas_call x8, Pallas kernels, call(): pl.pallas_call(kernel, out_shape=outs, in_specs=[SMEM] * smem + [VMEM] *...  7.66 us
    unnamed x18, local copies, waits for them, and re-layouts  4.15 us
    pallas_call x1, Pallas kernels, copying_call(): pl.pallas_call(kernel, out_shape=outs, in_specs=[SMEM] + [pl.BlockSpec(me...  3.04 us
  transfers between devices with their start and end apart: 33, of which 14 were waited for; matrix products, arithmetic and copies ran while one was open for 0% of the time, Pallas kernels for 7%

profile of v6, /device:TPU:0, one launch (start us, length us, event | category | flops | bytes accessed | tf_op | source)
XLA Modules:
  0.0 88.6 jit_solution(10210910734437431429)
XLA Ops:
  0.6 0.6 pad_add_fusion.place
  1.2 3.0 %shard_map.163 = (bf16[32,1152]{1,0:T(8,128)(2,1)}, bf16[32,1152]{1,0:T(8,128)(2,1)}, bf16[32,1152]{1,0:T(8,128)(2,1)}, bf16[32,1152]{1,0:T(8,128)(2,1)}, bf16[1...) custom-call(s32[3]{0:T(128)} %pad_add_fusion.place, ...), custom_call_target="tpu_custom_call" | custom-call | tf_op jit(solution)/shard_map/pallas_call | solution.py:61
  4.3 3.0 %collective-permute-start = (bf16[1056,128]{1,0:T(8,128)(2,1)}, bf16[1056,128]{1,0:T(8,128)(2,1)S(1)}, u32[]{:S(2)}, u32[]{:S(2)}) collective-permute-start(bf16[1056,128]{1,0:T(8,128)(2,1)} %get-tuple-element.66), channel_id=1, source_target_pairs={{0,1},{1,0},{2,3},{3,2},{4,5},{5,4},{6,7},{7,6},{8,9},{9,8},{10,11... | collective-permute-start | bytes 811016 | tf_op jit(solution)/shard_map/ppermute | solution.py:369
  7.3 2.6 %collective-permute-start.4 = (bf16[32,1152]{1,0:T(8,128)(2,1)}, bf16[32,1152]{1,0:T(8,128)(2,1)S(1)}, u32[]{:S(2)}, u32[]{:S(2)}) collective-permute-start(bf16[32,1152]{1,0:T(8,128)(2,1)} %get-tuple-element.69), channel_id=1, source_target_pairs={{0,5},{1,4},{2,7},{3,6},{4,1},{5,0},{6,3},{7,2},{8,13},{9,12},{10,... | collective-permute-start | bytes 221192 | tf_op jit(solution)/shard_map/ppermute | solution.py:369
  9.8 1.3 %collective-permute-start.5 = (bf16[32,1152]{1,0:T(8,128)(2,1)}, bf16[32,1152]{1,0:T(8,128)(2,1)S(1)}, u32[]{:S(2)}, u32[]{:S(2)}) collective-permute-start(bf16[32,1152]{1,0:T(8,128)(2,1)} %get-tuple-element.70), channel_id=1, source_target_pairs={{0,6},{1,7},{2,4},{3,5},{4,2},{5,3},{6,0},{7,1},{8,14},{9,15},{10,... | collective-permute-start | bytes 221192 | tf_op jit(solution)/shard_map/ppermute | solution.py:369
  11.2 0.2 collective-permute-start.1
  11.4 2.7 %collective-permute-start.2 = (bf16[544,128]{1,0:T(8,128)(2,1)}, bf16[544,128]{1,0:T(8,128)(2,1)S(1)}, u32[]{:S(2)}, u32[]{:S(2)}) collective-permute-start(bf16[544,128]{1,0:T(8,128)(2,1)} %get-tuple-element.68), channel_id=1, source_target_pairs={{0,3},{1,2},{2,1},{3,0},{4,7},{5,6},{6,5},{7,4},{8,11},{9,10},{10,... | collective-permute-start | bytes 417800 | tf_op jit(solution)/shard_map/ppermute | solution.py:369
  14.1 1.6 %collective-permute-done.4.refs_5_ = bf16[32,1152]{1,0:T(8,128)(2,1)S(1)} collective-permute-done((bf16[32,1152]{1,0:T(8,128)(2,1)}, bf16[32,1152]{1,0:T(8,128)(2,1)S(1)}, u32[]{:S(2)}, u32[]{:S(2)}) %collective-permute-start.4) | collective-permute-done | bytes 73760 | tf_op jit(solution)/shard_map/ppermute | solution.py:369
  15.8 4.2 %collective-permute-start.6 = (bf16[32,1152]{1,0:T(8,128)(2,1)}, bf16[32,1152]{1,0:T(8,128)(2,1)S(1)}, u32[]{:S(2)}, u32[]{:S(2)}) collective-permute-start(bf16[32,1152]{1,0:T(8,128)(2,1)} %get-tuple-element.71), channel_id=1, source_target_pairs={{0,7},{1,6},{2,5},{3,4},{4,3},{5,2},{6,1},{7,0},{8,15},{9,14},{10,... | collective-permute-start | bytes 221192 | tf_op jit(solution)/shard_map/ppermute | solution.py:369
  20.0 0.0 collective-permute-start.3
  20.0 4.7 %collective-permute-done.6.refs_7_ = bf16[32,1152]{1,0:T(8,128)(2,1)S(1)} collective-permute-done((bf16[32,1152]{1,0:T(8,128)(2,1)}, bf16[32,1152]{1,0:T(8,128)(2,1)S(1)}, u32[]{:S(2)}, u32[]{:S(2)}) %collective-permute-start.6) | collective-permute-done | bytes 73760 | tf_op jit(solution)/shard_map/ppermute | solution.py:369
  24.7 0.0 collective-permute-start.11
  24.7 1.4 %collective-permute-done.3.refs_4_ = bf16[32,1152]{1,0:T(8,128)(2,1)S(1)} collective-permute-done((bf16[32,1152]{1,0:T(8,128)(2,1)}, bf16[32,1152]{1,0:T(8,128)(2,1)S(1)}, u32[]{:S(2)}, u32[]{:S(2)}) %collective-permute-start.3) | collective-permute-done | bytes 73760 | tf_op jit(solution)/shard_map/ppermute | solution.py:369
  26.1 0.5 collective-permute-start.10
  26.6 0.0 collective-permute-done.1.refs_2_
  26.6 0.0 collective-permute-done.2.refs_3_
  26.6 0.0 collective-permute-done.refs_1_
  26.6 0.0 copy-start.1
  26.6 0.8 copy-done.1
  27.4 0.9 copy-done.6
  28.3 0.6 copy-done.7
  28.9 1.4 %shard_map.164 = (bf16[128,256]{1,0:T(8,128)(2,1)S(1)}, bf16[128,256]{1,0:T(8,128)(2,1)S(1)}, bf16[128,256]{1,0:T(8,128)(2,1)S(1)}, bf16[128,256]{1,0:T(8,128)(2...) custom-call(s32[3]{0:T(128)S(1)} %copy-done.7, ...), custom_call_target="tpu_custom_call" | custom-call | flops 150994944 | bytes 2261004 | tf_op jit(solution)/shard_map/pallas_call | solution.py:49
  30.3 1.7 %collective-permute-start.7 = (bf16[128,256]{1,0:T(8,128)(2,1)S(1)}, bf16[128,256]{1,0:T(8,128)(2,1)S(1)}, u32[]{:S(2)}, u32[]{:S(2)}) collective-permute-start(bf16[128,256]{1,0:T(8,128)(2,1)S(1)} %get-tuple-element.76), channel_id=1, source_target_pairs={{0,1},{1,0},{2,3},{3,2},{4,5},{5,4},{6,7},{7,6},{8,9},{9,8},{10,11... | collective-permute-start | bytes 196616 | tf_op jit(solution)/shard_map/ppermute | solution.py:369
  32.0 1.5 %collective-permute-start.8 = (bf16[128,256]{1,0:T(8,128)(2,1)S(1)}, bf16[128,256]{1,0:T(8,128)(2,1)S(1)}, u32[]{:S(2)}, u32[]{:S(2)}) collective-permute-start(bf16[128,256]{1,0:T(8,128)(2,1)S(1)} %get-tuple-element.77), channel_id=1, source_target_pairs={{0,2},{1,3},{2,0},{3,1},{4,6},{5,7},{6,4},{7,5},{8,10},{9,11},{10,... | collective-permute-start | bytes 196616 | tf_op jit(solution)/shard_map/ppermute | solution.py:369
  33.5 0.4 collective-permute-start.9
  33.9 0.8 collective-permute-done.7.refs_1_
  34.6 1.9 %collective-permute-done.8.refs_2_ = bf16[128,256]{1,0:T(8,128)(2,1)S(1)} collective-permute-done((bf16[128,256]{1,0:T(8,128)(2,1)S(1)}, bf16[128,256]{1,0:T(8,128)(2,1)S(1)}, u32[]{:S(2)}, u32[]{:S(2)}) %collective-permute-start.8) | collective-permute-done | bytes 65568 | tf_op jit(solution)/shard_map/ppermute | solution.py:369
  36.5 2.1 %collective-permute-done.9.refs_3_ = bf16[128,256]{1,0:T(8,128)(2,1)S(1)} collective-permute-done((bf16[128,256]{1,0:T(8,128)(2,1)S(1)}, bf16[128,256]{1,0:T(8,128)(2,1)S(1)}, u32[]{:S(2)}, u32[]{:S(2)}) %collective-permute-start.9) | collective-permute-done | bytes 65568 | tf_op jit(solution)/shard_map/ppermute | solution.py:369
  38.7 0.9 %copy-done = f32[128,256]{1,0:T(8,128)S(1)} copy-done((f32[128,256]{1,0:T(8,128)S(1)}, f32[128,256]{1,0:T(8,128)}, u32[]{:S(2)}) %copy-start) | copy-done | bytes 131096
  39.6 0.1 shard_map.165
  39.7 0.1 collective-permute-start.14
  39.8 1.6 %collective-permute-start.13 = (f32[2,128]{1,0:T(2,128)S(1)}, f32[2,128]{1,0:T(2,128)S(1)}, u32[]{:S(2)}, u32[]{:S(2)}) collective-permute-start(f32[2,128]{1,0:T(2,128)S(1)} %get-tuple-element.87.refs_0_), channel_id=1, source_target_pairs={{0,16},{8,24},{16,0},{24,8},{1,17},{9,25},{17,1},{25,9},{2,18},{10... | collective-permute-start | bytes 3080 | tf_op jit(solution)/shard_map/ppermute | solution.py:369
  41.4 0.3 collective-permute-start.12
  41.6 1.9 %collective-permute-start.19 = (bf16[128,256]{1,0:T(8,128)(2,1)S(1)}, bf16[128,256]{1,0:T(8,128)(2,1)S(1)}, u32[]{:S(2)}, u32[]{:S(2)}) collective-permute-start(bf16[128,256]{1,0:T(8,128)(2,1)S(1)} %bitcast.5), channel_id=1, source_target_pairs={{0,4},{1,5},{2,6},{3,7},{4,0},{5,1},{6,2},{7,3},{8,12},{9,13},{10,... | collective-permute-start | bytes 196616 | tf_op jit(solution)/shard_map/ppermute | solution.py:369
  43.6 0.1 shard_map.166.refs_4_
  43.7 1.8 %collective-permute-start.18 = (bf16[128,256]{1,0:T(8,128)(2,1)S(1)}, bf16[128,256]{1,0:T(8,128)(2,1)S(1)}, u32[]{:S(2)}, u32[]{:S(2)}) collective-permute-start(bf16[128,256]{1,0:T(8,128)(2,1)S(1)} %shard_map.166.refs_4_), channel_id=1, source_target_pairs={{0,4},{1,5},{2,6},{3,7},{4,0},{5,1},{6,2},{7,3},{8,12},{9,13},{10,... | collective-permute-start | bytes 196616 | tf_op jit(solution)/shard_map/ppermute | solution.py:369
  45.5 0.7 collective-permute-start.17
  46.2 3.4 %collective-permute-done.19.right = bf16[128,256]{1,0:T(8,128)(2,1)S(1)} collective-permute-done((bf16[128,256]{1,0:T(8,128)(2,1)S(1)}, bf16[128,256]{1,0:T(8,128)(2,1)S(1)}, u32[]{:S(2)}, u32[]{:S(2)}) %collective-permute-start.19) | collective-permute-done | bytes 65568 | tf_op jit(solution)/shard_map/ppermute | solution.py:369
  49.6 1.3 %collective-permute-done.18.left = bf16[128,256]{1,0:T(8,128)(2,1)S(1)} collective-permute-done((bf16[128,256]{1,0:T(8,128)(2,1)S(1)}, bf16[128,256]{1,0:T(8,128)(2,1)S(1)}, u32[]{:S(2)}, u32[]{:S(2)}) %collective-permute-start.18) | collective-permute-done | bytes 65568 | tf_op jit(solution)/shard_map/ppermute | solution.py:369
  51.0 0.1 collective-permute-start.22
  51.1 2.0 %collective-permute-start.21 = (bf16[128,512]{1,0:T(8,128)(2,1)S(1)}, bf16[128,512]{1,0:T(8,128)(2,1)S(1)}, u32[]{:S(2)}, u32[]{:S(2)}) collective-permute-start(bf16[128,512]{1,0:T(8,128)(2,1)S(1)} %shard_map.169.refs_4_), channel_id=1, source_target_pairs={{0,2},{1,3},{2,0},{3,1},{4,6},{5,7},{6,4},{7,5},{8,10},{9,11},{10,... | collective-permute-start | bytes 393224 | tf_op jit(solution)/shard_map/ppermute | solution.py:369
  53.1 1.5 %collective-permute-start.20 = (bf16[128,512]{1,0:T(8,128)(2,1)S(1)}, bf16[128,512]{1,0:T(8,128)(2,1)S(1)}, u32[]{:S(2)}, u32[]{:S(2)}) collective-permute-start(bf16[128,512]{1,0:T(8,128)(2,1)S(1)} %shard_map.169.refs_4_), channel_id=1, source_target_pairs={{0,1},{1,0},{2,3},{3,2},{4,5},{5,4},{6,7},{7,6},{8,9},{9,8},{10,11... | collective-permute-start | bytes 393224 | tf_op jit(solution)/shard_map/ppermute | solution.py:369
  54.6 0.6 collective-permute-start.15
  55.2 0.9 %copy-done.4 = bf16[128,512]{1,0:T(8,128)(2,1)S(1)} copy-done((bf16[128,512]{1,0:T(8,128)(2,1)S(1)}, bf16[128,512]{1,0:T(8,128)(2,1)}, u32[]{:S(2)}) %copy-start.4) | copy-done | bytes 131096
  56.1 0.7 shard_map.168
  56.9 3.5 %collective-permute-done.16.refs_6_ = bf16[128,256]{1,0:T(8,128)(2,1)S(1)} collective-permute-done((bf16[128,256]{1,0:T(8,128)(2,1)S(1)}, bf16[128,256]{1,0:T(8,128)(2,1)S(1)}, u32[]{:S(2)}, u32[]{:S(2)}) %collective-permute-start.16) | collective-permute-done | bytes 65568 | tf_op jit(solution)/shard_map/ppermute | solution.py:369
  60.4 1.3 %collective-permute-done.15.refs_5_ = bf16[128,256]{1,0:T(8,128)(2,1)S(1)} collective-permute-done((bf16[128,256]{1,0:T(8,128)(2,1)S(1)}, bf16[128,256]{1,0:T(8,128)(2,1)S(1)}, u32[]{:S(2)}, u32[]{:S(2)}) %collective-permute-start.15) | collective-permute-done | bytes 65568 | tf_op jit(solution)/shard_map/ppermute | solution.py:369
  61.6 0.8 shard_map.167
  62.5 0.6 collective-permute-start.23
  63.1 0.3 collective-permute-start.24
  63.4 2.6 %collective-permute-start.25 = (bf16[128,256]{1,0:T(8,128)(2,1)S(1)}, bf16[128,256]{1,0:T(8,128)(2,1)S(1)}, u32[]{:S(2)}, u32[]{:S(2)}) collective-permute-start(bf16[128,256]{1,0:T(8,128)(2,1)S(1)} %get-tuple-element.108), channel_id=1, source_target_pairs={{0,3},{1,2},{2,1},{3,0},{4,7},{5,6},{6,5},{7,4},{8,11},{9,10},{10,... | collective-permute-start | bytes 196616 | tf_op jit(solution)/shard_map/ppermute | solution.py:369
  66.0 3.0 %shard_map.170 = (bf16[128,512]{1,0:T(8,128)(2,1)S(1)}, bf16[32,576]{1,0:T(8,128)(2,1)S(1)}, bf16[672,128]{1,0:T(8,128)(2,1)S(1)}, bf16[672,128]{1,0:T(8,128)(2,...) custom-call(s32[3]{0:T(128)S(1)} %copy-done.8, ...), custom_call_target="tpu_custom_call" | custom-call | flops 1207959552 | bytes 5517324 | tf_op jit(solution)/shard_map/pallas_call | solution.py:49
  69.0 0.1 collective-permute-done.25.refs_3_
  69.1 0.8 collective-permute-start.26
  69.9 1.9 %collective-permute-start.27 = (bf16[672,128]{1,0:T(8,128)(2,1)S(1)}, bf16[672,128]{1,0:T(8,128)(2,1)S(1)}, u32[]{:S(2)}, u32[]{:S(2)}) collective-permute-start(bf16[672,128]{1,0:T(8,128)(2,1)S(1)} %get-tuple-element.116), channel_id=1, source_target_pairs={{0,2},{1,3},{2,0},{3,1},{4,6},{5,7},{6,4},{7,5},{8,10},{9,11},{10,... | collective-permute-start | bytes 516104 | tf_op jit(solution)/shard_map/ppermute | solution.py:369
  71.7 0.9 collective-permute-start.28
  72.6 1.3 %collective-permute-start.29 = (bf16[32,576]{1,0:T(8,128)(2,1)S(1)}, bf16[32,576]{1,0:T(8,128)(2,1)S(1)}, u32[]{:S(2)}, u32[]{:S(2)}) collective-permute-start(bf16[32,576]{1,0:T(8,128)(2,1)S(1)} %get-tuple-element.118), channel_id=1, source_target_pairs={{0,4},{1,5},{2,6},{3,7},{4,0},{5,1},{6,2},{7,3},{8,12},{9,13},{10,... | collective-permute-start | bytes 110600 | tf_op jit(solution)/shard_map/ppermute | solution.py:369
  73.9 1.8 %collective-permute-start.30 = (bf16[32,576]{1,0:T(8,128)(2,1)S(1)}, bf16[32,576]{1,0:T(8,128)(2,1)S(1)}, u32[]{:S(2)}, u32[]{:S(2)}) collective-permute-start(bf16[32,576]{1,0:T(8,128)(2,1)S(1)} %get-tuple-element.119), channel_id=1, source_target_pairs={{0,5},{1,4},{2,7},{3,6},{4,1},{5,0},{6,3},{7,2},{8,13},{9,12},{10,... | collective-permute-start | bytes 110600 | tf_op jit(solution)/shard_map/ppermute | solution.py:369
  75.7 3.3 %collective-permute-done.29.refs_8_ = bf16[32,576]{1,0:T(8,128)(2,1)S(1)} collective-permute-done((bf16[32,576]{1,0:T(8,128)(2,1)S(1)}, bf16[32,576]{1,0:T(8,128)(2,1)S(1)}, u32[]{:S(2)}, u32[]{:S(2)}) %collective-permute-start.29) | collective-permute-done | bytes 36896 | tf_op jit(solution)/shard_map/ppermute | solution.py:369
  79.1 1.4 %collective-permute-start.31 = (bf16[32,576]{1,0:T(8,128)(2,1)S(1)}, bf16[32,576]{1,0:T(8,128)(2,1)S(1)}, u32[]{:S(2)}, u32[]{:S(2)}) collective-permute-start(bf16[32,576]{1,0:T(8,128)(2,1)S(1)} %get-tuple-element.120), channel_id=1, source_target_pairs={{0,6},{1,7},{2,4},{3,5},{4,2},{5,3},{6,0},{7,1},{8,14},{9,15},{10,... | collective-permute-start | bytes 110600 | tf_op jit(solution)/shard_map/ppermute | solution.py:369
  80.4 2.7 %collective-permute-start.32 = (bf16[32,576]{1,0:T(8,128)(2,1)S(1)}, bf16[32,576]{1,0:T(8,128)(2,1)S(1)}, u32[]{:S(2)}, u32[]{:S(2)}) collective-permute-start(bf16[32,576]{1,0:T(8,128)(2,1)S(1)} %get-tuple-element.121), channel_id=1, source_target_pairs={{0,7},{1,6},{2,5},{3,4},{4,3},{5,2},{6,1},{7,0},{8,15},{9,14},{10,... | collective-permute-start | bytes 110600 | tf_op jit(solution)/shard_map/ppermute | solution.py:369
  83.1 1.8 %collective-permute-done.31.refs_10_ = bf16[32,576]{1,0:T(8,128)(2,1)S(1)} collective-permute-done((bf16[32,576]{1,0:T(8,128)(2,1)S(1)}, bf16[32,576]{1,0:T(8,128)(2,1)S(1)}, u32[]{:S(2)}, u32[]{:S(2)}) %collective-permute-start.31) | collective-permute-done | bytes 36896 | tf_op jit(solution)/shard_map/ppermute | solution.py:369
  84.9 2.2 %collective-permute-done.32.refs_11_ = bf16[32,576]{1,0:T(8,128)(2,1)S(1)} collective-permute-done((bf16[32,576]{1,0:T(8,128)(2,1)S(1)}, bf16[32,576]{1,0:T(8,128)(2,1)S(1)}, u32[]{:S(2)}, u32[]{:S(2)}) %collective-permute-start.32) | collective-permute-done | bytes 36896 | tf_op jit(solution)/shard_map/ppermute | solution.py:369
  87.2 1.5 %shard_map.171 = (bf16[1,128,256]{2,1,0:T(8,128)(2,1)}, bf16[1,128,256]{2,1,0:T(8,128)(2,1)}, bf16[1,128,256]{2,1,0:T(8,128)(2,1)}, f32[1,32,768]{2,1,0:T(8,128)...) custom-call(s32[3]{0:T(128)S(1)} %copy-done.8, f32[128,256]{1,0:T(8,128)S(1)} %copy-done.3, ...), custom_call_target="tpu_custom_call" | custom-call | bytes 1716236 | tf_op jit(solution)/shard_map/pallas_call | solution.py:49
  (30 shorter events, 0.1 us)
Async XLA Ops:
  4.3 22.3 %collective-permute-start = (bf16[1056,128]{1,0:T(8,128)(2,1)}, bf16[1056,128]{1,0:T(8,128)(2,1)S(1)}, u32[]{:S(2)}, u32[]{:S(2)}) collective-permute-start(bf16[1056,128]{1,0:T(8,128)(2,1)} %get-tuple-element.66), channel_id=1, source_target_pairs={{0,1},{1,0},{2,3},{3,2},{4,5},{5,4},{6,7},{7,6},{8,9},{9,8},{10,11... | collective-permute-start | bytes 811016 | tf_op jit(solution)/shard_map/ppermute | solution.py:369
  7.3 8.5 %collective-permute-start.4 = (bf16[32,1152]{1,0:T(8,128)(2,1)}, bf16[32,1152]{1,0:T(8,128)(2,1)S(1)}, u32[]{:S(2)}, u32[]{:S(2)}) collective-permute-start(bf16[32,1152]{1,0:T(8,128)(2,1)} %get-tuple-element.69), channel_id=1, source_target_pairs={{0,5},{1,4},{2,7},{3,6},{4,1},{5,0},{6,3},{7,2},{8,13},{9,12},{10,... | collective-permute-start | bytes 221192 | tf_op jit(solution)/shard_map/ppermute | solution.py:369
  9.8 10.1 %collective-permute-start.5 = (bf16[32,1152]{1,0:T(8,128)(2,1)}, bf16[32,1152]{1,0:T(8,128)(2,1)S(1)}, u32[]{:S(2)}, u32[]{:S(2)}) collective-permute-start(bf16[32,1152]{1,0:T(8,128)(2,1)} %get-tuple-element.70), channel_id=1, source_target_pairs={{0,6},{1,7},{2,4},{3,5},{4,2},{5,3},{6,0},{7,1},{8,14},{9,15},{10,... | collective-permute-start | bytes 221192 | tf_op jit(solution)/shard_map/ppermute | solution.py:369
  11.2 15.4 %collective-permute-start.1 = (bf16[544,128]{1,0:T(8,128)(2,1)}, bf16[544,128]{1,0:T(8,128)(2,1)S(1)}, u32[]{:S(2)}, u32[]{:S(2)}) collective-permute-start(bf16[544,128]{1,0:T(8,128)(2,1)} %get-tuple-element.67), channel_id=1, source_target_pairs={{0,2},{1,3},{2,0},{3,1},{4,6},{5,7},{6,4},{7,5},{8,10},{9,11},{10,... | collective-permute-start | bytes 417800 | tf_op jit(solution)/shard_map/ppermute | solution.py:369
  11.4 15.1 %collective-permute-start.2 = (bf16[544,128]{1,0:T(8,128)(2,1)}, bf16[544,128]{1,0:T(8,128)(2,1)S(1)}, u32[]{:S(2)}, u32[]{:S(2)}) collective-permute-start(bf16[544,128]{1,0:T(8,128)(2,1)} %get-tuple-element.68), channel_id=1, source_target_pairs={{0,3},{1,2},{2,1},{3,0},{4,7},{5,6},{6,5},{7,4},{8,11},{9,10},{10,... | collective-permute-start | bytes 417800 | tf_op jit(solution)/shard_map/ppermute | solution.py:369
  15.8 8.9 %collective-permute-start.6 = (bf16[32,1152]{1,0:T(8,128)(2,1)}, bf16[32,1152]{1,0:T(8,128)(2,1)S(1)}, u32[]{:S(2)}, u32[]{:S(2)}) collective-permute-start(bf16[32,1152]{1,0:T(8,128)(2,1)} %get-tuple-element.71), channel_id=1, source_target_pairs={{0,7},{1,6},{2,5},{3,4},{4,3},{5,2},{6,1},{7,0},{8,15},{9,14},{10,... | collective-permute-start | bytes 221192 | tf_op jit(solution)/shard_map/ppermute | solution.py:369
  20.0 6.1 %collective-permute-start.3 = (bf16[32,1152]{1,0:T(8,128)(2,1)}, bf16[32,1152]{1,0:T(8,128)(2,1)S(1)}, u32[]{:S(2)}, u32[]{:S(2)}) collective-permute-start(bf16[32,1152]{1,0:T(8,128)(2,1)} %get-tuple-element.65.refs_0_), channel_id=1, source_target_pairs={{0,4},{1,5},{2,6},{3,7},{4,0},{5,1},{6,2},{7,3},{8,12},{9,13},{10,... | collective-permute-start | bytes 221192 | tf_op jit(solution)/shard_map/ppermute | solution.py:369
  24.7 9.2 %collective-permute-start.11 = (bf16[128,512]{1,0:T(8,128)(2,1)}, bf16[128,512]{1,0:T(8,128)(2,1)S(1)}, u32[]{:S(2)}, u32[]{:S(2)}) collective-permute-start(bf16[128,512]{1,0:T(8,128)(2,1)} %get-tuple-element.89.refs_0_), channel_id=1, source_target_pairs={{0,3},{1,2},{2,1},{3,0},{4,7},{5,6},{6,5},{7,4},{8,11},{9,10},{10,... | collective-permute-start | bytes 393224 | tf_op jit(solution)/shard_map/ppermute | solution.py:369
  26.1 7.8 %collective-permute-start.10 = (bf16[128,512]{1,0:T(8,128)(2,1)}, bf16[128,512]{1,0:T(8,128)(2,1)S(1)}, u32[]{:S(2)}, u32[]{:S(2)}) collective-permute-start(bf16[128,512]{1,0:T(8,128)(2,1)} %get-tuple-element.89.refs_0_), channel_id=1, source_target_pairs={{0,2},{1,3},{2,0},{3,1},{4,6},{5,7},{6,4},{7,5},{8,10},{9,11},{10,... | collective-permute-start | bytes 393224 | tf_op jit(solution)/shard_map/ppermute | solution.py:369
  26.6 0.8 copy-start.1
  27.4 0.9 copy-start.6
  28.3 0.6 copy-start.7
  28.9 32.7 %copy-start.2 = (bf16[1,128,256]{2,1,0:T(8,128)(2,1)S(1)}, bf16[1,128,256]{2,1,0:T(8,128)(2,1)}, u32[]{:S(2)}) copy-start(bf16[1,128,256]{2,1,0:T(8,128)(2,1)} %refs_6_.1) | copy-start | bytes 196612
  30.3 4.3 %collective-permute-start.7 = (bf16[128,256]{1,0:T(8,128)(2,1)S(1)}, bf16[128,256]{1,0:T(8,128)(2,1)S(1)}, u32[]{:S(2)}, u32[]{:S(2)}) collective-permute-start(bf16[128,256]{1,0:T(8,128)(2,1)S(1)} %get-tuple-element.76), channel_id=1, source_target_pairs={{0,1},{1,0},{2,3},{3,2},{4,5},{5,4},{6,7},{7,6},{8,9},{9,8},{10,11... | collective-permute-start | bytes 196616 | tf_op jit(solution)/shard_map/ppermute | solution.py:369
  32.0 4.5 %collective-permute-start.8 = (bf16[128,256]{1,0:T(8,128)(2,1)S(1)}, bf16[128,256]{1,0:T(8,128)(2,1)S(1)}, u32[]{:S(2)}, u32[]{:S(2)}) collective-permute-start(bf16[128,256]{1,0:T(8,128)(2,1)S(1)} %get-tuple-element.77), channel_id=1, source_target_pairs={{0,2},{1,3},{2,0},{3,1},{4,6},{5,7},{6,4},{7,5},{8,10},{9,11},{10,... | collective-permute-start | bytes 196616 | tf_op jit(solution)/shard_map/ppermute | solution.py:369
  33.5 5.2 %collective-permute-start.9 = (bf16[128,256]{1,0:T(8,128)(2,1)S(1)}, bf16[128,256]{1,0:T(8,128)(2,1)S(1)}, u32[]{:S(2)}, u32[]{:S(2)}) collective-permute-start(bf16[128,256]{1,0:T(8,128)(2,1)S(1)} %get-tuple-element.78), channel_id=1, source_target_pairs={{0,3},{1,2},{2,1},{3,0},{4,7},{5,6},{6,5},{7,4},{8,11},{9,10},{10,... | collective-permute-start | bytes 196616 | tf_op jit(solution)/shard_map/ppermute | solution.py:369
  38.7 0.9 %copy-start = (f32[128,256]{1,0:T(8,128)S(1)}, f32[128,256]{1,0:T(8,128)}, u32[]{:S(2)}) copy-start(f32[128,256]{1,0:T(8,128)} %get-tuple-element.74.gg) | copy-start | bytes 393220
  39.7 3.8 %collective-permute-start.14 = (f32[2,128]{1,0:T(2,128)S(1)}, f32[2,128]{1,0:T(2,128)S(1)}, u32[]{:S(2)}, u32[]{:S(2)}) collective-permute-start(f32[2,128]{1,0:T(2,128)S(1)} %get-tuple-element.87.refs_0_), channel_id=1, source_target_pairs={{0,24},{8,16},{16,8},{24,0},{1,25},{9,17},{17,9},{25,1},{2,26},{10... | collective-permute-start | bytes 3080 | tf_op jit(solution)/shard_map/ppermute | solution.py:369
  39.8 3.8 %collective-permute-start.13 = (f32[2,128]{1,0:T(2,128)S(1)}, f32[2,128]{1,0:T(2,128)S(1)}, u32[]{:S(2)}, u32[]{:S(2)}) collective-permute-start(f32[2,128]{1,0:T(2,128)S(1)} %get-tuple-element.87.refs_0_), channel_id=1, source_target_pairs={{0,16},{8,24},{16,0},{24,8},{1,17},{9,25},{17,1},{25,9},{2,18},{10... | collective-permute-start | bytes 3080 | tf_op jit(solution)/shard_map/ppermute | solution.py:369
  41.4 2.2 %collective-permute-start.12 = (f32[2,128]{1,0:T(2,128)S(1)}, f32[2,128]{1,0:T(2,128)S(1)}, u32[]{:S(2)}, u32[]{:S(2)}) collective-permute-start(f32[2,128]{1,0:T(2,128)S(1)} %get-tuple-element.87.refs_0_), channel_id=1, source_target_pairs={{0,8},{8,0},{16,24},{24,16},{1,9},{9,1},{17,25},{25,17},{2,10},{10... | collective-permute-start | bytes 3080 | tf_op jit(solution)/shard_map/ppermute | solution.py:369
  41.6 8.0 %collective-permute-start.19 = (bf16[128,256]{1,0:T(8,128)(2,1)S(1)}, bf16[128,256]{1,0:T(8,128)(2,1)S(1)}, u32[]{:S(2)}, u32[]{:S(2)}) collective-permute-start(bf16[128,256]{1,0:T(8,128)(2,1)S(1)} %bitcast.5), channel_id=1, source_target_pairs={{0,4},{1,5},{2,6},{3,7},{4,0},{5,1},{6,2},{7,3},{8,12},{9,13},{10,... | collective-permute-start | bytes 196616 | tf_op jit(solution)/shard_map/ppermute | solution.py:369
  43.7 7.3 %collective-permute-start.18 = (bf16[128,256]{1,0:T(8,128)(2,1)S(1)}, bf16[128,256]{1,0:T(8,128)(2,1)S(1)}, u32[]{:S(2)}, u32[]{:S(2)}) collective-permute-start(bf16[128,256]{1,0:T(8,128)(2,1)S(1)} %shard_map.166.refs_4_), channel_id=1, source_target_pairs={{0,4},{1,5},{2,6},{3,7},{4,0},{5,1},{6,2},{7,3},{8,12},{9,13},{10,... | collective-permute-start | bytes 196616 | tf_op jit(solution)/shard_map/ppermute | solution.py:369
  45.5 9.0 %collective-permute-start.17 = (bf16[128,256]{1,0:T(8,128)(2,1)S(1)}, bf16[128,256]{1,0:T(8,128)(2,1)S(1)}, u32[]{:S(2)}, u32[]{:S(2)}) collective-permute-start(bf16[128,256]{1,0:T(8,128)(2,1)S(1)} %shard_map.166.refs_4_), channel_id=1, source_target_pairs={{0,3},{1,2},{2,1},{3,0},{4,7},{5,6},{6,5},{7,4},{8,11},{9,10},{10,... | collective-permute-start | bytes 196616 | tf_op jit(solution)/shard_map/ppermute | solution.py:369
  51.0 12.4 %collective-permute-start.22 = (bf16[128,512]{1,0:T(8,128)(2,1)S(1)}, bf16[128,512]{1,0:T(8,128)(2,1)S(1)}, u32[]{:S(2)}, u32[]{:S(2)}) collective-permute-start(bf16[128,512]{1,0:T(8,128)(2,1)S(1)} %shard_map.169.refs_4_), channel_id=1, source_target_pairs={{0,3},{1,2},{2,1},{3,0},{4,7},{5,6},{6,5},{7,4},{8,11},{9,10},{10,... | collective-permute-start | bytes 393224 | tf_op jit(solution)/shard_map/ppermute | solution.py:369
  51.1 14.9 %collective-permute-start.21 = (bf16[128,512]{1,0:T(8,128)(2,1)S(1)}, bf16[128,512]{1,0:T(8,128)(2,1)S(1)}, u32[]{:S(2)}, u32[]{:S(2)}) collective-permute-start(bf16[128,512]{1,0:T(8,128)(2,1)S(1)} %shard_map.169.refs_4_), channel_id=1, source_target_pairs={{0,2},{1,3},{2,0},{3,1},{4,6},{5,7},{6,4},{7,5},{8,10},{9,11},{10,... | collective-permute-start | bytes 393224 | tf_op jit(solution)/shard_map/ppermute | solution.py:369
  53.1 12.9 %collective-permute-start.20 = (bf16[128,512]{1,0:T(8,128)(2,1)S(1)}, bf16[128,512]{1,0:T(8,128)(2,1)S(1)}, u32[]{:S(2)}, u32[]{:S(2)}) collective-permute-start(bf16[128,512]{1,0:T(8,128)(2,1)S(1)} %shard_map.169.refs_4_), channel_id=1, source_target_pairs={{0,1},{1,0},{2,3},{3,2},{4,5},{5,4},{6,7},{7,6},{8,9},{9,8},{10,11... | collective-permute-start | bytes 393224 | tf_op jit(solution)/shard_map/ppermute | solution.py:369
  54.6 5.8 %collective-permute-start.16 = (bf16[128,256]{1,0:T(8,128)(2,1)S(1)}, bf16[128,256]{1,0:T(8,128)(2,1)S(1)}, u32[]{:S(2)}, u32[]{:S(2)}) collective-permute-start(bf16[128,256]{1,0:T(8,128)(2,1)S(1)} %shard_map.166.refs_4_), channel_id=1, source_target_pairs={{0,2},{1,3},{2,0},{3,1},{4,6},{5,7},{6,4},{7,5},{8,10},{9,11},{10,... | collective-permute-start | bytes 196616 | tf_op jit(solution)/shard_map/ppermute | solution.py:369
  54.6 7.1 %collective-permute-start.15 = (bf16[128,256]{1,0:T(8,128)(2,1)S(1)}, bf16[128,256]{1,0:T(8,128)(2,1)S(1)}, u32[]{:S(2)}, u32[]{:S(2)}) collective-permute-start(bf16[128,256]{1,0:T(8,128)(2,1)S(1)} %shard_map.166.refs_4_), channel_id=1, source_target_pairs={{0,1},{1,0},{2,3},{3,2},{4,5},{5,4},{6,7},{7,6},{8,9},{9,8},{10,11... | collective-permute-start | bytes 196616 | tf_op jit(solution)/shard_map/ppermute | solution.py:369
  55.2 0.9 %copy-start.4 = (bf16[128,512]{1,0:T(8,128)(2,1)S(1)}, bf16[128,512]{1,0:T(8,128)(2,1)}, u32[]{:S(2)}) copy-start(bf16[128,512]{1,0:T(8,128)(2,1)} %get-tuple-element.89.refs_0_) | copy-start | bytes 393220
  56.1 9.9 %copy-start.5 = (bf16[128,512]{1,0:T(8,128)(2,1)S(1)}, bf16[128,512]{1,0:T(8,128)(2,1)}, u32[]{:S(2)}) copy-start(bf16[128,512]{1,0:T(8,128)(2,1)} %get-tuple-element.89.refs_0_) | copy-start | bytes 393220
  56.1 9.9 %copy-start.8 = (s32[3]{0:T(128)S(1)}, s32[3]{0:T(128)}, u32[]{:S(2)}) copy-start(s32[3]{0:T(128)} %pad_add_fusion.place) | copy-start | bytes 40
  62.5 6.6 %collective-permute-start.23 = (bf16[128,256]{1,0:T(8,128)(2,1)S(1)}, bf16[128,256]{1,0:T(8,128)(2,1)S(1)}, u32[]{:S(2)}, u32[]{:S(2)}) collective-permute-start(bf16[128,256]{1,0:T(8,128)(2,1)S(1)} %get-tuple-element.106), channel_id=1, source_target_pairs={{0,1},{1,0},{2,3},{3,2},{4,5},{5,4},{6,7},{7,6},{8,9},{9,8},{10,11... | collective-permute-start | bytes 196616 | tf_op jit(solution)/shard_map/ppermute | solution.py:369
  63.1 5.9 %collective-permute-start.24 = (bf16[128,256]{1,0:T(8,128)(2,1)S(1)}, bf16[128,256]{1,0:T(8,128)(2,1)S(1)}, u32[]{:S(2)}, u32[]{:S(2)}) collective-permute-start(bf16[128,256]{1,0:T(8,128)(2,1)S(1)} %get-tuple-element.107), channel_id=1, source_target_pairs={{0,2},{1,3},{2,0},{3,1},{4,6},{5,7},{6,4},{7,5},{8,10},{9,11},{10,... | collective-permute-start | bytes 196616 | tf_op jit(solution)/shard_map/ppermute | solution.py:369
  63.4 5.7 %collective-permute-start.25 = (bf16[128,256]{1,0:T(8,128)(2,1)S(1)}, bf16[128,256]{1,0:T(8,128)(2,1)S(1)}, u32[]{:S(2)}, u32[]{:S(2)}) collective-permute-start(bf16[128,256]{1,0:T(8,128)(2,1)S(1)} %get-tuple-element.108), channel_id=1, source_target_pairs={{0,3},{1,2},{2,1},{3,0},{4,7},{5,6},{6,5},{7,4},{8,11},{9,10},{10,... | collective-permute-start | bytes 196616 | tf_op jit(solution)/shard_map/ppermute | solution.py:369
  66.0 21.1 %copy-start.3 = (f32[128,256]{1,0:T(8,128)S(1)}, f32[128,256]{1,0:T(8,128)}, u32[]{:S(2)}) copy-start(f32[128,256]{1,0:T(8,128)} %get-tuple-element.64.rate) | copy-start | bytes 393220
  69.1 18.0 %collective-permute-start.26 = (bf16[672,128]{1,0:T(8,128)(2,1)S(1)}, bf16[672,128]{1,0:T(8,128)(2,1)S(1)}, u32[]{:S(2)}, u32[]{:S(2)}) collective-permute-start(bf16[672,128]{1,0:T(8,128)(2,1)S(1)} %get-tuple-element.115), channel_id=1, source_target_pairs={{0,1},{1,0},{2,3},{3,2},{4,5},{5,4},{6,7},{7,6},{8,9},{9,8},{10,11... | collective-permute-start | bytes 516104 | tf_op jit(solution)/shard_map/ppermute | solution.py:369
  69.9 17.3 %collective-permute-start.27 = (bf16[672,128]{1,0:T(8,128)(2,1)S(1)}, bf16[672,128]{1,0:T(8,128)(2,1)S(1)}, u32[]{:S(2)}, u32[]{:S(2)}) collective-permute-start(bf16[672,128]{1,0:T(8,128)(2,1)S(1)} %get-tuple-element.116), channel_id=1, source_target_pairs={{0,2},{1,3},{2,0},{3,1},{4,6},{5,7},{6,4},{7,5},{8,10},{9,11},{10,... | collective-permute-start | bytes 516104 | tf_op jit(solution)/shard_map/ppermute | solution.py:369
  71.7 15.4 %collective-permute-start.28 = (bf16[672,128]{1,0:T(8,128)(2,1)S(1)}, bf16[672,128]{1,0:T(8,128)(2,1)S(1)}, u32[]{:S(2)}, u32[]{:S(2)}) collective-permute-start(bf16[672,128]{1,0:T(8,128)(2,1)S(1)} %get-tuple-element.117), channel_id=1, source_target_pairs={{0,3},{1,2},{2,1},{3,0},{4,7},{5,6},{6,5},{7,4},{8,11},{9,10},{10,... | collective-permute-start | bytes 516104 | tf_op jit(solution)/shard_map/ppermute | solution.py:369
  72.6 6.4 %collective-permute-start.29 = (bf16[32,576]{1,0:T(8,128)(2,1)S(1)}, bf16[32,576]{1,0:T(8,128)(2,1)S(1)}, u32[]{:S(2)}, u32[]{:S(2)}) collective-permute-start(bf16[32,576]{1,0:T(8,128)(2,1)S(1)} %get-tuple-element.118), channel_id=1, source_target_pairs={{0,4},{1,5},{2,6},{3,7},{4,0},{5,1},{6,2},{7,3},{8,12},{9,13},{10,... | collective-permute-start | bytes 110600 | tf_op jit(solution)/shard_map/ppermute | solution.py:369
  73.9 6.5 %collective-permute-start.30 = (bf16[32,576]{1,0:T(8,128)(2,1)S(1)}, bf16[32,576]{1,0:T(8,128)(2,1)S(1)}, u32[]{:S(2)}, u32[]{:S(2)}) collective-permute-start(bf16[32,576]{1,0:T(8,128)(2,1)S(1)} %get-tuple-element.119), channel_id=1, source_target_pairs={{0,5},{1,4},{2,7},{3,6},{4,1},{5,0},{6,3},{7,2},{8,13},{9,12},{10,... | collective-permute-start | bytes 110600 | tf_op jit(solution)/shard_map/ppermute | solution.py:369
  79.1 5.8 %collective-permute-start.31 = (bf16[32,576]{1,0:T(8,128)(2,1)S(1)}, bf16[32,576]{1,0:T(8,128)(2,1)S(1)}, u32[]{:S(2)}, u32[]{:S(2)}) collective-permute-start(bf16[32,576]{1,0:T(8,128)(2,1)S(1)} %get-tuple-element.120), channel_id=1, source_target_pairs={{0,6},{1,7},{2,4},{3,5},{4,2},{5,3},{6,0},{7,1},{8,14},{9,15},{10,... | collective-permute-start | bytes 110600 | tf_op jit(solution)/shard_map/ppermute | solution.py:369
  80.4 6.7 %collective-permute-start.32 = (bf16[32,576]{1,0:T(8,128)(2,1)S(1)}, bf16[32,576]{1,0:T(8,128)(2,1)S(1)}, u32[]{:S(2)}, u32[]{:S(2)}) collective-permute-start(bf16[32,576]{1,0:T(8,128)(2,1)S(1)} %get-tuple-element.121), channel_id=1, source_target_pairs={{0,7},{1,6},{2,5},{3,4},{4,3},{5,2},{6,1},{7,0},{8,15},{9,14},{10,... | collective-permute-start | bytes 110600 | tf_op jit(solution)/shard_map/ppermute | solution.py:369

commit v7 on v5

--- a/solution.py
+++ b/solution.py
@@ -11,6 +11,7 @@
 EPS_ROOT = 1e-05
 BF = jnp.bfloat16
 F32 = jnp.float32
+LANES = 128
 VMEM = pl.BlockSpec(memory_space=pltpu.VMEM)
 SMEM = pl.BlockSpec(memory_space=pltpu.SMEM)
 
@@ -79,6 +80,36 @@
         copy.wait()
 
 
+def padded(rows):
+    return -(-rows // 16) * 16
+
+
+def tiles(cols):
+    return -(-cols // LANES)
+
+
+def put(out, at, value):
+    rows, cols = value.shape
+    for t in range(tiles(cols)):
+        wide = min(LANES, cols - t * LANES)
+        out[at : at + rows, 0:wide] = value[:, t * LANES : t * LANES + wide]
+        at += padded(rows)
+    return at
+
+
+def get(ref, at, rows, cols):
+    parts = []
+    for t in range(tiles(cols)):
+        wide = min(LANES, cols - t * LANES)
+        parts.append(ref[at : at + rows, 0:wide])
+        at += padded(rows)
+    return jnp.concatenate(parts, axis=1), at
+
+
+def message(*blocks):
+    return arr((sum(tiles(cols) * padded(rows) for rows, cols in blocks), LANES), BF)
+
+
 def token_pack_kernel(q, k, v, og, rates, gains, all_out, kv_out, gg_out, rate_out):
     tokens, feat = gg_out.shape
     rate = jnp.broadcast_to(rates[...], (feat, tokens)).T
@@ -168,13 +199,11 @@
 
 
 def near_kernel(slab, group, normed_ref, *refs):
-    q_near, od_near, outs, grads_out = refs[:group], refs[group : 2 * group], refs[2 * group : -1], refs[-1]
-    own, feat = od_near[0].shape
+    q_near, od_near, (grad_q, grads_out) = refs[:group], refs[group : 2 * group], refs[2 * group :]
+    feat = od_near[0].shape[1]
     normed = thirds(normed_ref, slab)
     delta_gate, delta_up, grads = query_side(stack(q_near, slice(0, feat)), stack(od_near), normed)
-    grad_q = (mm_nt(delta_gate, normed[0]) + mm_nt(delta_up, normed[1])).astype(BF)
-    for d in range(group):
-        outs[d][...] = grad_q[d * own : (d + 1) * own]
+    grad_q[...] = (mm_nt(delta_gate, normed[0]) + mm_nt(delta_up, normed[1])).astype(BF)
     for i in range(3):
         grads_out[i] = grads[i]
 
@@ -198,31 +227,28 @@
     factors[3] = k_proj * k_up * k_bend
 
 
-def backward_kernel(slab, group, tok_groups, place, w, normed_ref, grads, factors, rises, *refs):
+def backward_kernel(slab, group, tok_groups, place, w, normed_ref, grad_q, grads, factors, rises, *refs):
     far = group * (tok_groups - 1)
-    kvs, pairs, outs, refs = refs[:group], refs[group : group + far], refs[group + far : -4], refs[-4:]
-    inner_out, far_od, far_q, sums = refs
+    kvs, pairs, outs, (inner_buf, sums) = refs[:group], refs[group : group + far], refs[group + far : -2], refs[-2:]
     feat = w.shape[0]
-    own = outs[0].shape[0]
-    for i in range(far):
-        far_od[i // group, i % group] = pairs[i][:, 0:feat]
-        far_q[i // group, i % group] = pairs[i][:, feat : 2 * feat]
+    tok_out, outs = outs[0], outs[1:]
+    own = tok_out.shape[0]
     normed = thirds(normed_ref, slab)
-    sums[...] = grads[...]
-
-    def other(e, carry):
-        more = query_side(flat(far_q[e]), flat(far_od[e]), normed)[2]
-        for i in range(3):
-            sums[i] += more[i]
-        return carry
-
-    lax.fori_loop(0, tok_groups - 1, other, 0)
+    total = [grads[i] for i in range(3)]
+    for e in range(tok_groups - 1):
+        these = pairs[e * group : (e + 1) * group]
+        more = query_side(stack(these, slice(feat, 2 * feat)), stack(these, slice(0, feat)), normed)[2]
+        total = [total[i] + more[i] for i in range(3)]
+        if tok_groups > 2:
+            for i in range(3):
+                sums[i] = total[i]
+            total = [sums[i] for i in range(3)]
 
     saved, init, norm_init, norm_saved = columns(w, slab)
     cots, direct = [], []
     once = jnp.where(place[0] == 0, 1.0, 0.0)
     for i in range(3):
-        apply_grad = sums[i]
+        apply_grad = total[i]
         col_dot = jnp.sum(saved[i] * apply_grad, axis=0, keepdims=True)
         cot = apply_grad * (norm_init[i] / norm_saved[i]) - saved[i] * (
             col_dot * norm_init[i] / (norm_saved[i] * norm_saved[i] * norm_saved[i])
@@ -246,11 +272,24 @@
         + mm_nt(back_kup, init_bf[1])
     ).astype(BF)
     grad_v = (mm_nt(rises[0], cots[2]) + mm_nt(back_proj, init_bf[2])).astype(BF)
-    for d in range(group):
-        outs[d][:, 0:feat] = grad_k[d * own : (d + 1) * own]
-        outs[d][:, feat : 2 * feat] = grad_v[d * own : (d + 1) * own]
     inner = (mm_tn(keys, back_kgate), mm_tn(keys, back_kup), mm_tn(values, back_proj))
-    inner_out[...] = jnp.concatenate([inner[i] + direct[i] for i in range(3)], axis=1).astype(BF)
+    whole = jnp.concatenate([inner[i] + direct[i] for i in range(3)], axis=1)
+    rows = inner_buf.shape[1]
+    for p in range(inner_buf.shape[0]):
+        inner_buf[p] = whole[p * rows : (p + 1) * rows]
+    tok_out[:, 0:feat] = grad_q[0:own, :]
+    tok_out[:, feat : 2 * feat] = grad_k[0:own]
+    tok_out[:, 2 * feat : 3 * feat] = grad_v[0:own]
+    for d in range(inner_buf.shape[0]):
+        block = inner_buf[place[2] ^ d].astype(BF)
+        if 0 < d < group:
+            out = outs[d]
+            at = 0
+            for tok in (grad_q, grad_k, grad_v):
+                at = put(out, at, tok[d * own : (d + 1) * own, :])
+            put(out, at, block)
+        else:
+            outs[d][...] = block
 
 
 def total_of(refs):
@@ -260,22 +299,29 @@
     return total
 
 
-def tokens_kernel(group, rate, *refs):
-    queries, got, (gq, gk, gv) = refs[:group], refs[group:-3], refs[-3:]
-    feat = gq.shape[2]
-    gq[0] = total_of(queries).astype(BF)
-    total = total_of(got)
-    gk[0] = total[:, 0:feat].astype(BF)
-    gv[0] = (rate[...] * total[:, feat : 2 * feat]).astype(BF)
-
-
-def weights_kernel(group, slab, got, *outs):
-    cols = []
-    for j in range(group):
-        total = got[j].astype(F32)
-        for p in range(j + group, got.shape[0], group):
-            total += got[p].astype(F32)
-        cols.append(total)
+def final_kernel(group, order, slab, place, rate, tok, *refs):
+    given, (gq, gk, gv, *outs, buf) = refs[:-7], refs[-7:]
+    blocks = dict(zip(order, given))
+    _, own, feat = gq.shape
+    rows = buf.shape[1]
+    sums = [tok[:, i * feat : (i + 1) * feat].astype(F32) for i in range(3)]
+    for d in range(group):
+        block = blocks[d]
+        at = 0
+        if d:
+            for i in range(3):
+                more, at = get(block, at, own, feat)
+                sums[i] += more.astype(F32)
+            value = get(block, at, rows, 3 * slab)[0]
+        else:
+            value = block[...]
+        buf[d] = value.astype(F32)
+        for other in range(d + group, len(order), group):
+            buf[d] += blocks[other][...].astype(F32)
+    gq[0] = sums[0].astype(BF)
+    gk[0] = sums[1].astype(BF)
+    gv[0] = (rate[...] * sums[2]).astype(BF)
+    cols = [buf[place[1] ^ j] for j in range(group)]
     for i in range(3):
         outs[i][0] = jnp.concatenate([c[:, i * slab : (i + 1) * slab] for c in cols], axis=1)
 
@@ -328,7 +374,7 @@
             24,
             flops=3 * mflop,
         )
-        parts = [parts[0]] + [move(parts[d], d) for d in range(1, group)]
+        parts = [parts[0]] + [move(parts[d], d) for d in (*range(2, group), *range(1, min(2, group)))]
         *parts, kv_near = lax.optimization_barrier((*parts, kv_near))
         apply_out, sums = call(
             reduce_kernel, (arr((own, feat), F32), arr((2, own), F32)), (gg, *parts), 16
@@ -350,34 +396,46 @@
             call(pair_kernel, (arr((own, 2 * feat), BF),), pair, 16)[0] for pair in zip(od_mirror, q_mirror)
         ]
         pairs = [x for m in pairs for x in near_all(m)]
-        *grad_q, grads = call(
+        grad_q, grads = call(
             functools.partial(near_kernel, slab, group),
-            (*(block,) * group, arr((3, seq_n * rows, slab), F32)),
+            (arr((near, feat), BF), arr((3, seq_n * rows, slab), F32)),
             (normed, *q_near, *od_near),
             24,
             flops=12 * mflop,
         )
-        grad_q = [grad_q[0]] + [move(grad_q[d], d) for d in range(1, group)]
-
-        far = pltpu.VMEM((max(tok_groups - 1, 1), group, own, feat), BF)
-        *tok, inner = call(
+
+        q_block = (own, feat)
+        tok, *sends = call(
             functools.partial(backward_kernel, slab, group, tok_groups),
-            (*(arr((own, 2 * feat), BF),) * group, arr((seq_n * rows, 3 * slab), BF)),
-            (place, wall, normed, grads, factors, rises, *kv_near, *pairs),
-            32,
+            (
+                arr((own, 3 * feat), BF),
+                *[
+                    message(*(q_block,) * 3, (rows, 3 * slab)) if 0 < d < group else arr((rows, 3 * slab), BF)
+                    for d in range(seq_n)
+                ],
+            ),
+            (place, wall, normed, grad_q, grads, factors, rises, *kv_near, *pairs),
+            40,
             smem=1,
             flops=24 * mflop,
-            scratch=[far, far, pltpu.VMEM((3, seq_n * rows, slab), F32)],
-        )
-        inner = lax.all_to_all(inner.reshape(seq_n, rows, 3 * slab), "seq", 0, 0, tiled=True)
-        tok = [tok[0]] + [move(tok[d], d) for d in range(1, group)]
+            scratch=[
+                pltpu.VMEM((seq_n, rows, 3 * slab), F32),
+                pltpu.VMEM((3, seq_n * rows, slab), F32),
+            ],
+        )
+        far = list(range(group, seq_n))
+        order = [0, *far[:2], *range(2, group), *range(1, min(2, group)), *far[2:]]
+        got = [move(sends[d], d) if d else sends[d] for d in order]
         out_tok = arr((1, own, feat), BF)
         grad_w = arr((1, rows, hidden), F32)
-        grads_t = call(
-            functools.partial(tokens_kernel, group), (out_tok,) * 3, (rate, *grad_q, *tok), 16
-        )
-        grads_w = call(functools.partial(weights_kernel, group, slab), (grad_w,) * 3, (inner,), 16)
-        return (*grads_t, *grads_w)
+        return call(
+            functools.partial(final_kernel, group, order, slab),
+            (*(out_tok,) * 3, *(grad_w,) * 3),
+            (place, rate, tok, *got),
+            16,
+            smem=1,
+            scratch=[pltpu.VMEM((group, rows, 3 * slab), F32)],
+        )
 
     return local
 

time: 81.9 us -> 80.3 us (0.980)
  starting transfers between devices: 42.9 us -> 41 us
  waiting for transfers between devices: 26.5 us -> 27.7 us
  Pallas kernels: 9.92 us -> 9.07 us
    all_to_all x1 -> x0, starting transfers between devices: 4.59 us -> none  [local(): lax.all_to_all(inner.reshape(seq_n, rows, 3 * slab), 'seq', 0, 0, tiled=T...]
    ppermute x25 -> x26, starting transfers between devices: 31 us -> 33.8 us  [move(): return lax.ppermute(x, axis, [(i, i ^ dist) for i in range(size)])]
    ppermute x25 -> x26, waiting for transfers between devices: 26.5 us -> 27.7 us  [move(): return lax.ppermute(x, axis, [(i, i ^ dist) for i in range(size)])]
    pallas_call x10 -> x9, Pallas kernels: 7.95 us -> 7.11 us  [call(): pl.pallas_call(kernel, out_shape=outs, in_specs=[SMEM] * smem + [VMEM] *...]
  transfers between devices with their start and end apart: 27 -> 27, of which waited for: 14 -> 15; matrix products, arithmetic and copies ran while one was open for 0% -> 0% of each run, Pallas kernels for 4% -> 3%
where the time goes in v7:
time: 80.3 us; the launch traced here: 80.1 us
  starting transfers between devices  41 us (51%)
  waiting for transfers between devices  27.7 us (34%)
  Pallas kernels  9.07 us (11%)
  local copies, waits for them, and re-layouts  1.35 us (2%)
  between operations  0.83 us (1%)
    ppermute x26, starting transfers between devices, move(): return lax.ppermute(x, axis, [(i, i ^ dist) for i in range(size)])  33.8 us
    ppermute x26, waiting for transfers between devices, move(): return lax.ppermute(x, axis, [(i, i ^ dist) for i in range(size)])  27.7 us
    all_to_all x1, starting transfers between devices, local(): lax.all_to_all(packed, 'seq', 0, 0, tiled=True)  7.26 us
    pallas_call x9, Pallas kernels, call(): pl.pallas_call(kernel, out_shape=outs, in_specs=[SMEM] * smem + [VMEM] *...  7.11 us
    pallas_call x1, Pallas kernels, copying_call(): pl.pallas_call(kernel, out_shape=outs, in_specs=[pl.BlockSpec(memory_spac...  1.96 us
  transfers between devices with their start and end apart: 27, of which 15 were waited for; matrix products, arithmetic and copies ran while one was open for 0% of the time, Pallas kernels for 3%

profile of v7, /device:TPU:0, one launch (start us, length us, event | category | flops | bytes accessed | tf_op | source)
XLA Modules:
  0.0 80.1 jit_solution(3409694450191054035)
XLA Ops:
  0.7 2.0 %shard_map.164 = bf16[8,32,1152]{2,1,0:T(8,128)(2,1)} custom-call(bf16[1,32,768]{2,1,0:T(8,128)(2,1)} %refs_0_.1, bf16[1,32,768]{2,1,0:T(8,128)(2,1)} %refs_1_.1, bf16[1,32,768]{2,1,0:T(8,128)(2,1)} %refs_2_.1, bf16[1,32,768]{2,1,0:T(8,128)(2,1)} %refs_3_.1, bf16[1,32,768]{2,1,0:T(8,128)(2,1)} %refs_4_.1, bf16[1,32,768]{2,1,0:T(8,128)(2,1)} %refs_5_.1), custom_call_target="tpu_custom_call" | custom-call | tf_op jit(solution)/shard_map/pallas_call | solution.py:61
  2.6 7.3 %all-to-all-start = ((bf16[8,32,1152]{2,1,0:T(8,128)(2,1)}), bf16[8,32,1152]{2,1,0:T(8,128)(2,1)S(1)}, u32[]{:S(2)}, u32[]{:S(2)}) async-start(bf16[8,32,1152]{2,1,0:T(8,128)(2,1)} %shard_map.164), calls=%async_computation | async-start | bytes 1179648 | tf_op jit(solution)/shard_map/all_to_all | solution.py:356
  9.9 0.0 copy-start.4
  10.0 0.7 copy-done.4
  10.6 0.7 copy-done.5
  11.3 0.1 shard_map.163
  11.4 2.1 %collective-permute-start = (bf16[128,768]{1,0:T(8,128)(2,1)S(1)}, bf16[128,768]{1,0:T(8,128)(2,1)S(1)}, u32[]{:S(2)}, u32[]{:S(2)}) collective-permute-start(bf16[128,768]{1,0:T(8,128)(2,1)S(1)} %get-tuple-element.45), channel_id=1, source_target_pairs={{0,1},{1,0},{2,3},{3,2},{4,5},{5,4},{6,7},{7,6},{8,9},{9,8},{10,11... | collective-permute-start | bytes 589832 | tf_op jit(solution)/shard_map/ppermute | solution.py:333
  13.5 1.5 %collective-permute-start.2 = (bf16[128,256]{1,0:T(8,128)(2,1)S(1)}, bf16[128,256]{1,0:T(8,128)(2,1)S(1)}, u32[]{:S(2)}, u32[]{:S(2)}) collective-permute-start(bf16[128,256]{1,0:T(8,128)(2,1)S(1)} %bitcast.8), channel_id=1, source_target_pairs={{0,3},{1,2},{2,1},{3,0},{4,7},{5,6},{6,5},{7,4},{8,11},{9,10},{10,... | collective-permute-start | bytes 196616 | tf_op jit(solution)/shard_map/ppermute | solution.py:333
  14.9 0.1 collective-permute-start.1
  15.0 2.8 %collective-permute-start.7 = (bf16[128,512]{1,0:T(8,128)(2,1)S(1)}, bf16[128,512]{1,0:T(8,128)(2,1)S(1)}, u32[]{:S(2)}, u32[]{:S(2)}) collective-permute-start(bf16[128,512]{1,0:T(8,128)(2,1)S(1)} %get-tuple-element.62.refs_0_), channel_id=1, source_target_pairs={{0,3},{1,2},{2,1},{3,0},{4,7},{5,6},{6,5},{7,4},{8,11},{9,10},{10,... | collective-permute-start | bytes 393224 | tf_op jit(solution)/shard_map/ppermute | solution.py:333
  17.9 0.6 collective-permute-start.6
  18.4 4.8 %collective-permute-done.2.refs_3_ = bf16[128,256]{1,0:T(8,128)(2,1)S(1)} collective-permute-done((bf16[128,256]{1,0:T(8,128)(2,1)S(1)}, bf16[128,256]{1,0:T(8,128)(2,1)S(1)}, u32[]{:S(2)}, u32[]{:S(2)}) %collective-permute-start.2) | collective-permute-done | bytes 65568 | tf_op jit(solution)/shard_map/ppermute | solution.py:333
  23.3 0.4 collective-permute-done.1.refs_2_
  23.6 2.3 %collective-permute-done.refs_1_ = bf16[128,768]{1,0:T(8,128)(2,1)S(1)} collective-permute-done((bf16[128,768]{1,0:T(8,128)(2,1)S(1)}, bf16[128,768]{1,0:T(8,128)(2,1)S(1)}, u32[]{:S(2)}, u32[]{:S(2)}) %collective-permute-start) | collective-permute-done | bytes 196640 | tf_op jit(solution)/shard_map/ppermute | solution.py:333
  25.9 0.0 all-to-all-done
  25.9 0.8 shard_map.165
  26.7 1.8 %collective-permute-start.3 = (bf16[128,256]{1,0:T(8,128)(2,1)S(1)}, bf16[128,256]{1,0:T(8,128)(2,1)S(1)}, u32[]{:S(2)}, u32[]{:S(2)}) collective-permute-start(bf16[128,256]{1,0:T(8,128)(2,1)S(1)} %get-tuple-element.49), channel_id=1, source_target_pairs={{0,2},{1,3},{2,0},{3,1},{4,6},{5,7},{6,4},{7,5},{8,10},{9,11},{10,... | collective-permute-start | bytes 196616 | tf_op jit(solution)/shard_map/ppermute | solution.py:333
  28.5 1.1 %collective-permute-start.4 = (bf16[128,256]{1,0:T(8,128)(2,1)S(1)}, bf16[128,256]{1,0:T(8,128)(2,1)S(1)}, u32[]{:S(2)}, u32[]{:S(2)}) collective-permute-start(bf16[128,256]{1,0:T(8,128)(2,1)S(1)} %get-tuple-element.50), channel_id=1, source_target_pairs={{0,3},{1,2},{2,1},{3,0},{4,7},{5,6},{6,5},{7,4},{8,11},{9,10},{10,... | collective-permute-start | bytes 196616 | tf_op jit(solution)/shard_map/ppermute | solution.py:333
  29.7 0.6 collective-permute-start.5
  30.2 0.0 collective-permute-done.7.refs_3_
  30.3 0.5 collective-permute-done.6.refs_2_
  30.7 1.4 %collective-permute-done.3.refs_1_ = bf16[128,256]{1,0:T(8,128)(2,1)S(1)} collective-permute-done((bf16[128,256]{1,0:T(8,128)(2,1)S(1)}, bf16[128,256]{1,0:T(8,128)(2,1)S(1)}, u32[]{:S(2)}, u32[]{:S(2)}) %collective-permute-start.3) | collective-permute-done | bytes 65568 | tf_op jit(solution)/shard_map/ppermute | solution.py:333
  32.1 1.9 %collective-permute-done.4.refs_2_ = bf16[128,256]{1,0:T(8,128)(2,1)S(1)} collective-permute-done((bf16[128,256]{1,0:T(8,128)(2,1)S(1)}, bf16[128,256]{1,0:T(8,128)(2,1)S(1)}, u32[]{:S(2)}, u32[]{:S(2)}) %collective-permute-start.4) | collective-permute-done | bytes 65568 | tf_op jit(solution)/shard_map/ppermute | solution.py:333
  34.0 0.6 collective-permute-done.5.refs_3_
  34.6 0.1 shard_map.166
  34.8 0.1 collective-permute-start.10
  34.9 1.6 %collective-permute-start.9 = (f32[2,128]{1,0:T(2,128)S(1)}, f32[2,128]{1,0:T(2,128)S(1)}, u32[]{:S(2)}, u32[]{:S(2)}) collective-permute-start(f32[2,128]{1,0:T(2,128)S(1)} %get-tuple-element.59.refs_0_), channel_id=1, source_target_pairs={{0,16},{8,24},{16,0},{24,8},{1,17},{9,25},{17,1},{25,9},{2,18},{10... | collective-permute-start | bytes 3080 | tf_op jit(solution)/shard_map/ppermute | solution.py:333
  36.4 0.3 collective-permute-start.8
  36.7 2.4 %collective-permute-start.15 = (bf16[128,256]{1,0:T(8,128)(2,1)S(1)}, bf16[128,256]{1,0:T(8,128)(2,1)S(1)}, u32[]{:S(2)}, u32[]{:S(2)}) collective-permute-start(bf16[128,256]{1,0:T(8,128)(2,1)S(1)} %bitcast.11), channel_id=1, source_target_pairs={{0,4},{1,5},{2,6},{3,7},{4,0},{5,1},{6,2},{7,3},{8,12},{9,13},{10,... | collective-permute-start | bytes 196616 | tf_op jit(solution)/shard_map/ppermute | solution.py:333
  39.1 0.0 collective-permute-done.10.refs_3_
  39.1 0.0 collective-permute-done.9.refs_2_
  39.1 0.0 collective-permute-done.8.refs_1_
  39.1 0.1 shard_map.167.refs_4_
  39.3 1.8 %collective-permute-start.14 = (bf16[128,256]{1,0:T(8,128)(2,1)S(1)}, bf16[128,256]{1,0:T(8,128)(2,1)S(1)}, u32[]{:S(2)}, u32[]{:S(2)}) collective-permute-start(bf16[128,256]{1,0:T(8,128)(2,1)S(1)} %shard_map.167.refs_4_), channel_id=1, source_target_pairs={{0,4},{1,5},{2,6},{3,7},{4,0},{5,1},{6,2},{7,3},{8,12},{9,13},{10,... | collective-permute-start | bytes 196616 | tf_op jit(solution)/shard_map/ppermute | solution.py:333
  41.1 1.1 %collective-permute-start.13 = (bf16[128,256]{1,0:T(8,128)(2,1)S(1)}, bf16[128,256]{1,0:T(8,128)(2,1)S(1)}, u32[]{:S(2)}, u32[]{:S(2)}) collective-permute-start(bf16[128,256]{1,0:T(8,128)(2,1)S(1)} %shard_map.167.refs_4_), channel_id=1, source_target_pairs={{0,3},{1,2},{2,1},{3,0},{4,7},{5,6},{6,5},{7,4},{8,11},{9,10},{10,... | collective-permute-start | bytes 196616 | tf_op jit(solution)/shard_map/ppermute | solution.py:333
  42.2 0.9 %collective-permute-start.12 = (bf16[128,256]{1,0:T(8,128)(2,1)S(1)}, bf16[128,256]{1,0:T(8,128)(2,1)S(1)}, u32[]{:S(2)}, u32[]{:S(2)}) collective-permute-start(bf16[128,256]{1,0:T(8,128)(2,1)S(1)} %shard_map.167.refs_4_), channel_id=1, source_target_pairs={{0,2},{1,3},{2,0},{3,1},{4,6},{5,7},{6,4},{7,5},{8,10},{9,11},{10,... | collective-permute-start | bytes 196616 | tf_op jit(solution)/shard_map/ppermute | solution.py:333
  43.1 1.5 %collective-permute-start.11 = (bf16[128,256]{1,0:T(8,128)(2,1)S(1)}, bf16[128,256]{1,0:T(8,128)(2,1)S(1)}, u32[]{:S(2)}, u32[]{:S(2)}) collective-permute-start(bf16[128,256]{1,0:T(8,128)(2,1)S(1)} %shard_map.167.refs_4_), channel_id=1, source_target_pairs={{0,1},{1,0},{2,3},{3,2},{4,5},{5,4},{6,7},{7,6},{8,9},{9,8},{10,11... | collective-permute-start | bytes 196616 | tf_op jit(solution)/shard_map/ppermute | solution.py:333
  44.6 0.4 collective-permute-done.15.right
  45.0 1.1 %collective-permute-done.14.left = bf16[128,256]{1,0:T(8,128)(2,1)S(1)} collective-permute-done((bf16[128,256]{1,0:T(8,128)(2,1)S(1)}, bf16[128,256]{1,0:T(8,128)(2,1)S(1)}, u32[]{:S(2)}, u32[]{:S(2)}) %collective-permute-start.14) | collective-permute-done | bytes 65568 | tf_op jit(solution)/shard_map/ppermute | solution.py:333
  46.1 0.2 collective-permute-start.18
  46.3 1.8 %collective-permute-start.17 = (bf16[128,512]{1,0:T(8,128)(2,1)S(1)}, bf16[128,512]{1,0:T(8,128)(2,1)S(1)}, u32[]{:S(2)}, u32[]{:S(2)}) collective-permute-start(bf16[128,512]{1,0:T(8,128)(2,1)S(1)} %shard_map.170.refs_4_), channel_id=1, source_target_pairs={{0,2},{1,3},{2,0},{3,1},{4,6},{5,7},{6,4},{7,5},{8,10},{9,11},{10,... | collective-permute-start | bytes 393224 | tf_op jit(solution)/shard_map/ppermute | solution.py:333
  48.1 0.0 collective-permute-done.13.refs_7_
  48.1 1.5 %collective-permute-start.16 = (bf16[128,512]{1,0:T(8,128)(2,1)S(1)}, bf16[128,512]{1,0:T(8,128)(2,1)S(1)}, u32[]{:S(2)}, u32[]{:S(2)}) collective-permute-start(bf16[128,512]{1,0:T(8,128)(2,1)S(1)} %shard_map.170.refs_4_), channel_id=1, source_target_pairs={{0,1},{1,0},{2,3},{3,2},{4,5},{5,4},{6,7},{7,6},{8,9},{9,8},{10,11... | collective-permute-start | bytes 393224 | tf_op jit(solution)/shard_map/ppermute | solution.py:333
  49.6 0.1 pad_add_fusion.place
  49.7 0.7 shard_map.169
  50.5 0.0 collective-permute-done.12.refs_6_
  50.5 0.0 collective-permute-done.11.refs_5_
  50.5 0.8 %shard_map.168 = (bf16[512,256]{1,0:T(8,128)(2,1)S(1)}, f32[3,256,192]{2,1,0:T(8,128)S(1)}) custom-call(bf16[256,576]{1,0:T(8,128)(2,1)S(1)} %get-tuple-element.46.normed_ref, bf16[128,256]{1,0:T(8,128)(2,1)S(1)} %bitcast.12, bf16[128,768]{1,0:T(8,128)(2,1)S(1)} %collective-permute-done.refs_1_, bf16[128,256]{1,0:T(8,128)(2,1)S(1)} %collective-permute-done.1.refs_2_, ...), custom_call_target="tpu_custom_call" | custom-call | flops 603979776 | bytes 1802240 | tf_op jit(solution)/shard_map/pallas_call | solution.py:49
  51.3 2.1 %collective-permute-done.18.refs_7_ = bf16[128,512]{1,0:T(8,128)(2,1)S(1)} collective-permute-done((bf16[128,512]{1,0:T(8,128)(2,1)S(1)}, bf16[128,512]{1,0:T(8,128)(2,1)S(1)}, u32[]{:S(2)}, u32[]{:S(2)}) %collective-permute-start.18) | collective-permute-done | bytes 131104 | tf_op jit(solution)/shard_map/ppermute | solution.py:333
  53.4 0.6 collective-permute-done.17.refs_6_
  54.0 1.1 %collective-permute-done.16.refs_5_ = bf16[128,512]{1,0:T(8,128)(2,1)S(1)} collective-permute-done((bf16[128,512]{1,0:T(8,128)(2,1)S(1)}, bf16[128,512]{1,0:T(8,128)(2,1)S(1)}, u32[]{:S(2)}, u32[]{:S(2)}) %collective-permute-start.16) | collective-permute-done | bytes 131104 | tf_op jit(solution)/shard_map/ppermute | solution.py:333
  55.1 2.9 %shard_map.171 = (bf16[128,768]{1,0:T(8,128)(2,1)S(1)}, bf16[32,576]{1,0:T(8,128)(2,1)S(1)}, bf16[928,128]{1,0:T(8,128)(2,1)S(1)}, bf16[928,128]{1,0:T(8,128)(2,...) custom-call(s32[3]{0:T(128)S(1)} %pad_add_fusion.place, ...), custom_call_target="tpu_custom_call" | custom-call | flops 1207959552 | bytes 6107148 | tf_op jit(solution)/shard_map/pallas_call | solution.py:49
  58.0 0.1 collective-permute-start.21
  58.1 2.0 %collective-permute-start.22 = (bf16[928,128]{1,0:T(8,128)(2,1)S(1)}, bf16[928,128]{1,0:T(8,128)(2,1)S(1)}, u32[]{:S(2)}, u32[]{:S(2)}) collective-permute-start(bf16[928,128]{1,0:T(8,128)(2,1)S(1)} %get-tuple-element.74), channel_id=1, source_target_pairs={{0,3},{1,2},{2,1},{3,0},{4,7},{5,6},{6,5},{7,4},{8,11},{9,10},{10,... | collective-permute-start | bytes 712712 | tf_op jit(solution)/shard_map/ppermute | solution.py:333
  60.1 1.5 %collective-permute-start.23 = (bf16[928,128]{1,0:T(8,128)(2,1)S(1)}, bf16[928,128]{1,0:T(8,128)(2,1)S(1)}, u32[]{:S(2)}, u32[]{:S(2)}) collective-permute-start(bf16[928,128]{1,0:T(8,128)(2,1)S(1)} %get-tuple-element.75), channel_id=1, source_target_pairs={{0,1},{1,0},{2,3},{3,2},{4,5},{5,4},{6,7},{7,6},{8,9},{9,8},{10,11... | collective-permute-start | bytes 712712 | tf_op jit(solution)/shard_map/ppermute | solution.py:333
  61.6 1.0 %collective-permute-start.19 = (bf16[32,576]{1,0:T(8,128)(2,1)S(1)}, bf16[32,576]{1,0:T(8,128)(2,1)S(1)}, u32[]{:S(2)}, u32[]{:S(2)}) collective-permute-start(bf16[32,576]{1,0:T(8,128)(2,1)S(1)} %get-tuple-element.71), channel_id=1, source_target_pairs={{0,4},{1,5},{2,6},{3,7},{4,0},{5,1},{6,2},{7,3},{8,12},{9,13},{10,... | collective-permute-start | bytes 110600 | tf_op jit(solution)/shard_map/ppermute | solution.py:333
  62.6 1.9 %collective-permute-start.20 = (bf16[32,576]{1,0:T(8,128)(2,1)S(1)}, bf16[32,576]{1,0:T(8,128)(2,1)S(1)}, u32[]{:S(2)}, u32[]{:S(2)}) collective-permute-start(bf16[32,576]{1,0:T(8,128)(2,1)S(1)} %get-tuple-element.72), channel_id=1, source_target_pairs={{0,5},{1,4},{2,7},{3,6},{4,1},{5,0},{6,3},{7,2},{8,13},{9,12},{10,... | collective-permute-start | bytes 110600 | tf_op jit(solution)/shard_map/ppermute | solution.py:333
  64.5 5.3 %collective-permute-done.19.refs_1_ = bf16[32,576]{1,0:T(8,128)(2,1)S(1)} collective-permute-done((bf16[32,576]{1,0:T(8,128)(2,1)S(1)}, bf16[32,576]{1,0:T(8,128)(2,1)S(1)}, u32[]{:S(2)}, u32[]{:S(2)}) %collective-permute-start.19) | collective-permute-done | bytes 36896 | tf_op jit(solution)/shard_map/ppermute | solution.py:333
  69.8 2.0 %collective-permute-start.24 = (bf16[32,576]{1,0:T(8,128)(2,1)S(1)}, bf16[32,576]{1,0:T(8,128)(2,1)S(1)}, u32[]{:S(2)}, u32[]{:S(2)}) collective-permute-start(bf16[32,576]{1,0:T(8,128)(2,1)S(1)} %get-tuple-element.76), channel_id=1, source_target_pairs={{0,6},{1,7},{2,4},{3,5},{4,2},{5,3},{6,0},{7,1},{8,14},{9,15},{10,... | collective-permute-start | bytes 110600 | tf_op jit(solution)/shard_map/ppermute | solution.py:333
  71.9 0.0 collective-permute-done.20.refs_2_
  71.9 1.5 %collective-permute-start.25 = (bf16[32,576]{1,0:T(8,128)(2,1)S(1)}, bf16[32,576]{1,0:T(8,128)(2,1)S(1)}, u32[]{:S(2)}, u32[]{:S(2)}) collective-permute-start(bf16[32,576]{1,0:T(8,128)(2,1)S(1)} %get-tuple-element.77), channel_id=1, source_target_pairs={{0,7},{1,6},{2,5},{3,4},{4,3},{5,2},{6,1},{7,0},{8,15},{9,14},{10,... | collective-permute-start | bytes 110600 | tf_op jit(solution)/shard_map/ppermute | solution.py:333
  73.3 2.5 %collective-permute-done.24.refs_6_ = bf16[32,576]{1,0:T(8,128)(2,1)S(1)} collective-permute-done((bf16[32,576]{1,0:T(8,128)(2,1)S(1)}, bf16[32,576]{1,0:T(8,128)(2,1)S(1)}, u32[]{:S(2)}, u32[]{:S(2)}) %collective-permute-start.24) | collective-permute-done | bytes 36896 | tf_op jit(solution)/shard_map/ppermute | solution.py:333
  75.8 2.8 %collective-permute-done.25.refs_7_ = bf16[32,576]{1,0:T(8,128)(2,1)S(1)} collective-permute-done((bf16[32,576]{1,0:T(8,128)(2,1)S(1)}, bf16[32,576]{1,0:T(8,128)(2,1)S(1)}, u32[]{:S(2)}, u32[]{:S(2)}) %collective-permute-start.25) | collective-permute-done | bytes 36896 | tf_op jit(solution)/shard_map/ppermute | solution.py:333
  78.6 1.5 %shard_map.172 = (bf16[1,128,256]{2,1,0:T(8,128)(2,1)}, bf16[1,128,256]{2,1,0:T(8,128)(2,1)}, bf16[1,128,256]{2,1,0:T(8,128)(2,1)}, f32[1,32,768]{2,1,0:T(8,128)...) custom-call(s32[3]{0:T(128)S(1)} %pad_add_fusion.place, f32[128,256]{1,0:T(8,128)S(1)} %get-tuple-element.42.rate, ...), custom_call_target="tpu_custom_call" | custom-call | bytes 1716236 | tf_op jit(solution)/shard_map/pallas_call | solution.py:49
  (13 shorter events, 0.0 us)
Async XLA Ops:
  0.6 9.3 %copy-start = (bf16[1,128,256]{2,1,0:T(8,128)(2,1)S(1)}, bf16[1,128,256]{2,1,0:T(8,128)(2,1)}, u32[]{:S(2)}) copy-start(bf16[1,128,256]{2,1,0:T(8,128)(2,1)} %q.1) | copy-start | bytes 196612
  0.6 9.3 %copy-start.3 = (bf16[1,128,256]{2,1,0:T(8,128)(2,1)S(1)}, bf16[1,128,256]{2,1,0:T(8,128)(2,1)}, u32[]{:S(2)}) copy-start(bf16[1,128,256]{2,1,0:T(8,128)(2,1)} %og.1) | copy-start | bytes 196612
  0.7 9.3 %copy-start.2 = (bf16[1,128,256]{2,1,0:T(8,128)(2,1)S(1)}, bf16[1,128,256]{2,1,0:T(8,128)(2,1)}, u32[]{:S(2)}) copy-start(bf16[1,128,256]{2,1,0:T(8,128)(2,1)} %v.1) | copy-start | bytes 196612
  0.7 9.3 %copy-start.1 = (bf16[1,128,256]{2,1,0:T(8,128)(2,1)S(1)}, bf16[1,128,256]{2,1,0:T(8,128)(2,1)}, u32[]{:S(2)}) copy-start(bf16[1,128,256]{2,1,0:T(8,128)(2,1)} %k.1) | copy-start | bytes 196612
  2.6 23.3 %all-to-all-start = ((bf16[8,32,1152]{2,1,0:T(8,128)(2,1)}), bf16[8,32,1152]{2,1,0:T(8,128)(2,1)S(1)}, u32[]{:S(2)}, u32[]{:S(2)}) async-start(bf16[8,32,1152]{2,1,0:T(8,128)(2,1)} %shard_map.164), calls=%async_computation | async-start | bytes 1179648 | tf_op jit(solution)/shard_map/all_to_all | solution.py:356
  9.9 0.7 copy-start.4
  10.6 0.7 copy-start.5
  11.4 14.5 %collective-permute-start = (bf16[128,768]{1,0:T(8,128)(2,1)S(1)}, bf16[128,768]{1,0:T(8,128)(2,1)S(1)}, u32[]{:S(2)}, u32[]{:S(2)}) collective-permute-start(bf16[128,768]{1,0:T(8,128)(2,1)S(1)} %get-tuple-element.45), channel_id=1, source_target_pairs={{0,1},{1,0},{2,3},{3,2},{4,5},{5,4},{6,7},{7,6},{8,9},{9,8},{10,11... | collective-permute-start | bytes 589832 | tf_op jit(solution)/shard_map/ppermute | solution.py:333
  13.5 9.8 %collective-permute-start.2 = (bf16[128,256]{1,0:T(8,128)(2,1)S(1)}, bf16[128,256]{1,0:T(8,128)(2,1)S(1)}, u32[]{:S(2)}, u32[]{:S(2)}) collective-permute-start(bf16[128,256]{1,0:T(8,128)(2,1)S(1)} %bitcast.8), channel_id=1, source_target_pairs={{0,3},{1,2},{2,1},{3,0},{4,7},{5,6},{6,5},{7,4},{8,11},{9,10},{10,... | collective-permute-start | bytes 196616 | tf_op jit(solution)/shard_map/ppermute | solution.py:333
  14.9 8.7 %collective-permute-start.1 = (bf16[128,256]{1,0:T(8,128)(2,1)S(1)}, bf16[128,256]{1,0:T(8,128)(2,1)S(1)}, u32[]{:S(2)}, u32[]{:S(2)}) collective-permute-start(bf16[128,256]{1,0:T(8,128)(2,1)S(1)} %bitcast.9), channel_id=1, source_target_pairs={{0,2},{1,3},{2,0},{3,1},{4,6},{5,7},{6,4},{7,5},{8,10},{9,11},{10,... | collective-permute-start | bytes 196616 | tf_op jit(solution)/shard_map/ppermute | solution.py:333
  15.0 15.2 %collective-permute-start.7 = (bf16[128,512]{1,0:T(8,128)(2,1)S(1)}, bf16[128,512]{1,0:T(8,128)(2,1)S(1)}, u32[]{:S(2)}, u32[]{:S(2)}) collective-permute-start(bf16[128,512]{1,0:T(8,128)(2,1)S(1)} %get-tuple-element.62.refs_0_), channel_id=1, source_target_pairs={{0,3},{1,2},{2,1},{3,0},{4,7},{5,6},{6,5},{7,4},{8,11},{9,10},{10,... | collective-permute-start | bytes 393224 | tf_op jit(solution)/shard_map/ppermute | solution.py:333
  17.9 12.9 %collective-permute-start.6 = (bf16[128,512]{1,0:T(8,128)(2,1)S(1)}, bf16[128,512]{1,0:T(8,128)(2,1)S(1)}, u32[]{:S(2)}, u32[]{:S(2)}) collective-permute-start(bf16[128,512]{1,0:T(8,128)(2,1)S(1)} %get-tuple-element.62.refs_0_), channel_id=1, source_target_pairs={{0,2},{1,3},{2,0},{3,1},{4,6},{5,7},{6,4},{7,5},{8,10},{9,11},{10,... | collective-permute-start | bytes 393224 | tf_op jit(solution)/shard_map/ppermute | solution.py:333
  26.7 5.4 %collective-permute-start.3 = (bf16[128,256]{1,0:T(8,128)(2,1)S(1)}, bf16[128,256]{1,0:T(8,128)(2,1)S(1)}, u32[]{:S(2)}, u32[]{:S(2)}) collective-permute-start(bf16[128,256]{1,0:T(8,128)(2,1)S(1)} %get-tuple-element.49), channel_id=1, source_target_pairs={{0,2},{1,3},{2,0},{3,1},{4,6},{5,7},{6,4},{7,5},{8,10},{9,11},{10,... | collective-permute-start | bytes 196616 | tf_op jit(solution)/shard_map/ppermute | solution.py:333
  28.5 5.5 %collective-permute-start.4 = (bf16[128,256]{1,0:T(8,128)(2,1)S(1)}, bf16[128,256]{1,0:T(8,128)(2,1)S(1)}, u32[]{:S(2)}, u32[]{:S(2)}) collective-permute-start(bf16[128,256]{1,0:T(8,128)(2,1)S(1)} %get-tuple-element.50), channel_id=1, source_target_pairs={{0,3},{1,2},{2,1},{3,0},{4,7},{5,6},{6,5},{7,4},{8,11},{9,10},{10,... | collective-permute-start | bytes 196616 | tf_op jit(solution)/shard_map/ppermute | solution.py:333
  29.7 4.9 %collective-permute-start.5 = (bf16[128,256]{1,0:T(8,128)(2,1)S(1)}, bf16[128,256]{1,0:T(8,128)(2,1)S(1)}, u32[]{:S(2)}, u32[]{:S(2)}) collective-permute-start(bf16[128,256]{1,0:T(8,128)(2,1)S(1)} %get-tuple-element.51), channel_id=1, source_target_pairs={{0,1},{1,0},{2,3},{3,2},{4,5},{5,4},{6,7},{7,6},{8,9},{9,8},{10,11... | collective-permute-start | bytes 196616 | tf_op jit(solution)/shard_map/ppermute | solution.py:333
  34.8 4.3 %collective-permute-start.10 = (f32[2,128]{1,0:T(2,128)S(1)}, f32[2,128]{1,0:T(2,128)S(1)}, u32[]{:S(2)}, u32[]{:S(2)}) collective-permute-start(f32[2,128]{1,0:T(2,128)S(1)} %get-tuple-element.59.refs_0_), channel_id=1, source_target_pairs={{0,24},{8,16},{16,8},{24,0},{1,25},{9,17},{17,9},{25,1},{2,26},{10... | collective-permute-start | bytes 3080 | tf_op jit(solution)/shard_map/ppermute | solution.py:333
  34.9 4.3 %collective-permute-start.9 = (f32[2,128]{1,0:T(2,128)S(1)}, f32[2,128]{1,0:T(2,128)S(1)}, u32[]{:S(2)}, u32[]{:S(2)}) collective-permute-start(f32[2,128]{1,0:T(2,128)S(1)} %get-tuple-element.59.refs_0_), channel_id=1, source_target_pairs={{0,16},{8,24},{16,0},{24,8},{1,17},{9,25},{17,1},{25,9},{2,18},{10... | collective-permute-start | bytes 3080 | tf_op jit(solution)/shard_map/ppermute | solution.py:333
  36.4 2.7 %collective-permute-start.8 = (f32[2,128]{1,0:T(2,128)S(1)}, f32[2,128]{1,0:T(2,128)S(1)}, u32[]{:S(2)}, u32[]{:S(2)}) collective-permute-start(f32[2,128]{1,0:T(2,128)S(1)} %get-tuple-element.59.refs_0_), channel_id=1, source_target_pairs={{0,8},{8,0},{16,24},{24,16},{1,9},{9,1},{17,25},{25,17},{2,10},{10... | collective-permute-start | bytes 3080 | tf_op jit(solution)/shard_map/ppermute | solution.py:333
  36.7 8.3 %collective-permute-start.15 = (bf16[128,256]{1,0:T(8,128)(2,1)S(1)}, bf16[128,256]{1,0:T(8,128)(2,1)S(1)}, u32[]{:S(2)}, u32[]{:S(2)}) collective-permute-start(bf16[128,256]{1,0:T(8,128)(2,1)S(1)} %bitcast.11), channel_id=1, source_target_pairs={{0,4},{1,5},{2,6},{3,7},{4,0},{5,1},{6,2},{7,3},{8,12},{9,13},{10,... | collective-permute-start | bytes 196616 | tf_op jit(solution)/shard_map/ppermute | solution.py:333
  39.3 6.8 %collective-permute-start.14 = (bf16[128,256]{1,0:T(8,128)(2,1)S(1)}, bf16[128,256]{1,0:T(8,128)(2,1)S(1)}, u32[]{:S(2)}, u32[]{:S(2)}) collective-permute-start(bf16[128,256]{1,0:T(8,128)(2,1)S(1)} %shard_map.167.refs_4_), channel_id=1, source_target_pairs={{0,4},{1,5},{2,6},{3,7},{4,0},{5,1},{6,2},{7,3},{8,12},{9,13},{10,... | collective-permute-start | bytes 196616 | tf_op jit(solution)/shard_map/ppermute | solution.py:333
  41.1 7.0 %collective-permute-start.13 = (bf16[128,256]{1,0:T(8,128)(2,1)S(1)}, bf16[128,256]{1,0:T(8,128)(2,1)S(1)}, u32[]{:S(2)}, u32[]{:S(2)}) collective-permute-start(bf16[128,256]{1,0:T(8,128)(2,1)S(1)} %shard_map.167.refs_4_), channel_id=1, source_target_pairs={{0,3},{1,2},{2,1},{3,0},{4,7},{5,6},{6,5},{7,4},{8,11},{9,10},{10,... | collective-permute-start | bytes 196616 | tf_op jit(solution)/shard_map/ppermute | solution.py:333
  42.2 8.3 %collective-permute-start.12 = (bf16[128,256]{1,0:T(8,128)(2,1)S(1)}, bf16[128,256]{1,0:T(8,128)(2,1)S(1)}, u32[]{:S(2)}, u32[]{:S(2)}) collective-permute-start(bf16[128,256]{1,0:T(8,128)(2,1)S(1)} %shard_map.167.refs_4_), channel_id=1, source_target_pairs={{0,2},{1,3},{2,0},{3,1},{4,6},{5,7},{6,4},{7,5},{8,10},{9,11},{10,... | collective-permute-start | bytes 196616 | tf_op jit(solution)/shard_map/ppermute | solution.py:333
  43.1 7.4 %collective-permute-start.11 = (bf16[128,256]{1,0:T(8,128)(2,1)S(1)}, bf16[128,256]{1,0:T(8,128)(2,1)S(1)}, u32[]{:S(2)}, u32[]{:S(2)}) collective-permute-start(bf16[128,256]{1,0:T(8,128)(2,1)S(1)} %shard_map.167.refs_4_), channel_id=1, source_target_pairs={{0,1},{1,0},{2,3},{3,2},{4,5},{5,4},{6,7},{7,6},{8,9},{9,8},{10,11... | collective-permute-start | bytes 196616 | tf_op jit(solution)/shard_map/ppermute | solution.py:333
  46.1 7.4 %collective-permute-start.18 = (bf16[128,512]{1,0:T(8,128)(2,1)S(1)}, bf16[128,512]{1,0:T(8,128)(2,1)S(1)}, u32[]{:S(2)}, u32[]{:S(2)}) collective-permute-start(bf16[128,512]{1,0:T(8,128)(2,1)S(1)} %shard_map.170.refs_4_), channel_id=1, source_target_pairs={{0,3},{1,2},{2,1},{3,0},{4,7},{5,6},{6,5},{7,4},{8,11},{9,10},{10,... | collective-permute-start | bytes 393224 | tf_op jit(solution)/shard_map/ppermute | solution.py:333
  46.3 7.7 %collective-permute-start.17 = (bf16[128,512]{1,0:T(8,128)(2,1)S(1)}, bf16[128,512]{1,0:T(8,128)(2,1)S(1)}, u32[]{:S(2)}, u32[]{:S(2)}) collective-permute-start(bf16[128,512]{1,0:T(8,128)(2,1)S(1)} %shard_map.170.refs_4_), channel_id=1, source_target_pairs={{0,2},{1,3},{2,0},{3,1},{4,6},{5,7},{6,4},{7,5},{8,10},{9,11},{10,... | collective-permute-start | bytes 393224 | tf_op jit(solution)/shard_map/ppermute | solution.py:333
  48.1 6.9 %collective-permute-start.16 = (bf16[128,512]{1,0:T(8,128)(2,1)S(1)}, bf16[128,512]{1,0:T(8,128)(2,1)S(1)}, u32[]{:S(2)}, u32[]{:S(2)}) collective-permute-start(bf16[128,512]{1,0:T(8,128)(2,1)S(1)} %shard_map.170.refs_4_), channel_id=1, source_target_pairs={{0,1},{1,0},{2,3},{3,2},{4,5},{5,4},{6,7},{7,6},{8,9},{9,8},{10,11... | collective-permute-start | bytes 393224 | tf_op jit(solution)/shard_map/ppermute | solution.py:333
  58.0 20.6 %collective-permute-start.21 = (bf16[928,128]{1,0:T(8,128)(2,1)S(1)}, bf16[928,128]{1,0:T(8,128)(2,1)S(1)}, u32[]{:S(2)}, u32[]{:S(2)}) collective-permute-start(bf16[928,128]{1,0:T(8,128)(2,1)S(1)} %get-tuple-element.73), channel_id=1, source_target_pairs={{0,2},{1,3},{2,0},{3,1},{4,6},{5,7},{6,4},{7,5},{8,10},{9,11},{10,... | collective-permute-start | bytes 712712 | tf_op jit(solution)/shard_map/ppermute | solution.py:333
  58.1 20.5 %collective-permute-start.22 = (bf16[928,128]{1,0:T(8,128)(2,1)S(1)}, bf16[928,128]{1,0:T(8,128)(2,1)S(1)}, u32[]{:S(2)}, u32[]{:S(2)}) collective-permute-start(bf16[928,128]{1,0:T(8,128)(2,1)S(1)} %get-tuple-element.74), channel_id=1, source_target_pairs={{0,3},{1,2},{2,1},{3,0},{4,7},{5,6},{6,5},{7,4},{8,11},{9,10},{10,... | collective-permute-start | bytes 712712 | tf_op jit(solution)/shard_map/ppermute | solution.py:333
  60.1 18.5 %collective-permute-start.23 = (bf16[928,128]{1,0:T(8,128)(2,1)S(1)}, bf16[928,128]{1,0:T(8,128)(2,1)S(1)}, u32[]{:S(2)}, u32[]{:S(2)}) collective-permute-start(bf16[928,128]{1,0:T(8,128)(2,1)S(1)} %get-tuple-element.75), channel_id=1, source_target_pairs={{0,1},{1,0},{2,3},{3,2},{4,5},{5,4},{6,7},{7,6},{8,9},{9,8},{10,11... | collective-permute-start | bytes 712712 | tf_op jit(solution)/shard_map/ppermute | solution.py:333
  61.6 8.3 %collective-permute-start.19 = (bf16[32,576]{1,0:T(8,128)(2,1)S(1)}, bf16[32,576]{1,0:T(8,128)(2,1)S(1)}, u32[]{:S(2)}, u32[]{:S(2)}) collective-permute-start(bf16[32,576]{1,0:T(8,128)(2,1)S(1)} %get-tuple-element.71), channel_id=1, source_target_pairs={{0,4},{1,5},{2,6},{3,7},{4,0},{5,1},{6,2},{7,3},{8,12},{9,13},{10,... | collective-permute-start | bytes 110600 | tf_op jit(solution)/shard_map/ppermute | solution.py:333
  62.6 9.3 %collective-permute-start.20 = (bf16[32,576]{1,0:T(8,128)(2,1)S(1)}, bf16[32,576]{1,0:T(8,128)(2,1)S(1)}, u32[]{:S(2)}, u32[]{:S(2)}) collective-permute-start(bf16[32,576]{1,0:T(8,128)(2,1)S(1)} %get-tuple-element.72), channel_id=1, source_target_pairs={{0,5},{1,4},{2,7},{3,6},{4,1},{5,0},{6,3},{7,2},{8,13},{9,12},{10,... | collective-permute-start | bytes 110600 | tf_op jit(solution)/shard_map/ppermute | solution.py:333
  69.8 6.0 %collective-permute-start.24 = (bf16[32,576]{1,0:T(8,128)(2,1)S(1)}, bf16[32,576]{1,0:T(8,128)(2,1)S(1)}, u32[]{:S(2)}, u32[]{:S(2)}) collective-permute-start(bf16[32,576]{1,0:T(8,128)(2,1)S(1)} %get-tuple-element.76), channel_id=1, source_target_pairs={{0,6},{1,7},{2,4},{3,5},{4,2},{5,3},{6,0},{7,1},{8,14},{9,15},{10,... | collective-permute-start | bytes 110600 | tf_op jit(solution)/shard_map/ppermute | solution.py:333
  71.9 6.7 %collective-permute-start.25 = (bf16[32,576]{1,0:T(8,128)(2,1)S(1)}, bf16[32,576]{1,0:T(8,128)(2,1)S(1)}, u32[]{:S(2)}, u32[]{:S(2)}) collective-permute-start(bf16[32,576]{1,0:T(8,128)(2,1)S(1)} %get-tuple-element.77), channel_id=1, source_target_pairs={{0,7},{1,6},{2,5},{3,4},{4,3},{5,2},{6,1},{7,0},{8,15},{9,14},{10,... | collective-permute-start | bytes 110600 | tf_op jit(solution)/shard_map/ppermute | solution.py:333

commit v8 on v5

--- a/solution.py
+++ b/solution.py
@@ -168,20 +168,23 @@
 
 
 def near_kernel(slab, group, normed_ref, *refs):
-    q_near, od_near, outs, grads_out = refs[:group], refs[group : 2 * group], refs[2 * group : -1], refs[-1]
-    own, feat = od_near[0].shape
+    q_near, od_near, (grad_q, grads_out) = refs[:group], refs[group : 2 * group], refs[2 * group :]
+    feat = od_near[0].shape[1]
     normed = thirds(normed_ref, slab)
     delta_gate, delta_up, grads = query_side(stack(q_near, slice(0, feat)), stack(od_near), normed)
-    grad_q = (mm_nt(delta_gate, normed[0]) + mm_nt(delta_up, normed[1])).astype(BF)
-    for d in range(group):
-        outs[d][...] = grad_q[d * own : (d + 1) * own]
+    grad_q[...] = (mm_nt(delta_gate, normed[0]) + mm_nt(delta_up, normed[1])).astype(BF)
     for i in range(3):
         grads_out[i] = grads[i]
 
 
 def key_kernel(slab, group, w, *refs):
-    kvs, (factors, rises) = refs[:group], refs[group:]
+    kvs, (factors, rises, ratio, minus, plus) = refs[:group], refs[group:]
     feat = w.shape[0]
+    saved, start, norm_init, norm_saved = columns(w, slab)
+    for i in range(3):
+        ratio[i : i + 1, :] = norm_init[i] / norm_saved[i]
+        minus[i] = saved[i] * (norm_init[i] / (norm_saved[i] * norm_saved[i] * norm_saved[i]))
+        plus[i] = start[i] / (norm_init[i] * norm_saved[i])
     init = [w[:, pl.ds((3 + i) * slab, slab)] for i in range(3)]
     keys = stack(kvs, slice(-2 * feat, -feat))
     values = stack(kvs, slice(-feat, None))
@@ -198,37 +201,33 @@
     factors[3] = k_proj * k_up * k_bend
 
 
-def backward_kernel(slab, group, tok_groups, place, w, normed_ref, grads, factors, rises, *refs):
+def backward_kernel(
+    slab, group, tok_groups, place, w, normed_ref, grad_q, grads, factors, rises, ratio, minus, plus, *refs
+):
     far = group * (tok_groups - 1)
-    kvs, pairs, outs, refs = refs[:group], refs[group : group + far], refs[group + far : -4], refs[-4:]
-    inner_out, far_od, far_q, sums = refs
+    kvs, pairs, outs, (home, sums) = refs[:group], refs[group : group + far], refs[group + far : -2], refs[-2:]
     feat = w.shape[0]
+    outs, homes = outs[:group], outs[group:]
     own = outs[0].shape[0]
-    for i in range(far):
-        far_od[i // group, i % group] = pairs[i][:, 0:feat]
-        far_q[i // group, i % group] = pairs[i][:, feat : 2 * feat]
     normed = thirds(normed_ref, slab)
-    sums[...] = grads[...]
-
-    def other(e, carry):
-        more = query_side(flat(far_q[e]), flat(far_od[e]), normed)[2]
-        for i in range(3):
-            sums[i] += more[i]
-        return carry
-
-    lax.fori_loop(0, tok_groups - 1, other, 0)
-
-    saved, init, norm_init, norm_saved = columns(w, slab)
+    total = [grads[i] for i in range(3)]
+    for e in range(tok_groups - 1):
+        these = pairs[e * group : (e + 1) * group]
+        more = query_side(stack(these, slice(feat, 2 * feat)), stack(these, slice(0, feat)), normed)[2]
+        total = [total[i] + more[i] for i in range(3)]
+        if tok_groups > 2:
+            for i in range(3):
+                sums[i] = total[i]
+            total = [sums[i] for i in range(3)]
+
     cots, direct = [], []
     once = jnp.where(place[0] == 0, 1.0, 0.0)
     for i in range(3):
-        apply_grad = sums[i]
-        col_dot = jnp.sum(saved[i] * apply_grad, axis=0, keepdims=True)
-        cot = apply_grad * (norm_init[i] / norm_saved[i]) - saved[i] * (
-            col_dot * norm_init[i] / (norm_saved[i] * norm_saved[i] * norm_saved[i])
-        )
+        saved = w[:, pl.ds(i * slab, slab)].astype(F32)
+        col_dot = jnp.sum(saved * total[i], axis=0, keepdims=True)
+        cot = total[i] * ratio[i : i + 1, :] - minus[i] * col_dot
         cots.append(cot.astype(BF))
-        direct.append((cot + init[i] * (col_dot / (norm_init[i] * norm_saved[i]))) * once)
+        direct.append((cot + plus[i] * col_dot) * once)
 
     init_bf = [w[:, pl.ds((3 + i) * slab, slab)] for i in range(3)]
     keys = stack(kvs, slice(-2 * feat, -feat))
@@ -246,11 +245,25 @@
         + mm_nt(back_kup, init_bf[1])
     ).astype(BF)
     grad_v = (mm_nt(rises[0], cots[2]) + mm_nt(back_proj, init_bf[2])).astype(BF)
+    inner = (mm_tn(keys, back_kgate), mm_tn(keys, back_kup), mm_tn(values, back_proj))
+    whole = jnp.concatenate([inner[i] + direct[i] for i in range(3)], axis=1)
+    rows = home.shape[1]
+    for t in range(tok_groups):
+        home[t] = whole[t * rows : (t + 1) * rows]
+    for e, out in enumerate(homes):
+        out[...] = home[place[0] ^ e].astype(out.dtype)
     for d in range(group):
-        outs[d][:, 0:feat] = grad_k[d * own : (d + 1) * own]
-        outs[d][:, feat : 2 * feat] = grad_v[d * own : (d + 1) * own]
-    inner = (mm_tn(keys, back_kgate), mm_tn(keys, back_kup), mm_tn(values, back_proj))
-    inner_out[...] = jnp.concatenate([inner[i] + direct[i] for i in range(3)], axis=1).astype(BF)
+        outs[d][:, 0:feat] = grad_q[d * own : (d + 1) * own, :]
+        outs[d][:, feat : 2 * feat] = grad_k[d * own : (d + 1) * own]
+        outs[d][:, 2 * feat : 3 * feat] = grad_v[d * own : (d + 1) * own]
+
+
+def home_kernel(*refs):
+    blocks, out = refs[:-1], refs[-1]
+    group, rows, _ = out.shape
+    whole = total_of(blocks).astype(BF)
+    for j in range(group):
+        out[j] = whole[j * rows : (j + 1) * rows]
 
 
 def total_of(refs):
@@ -260,28 +273,24 @@
     return total
 
 
-def tokens_kernel(group, rate, *refs):
-    queries, got, (gq, gk, gv) = refs[:group], refs[group:-3], refs[-3:]
+def tokens_kernel(rate, *refs):
+    got, (gq, gk, gv) = refs[:-3], refs[-3:]
     feat = gq.shape[2]
-    gq[0] = total_of(queries).astype(BF)
     total = total_of(got)
-    gk[0] = total[:, 0:feat].astype(BF)
-    gv[0] = (rate[...] * total[:, feat : 2 * feat]).astype(BF)
-
-
-def weights_kernel(group, slab, got, *outs):
-    cols = []
-    for j in range(group):
-        total = got[j].astype(F32)
-        for p in range(j + group, got.shape[0], group):
-            total += got[p].astype(F32)
-        cols.append(total)
+    gq[0] = total[:, 0:feat].astype(BF)
+    gk[0] = total[:, feat : 2 * feat].astype(BF)
+    gv[0] = (rate[...] * total[:, 2 * feat : 3 * feat]).astype(BF)
+
+
+def weights_kernel(slab, got, *outs):
     for i in range(3):
-        outs[i][0] = jnp.concatenate([c[:, i * slab : (i + 1) * slab] for c in cols], axis=1)
+        cols = [got[j, :, i * slab : (i + 1) * slab].astype(F32) for j in range(got.shape[0])]
+        outs[i][0] = jnp.concatenate(cols, axis=1)
 
 
 def make_local(seq_n, head_n, group):
     tok_groups = seq_n // group
+    groups = [[t * group + j for j in range(group)] for t in range(tok_groups)]
 
     def move(x, dist, axis="seq", size=seq_n):
         return lax.ppermute(x, axis, [(i, i ^ dist) for i in range(size)])
@@ -328,7 +337,7 @@
             24,
             flops=3 * mflop,
         )
-        parts = [parts[0]] + [move(parts[d], d) for d in range(1, group)]
+        parts = [parts[0]] + [move(parts[d], d) for d in (*range(2, group), *range(1, min(2, group)))]
         *parts, kv_near = lax.optimization_barrier((*parts, kv_near))
         apply_out, sums = call(
             reduce_kernel, (arr((own, feat), F32), arr((2, own), F32)), (gg, *parts), 16
@@ -339,9 +348,10 @@
         (od,) = call(functools.partial(delta_kernel, head_n * feat), (block,), (apply_out, gg, *sums), 16)
         od_mirror = mirror(od)
         od_near = near_all(od)
-        factors, rises = call(
+        column = arr((3, seq_n * rows, slab), F32)
+        factors, rises, *stats = call(
             functools.partial(key_kernel, slab, group),
-            (arr((4, near, slab), F32), arr((3, near, slab), BF)),
+            (arr((4, near, slab), F32), arr((3, near, slab), BF), arr((3, slab), F32), column, column),
             (wall, *kv_near),
             24,
             flops=12 * mflop,
@@ -350,33 +360,40 @@
             call(pair_kernel, (arr((own, 2 * feat), BF),), pair, 16)[0] for pair in zip(od_mirror, q_mirror)
         ]
         pairs = [x for m in pairs for x in near_all(m)]
-        *grad_q, grads = call(
+        grad_q, grads = call(
             functools.partial(near_kernel, slab, group),
-            (*(block,) * group, arr((3, seq_n * rows, slab), F32)),
+            (arr((near, feat), BF), arr((3, seq_n * rows, slab), F32)),
             (normed, *q_near, *od_near),
             24,
             flops=12 * mflop,
         )
-        grad_q = [grad_q[0]] + [move(grad_q[d], d) for d in range(1, group)]
-
-        far = pltpu.VMEM((max(tok_groups - 1, 1), group, own, feat), BF)
-        *tok, inner = call(
+
+        home = (group * rows, 3 * slab)
+        result = call(
             functools.partial(backward_kernel, slab, group, tok_groups),
-            (*(arr((own, 2 * feat), BF),) * group, arr((seq_n * rows, 3 * slab), BF)),
-            (place, wall, normed, grads, factors, rises, *kv_near, *pairs),
-            32,
+            (
+                *(arr((own, 3 * feat), BF),) * group,
+                arr(home, F32),
+                *(arr(home, BF),) * (tok_groups - 1),
+            ),
+            (place, wall, normed, grad_q, grads, factors, rises, *stats, *kv_near, *pairs),
+            40,
             smem=1,
             flops=24 * mflop,
-            scratch=[far, far, pltpu.VMEM((3, seq_n * rows, slab), F32)],
-        )
-        inner = lax.all_to_all(inner.reshape(seq_n, rows, 3 * slab), "seq", 0, 0, tiled=True)
-        tok = [tok[0]] + [move(tok[d], d) for d in range(1, group)]
+            scratch=[
+                pltpu.VMEM((tok_groups, *home), F32),
+                pltpu.VMEM((3, seq_n * rows, slab), F32),
+            ],
+        )
+        tok, inner = result[:group], result[group:]
+        inner = [inner[0]] + [move(inner[e], e * group) for e in range(1, tok_groups)]
+        tok = [tok[0]] + [move(tok[d], d) for d in (*range(2, group), *range(1, min(2, group)))]
+        (inner,) = call(home_kernel, (arr((group, rows, 3 * slab), BF),), inner, 16)
+        inner = lax.all_to_all(inner, "seq", 0, 0, axis_index_groups=groups, tiled=True)
         out_tok = arr((1, own, feat), BF)
         grad_w = arr((1, rows, hidden), F32)
-        grads_t = call(
-            functools.partial(tokens_kernel, group), (out_tok,) * 3, (rate, *grad_q, *tok), 16
-        )
-        grads_w = call(functools.partial(weights_kernel, group, slab), (grad_w,) * 3, (inner,), 16)
+        grads_t = call(tokens_kernel, (out_tok,) * 3, (rate, *tok), 16)
+        grads_w = call(functools.partial(weights_kernel, slab), (grad_w,) * 3, (inner,), 16)
         return (*grads_t, *grads_w)
 
     return local

time: 81.9 us -> 87.4 us (1.067)
  waiting for transfers between devices: 26.5 us -> 36 us
  starting transfers between devices: 42.9 us -> 38.8 us
    ppermute x25 -> x23, waiting for transfers between devices: 26.5 us -> 36 us  [move(): return lax.ppermute(x, axis, [(i, i ^ dist) for i in range(size)])]
    ppermute x25 -> x23, starting transfers between devices: 31 us -> 28.2 us  [move(): return lax.ppermute(x, axis, [(i, i ^ dist) for i in range(size)])]
    all_to_all x1, starting transfers between devices: 4.59 us -> 3.34 us  [local(): lax.all_to_all(inner, 'seq', 0, 0, axis_index_groups=groups, tiled=True)]
    pallas_call x10 -> x11, Pallas kernels: 7.95 us -> 8.08 us  [call(): pl.pallas_call(kernel, out_shape=outs, in_specs=[SMEM] * smem + [VMEM] *...]
  transfers between devices with their start and end apart: 27 -> 25, of which waited for: 14 -> 15; matrix products, arithmetic and copies ran while one was open for 0% -> 0% of each run, Pallas kernels for 4% -> 4%
where the time goes in v8:
time: 87.4 us; the launch traced here: 87.1 us
  starting transfers between devices  38.8 us (44%)
  waiting for transfers between devices  36 us (41%)
  Pallas kernels  10.1 us (12%)
  local copies, waits for them, and re-layouts  1.35 us (2%)
    ppermute x23, waiting for transfers between devices, move(): return lax.ppermute(x, axis, [(i, i ^ dist) for i in range(size)])  36 us
    ppermute x23, starting transfers between devices, move(): return lax.ppermute(x, axis, [(i, i ^ dist) for i in range(size)])  28.2 us
    pallas_call x11, Pallas kernels, call(): pl.pallas_call(kernel, out_shape=outs, in_specs=[SMEM] * smem + [VMEM] *...  8.08 us
    all_to_all x1, starting transfers between devices, local(): lax.all_to_all(packed, 'seq', 0, 0, tiled=True)  7.26 us
    all_to_all x1, starting transfers between devices, local(): lax.all_to_all(inner, 'seq', 0, 0, axis_index_groups=groups, tiled=True)  3.34 us
    pallas_call x1, Pallas kernels, copying_call(): pl.pallas_call(kernel, out_shape=outs, in_specs=[pl.BlockSpec(memory_spac...  1.98 us
  transfers between devices with their start and end apart: 25, of which 15 were waited for; matrix products, arithmetic and copies ran while one was open for 0% of the time, Pallas kernels for 4%

profile of v8, /device:TPU:0, one launch (start us, length us, event | category | flops | bytes accessed | tf_op | source)
XLA Modules:
  0.0 87.1 jit_solution(8379849379904554812)
XLA Ops:
  0.7 2.0 %shard_map.164 = bf16[8,32,1152]{2,1,0:T(8,128)(2,1)} custom-call(bf16[1,32,768]{2,1,0:T(8,128)(2,1)} %refs_0_.1, bf16[1,32,768]{2,1,0:T(8,128)(2,1)} %refs_1_.1, bf16[1,32,768]{2,1,0:T(8,128)(2,1)} %refs_2_.1, bf16[1,32,768]{2,1,0:T(8,128)(2,1)} %refs_3_.1, bf16[1,32,768]{2,1,0:T(8,128)(2,1)} %refs_4_.1, bf16[1,32,768]{2,1,0:T(8,128)(2,1)} %refs_5_.1), custom_call_target="tpu_custom_call" | custom-call | tf_op jit(solution)/shard_map/pallas_call | solution.py:60
  2.7 7.3 %all-to-all-start = ((bf16[8,32,1152]{2,1,0:T(8,128)(2,1)}), bf16[8,32,1152]{2,1,0:T(8,128)(2,1)S(1)}, u32[]{:S(2)}, u32[]{:S(2)}) async-start(bf16[8,32,1152]{2,1,0:T(8,128)(2,1)} %shard_map.164), calls=%async_computation | async-start | bytes 1179648 | tf_op jit(solution)/shard_map/all_to_all | solution.py:319
  10.0 0.0 copy-start.4
  10.0 0.7 copy-done.4
  10.6 0.7 copy-done.5
  11.3 0.1 shard_map.163
  11.4 2.1 %collective-permute-start = (bf16[128,768]{1,0:T(8,128)(2,1)S(1)}, bf16[128,768]{1,0:T(8,128)(2,1)S(1)}, u32[]{:S(2)}, u32[]{:S(2)}) collective-permute-start(bf16[128,768]{1,0:T(8,128)(2,1)S(1)} %get-tuple-element.51), channel_id=1, source_target_pairs={{0,1},{1,0},{2,3},{3,2},{4,5},{5,4},{6,7},{7,6},{8,9},{9,8},{10,11... | collective-permute-start | bytes 589832 | tf_op jit(solution)/shard_map/ppermute | solution.py:296
  13.5 1.5 %collective-permute-start.2 = (bf16[128,256]{1,0:T(8,128)(2,1)S(1)}, bf16[128,256]{1,0:T(8,128)(2,1)S(1)}, u32[]{:S(2)}, u32[]{:S(2)}) collective-permute-start(bf16[128,256]{1,0:T(8,128)(2,1)S(1)} %bitcast.8), channel_id=1, source_target_pairs={{0,3},{1,2},{2,1},{3,0},{4,7},{5,6},{6,5},{7,4},{8,11},{9,10},{10,... | collective-permute-start | bytes 196616 | tf_op jit(solution)/shard_map/ppermute | solution.py:296
  14.9 0.1 collective-permute-start.1
  15.0 2.8 %collective-permute-start.7 = (bf16[128,512]{1,0:T(8,128)(2,1)S(1)}, bf16[128,512]{1,0:T(8,128)(2,1)S(1)}, u32[]{:S(2)}, u32[]{:S(2)}) collective-permute-start(bf16[128,512]{1,0:T(8,128)(2,1)S(1)} %get-tuple-element.68.refs_0_), channel_id=1, source_target_pairs={{0,3},{1,2},{2,1},{3,0},{4,7},{5,6},{6,5},{7,4},{8,11},{9,10},{10,... | collective-permute-start | bytes 393224 | tf_op jit(solution)/shard_map/ppermute | solution.py:296
  17.9 0.6 collective-permute-start.6
  18.4 4.8 %collective-permute-done.2.refs_3_ = bf16[128,256]{1,0:T(8,128)(2,1)S(1)} collective-permute-done((bf16[128,256]{1,0:T(8,128)(2,1)S(1)}, bf16[128,256]{1,0:T(8,128)(2,1)S(1)}, u32[]{:S(2)}, u32[]{:S(2)}) %collective-permute-start.2) | collective-permute-done | bytes 65568 | tf_op jit(solution)/shard_map/ppermute | solution.py:296
  23.3 0.4 collective-permute-done.1.refs_2_
  23.6 2.3 %collective-permute-done.refs_1_ = bf16[128,768]{1,0:T(8,128)(2,1)S(1)} collective-permute-done((bf16[128,768]{1,0:T(8,128)(2,1)S(1)}, bf16[128,768]{1,0:T(8,128)(2,1)S(1)}, u32[]{:S(2)}, u32[]{:S(2)}) %collective-permute-start) | collective-permute-done | bytes 196640 | tf_op jit(solution)/shard_map/ppermute | solution.py:296
  25.9 0.0 all-to-all-done
  25.9 0.8 shard_map.165
  26.7 1.8 %collective-permute-start.3 = (bf16[128,256]{1,0:T(8,128)(2,1)S(1)}, bf16[128,256]{1,0:T(8,128)(2,1)S(1)}, u32[]{:S(2)}, u32[]{:S(2)}) collective-permute-start(bf16[128,256]{1,0:T(8,128)(2,1)S(1)} %get-tuple-element.55), channel_id=1, source_target_pairs={{0,2},{1,3},{2,0},{3,1},{4,6},{5,7},{6,4},{7,5},{8,10},{9,11},{10,... | collective-permute-start | bytes 196616 | tf_op jit(solution)/shard_map/ppermute | solution.py:296
  28.6 1.1 %collective-permute-start.4 = (bf16[128,256]{1,0:T(8,128)(2,1)S(1)}, bf16[128,256]{1,0:T(8,128)(2,1)S(1)}, u32[]{:S(2)}, u32[]{:S(2)}) collective-permute-start(bf16[128,256]{1,0:T(8,128)(2,1)S(1)} %get-tuple-element.56), channel_id=1, source_target_pairs={{0,3},{1,2},{2,1},{3,0},{4,7},{5,6},{6,5},{7,4},{8,11},{9,10},{10,... | collective-permute-start | bytes 196616 | tf_op jit(solution)/shard_map/ppermute | solution.py:296
  29.7 0.6 collective-permute-start.5
  30.3 0.0 collective-permute-done.7.refs_3_
  30.3 0.5 collective-permute-done.6.refs_2_
  30.7 1.4 %collective-permute-done.3.refs_1_ = bf16[128,256]{1,0:T(8,128)(2,1)S(1)} collective-permute-done((bf16[128,256]{1,0:T(8,128)(2,1)S(1)}, bf16[128,256]{1,0:T(8,128)(2,1)S(1)}, u32[]{:S(2)}, u32[]{:S(2)}) %collective-permute-start.3) | collective-permute-done | bytes 65568 | tf_op jit(solution)/shard_map/ppermute | solution.py:296
  32.1 1.9 %collective-permute-done.4.refs_2_ = bf16[128,256]{1,0:T(8,128)(2,1)S(1)} collective-permute-done((bf16[128,256]{1,0:T(8,128)(2,1)S(1)}, bf16[128,256]{1,0:T(8,128)(2,1)S(1)}, u32[]{:S(2)}, u32[]{:S(2)}) %collective-permute-start.4) | collective-permute-done | bytes 65568 | tf_op jit(solution)/shard_map/ppermute | solution.py:296
  34.0 0.6 collective-permute-done.5.refs_3_
  34.6 0.1 shard_map.166
  34.8 0.1 collective-permute-start.10
  34.9 1.6 %collective-permute-start.9 = (f32[2,128]{1,0:T(2,128)S(1)}, f32[2,128]{1,0:T(2,128)S(1)}, u32[]{:S(2)}, u32[]{:S(2)}) collective-permute-start(f32[2,128]{1,0:T(2,128)S(1)} %get-tuple-element.65.refs_0_), channel_id=1, source_target_pairs={{0,16},{8,24},{16,0},{24,8},{1,17},{9,25},{17,1},{25,9},{2,18},{10... | collective-permute-start | bytes 3080 | tf_op jit(solution)/shard_map/ppermute | solution.py:296
  36.5 0.3 collective-permute-start.8
  36.7 2.4 %collective-permute-start.15 = (bf16[128,256]{1,0:T(8,128)(2,1)S(1)}, bf16[128,256]{1,0:T(8,128)(2,1)S(1)}, u32[]{:S(2)}, u32[]{:S(2)}) collective-permute-start(bf16[128,256]{1,0:T(8,128)(2,1)S(1)} %bitcast.11), channel_id=1, source_target_pairs={{0,4},{1,5},{2,6},{3,7},{4,0},{5,1},{6,2},{7,3},{8,12},{9,13},{10,... | collective-permute-start | bytes 196616 | tf_op jit(solution)/shard_map/ppermute | solution.py:296
  39.1 0.0 collective-permute-done.10.refs_3_
  39.1 0.0 collective-permute-done.9.refs_2_
  39.1 0.0 collective-permute-done.8.refs_1_
  39.1 0.1 shard_map.167.refs_4_
  39.3 1.8 %collective-permute-start.14 = (bf16[128,256]{1,0:T(8,128)(2,1)S(1)}, bf16[128,256]{1,0:T(8,128)(2,1)S(1)}, u32[]{:S(2)}, u32[]{:S(2)}) collective-permute-start(bf16[128,256]{1,0:T(8,128)(2,1)S(1)} %shard_map.167.refs_4_), channel_id=1, source_target_pairs={{0,4},{1,5},{2,6},{3,7},{4,0},{5,1},{6,2},{7,3},{8,12},{9,13},{10,... | collective-permute-start | bytes 196616 | tf_op jit(solution)/shard_map/ppermute | solution.py:296
  41.1 1.1 %collective-permute-start.13 = (bf16[128,256]{1,0:T(8,128)(2,1)S(1)}, bf16[128,256]{1,0:T(8,128)(2,1)S(1)}, u32[]{:S(2)}, u32[]{:S(2)}) collective-permute-start(bf16[128,256]{1,0:T(8,128)(2,1)S(1)} %shard_map.167.refs_4_), channel_id=1, source_target_pairs={{0,3},{1,2},{2,1},{3,0},{4,7},{5,6},{6,5},{7,4},{8,11},{9,10},{10,... | collective-permute-start | bytes 196616 | tf_op jit(solution)/shard_map/ppermute | solution.py:296
  42.2 0.9 %collective-permute-start.12 = (bf16[128,256]{1,0:T(8,128)(2,1)S(1)}, bf16[128,256]{1,0:T(8,128)(2,1)S(1)}, u32[]{:S(2)}, u32[]{:S(2)}) collective-permute-start(bf16[128,256]{1,0:T(8,128)(2,1)S(1)} %shard_map.167.refs_4_), channel_id=1, source_target_pairs={{0,2},{1,3},{2,0},{3,1},{4,6},{5,7},{6,4},{7,5},{8,10},{9,11},{10,... | collective-permute-start | bytes 196616 | tf_op jit(solution)/shard_map/ppermute | solution.py:296
  43.1 1.5 %collective-permute-start.11 = (bf16[128,256]{1,0:T(8,128)(2,1)S(1)}, bf16[128,256]{1,0:T(8,128)(2,1)S(1)}, u32[]{:S(2)}, u32[]{:S(2)}) collective-permute-start(bf16[128,256]{1,0:T(8,128)(2,1)S(1)} %shard_map.167.refs_4_), channel_id=1, source_target_pairs={{0,1},{1,0},{2,3},{3,2},{4,5},{5,4},{6,7},{7,6},{8,9},{9,8},{10,11... | collective-permute-start | bytes 196616 | tf_op jit(solution)/shard_map/ppermute | solution.py:296
  44.6 0.4 collective-permute-done.15.right
  45.0 1.1 %collective-permute-done.14.left = bf16[128,256]{1,0:T(8,128)(2,1)S(1)} collective-permute-done((bf16[128,256]{1,0:T(8,128)(2,1)S(1)}, bf16[128,256]{1,0:T(8,128)(2,1)S(1)}, u32[]{:S(2)}, u32[]{:S(2)}) %collective-permute-start.14) | collective-permute-done | bytes 65568 | tf_op jit(solution)/shard_map/ppermute | solution.py:296
  46.1 0.2 collective-permute-start.18
  46.3 1.8 %collective-permute-start.17 = (bf16[128,512]{1,0:T(8,128)(2,1)S(1)}, bf16[128,512]{1,0:T(8,128)(2,1)S(1)}, u32[]{:S(2)}, u32[]{:S(2)}) collective-permute-start(bf16[128,512]{1,0:T(8,128)(2,1)S(1)} %shard_map.170.refs_4_), channel_id=1, source_target_pairs={{0,2},{1,3},{2,0},{3,1},{4,6},{5,7},{6,4},{7,5},{8,10},{9,11},{10,... | collective-permute-start | bytes 393224 | tf_op jit(solution)/shard_map/ppermute | solution.py:296
  48.1 0.0 collective-permute-done.13.refs_7_
  48.1 1.5 %collective-permute-start.16 = (bf16[128,512]{1,0:T(8,128)(2,1)S(1)}, bf16[128,512]{1,0:T(8,128)(2,1)S(1)}, u32[]{:S(2)}, u32[]{:S(2)}) collective-permute-start(bf16[128,512]{1,0:T(8,128)(2,1)S(1)} %shard_map.170.refs_4_), channel_id=1, source_target_pairs={{0,1},{1,0},{2,3},{3,2},{4,5},{5,4},{6,7},{7,6},{8,9},{9,8},{10,11... | collective-permute-start | bytes 393224 | tf_op jit(solution)/shard_map/ppermute | solution.py:296
  49.7 0.1 pad_add_fusion.place
  49.7 1.1 %shard_map.169 = (f32[4,512,192]{2,1,0:T(8,128)S(1)}, bf16[3,512,192]{2,1,0:T(8,128)(2,1)S(1)}, f32[3,192]{1,0:T(4,128)S(1)}, f32[3,256,192]{2,1,0:T(8,128)S(1)}, f32[3,256,192]{2,1,0:T(8,128)S(1)}) custom-call(bf16[256,1152]{1,0:T(8,128)(2,1)S(1)} %bitcast.6, bf16[128,512]{1,0:T(8,128)(2,1)S(1)} %get-tuple-element.68.refs_0_, ...), custom_call_target="tpu_custom_call" | custom-call | flops 603979776 | bytes 4524288 | tf_op jit(solution)/shard_map/pallas_call | solution.py:48
  50.9 0.0 collective-permute-done.12.refs_6_
  50.9 0.0 collective-permute-done.11.refs_5_
  50.9 0.8 shard_map.168
  51.7 1.7 %collective-permute-done.18.refs_7_ = bf16[128,512]{1,0:T(8,128)(2,1)S(1)} collective-permute-done((bf16[128,512]{1,0:T(8,128)(2,1)S(1)}, bf16[128,512]{1,0:T(8,128)(2,1)S(1)}, u32[]{:S(2)}, u32[]{:S(2)}) %collective-permute-start.18) | collective-permute-done | bytes 131104 | tf_op jit(solution)/shard_map/ppermute | solution.py:296
  53.5 0.6 collective-permute-done.17.refs_6_
  54.0 1.1 %collective-permute-done.16.refs_5_ = bf16[128,512]{1,0:T(8,128)(2,1)S(1)} collective-permute-done((bf16[128,512]{1,0:T(8,128)(2,1)S(1)}, bf16[128,512]{1,0:T(8,128)(2,1)S(1)}, u32[]{:S(2)}, u32[]{:S(2)}) %collective-permute-start.16) | collective-permute-done | bytes 131104 | tf_op jit(solution)/shard_map/ppermute | solution.py:296
  55.1 2.8 %shard_map.171 = (bf16[128,768]{1,0:T(8,128)(2,1)S(1)}, bf16[128,768]{1,0:T(8,128)(2,1)S(1)}, bf16[128,768]{1,0:T(8,128)(2,1)S(1)}, bf16[128,768]{1,0:T(8,128)(2...) custom-call(s32[3]{0:T(128)S(1)} %pad_add_fusion.place, bf16[256,1152]{1,0:T(8,128)(2,1)S(1)} %bitcast.7, ...), custom_call_target="tpu_custom_call" | custom-call | flops 1207959552 | bytes 7424268 | tf_op jit(solution)/shard_map/pallas_call | solution.py:48
  57.9 0.8 collective-permute-start.22
  58.7 8.9 %collective-permute-done.22.refs_1_ = bf16[128,576]{1,0:T(8,128)(2,1)S(1)} collective-permute-done((bf16[128,576]{1,0:T(8,128)(2,1)S(1)}, bf16[128,576]{1,0:T(8,128)(2,1)S(1)}, u32[]{:S(2)}, u32[]{:S(2)}) %collective-permute-start.22) | collective-permute-done | bytes 147488 | tf_op jit(solution)/shard_map/ppermute | solution.py:296
  67.6 0.7 shard_map.173
  68.3 3.3 %all-to-all-start.1 = ((bf16[4,32,576]{2,1,0:T(8,128)(2,1)}), bf16[4,32,576]{2,1,0:T(8,128)(2,1)S(1)}, u32[]{:S(2)}, u32[]{:S(2)}) async-start(bf16[4,32,576]{2,1,0:T(8,128)(2,1)} %shard_map.173), calls=%async_computation.1 | async-start | bytes 327680 | tf_op jit(solution)/shard_map/all_to_all | solution.py:392
  71.7 2.0 %collective-permute-start.19 = (bf16[128,768]{1,0:T(8,128)(2,1)S(1)}, bf16[128,768]{1,0:T(8,128)(2,1)S(1)}, u32[]{:S(2)}, u32[]{:S(2)}) collective-permute-start(bf16[128,768]{1,0:T(8,128)(2,1)S(1)} %get-tuple-element.79), channel_id=1, source_target_pairs={{0,2},{1,3},{2,0},{3,1},{4,6},{5,7},{6,4},{7,5},{8,10},{9,11},{10,... | collective-permute-start | bytes 589832 | tf_op jit(solution)/shard_map/ppermute | solution.py:296
  73.7 1.5 %collective-permute-start.20 = (bf16[128,768]{1,0:T(8,128)(2,1)S(1)}, bf16[128,768]{1,0:T(8,128)(2,1)S(1)}, u32[]{:S(2)}, u32[]{:S(2)}) collective-permute-start(bf16[128,768]{1,0:T(8,128)(2,1)S(1)} %get-tuple-element.80), channel_id=1, source_target_pairs={{0,3},{1,2},{2,1},{3,0},{4,7},{5,6},{6,5},{7,4},{8,11},{9,10},{10,... | collective-permute-start | bytes 589832 | tf_op jit(solution)/shard_map/ppermute | solution.py:296
  75.1 0.1 collective-permute-start.21
  75.2 6.1 %collective-permute-done.19.refs_1_ = bf16[128,768]{1,0:T(8,128)(2,1)S(1)} collective-permute-done((bf16[128,768]{1,0:T(8,128)(2,1)S(1)}, bf16[128,768]{1,0:T(8,128)(2,1)S(1)}, u32[]{:S(2)}, u32[]{:S(2)}) %collective-permute-start.19) | collective-permute-done | bytes 196640 | tf_op jit(solution)/shard_map/ppermute | solution.py:296
  81.4 4.2 %collective-permute-done.20.refs_2_ = bf16[128,768]{1,0:T(8,128)(2,1)S(1)} collective-permute-done((bf16[128,768]{1,0:T(8,128)(2,1)S(1)}, bf16[128,768]{1,0:T(8,128)(2,1)S(1)}, u32[]{:S(2)}, u32[]{:S(2)}) %collective-permute-start.20) | collective-permute-done | bytes 196640 | tf_op jit(solution)/shard_map/ppermute | solution.py:296
  85.5 0.0 collective-permute-done.21.refs_3_
  85.5 0.7 shard_map.172
  86.3 0.8 shard_map.174
  (11 shorter events, 0.0 us)
Async XLA Ops:
  0.6 9.3 %copy-start = (bf16[1,128,256]{2,1,0:T(8,128)(2,1)S(1)}, bf16[1,128,256]{2,1,0:T(8,128)(2,1)}, u32[]{:S(2)}) copy-start(bf16[1,128,256]{2,1,0:T(8,128)(2,1)} %q.1) | copy-start | bytes 196612
  0.6 9.3 %copy-start.3 = (bf16[1,128,256]{2,1,0:T(8,128)(2,1)S(1)}, bf16[1,128,256]{2,1,0:T(8,128)(2,1)}, u32[]{:S(2)}) copy-start(bf16[1,128,256]{2,1,0:T(8,128)(2,1)} %og.1) | copy-start | bytes 196612
  0.7 9.3 %copy-start.2 = (bf16[1,128,256]{2,1,0:T(8,128)(2,1)S(1)}, bf16[1,128,256]{2,1,0:T(8,128)(2,1)}, u32[]{:S(2)}) copy-start(bf16[1,128,256]{2,1,0:T(8,128)(2,1)} %v.1) | copy-start | bytes 196612
  0.7 9.3 %copy-start.1 = (bf16[1,128,256]{2,1,0:T(8,128)(2,1)S(1)}, bf16[1,128,256]{2,1,0:T(8,128)(2,1)}, u32[]{:S(2)}) copy-start(bf16[1,128,256]{2,1,0:T(8,128)(2,1)} %k.1) | copy-start | bytes 196612
  2.7 23.3 %all-to-all-start = ((bf16[8,32,1152]{2,1,0:T(8,128)(2,1)}), bf16[8,32,1152]{2,1,0:T(8,128)(2,1)S(1)}, u32[]{:S(2)}, u32[]{:S(2)}) async-start(bf16[8,32,1152]{2,1,0:T(8,128)(2,1)} %shard_map.164), calls=%async_computation | async-start | bytes 1179648 | tf_op jit(solution)/shard_map/all_to_all | solution.py:319
  10.0 0.7 copy-start.4
  10.6 0.7 copy-start.5
  11.4 14.5 %collective-permute-start = (bf16[128,768]{1,0:T(8,128)(2,1)S(1)}, bf16[128,768]{1,0:T(8,128)(2,1)S(1)}, u32[]{:S(2)}, u32[]{:S(2)}) collective-permute-start(bf16[128,768]{1,0:T(8,128)(2,1)S(1)} %get-tuple-element.51), channel_id=1, source_target_pairs={{0,1},{1,0},{2,3},{3,2},{4,5},{5,4},{6,7},{7,6},{8,9},{9,8},{10,11... | collective-permute-start | bytes 589832 | tf_op jit(solution)/shard_map/ppermute | solution.py:296
  13.5 9.8 %collective-permute-start.2 = (bf16[128,256]{1,0:T(8,128)(2,1)S(1)}, bf16[128,256]{1,0:T(8,128)(2,1)S(1)}, u32[]{:S(2)}, u32[]{:S(2)}) collective-permute-start(bf16[128,256]{1,0:T(8,128)(2,1)S(1)} %bitcast.8), channel_id=1, source_target_pairs={{0,3},{1,2},{2,1},{3,0},{4,7},{5,6},{6,5},{7,4},{8,11},{9,10},{10,... | collective-permute-start | bytes 196616 | tf_op jit(solution)/shard_map/ppermute | solution.py:296
  14.9 8.7 %collective-permute-start.1 = (bf16[128,256]{1,0:T(8,128)(2,1)S(1)}, bf16[128,256]{1,0:T(8,128)(2,1)S(1)}, u32[]{:S(2)}, u32[]{:S(2)}) collective-permute-start(bf16[128,256]{1,0:T(8,128)(2,1)S(1)} %bitcast.9), channel_id=1, source_target_pairs={{0,2},{1,3},{2,0},{3,1},{4,6},{5,7},{6,4},{7,5},{8,10},{9,11},{10,... | collective-permute-start | bytes 196616 | tf_op jit(solution)/shard_map/ppermute | solution.py:296
  15.0 15.2 %collective-permute-start.7 = (bf16[128,512]{1,0:T(8,128)(2,1)S(1)}, bf16[128,512]{1,0:T(8,128)(2,1)S(1)}, u32[]{:S(2)}, u32[]{:S(2)}) collective-permute-start(bf16[128,512]{1,0:T(8,128)(2,1)S(1)} %get-tuple-element.68.refs_0_), channel_id=1, source_target_pairs={{0,3},{1,2},{2,1},{3,0},{4,7},{5,6},{6,5},{7,4},{8,11},{9,10},{10,... | collective-permute-start | bytes 393224 | tf_op jit(solution)/shard_map/ppermute | solution.py:296
  17.9 12.9 %collective-permute-start.6 = (bf16[128,512]{1,0:T(8,128)(2,1)S(1)}, bf16[128,512]{1,0:T(8,128)(2,1)S(1)}, u32[]{:S(2)}, u32[]{:S(2)}) collective-permute-start(bf16[128,512]{1,0:T(8,128)(2,1)S(1)} %get-tuple-element.68.refs_0_), channel_id=1, source_target_pairs={{0,2},{1,3},{2,0},{3,1},{4,6},{5,7},{6,4},{7,5},{8,10},{9,11},{10,... | collective-permute-start | bytes 393224 | tf_op jit(solution)/shard_map/ppermute | solution.py:296
  26.7 5.4 %collective-permute-start.3 = (bf16[128,256]{1,0:T(8,128)(2,1)S(1)}, bf16[128,256]{1,0:T(8,128)(2,1)S(1)}, u32[]{:S(2)}, u32[]{:S(2)}) collective-permute-start(bf16[128,256]{1,0:T(8,128)(2,1)S(1)} %get-tuple-element.55), channel_id=1, source_target_pairs={{0,2},{1,3},{2,0},{3,1},{4,6},{5,7},{6,4},{7,5},{8,10},{9,11},{10,... | collective-permute-start | bytes 196616 | tf_op jit(solution)/shard_map/ppermute | solution.py:296
  28.6 5.5 %collective-permute-start.4 = (bf16[128,256]{1,0:T(8,128)(2,1)S(1)}, bf16[128,256]{1,0:T(8,128)(2,1)S(1)}, u32[]{:S(2)}, u32[]{:S(2)}) collective-permute-start(bf16[128,256]{1,0:T(8,128)(2,1)S(1)} %get-tuple-element.56), channel_id=1, source_target_pairs={{0,3},{1,2},{2,1},{3,0},{4,7},{5,6},{6,5},{7,4},{8,11},{9,10},{10,... | collective-permute-start | bytes 196616 | tf_op jit(solution)/shard_map/ppermute | solution.py:296
  29.7 4.9 %collective-permute-start.5 = (bf16[128,256]{1,0:T(8,128)(2,1)S(1)}, bf16[128,256]{1,0:T(8,128)(2,1)S(1)}, u32[]{:S(2)}, u32[]{:S(2)}) collective-permute-start(bf16[128,256]{1,0:T(8,128)(2,1)S(1)} %get-tuple-element.57), channel_id=1, source_target_pairs={{0,1},{1,0},{2,3},{3,2},{4,5},{5,4},{6,7},{7,6},{8,9},{9,8},{10,11... | collective-permute-start | bytes 196616 | tf_op jit(solution)/shard_map/ppermute | solution.py:296
  34.8 4.3 %collective-permute-start.10 = (f32[2,128]{1,0:T(2,128)S(1)}, f32[2,128]{1,0:T(2,128)S(1)}, u32[]{:S(2)}, u32[]{:S(2)}) collective-permute-start(f32[2,128]{1,0:T(2,128)S(1)} %get-tuple-element.65.refs_0_), channel_id=1, source_target_pairs={{0,24},{8,16},{16,8},{24,0},{1,25},{9,17},{17,9},{25,1},{2,26},{10... | collective-permute-start | bytes 3080 | tf_op jit(solution)/shard_map/ppermute | solution.py:296
  34.9 4.3 %collective-permute-start.9 = (f32[2,128]{1,0:T(2,128)S(1)}, f32[2,128]{1,0:T(2,128)S(1)}, u32[]{:S(2)}, u32[]{:S(2)}) collective-permute-start(f32[2,128]{1,0:T(2,128)S(1)} %get-tuple-element.65.refs_0_), channel_id=1, source_target_pairs={{0,16},{8,24},{16,0},{24,8},{1,17},{9,25},{17,1},{25,9},{2,18},{10... | collective-permute-start | bytes 3080 | tf_op jit(solution)/shard_map/ppermute | solution.py:296
  36.5 2.7 %collective-permute-start.8 = (f32[2,128]{1,0:T(2,128)S(1)}, f32[2,128]{1,0:T(2,128)S(1)}, u32[]{:S(2)}, u32[]{:S(2)}) collective-permute-start(f32[2,128]{1,0:T(2,128)S(1)} %get-tuple-element.65.refs_0_), channel_id=1, source_target_pairs={{0,8},{8,0},{16,24},{24,16},{1,9},{9,1},{17,25},{25,17},{2,10},{10... | collective-permute-start | bytes 3080 | tf_op jit(solution)/shard_map/ppermute | solution.py:296
  36.7 8.3 %collective-permute-start.15 = (bf16[128,256]{1,0:T(8,128)(2,1)S(1)}, bf16[128,256]{1,0:T(8,128)(2,1)S(1)}, u32[]{:S(2)}, u32[]{:S(2)}) collective-permute-start(bf16[128,256]{1,0:T(8,128)(2,1)S(1)} %bitcast.11), channel_id=1, source_target_pairs={{0,4},{1,5},{2,6},{3,7},{4,0},{5,1},{6,2},{7,3},{8,12},{9,13},{10,... | collective-permute-start | bytes 196616 | tf_op jit(solution)/shard_map/ppermute | solution.py:296
  39.3 6.8 %collective-permute-start.14 = (bf16[128,256]{1,0:T(8,128)(2,1)S(1)}, bf16[128,256]{1,0:T(8,128)(2,1)S(1)}, u32[]{:S(2)}, u32[]{:S(2)}) collective-permute-start(bf16[128,256]{1,0:T(8,128)(2,1)S(1)} %shard_map.167.refs_4_), channel_id=1, source_target_pairs={{0,4},{1,5},{2,6},{3,7},{4,0},{5,1},{6,2},{7,3},{8,12},{9,13},{10,... | collective-permute-start | bytes 196616 | tf_op jit(solution)/shard_map/ppermute | solution.py:296
  41.1 7.0 %collective-permute-start.13 = (bf16[128,256]{1,0:T(8,128)(2,1)S(1)}, bf16[128,256]{1,0:T(8,128)(2,1)S(1)}, u32[]{:S(2)}, u32[]{:S(2)}) collective-permute-start(bf16[128,256]{1,0:T(8,128)(2,1)S(1)} %shard_map.167.refs_4_), channel_id=1, source_target_pairs={{0,3},{1,2},{2,1},{3,0},{4,7},{5,6},{6,5},{7,4},{8,11},{9,10},{10,... | collective-permute-start | bytes 196616 | tf_op jit(solution)/shard_map/ppermute | solution.py:296
  42.2 8.7 %collective-permute-start.12 = (bf16[128,256]{1,0:T(8,128)(2,1)S(1)}, bf16[128,256]{1,0:T(8,128)(2,1)S(1)}, u32[]{:S(2)}, u32[]{:S(2)}) collective-permute-start(bf16[128,256]{1,0:T(8,128)(2,1)S(1)} %shard_map.167.refs_4_), channel_id=1, source_target_pairs={{0,2},{1,3},{2,0},{3,1},{4,6},{5,7},{6,4},{7,5},{8,10},{9,11},{10,... | collective-permute-start | bytes 196616 | tf_op jit(solution)/shard_map/ppermute | solution.py:296
  43.1 7.8 %collective-permute-start.11 = (bf16[128,256]{1,0:T(8,128)(2,1)S(1)}, bf16[128,256]{1,0:T(8,128)(2,1)S(1)}, u32[]{:S(2)}, u32[]{:S(2)}) collective-permute-start(bf16[128,256]{1,0:T(8,128)(2,1)S(1)} %shard_map.167.refs_4_), channel_id=1, source_target_pairs={{0,1},{1,0},{2,3},{3,2},{4,5},{5,4},{6,7},{7,6},{8,9},{9,8},{10,11... | collective-permute-start | bytes 196616 | tf_op jit(solution)/shard_map/ppermute | solution.py:296
  46.1 7.4 %collective-permute-start.18 = (bf16[128,512]{1,0:T(8,128)(2,1)S(1)}, bf16[128,512]{1,0:T(8,128)(2,1)S(1)}, u32[]{:S(2)}, u32[]{:S(2)}) collective-permute-start(bf16[128,512]{1,0:T(8,128)(2,1)S(1)} %shard_map.170.refs_4_), channel_id=1, source_target_pairs={{0,3},{1,2},{2,1},{3,0},{4,7},{5,6},{6,5},{7,4},{8,11},{9,10},{10,... | collective-permute-start | bytes 393224 | tf_op jit(solution)/shard_map/ppermute | solution.py:296
  46.3 7.7 %collective-permute-start.17 = (bf16[128,512]{1,0:T(8,128)(2,1)S(1)}, bf16[128,512]{1,0:T(8,128)(2,1)S(1)}, u32[]{:S(2)}, u32[]{:S(2)}) collective-permute-start(bf16[128,512]{1,0:T(8,128)(2,1)S(1)} %shard_map.170.refs_4_), channel_id=1, source_target_pairs={{0,2},{1,3},{2,0},{3,1},{4,6},{5,7},{6,4},{7,5},{8,10},{9,11},{10,... | collective-permute-start | bytes 393224 | tf_op jit(solution)/shard_map/ppermute | solution.py:296
  48.1 6.9 %collective-permute-start.16 = (bf16[128,512]{1,0:T(8,128)(2,1)S(1)}, bf16[128,512]{1,0:T(8,128)(2,1)S(1)}, u32[]{:S(2)}, u32[]{:S(2)}) collective-permute-start(bf16[128,512]{1,0:T(8,128)(2,1)S(1)} %shard_map.170.refs_4_), channel_id=1, source_target_pairs={{0,1},{1,0},{2,3},{3,2},{4,5},{5,4},{6,7},{7,6},{8,9},{9,8},{10,11... | collective-permute-start | bytes 393224 | tf_op jit(solution)/shard_map/ppermute | solution.py:296
  57.9 9.8 %collective-permute-start.22 = (bf16[128,576]{1,0:T(8,128)(2,1)S(1)}, bf16[128,576]{1,0:T(8,128)(2,1)S(1)}, u32[]{:S(2)}, u32[]{:S(2)}) collective-permute-start(bf16[128,576]{1,0:T(8,128)(2,1)S(1)} %get-tuple-element.86), channel_id=1, source_target_pairs={{0,4},{1,5},{2,6},{3,7},{4,0},{5,1},{6,2},{7,3},{8,12},{9,13},{10,... | collective-permute-start | bytes 442376 | tf_op jit(solution)/shard_map/ppermute | solution.py:296
  68.3 18.0 %all-to-all-start.1 = ((bf16[4,32,576]{2,1,0:T(8,128)(2,1)}), bf16[4,32,576]{2,1,0:T(8,128)(2,1)S(1)}, u32[]{:S(2)}, u32[]{:S(2)}) async-start(bf16[4,32,576]{2,1,0:T(8,128)(2,1)} %shard_map.173), calls=%async_computation.1 | async-start | bytes 327680 | tf_op jit(solution)/shard_map/all_to_all | solution.py:392
  71.7 9.7 %collective-permute-start.19 = (bf16[128,768]{1,0:T(8,128)(2,1)S(1)}, bf16[128,768]{1,0:T(8,128)(2,1)S(1)}, u32[]{:S(2)}, u32[]{:S(2)}) collective-permute-start(bf16[128,768]{1,0:T(8,128)(2,1)S(1)} %get-tuple-element.79), channel_id=1, source_target_pairs={{0,2},{1,3},{2,0},{3,1},{4,6},{5,7},{6,4},{7,5},{8,10},{9,11},{10,... | collective-permute-start | bytes 589832 | tf_op jit(solution)/shard_map/ppermute | solution.py:296
  73.7 11.9 %collective-permute-start.20 = (bf16[128,768]{1,0:T(8,128)(2,1)S(1)}, bf16[128,768]{1,0:T(8,128)(2,1)S(1)}, u32[]{:S(2)}, u32[]{:S(2)}) collective-permute-start(bf16[128,768]{1,0:T(8,128)(2,1)S(1)} %get-tuple-element.80), channel_id=1, source_target_pairs={{0,3},{1,2},{2,1},{3,0},{4,7},{5,6},{6,5},{7,4},{8,11},{9,10},{10,... | collective-permute-start | bytes 589832 | tf_op jit(solution)/shard_map/ppermute | solution.py:296
  75.1 10.4 %collective-permute-start.21 = (bf16[128,768]{1,0:T(8,128)(2,1)S(1)}, bf16[128,768]{1,0:T(8,128)(2,1)S(1)}, u32[]{:S(2)}, u32[]{:S(2)}) collective-permute-start(bf16[128,768]{1,0:T(8,128)(2,1)S(1)} %get-tuple-element.81), channel_id=1, source_target_pairs={{0,1},{1,0},{2,3},{3,2},{4,5},{5,4},{6,7},{7,6},{8,9},{9,8},{10,11... | collective-permute-start | bytes 589832 | tf_op jit(solution)/shard_map/ppermute | solution.py:296

commit v9 on v7

--- a/solution.py
+++ b/solution.py
@@ -209,8 +209,13 @@
 
 
 def key_kernel(slab, group, w, *refs):
-    kvs, (factors, rises) = refs[:group], refs[group:]
+    kvs, (factors, rises, ratio, minus, plus) = refs[:group], refs[group:]
     feat = w.shape[0]
+    saved, start, norm_init, norm_saved = columns(w, slab)
+    for i in range(3):
+        ratio[i : i + 1, :] = norm_init[i] / norm_saved[i]
+        minus[i] = saved[i] * (norm_init[i] / (norm_saved[i] * norm_saved[i] * norm_saved[i]))
+        plus[i] = start[i] / (norm_init[i] * norm_saved[i])
     init = [w[:, pl.ds((3 + i) * slab, slab)] for i in range(3)]
     keys = stack(kvs, slice(-2 * feat, -feat))
     values = stack(kvs, slice(-feat, None))
@@ -227,7 +232,9 @@
     factors[3] = k_proj * k_up * k_bend
 
 
-def backward_kernel(slab, group, tok_groups, place, w, normed_ref, grad_q, grads, factors, rises, *refs):
+def backward_kernel(
+    slab, group, tok_groups, place, w, normed_ref, grad_q, grads, factors, rises, ratio, minus, plus, *refs
+):
     far = group * (tok_groups - 1)
     kvs, pairs, outs, (inner_buf, sums) = refs[:group], refs[group : group + far], refs[group + far : -2], refs[-2:]
     feat = w.shape[0]
@@ -244,17 +251,14 @@
                 sums[i] = total[i]
             total = [sums[i] for i in range(3)]
 
-    saved, init, norm_init, norm_saved = columns(w, slab)
     cots, direct = [], []
     once = jnp.where(place[0] == 0, 1.0, 0.0)
     for i in range(3):
-        apply_grad = total[i]
-        col_dot = jnp.sum(saved[i] * apply_grad, axis=0, keepdims=True)
-        cot = apply_grad * (norm_init[i] / norm_saved[i]) - saved[i] * (
-            col_dot * norm_init[i] / (norm_saved[i] * norm_saved[i] * norm_saved[i])
-        )
+        saved = w[:, pl.ds(i * slab, slab)].astype(F32)
+        col_dot = jnp.sum(saved * total[i], axis=0, keepdims=True)
+        cot = total[i] * ratio[i : i + 1, :] - minus[i] * col_dot
         cots.append(cot.astype(BF))
-        direct.append((cot + init[i] * (col_dot / (norm_init[i] * norm_saved[i]))) * once)
+        direct.append((cot + plus[i] * col_dot) * once)
 
     init_bf = [w[:, pl.ds((3 + i) * slab, slab)] for i in range(3)]
     keys = stack(kvs, slice(-2 * feat, -feat))
@@ -280,16 +284,25 @@
     tok_out[:, 0:feat] = grad_q[0:own, :]
     tok_out[:, feat : 2 * feat] = grad_k[0:own]
     tok_out[:, 2 * feat : 3 * feat] = grad_v[0:own]
-    for d in range(inner_buf.shape[0]):
-        block = inner_buf[place[2] ^ d].astype(BF)
-        if 0 < d < group:
-            out = outs[d]
-            at = 0
-            for tok in (grad_q, grad_k, grad_v):
-                at = put(out, at, tok[d * own : (d + 1) * own, :])
-            put(out, at, block)
-        else:
-            outs[d][...] = block
+    outs[0][...] = inner_buf[place[2]].astype(BF)
+    for d in range(1, group):
+        out, at = outs[d], 0
+        for tok in (grad_q, grad_k, grad_v):
+            at = put(out, at, tok[d * own : (d + 1) * own, :])
+        put(out, at, inner_buf[place[2] ^ d].astype(BF))
+    for dist, out in zip(far_distances(group, tok_groups), outs[group:]):
+        for i in range(2):
+            out[i * padded(rows) : i * padded(rows) + rows, :] = inner_buf[place[2] ^ dist ^ i].astype(BF)
+
+
+def relay_kernel(rows, *refs):
+    out, step = refs[-1], padded(rows)
+    for i, block in enumerate(refs[:-1]):
+        out[i * step : i * step + rows, :] = block[step : step + rows, :]
+
+
+def far_distances(group, tok_groups):
+    return [e * group + d for e in range(1, tok_groups) for d in range(0, group, 2)]
 
 
 def total_of(refs):
@@ -299,31 +312,34 @@
     return total
 
 
-def final_kernel(group, order, slab, place, rate, tok, *refs):
-    given, (gq, gk, gv, *outs, buf) = refs[:-7], refs[-7:]
-    blocks = dict(zip(order, given))
+def tokens_kernel(rate, tok, *refs):
+    blocks, (gq, gk, gv) = refs[:-3], refs[-3:]
     _, own, feat = gq.shape
-    rows = buf.shape[1]
     sums = [tok[:, i * feat : (i + 1) * feat].astype(F32) for i in range(3)]
-    for d in range(group):
-        block = blocks[d]
+    for block in blocks:
         at = 0
-        if d:
-            for i in range(3):
-                more, at = get(block, at, own, feat)
-                sums[i] += more.astype(F32)
-            value = get(block, at, rows, 3 * slab)[0]
-        else:
-            value = block[...]
-        buf[d] = value.astype(F32)
-        for other in range(d + group, len(order), group):
-            buf[d] += blocks[other][...].astype(F32)
+        for i in range(3):
+            more, at = get(block, at, own, feat)
+            sums[i] += more.astype(F32)
     gq[0] = sums[0].astype(BF)
     gk[0] = sums[1].astype(BF)
     gv[0] = (rate[...] * sums[2]).astype(BF)
-    cols = [buf[place[1] ^ j] for j in range(group)]
+
+
+def weights_kernel(group, tok_groups, slab, at, place, relayed, inner, *refs):
+    blocks, (*outs, buf) = refs[:-4], refs[-4:]
+    _, rows, cols = buf.shape
+    step = padded(rows)
+    buf[0] = inner[...].astype(F32)
+    for d in range(1, group):
+        buf[d] = get(blocks[d - 1], at, rows, cols)[0].astype(F32)
+    for i, dist in enumerate(far_distances(group, tok_groups)):
+        d = dist % group
+        buf[d] += blocks[group - 1 + i][0:rows, :].astype(F32)
+        buf[d ^ 1] += relayed[i * step : i * step + rows, :].astype(F32)
+    total = [buf[place[1] ^ j] for j in range(group)]
     for i in range(3):
-        outs[i][0] = jnp.concatenate([c[:, i * slab : (i + 1) * slab] for c in cols], axis=1)
+        outs[i][0] = jnp.concatenate([t[:, i * slab : (i + 1) * slab] for t in total], axis=1)
 
 
 def make_local(seq_n, head_n, group):
@@ -385,9 +401,10 @@
         (od,) = call(functools.partial(delta_kernel, head_n * feat), (block,), (apply_out, gg, *sums), 16)
         od_mirror = mirror(od)
         od_near = near_all(od)
-        factors, rises = call(
+        column = arr((3, seq_n * rows, slab), F32)
+        factors, rises, *stats = call(
             functools.partial(key_kernel, slab, group),
-            (arr((4, near, slab), F32), arr((3, near, slab), BF)),
+            (arr((4, near, slab), F32), arr((3, near, slab), BF), arr((3, slab), F32), column, column),
             (wall, *kv_near),
             24,
             flops=12 * mflop,
@@ -405,16 +422,16 @@
         )
 
         q_block = (own, feat)
-        tok, *sends = call(
+        far = far_distances(group, tok_groups)
+        tok, inner, *sends = call(
             functools.partial(backward_kernel, slab, group, tok_groups),
             (
                 arr((own, 3 * feat), BF),
-                *[
-                    message(*(q_block,) * 3, (rows, 3 * slab)) if 0 < d < group else arr((rows, 3 * slab), BF)
-                    for d in range(seq_n)
-                ],
+                arr((rows, 3 * slab), BF),
+                *(message(*(q_block,) * 3, (rows, 3 * slab)),) * (group - 1),
+                *(arr((2 * padded(rows), 3 * slab), BF),) * len(far),
             ),
-            (place, wall, normed, grad_q, grads, factors, rises, *kv_near, *pairs),
+            (place, wall, normed, grad_q, grads, factors, rises, *stats, *kv_near, *pairs),
             40,
             smem=1,
             flops=24 * mflop,
@@ -423,19 +440,29 @@
                 pltpu.VMEM((3, seq_n * rows, slab), F32),
             ],
         )
-        far = list(range(group, seq_n))
-        order = [0, *far[:2], *range(2, group), *range(1, min(2, group)), *far[2:]]
-        got = [move(sends[d], d) if d else sends[d] for d in order]
+        near_got = {d: move(sends[d - 1], d) for d in (*range(2, group), *range(1, min(2, group)))}
+        near_got = [near_got[d] for d in range(1, group)]
+        far_got = [move(x, d) for x, d in zip(sends[group - 1 :], far)]
+        (relayed,) = call(
+            functools.partial(relay_kernel, rows),
+            (arr((len(far) * padded(rows), 3 * slab), BF),),
+            far_got,
+            16,
+        )
+        relayed = move(relayed, 1)
         out_tok = arr((1, own, feat), BF)
         grad_w = arr((1, rows, hidden), F32)
-        return call(
-            functools.partial(final_kernel, group, order, slab),
-            (*(out_tok,) * 3, *(grad_w,) * 3),
-            (place, rate, tok, *got),
+        grads_t = call(tokens_kernel, (out_tok,) * 3, (rate, tok, *near_got), 16)
+        at = 3 * tiles(feat) * padded(own)
+        grads_w = call(
+            functools.partial(weights_kernel, group, tok_groups, slab, at),
+            (grad_w,) * 3,
+            (place, relayed, inner, *near_got, *far_got),
             16,
             smem=1,
             scratch=[pltpu.VMEM((group, rows, 3 * slab), F32)],
         )
+        return (*grads_t, *grads_w)
 
     return local
 

time: 80.3 us -> 81.2 us (1.011)
  starting transfers between devices: 41 us -> 38 us
  waiting for transfers between devices: 27.7 us -> 30.7 us
  Pallas kernels: 9.07 us -> 10 us
    ppermute x26 -> x25, starting transfers between devices: 33.8 us -> 30.8 us  [move(): return lax.ppermute(x, axis, [(i, i ^ dist) for i in range(size)])]
    ppermute x26 -> x25, waiting for transfers between devices: 27.7 us -> 30.7 us  [move(): return lax.ppermute(x, axis, [(i, i ^ dist) for i in range(size)])]
    pallas_call x9 -> x11, Pallas kernels: 7.11 us -> 8.06 us  [call(): pl.pallas_call(kernel, out_shape=outs, in_specs=[SMEM] * smem + [VMEM] *...]
  transfers between devices with their start and end apart: 27 -> 26, of which waited for: 15 -> 15; matrix products, arithmetic and copies ran while one was open for 0% -> 0% of each run, Pallas kernels for 3% -> 5%
where the time goes in v9:
time: 81.2 us; the launch traced here: 81 us
  starting transfers between devices  38 us (47%)
  waiting for transfers between devices  30.7 us (38%)
  Pallas kernels  10 us (12%)
  local copies, waits for them, and re-layouts  1.35 us (2%)
  between operations  0.82 us (1%)
    ppermute x25, starting transfers between devices, move(): return lax.ppermute(x, axis, [(i, i ^ dist) for i in range(size)])  30.8 us
    ppermute x25, waiting for transfers between devices, move(): return lax.ppermute(x, axis, [(i, i ^ dist) for i in range(size)])  30.7 us
    pallas_call x11, Pallas kernels, call(): pl.pallas_call(kernel, out_shape=outs, in_specs=[SMEM] * smem + [VMEM] *...  8.06 us
    all_to_all x1, starting transfers between devices, local(): lax.all_to_all(packed, 'seq', 0, 0, tiled=True)  7.26 us
    pallas_call x1, Pallas kernels, copying_call(): pl.pallas_call(kernel, out_shape=outs, in_specs=[pl.BlockSpec(memory_spac...  1.98 us
  transfers between devices with their start and end apart: 26, of which 15 were waited for; matrix products, arithmetic and copies ran while one was open for 0% of the time, Pallas kernels for 5%

profile of v9, /device:TPU:0, one launch (start us, length us, event | category | flops | bytes accessed | tf_op | source)
XLA Modules:
  0.0 81.0 jit_solution(11295761331297735961)
XLA Ops:
  0.7 2.0 %shard_map.164 = bf16[8,32,1152]{2,1,0:T(8,128)(2,1)} custom-call(bf16[1,32,768]{2,1,0:T(8,128)(2,1)} %refs_0_.1, bf16[1,32,768]{2,1,0:T(8,128)(2,1)} %refs_1_.1, bf16[1,32,768]{2,1,0:T(8,128)(2,1)} %refs_2_.1, bf16[1,32,768]{2,1,0:T(8,128)(2,1)} %refs_3_.1, bf16[1,32,768]{2,1,0:T(8,128)(2,1)} %refs_4_.1, bf16[1,32,768]{2,1,0:T(8,128)(2,1)} %refs_5_.1), custom_call_target="tpu_custom_call" | custom-call | tf_op jit(solution)/shard_map/pallas_call | solution.py:61
  2.7 7.3 %all-to-all-start = ((bf16[8,32,1152]{2,1,0:T(8,128)(2,1)}), bf16[8,32,1152]{2,1,0:T(8,128)(2,1)S(1)}, u32[]{:S(2)}, u32[]{:S(2)}) async-start(bf16[8,32,1152]{2,1,0:T(8,128)(2,1)} %shard_map.164), calls=%async_computation | async-start | bytes 1179648 | tf_op jit(solution)/shard_map/all_to_all | solution.py:372
  10.0 0.0 copy-start.4
  10.0 0.7 copy-done.4
  10.6 0.7 copy-done.5
  11.3 0.1 shard_map.163
  11.4 2.1 %collective-permute-start = (bf16[128,768]{1,0:T(8,128)(2,1)S(1)}, bf16[128,768]{1,0:T(8,128)(2,1)S(1)}, u32[]{:S(2)}, u32[]{:S(2)}) collective-permute-start(bf16[128,768]{1,0:T(8,128)(2,1)S(1)} %get-tuple-element.52), channel_id=1, source_target_pairs={{0,1},{1,0},{2,3},{3,2},{4,5},{5,4},{6,7},{7,6},{8,9},{9,8},{10,11... | collective-permute-start | bytes 589832 | tf_op jit(solution)/shard_map/ppermute | solution.py:349
  13.5 1.5 %collective-permute-start.2 = (bf16[128,256]{1,0:T(8,128)(2,1)S(1)}, bf16[128,256]{1,0:T(8,128)(2,1)S(1)}, u32[]{:S(2)}, u32[]{:S(2)}) collective-permute-start(bf16[128,256]{1,0:T(8,128)(2,1)S(1)} %bitcast.8), channel_id=1, source_target_pairs={{0,3},{1,2},{2,1},{3,0},{4,7},{5,6},{6,5},{7,4},{8,11},{9,10},{10,... | collective-permute-start | bytes 196616 | tf_op jit(solution)/shard_map/ppermute | solution.py:349
  14.9 0.1 collective-permute-start.1
  15.0 2.8 %collective-permute-start.7 = (bf16[128,512]{1,0:T(8,128)(2,1)S(1)}, bf16[128,512]{1,0:T(8,128)(2,1)S(1)}, u32[]{:S(2)}, u32[]{:S(2)}) collective-permute-start(bf16[128,512]{1,0:T(8,128)(2,1)S(1)} %get-tuple-element.69.refs_0_), channel_id=1, source_target_pairs={{0,3},{1,2},{2,1},{3,0},{4,7},{5,6},{6,5},{7,4},{8,11},{9,10},{10,... | collective-permute-start | bytes 393224 | tf_op jit(solution)/shard_map/ppermute | solution.py:349
  17.9 0.6 collective-permute-start.6
  18.4 4.8 %collective-permute-done.2.refs_3_ = bf16[128,256]{1,0:T(8,128)(2,1)S(1)} collective-permute-done((bf16[128,256]{1,0:T(8,128)(2,1)S(1)}, bf16[128,256]{1,0:T(8,128)(2,1)S(1)}, u32[]{:S(2)}, u32[]{:S(2)}) %collective-permute-start.2) | collective-permute-done | bytes 65568 | tf_op jit(solution)/shard_map/ppermute | solution.py:349
  23.3 0.4 collective-permute-done.1.refs_2_
  23.6 2.3 %collective-permute-done.refs_1_ = bf16[128,768]{1,0:T(8,128)(2,1)S(1)} collective-permute-done((bf16[128,768]{1,0:T(8,128)(2,1)S(1)}, bf16[128,768]{1,0:T(8,128)(2,1)S(1)}, u32[]{:S(2)}, u32[]{:S(2)}) %collective-permute-start) | collective-permute-done | bytes 196640 | tf_op jit(solution)/shard_map/ppermute | solution.py:349
  25.9 0.0 all-to-all-done
  25.9 0.8 shard_map.165
  26.7 1.8 %collective-permute-start.3 = (bf16[128,256]{1,0:T(8,128)(2,1)S(1)}, bf16[128,256]{1,0:T(8,128)(2,1)S(1)}, u32[]{:S(2)}, u32[]{:S(2)}) collective-permute-start(bf16[128,256]{1,0:T(8,128)(2,1)S(1)} %get-tuple-element.56), channel_id=1, source_target_pairs={{0,2},{1,3},{2,0},{3,1},{4,6},{5,7},{6,4},{7,5},{8,10},{9,11},{10,... | collective-permute-start | bytes 196616 | tf_op jit(solution)/shard_map/ppermute | solution.py:349
  28.6 1.1 %collective-permute-start.4 = (bf16[128,256]{1,0:T(8,128)(2,1)S(1)}, bf16[128,256]{1,0:T(8,128)(2,1)S(1)}, u32[]{:S(2)}, u32[]{:S(2)}) collective-permute-start(bf16[128,256]{1,0:T(8,128)(2,1)S(1)} %get-tuple-element.57), channel_id=1, source_target_pairs={{0,3},{1,2},{2,1},{3,0},{4,7},{5,6},{6,5},{7,4},{8,11},{9,10},{10,... | collective-permute-start | bytes 196616 | tf_op jit(solution)/shard_map/ppermute | solution.py:349
  29.7 0.6 collective-permute-start.5
  30.3 0.0 collective-permute-done.7.refs_3_
  30.3 0.5 collective-permute-done.6.refs_2_
  30.7 1.4 %collective-permute-done.3.refs_1_ = bf16[128,256]{1,0:T(8,128)(2,1)S(1)} collective-permute-done((bf16[128,256]{1,0:T(8,128)(2,1)S(1)}, bf16[128,256]{1,0:T(8,128)(2,1)S(1)}, u32[]{:S(2)}, u32[]{:S(2)}) %collective-permute-start.3) | collective-permute-done | bytes 65568 | tf_op jit(solution)/shard_map/ppermute | solution.py:349
  32.1 1.9 %collective-permute-done.4.refs_2_ = bf16[128,256]{1,0:T(8,128)(2,1)S(1)} collective-permute-done((bf16[128,256]{1,0:T(8,128)(2,1)S(1)}, bf16[128,256]{1,0:T(8,128)(2,1)S(1)}, u32[]{:S(2)}, u32[]{:S(2)}) %collective-permute-start.4) | collective-permute-done | bytes 65568 | tf_op jit(solution)/shard_map/ppermute | solution.py:349
  34.0 0.6 collective-permute-done.5.refs_3_
  34.6 0.1 shard_map.166
  34.8 0.1 collective-permute-start.10
  34.9 1.6 %collective-permute-start.9 = (f32[2,128]{1,0:T(2,128)S(1)}, f32[2,128]{1,0:T(2,128)S(1)}, u32[]{:S(2)}, u32[]{:S(2)}) collective-permute-start(f32[2,128]{1,0:T(2,128)S(1)} %get-tuple-element.66.refs_0_), channel_id=1, source_target_pairs={{0,16},{8,24},{16,0},{24,8},{1,17},{9,25},{17,1},{25,9},{2,18},{10... | collective-permute-start | bytes 3080 | tf_op jit(solution)/shard_map/ppermute | solution.py:349
  36.5 0.3 collective-permute-start.8
  36.7 2.4 %collective-permute-start.15 = (bf16[128,256]{1,0:T(8,128)(2,1)S(1)}, bf16[128,256]{1,0:T(8,128)(2,1)S(1)}, u32[]{:S(2)}, u32[]{:S(2)}) collective-permute-start(bf16[128,256]{1,0:T(8,128)(2,1)S(1)} %bitcast.11), channel_id=1, source_target_pairs={{0,4},{1,5},{2,6},{3,7},{4,0},{5,1},{6,2},{7,3},{8,12},{9,13},{10,... | collective-permute-start | bytes 196616 | tf_op jit(solution)/shard_map/ppermute | solution.py:349
  39.1 0.0 collective-permute-done.10.refs_3_
  39.1 0.0 collective-permute-done.9.refs_2_
  39.1 0.0 collective-permute-done.8.refs_1_
  39.1 0.1 shard_map.167.refs_4_
  39.3 1.8 %collective-permute-start.14 = (bf16[128,256]{1,0:T(8,128)(2,1)S(1)}, bf16[128,256]{1,0:T(8,128)(2,1)S(1)}, u32[]{:S(2)}, u32[]{:S(2)}) collective-permute-start(bf16[128,256]{1,0:T(8,128)(2,1)S(1)} %shard_map.167.refs_4_), channel_id=1, source_target_pairs={{0,4},{1,5},{2,6},{3,7},{4,0},{5,1},{6,2},{7,3},{8,12},{9,13},{10,... | collective-permute-start | bytes 196616 | tf_op jit(solution)/shard_map/ppermute | solution.py:349
  41.1 1.1 %collective-permute-start.13 = (bf16[128,256]{1,0:T(8,128)(2,1)S(1)}, bf16[128,256]{1,0:T(8,128)(2,1)S(1)}, u32[]{:S(2)}, u32[]{:S(2)}) collective-permute-start(bf16[128,256]{1,0:T(8,128)(2,1)S(1)} %shard_map.167.refs_4_), channel_id=1, source_target_pairs={{0,3},{1,2},{2,1},{3,0},{4,7},{5,6},{6,5},{7,4},{8,11},{9,10},{10,... | collective-permute-start | bytes 196616 | tf_op jit(solution)/shard_map/ppermute | solution.py:349
  42.2 0.9 %collective-permute-start.12 = (bf16[128,256]{1,0:T(8,128)(2,1)S(1)}, bf16[128,256]{1,0:T(8,128)(2,1)S(1)}, u32[]{:S(2)}, u32[]{:S(2)}) collective-permute-start(bf16[128,256]{1,0:T(8,128)(2,1)S(1)} %shard_map.167.refs_4_), channel_id=1, source_target_pairs={{0,2},{1,3},{2,0},{3,1},{4,6},{5,7},{6,4},{7,5},{8,10},{9,11},{10,... | collective-permute-start | bytes 196616 | tf_op jit(solution)/shard_map/ppermute | solution.py:349
  43.1 1.5 %collective-permute-start.11 = (bf16[128,256]{1,0:T(8,128)(2,1)S(1)}, bf16[128,256]{1,0:T(8,128)(2,1)S(1)}, u32[]{:S(2)}, u32[]{:S(2)}) collective-permute-start(bf16[128,256]{1,0:T(8,128)(2,1)S(1)} %shard_map.167.refs_4_), channel_id=1, source_target_pairs={{0,1},{1,0},{2,3},{3,2},{4,5},{5,4},{6,7},{7,6},{8,9},{9,8},{10,11... | collective-permute-start | bytes 196616 | tf_op jit(solution)/shard_map/ppermute | solution.py:349
  44.6 0.4 collective-permute-done.15.right
  45.0 1.1 %collective-permute-done.14.left = bf16[128,256]{1,0:T(8,128)(2,1)S(1)} collective-permute-done((bf16[128,256]{1,0:T(8,128)(2,1)S(1)}, bf16[128,256]{1,0:T(8,128)(2,1)S(1)}, u32[]{:S(2)}, u32[]{:S(2)}) %collective-permute-start.14) | collective-permute-done | bytes 65568 | tf_op jit(solution)/shard_map/ppermute | solution.py:349
  46.1 0.2 collective-permute-start.18
  46.3 1.8 %collective-permute-start.17 = (bf16[128,512]{1,0:T(8,128)(2,1)S(1)}, bf16[128,512]{1,0:T(8,128)(2,1)S(1)}, u32[]{:S(2)}, u32[]{:S(2)}) collective-permute-start(bf16[128,512]{1,0:T(8,128)(2,1)S(1)} %shard_map.170.refs_4_), channel_id=1, source_target_pairs={{0,2},{1,3},{2,0},{3,1},{4,6},{5,7},{6,4},{7,5},{8,10},{9,11},{10,... | collective-permute-start | bytes 393224 | tf_op jit(solution)/shard_map/ppermute | solution.py:349
  48.1 0.0 collective-permute-done.13.refs_7_
  48.1 1.5 %collective-permute-start.16 = (bf16[128,512]{1,0:T(8,128)(2,1)S(1)}, bf16[128,512]{1,0:T(8,128)(2,1)S(1)}, u32[]{:S(2)}, u32[]{:S(2)}) collective-permute-start(bf16[128,512]{1,0:T(8,128)(2,1)S(1)} %shard_map.170.refs_4_), channel_id=1, source_target_pairs={{0,1},{1,0},{2,3},{3,2},{4,5},{5,4},{6,7},{7,6},{8,9},{9,8},{10,11... | collective-permute-start | bytes 393224 | tf_op jit(solution)/shard_map/ppermute | solution.py:349
  49.7 0.1 pad_add_fusion.place
  49.7 1.1 %shard_map.169 = (f32[4,512,192]{2,1,0:T(8,128)S(1)}, bf16[3,512,192]{2,1,0:T(8,128)(2,1)S(1)}, f32[3,192]{1,0:T(4,128)S(1)}, f32[3,256,192]{2,1,0:T(8,128)S(1)}, f32[3,256,192]{2,1,0:T(8,128)S(1)}) custom-call(bf16[256,1152]{1,0:T(8,128)(2,1)S(1)} %bitcast.6, bf16[128,512]{1,0:T(8,128)(2,1)S(1)} %get-tuple-element.69.refs_0_, ...), custom_call_target="tpu_custom_call" | custom-call | flops 603979776 | bytes 4524288 | tf_op jit(solution)/shard_map/pallas_call | solution.py:49
  50.9 0.0 collective-permute-done.12.refs_6_
  50.9 0.0 collective-permute-done.11.refs_5_
  50.9 0.8 %shard_map.168 = (bf16[512,256]{1,0:T(8,128)(2,1)S(1)}, f32[3,256,192]{2,1,0:T(8,128)S(1)}) custom-call(bf16[256,576]{1,0:T(8,128)(2,1)S(1)} %get-tuple-element.53.normed_ref, bf16[128,256]{1,0:T(8,128)(2,1)S(1)} %bitcast.12, bf16[128,768]{1,0:T(8,128)(2,1)S(1)} %collective-permute-done.refs_1_, bf16[128,256]{1,0:T(8,128)(2,1)S(1)} %collective-permute-done.1.refs_2_, ...), custom_call_target="tpu_custom_call" | custom-call | flops 603979776 | bytes 1802240 | tf_op jit(solution)/shard_map/pallas_call | solution.py:49
  51.7 1.7 %collective-permute-done.18.refs_7_ = bf16[128,512]{1,0:T(8,128)(2,1)S(1)} collective-permute-done((bf16[128,512]{1,0:T(8,128)(2,1)S(1)}, bf16[128,512]{1,0:T(8,128)(2,1)S(1)}, u32[]{:S(2)}, u32[]{:S(2)}) %collective-permute-start.18) | collective-permute-done | bytes 131104 | tf_op jit(solution)/shard_map/ppermute | solution.py:349
  53.5 0.6 collective-permute-done.17.refs_6_
  54.0 1.1 %collective-permute-done.16.refs_5_ = bf16[128,512]{1,0:T(8,128)(2,1)S(1)} collective-permute-done((bf16[128,512]{1,0:T(8,128)(2,1)S(1)}, bf16[128,512]{1,0:T(8,128)(2,1)S(1)}, u32[]{:S(2)}, u32[]{:S(2)}) %collective-permute-start.16) | collective-permute-done | bytes 131104 | tf_op jit(solution)/shard_map/ppermute | solution.py:349
  55.1 2.8 %shard_map.171 = (bf16[128,768]{1,0:T(8,128)(2,1)S(1)}, bf16[32,576]{1,0:T(8,128)(2,1)S(1)}, bf16[928,128]{1,0:T(8,128)(2,1)S(1)}, bf16[928,128]{1,0:T(8,128)(2,...) custom-call(s32[3]{0:T(128)S(1)} %pad_add_fusion.place, ...), custom_call_target="tpu_custom_call" | custom-call | flops 1207959552 | bytes 7289100 | tf_op jit(solution)/shard_map/pallas_call | solution.py:49
  57.9 0.6 collective-permute-start.19
  58.5 0.3 collective-permute-start.20
  58.8 2.6 %collective-permute-start.21 = (bf16[928,128]{1,0:T(8,128)(2,1)S(1)}, bf16[928,128]{1,0:T(8,128)(2,1)S(1)}, u32[]{:S(2)}, u32[]{:S(2)}) collective-permute-start(bf16[928,128]{1,0:T(8,128)(2,1)S(1)} %get-tuple-element.82), channel_id=1, source_target_pairs={{0,3},{1,2},{2,1},{3,0},{4,7},{5,6},{6,5},{7,4},{8,11},{9,10},{10,... | collective-permute-start | bytes 712712 | tf_op jit(solution)/shard_map/ppermute | solution.py:349
  61.4 0.9 %collective-permute-start.22 = (bf16[64,576]{1,0:T(8,128)(2,1)S(1)}, bf16[64,576]{1,0:T(8,128)(2,1)S(1)}, u32[]{:S(2)}, u32[]{:S(2)}) collective-permute-start(bf16[64,576]{1,0:T(8,128)(2,1)S(1)} %get-tuple-element.86), channel_id=1, source_target_pairs={{0,4},{1,5},{2,6},{3,7},{4,0},{5,1},{6,2},{7,3},{8,12},{9,13},{10,... | collective-permute-start | bytes 221192 | tf_op jit(solution)/shard_map/ppermute | solution.py:349
  62.3 1.5 %collective-permute-start.23 = (bf16[64,576]{1,0:T(8,128)(2,1)S(1)}, bf16[64,576]{1,0:T(8,128)(2,1)S(1)}, u32[]{:S(2)}, u32[]{:S(2)}) collective-permute-start(bf16[64,576]{1,0:T(8,128)(2,1)S(1)} %get-tuple-element.87), channel_id=1, source_target_pairs={{0,6},{1,7},{2,4},{3,5},{4,2},{5,3},{6,0},{7,1},{8,14},{9,15},{10,... | collective-permute-start | bytes 221192 | tf_op jit(solution)/shard_map/ppermute | solution.py:349
  63.8 7.2 %collective-permute-done.22.refs_0_.refs_3_ = bf16[64,576]{1,0:T(8,128)(2,1)S(1)} collective-permute-done((bf16[64,576]{1,0:T(8,128)(2,1)S(1)}, bf16[64,576]{1,0:T(8,128)(2,1)S(1)}, u32[]{:S(2)}, u32[]{:S(2)}) %collective-permute-start.22) | collective-permute-done | bytes 73760 | tf_op jit(solution)/shard_map/ppermute | solution.py:349
  71.0 4.0 %collective-permute-done.23.refs_1_.refs_4_ = bf16[64,576]{1,0:T(8,128)(2,1)S(1)} collective-permute-done((bf16[64,576]{1,0:T(8,128)(2,1)S(1)}, bf16[64,576]{1,0:T(8,128)(2,1)S(1)}, u32[]{:S(2)}, u32[]{:S(2)}) %collective-permute-start.23) | collective-permute-done | bytes 73760 | tf_op jit(solution)/shard_map/ppermute | solution.py:349
  75.1 1.1 %collective-permute-start.24 = (bf16[64,576]{1,0:T(8,128)(2,1)S(1)}, bf16[64,576]{1,0:T(8,128)(2,1)S(1)}, u32[]{:S(2)}, u32[]{:S(2)}) collective-permute-start(bf16[64,576]{1,0:T(8,128)(2,1)S(1)} %shard_map.173), channel_id=1, source_target_pairs={{0,1},{1,0},{2,3},{3,2},{4,5},{5,4},{6,7},{7,6},{8,9},{9,8},{10,11... | collective-permute-start | bytes 221192 | tf_op jit(solution)/shard_map/ppermute | solution.py:349
  76.1 0.0 collective-permute-done.19.refs_0_
  76.1 0.8 shard_map.172
  76.9 2.7 %collective-permute-done.24.relayed = bf16[64,576]{1,0:T(8,128)(2,1)S(1)} collective-permute-done((bf16[64,576]{1,0:T(8,128)(2,1)S(1)}, bf16[64,576]{1,0:T(8,128)(2,1)S(1)}, u32[]{:S(2)}, u32[]{:S(2)}) %collective-permute-start.24) | collective-permute-done | bytes 73760 | tf_op jit(solution)/shard_map/ppermute | solution.py:349
  79.6 1.4 %shard_map.174 = (f32[1,32,768]{2,1,0:T(8,128)}, f32[1,32,768]{2,1,0:T(8,128)}, f32[1,32,768]{2,1,0:T(8,128)}) custom-call(s32[3]{0:T(128)S(1)} %pad_add_fusion.place, bf16[64,576]{1,0:T(8,128)(2,1)S(1)} %collective-permute-done.24.relayed, bf16[32,576]{1,0:T(8,128)(2,1)S(1)} %get-tuple-element.88.inner, ...), custom_call_target="tpu_custom_call" | custom-call | bytes 1265676 | tf_op jit(solution)/shard_map/pallas_call | solution.py:49
  (13 shorter events, 0.0 us)
Async XLA Ops:
  0.6 9.3 %copy-start = (bf16[1,128,256]{2,1,0:T(8,128)(2,1)S(1)}, bf16[1,128,256]{2,1,0:T(8,128)(2,1)}, u32[]{:S(2)}) copy-start(bf16[1,128,256]{2,1,0:T(8,128)(2,1)} %q.1) | copy-start | bytes 196612
  0.6 9.3 %copy-start.3 = (bf16[1,128,256]{2,1,0:T(8,128)(2,1)S(1)}, bf16[1,128,256]{2,1,0:T(8,128)(2,1)}, u32[]{:S(2)}) copy-start(bf16[1,128,256]{2,1,0:T(8,128)(2,1)} %og.1) | copy-start | bytes 196612
  0.7 9.3 %copy-start.2 = (bf16[1,128,256]{2,1,0:T(8,128)(2,1)S(1)}, bf16[1,128,256]{2,1,0:T(8,128)(2,1)}, u32[]{:S(2)}) copy-start(bf16[1,128,256]{2,1,0:T(8,128)(2,1)} %v.1) | copy-start | bytes 196612
  0.7 9.3 %copy-start.1 = (bf16[1,128,256]{2,1,0:T(8,128)(2,1)S(1)}, bf16[1,128,256]{2,1,0:T(8,128)(2,1)}, u32[]{:S(2)}) copy-start(bf16[1,128,256]{2,1,0:T(8,128)(2,1)} %k.1) | copy-start | bytes 196612
  2.7 23.3 %all-to-all-start = ((bf16[8,32,1152]{2,1,0:T(8,128)(2,1)}), bf16[8,32,1152]{2,1,0:T(8,128)(2,1)S(1)}, u32[]{:S(2)}, u32[]{:S(2)}) async-start(bf16[8,32,1152]{2,1,0:T(8,128)(2,1)} %shard_map.164), calls=%async_computation | async-start | bytes 1179648 | tf_op jit(solution)/shard_map/all_to_all | solution.py:372
  10.0 0.7 copy-start.4
  10.6 0.7 copy-start.5
  11.4 14.5 %collective-permute-start = (bf16[128,768]{1,0:T(8,128)(2,1)S(1)}, bf16[128,768]{1,0:T(8,128)(2,1)S(1)}, u32[]{:S(2)}, u32[]{:S(2)}) collective-permute-start(bf16[128,768]{1,0:T(8,128)(2,1)S(1)} %get-tuple-element.52), channel_id=1, source_target_pairs={{0,1},{1,0},{2,3},{3,2},{4,5},{5,4},{6,7},{7,6},{8,9},{9,8},{10,11... | collective-permute-start | bytes 589832 | tf_op jit(solution)/shard_map/ppermute | solution.py:349
  13.5 9.8 %collective-permute-start.2 = (bf16[128,256]{1,0:T(8,128)(2,1)S(1)}, bf16[128,256]{1,0:T(8,128)(2,1)S(1)}, u32[]{:S(2)}, u32[]{:S(2)}) collective-permute-start(bf16[128,256]{1,0:T(8,128)(2,1)S(1)} %bitcast.8), channel_id=1, source_target_pairs={{0,3},{1,2},{2,1},{3,0},{4,7},{5,6},{6,5},{7,4},{8,11},{9,10},{10,... | collective-permute-start | bytes 196616 | tf_op jit(solution)/shard_map/ppermute | solution.py:349
  14.9 8.7 %collective-permute-start.1 = (bf16[128,256]{1,0:T(8,128)(2,1)S(1)}, bf16[128,256]{1,0:T(8,128)(2,1)S(1)}, u32[]{:S(2)}, u32[]{:S(2)}) collective-permute-start(bf16[128,256]{1,0:T(8,128)(2,1)S(1)} %bitcast.9), channel_id=1, source_target_pairs={{0,2},{1,3},{2,0},{3,1},{4,6},{5,7},{6,4},{7,5},{8,10},{9,11},{10,... | collective-permute-start | bytes 196616 | tf_op jit(solution)/shard_map/ppermute | solution.py:349
  15.0 15.2 %collective-permute-start.7 = (bf16[128,512]{1,0:T(8,128)(2,1)S(1)}, bf16[128,512]{1,0:T(8,128)(2,1)S(1)}, u32[]{:S(2)}, u32[]{:S(2)}) collective-permute-start(bf16[128,512]{1,0:T(8,128)(2,1)S(1)} %get-tuple-element.69.refs_0_), channel_id=1, source_target_pairs={{0,3},{1,2},{2,1},{3,0},{4,7},{5,6},{6,5},{7,4},{8,11},{9,10},{10,... | collective-permute-start | bytes 393224 | tf_op jit(solution)/shard_map/ppermute | solution.py:349
  17.9 12.9 %collective-permute-start.6 = (bf16[128,512]{1,0:T(8,128)(2,1)S(1)}, bf16[128,512]{1,0:T(8,128)(2,1)S(1)}, u32[]{:S(2)}, u32[]{:S(2)}) collective-permute-start(bf16[128,512]{1,0:T(8,128)(2,1)S(1)} %get-tuple-element.69.refs_0_), channel_id=1, source_target_pairs={{0,2},{1,3},{2,0},{3,1},{4,6},{5,7},{6,4},{7,5},{8,10},{9,11},{10,... | collective-permute-start | bytes 393224 | tf_op jit(solution)/shard_map/ppermute | solution.py:349
  26.7 5.4 %collective-permute-start.3 = (bf16[128,256]{1,0:T(8,128)(2,1)S(1)}, bf16[128,256]{1,0:T(8,128)(2,1)S(1)}, u32[]{:S(2)}, u32[]{:S(2)}) collective-permute-start(bf16[128,256]{1,0:T(8,128)(2,1)S(1)} %get-tuple-element.56), channel_id=1, source_target_pairs={{0,2},{1,3},{2,0},{3,1},{4,6},{5,7},{6,4},{7,5},{8,10},{9,11},{10,... | collective-permute-start | bytes 196616 | tf_op jit(solution)/shard_map/ppermute | solution.py:349
  28.6 5.5 %collective-permute-start.4 = (bf16[128,256]{1,0:T(8,128)(2,1)S(1)}, bf16[128,256]{1,0:T(8,128)(2,1)S(1)}, u32[]{:S(2)}, u32[]{:S(2)}) collective-permute-start(bf16[128,256]{1,0:T(8,128)(2,1)S(1)} %get-tuple-element.57), channel_id=1, source_target_pairs={{0,3},{1,2},{2,1},{3,0},{4,7},{5,6},{6,5},{7,4},{8,11},{9,10},{10,... | collective-permute-start | bytes 196616 | tf_op jit(solution)/shard_map/ppermute | solution.py:349
  29.7 4.9 %collective-permute-start.5 = (bf16[128,256]{1,0:T(8,128)(2,1)S(1)}, bf16[128,256]{1,0:T(8,128)(2,1)S(1)}, u32[]{:S(2)}, u32[]{:S(2)}) collective-permute-start(bf16[128,256]{1,0:T(8,128)(2,1)S(1)} %get-tuple-element.58), channel_id=1, source_target_pairs={{0,1},{1,0},{2,3},{3,2},{4,5},{5,4},{6,7},{7,6},{8,9},{9,8},{10,11... | collective-permute-start | bytes 196616 | tf_op jit(solution)/shard_map/ppermute | solution.py:349
  34.8 4.3 %collective-permute-start.10 = (f32[2,128]{1,0:T(2,128)S(1)}, f32[2,128]{1,0:T(2,128)S(1)}, u32[]{:S(2)}, u32[]{:S(2)}) collective-permute-start(f32[2,128]{1,0:T(2,128)S(1)} %get-tuple-element.66.refs_0_), channel_id=1, source_target_pairs={{0,24},{8,16},{16,8},{24,0},{1,25},{9,17},{17,9},{25,1},{2,26},{10... | collective-permute-start | bytes 3080 | tf_op jit(solution)/shard_map/ppermute | solution.py:349
  34.9 4.3 %collective-permute-start.9 = (f32[2,128]{1,0:T(2,128)S(1)}, f32[2,128]{1,0:T(2,128)S(1)}, u32[]{:S(2)}, u32[]{:S(2)}) collective-permute-start(f32[2,128]{1,0:T(2,128)S(1)} %get-tuple-element.66.refs_0_), channel_id=1, source_target_pairs={{0,16},{8,24},{16,0},{24,8},{1,17},{9,25},{17,1},{25,9},{2,18},{10... | collective-permute-start | bytes 3080 | tf_op jit(solution)/shard_map/ppermute | solution.py:349
  36.5 2.7 %collective-permute-start.8 = (f32[2,128]{1,0:T(2,128)S(1)}, f32[2,128]{1,0:T(2,128)S(1)}, u32[]{:S(2)}, u32[]{:S(2)}) collective-permute-start(f32[2,128]{1,0:T(2,128)S(1)} %get-tuple-element.66.refs_0_), channel_id=1, source_target_pairs={{0,8},{8,0},{16,24},{24,16},{1,9},{9,1},{17,25},{25,17},{2,10},{10... | collective-permute-start | bytes 3080 | tf_op jit(solution)/shard_map/ppermute | solution.py:349
  36.7 8.3 %collective-permute-start.15 = (bf16[128,256]{1,0:T(8,128)(2,1)S(1)}, bf16[128,256]{1,0:T(8,128)(2,1)S(1)}, u32[]{:S(2)}, u32[]{:S(2)}) collective-permute-start(bf16[128,256]{1,0:T(8,128)(2,1)S(1)} %bitcast.11), channel_id=1, source_target_pairs={{0,4},{1,5},{2,6},{3,7},{4,0},{5,1},{6,2},{7,3},{8,12},{9,13},{10,... | collective-permute-start | bytes 196616 | tf_op jit(solution)/shard_map/ppermute | solution.py:349
  39.3 6.8 %collective-permute-start.14 = (bf16[128,256]{1,0:T(8,128)(2,1)S(1)}, bf16[128,256]{1,0:T(8,128)(2,1)S(1)}, u32[]{:S(2)}, u32[]{:S(2)}) collective-permute-start(bf16[128,256]{1,0:T(8,128)(2,1)S(1)} %shard_map.167.refs_4_), channel_id=1, source_target_pairs={{0,4},{1,5},{2,6},{3,7},{4,0},{5,1},{6,2},{7,3},{8,12},{9,13},{10,... | collective-permute-start | bytes 196616 | tf_op jit(solution)/shard_map/ppermute | solution.py:349
  41.1 7.0 %collective-permute-start.13 = (bf16[128,256]{1,0:T(8,128)(2,1)S(1)}, bf16[128,256]{1,0:T(8,128)(2,1)S(1)}, u32[]{:S(2)}, u32[]{:S(2)}) collective-permute-start(bf16[128,256]{1,0:T(8,128)(2,1)S(1)} %shard_map.167.refs_4_), channel_id=1, source_target_pairs={{0,3},{1,2},{2,1},{3,0},{4,7},{5,6},{6,5},{7,4},{8,11},{9,10},{10,... | collective-permute-start | bytes 196616 | tf_op jit(solution)/shard_map/ppermute | solution.py:349
  42.2 8.7 %collective-permute-start.12 = (bf16[128,256]{1,0:T(8,128)(2,1)S(1)}, bf16[128,256]{1,0:T(8,128)(2,1)S(1)}, u32[]{:S(2)}, u32[]{:S(2)}) collective-permute-start(bf16[128,256]{1,0:T(8,128)(2,1)S(1)} %shard_map.167.refs_4_), channel_id=1, source_target_pairs={{0,2},{1,3},{2,0},{3,1},{4,6},{5,7},{6,4},{7,5},{8,10},{9,11},{10,... | collective-permute-start | bytes 196616 | tf_op jit(solution)/shard_map/ppermute | solution.py:349
  43.1 7.8 %collective-permute-start.11 = (bf16[128,256]{1,0:T(8,128)(2,1)S(1)}, bf16[128,256]{1,0:T(8,128)(2,1)S(1)}, u32[]{:S(2)}, u32[]{:S(2)}) collective-permute-start(bf16[128,256]{1,0:T(8,128)(2,1)S(1)} %shard_map.167.refs_4_), channel_id=1, source_target_pairs={{0,1},{1,0},{2,3},{3,2},{4,5},{5,4},{6,7},{7,6},{8,9},{9,8},{10,11... | collective-permute-start | bytes 196616 | tf_op jit(solution)/shard_map/ppermute | solution.py:349
  46.1 7.4 %collective-permute-start.18 = (bf16[128,512]{1,0:T(8,128)(2,1)S(1)}, bf16[128,512]{1,0:T(8,128)(2,1)S(1)}, u32[]{:S(2)}, u32[]{:S(2)}) collective-permute-start(bf16[128,512]{1,0:T(8,128)(2,1)S(1)} %shard_map.170.refs_4_), channel_id=1, source_target_pairs={{0,3},{1,2},{2,1},{3,0},{4,7},{5,6},{6,5},{7,4},{8,11},{9,10},{10,... | collective-permute-start | bytes 393224 | tf_op jit(solution)/shard_map/ppermute | solution.py:349
  46.3 7.7 %collective-permute-start.17 = (bf16[128,512]{1,0:T(8,128)(2,1)S(1)}, bf16[128,512]{1,0:T(8,128)(2,1)S(1)}, u32[]{:S(2)}, u32[]{:S(2)}) collective-permute-start(bf16[128,512]{1,0:T(8,128)(2,1)S(1)} %shard_map.170.refs_4_), channel_id=1, source_target_pairs={{0,2},{1,3},{2,0},{3,1},{4,6},{5,7},{6,4},{7,5},{8,10},{9,11},{10,... | collective-permute-start | bytes 393224 | tf_op jit(solution)/shard_map/ppermute | solution.py:349
  48.1 6.9 %collective-permute-start.16 = (bf16[128,512]{1,0:T(8,128)(2,1)S(1)}, bf16[128,512]{1,0:T(8,128)(2,1)S(1)}, u32[]{:S(2)}, u32[]{:S(2)}) collective-permute-start(bf16[128,512]{1,0:T(8,128)(2,1)S(1)} %shard_map.170.refs_4_), channel_id=1, source_target_pairs={{0,1},{1,0},{2,3},{3,2},{4,5},{5,4},{6,7},{7,6},{8,9},{9,8},{10,11... | collective-permute-start | bytes 393224 | tf_op jit(solution)/shard_map/ppermute | solution.py:349
  57.9 18.3 %collective-permute-start.19 = (bf16[928,128]{1,0:T(8,128)(2,1)S(1)}, bf16[928,128]{1,0:T(8,128)(2,1)S(1)}, u32[]{:S(2)}, u32[]{:S(2)}) collective-permute-start(bf16[928,128]{1,0:T(8,128)(2,1)S(1)} %get-tuple-element.80), channel_id=1, source_target_pairs={{0,1},{1,0},{2,3},{3,2},{4,5},{5,4},{6,7},{7,6},{8,9},{9,8},{10,11... | collective-permute-start | bytes 712712 | tf_op jit(solution)/shard_map/ppermute | solution.py:349
  58.5 17.6 %collective-permute-start.20 = (bf16[928,128]{1,0:T(8,128)(2,1)S(1)}, bf16[928,128]{1,0:T(8,128)(2,1)S(1)}, u32[]{:S(2)}, u32[]{:S(2)}) collective-permute-start(bf16[928,128]{1,0:T(8,128)(2,1)S(1)} %get-tuple-element.81), channel_id=1, source_target_pairs={{0,2},{1,3},{2,0},{3,1},{4,6},{5,7},{6,4},{7,5},{8,10},{9,11},{10,... | collective-permute-start | bytes 712712 | tf_op jit(solution)/shard_map/ppermute | solution.py:349
  58.8 17.4 %collective-permute-start.21 = (bf16[928,128]{1,0:T(8,128)(2,1)S(1)}, bf16[928,128]{1,0:T(8,128)(2,1)S(1)}, u32[]{:S(2)}, u32[]{:S(2)}) collective-permute-start(bf16[928,128]{1,0:T(8,128)(2,1)S(1)} %get-tuple-element.82), channel_id=1, source_target_pairs={{0,3},{1,2},{2,1},{3,0},{4,7},{5,6},{6,5},{7,4},{8,11},{9,10},{10,... | collective-permute-start | bytes 712712 | tf_op jit(solution)/shard_map/ppermute | solution.py:349
  61.4 9.6 %collective-permute-start.22 = (bf16[64,576]{1,0:T(8,128)(2,1)S(1)}, bf16[64,576]{1,0:T(8,128)(2,1)S(1)}, u32[]{:S(2)}, u32[]{:S(2)}) collective-permute-start(bf16[64,576]{1,0:T(8,128)(2,1)S(1)} %get-tuple-element.86), channel_id=1, source_target_pairs={{0,4},{1,5},{2,6},{3,7},{4,0},{5,1},{6,2},{7,3},{8,12},{9,13},{10,... | collective-permute-start | bytes 221192 | tf_op jit(solution)/shard_map/ppermute | solution.py:349
  62.3 12.7 %collective-permute-start.23 = (bf16[64,576]{1,0:T(8,128)(2,1)S(1)}, bf16[64,576]{1,0:T(8,128)(2,1)S(1)}, u32[]{:S(2)}, u32[]{:S(2)}) collective-permute-start(bf16[64,576]{1,0:T(8,128)(2,1)S(1)} %get-tuple-element.87), channel_id=1, source_target_pairs={{0,6},{1,7},{2,4},{3,5},{4,2},{5,3},{6,0},{7,1},{8,14},{9,15},{10,... | collective-permute-start | bytes 221192 | tf_op jit(solution)/shard_map/ppermute | solution.py:349
  75.1 4.5 %collective-permute-start.24 = (bf16[64,576]{1,0:T(8,128)(2,1)S(1)}, bf16[64,576]{1,0:T(8,128)(2,1)S(1)}, u32[]{:S(2)}, u32[]{:S(2)}) collective-permute-start(bf16[64,576]{1,0:T(8,128)(2,1)S(1)} %shard_map.173), channel_id=1, source_target_pairs={{0,1},{1,0},{2,3},{3,2},{4,5},{5,4},{6,7},{7,6},{8,9},{9,8},{10,11... | collective-permute-start | bytes 221192 | tf_op jit(solution)/shard_map/ppermute | solution.py:349

commit v10 on v9

--- a/solution.py
+++ b/solution.py
@@ -198,12 +198,14 @@
     return delta_gate, delta_up, grads
 
 
-def near_kernel(slab, group, normed_ref, *refs):
+def near_kernel(slab, group, place, normed_ref, *refs):
     q_near, od_near, (grad_q, grads_out) = refs[:group], refs[group : 2 * group], refs[2 * group :]
-    feat = od_near[0].shape[1]
+    own = od_near[0].shape[0]
     normed = thirds(normed_ref, slab)
-    delta_gate, delta_up, grads = query_side(stack(q_near, slice(0, feat)), stack(od_near), normed)
-    grad_q[...] = (mm_nt(delta_gate, normed[0]) + mm_nt(delta_up, normed[1])).astype(BF)
+    delta_gate, delta_up, grads = query_side(stack(q_near, slice(0, od_near[0].shape[1])), stack(od_near), normed)
+    found = (mm_nt(delta_gate, normed[0]) + mm_nt(delta_up, normed[1])).astype(BF)
+    for d in range(group):
+        grad_q[place[1] ^ d] = found[d * own : (d + 1) * own]
     for i in range(3):
         grads_out[i] = grads[i]
 
@@ -233,7 +235,7 @@
 
 
 def backward_kernel(
-    slab, group, tok_groups, place, w, normed_ref, grad_q, grads, factors, rises, ratio, minus, plus, *refs
+    slab, group, tok_groups, place, w, normed_ref, grads, factors, rises, ratio, minus, plus, *refs
 ):
     far = group * (tok_groups - 1)
     kvs, pairs, outs, (inner_buf, sums) = refs[:group], refs[group : group + far], refs[group + far : -2], refs[-2:]
@@ -281,28 +283,16 @@
     rows = inner_buf.shape[1]
     for p in range(inner_buf.shape[0]):
         inner_buf[p] = whole[p * rows : (p + 1) * rows]
-    tok_out[:, 0:feat] = grad_q[0:own, :]
-    tok_out[:, feat : 2 * feat] = grad_k[0:own]
-    tok_out[:, 2 * feat : 3 * feat] = grad_v[0:own]
+    tok_out[:, 0:feat] = grad_k[0:own]
+    tok_out[:, feat : 2 * feat] = grad_v[0:own]
     outs[0][...] = inner_buf[place[2]].astype(BF)
     for d in range(1, group):
         out, at = outs[d], 0
-        for tok in (grad_q, grad_k, grad_v):
+        for tok in (grad_k, grad_v):
             at = put(out, at, tok[d * own : (d + 1) * own, :])
         put(out, at, inner_buf[place[2] ^ d].astype(BF))
-    for dist, out in zip(far_distances(group, tok_groups), outs[group:]):
-        for i in range(2):
-            out[i * padded(rows) : i * padded(rows) + rows, :] = inner_buf[place[2] ^ dist ^ i].astype(BF)
-
-
-def relay_kernel(rows, *refs):
-    out, step = refs[-1], padded(rows)
-    for i, block in enumerate(refs[:-1]):
-        out[i * step : i * step + rows, :] = block[step : step + rows, :]
-
-
-def far_distances(group, tok_groups):
-    return [e * group + d for e in range(1, tok_groups) for d in range(0, group, 2)]
+    for dist in range(group, inner_buf.shape[0]):
+        outs[dist][...] = inner_buf[place[2] ^ dist].astype(BF)
 
 
 def total_of(refs):
@@ -312,31 +302,31 @@
     return total
 
 
-def tokens_kernel(rate, tok, *refs):
+def tokens_kernel(rate, queries, tok, *refs):
     blocks, (gq, gk, gv) = refs[:-3], refs[-3:]
     _, own, feat = gq.shape
-    sums = [tok[:, i * feat : (i + 1) * feat].astype(F32) for i in range(3)]
+    total = queries[0].astype(F32)
+    for j in range(1, queries.shape[0]):
+        total += queries[j].astype(F32)
+    gq[0] = total.astype(BF)
+    sums = [tok[:, i * feat : (i + 1) * feat].astype(F32) for i in range(2)]
     for block in blocks:
         at = 0
-        for i in range(3):
+        for i in range(2):
             more, at = get(block, at, own, feat)
             sums[i] += more.astype(F32)
-    gq[0] = sums[0].astype(BF)
-    gk[0] = sums[1].astype(BF)
-    gv[0] = (rate[...] * sums[2]).astype(BF)
-
-
-def weights_kernel(group, tok_groups, slab, at, place, relayed, inner, *refs):
+    gk[0] = sums[0].astype(BF)
+    gv[0] = (rate[...] * sums[1]).astype(BF)
+
+
+def weights_kernel(group, slab, at, place, inner, *refs):
     blocks, (*outs, buf) = refs[:-4], refs[-4:]
     _, rows, cols = buf.shape
-    step = padded(rows)
-    buf[0] = inner[...].astype(F32)
-    for d in range(1, group):
-        buf[d] = get(blocks[d - 1], at, rows, cols)[0].astype(F32)
-    for i, dist in enumerate(far_distances(group, tok_groups)):
-        d = dist % group
-        buf[d] += blocks[group - 1 + i][0:rows, :].astype(F32)
-        buf[d ^ 1] += relayed[i * step : i * step + rows, :].astype(F32)
+    for d in range(group):
+        total = (get(blocks[d - 1], at, rows, cols)[0] if d else inner[...]).astype(F32)
+        for far in blocks[group - 1 + d :: group]:
+            total += far[...].astype(F32)
+        buf[d] = total
     total = [buf[place[1] ^ j] for j in range(group)]
     for i in range(3):
         outs[i][0] = jnp.concatenate([t[:, i * slab : (i + 1) * slab] for t in total], axis=1)
@@ -344,6 +334,7 @@
 
 def make_local(seq_n, head_n, group):
     tok_groups = seq_n // group
+    groups = [[t * group + j for j in range(group)] for t in range(tok_groups)]
 
     def move(x, dist, axis="seq", size=seq_n):
         return lax.ppermute(x, axis, [(i, i ^ dist) for i in range(size)])
@@ -415,23 +406,24 @@
         pairs = [x for m in pairs for x in near_all(m)]
         grad_q, grads = call(
             functools.partial(near_kernel, slab, group),
-            (arr((near, feat), BF), arr((3, seq_n * rows, slab), F32)),
-            (normed, *q_near, *od_near),
+            (arr((group, own, feat), BF), arr((3, seq_n * rows, slab), F32)),
+            (place, normed, *q_near, *od_near),
             24,
+            smem=1,
             flops=12 * mflop,
         )
 
         q_block = (own, feat)
-        far = far_distances(group, tok_groups)
+        grad_q = lax.all_to_all(grad_q, "seq", 0, 0, axis_index_groups=groups, tiled=True)
         tok, inner, *sends = call(
             functools.partial(backward_kernel, slab, group, tok_groups),
             (
-                arr((own, 3 * feat), BF),
+                arr((own, 2 * feat), BF),
                 arr((rows, 3 * slab), BF),
-                *(message(*(q_block,) * 3, (rows, 3 * slab)),) * (group - 1),
-                *(arr((2 * padded(rows), 3 * slab), BF),) * len(far),
+                *(message(*(q_block,) * 2, (rows, 3 * slab)),) * (group - 1),
+                *(arr((rows, 3 * slab), BF),) * (seq_n - group),
             ),
-            (place, wall, normed, grad_q, grads, factors, rises, *stats, *kv_near, *pairs),
+            (place, wall, normed, grads, factors, rises, *stats, *kv_near, *pairs),
             40,
             smem=1,
             flops=24 * mflop,
@@ -440,24 +432,18 @@
                 pltpu.VMEM((3, seq_n * rows, slab), F32),
             ],
         )
+        sends, grad_q = lax.optimization_barrier((sends, grad_q))
         near_got = {d: move(sends[d - 1], d) for d in (*range(2, group), *range(1, min(2, group)))}
         near_got = [near_got[d] for d in range(1, group)]
-        far_got = [move(x, d) for x, d in zip(sends[group - 1 :], far)]
-        (relayed,) = call(
-            functools.partial(relay_kernel, rows),
-            (arr((len(far) * padded(rows), 3 * slab), BF),),
-            far_got,
-            16,
-        )
-        relayed = move(relayed, 1)
+        far_got = [move(sends[d - 1], d) for d in range(group, seq_n)]
         out_tok = arr((1, own, feat), BF)
         grad_w = arr((1, rows, hidden), F32)
-        grads_t = call(tokens_kernel, (out_tok,) * 3, (rate, tok, *near_got), 16)
-        at = 3 * tiles(feat) * padded(own)
+        grads_t = call(tokens_kernel, (out_tok,) * 3, (rate, grad_q, tok, *near_got), 16)
+        at = 2 * tiles(feat) * padded(own)
         grads_w = call(
-            functools.partial(weights_kernel, group, tok_groups, slab, at),
+            functools.partial(weights_kernel, group, slab, at),
             (grad_w,) * 3,
-            (place, relayed, inner, *near_got, *far_got),
+            (place, inner, *near_got, *far_got),
             16,
             smem=1,
             scratch=[pltpu.VMEM((group, rows, 3 * slab), F32)],

time: 81.2 us -> 90.8 us (1.12)
  starting transfers between devices: 38 us -> 46.5 us
  Pallas kernels: 10 us -> 11 us
    ppermute x25 -> x26, starting transfers between devices: 30.8 us -> 35.8 us  [move(): return lax.ppermute(x, axis, [(i, i ^ dist) for i in range(size)])]
    all_to_all x0 -> x1, starting transfers between devices: none -> 3.4 us  [local(): lax.all_to_all(grad_q, 'seq', 0, 0, axis_index_groups=groups, tiled=True)]
    pallas_call x11 -> x10, Pallas kernels: 8.06 us -> 9.03 us  [call(): pl.pallas_call(kernel, out_shape=outs, in_specs=[SMEM] * smem + [VMEM] *...]
    unnamed x12 -> x14, local copies, waits for them, and re-layouts: 1.35 us -> 1.96 us
    ppermute x25 -> x26, waiting for transfers between devices: 30.7 us -> 30.1 us  [move(): return lax.ppermute(x, axis, [(i, i ^ dist) for i in range(size)])]
  transfers between devices with their start and end apart: 26 -> 28, of which waited for: 15 -> 18; matrix products, arithmetic and copies ran while one was open for 0% -> 0% of each run, Pallas kernels for 5% -> 6%
where the time goes in v10:
time: 90.8 us; the launch traced here: 90.4 us
  starting transfers between devices  46.5 us (51%)
  waiting for transfers between devices  30.1 us (33%)
  Pallas kernels  11 us (12%)
  local copies, waits for them, and re-layouts  1.96 us (2%)
    ppermute x26, starting transfers between devices, move(): return lax.ppermute(x, axis, [(i, i ^ dist) for i in range(size)])  35.8 us
    ppermute x26, waiting for transfers between devices, move(): return lax.ppermute(x, axis, [(i, i ^ dist) for i in range(size)])  30.1 us
    pallas_call x10, Pallas kernels, call(): pl.pallas_call(kernel, out_shape=outs, in_specs=[SMEM] * smem + [VMEM] *...  9.03 us
    all_to_all x1, starting transfers between devices, local(): lax.all_to_all(packed, 'seq', 0, 0, tiled=True)  7.26 us
    all_to_all x1, starting transfers between devices, local(): lax.all_to_all(grad_q, 'seq', 0, 0, axis_index_groups=groups, tiled=True)  3.4 us
    pallas_call x1, Pallas kernels, copying_call(): pl.pallas_call(kernel, out_shape=outs, in_specs=[pl.BlockSpec(memory_spac...  1.96 us
    unnamed x14, local copies, waits for them, and re-layouts  1.96 us
  transfers between devices with their start and end apart: 28, of which 18 were waited for; matrix products, arithmetic and copies ran while one was open for 0% of the time, Pallas kernels for 6%

profile of v10, /device:TPU:0, one launch (start us, length us, event | category | flops | bytes accessed | tf_op | source)
XLA Modules:
  0.0 90.4 jit_solution(8720166414892983892)
XLA Ops:
  0.7 2.0 %shard_map.164 = bf16[8,32,1152]{2,1,0:T(8,128)(2,1)} custom-call(bf16[1,32,768]{2,1,0:T(8,128)(2,1)} %refs_0_.1, bf16[1,32,768]{2,1,0:T(8,128)(2,1)} %refs_1_.1, bf16[1,32,768]{2,1,0:T(8,128)(2,1)} %refs_2_.1, bf16[1,32,768]{2,1,0:T(8,128)(2,1)} %refs_3_.1, bf16[1,32,768]{2,1,0:T(8,128)(2,1)} %refs_4_.1, bf16[1,32,768]{2,1,0:T(8,128)(2,1)} %refs_5_.1), custom_call_target="tpu_custom_call" | custom-call | tf_op jit(solution)/shard_map/pallas_call | solution.py:61
  2.6 7.3 %all-to-all-start = ((bf16[8,32,1152]{2,1,0:T(8,128)(2,1)}), bf16[8,32,1152]{2,1,0:T(8,128)(2,1)S(1)}, u32[]{:S(2)}, u32[]{:S(2)}) async-start(bf16[8,32,1152]{2,1,0:T(8,128)(2,1)} %shard_map.164), calls=%async_computation | async-start | bytes 1179648 | tf_op jit(solution)/shard_map/all_to_all | solution.py:363
  9.9 0.0 copy-start.4
  10.0 0.7 copy-done.4
  10.6 0.7 copy-done.5
  11.3 0.1 shard_map.163
  11.4 2.1 %collective-permute-start = (bf16[128,768]{1,0:T(8,128)(2,1)S(1)}, bf16[128,768]{1,0:T(8,128)(2,1)S(1)}, u32[]{:S(2)}, u32[]{:S(2)}) collective-permute-start(bf16[128,768]{1,0:T(8,128)(2,1)S(1)} %get-tuple-element.62), channel_id=1, source_target_pairs={{0,1},{1,0},{2,3},{3,2},{4,5},{5,4},{6,7},{7,6},{8,9},{9,8},{10,11... | collective-permute-start | bytes 589832 | tf_op jit(solution)/shard_map/ppermute | solution.py:340
  13.5 1.5 %collective-permute-start.2 = (bf16[128,256]{1,0:T(8,128)(2,1)S(1)}, bf16[128,256]{1,0:T(8,128)(2,1)S(1)}, u32[]{:S(2)}, u32[]{:S(2)}) collective-permute-start(bf16[128,256]{1,0:T(8,128)(2,1)S(1)} %bitcast.8), channel_id=1, source_target_pairs={{0,3},{1,2},{2,1},{3,0},{4,7},{5,6},{6,5},{7,4},{8,11},{9,10},{10,... | collective-permute-start | bytes 196616 | tf_op jit(solution)/shard_map/ppermute | solution.py:340
  14.9 0.1 collective-permute-start.1
  15.0 2.8 %collective-permute-start.7 = (bf16[128,512]{1,0:T(8,128)(2,1)S(1)}, bf16[128,512]{1,0:T(8,128)(2,1)S(1)}, u32[]{:S(2)}, u32[]{:S(2)}) collective-permute-start(bf16[128,512]{1,0:T(8,128)(2,1)S(1)} %get-tuple-element.78.refs_0_), channel_id=1, source_target_pairs={{0,3},{1,2},{2,1},{3,0},{4,7},{5,6},{6,5},{7,4},{8,11},{9,10},{10,... | collective-permute-start | bytes 393224 | tf_op jit(solution)/shard_map/ppermute | solution.py:340
  17.9 0.6 collective-permute-start.6
  18.4 4.8 %collective-permute-done.2.refs_3_ = bf16[128,256]{1,0:T(8,128)(2,1)S(1)} collective-permute-done((bf16[128,256]{1,0:T(8,128)(2,1)S(1)}, bf16[128,256]{1,0:T(8,128)(2,1)S(1)}, u32[]{:S(2)}, u32[]{:S(2)}) %collective-permute-start.2) | collective-permute-done | bytes 65568 | tf_op jit(solution)/shard_map/ppermute | solution.py:340
  23.3 0.4 collective-permute-done.1.refs_2_
  23.6 2.3 %collective-permute-done.refs_1_ = bf16[128,768]{1,0:T(8,128)(2,1)S(1)} collective-permute-done((bf16[128,768]{1,0:T(8,128)(2,1)S(1)}, bf16[128,768]{1,0:T(8,128)(2,1)S(1)}, u32[]{:S(2)}, u32[]{:S(2)}) %collective-permute-start) | collective-permute-done | bytes 196640 | tf_op jit(solution)/shard_map/ppermute | solution.py:340
  25.9 0.0 all-to-all-done
  25.9 0.8 shard_map.165
  26.7 1.8 %collective-permute-start.3 = (bf16[128,256]{1,0:T(8,128)(2,1)S(1)}, bf16[128,256]{1,0:T(8,128)(2,1)S(1)}, u32[]{:S(2)}, u32[]{:S(2)}) collective-permute-start(bf16[128,256]{1,0:T(8,128)(2,1)S(1)} %get-tuple-element.66), channel_id=1, source_target_pairs={{0,2},{1,3},{2,0},{3,1},{4,6},{5,7},{6,4},{7,5},{8,10},{9,11},{10,... | collective-permute-start | bytes 196616 | tf_op jit(solution)/shard_map/ppermute | solution.py:340
  28.5 1.1 %collective-permute-start.4 = (bf16[128,256]{1,0:T(8,128)(2,1)S(1)}, bf16[128,256]{1,0:T(8,128)(2,1)S(1)}, u32[]{:S(2)}, u32[]{:S(2)}) collective-permute-start(bf16[128,256]{1,0:T(8,128)(2,1)S(1)} %get-tuple-element.67), channel_id=1, source_target_pairs={{0,3},{1,2},{2,1},{3,0},{4,7},{5,6},{6,5},{7,4},{8,11},{9,10},{10,... | collective-permute-start | bytes 196616 | tf_op jit(solution)/shard_map/ppermute | solution.py:340
  29.7 0.6 collective-permute-start.5
  30.3 0.0 collective-permute-done.7.refs_3_
  30.3 0.5 collective-permute-done.6.refs_2_
  30.7 1.4 %collective-permute-done.3.refs_1_ = bf16[128,256]{1,0:T(8,128)(2,1)S(1)} collective-permute-done((bf16[128,256]{1,0:T(8,128)(2,1)S(1)}, bf16[128,256]{1,0:T(8,128)(2,1)S(1)}, u32[]{:S(2)}, u32[]{:S(2)}) %collective-permute-start.3) | collective-permute-done | bytes 65568 | tf_op jit(solution)/shard_map/ppermute | solution.py:340
  32.1 1.9 %collective-permute-done.4.refs_2_ = bf16[128,256]{1,0:T(8,128)(2,1)S(1)} collective-permute-done((bf16[128,256]{1,0:T(8,128)(2,1)S(1)}, bf16[128,256]{1,0:T(8,128)(2,1)S(1)}, u32[]{:S(2)}, u32[]{:S(2)}) %collective-permute-start.4) | collective-permute-done | bytes 65568 | tf_op jit(solution)/shard_map/ppermute | solution.py:340
  34.0 0.6 collective-permute-done.5.refs_3_
  34.6 0.1 shard_map.166
  34.8 0.1 collective-permute-start.10
  34.9 1.6 %collective-permute-start.9 = (f32[2,128]{1,0:T(2,128)S(1)}, f32[2,128]{1,0:T(2,128)S(1)}, u32[]{:S(2)}, u32[]{:S(2)}) collective-permute-start(f32[2,128]{1,0:T(2,128)S(1)} %get-tuple-element.76.refs_0_), channel_id=1, source_target_pairs={{0,16},{8,24},{16,0},{24,8},{1,17},{9,25},{17,1},{25,9},{2,18},{10... | collective-permute-start | bytes 3080 | tf_op jit(solution)/shard_map/ppermute | solution.py:340
  36.4 0.3 collective-permute-start.8
  36.7 1.1 %collective-permute-done.10.refs_3_ = f32[2,128]{1,0:T(2,128)S(1)} collective-permute-done((f32[2,128]{1,0:T(2,128)S(1)}, f32[2,128]{1,0:T(2,128)S(1)}, u32[]{:S(2)}, u32[]{:S(2)}) %collective-permute-start.10) | collective-permute-done | bytes 1056 | tf_op jit(solution)/shard_map/ppermute | solution.py:340
  37.8 0.7 collective-permute-done.9.refs_2_
  38.5 0.0 collective-permute-done.8.refs_1_
  38.5 0.1 shard_map.167.refs_4_
  38.6 1.2 %collective-permute-start.13 = (bf16[128,256]{1,0:T(8,128)(2,1)S(1)}, bf16[128,256]{1,0:T(8,128)(2,1)S(1)}, u32[]{:S(2)}, u32[]{:S(2)}) collective-permute-start(bf16[128,256]{1,0:T(8,128)(2,1)S(1)} %shard_map.167.refs_4_), channel_id=1, source_target_pairs={{0,3},{1,2},{2,1},{3,0},{4,7},{5,6},{6,5},{7,4},{8,11},{9,10},{10,... | collective-permute-start | bytes 196616 | tf_op jit(solution)/shard_map/ppermute | solution.py:340
  39.8 0.9 collective-permute-start.12
  40.7 1.5 %collective-permute-start.11 = (bf16[128,256]{1,0:T(8,128)(2,1)S(1)}, bf16[128,256]{1,0:T(8,128)(2,1)S(1)}, u32[]{:S(2)}, u32[]{:S(2)}) collective-permute-start(bf16[128,256]{1,0:T(8,128)(2,1)S(1)} %shard_map.167.refs_4_), channel_id=1, source_target_pairs={{0,1},{1,0},{2,3},{3,2},{4,5},{5,4},{6,7},{7,6},{8,9},{9,8},{10,11... | collective-permute-start | bytes 196616 | tf_op jit(solution)/shard_map/ppermute | solution.py:340
  42.2 0.1 pad_add_fusion.place
  42.3 2.2 %collective-permute-done.13.refs_7_ = bf16[128,256]{1,0:T(8,128)(2,1)S(1)} collective-permute-done((bf16[128,256]{1,0:T(8,128)(2,1)S(1)}, bf16[128,256]{1,0:T(8,128)(2,1)S(1)}, u32[]{:S(2)}, u32[]{:S(2)}) %collective-permute-start.13) | collective-permute-done | bytes 65568 | tf_op jit(solution)/shard_map/ppermute | solution.py:340
  44.5 0.9 %collective-permute-done.11.refs_5_ = bf16[128,256]{1,0:T(8,128)(2,1)S(1)} collective-permute-done((bf16[128,256]{1,0:T(8,128)(2,1)S(1)}, bf16[128,256]{1,0:T(8,128)(2,1)S(1)}, u32[]{:S(2)}, u32[]{:S(2)}) %collective-permute-start.11) | collective-permute-done | bytes 65568 | tf_op jit(solution)/shard_map/ppermute | solution.py:340
  45.4 2.0 %shard_map.168 = (bf16[4,128,256]{2,1,0:T(8,128)(2,1)}, f32[3,256,192]{2,1,0:T(8,128)S(1)}) custom-call(s32[3]{0:T(128)S(1)} %pad_add_fusion.place, bf16[256,576]{1,0:T(8,128)(2,1)S(1)} %get-tuple-element.63.normed_ref, bf16[128,256]{1,0:T(8,128)(2,1)S(1)} %bitcast.11, bf16[128,768]{1,0:T(8,128)(2,1)S(1)} %collective-permute-done.refs_1_, ...), custom_call_target="tpu_custom_call" | custom-call | flops 603979776 | bytes 1802252 | tf_op jit(solution)/shard_map/pallas_call | solution.py:49
  47.5 3.4 %all-to-all-start.1 = ((bf16[4,128,256]{2,1,0:T(8,128)(2,1)}), bf16[4,128,256]{2,1,0:T(8,128)(2,1)S(1)}, u32[]{:S(2)}, u32[]{:S(2)}) async-start(bf16[4,128,256]{2,1,0:T(8,128)(2,1)} %get-tuple-element.95), calls=%async_computation.1 | async-start | bytes 524288 | tf_op jit(solution)/shard_map/all_to_all | solution.py:417
  50.9 2.5 %collective-permute-start.15 = (bf16[128,256]{1,0:T(8,128)(2,1)S(1)}, bf16[128,256]{1,0:T(8,128)(2,1)S(1)}, u32[]{:S(2)}, u32[]{:S(2)}) collective-permute-start(bf16[128,256]{1,0:T(8,128)(2,1)S(1)} %bitcast.12), channel_id=1, source_target_pairs={{0,4},{1,5},{2,6},{3,7},{4,0},{5,1},{6,2},{7,3},{8,12},{9,13},{10,... | collective-permute-start | bytes 196616 | tf_op jit(solution)/shard_map/ppermute | solution.py:340
  53.4 0.5 collective-permute-start.14
  53.9 2.3 %collective-permute-done.15.right = bf16[128,256]{1,0:T(8,128)(2,1)S(1)} collective-permute-done((bf16[128,256]{1,0:T(8,128)(2,1)S(1)}, bf16[128,256]{1,0:T(8,128)(2,1)S(1)}, u32[]{:S(2)}, u32[]{:S(2)}) %collective-permute-start.15) | collective-permute-done | bytes 65568 | tf_op jit(solution)/shard_map/ppermute | solution.py:340
  56.2 3.0 %collective-permute-done.14.left = bf16[128,256]{1,0:T(8,128)(2,1)S(1)} collective-permute-done((bf16[128,256]{1,0:T(8,128)(2,1)S(1)}, bf16[128,256]{1,0:T(8,128)(2,1)S(1)}, u32[]{:S(2)}, u32[]{:S(2)}) %collective-permute-start.14) | collective-permute-done | bytes 65568 | tf_op jit(solution)/shard_map/ppermute | solution.py:340
  59.2 3.2 %collective-permute-start.18 = (bf16[128,512]{1,0:T(8,128)(2,1)S(1)}, bf16[128,512]{1,0:T(8,128)(2,1)S(1)}, u32[]{:S(2)}, u32[]{:S(2)}) collective-permute-start(bf16[128,512]{1,0:T(8,128)(2,1)S(1)} %shard_map.170.refs_4_), channel_id=1, source_target_pairs={{0,3},{1,2},{2,1},{3,0},{4,7},{5,6},{6,5},{7,4},{8,11},{9,10},{10,... | collective-permute-start | bytes 393224 | tf_op jit(solution)/shard_map/ppermute | solution.py:340
  62.4 1.7 %collective-permute-start.17 = (bf16[128,512]{1,0:T(8,128)(2,1)S(1)}, bf16[128,512]{1,0:T(8,128)(2,1)S(1)}, u32[]{:S(2)}, u32[]{:S(2)}) collective-permute-start(bf16[128,512]{1,0:T(8,128)(2,1)S(1)} %shard_map.170.refs_4_), channel_id=1, source_target_pairs={{0,2},{1,3},{2,0},{3,1},{4,6},{5,7},{6,4},{7,5},{8,10},{9,11},{10,... | collective-permute-start | bytes 393224 | tf_op jit(solution)/shard_map/ppermute | solution.py:340
  64.1 1.1 %shard_map.169 = (f32[4,512,192]{2,1,0:T(8,128)S(1)}, bf16[3,512,192]{2,1,0:T(8,128)(2,1)S(1)}, f32[3,192]{1,0:T(4,128)S(1)}, f32[3,256,192]{2,1,0:T(8,128)S(1)}, f32[3,256,192]{2,1,0:T(8,128)S(1)}) custom-call(bf16[256,1152]{1,0:T(8,128)(2,1)S(1)} %bitcast.6, bf16[128,512]{1,0:T(8,128)(2,1)S(1)} %get-tuple-element.78.refs_0_, ...), custom_call_target="tpu_custom_call" | custom-call | flops 603979776 | bytes 4524288 | tf_op jit(solution)/shard_map/pallas_call | solution.py:49
  65.2 1.2 %collective-permute-done.18.refs_7_ = bf16[128,512]{1,0:T(8,128)(2,1)S(1)} collective-permute-done((bf16[128,512]{1,0:T(8,128)(2,1)S(1)}, bf16[128,512]{1,0:T(8,128)(2,1)S(1)}, u32[]{:S(2)}, u32[]{:S(2)}) %collective-permute-start.18) | collective-permute-done | bytes 131104 | tf_op jit(solution)/shard_map/ppermute | solution.py:340
  66.4 2.0 %collective-permute-done.17.refs_6_ = bf16[128,512]{1,0:T(8,128)(2,1)S(1)} collective-permute-done((bf16[128,512]{1,0:T(8,128)(2,1)S(1)}, bf16[128,512]{1,0:T(8,128)(2,1)S(1)}, u32[]{:S(2)}, u32[]{:S(2)}) %collective-permute-start.17) | collective-permute-done | bytes 131104 | tf_op jit(solution)/shard_map/ppermute | solution.py:340
  68.4 0.6 collective-permute-done.16.refs_5_
  69.1 2.6 %shard_map.171 = (bf16[128,512]{1,0:T(8,128)(2,1)S(1)}, bf16[32,576]{1,0:T(8,128)(2,1)S(1)}, bf16[672,128]{1,0:T(8,128)(2,1)S(1)}, bf16[672,128]{1,0:T(8,128)(2,...) custom-call(s32[3]{0:T(128)S(1)} %pad_add_fusion.place, ...), custom_call_target="tpu_custom_call" | custom-call | flops 1207959552 | bytes 6764812 | tf_op jit(solution)/shard_map/pallas_call | solution.py:49
  71.6 0.0 copy-start.6
  71.6 0.6 copy-done.6
  72.2 0.8 collective-permute-start.19
  73.1 1.1 %collective-permute-start.20 = (bf16[672,128]{1,0:T(8,128)(2,1)S(1)}, bf16[672,128]{1,0:T(8,128)(2,1)S(1)}, u32[]{:S(2)}, u32[]{:S(2)}) collective-permute-start(bf16[672,128]{1,0:T(8,128)(2,1)S(1)} %get-tuple-element.99), channel_id=1, source_target_pairs={{0,2},{1,3},{2,0},{3,1},{4,6},{5,7},{6,4},{7,5},{8,10},{9,11},{10,... | collective-permute-start | bytes 516104 | tf_op jit(solution)/shard_map/ppermute | solution.py:340
  74.2 1.6 %collective-permute-start.21 = (bf16[672,128]{1,0:T(8,128)(2,1)S(1)}, bf16[672,128]{1,0:T(8,128)(2,1)S(1)}, u32[]{:S(2)}, u32[]{:S(2)}) collective-permute-start(bf16[672,128]{1,0:T(8,128)(2,1)S(1)} %get-tuple-element.100), channel_id=1, source_target_pairs={{0,3},{1,2},{2,1},{3,0},{4,7},{5,6},{6,5},{7,4},{8,11},{9,10},{10,... | collective-permute-start | bytes 516104 | tf_op jit(solution)/shard_map/ppermute | solution.py:340
  75.7 1.6 %collective-permute-start.22 = (bf16[32,576]{1,0:T(8,128)(2,1)}, bf16[32,576]{1,0:T(8,128)(2,1)S(1)}, u32[]{:S(2)}, u32[]{:S(2)}) collective-permute-start(bf16[32,576]{1,0:T(8,128)(2,1)} %copy-done.6), channel_id=1, source_target_pairs={{0,4},{1,5},{2,6},{3,7},{4,0},{5,1},{6,2},{7,3},{8,12},{9,13},{10,... | collective-permute-start | bytes 110600 | tf_op jit(solution)/shard_map/ppermute | solution.py:340
  77.4 1.6 %collective-permute-start.23 = (bf16[32,576]{1,0:T(8,128)(2,1)S(1)}, bf16[32,576]{1,0:T(8,128)(2,1)S(1)}, u32[]{:S(2)}, u32[]{:S(2)}) collective-permute-start(bf16[32,576]{1,0:T(8,128)(2,1)S(1)} %get-tuple-element.106), channel_id=1, source_target_pairs={{0,5},{1,4},{2,7},{3,6},{4,1},{5,0},{6,3},{7,2},{8,13},{9,12},{10,... | collective-permute-start | bytes 110600 | tf_op jit(solution)/shard_map/ppermute | solution.py:340
  78.9 3.4 %collective-permute-start.24 = (bf16[32,576]{1,0:T(8,128)(2,1)S(1)}, bf16[32,576]{1,0:T(8,128)(2,1)S(1)}, u32[]{:S(2)}, u32[]{:S(2)}) collective-permute-start(bf16[32,576]{1,0:T(8,128)(2,1)S(1)} %get-tuple-element.107), channel_id=1, source_target_pairs={{0,6},{1,7},{2,4},{3,5},{4,2},{5,3},{6,0},{7,1},{8,14},{9,15},{10,... | collective-permute-start | bytes 110600 | tf_op jit(solution)/shard_map/ppermute | solution.py:340
  82.4 1.8 %collective-permute-start.25 = (bf16[32,576]{1,0:T(8,128)(2,1)S(1)}, bf16[32,576]{1,0:T(8,128)(2,1)S(1)}, u32[]{:S(2)}, u32[]{:S(2)}) collective-permute-start(bf16[32,576]{1,0:T(8,128)(2,1)S(1)} %get-tuple-element.108), channel_id=1, source_target_pairs={{0,7},{1,6},{2,5},{3,4},{4,3},{5,2},{6,1},{7,0},{8,15},{9,14},{10,... | collective-permute-start | bytes 110600 | tf_op jit(solution)/shard_map/ppermute | solution.py:340
  84.2 0.7 shard_map.172
  85.0 1.9 %collective-permute-done.24.refs_5_ = bf16[32,576]{1,0:T(8,128)(2,1)S(1)} collective-permute-done((bf16[32,576]{1,0:T(8,128)(2,1)S(1)}, bf16[32,576]{1,0:T(8,128)(2,1)S(1)}, u32[]{:S(2)}, u32[]{:S(2)}) %collective-permute-start.24) | collective-permute-done | bytes 36896 | tf_op jit(solution)/shard_map/ppermute | solution.py:340
  86.9 2.2 %collective-permute-done.25.refs_6_ = bf16[32,576]{1,0:T(8,128)(2,1)S(1)} collective-permute-done((bf16[32,576]{1,0:T(8,128)(2,1)S(1)}, bf16[32,576]{1,0:T(8,128)(2,1)S(1)}, u32[]{:S(2)}, u32[]{:S(2)}) %collective-permute-start.25) | collective-permute-done | bytes 36896 | tf_op jit(solution)/shard_map/ppermute | solution.py:340
  89.1 1.4 %shard_map.173 = (f32[1,32,768]{2,1,0:T(8,128)}, f32[1,32,768]{2,1,0:T(8,128)}, f32[1,32,768]{2,1,0:T(8,128)}) custom-call(s32[3]{0:T(128)S(1)} %pad_add_fusion.place, bf16[32,576]{1,0:T(8,128)(2,1)S(1)} %get-tuple-element.104.inner, bf16[672,128]{1,0:T(8,128)(2,1)S(1)} %collective-permute-done.19.refs_0_, ...), custom_call_target="tpu_custom_call" | custom-call | bytes 995340 | tf_op jit(solution)/shard_map/pallas_call | solution.py:49
  (18 shorter events, 0.0 us)
Async XLA Ops:
  0.6 9.3 %copy-start = (bf16[1,128,256]{2,1,0:T(8,128)(2,1)S(1)}, bf16[1,128,256]{2,1,0:T(8,128)(2,1)}, u32[]{:S(2)}) copy-start(bf16[1,128,256]{2,1,0:T(8,128)(2,1)} %q.1) | copy-start | bytes 196612
  0.6 9.3 %copy-start.3 = (bf16[1,128,256]{2,1,0:T(8,128)(2,1)S(1)}, bf16[1,128,256]{2,1,0:T(8,128)(2,1)}, u32[]{:S(2)}) copy-start(bf16[1,128,256]{2,1,0:T(8,128)(2,1)} %og.1) | copy-start | bytes 196612
  0.7 9.3 %copy-start.2 = (bf16[1,128,256]{2,1,0:T(8,128)(2,1)S(1)}, bf16[1,128,256]{2,1,0:T(8,128)(2,1)}, u32[]{:S(2)}) copy-start(bf16[1,128,256]{2,1,0:T(8,128)(2,1)} %v.1) | copy-start | bytes 196612
  0.7 9.3 %copy-start.1 = (bf16[1,128,256]{2,1,0:T(8,128)(2,1)S(1)}, bf16[1,128,256]{2,1,0:T(8,128)(2,1)}, u32[]{:S(2)}) copy-start(bf16[1,128,256]{2,1,0:T(8,128)(2,1)} %k.1) | copy-start | bytes 196612
  2.6 23.3 %all-to-all-start = ((bf16[8,32,1152]{2,1,0:T(8,128)(2,1)}), bf16[8,32,1152]{2,1,0:T(8,128)(2,1)S(1)}, u32[]{:S(2)}, u32[]{:S(2)}) async-start(bf16[8,32,1152]{2,1,0:T(8,128)(2,1)} %shard_map.164), calls=%async_computation | async-start | bytes 1179648 | tf_op jit(solution)/shard_map/all_to_all | solution.py:363
  9.9 0.7 copy-start.4
  10.6 0.7 copy-start.5
  11.4 14.5 %collective-permute-start = (bf16[128,768]{1,0:T(8,128)(2,1)S(1)}, bf16[128,768]{1,0:T(8,128)(2,1)S(1)}, u32[]{:S(2)}, u32[]{:S(2)}) collective-permute-start(bf16[128,768]{1,0:T(8,128)(2,1)S(1)} %get-tuple-element.62), channel_id=1, source_target_pairs={{0,1},{1,0},{2,3},{3,2},{4,5},{5,4},{6,7},{7,6},{8,9},{9,8},{10,11... | collective-permute-start | bytes 589832 | tf_op jit(solution)/shard_map/ppermute | solution.py:340
  13.5 9.8 %collective-permute-start.2 = (bf16[128,256]{1,0:T(8,128)(2,1)S(1)}, bf16[128,256]{1,0:T(8,128)(2,1)S(1)}, u32[]{:S(2)}, u32[]{:S(2)}) collective-permute-start(bf16[128,256]{1,0:T(8,128)(2,1)S(1)} %bitcast.8), channel_id=1, source_target_pairs={{0,3},{1,2},{2,1},{3,0},{4,7},{5,6},{6,5},{7,4},{8,11},{9,10},{10,... | collective-permute-start | bytes 196616 | tf_op jit(solution)/shard_map/ppermute | solution.py:340
  14.9 8.7 %collective-permute-start.1 = (bf16[128,256]{1,0:T(8,128)(2,1)S(1)}, bf16[128,256]{1,0:T(8,128)(2,1)S(1)}, u32[]{:S(2)}, u32[]{:S(2)}) collective-permute-start(bf16[128,256]{1,0:T(8,128)(2,1)S(1)} %bitcast.9), channel_id=1, source_target_pairs={{0,2},{1,3},{2,0},{3,1},{4,6},{5,7},{6,4},{7,5},{8,10},{9,11},{10,... | collective-permute-start | bytes 196616 | tf_op jit(solution)/shard_map/ppermute | solution.py:340
  15.0 15.2 %collective-permute-start.7 = (bf16[128,512]{1,0:T(8,128)(2,1)S(1)}, bf16[128,512]{1,0:T(8,128)(2,1)S(1)}, u32[]{:S(2)}, u32[]{:S(2)}) collective-permute-start(bf16[128,512]{1,0:T(8,128)(2,1)S(1)} %get-tuple-element.78.refs_0_), channel_id=1, source_target_pairs={{0,3},{1,2},{2,1},{3,0},{4,7},{5,6},{6,5},{7,4},{8,11},{9,10},{10,... | collective-permute-start | bytes 393224 | tf_op jit(solution)/shard_map/ppermute | solution.py:340
  17.9 12.9 %collective-permute-start.6 = (bf16[128,512]{1,0:T(8,128)(2,1)S(1)}, bf16[128,512]{1,0:T(8,128)(2,1)S(1)}, u32[]{:S(2)}, u32[]{:S(2)}) collective-permute-start(bf16[128,512]{1,0:T(8,128)(2,1)S(1)} %get-tuple-element.78.refs_0_), channel_id=1, source_target_pairs={{0,2},{1,3},{2,0},{3,1},{4,6},{5,7},{6,4},{7,5},{8,10},{9,11},{10,... | collective-permute-start | bytes 393224 | tf_op jit(solution)/shard_map/ppermute | solution.py:340
  26.7 5.4 %collective-permute-start.3 = (bf16[128,256]{1,0:T(8,128)(2,1)S(1)}, bf16[128,256]{1,0:T(8,128)(2,1)S(1)}, u32[]{:S(2)}, u32[]{:S(2)}) collective-permute-start(bf16[128,256]{1,0:T(8,128)(2,1)S(1)} %get-tuple-element.66), channel_id=1, source_target_pairs={{0,2},{1,3},{2,0},{3,1},{4,6},{5,7},{6,4},{7,5},{8,10},{9,11},{10,... | collective-permute-start | bytes 196616 | tf_op jit(solution)/shard_map/ppermute | solution.py:340
  28.5 5.4 %collective-permute-start.4 = (bf16[128,256]{1,0:T(8,128)(2,1)S(1)}, bf16[128,256]{1,0:T(8,128)(2,1)S(1)}, u32[]{:S(2)}, u32[]{:S(2)}) collective-permute-start(bf16[128,256]{1,0:T(8,128)(2,1)S(1)} %get-tuple-element.67), channel_id=1, source_target_pairs={{0,3},{1,2},{2,1},{3,0},{4,7},{5,6},{6,5},{7,4},{8,11},{9,10},{10,... | collective-permute-start | bytes 196616 | tf_op jit(solution)/shard_map/ppermute | solution.py:340
  29.7 4.9 %collective-permute-start.5 = (bf16[128,256]{1,0:T(8,128)(2,1)S(1)}, bf16[128,256]{1,0:T(8,128)(2,1)S(1)}, u32[]{:S(2)}, u32[]{:S(2)}) collective-permute-start(bf16[128,256]{1,0:T(8,128)(2,1)S(1)} %get-tuple-element.68), channel_id=1, source_target_pairs={{0,1},{1,0},{2,3},{3,2},{4,5},{5,4},{6,7},{7,6},{8,9},{9,8},{10,11... | collective-permute-start | bytes 196616 | tf_op jit(solution)/shard_map/ppermute | solution.py:340
  34.8 3.1 %collective-permute-start.10 = (f32[2,128]{1,0:T(2,128)S(1)}, f32[2,128]{1,0:T(2,128)S(1)}, u32[]{:S(2)}, u32[]{:S(2)}) collective-permute-start(f32[2,128]{1,0:T(2,128)S(1)} %get-tuple-element.76.refs_0_), channel_id=1, source_target_pairs={{0,24},{8,16},{16,8},{24,0},{1,25},{9,17},{17,9},{25,1},{2,26},{10... | collective-permute-start | bytes 3080 | tf_op jit(solution)/shard_map/ppermute | solution.py:340
  34.9 3.6 %collective-permute-start.9 = (f32[2,128]{1,0:T(2,128)S(1)}, f32[2,128]{1,0:T(2,128)S(1)}, u32[]{:S(2)}, u32[]{:S(2)}) collective-permute-start(f32[2,128]{1,0:T(2,128)S(1)} %get-tuple-element.76.refs_0_), channel_id=1, source_target_pairs={{0,16},{8,24},{16,0},{24,8},{1,17},{9,25},{17,1},{25,9},{2,18},{10... | collective-permute-start | bytes 3080 | tf_op jit(solution)/shard_map/ppermute | solution.py:340
  36.4 2.1 %collective-permute-start.8 = (f32[2,128]{1,0:T(2,128)S(1)}, f32[2,128]{1,0:T(2,128)S(1)}, u32[]{:S(2)}, u32[]{:S(2)}) collective-permute-start(f32[2,128]{1,0:T(2,128)S(1)} %get-tuple-element.76.refs_0_), channel_id=1, source_target_pairs={{0,8},{8,0},{16,24},{24,16},{1,9},{9,1},{17,25},{25,17},{2,10},{10... | collective-permute-start | bytes 3080 | tf_op jit(solution)/shard_map/ppermute | solution.py:340
  38.6 5.9 %collective-permute-start.13 = (bf16[128,256]{1,0:T(8,128)(2,1)S(1)}, bf16[128,256]{1,0:T(8,128)(2,1)S(1)}, u32[]{:S(2)}, u32[]{:S(2)}) collective-permute-start(bf16[128,256]{1,0:T(8,128)(2,1)S(1)} %shard_map.167.refs_4_), channel_id=1, source_target_pairs={{0,3},{1,2},{2,1},{3,0},{4,7},{5,6},{6,5},{7,4},{8,11},{9,10},{10,... | collective-permute-start | bytes 196616 | tf_op jit(solution)/shard_map/ppermute | solution.py:340
  39.8 4.7 %collective-permute-start.12 = (bf16[128,256]{1,0:T(8,128)(2,1)S(1)}, bf16[128,256]{1,0:T(8,128)(2,1)S(1)}, u32[]{:S(2)}, u32[]{:S(2)}) collective-permute-start(bf16[128,256]{1,0:T(8,128)(2,1)S(1)} %shard_map.167.refs_4_), channel_id=1, source_target_pairs={{0,2},{1,3},{2,0},{3,1},{4,6},{5,7},{6,4},{7,5},{8,10},{9,11},{10,... | collective-permute-start | bytes 196616 | tf_op jit(solution)/shard_map/ppermute | solution.py:340
  40.7 4.8 %collective-permute-start.11 = (bf16[128,256]{1,0:T(8,128)(2,1)S(1)}, bf16[128,256]{1,0:T(8,128)(2,1)S(1)}, u32[]{:S(2)}, u32[]{:S(2)}) collective-permute-start(bf16[128,256]{1,0:T(8,128)(2,1)S(1)} %shard_map.167.refs_4_), channel_id=1, source_target_pairs={{0,1},{1,0},{2,3},{3,2},{4,5},{5,4},{6,7},{7,6},{8,9},{9,8},{10,11... | collective-permute-start | bytes 196616 | tf_op jit(solution)/shard_map/ppermute | solution.py:340
  47.5 24.8 %all-to-all-start.1 = ((bf16[4,128,256]{2,1,0:T(8,128)(2,1)}), bf16[4,128,256]{2,1,0:T(8,128)(2,1)S(1)}, u32[]{:S(2)}, u32[]{:S(2)}) async-start(bf16[4,128,256]{2,1,0:T(8,128)(2,1)} %get-tuple-element.95), calls=%async_computation.1 | async-start | bytes 524288 | tf_op jit(solution)/shard_map/all_to_all | solution.py:417
  50.9 5.3 %collective-permute-start.15 = (bf16[128,256]{1,0:T(8,128)(2,1)S(1)}, bf16[128,256]{1,0:T(8,128)(2,1)S(1)}, u32[]{:S(2)}, u32[]{:S(2)}) collective-permute-start(bf16[128,256]{1,0:T(8,128)(2,1)S(1)} %bitcast.12), channel_id=1, source_target_pairs={{0,4},{1,5},{2,6},{3,7},{4,0},{5,1},{6,2},{7,3},{8,12},{9,13},{10,... | collective-permute-start | bytes 196616 | tf_op jit(solution)/shard_map/ppermute | solution.py:340
  53.4 5.9 %collective-permute-start.14 = (bf16[128,256]{1,0:T(8,128)(2,1)S(1)}, bf16[128,256]{1,0:T(8,128)(2,1)S(1)}, u32[]{:S(2)}, u32[]{:S(2)}) collective-permute-start(bf16[128,256]{1,0:T(8,128)(2,1)S(1)} %shard_map.167.refs_4_), channel_id=1, source_target_pairs={{0,4},{1,5},{2,6},{3,7},{4,0},{5,1},{6,2},{7,3},{8,12},{9,13},{10,... | collective-permute-start | bytes 196616 | tf_op jit(solution)/shard_map/ppermute | solution.py:340
  59.2 7.2 %collective-permute-start.18 = (bf16[128,512]{1,0:T(8,128)(2,1)S(1)}, bf16[128,512]{1,0:T(8,128)(2,1)S(1)}, u32[]{:S(2)}, u32[]{:S(2)}) collective-permute-start(bf16[128,512]{1,0:T(8,128)(2,1)S(1)} %shard_map.170.refs_4_), channel_id=1, source_target_pairs={{0,3},{1,2},{2,1},{3,0},{4,7},{5,6},{6,5},{7,4},{8,11},{9,10},{10,... | collective-permute-start | bytes 393224 | tf_op jit(solution)/shard_map/ppermute | solution.py:340
  62.4 6.0 %collective-permute-start.17 = (bf16[128,512]{1,0:T(8,128)(2,1)S(1)}, bf16[128,512]{1,0:T(8,128)(2,1)S(1)}, u32[]{:S(2)}, u32[]{:S(2)}) collective-permute-start(bf16[128,512]{1,0:T(8,128)(2,1)S(1)} %shard_map.170.refs_4_), channel_id=1, source_target_pairs={{0,2},{1,3},{2,0},{3,1},{4,6},{5,7},{6,4},{7,5},{8,10},{9,11},{10,... | collective-permute-start | bytes 393224 | tf_op jit(solution)/shard_map/ppermute | solution.py:340
  64.1 5.0 %collective-permute-start.16 = (bf16[128,512]{1,0:T(8,128)(2,1)S(1)}, bf16[128,512]{1,0:T(8,128)(2,1)S(1)}, u32[]{:S(2)}, u32[]{:S(2)}) collective-permute-start(bf16[128,512]{1,0:T(8,128)(2,1)S(1)} %shard_map.170.refs_4_), channel_id=1, source_target_pairs={{0,1},{1,0},{2,3},{3,2},{4,5},{5,4},{6,7},{7,6},{8,9},{9,8},{10,11... | collective-permute-start | bytes 393224 | tf_op jit(solution)/shard_map/ppermute | solution.py:340
  71.6 0.6 copy-start.6
  72.2 6.7 %collective-permute-start.19 = (bf16[672,128]{1,0:T(8,128)(2,1)S(1)}, bf16[672,128]{1,0:T(8,128)(2,1)S(1)}, u32[]{:S(2)}, u32[]{:S(2)}) collective-permute-start(bf16[672,128]{1,0:T(8,128)(2,1)S(1)} %get-tuple-element.98), channel_id=1, source_target_pairs={{0,1},{1,0},{2,3},{3,2},{4,5},{5,4},{6,7},{7,6},{8,9},{9,8},{10,11... | collective-permute-start | bytes 516104 | tf_op jit(solution)/shard_map/ppermute | solution.py:340
  73.1 9.3 %collective-permute-start.20 = (bf16[672,128]{1,0:T(8,128)(2,1)S(1)}, bf16[672,128]{1,0:T(8,128)(2,1)S(1)}, u32[]{:S(2)}, u32[]{:S(2)}) collective-permute-start(bf16[672,128]{1,0:T(8,128)(2,1)S(1)} %get-tuple-element.99), channel_id=1, source_target_pairs={{0,2},{1,3},{2,0},{3,1},{4,6},{5,7},{6,4},{7,5},{8,10},{9,11},{10,... | collective-permute-start | bytes 516104 | tf_op jit(solution)/shard_map/ppermute | solution.py:340
  74.2 10.0 %collective-permute-start.21 = (bf16[672,128]{1,0:T(8,128)(2,1)S(1)}, bf16[672,128]{1,0:T(8,128)(2,1)S(1)}, u32[]{:S(2)}, u32[]{:S(2)}) collective-permute-start(bf16[672,128]{1,0:T(8,128)(2,1)S(1)} %get-tuple-element.100), channel_id=1, source_target_pairs={{0,3},{1,2},{2,1},{3,0},{4,7},{5,6},{6,5},{7,4},{8,11},{9,10},{10,... | collective-permute-start | bytes 516104 | tf_op jit(solution)/shard_map/ppermute | solution.py:340
  75.7 9.2 %collective-permute-start.22 = (bf16[32,576]{1,0:T(8,128)(2,1)}, bf16[32,576]{1,0:T(8,128)(2,1)S(1)}, u32[]{:S(2)}, u32[]{:S(2)}) collective-permute-start(bf16[32,576]{1,0:T(8,128)(2,1)} %copy-done.6), channel_id=1, source_target_pairs={{0,4},{1,5},{2,6},{3,7},{4,0},{5,1},{6,2},{7,3},{8,12},{9,13},{10,... | collective-permute-start | bytes 110600 | tf_op jit(solution)/shard_map/ppermute | solution.py:340
  77.4 7.6 %collective-permute-start.23 = (bf16[32,576]{1,0:T(8,128)(2,1)S(1)}, bf16[32,576]{1,0:T(8,128)(2,1)S(1)}, u32[]{:S(2)}, u32[]{:S(2)}) collective-permute-start(bf16[32,576]{1,0:T(8,128)(2,1)S(1)} %get-tuple-element.106), channel_id=1, source_target_pairs={{0,5},{1,4},{2,7},{3,6},{4,1},{5,0},{6,3},{7,2},{8,13},{9,12},{10,... | collective-permute-start | bytes 110600 | tf_op jit(solution)/shard_map/ppermute | solution.py:340
  78.9 7.9 %collective-permute-start.24 = (bf16[32,576]{1,0:T(8,128)(2,1)S(1)}, bf16[32,576]{1,0:T(8,128)(2,1)S(1)}, u32[]{:S(2)}, u32[]{:S(2)}) collective-permute-start(bf16[32,576]{1,0:T(8,128)(2,1)S(1)} %get-tuple-element.107), channel_id=1, source_target_pairs={{0,6},{1,7},{2,4},{3,5},{4,2},{5,3},{6,0},{7,1},{8,14},{9,15},{10,... | collective-permute-start | bytes 110600 | tf_op jit(solution)/shard_map/ppermute | solution.py:340
  82.4 6.7 %collective-permute-start.25 = (bf16[32,576]{1,0:T(8,128)(2,1)S(1)}, bf16[32,576]{1,0:T(8,128)(2,1)S(1)}, u32[]{:S(2)}, u32[]{:S(2)}) collective-permute-start(bf16[32,576]{1,0:T(8,128)(2,1)S(1)} %get-tuple-element.108), channel_id=1, source_target_pairs={{0,7},{1,6},{2,5},{3,4},{4,3},{5,2},{6,1},{7,0},{8,15},{9,14},{10,... | collective-permute-start | bytes 110600 | tf_op jit(solution)/shard_map/ppermute | solution.py:340

commit v11 on v10

--- a/solution.py
+++ b/solution.py
@@ -400,6 +400,7 @@
             24,
             flops=12 * mflop,
         )
+        *od_mirror, stats[0] = lax.optimization_barrier((*od_mirror, stats[0]))
         pairs = [
             call(pair_kernel, (arr((own, 2 * feat), BF),), pair, 16)[0] for pair in zip(od_mirror, q_mirror)
         ]
@@ -410,7 +411,7 @@
             (place, normed, *q_near, *od_near),
             24,
             smem=1,
-            flops=12 * mflop,
+            flops=300 * mflop,
         )
 
         q_block = (own, feat)
@@ -426,7 +427,7 @@
             (place, wall, normed, grads, factors, rises, *stats, *kv_near, *pairs),
             40,
             smem=1,
-            flops=24 * mflop,
+            flops=600 * mflop,
             scratch=[
                 pltpu.VMEM((seq_n, rows, 3 * slab), F32),
                 pltpu.VMEM((3, seq_n * rows, slab), F32),

time: 90.8 us -> 84.6 us (0.932)
  waiting for transfers between devices: 30.1 us -> 15 us
  local copies, waits for them, and re-layouts: 1.96 us -> 9.71 us
    ppermute x26, waiting for transfers between devices: 30.1 us -> 15 us  [move(): return lax.ppermute(x, axis, [(i, i ^ dist) for i in range(size)])]
    unnamed x14 -> x32, local copies, waits for them, and re-layouts: 1.96 us -> 9.71 us
    ppermute x26, starting transfers between devices: 35.8 us -> 36.8 us  [move(): return lax.ppermute(x, axis, [(i, i ^ dist) for i in range(size)])]
  transfers between devices with their start and end apart: 28 -> 28, of which waited for: 18 -> 8; matrix products, arithmetic and copies ran while one was open for 0% -> 0% of each run, Pallas kernels for 6% -> 9%
where the time goes in v11:
time: 84.6 us; the launch traced here: 84 us
  starting transfers between devices  47.4 us (56%)
  waiting for transfers between devices  15 us (18%)
  Pallas kernels  11 us (13%)
  local copies, waits for them, and re-layouts  9.71 us (11%)
  between operations  0.89 us (1%)
    ppermute x26, starting transfers between devices, move(): return lax.ppermute(x, axis, [(i, i ^ dist) for i in range(size)])  36.8 us
    ppermute x26, waiting for transfers between devices, move(): return lax.ppermute(x, axis, [(i, i ^ dist) for i in range(size)])  15 us
    unnamed x32, local copies, waits for them, and re-layouts  9.71 us
    pallas_call x10, Pallas kernels, call(): pl.pallas_call(kernel, out_shape=outs, in_specs=[SMEM] * smem + [VMEM] *...  9.01 us
    all_to_all x1, starting transfers between devices, local(): lax.all_to_all(packed, 'seq', 0, 0, tiled=True)  7.26 us
    all_to_all x1, starting transfers between devices, local(): lax.all_to_all(grad_q, 'seq', 0, 0, axis_index_groups=groups, tiled=True)  3.4 us
    pallas_call x1, Pallas kernels, copying_call(): pl.pallas_call(kernel, out_shape=outs, in_specs=[pl.BlockSpec(memory_spac...  1.96 us
  transfers between devices with their start and end apart: 28, of which 8 were waited for; matrix products, arithmetic and copies ran while one was open for 0% of the time, Pallas kernels for 9%

profile of v11, /device:TPU:0, one launch (start us, length us, event | category | flops | bytes accessed | tf_op | source)
XLA Modules:
  0.0 84.0 jit_solution(16411884472323127565)
XLA Ops:
  0.7 2.0 %shard_map.164 = bf16[8,32,1152]{2,1,0:T(8,128)(2,1)} custom-call(bf16[1,32,768]{2,1,0:T(8,128)(2,1)} %refs_0_.1, bf16[1,32,768]{2,1,0:T(8,128)(2,1)} %refs_1_.1, bf16[1,32,768]{2,1,0:T(8,128)(2,1)} %refs_2_.1, bf16[1,32,768]{2,1,0:T(8,128)(2,1)} %refs_3_.1, bf16[1,32,768]{2,1,0:T(8,128)(2,1)} %refs_4_.1, bf16[1,32,768]{2,1,0:T(8,128)(2,1)} %refs_5_.1), custom_call_target="tpu_custom_call" | custom-call | tf_op jit(solution)/shard_map/pallas_call | solution.py:61
  2.6 7.3 %all-to-all-start = ((bf16[8,32,1152]{2,1,0:T(8,128)(2,1)}), bf16[8,32,1152]{2,1,0:T(8,128)(2,1)S(1)}, u32[]{:S(2)}, u32[]{:S(2)}) async-start(bf16[8,32,1152]{2,1,0:T(8,128)(2,1)} %shard_map.164), calls=%async_computation | async-start | bytes 1179648 | tf_op jit(solution)/shard_map/all_to_all | solution.py:363
  9.9 0.0 copy-start.4
  10.0 0.7 copy-done.4
  10.6 0.7 copy-done.5
  11.3 0.1 shard_map.163
  11.4 2.1 %collective-permute-start = (bf16[128,768]{1,0:T(8,128)(2,1)S(1)}, bf16[128,768]{1,0:T(8,128)(2,1)S(1)}, u32[]{:S(2)}, u32[]{:S(2)}) collective-permute-start(bf16[128,768]{1,0:T(8,128)(2,1)S(1)} %get-tuple-element.64), channel_id=1, source_target_pairs={{0,1},{1,0},{2,3},{3,2},{4,5},{5,4},{6,7},{7,6},{8,9},{9,8},{10,11... | collective-permute-start | bytes 589832 | tf_op jit(solution)/shard_map/ppermute | solution.py:340
  13.5 1.5 %collective-permute-start.2 = (bf16[128,256]{1,0:T(8,128)(2,1)S(1)}, bf16[128,256]{1,0:T(8,128)(2,1)S(1)}, u32[]{:S(2)}, u32[]{:S(2)}) collective-permute-start(bf16[128,256]{1,0:T(8,128)(2,1)S(1)} %bitcast.8), channel_id=1, source_target_pairs={{0,3},{1,2},{2,1},{3,0},{4,7},{5,6},{6,5},{7,4},{8,11},{9,10},{10,... | collective-permute-start | bytes 196616 | tf_op jit(solution)/shard_map/ppermute | solution.py:340
  14.9 0.1 collective-permute-start.1
  15.0 2.8 %collective-permute-start.7 = (bf16[128,512]{1,0:T(8,128)(2,1)S(1)}, bf16[128,512]{1,0:T(8,128)(2,1)S(1)}, u32[]{:S(2)}, u32[]{:S(2)}) collective-permute-start(bf16[128,512]{1,0:T(8,128)(2,1)S(1)} %get-tuple-element.80.refs_0_), channel_id=1, source_target_pairs={{0,3},{1,2},{2,1},{3,0},{4,7},{5,6},{6,5},{7,4},{8,11},{9,10},{10,... | collective-permute-start | bytes 393224 | tf_op jit(solution)/shard_map/ppermute | solution.py:340
  17.9 0.6 collective-permute-start.6
  18.4 4.8 %collective-permute-done.2.refs_3_ = bf16[128,256]{1,0:T(8,128)(2,1)S(1)} collective-permute-done((bf16[128,256]{1,0:T(8,128)(2,1)S(1)}, bf16[128,256]{1,0:T(8,128)(2,1)S(1)}, u32[]{:S(2)}, u32[]{:S(2)}) %collective-permute-start.2) | collective-permute-done | bytes 65568 | tf_op jit(solution)/shard_map/ppermute | solution.py:340
  23.3 0.4 collective-permute-done.1.refs_2_
  23.6 2.3 %collective-permute-done.refs_1_ = bf16[128,768]{1,0:T(8,128)(2,1)S(1)} collective-permute-done((bf16[128,768]{1,0:T(8,128)(2,1)S(1)}, bf16[128,768]{1,0:T(8,128)(2,1)S(1)}, u32[]{:S(2)}, u32[]{:S(2)}) %collective-permute-start) | collective-permute-done | bytes 196640 | tf_op jit(solution)/shard_map/ppermute | solution.py:340
  25.9 0.0 all-to-all-done
  25.9 0.8 shard_map.165
  26.7 1.8 %collective-permute-start.3 = (bf16[128,256]{1,0:T(8,128)(2,1)S(1)}, bf16[128,256]{1,0:T(8,128)(2,1)S(1)}, u32[]{:S(2)}, u32[]{:S(2)}) collective-permute-start(bf16[128,256]{1,0:T(8,128)(2,1)S(1)} %get-tuple-element.68), channel_id=1, source_target_pairs={{0,2},{1,3},{2,0},{3,1},{4,6},{5,7},{6,4},{7,5},{8,10},{9,11},{10,... | collective-permute-start | bytes 196616 | tf_op jit(solution)/shard_map/ppermute | solution.py:340
  28.5 1.1 %collective-permute-start.4 = (bf16[128,256]{1,0:T(8,128)(2,1)S(1)}, bf16[128,256]{1,0:T(8,128)(2,1)S(1)}, u32[]{:S(2)}, u32[]{:S(2)}) collective-permute-start(bf16[128,256]{1,0:T(8,128)(2,1)S(1)} %get-tuple-element.69), channel_id=1, source_target_pairs={{0,3},{1,2},{2,1},{3,0},{4,7},{5,6},{6,5},{7,4},{8,11},{9,10},{10,... | collective-permute-start | bytes 196616 | tf_op jit(solution)/shard_map/ppermute | solution.py:340
  29.7 0.6 collective-permute-start.5
  30.3 0.0 collective-permute-done.7.refs_3_
  30.3 0.5 collective-permute-done.6.refs_2_
  30.7 1.4 %collective-permute-done.3.refs_1_ = bf16[128,256]{1,0:T(8,128)(2,1)S(1)} collective-permute-done((bf16[128,256]{1,0:T(8,128)(2,1)S(1)}, bf16[128,256]{1,0:T(8,128)(2,1)S(1)}, u32[]{:S(2)}, u32[]{:S(2)}) %collective-permute-start.3) | collective-permute-done | bytes 65568 | tf_op jit(solution)/shard_map/ppermute | solution.py:340
  32.1 1.9 %collective-permute-done.4.refs_2_ = bf16[128,256]{1,0:T(8,128)(2,1)S(1)} collective-permute-done((bf16[128,256]{1,0:T(8,128)(2,1)S(1)}, bf16[128,256]{1,0:T(8,128)(2,1)S(1)}, u32[]{:S(2)}, u32[]{:S(2)}) %collective-permute-start.4) | collective-permute-done | bytes 65568 | tf_op jit(solution)/shard_map/ppermute | solution.py:340
  34.0 0.6 collective-permute-done.5.refs_3_
  34.6 0.1 shard_map.166
  34.8 0.1 collective-permute-start.10
  34.9 1.6 %collective-permute-start.9 = (f32[2,128]{1,0:T(2,128)S(1)}, f32[2,128]{1,0:T(2,128)S(1)}, u32[]{:S(2)}, u32[]{:S(2)}) collective-permute-start(f32[2,128]{1,0:T(2,128)S(1)} %get-tuple-element.78.refs_0_), channel_id=1, source_target_pairs={{0,16},{8,24},{16,0},{24,8},{1,17},{9,25},{17,1},{25,9},{2,18},{10... | collective-permute-start | bytes 3080 | tf_op jit(solution)/shard_map/ppermute | solution.py:340
  36.4 0.3 collective-permute-start.8
  36.7 2.4 %collective-permute-start.15 = (bf16[128,256]{1,0:T(8,128)(2,1)S(1)}, bf16[128,256]{1,0:T(8,128)(2,1)S(1)}, u32[]{:S(2)}, u32[]{:S(2)}) collective-permute-start(bf16[128,256]{1,0:T(8,128)(2,1)S(1)} %bitcast.11), channel_id=1, source_target_pairs={{0,4},{1,5},{2,6},{3,7},{4,0},{5,1},{6,2},{7,3},{8,12},{9,13},{10,... | collective-permute-start | bytes 196616 | tf_op jit(solution)/shard_map/ppermute | solution.py:340
  39.1 0.0 collective-permute-done.10.refs_3_
  39.1 0.0 collective-permute-done.9.refs_2_
  39.1 0.0 collective-permute-done.8.refs_1_
  39.1 0.1 shard_map.167.refs_4_
  39.3 1.8 %collective-permute-start.14 = (bf16[128,256]{1,0:T(8,128)(2,1)S(1)}, bf16[128,256]{1,0:T(8,128)(2,1)S(1)}, u32[]{:S(2)}, u32[]{:S(2)}) collective-permute-start(bf16[128,256]{1,0:T(8,128)(2,1)S(1)} %shard_map.167.refs_4_), channel_id=1, source_target_pairs={{0,4},{1,5},{2,6},{3,7},{4,0},{5,1},{6,2},{7,3},{8,12},{9,13},{10,... | collective-permute-start | bytes 196616 | tf_op jit(solution)/shard_map/ppermute | solution.py:340
  41.1 1.1 %collective-permute-start.13 = (bf16[128,256]{1,0:T(8,128)(2,1)S(1)}, bf16[128,256]{1,0:T(8,128)(2,1)S(1)}, u32[]{:S(2)}, u32[]{:S(2)}) collective-permute-start(bf16[128,256]{1,0:T(8,128)(2,1)S(1)} %shard_map.167.refs_4_), channel_id=1, source_target_pairs={{0,3},{1,2},{2,1},{3,0},{4,7},{5,6},{6,5},{7,4},{8,11},{9,10},{10,... | collective-permute-start | bytes 196616 | tf_op jit(solution)/shard_map/ppermute | solution.py:340
  42.2 0.9 %collective-permute-start.12 = (bf16[128,256]{1,0:T(8,128)(2,1)S(1)}, bf16[128,256]{1,0:T(8,128)(2,1)S(1)}, u32[]{:S(2)}, u32[]{:S(2)}) collective-permute-start(bf16[128,256]{1,0:T(8,128)(2,1)S(1)} %shard_map.167.refs_4_), channel_id=1, source_target_pairs={{0,2},{1,3},{2,0},{3,1},{4,6},{5,7},{6,4},{7,5},{8,10},{9,11},{10,... | collective-permute-start | bytes 196616 | tf_op jit(solution)/shard_map/ppermute | solution.py:340
  43.1 1.5 %collective-permute-start.11 = (bf16[128,256]{1,0:T(8,128)(2,1)S(1)}, bf16[128,256]{1,0:T(8,128)(2,1)S(1)}, u32[]{:S(2)}, u32[]{:S(2)}) collective-permute-start(bf16[128,256]{1,0:T(8,128)(2,1)S(1)} %shard_map.167.refs_4_), channel_id=1, source_target_pairs={{0,1},{1,0},{2,3},{3,2},{4,5},{5,4},{6,7},{7,6},{8,9},{9,8},{10,11... | collective-permute-start | bytes 196616 | tf_op jit(solution)/shard_map/ppermute | solution.py:340
  44.6 0.1 pad_add_fusion.place
  44.7 1.1 %shard_map.169 = (f32[4,512,192]{2,1,0:T(8,128)S(1)}, bf16[3,512,192]{2,1,0:T(8,128)(2,1)S(1)}, f32[3,192]{1,0:T(4,128)S(1)}, f32[3,256,192]{2,1,0:T(8,128)S(1)}, f32[3,256,192]{2,1,0:T(8,128)S(1)}) custom-call(bf16[256,1152]{1,0:T(8,128)(2,1)S(1)} %bitcast.6, bf16[128,512]{1,0:T(8,128)(2,1)S(1)} %get-tuple-element.80.refs_0_, ...), custom_call_target="tpu_custom_call" | custom-call | flops 603979776 | bytes 4524288 | tf_op jit(solution)/shard_map/pallas_call | solution.py:49
  45.8 1.3 %copy-done.6 = f32[4,512,192]{2,1,0:T(8,128)} copy-done((f32[4,512,192]{2,1,0:T(8,128)}, f32[4,512,192]{2,1,0:T(8,128)S(1)}, u32[]{:S(2)}) %copy-start.6) | copy-done | bytes 1572888
  47.1 0.0 collective-permute-done.15.right
  47.2 1.2 %collective-permute-start.18 = (bf16[128,512]{1,0:T(8,128)(2,1)S(1)}, bf16[128,512]{1,0:T(8,128)(2,1)S(1)}, u32[]{:S(2)}, u32[]{:S(2)}) collective-permute-start(bf16[128,512]{1,0:T(8,128)(2,1)S(1)} %shard_map.170.refs_4_), channel_id=1, source_target_pairs={{0,3},{1,2},{2,1},{3,0},{4,7},{5,6},{6,5},{7,4},{8,11},{9,10},{10,... | collective-permute-start | bytes 393224 | tf_op jit(solution)/shard_map/ppermute | solution.py:340
  48.3 0.9 %collective-permute-start.17 = (bf16[128,512]{1,0:T(8,128)(2,1)S(1)}, bf16[128,512]{1,0:T(8,128)(2,1)S(1)}, u32[]{:S(2)}, u32[]{:S(2)}) collective-permute-start(bf16[128,512]{1,0:T(8,128)(2,1)S(1)} %shard_map.170.refs_4_), channel_id=1, source_target_pairs={{0,2},{1,3},{2,0},{3,1},{4,6},{5,7},{6,4},{7,5},{8,10},{9,11},{10,... | collective-permute-start | bytes 393224 | tf_op jit(solution)/shard_map/ppermute | solution.py:340
  49.2 0.0 collective-permute-done.13.refs_7_
  49.2 1.5 %collective-permute-start.16 = (bf16[128,512]{1,0:T(8,128)(2,1)S(1)}, bf16[128,512]{1,0:T(8,128)(2,1)S(1)}, u32[]{:S(2)}, u32[]{:S(2)}) collective-permute-start(bf16[128,512]{1,0:T(8,128)(2,1)S(1)} %shard_map.170.refs_4_), channel_id=1, source_target_pairs={{0,1},{1,0},{2,3},{3,2},{4,5},{5,4},{6,7},{7,6},{8,9},{9,8},{10,11... | collective-permute-start | bytes 393224 | tf_op jit(solution)/shard_map/ppermute | solution.py:340
  50.7 2.0 %shard_map.168 = (bf16[4,128,256]{2,1,0:T(8,128)(2,1)}, f32[3,256,192]{2,1,0:T(8,128)S(1)}) custom-call(s32[3]{0:T(128)S(1)} %pad_add_fusion.place, bf16[256,576]{1,0:T(8,128)(2,1)S(1)} %get-tuple-element.65.normed_ref, bf16[128,256]{1,0:T(8,128)(2,1)S(1)} %bitcast.12, bf16[128,768]{1,0:T(8,128)(2,1)S(1)} %collective-permute-done.refs_1_, ...), custom_call_target="tpu_custom_call" | custom-call | flops 15099494400 | bytes 1802252 | tf_op jit(solution)/shard_map/pallas_call | solution.py:49
  52.8 0.9 %copy-done.14 = f32[3,256,192]{2,1,0:T(8,128)} copy-done((f32[3,256,192]{2,1,0:T(8,128)}, f32[3,256,192]{2,1,0:T(8,128)S(1)}, u32[]{:S(2)}) %copy-start.14) | copy-done | bytes 589848
  53.7 3.4 %all-to-all-start.1 = ((bf16[4,128,256]{2,1,0:T(8,128)(2,1)}), bf16[4,128,256]{2,1,0:T(8,128)(2,1)S(1)}, u32[]{:S(2)}, u32[]{:S(2)}) async-start(bf16[4,128,256]{2,1,0:T(8,128)(2,1)} %get-tuple-element.99), calls=%async_computation.1 | async-start | bytes 524288 | tf_op jit(solution)/shard_map/all_to_all | solution.py:418
  57.2 1.6 %copy-done.7 = f32[4,512,192]{2,1,0:T(8,128)S(1)} copy-done((f32[4,512,192]{2,1,0:T(8,128)S(1)}, f32[4,512,192]{2,1,0:T(8,128)}, u32[]{:S(2)}) %copy-start.7) | copy-done | bytes 1572888
  58.8 1.1 %copy-done.9 = bf16[3,512,192]{2,1,0:T(8,128)(2,1)S(1)} copy-done((bf16[3,512,192]{2,1,0:T(8,128)(2,1)S(1)}, bf16[3,512,192]{2,1,0:T(8,128)(2,1)}, u32[]{:S(2)}) %copy-start.9) | copy-done | bytes 589848
  59.9 1.1 %copy-done.11 = f32[3,256,192]{2,1,0:T(8,128)S(1)} copy-done((f32[3,256,192]{2,1,0:T(8,128)S(1)}, f32[3,256,192]{2,1,0:T(8,128)}, u32[]{:S(2)}) %copy-start.11) | copy-done | bytes 589848
  61.0 1.1 %copy-done.13 = f32[3,256,192]{2,1,0:T(8,128)S(1)} copy-done((f32[3,256,192]{2,1,0:T(8,128)S(1)}, f32[3,256,192]{2,1,0:T(8,128)}, u32[]{:S(2)}) %copy-start.13) | copy-done | bytes 589848
  62.2 1.1 %copy-done.15 = f32[3,256,192]{2,1,0:T(8,128)S(1)} copy-done((f32[3,256,192]{2,1,0:T(8,128)S(1)}, f32[3,256,192]{2,1,0:T(8,128)}, u32[]{:S(2)}) %copy-start.15) | copy-done | bytes 589848
  63.3 2.5 %shard_map.171 = (bf16[128,512]{1,0:T(8,128)(2,1)S(1)}, bf16[32,576]{1,0:T(8,128)(2,1)S(1)}, bf16[672,128]{1,0:T(8,128)(2,1)S(1)}, bf16[672,128]{1,0:T(8,128)(2,...) custom-call(s32[3]{0:T(128)S(1)} %pad_add_fusion.place, ...), custom_call_target="tpu_custom_call" | custom-call | flops 30198988800 | bytes 6764812 | tf_op jit(solution)/shard_map/pallas_call | solution.py:49
  65.9 2.0 %collective-permute-start.19 = (bf16[672,128]{1,0:T(8,128)(2,1)S(1)}, bf16[672,128]{1,0:T(8,128)(2,1)S(1)}, u32[]{:S(2)}, u32[]{:S(2)}) collective-permute-start(bf16[672,128]{1,0:T(8,128)(2,1)S(1)} %get-tuple-element.102), channel_id=1, source_target_pairs={{0,1},{1,0},{2,3},{3,2},{4,5},{5,4},{6,7},{7,6},{8,9},{9,8},{10,11... | collective-permute-start | bytes 516104 | tf_op jit(solution)/shard_map/ppermute | solution.py:340
  67.9 1.5 %collective-permute-start.20 = (bf16[672,128]{1,0:T(8,128)(2,1)S(1)}, bf16[672,128]{1,0:T(8,128)(2,1)S(1)}, u32[]{:S(2)}, u32[]{:S(2)}) collective-permute-start(bf16[672,128]{1,0:T(8,128)(2,1)S(1)} %get-tuple-element.103), channel_id=1, source_target_pairs={{0,2},{1,3},{2,0},{3,1},{4,6},{5,7},{6,4},{7,5},{8,10},{9,11},{10,... | collective-permute-start | bytes 516104 | tf_op jit(solution)/shard_map/ppermute | solution.py:340
  69.4 0.1 collective-permute-start.21
  69.4 1.1 %collective-permute-start.22 = (bf16[32,576]{1,0:T(8,128)(2,1)S(1)}, bf16[32,576]{1,0:T(8,128)(2,1)S(1)}, u32[]{:S(2)}, u32[]{:S(2)}) collective-permute-start(bf16[32,576]{1,0:T(8,128)(2,1)S(1)} %get-tuple-element.109), channel_id=1, source_target_pairs={{0,4},{1,5},{2,6},{3,7},{4,0},{5,1},{6,2},{7,3},{8,12},{9,13},{10,... | collective-permute-start | bytes 110600 | tf_op jit(solution)/shard_map/ppermute | solution.py:340
  70.6 3.2 %collective-permute-start.23 = (bf16[32,576]{1,0:T(8,128)(2,1)S(1)}, bf16[32,576]{1,0:T(8,128)(2,1)S(1)}, u32[]{:S(2)}, u32[]{:S(2)}) collective-permute-start(bf16[32,576]{1,0:T(8,128)(2,1)S(1)} %get-tuple-element.110), channel_id=1, source_target_pairs={{0,5},{1,4},{2,7},{3,6},{4,1},{5,0},{6,3},{7,2},{8,13},{9,12},{10,... | collective-permute-start | bytes 110600 | tf_op jit(solution)/shard_map/ppermute | solution.py:340
  73.7 2.2 %collective-permute-start.24 = (bf16[32,576]{1,0:T(8,128)(2,1)S(1)}, bf16[32,576]{1,0:T(8,128)(2,1)S(1)}, u32[]{:S(2)}, u32[]{:S(2)}) collective-permute-start(bf16[32,576]{1,0:T(8,128)(2,1)S(1)} %get-tuple-element.111), channel_id=1, source_target_pairs={{0,6},{1,7},{2,4},{3,5},{4,2},{5,3},{6,0},{7,1},{8,14},{9,15},{10,... | collective-permute-start | bytes 110600 | tf_op jit(solution)/shard_map/ppermute | solution.py:340
  76.0 2.9 %collective-permute-start.25 = (bf16[32,576]{1,0:T(8,128)(2,1)S(1)}, bf16[32,576]{1,0:T(8,128)(2,1)S(1)}, u32[]{:S(2)}, u32[]{:S(2)}) collective-permute-start(bf16[32,576]{1,0:T(8,128)(2,1)S(1)} %get-tuple-element.112), channel_id=1, source_target_pairs={{0,7},{1,6},{2,5},{3,4},{4,3},{5,2},{6,1},{7,0},{8,15},{9,14},{10,... | collective-permute-start | bytes 110600 | tf_op jit(solution)/shard_map/ppermute | solution.py:340
  78.8 0.7 shard_map.172
  79.6 3.0 %collective-permute-done.25.refs_6_ = bf16[32,576]{1,0:T(8,128)(2,1)S(1)} collective-permute-done((bf16[32,576]{1,0:T(8,128)(2,1)S(1)}, bf16[32,576]{1,0:T(8,128)(2,1)S(1)}, u32[]{:S(2)}, u32[]{:S(2)}) %collective-permute-start.25) | collective-permute-done | bytes 36896 | tf_op jit(solution)/shard_map/ppermute | solution.py:340
  82.7 1.4 %shard_map.173 = (f32[1,32,768]{2,1,0:T(8,128)}, f32[1,32,768]{2,1,0:T(8,128)}, f32[1,32,768]{2,1,0:T(8,128)}) custom-call(s32[3]{0:T(128)S(1)} %pad_add_fusion.place, bf16[32,576]{1,0:T(8,128)(2,1)S(1)} %get-tuple-element.108.inner, bf16[672,128]{1,0:T(8,128)(2,1)S(1)} %collective-permute-done.19.refs_0_, ...), custom_call_target="tpu_custom_call" | custom-call | bytes 995340 | tf_op jit(solution)/shard_map/pallas_call | solution.py:49
  (36 shorter events, 0.1 us)
Async XLA Ops:
  0.6 9.3 %copy-start = (bf16[1,128,256]{2,1,0:T(8,128)(2,1)S(1)}, bf16[1,128,256]{2,1,0:T(8,128)(2,1)}, u32[]{:S(2)}) copy-start(bf16[1,128,256]{2,1,0:T(8,128)(2,1)} %q.1) | copy-start | bytes 196612
  0.6 9.3 %copy-start.3 = (bf16[1,128,256]{2,1,0:T(8,128)(2,1)S(1)}, bf16[1,128,256]{2,1,0:T(8,128)(2,1)}, u32[]{:S(2)}) copy-start(bf16[1,128,256]{2,1,0:T(8,128)(2,1)} %og.1) | copy-start | bytes 196612
  0.7 9.3 %copy-start.2 = (bf16[1,128,256]{2,1,0:T(8,128)(2,1)S(1)}, bf16[1,128,256]{2,1,0:T(8,128)(2,1)}, u32[]{:S(2)}) copy-start(bf16[1,128,256]{2,1,0:T(8,128)(2,1)} %v.1) | copy-start | bytes 196612
  0.7 9.3 %copy-start.1 = (bf16[1,128,256]{2,1,0:T(8,128)(2,1)S(1)}, bf16[1,128,256]{2,1,0:T(8,128)(2,1)}, u32[]{:S(2)}) copy-start(bf16[1,128,256]{2,1,0:T(8,128)(2,1)} %k.1) | copy-start | bytes 196612
  2.6 23.3 %all-to-all-start = ((bf16[8,32,1152]{2,1,0:T(8,128)(2,1)}), bf16[8,32,1152]{2,1,0:T(8,128)(2,1)S(1)}, u32[]{:S(2)}, u32[]{:S(2)}) async-start(bf16[8,32,1152]{2,1,0:T(8,128)(2,1)} %shard_map.164), calls=%async_computation | async-start | bytes 1179648 | tf_op jit(solution)/shard_map/all_to_all | solution.py:363
  9.9 0.7 copy-start.4
  10.6 0.7 copy-start.5
  11.4 14.5 %collective-permute-start = (bf16[128,768]{1,0:T(8,128)(2,1)S(1)}, bf16[128,768]{1,0:T(8,128)(2,1)S(1)}, u32[]{:S(2)}, u32[]{:S(2)}) collective-permute-start(bf16[128,768]{1,0:T(8,128)(2,1)S(1)} %get-tuple-element.64), channel_id=1, source_target_pairs={{0,1},{1,0},{2,3},{3,2},{4,5},{5,4},{6,7},{7,6},{8,9},{9,8},{10,11... | collective-permute-start | bytes 589832 | tf_op jit(solution)/shard_map/ppermute | solution.py:340
  13.5 9.8 %collective-permute-start.2 = (bf16[128,256]{1,0:T(8,128)(2,1)S(1)}, bf16[128,256]{1,0:T(8,128)(2,1)S(1)}, u32[]{:S(2)}, u32[]{:S(2)}) collective-permute-start(bf16[128,256]{1,0:T(8,128)(2,1)S(1)} %bitcast.8), channel_id=1, source_target_pairs={{0,3},{1,2},{2,1},{3,0},{4,7},{5,6},{6,5},{7,4},{8,11},{9,10},{10,... | collective-permute-start | bytes 196616 | tf_op jit(solution)/shard_map/ppermute | solution.py:340
  14.9 8.7 %collective-permute-start.1 = (bf16[128,256]{1,0:T(8,128)(2,1)S(1)}, bf16[128,256]{1,0:T(8,128)(2,1)S(1)}, u32[]{:S(2)}, u32[]{:S(2)}) collective-permute-start(bf16[128,256]{1,0:T(8,128)(2,1)S(1)} %bitcast.9), channel_id=1, source_target_pairs={{0,2},{1,3},{2,0},{3,1},{4,6},{5,7},{6,4},{7,5},{8,10},{9,11},{10,... | collective-permute-start | bytes 196616 | tf_op jit(solution)/shard_map/ppermute | solution.py:340
  15.0 15.2 %collective-permute-start.7 = (bf16[128,512]{1,0:T(8,128)(2,1)S(1)}, bf16[128,512]{1,0:T(8,128)(2,1)S(1)}, u32[]{:S(2)}, u32[]{:S(2)}) collective-permute-start(bf16[128,512]{1,0:T(8,128)(2,1)S(1)} %get-tuple-element.80.refs_0_), channel_id=1, source_target_pairs={{0,3},{1,2},{2,1},{3,0},{4,7},{5,6},{6,5},{7,4},{8,11},{9,10},{10,... | collective-permute-start | bytes 393224 | tf_op jit(solution)/shard_map/ppermute | solution.py:340
  17.9 12.9 %collective-permute-start.6 = (bf16[128,512]{1,0:T(8,128)(2,1)S(1)}, bf16[128,512]{1,0:T(8,128)(2,1)S(1)}, u32[]{:S(2)}, u32[]{:S(2)}) collective-permute-start(bf16[128,512]{1,0:T(8,128)(2,1)S(1)} %get-tuple-element.80.refs_0_), channel_id=1, source_target_pairs={{0,2},{1,3},{2,0},{3,1},{4,6},{5,7},{6,4},{7,5},{8,10},{9,11},{10,... | collective-permute-start | bytes 393224 | tf_op jit(solution)/shard_map/ppermute | solution.py:340
  26.7 5.4 %collective-permute-start.3 = (bf16[128,256]{1,0:T(8,128)(2,1)S(1)}, bf16[128,256]{1,0:T(8,128)(2,1)S(1)}, u32[]{:S(2)}, u32[]{:S(2)}) collective-permute-start(bf16[128,256]{1,0:T(8,128)(2,1)S(1)} %get-tuple-element.68), channel_id=1, source_target_pairs={{0,2},{1,3},{2,0},{3,1},{4,6},{5,7},{6,4},{7,5},{8,10},{9,11},{10,... | collective-permute-start | bytes 196616 | tf_op jit(solution)/shard_map/ppermute | solution.py:340
  28.5 5.5 %collective-permute-start.4 = (bf16[128,256]{1,0:T(8,128)(2,1)S(1)}, bf16[128,256]{1,0:T(8,128)(2,1)S(1)}, u32[]{:S(2)}, u32[]{:S(2)}) collective-permute-start(bf16[128,256]{1,0:T(8,128)(2,1)S(1)} %get-tuple-element.69), channel_id=1, source_target_pairs={{0,3},{1,2},{2,1},{3,0},{4,7},{5,6},{6,5},{7,4},{8,11},{9,10},{10,... | collective-permute-start | bytes 196616 | tf_op jit(solution)/shard_map/ppermute | solution.py:340
  29.7 4.9 %collective-permute-start.5 = (bf16[128,256]{1,0:T(8,128)(2,1)S(1)}, bf16[128,256]{1,0:T(8,128)(2,1)S(1)}, u32[]{:S(2)}, u32[]{:S(2)}) collective-permute-start(bf16[128,256]{1,0:T(8,128)(2,1)S(1)} %get-tuple-element.70), channel_id=1, source_target_pairs={{0,1},{1,0},{2,3},{3,2},{4,5},{5,4},{6,7},{7,6},{8,9},{9,8},{10,11... | collective-permute-start | bytes 196616 | tf_op jit(solution)/shard_map/ppermute | solution.py:340
  34.8 4.3 %collective-permute-start.10 = (f32[2,128]{1,0:T(2,128)S(1)}, f32[2,128]{1,0:T(2,128)S(1)}, u32[]{:S(2)}, u32[]{:S(2)}) collective-permute-start(f32[2,128]{1,0:T(2,128)S(1)} %get-tuple-element.78.refs_0_), channel_id=1, source_target_pairs={{0,24},{8,16},{16,8},{24,0},{1,25},{9,17},{17,9},{25,1},{2,26},{10... | collective-permute-start | bytes 3080 | tf_op jit(solution)/shard_map/ppermute | solution.py:340
  34.9 4.3 %collective-permute-start.9 = (f32[2,128]{1,0:T(2,128)S(1)}, f32[2,128]{1,0:T(2,128)S(1)}, u32[]{:S(2)}, u32[]{:S(2)}) collective-permute-start(f32[2,128]{1,0:T(2,128)S(1)} %get-tuple-element.78.refs_0_), channel_id=1, source_target_pairs={{0,16},{8,24},{16,0},{24,8},{1,17},{9,25},{17,1},{25,9},{2,18},{10... | collective-permute-start | bytes 3080 | tf_op jit(solution)/shard_map/ppermute | solution.py:340
  36.4 2.7 %collective-permute-start.8 = (f32[2,128]{1,0:T(2,128)S(1)}, f32[2,128]{1,0:T(2,128)S(1)}, u32[]{:S(2)}, u32[]{:S(2)}) collective-permute-start(f32[2,128]{1,0:T(2,128)S(1)} %get-tuple-element.78.refs_0_), channel_id=1, source_target_pairs={{0,8},{8,0},{16,24},{24,16},{1,9},{9,1},{17,25},{25,17},{2,10},{10... | collective-permute-start | bytes 3080 | tf_op jit(solution)/shard_map/ppermute | solution.py:340
  36.7 10.4 %collective-permute-start.15 = (bf16[128,256]{1,0:T(8,128)(2,1)S(1)}, bf16[128,256]{1,0:T(8,128)(2,1)S(1)}, u32[]{:S(2)}, u32[]{:S(2)}) collective-permute-start(bf16[128,256]{1,0:T(8,128)(2,1)S(1)} %bitcast.11), channel_id=1, source_target_pairs={{0,4},{1,5},{2,6},{3,7},{4,0},{5,1},{6,2},{7,3},{8,12},{9,13},{10,... | collective-permute-start | bytes 196616 | tf_op jit(solution)/shard_map/ppermute | solution.py:340
  39.3 7.9 %collective-permute-start.14 = (bf16[128,256]{1,0:T(8,128)(2,1)S(1)}, bf16[128,256]{1,0:T(8,128)(2,1)S(1)}, u32[]{:S(2)}, u32[]{:S(2)}) collective-permute-start(bf16[128,256]{1,0:T(8,128)(2,1)S(1)} %shard_map.167.refs_4_), channel_id=1, source_target_pairs={{0,4},{1,5},{2,6},{3,7},{4,0},{5,1},{6,2},{7,3},{8,12},{9,13},{10,... | collective-permute-start | bytes 196616 | tf_op jit(solution)/shard_map/ppermute | solution.py:340
  41.1 8.1 %collective-permute-start.13 = (bf16[128,256]{1,0:T(8,128)(2,1)S(1)}, bf16[128,256]{1,0:T(8,128)(2,1)S(1)}, u32[]{:S(2)}, u32[]{:S(2)}) collective-permute-start(bf16[128,256]{1,0:T(8,128)(2,1)S(1)} %shard_map.167.refs_4_), channel_id=1, source_target_pairs={{0,3},{1,2},{2,1},{3,0},{4,7},{5,6},{6,5},{7,4},{8,11},{9,10},{10,... | collective-permute-start | bytes 196616 | tf_op jit(solution)/shard_map/ppermute | solution.py:340
  42.2 8.5 %collective-permute-start.12 = (bf16[128,256]{1,0:T(8,128)(2,1)S(1)}, bf16[128,256]{1,0:T(8,128)(2,1)S(1)}, u32[]{:S(2)}, u32[]{:S(2)}) collective-permute-start(bf16[128,256]{1,0:T(8,128)(2,1)S(1)} %shard_map.167.refs_4_), channel_id=1, source_target_pairs={{0,2},{1,3},{2,0},{3,1},{4,6},{5,7},{6,4},{7,5},{8,10},{9,11},{10,... | collective-permute-start | bytes 196616 | tf_op jit(solution)/shard_map/ppermute | solution.py:340
  43.1 7.6 %collective-permute-start.11 = (bf16[128,256]{1,0:T(8,128)(2,1)S(1)}, bf16[128,256]{1,0:T(8,128)(2,1)S(1)}, u32[]{:S(2)}, u32[]{:S(2)}) collective-permute-start(bf16[128,256]{1,0:T(8,128)(2,1)S(1)} %shard_map.167.refs_4_), channel_id=1, source_target_pairs={{0,1},{1,0},{2,3},{3,2},{4,5},{5,4},{6,7},{7,6},{8,9},{9,8},{10,11... | collective-permute-start | bytes 196616 | tf_op jit(solution)/shard_map/ppermute | solution.py:340
  45.8 1.3 %copy-start.6 = (f32[4,512,192]{2,1,0:T(8,128)}, f32[4,512,192]{2,1,0:T(8,128)S(1)}, u32[]{:S(2)}) copy-start(f32[4,512,192]{2,1,0:T(8,128)S(1)} %get-tuple-element.84.factors) | copy-start | bytes 4718596
  47.1 5.7 %copy-start.8 = (bf16[3,512,192]{2,1,0:T(8,128)(2,1)}, bf16[3,512,192]{2,1,0:T(8,128)(2,1)S(1)}, u32[]{:S(2)}) copy-start(bf16[3,512,192]{2,1,0:T(8,128)(2,1)S(1)} %get-tuple-element.85.rises) | copy-start | bytes 1769476
  47.1 5.7 %copy-start.10 = (f32[3,256,192]{2,1,0:T(8,128)}, f32[3,256,192]{2,1,0:T(8,128)S(1)}, u32[]{:S(2)}) copy-start(f32[3,256,192]{2,1,0:T(8,128)S(1)} %get-tuple-element.88.minus) | copy-start | bytes 1769476
  47.1 5.7 %copy-start.12 = (f32[3,256,192]{2,1,0:T(8,128)}, f32[3,256,192]{2,1,0:T(8,128)S(1)}, u32[]{:S(2)}) copy-start(f32[3,256,192]{2,1,0:T(8,128)S(1)} %get-tuple-element.89.plus) | copy-start | bytes 1769476
  47.2 10.0 %collective-permute-start.18 = (bf16[128,512]{1,0:T(8,128)(2,1)S(1)}, bf16[128,512]{1,0:T(8,128)(2,1)S(1)}, u32[]{:S(2)}, u32[]{:S(2)}) collective-permute-start(bf16[128,512]{1,0:T(8,128)(2,1)S(1)} %shard_map.170.refs_4_), channel_id=1, source_target_pairs={{0,3},{1,2},{2,1},{3,0},{4,7},{5,6},{6,5},{7,4},{8,11},{9,10},{10,... | collective-permute-start | bytes 393224 | tf_op jit(solution)/shard_map/ppermute | solution.py:340
  48.3 8.8 %collective-permute-start.17 = (bf16[128,512]{1,0:T(8,128)(2,1)S(1)}, bf16[128,512]{1,0:T(8,128)(2,1)S(1)}, u32[]{:S(2)}, u32[]{:S(2)}) collective-permute-start(bf16[128,512]{1,0:T(8,128)(2,1)S(1)} %shard_map.170.refs_4_), channel_id=1, source_target_pairs={{0,2},{1,3},{2,0},{3,1},{4,6},{5,7},{6,4},{7,5},{8,10},{9,11},{10,... | collective-permute-start | bytes 393224 | tf_op jit(solution)/shard_map/ppermute | solution.py:340
  49.2 7.9 %collective-permute-start.16 = (bf16[128,512]{1,0:T(8,128)(2,1)S(1)}, bf16[128,512]{1,0:T(8,128)(2,1)S(1)}, u32[]{:S(2)}, u32[]{:S(2)}) collective-permute-start(bf16[128,512]{1,0:T(8,128)(2,1)S(1)} %shard_map.170.refs_4_), channel_id=1, source_target_pairs={{0,1},{1,0},{2,3},{3,2},{4,5},{5,4},{6,7},{7,6},{8,9},{9,8},{10,11... | collective-permute-start | bytes 393224 | tf_op jit(solution)/shard_map/ppermute | solution.py:340
  52.8 0.9 %copy-start.14 = (f32[3,256,192]{2,1,0:T(8,128)}, f32[3,256,192]{2,1,0:T(8,128)S(1)}, u32[]{:S(2)}) copy-start(f32[3,256,192]{2,1,0:T(8,128)S(1)} %get-tuple-element.79.grads) | copy-start | bytes 1769476
  53.7 12.1 %all-to-all-start.1 = ((bf16[4,128,256]{2,1,0:T(8,128)(2,1)}), bf16[4,128,256]{2,1,0:T(8,128)(2,1)S(1)}, u32[]{:S(2)}, u32[]{:S(2)}) async-start(bf16[4,128,256]{2,1,0:T(8,128)(2,1)} %get-tuple-element.99), calls=%async_computation.1 | async-start | bytes 524288 | tf_op jit(solution)/shard_map/all_to_all | solution.py:418
  57.2 1.6 %copy-start.7 = (f32[4,512,192]{2,1,0:T(8,128)S(1)}, f32[4,512,192]{2,1,0:T(8,128)}, u32[]{:S(2)}) copy-start(f32[4,512,192]{2,1,0:T(8,128)} %copy-done.6) | copy-start | bytes 4718596
  58.8 1.1 %copy-start.9 = (bf16[3,512,192]{2,1,0:T(8,128)(2,1)S(1)}, bf16[3,512,192]{2,1,0:T(8,128)(2,1)}, u32[]{:S(2)}) copy-start(bf16[3,512,192]{2,1,0:T(8,128)(2,1)} %copy-done.8) | copy-start | bytes 1769476
  59.9 1.1 %copy-start.11 = (f32[3,256,192]{2,1,0:T(8,128)S(1)}, f32[3,256,192]{2,1,0:T(8,128)}, u32[]{:S(2)}) copy-start(f32[3,256,192]{2,1,0:T(8,128)} %copy-done.10) | copy-start | bytes 1769476
  61.0 1.1 %copy-start.13 = (f32[3,256,192]{2,1,0:T(8,128)S(1)}, f32[3,256,192]{2,1,0:T(8,128)}, u32[]{:S(2)}) copy-start(f32[3,256,192]{2,1,0:T(8,128)} %copy-done.12) | copy-start | bytes 1769476
  62.2 1.1 %copy-start.15 = (f32[3,256,192]{2,1,0:T(8,128)S(1)}, f32[3,256,192]{2,1,0:T(8,128)}, u32[]{:S(2)}) copy-start(f32[3,256,192]{2,1,0:T(8,128)} %copy-done.14) | copy-start | bytes 1769476
  65.9 7.9 %collective-permute-start.19 = (bf16[672,128]{1,0:T(8,128)(2,1)S(1)}, bf16[672,128]{1,0:T(8,128)(2,1)S(1)}, u32[]{:S(2)}, u32[]{:S(2)}) collective-permute-start(bf16[672,128]{1,0:T(8,128)(2,1)S(1)} %get-tuple-element.102), channel_id=1, source_target_pairs={{0,1},{1,0},{2,3},{3,2},{4,5},{5,4},{6,7},{7,6},{8,9},{9,8},{10,11... | collective-permute-start | bytes 516104 | tf_op jit(solution)/shard_map/ppermute | solution.py:340
  67.9 8.1 %collective-permute-start.20 = (bf16[672,128]{1,0:T(8,128)(2,1)S(1)}, bf16[672,128]{1,0:T(8,128)(2,1)S(1)}, u32[]{:S(2)}, u32[]{:S(2)}) collective-permute-start(bf16[672,128]{1,0:T(8,128)(2,1)S(1)} %get-tuple-element.103), channel_id=1, source_target_pairs={{0,2},{1,3},{2,0},{3,1},{4,6},{5,7},{6,4},{7,5},{8,10},{9,11},{10,... | collective-permute-start | bytes 516104 | tf_op jit(solution)/shard_map/ppermute | solution.py:340
  69.4 9.5 %collective-permute-start.21 = (bf16[672,128]{1,0:T(8,128)(2,1)S(1)}, bf16[672,128]{1,0:T(8,128)(2,1)S(1)}, u32[]{:S(2)}, u32[]{:S(2)}) collective-permute-start(bf16[672,128]{1,0:T(8,128)(2,1)S(1)} %get-tuple-element.104), channel_id=1, source_target_pairs={{0,3},{1,2},{2,1},{3,0},{4,7},{5,6},{6,5},{7,4},{8,11},{9,10},{10,... | collective-permute-start | bytes 516104 | tf_op jit(solution)/shard_map/ppermute | solution.py:340
  69.4 10.2 %collective-permute-start.22 = (bf16[32,576]{1,0:T(8,128)(2,1)S(1)}, bf16[32,576]{1,0:T(8,128)(2,1)S(1)}, u32[]{:S(2)}, u32[]{:S(2)}) collective-permute-start(bf16[32,576]{1,0:T(8,128)(2,1)S(1)} %get-tuple-element.109), channel_id=1, source_target_pairs={{0,4},{1,5},{2,6},{3,7},{4,0},{5,1},{6,2},{7,3},{8,12},{9,13},{10,... | collective-permute-start | bytes 110600 | tf_op jit(solution)/shard_map/ppermute | solution.py:340
  70.6 9.0 %collective-permute-start.23 = (bf16[32,576]{1,0:T(8,128)(2,1)S(1)}, bf16[32,576]{1,0:T(8,128)(2,1)S(1)}, u32[]{:S(2)}, u32[]{:S(2)}) collective-permute-start(bf16[32,576]{1,0:T(8,128)(2,1)S(1)} %get-tuple-element.110), channel_id=1, source_target_pairs={{0,5},{1,4},{2,7},{3,6},{4,1},{5,0},{6,3},{7,2},{8,13},{9,12},{10,... | collective-permute-start | bytes 110600 | tf_op jit(solution)/shard_map/ppermute | solution.py:340
  73.7 5.9 %collective-permute-start.24 = (bf16[32,576]{1,0:T(8,128)(2,1)S(1)}, bf16[32,576]{1,0:T(8,128)(2,1)S(1)}, u32[]{:S(2)}, u32[]{:S(2)}) collective-permute-start(bf16[32,576]{1,0:T(8,128)(2,1)S(1)} %get-tuple-element.111), channel_id=1, source_target_pairs={{0,6},{1,7},{2,4},{3,5},{4,2},{5,3},{6,0},{7,1},{8,14},{9,15},{10,... | collective-permute-start | bytes 110600 | tf_op jit(solution)/shard_map/ppermute | solution.py:340
  76.0 6.7 %collective-permute-start.25 = (bf16[32,576]{1,0:T(8,128)(2,1)S(1)}, bf16[32,576]{1,0:T(8,128)(2,1)S(1)}, u32[]{:S(2)}, u32[]{:S(2)}) collective-permute-start(bf16[32,576]{1,0:T(8,128)(2,1)S(1)} %get-tuple-element.112), channel_id=1, source_target_pairs={{0,7},{1,6},{2,5},{3,4},{4,3},{5,2},{6,1},{7,0},{8,15},{9,14},{10,... | collective-permute-start | bytes 110600 | tf_op jit(solution)/shard_map/ppermute | solution.py:340

commit v12 on v11

--- a/solution.py
+++ b/solution.py
@@ -397,7 +397,7 @@
             functools.partial(key_kernel, slab, group),
             (arr((4, near, slab), F32), arr((3, near, slab), BF), arr((3, slab), F32), column, column),
             (wall, *kv_near),
-            24,
+            16,
             flops=12 * mflop,
         )
         *od_mirror, stats[0] = lax.optimization_barrier((*od_mirror, stats[0]))
@@ -409,9 +409,9 @@
             functools.partial(near_kernel, slab, group),
             (arr((group, own, feat), BF), arr((3, seq_n * rows, slab), F32)),
             (place, normed, *q_near, *od_near),
-            24,
+            12,
             smem=1,
-            flops=300 * mflop,
+            flops=60 * mflop,
         )
 
         q_block = (own, feat)
@@ -425,9 +425,9 @@
                 *(arr((rows, 3 * slab), BF),) * (seq_n - group),
             ),
             (place, wall, normed, grads, factors, rises, *stats, *kv_near, *pairs),
-            40,
+            24,
             smem=1,
-            flops=600 * mflop,
+            flops=120 * mflop,
             scratch=[
                 pltpu.VMEM((seq_n, rows, 3 * slab), F32),
                 pltpu.VMEM((3, seq_n * rows, slab), F32),

time: 84.6 us -> 84.1 us (level)
  waiting for transfers between devices: 15 us -> 16.9 us
  local copies, waits for them, and re-layouts: 9.71 us -> 8.39 us
  starting transfers between devices: 47.4 us -> 46.3 us
    ppermute x26, waiting for transfers between devices: 15 us -> 16.9 us  [move(): return lax.ppermute(x, axis, [(i, i ^ dist) for i in range(size)])]
    unnamed x32, local copies, waits for them, and re-layouts: 9.71 us -> 8.39 us
    ppermute x26, starting transfers between devices: 36.8 us -> 35.6 us  [move(): return lax.ppermute(x, axis, [(i, i ^ dist) for i in range(size)])]
  transfers between devices with their start and end apart: 28 -> 28, of which waited for: 8 -> 11; matrix products, arithmetic and copies ran while one was open for 0% -> 0% of each run, Pallas kernels for 9% -> 9%
where the time goes in v12:
time: 84.1 us; the launch traced here: 83.5 us
  starting transfers between devices  46.3 us (55%)
  waiting for transfers between devices  16.9 us (20%)
  Pallas kernels  11 us (13%)
  local copies, waits for them, and re-layouts  8.39 us (10%)
  between operations  0.9 us (1%)
    ppermute x26, starting transfers between devices, move(): return lax.ppermute(x, axis, [(i, i ^ dist) for i in range(size)])  35.6 us
    ppermute x26, waiting for transfers between devices, move(): return lax.ppermute(x, axis, [(i, i ^ dist) for i in range(size)])  16.9 us
    pallas_call x10, Pallas kernels, call(): pl.pallas_call(kernel, out_shape=outs, in_specs=[SMEM] * smem + [VMEM] *...  9.01 us
    unnamed x32, local copies, waits for them, and re-layouts  8.39 us
    all_to_all x1, starting transfers between devices, local(): lax.all_to_all(packed, 'seq', 0, 0, tiled=True)  7.26 us
    all_to_all x1, starting transfers between devices, local(): lax.all_to_all(grad_q, 'seq', 0, 0, axis_index_groups=groups, tiled=True)  3.4 us
    pallas_call x1, Pallas kernels, copying_call(): pl.pallas_call(kernel, out_shape=outs, in_specs=[pl.BlockSpec(memory_spac...  1.96 us
  transfers between devices with their start and end apart: 28, of which 11 were waited for; matrix products, arithmetic and copies ran while one was open for 0% of the time, Pallas kernels for 9%

profile of v12, /device:TPU:0, one launch (start us, length us, event | category | flops | bytes accessed | tf_op | source)
XLA Modules:
  0.0 83.5 jit_solution(10308900253195614533)
XLA Ops:
  0.7 2.0 %shard_map.164 = bf16[8,32,1152]{2,1,0:T(8,128)(2,1)} custom-call(bf16[1,32,768]{2,1,0:T(8,128)(2,1)} %refs_0_.1, bf16[1,32,768]{2,1,0:T(8,128)(2,1)} %refs_1_.1, bf16[1,32,768]{2,1,0:T(8,128)(2,1)} %refs_2_.1, bf16[1,32,768]{2,1,0:T(8,128)(2,1)} %refs_3_.1, bf16[1,32,768]{2,1,0:T(8,128)(2,1)} %refs_4_.1, bf16[1,32,768]{2,1,0:T(8,128)(2,1)} %refs_5_.1), custom_call_target="tpu_custom_call" | custom-call | tf_op jit(solution)/shard_map/pallas_call | solution.py:61
  2.6 7.3 %all-to-all-start = ((bf16[8,32,1152]{2,1,0:T(8,128)(2,1)}), bf16[8,32,1152]{2,1,0:T(8,128)(2,1)S(1)}, u32[]{:S(2)}, u32[]{:S(2)}) async-start(bf16[8,32,1152]{2,1,0:T(8,128)(2,1)} %shard_map.164), calls=%async_computation | async-start | bytes 1179648 | tf_op jit(solution)/shard_map/all_to_all | solution.py:363
  9.9 0.0 copy-start.4
  10.0 0.7 copy-done.4
  10.6 0.7 copy-done.5
  11.3 0.1 shard_map.163
  11.4 2.1 %collective-permute-start = (bf16[128,768]{1,0:T(8,128)(2,1)S(1)}, bf16[128,768]{1,0:T(8,128)(2,1)S(1)}, u32[]{:S(2)}, u32[]{:S(2)}) collective-permute-start(bf16[128,768]{1,0:T(8,128)(2,1)S(1)} %get-tuple-element.64), channel_id=1, source_target_pairs={{0,1},{1,0},{2,3},{3,2},{4,5},{5,4},{6,7},{7,6},{8,9},{9,8},{10,11... | collective-permute-start | bytes 589832 | tf_op jit(solution)/shard_map/ppermute | solution.py:340
  13.5 1.5 %collective-permute-start.2 = (bf16[128,256]{1,0:T(8,128)(2,1)S(1)}, bf16[128,256]{1,0:T(8,128)(2,1)S(1)}, u32[]{:S(2)}, u32[]{:S(2)}) collective-permute-start(bf16[128,256]{1,0:T(8,128)(2,1)S(1)} %bitcast.8), channel_id=1, source_target_pairs={{0,3},{1,2},{2,1},{3,0},{4,7},{5,6},{6,5},{7,4},{8,11},{9,10},{10,... | collective-permute-start | bytes 196616 | tf_op jit(solution)/shard_map/ppermute | solution.py:340
  14.9 0.1 collective-permute-start.1
  15.0 2.8 %collective-permute-start.7 = (bf16[128,512]{1,0:T(8,128)(2,1)S(1)}, bf16[128,512]{1,0:T(8,128)(2,1)S(1)}, u32[]{:S(2)}, u32[]{:S(2)}) collective-permute-start(bf16[128,512]{1,0:T(8,128)(2,1)S(1)} %get-tuple-element.80.refs_0_), channel_id=1, source_target_pairs={{0,3},{1,2},{2,1},{3,0},{4,7},{5,6},{6,5},{7,4},{8,11},{9,10},{10,... | collective-permute-start | bytes 393224 | tf_op jit(solution)/shard_map/ppermute | solution.py:340
  17.9 0.6 collective-permute-start.6
  18.4 4.8 %collective-permute-done.2.refs_3_ = bf16[128,256]{1,0:T(8,128)(2,1)S(1)} collective-permute-done((bf16[128,256]{1,0:T(8,128)(2,1)S(1)}, bf16[128,256]{1,0:T(8,128)(2,1)S(1)}, u32[]{:S(2)}, u32[]{:S(2)}) %collective-permute-start.2) | collective-permute-done | bytes 65568 | tf_op jit(solution)/shard_map/ppermute | solution.py:340
  23.3 0.4 collective-permute-done.1.refs_2_
  23.6 2.3 %collective-permute-done.refs_1_ = bf16[128,768]{1,0:T(8,128)(2,1)S(1)} collective-permute-done((bf16[128,768]{1,0:T(8,128)(2,1)S(1)}, bf16[128,768]{1,0:T(8,128)(2,1)S(1)}, u32[]{:S(2)}, u32[]{:S(2)}) %collective-permute-start) | collective-permute-done | bytes 196640 | tf_op jit(solution)/shard_map/ppermute | solution.py:340
  25.9 0.8 shard_map.165
  26.7 1.8 %collective-permute-start.3 = (bf16[128,256]{1,0:T(8,128)(2,1)S(1)}, bf16[128,256]{1,0:T(8,128)(2,1)S(1)}, u32[]{:S(2)}, u32[]{:S(2)}) collective-permute-start(bf16[128,256]{1,0:T(8,128)(2,1)S(1)} %get-tuple-element.68), channel_id=1, source_target_pairs={{0,2},{1,3},{2,0},{3,1},{4,6},{5,7},{6,4},{7,5},{8,10},{9,11},{10,... | collective-permute-start | bytes 196616 | tf_op jit(solution)/shard_map/ppermute | solution.py:340
  28.5 1.1 %collective-permute-start.4 = (bf16[128,256]{1,0:T(8,128)(2,1)S(1)}, bf16[128,256]{1,0:T(8,128)(2,1)S(1)}, u32[]{:S(2)}, u32[]{:S(2)}) collective-permute-start(bf16[128,256]{1,0:T(8,128)(2,1)S(1)} %get-tuple-element.69), channel_id=1, source_target_pairs={{0,3},{1,2},{2,1},{3,0},{4,7},{5,6},{6,5},{7,4},{8,11},{9,10},{10,... | collective-permute-start | bytes 196616 | tf_op jit(solution)/shard_map/ppermute | solution.py:340
  29.7 0.6 collective-permute-start.5
  30.3 0.5 collective-permute-done.6.refs_2_
  30.7 1.4 %collective-permute-done.3.refs_1_ = bf16[128,256]{1,0:T(8,128)(2,1)S(1)} collective-permute-done((bf16[128,256]{1,0:T(8,128)(2,1)S(1)}, bf16[128,256]{1,0:T(8,128)(2,1)S(1)}, u32[]{:S(2)}, u32[]{:S(2)}) %collective-permute-start.3) | collective-permute-done | bytes 65568 | tf_op jit(solution)/shard_map/ppermute | solution.py:340
  32.1 1.9 %collective-permute-done.4.refs_2_ = bf16[128,256]{1,0:T(8,128)(2,1)S(1)} collective-permute-done((bf16[128,256]{1,0:T(8,128)(2,1)S(1)}, bf16[128,256]{1,0:T(8,128)(2,1)S(1)}, u32[]{:S(2)}, u32[]{:S(2)}) %collective-permute-start.4) | collective-permute-done | bytes 65568 | tf_op jit(solution)/shard_map/ppermute | solution.py:340
  34.0 0.6 collective-permute-done.5.refs_3_
  34.6 0.1 shard_map.166
  34.8 0.1 collective-permute-start.10
  34.9 1.6 %collective-permute-start.9 = (f32[2,128]{1,0:T(2,128)S(1)}, f32[2,128]{1,0:T(2,128)S(1)}, u32[]{:S(2)}, u32[]{:S(2)}) collective-permute-start(f32[2,128]{1,0:T(2,128)S(1)} %get-tuple-element.78.refs_0_), channel_id=1, source_target_pairs={{0,16},{8,24},{16,0},{24,8},{1,17},{9,25},{17,1},{25,9},{2,18},{10... | collective-permute-start | bytes 3080 | tf_op jit(solution)/shard_map/ppermute | solution.py:340
  36.4 0.3 collective-permute-start.8
  36.7 2.4 %collective-permute-start.15 = (bf16[128,256]{1,0:T(8,128)(2,1)S(1)}, bf16[128,256]{1,0:T(8,128)(2,1)S(1)}, u32[]{:S(2)}, u32[]{:S(2)}) collective-permute-start(bf16[128,256]{1,0:T(8,128)(2,1)S(1)} %bitcast.11), channel_id=1, source_target_pairs={{0,4},{1,5},{2,6},{3,7},{4,0},{5,1},{6,2},{7,3},{8,12},{9,13},{10,... | collective-permute-start | bytes 196616 | tf_op jit(solution)/shard_map/ppermute | solution.py:340
  39.1 0.0 collective-permute-done.10.refs_3_
  39.1 0.0 collective-permute-done.9.refs_2_
  39.1 0.0 collective-permute-done.8.refs_1_
  39.1 0.1 shard_map.167.refs_4_
  39.3 1.8 %collective-permute-start.14 = (bf16[128,256]{1,0:T(8,128)(2,1)S(1)}, bf16[128,256]{1,0:T(8,128)(2,1)S(1)}, u32[]{:S(2)}, u32[]{:S(2)}) collective-permute-start(bf16[128,256]{1,0:T(8,128)(2,1)S(1)} %shard_map.167.refs_4_), channel_id=1, source_target_pairs={{0,4},{1,5},{2,6},{3,7},{4,0},{5,1},{6,2},{7,3},{8,12},{9,13},{10,... | collective-permute-start | bytes 196616 | tf_op jit(solution)/shard_map/ppermute | solution.py:340
  41.1 1.1 %collective-permute-start.13 = (bf16[128,256]{1,0:T(8,128)(2,1)S(1)}, bf16[128,256]{1,0:T(8,128)(2,1)S(1)}, u32[]{:S(2)}, u32[]{:S(2)}) collective-permute-start(bf16[128,256]{1,0:T(8,128)(2,1)S(1)} %shard_map.167.refs_4_), channel_id=1, source_target_pairs={{0,3},{1,2},{2,1},{3,0},{4,7},{5,6},{6,5},{7,4},{8,11},{9,10},{10,... | collective-permute-start | bytes 196616 | tf_op jit(solution)/shard_map/ppermute | solution.py:340
  42.2 0.9 %collective-permute-start.12 = (bf16[128,256]{1,0:T(8,128)(2,1)S(1)}, bf16[128,256]{1,0:T(8,128)(2,1)S(1)}, u32[]{:S(2)}, u32[]{:S(2)}) collective-permute-start(bf16[128,256]{1,0:T(8,128)(2,1)S(1)} %shard_map.167.refs_4_), channel_id=1, source_target_pairs={{0,2},{1,3},{2,0},{3,1},{4,6},{5,7},{6,4},{7,5},{8,10},{9,11},{10,... | collective-permute-start | bytes 196616 | tf_op jit(solution)/shard_map/ppermute | solution.py:340
  43.1 1.5 %collective-permute-start.11 = (bf16[128,256]{1,0:T(8,128)(2,1)S(1)}, bf16[128,256]{1,0:T(8,128)(2,1)S(1)}, u32[]{:S(2)}, u32[]{:S(2)}) collective-permute-start(bf16[128,256]{1,0:T(8,128)(2,1)S(1)} %shard_map.167.refs_4_), channel_id=1, source_target_pairs={{0,1},{1,0},{2,3},{3,2},{4,5},{5,4},{6,7},{7,6},{8,9},{9,8},{10,11... | collective-permute-start | bytes 196616 | tf_op jit(solution)/shard_map/ppermute | solution.py:340
  44.6 0.1 pad_add_fusion.place
  44.7 1.1 %shard_map.169 = (f32[4,512,192]{2,1,0:T(8,128)S(1)}, bf16[3,512,192]{2,1,0:T(8,128)(2,1)S(1)}, f32[3,192]{1,0:T(4,128)S(1)}, f32[3,256,192]{2,1,0:T(8,128)S(1)}, f32[3,256,192]{2,1,0:T(8,128)S(1)}) custom-call(bf16[256,1152]{1,0:T(8,128)(2,1)S(1)} %bitcast.6, bf16[128,512]{1,0:T(8,128)(2,1)S(1)} %get-tuple-element.80.refs_0_, ...), custom_call_target="tpu_custom_call" | custom-call | flops 603979776 | bytes 4524288 | tf_op jit(solution)/shard_map/pallas_call | solution.py:49
  45.8 0.2 collective-permute-done.14.left
  46.1 0.9 %collective-permute-start.18 = (bf16[128,512]{1,0:T(8,128)(2,1)S(1)}, bf16[128,512]{1,0:T(8,128)(2,1)S(1)}, u32[]{:S(2)}, u32[]{:S(2)}) collective-permute-start(bf16[128,512]{1,0:T(8,128)(2,1)S(1)} %shard_map.170.refs_4_), channel_id=1, source_target_pairs={{0,3},{1,2},{2,1},{3,0},{4,7},{5,6},{6,5},{7,4},{8,11},{9,10},{10,... | collective-permute-start | bytes 393224 | tf_op jit(solution)/shard_map/ppermute | solution.py:340
  47.0 1.1 %collective-permute-start.17 = (bf16[128,512]{1,0:T(8,128)(2,1)S(1)}, bf16[128,512]{1,0:T(8,128)(2,1)S(1)}, u32[]{:S(2)}, u32[]{:S(2)}) collective-permute-start(bf16[128,512]{1,0:T(8,128)(2,1)S(1)} %shard_map.170.refs_4_), channel_id=1, source_target_pairs={{0,2},{1,3},{2,0},{3,1},{4,6},{5,7},{6,4},{7,5},{8,10},{9,11},{10,... | collective-permute-start | bytes 393224 | tf_op jit(solution)/shard_map/ppermute | solution.py:340
  48.1 1.5 %collective-permute-start.16 = (bf16[128,512]{1,0:T(8,128)(2,1)S(1)}, bf16[128,512]{1,0:T(8,128)(2,1)S(1)}, u32[]{:S(2)}, u32[]{:S(2)}) collective-permute-start(bf16[128,512]{1,0:T(8,128)(2,1)S(1)} %shard_map.170.refs_4_), channel_id=1, source_target_pairs={{0,1},{1,0},{2,3},{3,2},{4,5},{5,4},{6,7},{7,6},{8,9},{9,8},{10,11... | collective-permute-start | bytes 393224 | tf_op jit(solution)/shard_map/ppermute | solution.py:340
  49.6 2.0 %shard_map.168 = (bf16[4,128,256]{2,1,0:T(8,128)(2,1)}, f32[3,256,192]{2,1,0:T(8,128)S(1)}) custom-call(s32[3]{0:T(128)S(1)} %pad_add_fusion.place, bf16[256,576]{1,0:T(8,128)(2,1)S(1)} %get-tuple-element.65.normed_ref, bf16[128,256]{1,0:T(8,128)(2,1)S(1)} %bitcast.12, bf16[128,768]{1,0:T(8,128)(2,1)S(1)} %collective-permute-done.refs_1_, ...), custom_call_target="tpu_custom_call" | custom-call | flops 3019898880 | bytes 1802252 | tf_op jit(solution)/shard_map/pallas_call | solution.py:49
  51.7 0.9 %copy-done.14 = f32[3,256,192]{2,1,0:T(8,128)} copy-done((f32[3,256,192]{2,1,0:T(8,128)}, f32[3,256,192]{2,1,0:T(8,128)S(1)}, u32[]{:S(2)}) %copy-start.14) | copy-done | bytes 589848
  52.6 3.4 %all-to-all-start.1 = ((bf16[4,128,256]{2,1,0:T(8,128)(2,1)}), bf16[4,128,256]{2,1,0:T(8,128)(2,1)S(1)}, u32[]{:S(2)}, u32[]{:S(2)}) async-start(bf16[4,128,256]{2,1,0:T(8,128)(2,1)} %get-tuple-element.99), calls=%async_computation.1 | async-start | bytes 524288 | tf_op jit(solution)/shard_map/all_to_all | solution.py:418
  56.1 0.0 collective-permute-done.16.refs_5_
  56.1 1.6 %copy-done.7 = f32[4,512,192]{2,1,0:T(8,128)S(1)} copy-done((f32[4,512,192]{2,1,0:T(8,128)S(1)}, f32[4,512,192]{2,1,0:T(8,128)}, u32[]{:S(2)}) %copy-start.7) | copy-done | bytes 1572888
  57.7 1.1 %copy-done.9 = bf16[3,512,192]{2,1,0:T(8,128)(2,1)S(1)} copy-done((bf16[3,512,192]{2,1,0:T(8,128)(2,1)S(1)}, bf16[3,512,192]{2,1,0:T(8,128)(2,1)}, u32[]{:S(2)}) %copy-start.9) | copy-done | bytes 589848
  58.8 1.1 %copy-done.11 = f32[3,256,192]{2,1,0:T(8,128)S(1)} copy-done((f32[3,256,192]{2,1,0:T(8,128)S(1)}, f32[3,256,192]{2,1,0:T(8,128)}, u32[]{:S(2)}) %copy-start.11) | copy-done | bytes 589848
  59.9 1.1 %copy-done.13 = f32[3,256,192]{2,1,0:T(8,128)S(1)} copy-done((f32[3,256,192]{2,1,0:T(8,128)S(1)}, f32[3,256,192]{2,1,0:T(8,128)}, u32[]{:S(2)}) %copy-start.13) | copy-done | bytes 589848
  61.1 1.1 %copy-done.15 = f32[3,256,192]{2,1,0:T(8,128)S(1)} copy-done((f32[3,256,192]{2,1,0:T(8,128)S(1)}, f32[3,256,192]{2,1,0:T(8,128)}, u32[]{:S(2)}) %copy-start.15) | copy-done | bytes 589848
  62.2 2.6 %shard_map.171 = (bf16[128,512]{1,0:T(8,128)(2,1)S(1)}, bf16[32,576]{1,0:T(8,128)(2,1)S(1)}, bf16[672,128]{1,0:T(8,128)(2,1)S(1)}, bf16[672,128]{1,0:T(8,128)(2,...) custom-call(s32[3]{0:T(128)S(1)} %pad_add_fusion.place, ...), custom_call_target="tpu_custom_call" | custom-call | flops 6039797760 | bytes 6764812 | tf_op jit(solution)/shard_map/pallas_call | solution.py:49
  64.8 2.0 %collective-permute-start.19 = (bf16[672,128]{1,0:T(8,128)(2,1)S(1)}, bf16[672,128]{1,0:T(8,128)(2,1)S(1)}, u32[]{:S(2)}, u32[]{:S(2)}) collective-permute-start(bf16[672,128]{1,0:T(8,128)(2,1)S(1)} %get-tuple-element.102), channel_id=1, source_target_pairs={{0,1},{1,0},{2,3},{3,2},{4,5},{5,4},{6,7},{7,6},{8,9},{9,8},{10,11... | collective-permute-start | bytes 516104 | tf_op jit(solution)/shard_map/ppermute | solution.py:340
  66.8 1.5 %collective-permute-start.20 = (bf16[672,128]{1,0:T(8,128)(2,1)S(1)}, bf16[672,128]{1,0:T(8,128)(2,1)S(1)}, u32[]{:S(2)}, u32[]{:S(2)}) collective-permute-start(bf16[672,128]{1,0:T(8,128)(2,1)S(1)} %get-tuple-element.103), channel_id=1, source_target_pairs={{0,2},{1,3},{2,0},{3,1},{4,6},{5,7},{6,4},{7,5},{8,10},{9,11},{10,... | collective-permute-start | bytes 516104 | tf_op jit(solution)/shard_map/ppermute | solution.py:340
  68.3 0.1 collective-permute-start.21
  68.3 1.5 %collective-permute-start.22 = (bf16[32,576]{1,0:T(8,128)(2,1)S(1)}, bf16[32,576]{1,0:T(8,128)(2,1)S(1)}, u32[]{:S(2)}, u32[]{:S(2)}) collective-permute-start(bf16[32,576]{1,0:T(8,128)(2,1)S(1)} %get-tuple-element.109), channel_id=1, source_target_pairs={{0,4},{1,5},{2,6},{3,7},{4,0},{5,1},{6,2},{7,3},{8,12},{9,13},{10,... | collective-permute-start | bytes 110600 | tf_op jit(solution)/shard_map/ppermute | solution.py:340
  69.8 2.8 %collective-permute-start.23 = (bf16[32,576]{1,0:T(8,128)(2,1)S(1)}, bf16[32,576]{1,0:T(8,128)(2,1)S(1)}, u32[]{:S(2)}, u32[]{:S(2)}) collective-permute-start(bf16[32,576]{1,0:T(8,128)(2,1)S(1)} %get-tuple-element.110), channel_id=1, source_target_pairs={{0,5},{1,4},{2,7},{3,6},{4,1},{5,0},{6,3},{7,2},{8,13},{9,12},{10,... | collective-permute-start | bytes 110600 | tf_op jit(solution)/shard_map/ppermute | solution.py:340
  72.7 2.8 %collective-permute-start.24 = (bf16[32,576]{1,0:T(8,128)(2,1)S(1)}, bf16[32,576]{1,0:T(8,128)(2,1)S(1)}, u32[]{:S(2)}, u32[]{:S(2)}) collective-permute-start(bf16[32,576]{1,0:T(8,128)(2,1)S(1)} %get-tuple-element.111), channel_id=1, source_target_pairs={{0,6},{1,7},{2,4},{3,5},{4,2},{5,3},{6,0},{7,1},{8,14},{9,15},{10,... | collective-permute-start | bytes 110600 | tf_op jit(solution)/shard_map/ppermute | solution.py:340
  75.4 1.2 %collective-permute-start.25 = (bf16[32,576]{1,0:T(8,128)(2,1)S(1)}, bf16[32,576]{1,0:T(8,128)(2,1)S(1)}, u32[]{:S(2)}, u32[]{:S(2)}) collective-permute-start(bf16[32,576]{1,0:T(8,128)(2,1)S(1)} %get-tuple-element.112), channel_id=1, source_target_pairs={{0,7},{1,6},{2,5},{3,4},{4,3},{5,2},{6,1},{7,0},{8,15},{9,14},{10,... | collective-permute-start | bytes 110600 | tf_op jit(solution)/shard_map/ppermute | solution.py:340
  76.6 1.4 %collective-permute-done.21.refs_2_ = bf16[672,128]{1,0:T(8,128)(2,1)S(1)} collective-permute-done((bf16[672,128]{1,0:T(8,128)(2,1)S(1)}, bf16[672,128]{1,0:T(8,128)(2,1)S(1)}, u32[]{:S(2)}, u32[]{:S(2)}) %collective-permute-start.21) | collective-permute-done | bytes 172064 | tf_op jit(solution)/shard_map/ppermute | solution.py:340
  78.0 0.7 shard_map.172
  78.8 0.0 collective-permute-done.22.refs_3_
  78.8 0.2 collective-permute-done.24.refs_5_
  79.0 3.1 %collective-permute-done.25.refs_6_ = bf16[32,576]{1,0:T(8,128)(2,1)S(1)} collective-permute-done((bf16[32,576]{1,0:T(8,128)(2,1)S(1)}, bf16[32,576]{1,0:T(8,128)(2,1)S(1)}, u32[]{:S(2)}, u32[]{:S(2)}) %collective-permute-start.25) | collective-permute-done | bytes 36896 | tf_op jit(solution)/shard_map/ppermute | solution.py:340
  82.1 1.4 %shard_map.173 = (f32[1,32,768]{2,1,0:T(8,128)}, f32[1,32,768]{2,1,0:T(8,128)}, f32[1,32,768]{2,1,0:T(8,128)}) custom-call(s32[3]{0:T(128)S(1)} %pad_add_fusion.place, bf16[32,576]{1,0:T(8,128)(2,1)S(1)} %get-tuple-element.108.inner, bf16[672,128]{1,0:T(8,128)(2,1)S(1)} %collective-permute-done.19.refs_0_, ...), custom_call_target="tpu_custom_call" | custom-call | bytes 995340 | tf_op jit(solution)/shard_map/pallas_call | solution.py:49
  (36 shorter events, 0.1 us)
Async XLA Ops:
  0.6 9.3 %copy-start = (bf16[1,128,256]{2,1,0:T(8,128)(2,1)S(1)}, bf16[1,128,256]{2,1,0:T(8,128)(2,1)}, u32[]{:S(2)}) copy-start(bf16[1,128,256]{2,1,0:T(8,128)(2,1)} %q.1) | copy-start | bytes 196612
  0.6 9.3 %copy-start.3 = (bf16[1,128,256]{2,1,0:T(8,128)(2,1)S(1)}, bf16[1,128,256]{2,1,0:T(8,128)(2,1)}, u32[]{:S(2)}) copy-start(bf16[1,128,256]{2,1,0:T(8,128)(2,1)} %og.1) | copy-start | bytes 196612
  0.7 9.3 %copy-start.2 = (bf16[1,128,256]{2,1,0:T(8,128)(2,1)S(1)}, bf16[1,128,256]{2,1,0:T(8,128)(2,1)}, u32[]{:S(2)}) copy-start(bf16[1,128,256]{2,1,0:T(8,128)(2,1)} %v.1) | copy-start | bytes 196612
  0.7 9.3 %copy-start.1 = (bf16[1,128,256]{2,1,0:T(8,128)(2,1)S(1)}, bf16[1,128,256]{2,1,0:T(8,128)(2,1)}, u32[]{:S(2)}) copy-start(bf16[1,128,256]{2,1,0:T(8,128)(2,1)} %k.1) | copy-start | bytes 196612
  2.6 23.3 %all-to-all-start = ((bf16[8,32,1152]{2,1,0:T(8,128)(2,1)}), bf16[8,32,1152]{2,1,0:T(8,128)(2,1)S(1)}, u32[]{:S(2)}, u32[]{:S(2)}) async-start(bf16[8,32,1152]{2,1,0:T(8,128)(2,1)} %shard_map.164), calls=%async_computation | async-start | bytes 1179648 | tf_op jit(solution)/shard_map/all_to_all | solution.py:363
  9.9 0.7 copy-start.4
  10.6 0.7 copy-start.5
  11.4 14.5 %collective-permute-start = (bf16[128,768]{1,0:T(8,128)(2,1)S(1)}, bf16[128,768]{1,0:T(8,128)(2,1)S(1)}, u32[]{:S(2)}, u32[]{:S(2)}) collective-permute-start(bf16[128,768]{1,0:T(8,128)(2,1)S(1)} %get-tuple-element.64), channel_id=1, source_target_pairs={{0,1},{1,0},{2,3},{3,2},{4,5},{5,4},{6,7},{7,6},{8,9},{9,8},{10,11... | collective-permute-start | bytes 589832 | tf_op jit(solution)/shard_map/ppermute | solution.py:340
  13.5 9.8 %collective-permute-start.2 = (bf16[128,256]{1,0:T(8,128)(2,1)S(1)}, bf16[128,256]{1,0:T(8,128)(2,1)S(1)}, u32[]{:S(2)}, u32[]{:S(2)}) collective-permute-start(bf16[128,256]{1,0:T(8,128)(2,1)S(1)} %bitcast.8), channel_id=1, source_target_pairs={{0,3},{1,2},{2,1},{3,0},{4,7},{5,6},{6,5},{7,4},{8,11},{9,10},{10,... | collective-permute-start | bytes 196616 | tf_op jit(solution)/shard_map/ppermute | solution.py:340
  14.9 8.7 %collective-permute-start.1 = (bf16[128,256]{1,0:T(8,128)(2,1)S(1)}, bf16[128,256]{1,0:T(8,128)(2,1)S(1)}, u32[]{:S(2)}, u32[]{:S(2)}) collective-permute-start(bf16[128,256]{1,0:T(8,128)(2,1)S(1)} %bitcast.9), channel_id=1, source_target_pairs={{0,2},{1,3},{2,0},{3,1},{4,6},{5,7},{6,4},{7,5},{8,10},{9,11},{10,... | collective-permute-start | bytes 196616 | tf_op jit(solution)/shard_map/ppermute | solution.py:340
  15.0 15.2 %collective-permute-start.7 = (bf16[128,512]{1,0:T(8,128)(2,1)S(1)}, bf16[128,512]{1,0:T(8,128)(2,1)S(1)}, u32[]{:S(2)}, u32[]{:S(2)}) collective-permute-start(bf16[128,512]{1,0:T(8,128)(2,1)S(1)} %get-tuple-element.80.refs_0_), channel_id=1, source_target_pairs={{0,3},{1,2},{2,1},{3,0},{4,7},{5,6},{6,5},{7,4},{8,11},{9,10},{10,... | collective-permute-start | bytes 393224 | tf_op jit(solution)/shard_map/ppermute | solution.py:340
  17.9 12.9 %collective-permute-start.6 = (bf16[128,512]{1,0:T(8,128)(2,1)S(1)}, bf16[128,512]{1,0:T(8,128)(2,1)S(1)}, u32[]{:S(2)}, u32[]{:S(2)}) collective-permute-start(bf16[128,512]{1,0:T(8,128)(2,1)S(1)} %get-tuple-element.80.refs_0_), channel_id=1, source_target_pairs={{0,2},{1,3},{2,0},{3,1},{4,6},{5,7},{6,4},{7,5},{8,10},{9,11},{10,... | collective-permute-start | bytes 393224 | tf_op jit(solution)/shard_map/ppermute | solution.py:340
  26.7 5.4 %collective-permute-start.3 = (bf16[128,256]{1,0:T(8,128)(2,1)S(1)}, bf16[128,256]{1,0:T(8,128)(2,1)S(1)}, u32[]{:S(2)}, u32[]{:S(2)}) collective-permute-start(bf16[128,256]{1,0:T(8,128)(2,1)S(1)} %get-tuple-element.68), channel_id=1, source_target_pairs={{0,2},{1,3},{2,0},{3,1},{4,6},{5,7},{6,4},{7,5},{8,10},{9,11},{10,... | collective-permute-start | bytes 196616 | tf_op jit(solution)/shard_map/ppermute | solution.py:340
  28.5 5.5 %collective-permute-start.4 = (bf16[128,256]{1,0:T(8,128)(2,1)S(1)}, bf16[128,256]{1,0:T(8,128)(2,1)S(1)}, u32[]{:S(2)}, u32[]{:S(2)}) collective-permute-start(bf16[128,256]{1,0:T(8,128)(2,1)S(1)} %get-tuple-element.69), channel_id=1, source_target_pairs={{0,3},{1,2},{2,1},{3,0},{4,7},{5,6},{6,5},{7,4},{8,11},{9,10},{10,... | collective-permute-start | bytes 196616 | tf_op jit(solution)/shard_map/ppermute | solution.py:340
  29.7 4.9 %collective-permute-start.5 = (bf16[128,256]{1,0:T(8,128)(2,1)S(1)}, bf16[128,256]{1,0:T(8,128)(2,1)S(1)}, u32[]{:S(2)}, u32[]{:S(2)}) collective-permute-start(bf16[128,256]{1,0:T(8,128)(2,1)S(1)} %get-tuple-element.70), channel_id=1, source_target_pairs={{0,1},{1,0},{2,3},{3,2},{4,5},{5,4},{6,7},{7,6},{8,9},{9,8},{10,11... | collective-permute-start | bytes 196616 | tf_op jit(solution)/shard_map/ppermute | solution.py:340
  34.8 4.3 %collective-permute-start.10 = (f32[2,128]{1,0:T(2,128)S(1)}, f32[2,128]{1,0:T(2,128)S(1)}, u32[]{:S(2)}, u32[]{:S(2)}) collective-permute-start(f32[2,128]{1,0:T(2,128)S(1)} %get-tuple-element.78.refs_0_), channel_id=1, source_target_pairs={{0,24},{8,16},{16,8},{24,0},{1,25},{9,17},{17,9},{25,1},{2,26},{10... | collective-permute-start | bytes 3080 | tf_op jit(solution)/shard_map/ppermute | solution.py:340
  34.9 4.3 %collective-permute-start.9 = (f32[2,128]{1,0:T(2,128)S(1)}, f32[2,128]{1,0:T(2,128)S(1)}, u32[]{:S(2)}, u32[]{:S(2)}) collective-permute-start(f32[2,128]{1,0:T(2,128)S(1)} %get-tuple-element.78.refs_0_), channel_id=1, source_target_pairs={{0,16},{8,24},{16,0},{24,8},{1,17},{9,25},{17,1},{25,9},{2,18},{10... | collective-permute-start | bytes 3080 | tf_op jit(solution)/shard_map/ppermute | solution.py:340
  36.4 2.7 %collective-permute-start.8 = (f32[2,128]{1,0:T(2,128)S(1)}, f32[2,128]{1,0:T(2,128)S(1)}, u32[]{:S(2)}, u32[]{:S(2)}) collective-permute-start(f32[2,128]{1,0:T(2,128)S(1)} %get-tuple-element.78.refs_0_), channel_id=1, source_target_pairs={{0,8},{8,0},{16,24},{24,16},{1,9},{9,1},{17,25},{25,17},{2,10},{10... | collective-permute-start | bytes 3080 | tf_op jit(solution)/shard_map/ppermute | solution.py:340
  36.7 9.4 %collective-permute-start.15 = (bf16[128,256]{1,0:T(8,128)(2,1)S(1)}, bf16[128,256]{1,0:T(8,128)(2,1)S(1)}, u32[]{:S(2)}, u32[]{:S(2)}) collective-permute-start(bf16[128,256]{1,0:T(8,128)(2,1)S(1)} %bitcast.11), channel_id=1, source_target_pairs={{0,4},{1,5},{2,6},{3,7},{4,0},{5,1},{6,2},{7,3},{8,12},{9,13},{10,... | collective-permute-start | bytes 196616 | tf_op jit(solution)/shard_map/ppermute | solution.py:340
  39.3 6.8 %collective-permute-start.14 = (bf16[128,256]{1,0:T(8,128)(2,1)S(1)}, bf16[128,256]{1,0:T(8,128)(2,1)S(1)}, u32[]{:S(2)}, u32[]{:S(2)}) collective-permute-start(bf16[128,256]{1,0:T(8,128)(2,1)S(1)} %shard_map.167.refs_4_), channel_id=1, source_target_pairs={{0,4},{1,5},{2,6},{3,7},{4,0},{5,1},{6,2},{7,3},{8,12},{9,13},{10,... | collective-permute-start | bytes 196616 | tf_op jit(solution)/shard_map/ppermute | solution.py:340
  41.1 7.0 %collective-permute-start.13 = (bf16[128,256]{1,0:T(8,128)(2,1)S(1)}, bf16[128,256]{1,0:T(8,128)(2,1)S(1)}, u32[]{:S(2)}, u32[]{:S(2)}) collective-permute-start(bf16[128,256]{1,0:T(8,128)(2,1)S(1)} %shard_map.167.refs_4_), channel_id=1, source_target_pairs={{0,3},{1,2},{2,1},{3,0},{4,7},{5,6},{6,5},{7,4},{8,11},{9,10},{10,... | collective-permute-start | bytes 196616 | tf_op jit(solution)/shard_map/ppermute | solution.py:340
  42.2 7.5 %collective-permute-start.12 = (bf16[128,256]{1,0:T(8,128)(2,1)S(1)}, bf16[128,256]{1,0:T(8,128)(2,1)S(1)}, u32[]{:S(2)}, u32[]{:S(2)}) collective-permute-start(bf16[128,256]{1,0:T(8,128)(2,1)S(1)} %shard_map.167.refs_4_), channel_id=1, source_target_pairs={{0,2},{1,3},{2,0},{3,1},{4,6},{5,7},{6,4},{7,5},{8,10},{9,11},{10,... | collective-permute-start | bytes 196616 | tf_op jit(solution)/shard_map/ppermute | solution.py:340
  43.1 6.6 %collective-permute-start.11 = (bf16[128,256]{1,0:T(8,128)(2,1)S(1)}, bf16[128,256]{1,0:T(8,128)(2,1)S(1)}, u32[]{:S(2)}, u32[]{:S(2)}) collective-permute-start(bf16[128,256]{1,0:T(8,128)(2,1)S(1)} %shard_map.167.refs_4_), channel_id=1, source_target_pairs={{0,1},{1,0},{2,3},{3,2},{4,5},{5,4},{6,7},{7,6},{8,9},{9,8},{10,11... | collective-permute-start | bytes 196616 | tf_op jit(solution)/shard_map/ppermute | solution.py:340
  45.8 5.9 %copy-start.6 = (f32[4,512,192]{2,1,0:T(8,128)}, f32[4,512,192]{2,1,0:T(8,128)S(1)}, u32[]{:S(2)}) copy-start(f32[4,512,192]{2,1,0:T(8,128)S(1)} %get-tuple-element.84.factors) | copy-start | bytes 4718596
  45.8 5.9 %copy-start.8 = (bf16[3,512,192]{2,1,0:T(8,128)(2,1)}, bf16[3,512,192]{2,1,0:T(8,128)(2,1)S(1)}, u32[]{:S(2)}) copy-start(bf16[3,512,192]{2,1,0:T(8,128)(2,1)S(1)} %get-tuple-element.85.rises) | copy-start | bytes 1769476
  45.8 5.9 %copy-start.10 = (f32[3,256,192]{2,1,0:T(8,128)}, f32[3,256,192]{2,1,0:T(8,128)S(1)}, u32[]{:S(2)}) copy-start(f32[3,256,192]{2,1,0:T(8,128)S(1)} %get-tuple-element.88.minus) | copy-start | bytes 1769476
  45.8 5.9 %copy-start.12 = (f32[3,256,192]{2,1,0:T(8,128)}, f32[3,256,192]{2,1,0:T(8,128)S(1)}, u32[]{:S(2)}) copy-start(f32[3,256,192]{2,1,0:T(8,128)S(1)} %get-tuple-element.89.plus) | copy-start | bytes 1769476
  46.1 10.0 %collective-permute-start.18 = (bf16[128,512]{1,0:T(8,128)(2,1)S(1)}, bf16[128,512]{1,0:T(8,128)(2,1)S(1)}, u32[]{:S(2)}, u32[]{:S(2)}) collective-permute-start(bf16[128,512]{1,0:T(8,128)(2,1)S(1)} %shard_map.170.refs_4_), channel_id=1, source_target_pairs={{0,3},{1,2},{2,1},{3,0},{4,7},{5,6},{6,5},{7,4},{8,11},{9,10},{10,... | collective-permute-start | bytes 393224 | tf_op jit(solution)/shard_map/ppermute | solution.py:340
  47.0 9.0 %collective-permute-start.17 = (bf16[128,512]{1,0:T(8,128)(2,1)S(1)}, bf16[128,512]{1,0:T(8,128)(2,1)S(1)}, u32[]{:S(2)}, u32[]{:S(2)}) collective-permute-start(bf16[128,512]{1,0:T(8,128)(2,1)S(1)} %shard_map.170.refs_4_), channel_id=1, source_target_pairs={{0,2},{1,3},{2,0},{3,1},{4,6},{5,7},{6,4},{7,5},{8,10},{9,11},{10,... | collective-permute-start | bytes 393224 | tf_op jit(solution)/shard_map/ppermute | solution.py:340
  48.1 7.9 %collective-permute-start.16 = (bf16[128,512]{1,0:T(8,128)(2,1)S(1)}, bf16[128,512]{1,0:T(8,128)(2,1)S(1)}, u32[]{:S(2)}, u32[]{:S(2)}) collective-permute-start(bf16[128,512]{1,0:T(8,128)(2,1)S(1)} %shard_map.170.refs_4_), channel_id=1, source_target_pairs={{0,1},{1,0},{2,3},{3,2},{4,5},{5,4},{6,7},{7,6},{8,9},{9,8},{10,11... | collective-permute-start | bytes 393224 | tf_op jit(solution)/shard_map/ppermute | solution.py:340
  51.7 0.9 %copy-start.14 = (f32[3,256,192]{2,1,0:T(8,128)}, f32[3,256,192]{2,1,0:T(8,128)S(1)}, u32[]{:S(2)}) copy-start(f32[3,256,192]{2,1,0:T(8,128)S(1)} %get-tuple-element.79.grads) | copy-start | bytes 1769476
  52.6 12.1 %all-to-all-start.1 = ((bf16[4,128,256]{2,1,0:T(8,128)(2,1)}), bf16[4,128,256]{2,1,0:T(8,128)(2,1)S(1)}, u32[]{:S(2)}, u32[]{:S(2)}) async-start(bf16[4,128,256]{2,1,0:T(8,128)(2,1)} %get-tuple-element.99), calls=%async_computation.1 | async-start | bytes 524288 | tf_op jit(solution)/shard_map/all_to_all | solution.py:418
  56.1 1.6 %copy-start.7 = (f32[4,512,192]{2,1,0:T(8,128)S(1)}, f32[4,512,192]{2,1,0:T(8,128)}, u32[]{:S(2)}) copy-start(f32[4,512,192]{2,1,0:T(8,128)} %copy-done.6) | copy-start | bytes 4718596
  57.7 1.1 %copy-start.9 = (bf16[3,512,192]{2,1,0:T(8,128)(2,1)S(1)}, bf16[3,512,192]{2,1,0:T(8,128)(2,1)}, u32[]{:S(2)}) copy-start(bf16[3,512,192]{2,1,0:T(8,128)(2,1)} %copy-done.8) | copy-start | bytes 1769476
  58.8 1.1 %copy-start.11 = (f32[3,256,192]{2,1,0:T(8,128)S(1)}, f32[3,256,192]{2,1,0:T(8,128)}, u32[]{:S(2)}) copy-start(f32[3,256,192]{2,1,0:T(8,128)} %copy-done.10) | copy-start | bytes 1769476
  59.9 1.1 %copy-start.13 = (f32[3,256,192]{2,1,0:T(8,128)S(1)}, f32[3,256,192]{2,1,0:T(8,128)}, u32[]{:S(2)}) copy-start(f32[3,256,192]{2,1,0:T(8,128)} %copy-done.12) | copy-start | bytes 1769476
  61.1 1.1 %copy-start.15 = (f32[3,256,192]{2,1,0:T(8,128)S(1)}, f32[3,256,192]{2,1,0:T(8,128)}, u32[]{:S(2)}) copy-start(f32[3,256,192]{2,1,0:T(8,128)} %copy-done.14) | copy-start | bytes 1769476
  64.8 7.9 %collective-permute-start.19 = (bf16[672,128]{1,0:T(8,128)(2,1)S(1)}, bf16[672,128]{1,0:T(8,128)(2,1)S(1)}, u32[]{:S(2)}, u32[]{:S(2)}) collective-permute-start(bf16[672,128]{1,0:T(8,128)(2,1)S(1)} %get-tuple-element.102), channel_id=1, source_target_pairs={{0,1},{1,0},{2,3},{3,2},{4,5},{5,4},{6,7},{7,6},{8,9},{9,8},{10,11... | collective-permute-start | bytes 516104 | tf_op jit(solution)/shard_map/ppermute | solution.py:340
  66.8 8.6 %collective-permute-start.20 = (bf16[672,128]{1,0:T(8,128)(2,1)S(1)}, bf16[672,128]{1,0:T(8,128)(2,1)S(1)}, u32[]{:S(2)}, u32[]{:S(2)}) collective-permute-start(bf16[672,128]{1,0:T(8,128)(2,1)S(1)} %get-tuple-element.103), channel_id=1, source_target_pairs={{0,2},{1,3},{2,0},{3,1},{4,6},{5,7},{6,4},{7,5},{8,10},{9,11},{10,... | collective-permute-start | bytes 516104 | tf_op jit(solution)/shard_map/ppermute | solution.py:340
  68.3 9.8 %collective-permute-start.21 = (bf16[672,128]{1,0:T(8,128)(2,1)S(1)}, bf16[672,128]{1,0:T(8,128)(2,1)S(1)}, u32[]{:S(2)}, u32[]{:S(2)}) collective-permute-start(bf16[672,128]{1,0:T(8,128)(2,1)S(1)} %get-tuple-element.104), channel_id=1, source_target_pairs={{0,3},{1,2},{2,1},{3,0},{4,7},{5,6},{6,5},{7,4},{8,11},{9,10},{10,... | collective-permute-start | bytes 516104 | tf_op jit(solution)/shard_map/ppermute | solution.py:340
  68.3 10.4 %collective-permute-start.22 = (bf16[32,576]{1,0:T(8,128)(2,1)S(1)}, bf16[32,576]{1,0:T(8,128)(2,1)S(1)}, u32[]{:S(2)}, u32[]{:S(2)}) collective-permute-start(bf16[32,576]{1,0:T(8,128)(2,1)S(1)} %get-tuple-element.109), channel_id=1, source_target_pairs={{0,4},{1,5},{2,6},{3,7},{4,0},{5,1},{6,2},{7,3},{8,12},{9,13},{10,... | collective-permute-start | bytes 110600 | tf_op jit(solution)/shard_map/ppermute | solution.py:340
  69.8 9.0 %collective-permute-start.23 = (bf16[32,576]{1,0:T(8,128)(2,1)S(1)}, bf16[32,576]{1,0:T(8,128)(2,1)S(1)}, u32[]{:S(2)}, u32[]{:S(2)}) collective-permute-start(bf16[32,576]{1,0:T(8,128)(2,1)S(1)} %get-tuple-element.110), channel_id=1, source_target_pairs={{0,5},{1,4},{2,7},{3,6},{4,1},{5,0},{6,3},{7,2},{8,13},{9,12},{10,... | collective-permute-start | bytes 110600 | tf_op jit(solution)/shard_map/ppermute | solution.py:340
  72.7 6.4 %collective-permute-start.24 = (bf16[32,576]{1,0:T(8,128)(2,1)S(1)}, bf16[32,576]{1,0:T(8,128)(2,1)S(1)}, u32[]{:S(2)}, u32[]{:S(2)}) collective-permute-start(bf16[32,576]{1,0:T(8,128)(2,1)S(1)} %get-tuple-element.111), channel_id=1, source_target_pairs={{0,6},{1,7},{2,4},{3,5},{4,2},{5,3},{6,0},{7,1},{8,14},{9,15},{10,... | collective-permute-start | bytes 110600 | tf_op jit(solution)/shard_map/ppermute | solution.py:340
  75.4 6.7 %collective-permute-start.25 = (bf16[32,576]{1,0:T(8,128)(2,1)S(1)}, bf16[32,576]{1,0:T(8,128)(2,1)S(1)}, u32[]{:S(2)}, u32[]{:S(2)}) collective-permute-start(bf16[32,576]{1,0:T(8,128)(2,1)S(1)} %get-tuple-element.112), channel_id=1, source_target_pairs={{0,7},{1,6},{2,5},{3,4},{4,3},{5,2},{6,1},{7,0},{8,15},{9,14},{10,... | collective-permute-start | bytes 110600 | tf_op jit(solution)/shard_map/ppermute | solution.py:340

commit v13 on v12

--- a/solution.py
+++ b/solution.py
@@ -198,14 +198,14 @@
     return delta_gate, delta_up, grads
 
 
-def near_kernel(slab, group, place, normed_ref, *refs):
-    q_near, od_near, (grad_q, grads_out) = refs[:group], refs[group : 2 * group], refs[2 * group :]
+def near_kernel(slab, group, normed_ref, *refs):
+    q_near, od_near, (*grad_qs, grads_out) = refs[:group], refs[group : 2 * group], refs[2 * group :]
     own = od_near[0].shape[0]
     normed = thirds(normed_ref, slab)
     delta_gate, delta_up, grads = query_side(stack(q_near, slice(0, od_near[0].shape[1])), stack(od_near), normed)
     found = (mm_nt(delta_gate, normed[0]) + mm_nt(delta_up, normed[1])).astype(BF)
     for d in range(group):
-        grad_q[place[1] ^ d] = found[d * own : (d + 1) * own]
+        grad_qs[d][...] = found[d * own : (d + 1) * own]
     for i in range(3):
         grads_out[i] = grads[i]
 
@@ -302,13 +302,10 @@
     return total
 
 
-def tokens_kernel(rate, queries, tok, *refs):
-    blocks, (gq, gk, gv) = refs[:-3], refs[-3:]
+def tokens_kernel(group, rate, tok, *refs):
+    queries, blocks, (gq, gk, gv) = refs[:group], refs[group:-3], refs[-3:]
     _, own, feat = gq.shape
-    total = queries[0].astype(F32)
-    for j in range(1, queries.shape[0]):
-        total += queries[j].astype(F32)
-    gq[0] = total.astype(BF)
+    gq[0] = total_of(queries).astype(BF)
     sums = [tok[:, i * feat : (i + 1) * feat].astype(F32) for i in range(2)]
     for block in blocks:
         at = 0
@@ -334,7 +331,6 @@
 
 def make_local(seq_n, head_n, group):
     tok_groups = seq_n // group
-    groups = [[t * group + j for j in range(group)] for t in range(tok_groups)]
 
     def move(x, dist, axis="seq", size=seq_n):
         return lax.ppermute(x, axis, [(i, i ^ dist) for i in range(size)])
@@ -405,17 +401,16 @@
             call(pair_kernel, (arr((own, 2 * feat), BF),), pair, 16)[0] for pair in zip(od_mirror, q_mirror)
         ]
         pairs = [x for m in pairs for x in near_all(m)]
-        grad_q, grads = call(
+        *grad_q, grads = call(
             functools.partial(near_kernel, slab, group),
-            (arr((group, own, feat), BF), arr((3, seq_n * rows, slab), F32)),
-            (place, normed, *q_near, *od_near),
+            (*(block,) * group, arr((3, seq_n * rows, slab), F32)),
+            (normed, *q_near, *od_near),
             12,
-            smem=1,
             flops=60 * mflop,
         )
 
         q_block = (own, feat)
-        grad_q = lax.all_to_all(grad_q, "seq", 0, 0, axis_index_groups=groups, tiled=True)
+        grad_q = [grad_q[0]] + [move(grad_q[d], d) for d in (*range(2, group), *range(1, min(2, group)))]
         tok, inner, *sends = call(
             functools.partial(backward_kernel, slab, group, tok_groups),
             (
@@ -439,7 +434,9 @@
         far_got = [move(sends[d - 1], d) for d in range(group, seq_n)]
         out_tok = arr((1, own, feat), BF)
         grad_w = arr((1, rows, hidden), F32)
-        grads_t = call(tokens_kernel, (out_tok,) * 3, (rate, grad_q, tok, *near_got), 16)
+        grads_t = call(
+            functools.partial(tokens_kernel, group), (out_tok,) * 3, (rate, tok, *grad_q, *near_got), 16
+        )
         at = 2 * tiles(feat) * padded(own)
         grads_w = call(
             functools.partial(weights_kernel, group, slab, at),

time: 84.1 us -> 79.4 us (0.944)
  local copies, waits for them, and re-layouts: 8.39 us -> 1.35 us
  waiting for transfers between devices: 16.9 us -> 22 us
  starting transfers between devices: 46.3 us -> 45 us
  Pallas kernels: 11 us -> 9.95 us
    unnamed x32 -> x12, local copies, waits for them, and re-layouts: 8.39 us -> 1.35 us
    ppermute x26 -> x29, waiting for transfers between devices: 16.9 us -> 22 us  [move(): return lax.ppermute(x, axis, [(i, i ^ dist) for i in range(size)])]
    all_to_all x1 -> x0, starting transfers between devices: 3.4 us -> none  [local(): lax.all_to_all(grad_q, 'seq', 0, 0, axis_index_groups=groups, tiled=True)]
    ppermute x26 -> x29, starting transfers between devices: 35.6 us -> 37.8 us  [move(): return lax.ppermute(x, axis, [(i, i ^ dist) for i in range(size)])]
    pallas_call x10, Pallas kernels: 9.01 us -> 7.99 us  [call(): pl.pallas_call(kernel, out_shape=outs, in_specs=[SMEM] * smem + [VMEM] *...]
  transfers between devices with their start and end apart: 28 -> 30, of which waited for: 11 -> 15; matrix products, arithmetic and copies ran while one was open for 0% -> 0% of each run, Pallas kernels for 9% -> 7%
where the time goes in v13:
time: 79.4 us; the launch traced here: 79.2 us
  starting transfers between devices  45 us (57%)
  waiting for transfers between devices  22 us (28%)
  Pallas kernels  9.95 us (13%)
  local copies, waits for them, and re-layouts  1.35 us (2%)
  between operations  0.82 us (1%)
    ppermute x29, starting transfers between devices, move(): return lax.ppermute(x, axis, [(i, i ^ dist) for i in range(size)])  37.8 us
    ppermute x29, waiting for transfers between devices, move(): return lax.ppermute(x, axis, [(i, i ^ dist) for i in range(size)])  22 us
    pallas_call x10, Pallas kernels, call(): pl.pallas_call(kernel, out_shape=outs, in_specs=[SMEM] * smem + [VMEM] *...  7.99 us
    all_to_all x1, starting transfers between devices, local(): lax.all_to_all(packed, 'seq', 0, 0, tiled=True)  7.26 us
    pallas_call x1, Pallas kernels, copying_call(): pl.pallas_call(kernel, out_shape=outs, in_specs=[pl.BlockSpec(memory_spac...  1.96 us
  transfers between devices with their start and end apart: 30, of which 15 were waited for; matrix products, arithmetic and copies ran while one was open for 0% of the time, Pallas kernels for 7%

profile of v13, /device:TPU:0, one launch (start us, length us, event | category | flops | bytes accessed | tf_op | source)
XLA Modules:
  0.0 79.2 jit_solution(5844625481335274996)
XLA Ops:
  0.7 2.0 %shard_map.164 = bf16[8,32,1152]{2,1,0:T(8,128)(2,1)} custom-call(bf16[1,32,768]{2,1,0:T(8,128)(2,1)} %refs_0_.1, bf16[1,32,768]{2,1,0:T(8,128)(2,1)} %refs_1_.1, bf16[1,32,768]{2,1,0:T(8,128)(2,1)} %refs_2_.1, bf16[1,32,768]{2,1,0:T(8,128)(2,1)} %refs_3_.1, bf16[1,32,768]{2,1,0:T(8,128)(2,1)} %refs_4_.1, bf16[1,32,768]{2,1,0:T(8,128)(2,1)} %refs_5_.1), custom_call_target="tpu_custom_call" | custom-call | tf_op jit(solution)/shard_map/pallas_call | solution.py:61
  2.6 7.3 %all-to-all-start = ((bf16[8,32,1152]{2,1,0:T(8,128)(2,1)}), bf16[8,32,1152]{2,1,0:T(8,128)(2,1)S(1)}, u32[]{:S(2)}, u32[]{:S(2)}) async-start(bf16[8,32,1152]{2,1,0:T(8,128)(2,1)} %shard_map.164), calls=%async_computation | async-start | bytes 1179648 | tf_op jit(solution)/shard_map/all_to_all | solution.py:359
  9.9 0.0 copy-start.4
  10.0 0.7 copy-done.4
  10.6 0.7 copy-done.5
  11.3 0.1 shard_map.163
  11.4 2.1 %collective-permute-start = (bf16[128,768]{1,0:T(8,128)(2,1)S(1)}, bf16[128,768]{1,0:T(8,128)(2,1)S(1)}, u32[]{:S(2)}, u32[]{:S(2)}) collective-permute-start(bf16[128,768]{1,0:T(8,128)(2,1)S(1)} %get-tuple-element.70), channel_id=1, source_target_pairs={{0,1},{1,0},{2,3},{3,2},{4,5},{5,4},{6,7},{7,6},{8,9},{9,8},{10,11... | collective-permute-start | bytes 589832 | tf_op jit(solution)/shard_map/ppermute | solution.py:336
  13.5 1.5 %collective-permute-start.2 = (bf16[128,256]{1,0:T(8,128)(2,1)S(1)}, bf16[128,256]{1,0:T(8,128)(2,1)S(1)}, u32[]{:S(2)}, u32[]{:S(2)}) collective-permute-start(bf16[128,256]{1,0:T(8,128)(2,1)S(1)} %bitcast.8), channel_id=1, source_target_pairs={{0,3},{1,2},{2,1},{3,0},{4,7},{5,6},{6,5},{7,4},{8,11},{9,10},{10,... | collective-permute-start | bytes 196616 | tf_op jit(solution)/shard_map/ppermute | solution.py:336
  14.9 0.1 collective-permute-start.1
  15.0 2.8 %collective-permute-start.7 = (bf16[128,512]{1,0:T(8,128)(2,1)S(1)}, bf16[128,512]{1,0:T(8,128)(2,1)S(1)}, u32[]{:S(2)}, u32[]{:S(2)}) collective-permute-start(bf16[128,512]{1,0:T(8,128)(2,1)S(1)} %get-tuple-element.86.refs_0_), channel_id=1, source_target_pairs={{0,3},{1,2},{2,1},{3,0},{4,7},{5,6},{6,5},{7,4},{8,11},{9,10},{10,... | collective-permute-start | bytes 393224 | tf_op jit(solution)/shard_map/ppermute | solution.py:336
  17.9 0.6 collective-permute-start.6
  18.4 4.8 %collective-permute-done.2.refs_3_ = bf16[128,256]{1,0:T(8,128)(2,1)S(1)} collective-permute-done((bf16[128,256]{1,0:T(8,128)(2,1)S(1)}, bf16[128,256]{1,0:T(8,128)(2,1)S(1)}, u32[]{:S(2)}, u32[]{:S(2)}) %collective-permute-start.2) | collective-permute-done | bytes 65568 | tf_op jit(solution)/shard_map/ppermute | solution.py:336
  23.3 0.4 collective-permute-done.1.refs_2_
  23.6 2.3 %collective-permute-done.refs_1_ = bf16[128,768]{1,0:T(8,128)(2,1)S(1)} collective-permute-done((bf16[128,768]{1,0:T(8,128)(2,1)S(1)}, bf16[128,768]{1,0:T(8,128)(2,1)S(1)}, u32[]{:S(2)}, u32[]{:S(2)}) %collective-permute-start) | collective-permute-done | bytes 196640 | tf_op jit(solution)/shard_map/ppermute | solution.py:336
  25.9 0.8 shard_map.165
  26.7 1.8 %collective-permute-start.3 = (bf16[128,256]{1,0:T(8,128)(2,1)S(1)}, bf16[128,256]{1,0:T(8,128)(2,1)S(1)}, u32[]{:S(2)}, u32[]{:S(2)}) collective-permute-start(bf16[128,256]{1,0:T(8,128)(2,1)S(1)} %get-tuple-element.74), channel_id=1, source_target_pairs={{0,2},{1,3},{2,0},{3,1},{4,6},{5,7},{6,4},{7,5},{8,10},{9,11},{10,... | collective-permute-start | bytes 196616 | tf_op jit(solution)/shard_map/ppermute | solution.py:336
  28.5 1.1 %collective-permute-start.4 = (bf16[128,256]{1,0:T(8,128)(2,1)S(1)}, bf16[128,256]{1,0:T(8,128)(2,1)S(1)}, u32[]{:S(2)}, u32[]{:S(2)}) collective-permute-start(bf16[128,256]{1,0:T(8,128)(2,1)S(1)} %get-tuple-element.75), channel_id=1, source_target_pairs={{0,3},{1,2},{2,1},{3,0},{4,7},{5,6},{6,5},{7,4},{8,11},{9,10},{10,... | collective-permute-start | bytes 196616 | tf_op jit(solution)/shard_map/ppermute | solution.py:336
  29.7 0.6 collective-permute-start.5
  30.3 0.5 collective-permute-done.6.refs_2_
  30.7 1.4 %collective-permute-done.3.refs_1_ = bf16[128,256]{1,0:T(8,128)(2,1)S(1)} collective-permute-done((bf16[128,256]{1,0:T(8,128)(2,1)S(1)}, bf16[128,256]{1,0:T(8,128)(2,1)S(1)}, u32[]{:S(2)}, u32[]{:S(2)}) %collective-permute-start.3) | collective-permute-done | bytes 65568 | tf_op jit(solution)/shard_map/ppermute | solution.py:336
  32.1 1.9 %collective-permute-done.4.refs_2_ = bf16[128,256]{1,0:T(8,128)(2,1)S(1)} collective-permute-done((bf16[128,256]{1,0:T(8,128)(2,1)S(1)}, bf16[128,256]{1,0:T(8,128)(2,1)S(1)}, u32[]{:S(2)}, u32[]{:S(2)}) %collective-permute-start.4) | collective-permute-done | bytes 65568 | tf_op jit(solution)/shard_map/ppermute | solution.py:336
  34.0 0.6 collective-permute-done.5.refs_3_
  34.6 0.1 shard_map.166
  34.8 0.1 collective-permute-start.10
  34.9 1.6 %collective-permute-start.9 = (f32[2,128]{1,0:T(2,128)S(1)}, f32[2,128]{1,0:T(2,128)S(1)}, u32[]{:S(2)}, u32[]{:S(2)}) collective-permute-start(f32[2,128]{1,0:T(2,128)S(1)} %get-tuple-element.84.refs_0_), channel_id=1, source_target_pairs={{0,16},{8,24},{16,0},{24,8},{1,17},{9,25},{17,1},{25,9},{2,18},{10... | collective-permute-start | bytes 3080 | tf_op jit(solution)/shard_map/ppermute | solution.py:336
  36.4 0.3 collective-permute-start.8
  36.7 2.4 %collective-permute-start.15 = (bf16[128,256]{1,0:T(8,128)(2,1)S(1)}, bf16[128,256]{1,0:T(8,128)(2,1)S(1)}, u32[]{:S(2)}, u32[]{:S(2)}) collective-permute-start(bf16[128,256]{1,0:T(8,128)(2,1)S(1)} %bitcast.11), channel_id=1, source_target_pairs={{0,4},{1,5},{2,6},{3,7},{4,0},{5,1},{6,2},{7,3},{8,12},{9,13},{10,... | collective-permute-start | bytes 196616 | tf_op jit(solution)/shard_map/ppermute | solution.py:336
  39.1 0.0 collective-permute-done.10.refs_3_
  39.1 0.0 collective-permute-done.9.refs_2_
  39.1 0.0 collective-permute-done.8.refs_1_
  39.1 0.1 shard_map.167.refs_4_
  39.3 1.8 %collective-permute-start.14 = (bf16[128,256]{1,0:T(8,128)(2,1)S(1)}, bf16[128,256]{1,0:T(8,128)(2,1)S(1)}, u32[]{:S(2)}, u32[]{:S(2)}) collective-permute-start(bf16[128,256]{1,0:T(8,128)(2,1)S(1)} %shard_map.167.refs_4_), channel_id=1, source_target_pairs={{0,4},{1,5},{2,6},{3,7},{4,0},{5,1},{6,2},{7,3},{8,12},{9,13},{10,... | collective-permute-start | bytes 196616 | tf_op jit(solution)/shard_map/ppermute | solution.py:336
  41.1 1.1 %collective-permute-start.13 = (bf16[128,256]{1,0:T(8,128)(2,1)S(1)}, bf16[128,256]{1,0:T(8,128)(2,1)S(1)}, u32[]{:S(2)}, u32[]{:S(2)}) collective-permute-start(bf16[128,256]{1,0:T(8,128)(2,1)S(1)} %shard_map.167.refs_4_), channel_id=1, source_target_pairs={{0,3},{1,2},{2,1},{3,0},{4,7},{5,6},{6,5},{7,4},{8,11},{9,10},{10,... | collective-permute-start | bytes 196616 | tf_op jit(solution)/shard_map/ppermute | solution.py:336
  42.2 0.9 %collective-permute-start.12 = (bf16[128,256]{1,0:T(8,128)(2,1)S(1)}, bf16[128,256]{1,0:T(8,128)(2,1)S(1)}, u32[]{:S(2)}, u32[]{:S(2)}) collective-permute-start(bf16[128,256]{1,0:T(8,128)(2,1)S(1)} %shard_map.167.refs_4_), channel_id=1, source_target_pairs={{0,2},{1,3},{2,0},{3,1},{4,6},{5,7},{6,4},{7,5},{8,10},{9,11},{10,... | collective-permute-start | bytes 196616 | tf_op jit(solution)/shard_map/ppermute | solution.py:336
  43.1 1.5 %collective-permute-start.11 = (bf16[128,256]{1,0:T(8,128)(2,1)S(1)}, bf16[128,256]{1,0:T(8,128)(2,1)S(1)}, u32[]{:S(2)}, u32[]{:S(2)}) collective-permute-start(bf16[128,256]{1,0:T(8,128)(2,1)S(1)} %shard_map.167.refs_4_), channel_id=1, source_target_pairs={{0,1},{1,0},{2,3},{3,2},{4,5},{5,4},{6,7},{7,6},{8,9},{9,8},{10,11... | collective-permute-start | bytes 196616 | tf_op jit(solution)/shard_map/ppermute | solution.py:336
  44.6 0.1 pad_add_fusion.place
  44.7 1.1 %shard_map.169 = (f32[4,512,192]{2,1,0:T(8,128)S(1)}, bf16[3,512,192]{2,1,0:T(8,128)(2,1)S(1)}, f32[3,192]{1,0:T(4,128)S(1)}, f32[3,256,192]{2,1,0:T(8,128)S(1)}, f32[3,256,192]{2,1,0:T(8,128)S(1)}) custom-call(bf16[256,1152]{1,0:T(8,128)(2,1)S(1)} %bitcast.6, bf16[128,512]{1,0:T(8,128)(2,1)S(1)} %get-tuple-element.86.refs_0_, ...), custom_call_target="tpu_custom_call" | custom-call | flops 603979776 | bytes 4524288 | tf_op jit(solution)/shard_map/pallas_call | solution.py:49
  45.8 0.3 collective-permute-done.14.left
  46.1 0.9 %collective-permute-start.18 = (bf16[128,512]{1,0:T(8,128)(2,1)S(1)}, bf16[128,512]{1,0:T(8,128)(2,1)S(1)}, u32[]{:S(2)}, u32[]{:S(2)}) collective-permute-start(bf16[128,512]{1,0:T(8,128)(2,1)S(1)} %shard_map.170.refs_4_), channel_id=1, source_target_pairs={{0,3},{1,2},{2,1},{3,0},{4,7},{5,6},{6,5},{7,4},{8,11},{9,10},{10,... | collective-permute-start | bytes 393224 | tf_op jit(solution)/shard_map/ppermute | solution.py:336
  47.0 1.1 %collective-permute-start.17 = (bf16[128,512]{1,0:T(8,128)(2,1)S(1)}, bf16[128,512]{1,0:T(8,128)(2,1)S(1)}, u32[]{:S(2)}, u32[]{:S(2)}) collective-permute-start(bf16[128,512]{1,0:T(8,128)(2,1)S(1)} %shard_map.170.refs_4_), channel_id=1, source_target_pairs={{0,2},{1,3},{2,0},{3,1},{4,6},{5,7},{6,4},{7,5},{8,10},{9,11},{10,... | collective-permute-start | bytes 393224 | tf_op jit(solution)/shard_map/ppermute | solution.py:336
  48.1 1.5 %collective-permute-start.16 = (bf16[128,512]{1,0:T(8,128)(2,1)S(1)}, bf16[128,512]{1,0:T(8,128)(2,1)S(1)}, u32[]{:S(2)}, u32[]{:S(2)}) collective-permute-start(bf16[128,512]{1,0:T(8,128)(2,1)S(1)} %shard_map.170.refs_4_), channel_id=1, source_target_pairs={{0,1},{1,0},{2,3},{3,2},{4,5},{5,4},{6,7},{7,6},{8,9},{9,8},{10,11... | collective-permute-start | bytes 393224 | tf_op jit(solution)/shard_map/ppermute | solution.py:336
  49.6 0.8 %shard_map.168 = (bf16[128,256]{1,0:T(8,128)(2,1)S(1)}, bf16[128,256]{1,0:T(8,128)(2,1)S(1)}, bf16[128,256]{1,0:T(8,128)(2,1)S(1)}, bf16[128,256]{1,0:T(8,128)(2,1)S(1)}, f32[3,256,192]{2,1,0:T(8,128)S(1)}) custom-call(bf16[256,576]{1,0:T(8,128)(2,1)S(1)} %get-tuple-element.71.normed_ref, bf16[128,256]{1,0:T(8,128)(2,1)S(1)} %bitcast.12, ...), custom_call_target="tpu_custom_call" | custom-call | flops 3019898880 | bytes 1802240 | tf_op jit(solution)/shard_map/pallas_call | solution.py:49
  50.5 0.1 collective-permute-start.19
  50.6 2.0 %collective-permute-start.20 = (bf16[128,256]{1,0:T(8,128)(2,1)S(1)}, bf16[128,256]{1,0:T(8,128)(2,1)S(1)}, u32[]{:S(2)}, u32[]{:S(2)}) collective-permute-start(bf16[128,256]{1,0:T(8,128)(2,1)S(1)} %get-tuple-element.108), channel_id=1, source_target_pairs={{0,3},{1,2},{2,1},{3,0},{4,7},{5,6},{6,5},{7,4},{8,11},{9,10},{10,... | collective-permute-start | bytes 196616 | tf_op jit(solution)/shard_map/ppermute | solution.py:336
  52.5 0.9 %collective-permute-done.18.refs_7_ = bf16[128,512]{1,0:T(8,128)(2,1)S(1)} collective-permute-done((bf16[128,512]{1,0:T(8,128)(2,1)S(1)}, bf16[128,512]{1,0:T(8,128)(2,1)S(1)}, u32[]{:S(2)}, u32[]{:S(2)}) %collective-permute-start.18) | collective-permute-done | bytes 131104 | tf_op jit(solution)/shard_map/ppermute | solution.py:336
  53.4 0.6 collective-permute-start.21
  54.0 1.3 %collective-permute-done.17.refs_6_ = bf16[128,512]{1,0:T(8,128)(2,1)S(1)} collective-permute-done((bf16[128,512]{1,0:T(8,128)(2,1)S(1)}, bf16[128,512]{1,0:T(8,128)(2,1)S(1)}, u32[]{:S(2)}, u32[]{:S(2)}) %collective-permute-start.17) | collective-permute-done | bytes 131104 | tf_op jit(solution)/shard_map/ppermute | solution.py:336
  55.3 0.1 collective-permute-done.16.refs_5_
  55.4 2.8 %shard_map.171 = (bf16[128,512]{1,0:T(8,128)(2,1)S(1)}, bf16[32,576]{1,0:T(8,128)(2,1)S(1)}, bf16[672,128]{1,0:T(8,128)(2,1)S(1)}, bf16[672,128]{1,0:T(8,128)(2,...) custom-call(s32[3]{0:T(128)S(1)} %pad_add_fusion.place, ...), custom_call_target="tpu_custom_call" | custom-call | flops 6039797760 | bytes 6764812 | tf_op jit(solution)/shard_map/pallas_call | solution.py:49
  58.2 0.0 collective-permute-done.19.refs_1_
  58.2 0.2 collective-permute-done.21.refs_3_
  58.4 1.3 %collective-permute-start.22 = (bf16[672,128]{1,0:T(8,128)(2,1)S(1)}, bf16[672,128]{1,0:T(8,128)(2,1)S(1)}, u32[]{:S(2)}, u32[]{:S(2)}) collective-permute-start(bf16[672,128]{1,0:T(8,128)(2,1)S(1)} %get-tuple-element.114), channel_id=1, source_target_pairs={{0,1},{1,0},{2,3},{3,2},{4,5},{5,4},{6,7},{7,6},{8,9},{9,8},{10,11... | collective-permute-start | bytes 516104 | tf_op jit(solution)/shard_map/ppermute | solution.py:336
  59.7 0.4 collective-permute-start.23
  60.1 1.8 %collective-permute-start.24 = (bf16[672,128]{1,0:T(8,128)(2,1)S(1)}, bf16[672,128]{1,0:T(8,128)(2,1)S(1)}, u32[]{:S(2)}, u32[]{:S(2)}) collective-permute-start(bf16[672,128]{1,0:T(8,128)(2,1)S(1)} %get-tuple-element.116), channel_id=1, source_target_pairs={{0,3},{1,2},{2,1},{3,0},{4,7},{5,6},{6,5},{7,4},{8,11},{9,10},{10,... | collective-permute-start | bytes 516104 | tf_op jit(solution)/shard_map/ppermute | solution.py:336
  61.9 1.4 %collective-permute-start.25 = (bf16[32,576]{1,0:T(8,128)(2,1)S(1)}, bf16[32,576]{1,0:T(8,128)(2,1)S(1)}, u32[]{:S(2)}, u32[]{:S(2)}) collective-permute-start(bf16[32,576]{1,0:T(8,128)(2,1)S(1)} %get-tuple-element.121), channel_id=1, source_target_pairs={{0,4},{1,5},{2,6},{3,7},{4,0},{5,1},{6,2},{7,3},{8,12},{9,13},{10,... | collective-permute-start | bytes 110600 | tf_op jit(solution)/shard_map/ppermute | solution.py:336
  63.3 2.2 %collective-permute-start.26 = (bf16[32,576]{1,0:T(8,128)(2,1)S(1)}, bf16[32,576]{1,0:T(8,128)(2,1)S(1)}, u32[]{:S(2)}, u32[]{:S(2)}) collective-permute-start(bf16[32,576]{1,0:T(8,128)(2,1)S(1)} %get-tuple-element.122), channel_id=1, source_target_pairs={{0,5},{1,4},{2,7},{3,6},{4,1},{5,0},{6,3},{7,2},{8,13},{9,12},{10,... | collective-permute-start | bytes 110600 | tf_op jit(solution)/shard_map/ppermute | solution.py:336
  65.5 2.5 %collective-permute-done.25.refs_3_ = bf16[32,576]{1,0:T(8,128)(2,1)S(1)} collective-permute-done((bf16[32,576]{1,0:T(8,128)(2,1)S(1)}, bf16[32,576]{1,0:T(8,128)(2,1)S(1)}, u32[]{:S(2)}, u32[]{:S(2)}) %collective-permute-start.25) | collective-permute-done | bytes 36896 | tf_op jit(solution)/shard_map/ppermute | solution.py:336
  68.1 2.3 %collective-permute-start.27 = (bf16[32,576]{1,0:T(8,128)(2,1)S(1)}, bf16[32,576]{1,0:T(8,128)(2,1)S(1)}, u32[]{:S(2)}, u32[]{:S(2)}) collective-permute-start(bf16[32,576]{1,0:T(8,128)(2,1)S(1)} %get-tuple-element.123), channel_id=1, source_target_pairs={{0,6},{1,7},{2,4},{3,5},{4,2},{5,3},{6,0},{7,1},{8,14},{9,15},{10,... | collective-permute-start | bytes 110600 | tf_op jit(solution)/shard_map/ppermute | solution.py:336
  70.3 2.0 %collective-permute-start.28 = (bf16[32,576]{1,0:T(8,128)(2,1)S(1)}, bf16[32,576]{1,0:T(8,128)(2,1)S(1)}, u32[]{:S(2)}, u32[]{:S(2)}) collective-permute-start(bf16[32,576]{1,0:T(8,128)(2,1)S(1)} %get-tuple-element.124), channel_id=1, source_target_pairs={{0,7},{1,6},{2,5},{3,4},{4,3},{5,2},{6,1},{7,0},{8,15},{9,14},{10,... | collective-permute-start | bytes 110600 | tf_op jit(solution)/shard_map/ppermute | solution.py:336
  72.3 1.6 %collective-permute-done.27.refs_5_ = bf16[32,576]{1,0:T(8,128)(2,1)S(1)} collective-permute-done((bf16[32,576]{1,0:T(8,128)(2,1)S(1)}, bf16[32,576]{1,0:T(8,128)(2,1)S(1)}, u32[]{:S(2)}, u32[]{:S(2)}) %collective-permute-start.27) | collective-permute-done | bytes 36896 | tf_op jit(solution)/shard_map/ppermute | solution.py:336
  73.9 3.2 %collective-permute-done.28.refs_6_ = bf16[32,576]{1,0:T(8,128)(2,1)S(1)} collective-permute-done((bf16[32,576]{1,0:T(8,128)(2,1)S(1)}, bf16[32,576]{1,0:T(8,128)(2,1)S(1)}, u32[]{:S(2)}, u32[]{:S(2)}) %collective-permute-start.28) | collective-permute-done | bytes 36896 | tf_op jit(solution)/shard_map/ppermute | solution.py:336
  77.0 0.0 collective-permute-done.23.refs_5_.refs_1_
  77.0 1.4 %shard_map.173 = (f32[1,32,768]{2,1,0:T(8,128)}, f32[1,32,768]{2,1,0:T(8,128)}, f32[1,32,768]{2,1,0:T(8,128)}) custom-call(s32[3]{0:T(128)S(1)} %pad_add_fusion.place, bf16[32,576]{1,0:T(8,128)(2,1)S(1)} %get-tuple-element.120.inner, bf16[672,128]{1,0:T(8,128)(2,1)S(1)} %collective-permute-done.22.refs_4_.refs_0_, ...), custom_call_target="tpu_custom_call" | custom-call | bytes 995340 | tf_op jit(solution)/shard_map/pallas_call | solution.py:49
  78.4 0.7 shard_map.172
  (20 shorter events, 0.1 us)
Async XLA Ops:
  0.6 9.3 %copy-start = (bf16[1,128,256]{2,1,0:T(8,128)(2,1)S(1)}, bf16[1,128,256]{2,1,0:T(8,128)(2,1)}, u32[]{:S(2)}) copy-start(bf16[1,128,256]{2,1,0:T(8,128)(2,1)} %q.1) | copy-start | bytes 196612
  0.6 9.3 %copy-start.3 = (bf16[1,128,256]{2,1,0:T(8,128)(2,1)S(1)}, bf16[1,128,256]{2,1,0:T(8,128)(2,1)}, u32[]{:S(2)}) copy-start(bf16[1,128,256]{2,1,0:T(8,128)(2,1)} %og.1) | copy-start | bytes 196612
  0.7 9.3 %copy-start.2 = (bf16[1,128,256]{2,1,0:T(8,128)(2,1)S(1)}, bf16[1,128,256]{2,1,0:T(8,128)(2,1)}, u32[]{:S(2)}) copy-start(bf16[1,128,256]{2,1,0:T(8,128)(2,1)} %v.1) | copy-start | bytes 196612
  0.7 9.3 %copy-start.1 = (bf16[1,128,256]{2,1,0:T(8,128)(2,1)S(1)}, bf16[1,128,256]{2,1,0:T(8,128)(2,1)}, u32[]{:S(2)}) copy-start(bf16[1,128,256]{2,1,0:T(8,128)(2,1)} %k.1) | copy-start | bytes 196612
  2.6 23.3 %all-to-all-start = ((bf16[8,32,1152]{2,1,0:T(8,128)(2,1)}), bf16[8,32,1152]{2,1,0:T(8,128)(2,1)S(1)}, u32[]{:S(2)}, u32[]{:S(2)}) async-start(bf16[8,32,1152]{2,1,0:T(8,128)(2,1)} %shard_map.164), calls=%async_computation | async-start | bytes 1179648 | tf_op jit(solution)/shard_map/all_to_all | solution.py:359
  9.9 0.7 copy-start.4
  10.6 0.7 copy-start.5
  11.4 14.5 %collective-permute-start = (bf16[128,768]{1,0:T(8,128)(2,1)S(1)}, bf16[128,768]{1,0:T(8,128)(2,1)S(1)}, u32[]{:S(2)}, u32[]{:S(2)}) collective-permute-start(bf16[128,768]{1,0:T(8,128)(2,1)S(1)} %get-tuple-element.70), channel_id=1, source_target_pairs={{0,1},{1,0},{2,3},{3,2},{4,5},{5,4},{6,7},{7,6},{8,9},{9,8},{10,11... | collective-permute-start | bytes 589832 | tf_op jit(solution)/shard_map/ppermute | solution.py:336
  13.5 9.8 %collective-permute-start.2 = (bf16[128,256]{1,0:T(8,128)(2,1)S(1)}, bf16[128,256]{1,0:T(8,128)(2,1)S(1)}, u32[]{:S(2)}, u32[]{:S(2)}) collective-permute-start(bf16[128,256]{1,0:T(8,128)(2,1)S(1)} %bitcast.8), channel_id=1, source_target_pairs={{0,3},{1,2},{2,1},{3,0},{4,7},{5,6},{6,5},{7,4},{8,11},{9,10},{10,... | collective-permute-start | bytes 196616 | tf_op jit(solution)/shard_map/ppermute | solution.py:336
  14.9 8.7 %collective-permute-start.1 = (bf16[128,256]{1,0:T(8,128)(2,1)S(1)}, bf16[128,256]{1,0:T(8,128)(2,1)S(1)}, u32[]{:S(2)}, u32[]{:S(2)}) collective-permute-start(bf16[128,256]{1,0:T(8,128)(2,1)S(1)} %bitcast.9), channel_id=1, source_target_pairs={{0,2},{1,3},{2,0},{3,1},{4,6},{5,7},{6,4},{7,5},{8,10},{9,11},{10,... | collective-permute-start | bytes 196616 | tf_op jit(solution)/shard_map/ppermute | solution.py:336
  15.0 15.2 %collective-permute-start.7 = (bf16[128,512]{1,0:T(8,128)(2,1)S(1)}, bf16[128,512]{1,0:T(8,128)(2,1)S(1)}, u32[]{:S(2)}, u32[]{:S(2)}) collective-permute-start(bf16[128,512]{1,0:T(8,128)(2,1)S(1)} %get-tuple-element.86.refs_0_), channel_id=1, source_target_pairs={{0,3},{1,2},{2,1},{3,0},{4,7},{5,6},{6,5},{7,4},{8,11},{9,10},{10,... | collective-permute-start | bytes 393224 | tf_op jit(solution)/shard_map/ppermute | solution.py:336
  17.9 12.9 %collective-permute-start.6 = (bf16[128,512]{1,0:T(8,128)(2,1)S(1)}, bf16[128,512]{1,0:T(8,128)(2,1)S(1)}, u32[]{:S(2)}, u32[]{:S(2)}) collective-permute-start(bf16[128,512]{1,0:T(8,128)(2,1)S(1)} %get-tuple-element.86.refs_0_), channel_id=1, source_target_pairs={{0,2},{1,3},{2,0},{3,1},{4,6},{5,7},{6,4},{7,5},{8,10},{9,11},{10,... | collective-permute-start | bytes 393224 | tf_op jit(solution)/shard_map/ppermute | solution.py:336
  26.7 5.4 %collective-permute-start.3 = (bf16[128,256]{1,0:T(8,128)(2,1)S(1)}, bf16[128,256]{1,0:T(8,128)(2,1)S(1)}, u32[]{:S(2)}, u32[]{:S(2)}) collective-permute-start(bf16[128,256]{1,0:T(8,128)(2,1)S(1)} %get-tuple-element.74), channel_id=1, source_target_pairs={{0,2},{1,3},{2,0},{3,1},{4,6},{5,7},{6,4},{7,5},{8,10},{9,11},{10,... | collective-permute-start | bytes 196616 | tf_op jit(solution)/shard_map/ppermute | solution.py:336
  28.5 5.5 %collective-permute-start.4 = (bf16[128,256]{1,0:T(8,128)(2,1)S(1)}, bf16[128,256]{1,0:T(8,128)(2,1)S(1)}, u32[]{:S(2)}, u32[]{:S(2)}) collective-permute-start(bf16[128,256]{1,0:T(8,128)(2,1)S(1)} %get-tuple-element.75), channel_id=1, source_target_pairs={{0,3},{1,2},{2,1},{3,0},{4,7},{5,6},{6,5},{7,4},{8,11},{9,10},{10,... | collective-permute-start | bytes 196616 | tf_op jit(solution)/shard_map/ppermute | solution.py:336
  29.7 4.9 %collective-permute-start.5 = (bf16[128,256]{1,0:T(8,128)(2,1)S(1)}, bf16[128,256]{1,0:T(8,128)(2,1)S(1)}, u32[]{:S(2)}, u32[]{:S(2)}) collective-permute-start(bf16[128,256]{1,0:T(8,128)(2,1)S(1)} %get-tuple-element.76), channel_id=1, source_target_pairs={{0,1},{1,0},{2,3},{3,2},{4,5},{5,4},{6,7},{7,6},{8,9},{9,8},{10,11... | collective-permute-start | bytes 196616 | tf_op jit(solution)/shard_map/ppermute | solution.py:336
  34.8 4.3 %collective-permute-start.10 = (f32[2,128]{1,0:T(2,128)S(1)}, f32[2,128]{1,0:T(2,128)S(1)}, u32[]{:S(2)}, u32[]{:S(2)}) collective-permute-start(f32[2,128]{1,0:T(2,128)S(1)} %get-tuple-element.84.refs_0_), channel_id=1, source_target_pairs={{0,24},{8,16},{16,8},{24,0},{1,25},{9,17},{17,9},{25,1},{2,26},{10... | collective-permute-start | bytes 3080 | tf_op jit(solution)/shard_map/ppermute | solution.py:336
  34.9 4.3 %collective-permute-start.9 = (f32[2,128]{1,0:T(2,128)S(1)}, f32[2,128]{1,0:T(2,128)S(1)}, u32[]{:S(2)}, u32[]{:S(2)}) collective-permute-start(f32[2,128]{1,0:T(2,128)S(1)} %get-tuple-element.84.refs_0_), channel_id=1, source_target_pairs={{0,16},{8,24},{16,0},{24,8},{1,17},{9,25},{17,1},{25,9},{2,18},{10... | collective-permute-start | bytes 3080 | tf_op jit(solution)/shard_map/ppermute | solution.py:336
  36.4 2.7 %collective-permute-start.8 = (f32[2,128]{1,0:T(2,128)S(1)}, f32[2,128]{1,0:T(2,128)S(1)}, u32[]{:S(2)}, u32[]{:S(2)}) collective-permute-start(f32[2,128]{1,0:T(2,128)S(1)} %get-tuple-element.84.refs_0_), channel_id=1, source_target_pairs={{0,8},{8,0},{16,24},{24,16},{1,9},{9,1},{17,25},{25,17},{2,10},{10... | collective-permute-start | bytes 3080 | tf_op jit(solution)/shard_map/ppermute | solution.py:336
  36.7 9.4 %collective-permute-start.15 = (bf16[128,256]{1,0:T(8,128)(2,1)S(1)}, bf16[128,256]{1,0:T(8,128)(2,1)S(1)}, u32[]{:S(2)}, u32[]{:S(2)}) collective-permute-start(bf16[128,256]{1,0:T(8,128)(2,1)S(1)} %bitcast.11), channel_id=1, source_target_pairs={{0,4},{1,5},{2,6},{3,7},{4,0},{5,1},{6,2},{7,3},{8,12},{9,13},{10,... | collective-permute-start | bytes 196616 | tf_op jit(solution)/shard_map/ppermute | solution.py:336
  39.3 6.8 %collective-permute-start.14 = (bf16[128,256]{1,0:T(8,128)(2,1)S(1)}, bf16[128,256]{1,0:T(8,128)(2,1)S(1)}, u32[]{:S(2)}, u32[]{:S(2)}) collective-permute-start(bf16[128,256]{1,0:T(8,128)(2,1)S(1)} %shard_map.167.refs_4_), channel_id=1, source_target_pairs={{0,4},{1,5},{2,6},{3,7},{4,0},{5,1},{6,2},{7,3},{8,12},{9,13},{10,... | collective-permute-start | bytes 196616 | tf_op jit(solution)/shard_map/ppermute | solution.py:336
  41.1 7.0 %collective-permute-start.13 = (bf16[128,256]{1,0:T(8,128)(2,1)S(1)}, bf16[128,256]{1,0:T(8,128)(2,1)S(1)}, u32[]{:S(2)}, u32[]{:S(2)}) collective-permute-start(bf16[128,256]{1,0:T(8,128)(2,1)S(1)} %shard_map.167.refs_4_), channel_id=1, source_target_pairs={{0,3},{1,2},{2,1},{3,0},{4,7},{5,6},{6,5},{7,4},{8,11},{9,10},{10,... | collective-permute-start | bytes 196616 | tf_op jit(solution)/shard_map/ppermute | solution.py:336
  42.2 7.5 %collective-permute-start.12 = (bf16[128,256]{1,0:T(8,128)(2,1)S(1)}, bf16[128,256]{1,0:T(8,128)(2,1)S(1)}, u32[]{:S(2)}, u32[]{:S(2)}) collective-permute-start(bf16[128,256]{1,0:T(8,128)(2,1)S(1)} %shard_map.167.refs_4_), channel_id=1, source_target_pairs={{0,2},{1,3},{2,0},{3,1},{4,6},{5,7},{6,4},{7,5},{8,10},{9,11},{10,... | collective-permute-start | bytes 196616 | tf_op jit(solution)/shard_map/ppermute | solution.py:336
  43.1 6.6 %collective-permute-start.11 = (bf16[128,256]{1,0:T(8,128)(2,1)S(1)}, bf16[128,256]{1,0:T(8,128)(2,1)S(1)}, u32[]{:S(2)}, u32[]{:S(2)}) collective-permute-start(bf16[128,256]{1,0:T(8,128)(2,1)S(1)} %shard_map.167.refs_4_), channel_id=1, source_target_pairs={{0,1},{1,0},{2,3},{3,2},{4,5},{5,4},{6,7},{7,6},{8,9},{9,8},{10,11... | collective-permute-start | bytes 196616 | tf_op jit(solution)/shard_map/ppermute | solution.py:336
  46.1 7.4 %collective-permute-start.18 = (bf16[128,512]{1,0:T(8,128)(2,1)S(1)}, bf16[128,512]{1,0:T(8,128)(2,1)S(1)}, u32[]{:S(2)}, u32[]{:S(2)}) collective-permute-start(bf16[128,512]{1,0:T(8,128)(2,1)S(1)} %shard_map.170.refs_4_), channel_id=1, source_target_pairs={{0,3},{1,2},{2,1},{3,0},{4,7},{5,6},{6,5},{7,4},{8,11},{9,10},{10,... | collective-permute-start | bytes 393224 | tf_op jit(solution)/shard_map/ppermute | solution.py:336
  47.0 8.3 %collective-permute-start.17 = (bf16[128,512]{1,0:T(8,128)(2,1)S(1)}, bf16[128,512]{1,0:T(8,128)(2,1)S(1)}, u32[]{:S(2)}, u32[]{:S(2)}) collective-permute-start(bf16[128,512]{1,0:T(8,128)(2,1)S(1)} %shard_map.170.refs_4_), channel_id=1, source_target_pairs={{0,2},{1,3},{2,0},{3,1},{4,6},{5,7},{6,4},{7,5},{8,10},{9,11},{10,... | collective-permute-start | bytes 393224 | tf_op jit(solution)/shard_map/ppermute | solution.py:336
  48.1 7.3 %collective-permute-start.16 = (bf16[128,512]{1,0:T(8,128)(2,1)S(1)}, bf16[128,512]{1,0:T(8,128)(2,1)S(1)}, u32[]{:S(2)}, u32[]{:S(2)}) collective-permute-start(bf16[128,512]{1,0:T(8,128)(2,1)S(1)} %shard_map.170.refs_4_), channel_id=1, source_target_pairs={{0,1},{1,0},{2,3},{3,2},{4,5},{5,4},{6,7},{7,6},{8,9},{9,8},{10,11... | collective-permute-start | bytes 393224 | tf_op jit(solution)/shard_map/ppermute | solution.py:336
  50.5 7.7 %collective-permute-start.19 = (bf16[128,256]{1,0:T(8,128)(2,1)S(1)}, bf16[128,256]{1,0:T(8,128)(2,1)S(1)}, u32[]{:S(2)}, u32[]{:S(2)}) collective-permute-start(bf16[128,256]{1,0:T(8,128)(2,1)S(1)} %get-tuple-element.107), channel_id=1, source_target_pairs={{0,2},{1,3},{2,0},{3,1},{4,6},{5,7},{6,4},{7,5},{8,10},{9,11},{10,... | collective-permute-start | bytes 196616 | tf_op jit(solution)/shard_map/ppermute | solution.py:336
  50.6 7.7 %collective-permute-start.20 = (bf16[128,256]{1,0:T(8,128)(2,1)S(1)}, bf16[128,256]{1,0:T(8,128)(2,1)S(1)}, u32[]{:S(2)}, u32[]{:S(2)}) collective-permute-start(bf16[128,256]{1,0:T(8,128)(2,1)S(1)} %get-tuple-element.108), channel_id=1, source_target_pairs={{0,3},{1,2},{2,1},{3,0},{4,7},{5,6},{6,5},{7,4},{8,11},{9,10},{10,... | collective-permute-start | bytes 196616 | tf_op jit(solution)/shard_map/ppermute | solution.py:336
  53.4 5.0 %collective-permute-start.21 = (bf16[128,256]{1,0:T(8,128)(2,1)S(1)}, bf16[128,256]{1,0:T(8,128)(2,1)S(1)}, u32[]{:S(2)}, u32[]{:S(2)}) collective-permute-start(bf16[128,256]{1,0:T(8,128)(2,1)S(1)} %get-tuple-element.109), channel_id=1, source_target_pairs={{0,1},{1,0},{2,3},{3,2},{4,5},{5,4},{6,7},{7,6},{8,9},{9,8},{10,11... | collective-permute-start | bytes 196616 | tf_op jit(solution)/shard_map/ppermute | solution.py:336
  58.4 18.6 %collective-permute-start.22 = (bf16[672,128]{1,0:T(8,128)(2,1)S(1)}, bf16[672,128]{1,0:T(8,128)(2,1)S(1)}, u32[]{:S(2)}, u32[]{:S(2)}) collective-permute-start(bf16[672,128]{1,0:T(8,128)(2,1)S(1)} %get-tuple-element.114), channel_id=1, source_target_pairs={{0,1},{1,0},{2,3},{3,2},{4,5},{5,4},{6,7},{7,6},{8,9},{9,8},{10,11... | collective-permute-start | bytes 516104 | tf_op jit(solution)/shard_map/ppermute | solution.py:336
  59.7 17.4 %collective-permute-start.23 = (bf16[672,128]{1,0:T(8,128)(2,1)S(1)}, bf16[672,128]{1,0:T(8,128)(2,1)S(1)}, u32[]{:S(2)}, u32[]{:S(2)}) collective-permute-start(bf16[672,128]{1,0:T(8,128)(2,1)S(1)} %get-tuple-element.115), channel_id=1, source_target_pairs={{0,2},{1,3},{2,0},{3,1},{4,6},{5,7},{6,4},{7,5},{8,10},{9,11},{10,... | collective-permute-start | bytes 516104 | tf_op jit(solution)/shard_map/ppermute | solution.py:336
  60.1 17.0 %collective-permute-start.24 = (bf16[672,128]{1,0:T(8,128)(2,1)S(1)}, bf16[672,128]{1,0:T(8,128)(2,1)S(1)}, u32[]{:S(2)}, u32[]{:S(2)}) collective-permute-start(bf16[672,128]{1,0:T(8,128)(2,1)S(1)} %get-tuple-element.116), channel_id=1, source_target_pairs={{0,3},{1,2},{2,1},{3,0},{4,7},{5,6},{6,5},{7,4},{8,11},{9,10},{10,... | collective-permute-start | bytes 516104 | tf_op jit(solution)/shard_map/ppermute | solution.py:336
  61.9 6.2 %collective-permute-start.25 = (bf16[32,576]{1,0:T(8,128)(2,1)S(1)}, bf16[32,576]{1,0:T(8,128)(2,1)S(1)}, u32[]{:S(2)}, u32[]{:S(2)}) collective-permute-start(bf16[32,576]{1,0:T(8,128)(2,1)S(1)} %get-tuple-element.121), channel_id=1, source_target_pairs={{0,4},{1,5},{2,6},{3,7},{4,0},{5,1},{6,2},{7,3},{8,12},{9,13},{10,... | collective-permute-start | bytes 110600 | tf_op jit(solution)/shard_map/ppermute | solution.py:336
  63.3 7.0 %collective-permute-start.26 = (bf16[32,576]{1,0:T(8,128)(2,1)S(1)}, bf16[32,576]{1,0:T(8,128)(2,1)S(1)}, u32[]{:S(2)}, u32[]{:S(2)}) collective-permute-start(bf16[32,576]{1,0:T(8,128)(2,1)S(1)} %get-tuple-element.122), channel_id=1, source_target_pairs={{0,5},{1,4},{2,7},{3,6},{4,1},{5,0},{6,3},{7,2},{8,13},{9,12},{10,... | collective-permute-start | bytes 110600 | tf_op jit(solution)/shard_map/ppermute | solution.py:336
  68.1 5.8 %collective-permute-start.27 = (bf16[32,576]{1,0:T(8,128)(2,1)S(1)}, bf16[32,576]{1,0:T(8,128)(2,1)S(1)}, u32[]{:S(2)}, u32[]{:S(2)}) collective-permute-start(bf16[32,576]{1,0:T(8,128)(2,1)S(1)} %get-tuple-element.123), channel_id=1, source_target_pairs={{0,6},{1,7},{2,4},{3,5},{4,2},{5,3},{6,0},{7,1},{8,14},{9,15},{10,... | collective-permute-start | bytes 110600 | tf_op jit(solution)/shard_map/ppermute | solution.py:336
  70.3 6.7 %collective-permute-start.28 = (bf16[32,576]{1,0:T(8,128)(2,1)S(1)}, bf16[32,576]{1,0:T(8,128)(2,1)S(1)}, u32[]{:S(2)}, u32[]{:S(2)}) collective-permute-start(bf16[32,576]{1,0:T(8,128)(2,1)S(1)} %get-tuple-element.124), channel_id=1, source_target_pairs={{0,7},{1,6},{2,5},{3,4},{4,3},{5,2},{6,1},{7,0},{8,15},{9,14},{10,... | collective-permute-start | bytes 110600 | tf_op jit(solution)/shard_map/ppermute | solution.py:336

commit v14 on v13

--- a/solution.py
+++ b/solution.py
@@ -291,8 +291,19 @@
         for tok in (grad_k, grad_v):
             at = put(out, at, tok[d * own : (d + 1) * own, :])
         put(out, at, inner_buf[place[2] ^ d].astype(BF))
-    for dist in range(group, inner_buf.shape[0]):
-        outs[dist][...] = inner_buf[place[2] ^ dist].astype(BF)
+    for dist, out in zip(far_distances(group, tok_groups), outs[group:]):
+        for i in range(2):
+            out[i * padded(rows) : i * padded(rows) + rows, :] = inner_buf[place[2] ^ dist ^ i].astype(BF)
+
+
+def relay_kernel(rows, *refs):
+    out, step = refs[-1], padded(rows)
+    for i, block in enumerate(refs[:-1]):
+        out[i * step : i * step + rows, :] = block[step : step + rows, :]
+
+
+def far_distances(group, tok_groups):
+    return [e * group + d for e in range(1, tok_groups) for d in range(0, group, 2)]
 
 
 def total_of(refs):
@@ -316,14 +327,17 @@
     gv[0] = (rate[...] * sums[1]).astype(BF)
 
 
-def weights_kernel(group, slab, at, place, inner, *refs):
+def weights_kernel(group, tok_groups, slab, at, place, relayed, inner, *refs):
     blocks, (*outs, buf) = refs[:-4], refs[-4:]
     _, rows, cols = buf.shape
-    for d in range(group):
-        total = (get(blocks[d - 1], at, rows, cols)[0] if d else inner[...]).astype(F32)
-        for far in blocks[group - 1 + d :: group]:
-            total += far[...].astype(F32)
-        buf[d] = total
+    step = padded(rows)
+    buf[0] = inner[...].astype(F32)
+    for d in range(1, group):
+        buf[d] = get(blocks[d - 1], at, rows, cols)[0].astype(F32)
+    for i, dist in enumerate(far_distances(group, tok_groups)):
+        d = dist % group
+        buf[d] += blocks[group - 1 + i][0:rows, :].astype(F32)
+        buf[d ^ 1] += relayed[i * step : i * step + rows, :].astype(F32)
     total = [buf[place[1] ^ j] for j in range(group)]
     for i in range(3):
         outs[i][0] = jnp.concatenate([t[:, i * slab : (i + 1) * slab] for t in total], axis=1)
@@ -411,13 +425,14 @@
 
         q_block = (own, feat)
         grad_q = [grad_q[0]] + [move(grad_q[d], d) for d in (*range(2, group), *range(1, min(2, group)))]
+        far = far_distances(group, tok_groups)
         tok, inner, *sends = call(
             functools.partial(backward_kernel, slab, group, tok_groups),
             (
                 arr((own, 2 * feat), BF),
                 arr((rows, 3 * slab), BF),
                 *(message(*(q_block,) * 2, (rows, 3 * slab)),) * (group - 1),
-                *(arr((rows, 3 * slab), BF),) * (seq_n - group),
+                *(arr((2 * padded(rows), 3 * slab), BF),) * len(far),
             ),
             (place, wall, normed, grads, factors, rises, *stats, *kv_near, *pairs),
             24,
@@ -431,7 +446,14 @@
         sends, grad_q = lax.optimization_barrier((sends, grad_q))
         near_got = {d: move(sends[d - 1], d) for d in (*range(2, group), *range(1, min(2, group)))}
         near_got = [near_got[d] for d in range(1, group)]
-        far_got = [move(sends[d - 1], d) for d in range(group, seq_n)]
+        far_got = [move(x, d) for x, d in zip(sends[group - 1 :], far)]
+        (relayed,) = call(
+            functools.partial(relay_kernel, rows),
+            (arr((len(far) * padded(rows), 3 * slab), BF),),
+            far_got,
+            16,
+        )
+        relayed = move(relayed, 1)
         out_tok = arr((1, own, feat), BF)
         grad_w = arr((1, rows, hidden), F32)
         grads_t = call(
@@ -439,9 +461,9 @@
         )
         at = 2 * tiles(feat) * padded(own)
         grads_w = call(
-            functools.partial(weights_kernel, group, slab, at),
+            functools.partial(weights_kernel, group, tok_groups, slab, at),
             (grad_w,) * 3,
-            (place, inner, *near_got, *far_got),
+            (place, relayed, inner, *near_got, *far_got),
             16,
             smem=1,
             scratch=[pltpu.VMEM((group, rows, 3 * slab), F32)],

time: 79.4 us -> 79.2 us (level)
  starting transfers between devices: 45 us -> 41.1 us
  waiting for transfers between devices: 22 us -> 25.6 us
    ppermute x29 -> x28, starting transfers between devices: 37.8 us -> 33.9 us  [move(): return lax.ppermute(x, axis, [(i, i ^ dist) for i in range(size)])]
    ppermute x29 -> x28, waiting for transfers between devices: 22 us -> 25.6 us  [move(): return lax.ppermute(x, axis, [(i, i ^ dist) for i in range(size)])]
    pallas_call x10 -> x11, Pallas kernels: 7.99 us -> 8 us  [call(): pl.pallas_call(kernel, out_shape=outs, in_specs=[SMEM] * smem + [VMEM] *...]
  transfers between devices with their start and end apart: 30 -> 29, of which waited for: 15 -> 15; matrix products, arithmetic and copies ran while one was open for 0% -> 0% of each run, Pallas kernels for 7% -> 7%
where the time goes in v14:
time: 79.2 us; the launch traced here: 79 us
  starting transfers between devices  41.1 us (52%)
  waiting for transfers between devices  25.6 us (32%)
  Pallas kernels  9.96 us (13%)
  local copies, waits for them, and re-layouts  1.35 us (2%)
  between operations  0.83 us (1%)
    ppermute x28, starting transfers between devices, move(): return lax.ppermute(x, axis, [(i, i ^ dist) for i in range(size)])  33.9 us
    ppermute x28, waiting for transfers between devices, move(): return lax.ppermute(x, axis, [(i, i ^ dist) for i in range(size)])  25.6 us
    pallas_call x11, Pallas kernels, call(): pl.pallas_call(kernel, out_shape=outs, in_specs=[SMEM] * smem + [VMEM] *...  8 us
    all_to_all x1, starting transfers between devices, local(): lax.all_to_all(packed, 'seq', 0, 0, tiled=True)  7.26 us
    pallas_call x1, Pallas kernels, copying_call(): pl.pallas_call(kernel, out_shape=outs, in_specs=[pl.BlockSpec(memory_spac...  1.96 us
  transfers between devices with their start and end apart: 29, of which 15 were waited for; matrix products, arithmetic and copies ran while one was open for 0% of the time, Pallas kernels for 7%

profile of v14, /device:TPU:0, one launch (start us, length us, event | category | flops | bytes accessed | tf_op | source)
XLA Modules:
  0.0 79.0 jit_solution(4800641098039848042)
XLA Ops:
  0.7 2.0 %shard_map.164 = bf16[8,32,1152]{2,1,0:T(8,128)(2,1)} custom-call(bf16[1,32,768]{2,1,0:T(8,128)(2,1)} %refs_0_.1, bf16[1,32,768]{2,1,0:T(8,128)(2,1)} %refs_1_.1, bf16[1,32,768]{2,1,0:T(8,128)(2,1)} %refs_2_.1, bf16[1,32,768]{2,1,0:T(8,128)(2,1)} %refs_3_.1, bf16[1,32,768]{2,1,0:T(8,128)(2,1)} %refs_4_.1, bf16[1,32,768]{2,1,0:T(8,128)(2,1)} %refs_5_.1), custom_call_target="tpu_custom_call" | custom-call | tf_op jit(solution)/shard_map/pallas_call | solution.py:61
  2.6 7.3 %all-to-all-start = ((bf16[8,32,1152]{2,1,0:T(8,128)(2,1)}), bf16[8,32,1152]{2,1,0:T(8,128)(2,1)S(1)}, u32[]{:S(2)}, u32[]{:S(2)}) async-start(bf16[8,32,1152]{2,1,0:T(8,128)(2,1)} %shard_map.164), calls=%async_computation | async-start | bytes 1179648 | tf_op jit(solution)/shard_map/all_to_all | solution.py:373
  9.9 0.0 copy-start.4
  10.0 0.7 copy-done.4
  10.6 0.7 copy-done.5
  11.3 0.1 shard_map.163
  11.4 2.1 %collective-permute-start = (bf16[128,768]{1,0:T(8,128)(2,1)S(1)}, bf16[128,768]{1,0:T(8,128)(2,1)S(1)}, u32[]{:S(2)}, u32[]{:S(2)}) collective-permute-start(bf16[128,768]{1,0:T(8,128)(2,1)S(1)} %get-tuple-element.66), channel_id=1, source_target_pairs={{0,1},{1,0},{2,3},{3,2},{4,5},{5,4},{6,7},{7,6},{8,9},{9,8},{10,11... | collective-permute-start | bytes 589832 | tf_op jit(solution)/shard_map/ppermute | solution.py:350
  13.5 1.5 %collective-permute-start.2 = (bf16[128,256]{1,0:T(8,128)(2,1)S(1)}, bf16[128,256]{1,0:T(8,128)(2,1)S(1)}, u32[]{:S(2)}, u32[]{:S(2)}) collective-permute-start(bf16[128,256]{1,0:T(8,128)(2,1)S(1)} %bitcast.8), channel_id=1, source_target_pairs={{0,3},{1,2},{2,1},{3,0},{4,7},{5,6},{6,5},{7,4},{8,11},{9,10},{10,... | collective-permute-start | bytes 196616 | tf_op jit(solution)/shard_map/ppermute | solution.py:350
  14.9 0.1 collective-permute-start.1
  15.0 2.8 %collective-permute-start.7 = (bf16[128,512]{1,0:T(8,128)(2,1)S(1)}, bf16[128,512]{1,0:T(8,128)(2,1)S(1)}, u32[]{:S(2)}, u32[]{:S(2)}) collective-permute-start(bf16[128,512]{1,0:T(8,128)(2,1)S(1)} %get-tuple-element.82.refs_0_), channel_id=1, source_target_pairs={{0,3},{1,2},{2,1},{3,0},{4,7},{5,6},{6,5},{7,4},{8,11},{9,10},{10,... | collective-permute-start | bytes 393224 | tf_op jit(solution)/shard_map/ppermute | solution.py:350
  17.9 0.6 collective-permute-start.6
  18.4 4.8 %collective-permute-done.2.refs_3_ = bf16[128,256]{1,0:T(8,128)(2,1)S(1)} collective-permute-done((bf16[128,256]{1,0:T(8,128)(2,1)S(1)}, bf16[128,256]{1,0:T(8,128)(2,1)S(1)}, u32[]{:S(2)}, u32[]{:S(2)}) %collective-permute-start.2) | collective-permute-done | bytes 65568 | tf_op jit(solution)/shard_map/ppermute | solution.py:350
  23.3 0.4 collective-permute-done.1.refs_2_
  23.6 2.3 %collective-permute-done.refs_1_ = bf16[128,768]{1,0:T(8,128)(2,1)S(1)} collective-permute-done((bf16[128,768]{1,0:T(8,128)(2,1)S(1)}, bf16[128,768]{1,0:T(8,128)(2,1)S(1)}, u32[]{:S(2)}, u32[]{:S(2)}) %collective-permute-start) | collective-permute-done | bytes 196640 | tf_op jit(solution)/shard_map/ppermute | solution.py:350
  25.9 0.8 shard_map.165
  26.7 1.8 %collective-permute-start.3 = (bf16[128,256]{1,0:T(8,128)(2,1)S(1)}, bf16[128,256]{1,0:T(8,128)(2,1)S(1)}, u32[]{:S(2)}, u32[]{:S(2)}) collective-permute-start(bf16[128,256]{1,0:T(8,128)(2,1)S(1)} %get-tuple-element.70), channel_id=1, source_target_pairs={{0,2},{1,3},{2,0},{3,1},{4,6},{5,7},{6,4},{7,5},{8,10},{9,11},{10,... | collective-permute-start | bytes 196616 | tf_op jit(solution)/shard_map/ppermute | solution.py:350
  28.5 1.1 %collective-permute-start.4 = (bf16[128,256]{1,0:T(8,128)(2,1)S(1)}, bf16[128,256]{1,0:T(8,128)(2,1)S(1)}, u32[]{:S(2)}, u32[]{:S(2)}) collective-permute-start(bf16[128,256]{1,0:T(8,128)(2,1)S(1)} %get-tuple-element.71), channel_id=1, source_target_pairs={{0,3},{1,2},{2,1},{3,0},{4,7},{5,6},{6,5},{7,4},{8,11},{9,10},{10,... | collective-permute-start | bytes 196616 | tf_op jit(solution)/shard_map/ppermute | solution.py:350
  29.7 0.6 collective-permute-start.5
  30.2 0.0 collective-permute-done.7.refs_3_
  30.3 0.5 collective-permute-done.6.refs_2_
  30.7 1.4 %collective-permute-done.3.refs_1_ = bf16[128,256]{1,0:T(8,128)(2,1)S(1)} collective-permute-done((bf16[128,256]{1,0:T(8,128)(2,1)S(1)}, bf16[128,256]{1,0:T(8,128)(2,1)S(1)}, u32[]{:S(2)}, u32[]{:S(2)}) %collective-permute-start.3) | collective-permute-done | bytes 65568 | tf_op jit(solution)/shard_map/ppermute | solution.py:350
  32.1 1.9 %collective-permute-done.4.refs_2_ = bf16[128,256]{1,0:T(8,128)(2,1)S(1)} collective-permute-done((bf16[128,256]{1,0:T(8,128)(2,1)S(1)}, bf16[128,256]{1,0:T(8,128)(2,1)S(1)}, u32[]{:S(2)}, u32[]{:S(2)}) %collective-permute-start.4) | collective-permute-done | bytes 65568 | tf_op jit(solution)/shard_map/ppermute | solution.py:350
  34.0 0.6 collective-permute-done.5.refs_3_
  34.6 0.1 shard_map.166
  34.8 0.1 collective-permute-start.10
  34.9 1.6 %collective-permute-start.9 = (f32[2,128]{1,0:T(2,128)S(1)}, f32[2,128]{1,0:T(2,128)S(1)}, u32[]{:S(2)}, u32[]{:S(2)}) collective-permute-start(f32[2,128]{1,0:T(2,128)S(1)} %get-tuple-element.80.refs_0_), channel_id=1, source_target_pairs={{0,16},{8,24},{16,0},{24,8},{1,17},{9,25},{17,1},{25,9},{2,18},{10... | collective-permute-start | bytes 3080 | tf_op jit(solution)/shard_map/ppermute | solution.py:350
  36.4 0.3 collective-permute-start.8
  36.7 2.4 %collective-permute-start.15 = (bf16[128,256]{1,0:T(8,128)(2,1)S(1)}, bf16[128,256]{1,0:T(8,128)(2,1)S(1)}, u32[]{:S(2)}, u32[]{:S(2)}) collective-permute-start(bf16[128,256]{1,0:T(8,128)(2,1)S(1)} %bitcast.11), channel_id=1, source_target_pairs={{0,4},{1,5},{2,6},{3,7},{4,0},{5,1},{6,2},{7,3},{8,12},{9,13},{10,... | collective-permute-start | bytes 196616 | tf_op jit(solution)/shard_map/ppermute | solution.py:350
  39.1 0.0 collective-permute-done.10.refs_3_
  39.1 0.1 shard_map.167.refs_4_
  39.3 1.8 %collective-permute-start.14 = (bf16[128,256]{1,0:T(8,128)(2,1)S(1)}, bf16[128,256]{1,0:T(8,128)(2,1)S(1)}, u32[]{:S(2)}, u32[]{:S(2)}) collective-permute-start(bf16[128,256]{1,0:T(8,128)(2,1)S(1)} %shard_map.167.refs_4_), channel_id=1, source_target_pairs={{0,4},{1,5},{2,6},{3,7},{4,0},{5,1},{6,2},{7,3},{8,12},{9,13},{10,... | collective-permute-start | bytes 196616 | tf_op jit(solution)/shard_map/ppermute | solution.py:350
  41.1 1.1 %collective-permute-start.13 = (bf16[128,256]{1,0:T(8,128)(2,1)S(1)}, bf16[128,256]{1,0:T(8,128)(2,1)S(1)}, u32[]{:S(2)}, u32[]{:S(2)}) collective-permute-start(bf16[128,256]{1,0:T(8,128)(2,1)S(1)} %shard_map.167.refs_4_), channel_id=1, source_target_pairs={{0,3},{1,2},{2,1},{3,0},{4,7},{5,6},{6,5},{7,4},{8,11},{9,10},{10,... | collective-permute-start | bytes 196616 | tf_op jit(solution)/shard_map/ppermute | solution.py:350
  42.2 0.9 %collective-permute-start.12 = (bf16[128,256]{1,0:T(8,128)(2,1)S(1)}, bf16[128,256]{1,0:T(8,128)(2,1)S(1)}, u32[]{:S(2)}, u32[]{:S(2)}) collective-permute-start(bf16[128,256]{1,0:T(8,128)(2,1)S(1)} %shard_map.167.refs_4_), channel_id=1, source_target_pairs={{0,2},{1,3},{2,0},{3,1},{4,6},{5,7},{6,4},{7,5},{8,10},{9,11},{10,... | collective-permute-start | bytes 196616 | tf_op jit(solution)/shard_map/ppermute | solution.py:350
  43.1 1.5 %collective-permute-start.11 = (bf16[128,256]{1,0:T(8,128)(2,1)S(1)}, bf16[128,256]{1,0:T(8,128)(2,1)S(1)}, u32[]{:S(2)}, u32[]{:S(2)}) collective-permute-start(bf16[128,256]{1,0:T(8,128)(2,1)S(1)} %shard_map.167.refs_4_), channel_id=1, source_target_pairs={{0,1},{1,0},{2,3},{3,2},{4,5},{5,4},{6,7},{7,6},{8,9},{9,8},{10,11... | collective-permute-start | bytes 196616 | tf_op jit(solution)/shard_map/ppermute | solution.py:350
  44.6 0.1 pad_add_fusion.place
  44.7 1.1 %shard_map.169 = (f32[4,512,192]{2,1,0:T(8,128)S(1)}, bf16[3,512,192]{2,1,0:T(8,128)(2,1)S(1)}, f32[3,192]{1,0:T(4,128)S(1)}, f32[3,256,192]{2,1,0:T(8,128)S(1)}, f32[3,256,192]{2,1,0:T(8,128)S(1)}) custom-call(bf16[256,1152]{1,0:T(8,128)(2,1)S(1)} %bitcast.6, bf16[128,512]{1,0:T(8,128)(2,1)S(1)} %get-tuple-element.82.refs_0_, ...), custom_call_target="tpu_custom_call" | custom-call | flops 603979776 | bytes 4524288 | tf_op jit(solution)/shard_map/pallas_call | solution.py:49
  45.8 0.3 collective-permute-done.14.left
  46.1 0.9 %collective-permute-start.18 = (bf16[128,512]{1,0:T(8,128)(2,1)S(1)}, bf16[128,512]{1,0:T(8,128)(2,1)S(1)}, u32[]{:S(2)}, u32[]{:S(2)}) collective-permute-start(bf16[128,512]{1,0:T(8,128)(2,1)S(1)} %shard_map.170.refs_4_), channel_id=1, source_target_pairs={{0,3},{1,2},{2,1},{3,0},{4,7},{5,6},{6,5},{7,4},{8,11},{9,10},{10,... | collective-permute-start | bytes 393224 | tf_op jit(solution)/shard_map/ppermute | solution.py:350
  47.0 1.1 %collective-permute-start.17 = (bf16[128,512]{1,0:T(8,128)(2,1)S(1)}, bf16[128,512]{1,0:T(8,128)(2,1)S(1)}, u32[]{:S(2)}, u32[]{:S(2)}) collective-permute-start(bf16[128,512]{1,0:T(8,128)(2,1)S(1)} %shard_map.170.refs_4_), channel_id=1, source_target_pairs={{0,2},{1,3},{2,0},{3,1},{4,6},{5,7},{6,4},{7,5},{8,10},{9,11},{10,... | collective-permute-start | bytes 393224 | tf_op jit(solution)/shard_map/ppermute | solution.py:350
  48.1 0.0 collective-permute-done.13.refs_7_
  48.1 1.5 %collective-permute-start.16 = (bf16[128,512]{1,0:T(8,128)(2,1)S(1)}, bf16[128,512]{1,0:T(8,128)(2,1)S(1)}, u32[]{:S(2)}, u32[]{:S(2)}) collective-permute-start(bf16[128,512]{1,0:T(8,128)(2,1)S(1)} %shard_map.170.refs_4_), channel_id=1, source_target_pairs={{0,1},{1,0},{2,3},{3,2},{4,5},{5,4},{6,7},{7,6},{8,9},{9,8},{10,11... | collective-permute-start | bytes 393224 | tf_op jit(solution)/shard_map/ppermute | solution.py:350
  49.6 0.0 collective-permute-done.12.refs_6_
  49.6 0.0 collective-permute-done.11.refs_5_
  49.6 0.8 %shard_map.168 = (bf16[128,256]{1,0:T(8,128)(2,1)S(1)}, bf16[128,256]{1,0:T(8,128)(2,1)S(1)}, bf16[128,256]{1,0:T(8,128)(2,1)S(1)}, bf16[128,256]{1,0:T(8,128)(2,1)S(1)}, f32[3,256,192]{2,1,0:T(8,128)S(1)}) custom-call(bf16[256,576]{1,0:T(8,128)(2,1)S(1)} %get-tuple-element.67.normed_ref, bf16[128,256]{1,0:T(8,128)(2,1)S(1)} %bitcast.12, ...), custom_call_target="tpu_custom_call" | custom-call | flops 3019898880 | bytes 1802240 | tf_op jit(solution)/shard_map/pallas_call | solution.py:49
  50.5 0.1 collective-permute-start.19
  50.6 1.9 %collective-permute-start.20 = (bf16[128,256]{1,0:T(8,128)(2,1)S(1)}, bf16[128,256]{1,0:T(8,128)(2,1)S(1)}, u32[]{:S(2)}, u32[]{:S(2)}) collective-permute-start(bf16[128,256]{1,0:T(8,128)(2,1)S(1)} %get-tuple-element.102), channel_id=1, source_target_pairs={{0,3},{1,2},{2,1},{3,0},{4,7},{5,6},{6,5},{7,4},{8,11},{9,10},{10,... | collective-permute-start | bytes 196616 | tf_op jit(solution)/shard_map/ppermute | solution.py:350
  52.5 0.9 %collective-permute-done.18.refs_7_ = bf16[128,512]{1,0:T(8,128)(2,1)S(1)} collective-permute-done((bf16[128,512]{1,0:T(8,128)(2,1)S(1)}, bf16[128,512]{1,0:T(8,128)(2,1)S(1)}, u32[]{:S(2)}, u32[]{:S(2)}) %collective-permute-start.18) | collective-permute-done | bytes 131104 | tf_op jit(solution)/shard_map/ppermute | solution.py:350
  53.4 0.6 collective-permute-start.21
  54.0 1.3 %collective-permute-done.17.refs_6_ = bf16[128,512]{1,0:T(8,128)(2,1)S(1)} collective-permute-done((bf16[128,512]{1,0:T(8,128)(2,1)S(1)}, bf16[128,512]{1,0:T(8,128)(2,1)S(1)}, u32[]{:S(2)}, u32[]{:S(2)}) %collective-permute-start.17) | collective-permute-done | bytes 131104 | tf_op jit(solution)/shard_map/ppermute | solution.py:350
  55.3 0.1 collective-permute-done.16.refs_5_
  55.4 2.8 %shard_map.171 = (bf16[128,512]{1,0:T(8,128)(2,1)S(1)}, bf16[32,576]{1,0:T(8,128)(2,1)S(1)}, bf16[672,128]{1,0:T(8,128)(2,1)S(1)}, bf16[672,128]{1,0:T(8,128)(2,...) custom-call(s32[3]{0:T(128)S(1)} %pad_add_fusion.place, ...), custom_call_target="tpu_custom_call" | custom-call | flops 6039797760 | bytes 6764812 | tf_op jit(solution)/shard_map/pallas_call | solution.py:49
  58.2 0.0 collective-permute-done.19.refs_1_
  58.2 0.2 collective-permute-done.21.refs_3_
  58.4 1.3 %collective-permute-start.22 = (bf16[672,128]{1,0:T(8,128)(2,1)S(1)}, bf16[672,128]{1,0:T(8,128)(2,1)S(1)}, u32[]{:S(2)}, u32[]{:S(2)}) collective-permute-start(bf16[672,128]{1,0:T(8,128)(2,1)S(1)} %get-tuple-element.108), channel_id=1, source_target_pairs={{0,1},{1,0},{2,3},{3,2},{4,5},{5,4},{6,7},{7,6},{8,9},{9,8},{10,11... | collective-permute-start | bytes 516104 | tf_op jit(solution)/shard_map/ppermute | solution.py:350
  59.7 0.4 collective-permute-start.23
  60.1 1.8 %collective-permute-start.24 = (bf16[672,128]{1,0:T(8,128)(2,1)S(1)}, bf16[672,128]{1,0:T(8,128)(2,1)S(1)}, u32[]{:S(2)}, u32[]{:S(2)}) collective-permute-start(bf16[672,128]{1,0:T(8,128)(2,1)S(1)} %get-tuple-element.110), channel_id=1, source_target_pairs={{0,3},{1,2},{2,1},{3,0},{4,7},{5,6},{6,5},{7,4},{8,11},{9,10},{10,... | collective-permute-start | bytes 516104 | tf_op jit(solution)/shard_map/ppermute | solution.py:350
  61.9 1.4 %collective-permute-start.25 = (bf16[64,576]{1,0:T(8,128)(2,1)S(1)}, bf16[64,576]{1,0:T(8,128)(2,1)S(1)}, u32[]{:S(2)}, u32[]{:S(2)}) collective-permute-start(bf16[64,576]{1,0:T(8,128)(2,1)S(1)} %get-tuple-element.114), channel_id=1, source_target_pairs={{0,4},{1,5},{2,6},{3,7},{4,0},{5,1},{6,2},{7,3},{8,12},{9,13},{10,... | collective-permute-start | bytes 221192 | tf_op jit(solution)/shard_map/ppermute | solution.py:350
  63.3 1.5 %collective-permute-start.26 = (bf16[64,576]{1,0:T(8,128)(2,1)S(1)}, bf16[64,576]{1,0:T(8,128)(2,1)S(1)}, u32[]{:S(2)}, u32[]{:S(2)}) collective-permute-start(bf16[64,576]{1,0:T(8,128)(2,1)S(1)} %get-tuple-element.115), channel_id=1, source_target_pairs={{0,6},{1,7},{2,4},{3,5},{4,2},{5,3},{6,0},{7,1},{8,14},{9,15},{10,... | collective-permute-start | bytes 221192 | tf_op jit(solution)/shard_map/ppermute | solution.py:350
  64.7 4.2 %collective-permute-done.25.refs_0_.refs_3_ = bf16[64,576]{1,0:T(8,128)(2,1)S(1)} collective-permute-done((bf16[64,576]{1,0:T(8,128)(2,1)S(1)}, bf16[64,576]{1,0:T(8,128)(2,1)S(1)}, u32[]{:S(2)}, u32[]{:S(2)}) %collective-permute-start.25) | collective-permute-done | bytes 73760 | tf_op jit(solution)/shard_map/ppermute | solution.py:350
  68.9 3.4 %collective-permute-done.26.refs_1_.refs_4_ = bf16[64,576]{1,0:T(8,128)(2,1)S(1)} collective-permute-done((bf16[64,576]{1,0:T(8,128)(2,1)S(1)}, bf16[64,576]{1,0:T(8,128)(2,1)S(1)}, u32[]{:S(2)}, u32[]{:S(2)}) %collective-permute-start.26) | collective-permute-done | bytes 73760 | tf_op jit(solution)/shard_map/ppermute | solution.py:350
  72.3 1.1 %collective-permute-start.27 = (bf16[64,576]{1,0:T(8,128)(2,1)S(1)}, bf16[64,576]{1,0:T(8,128)(2,1)S(1)}, u32[]{:S(2)}, u32[]{:S(2)}) collective-permute-start(bf16[64,576]{1,0:T(8,128)(2,1)S(1)} %shard_map.173), channel_id=1, source_target_pairs={{0,1},{1,0},{2,3},{3,2},{4,5},{5,4},{6,7},{7,6},{8,9},{9,8},{10,11... | collective-permute-start | bytes 221192 | tf_op jit(solution)/shard_map/ppermute | solution.py:350
  73.4 3.4 %collective-permute-done.27.relayed = bf16[64,576]{1,0:T(8,128)(2,1)S(1)} collective-permute-done((bf16[64,576]{1,0:T(8,128)(2,1)S(1)}, bf16[64,576]{1,0:T(8,128)(2,1)S(1)}, u32[]{:S(2)}, u32[]{:S(2)}) %collective-permute-start.27) | collective-permute-done | bytes 73760 | tf_op jit(solution)/shard_map/ppermute | solution.py:350
  76.8 1.4 %shard_map.174 = (f32[1,32,768]{2,1,0:T(8,128)}, f32[1,32,768]{2,1,0:T(8,128)}, f32[1,32,768]{2,1,0:T(8,128)}) custom-call(s32[3]{0:T(128)S(1)} %pad_add_fusion.place, bf16[64,576]{1,0:T(8,128)(2,1)S(1)} %collective-permute-done.27.relayed, bf16[32,576]{1,0:T(8,128)(2,1)S(1)} %get-tuple-element.116.inner, ...), custom_call_target="tpu_custom_call" | custom-call | bytes 1069068 | tf_op jit(solution)/shard_map/pallas_call | solution.py:49
  78.2 0.7 shard_map.172
  (19 shorter events, 0.1 us)
Async XLA Ops:
  0.6 9.3 %copy-start = (bf16[1,128,256]{2,1,0:T(8,128)(2,1)S(1)}, bf16[1,128,256]{2,1,0:T(8,128)(2,1)}, u32[]{:S(2)}) copy-start(bf16[1,128,256]{2,1,0:T(8,128)(2,1)} %q.1) | copy-start | bytes 196612
  0.6 9.3 %copy-start.3 = (bf16[1,128,256]{2,1,0:T(8,128)(2,1)S(1)}, bf16[1,128,256]{2,1,0:T(8,128)(2,1)}, u32[]{:S(2)}) copy-start(bf16[1,128,256]{2,1,0:T(8,128)(2,1)} %og.1) | copy-start | bytes 196612
  0.7 9.3 %copy-start.2 = (bf16[1,128,256]{2,1,0:T(8,128)(2,1)S(1)}, bf16[1,128,256]{2,1,0:T(8,128)(2,1)}, u32[]{:S(2)}) copy-start(bf16[1,128,256]{2,1,0:T(8,128)(2,1)} %v.1) | copy-start | bytes 196612
  0.7 9.3 %copy-start.1 = (bf16[1,128,256]{2,1,0:T(8,128)(2,1)S(1)}, bf16[1,128,256]{2,1,0:T(8,128)(2,1)}, u32[]{:S(2)}) copy-start(bf16[1,128,256]{2,1,0:T(8,128)(2,1)} %k.1) | copy-start | bytes 196612
  2.6 23.3 %all-to-all-start = ((bf16[8,32,1152]{2,1,0:T(8,128)(2,1)}), bf16[8,32,1152]{2,1,0:T(8,128)(2,1)S(1)}, u32[]{:S(2)}, u32[]{:S(2)}) async-start(bf16[8,32,1152]{2,1,0:T(8,128)(2,1)} %shard_map.164), calls=%async_computation | async-start | bytes 1179648 | tf_op jit(solution)/shard_map/all_to_all | solution.py:373
  9.9 0.7 copy-start.4
  10.6 0.7 copy-start.5
  11.4 14.5 %collective-permute-start = (bf16[128,768]{1,0:T(8,128)(2,1)S(1)}, bf16[128,768]{1,0:T(8,128)(2,1)S(1)}, u32[]{:S(2)}, u32[]{:S(2)}) collective-permute-start(bf16[128,768]{1,0:T(8,128)(2,1)S(1)} %get-tuple-element.66), channel_id=1, source_target_pairs={{0,1},{1,0},{2,3},{3,2},{4,5},{5,4},{6,7},{7,6},{8,9},{9,8},{10,11... | collective-permute-start | bytes 589832 | tf_op jit(solution)/shard_map/ppermute | solution.py:350
  13.5 9.8 %collective-permute-start.2 = (bf16[128,256]{1,0:T(8,128)(2,1)S(1)}, bf16[128,256]{1,0:T(8,128)(2,1)S(1)}, u32[]{:S(2)}, u32[]{:S(2)}) collective-permute-start(bf16[128,256]{1,0:T(8,128)(2,1)S(1)} %bitcast.8), channel_id=1, source_target_pairs={{0,3},{1,2},{2,1},{3,0},{4,7},{5,6},{6,5},{7,4},{8,11},{9,10},{10,... | collective-permute-start | bytes 196616 | tf_op jit(solution)/shard_map/ppermute | solution.py:350
  14.9 8.7 %collective-permute-start.1 = (bf16[128,256]{1,0:T(8,128)(2,1)S(1)}, bf16[128,256]{1,0:T(8,128)(2,1)S(1)}, u32[]{:S(2)}, u32[]{:S(2)}) collective-permute-start(bf16[128,256]{1,0:T(8,128)(2,1)S(1)} %bitcast.9), channel_id=1, source_target_pairs={{0,2},{1,3},{2,0},{3,1},{4,6},{5,7},{6,4},{7,5},{8,10},{9,11},{10,... | collective-permute-start | bytes 196616 | tf_op jit(solution)/shard_map/ppermute | solution.py:350
  15.0 15.2 %collective-permute-start.7 = (bf16[128,512]{1,0:T(8,128)(2,1)S(1)}, bf16[128,512]{1,0:T(8,128)(2,1)S(1)}, u32[]{:S(2)}, u32[]{:S(2)}) collective-permute-start(bf16[128,512]{1,0:T(8,128)(2,1)S(1)} %get-tuple-element.82.refs_0_), channel_id=1, source_target_pairs={{0,3},{1,2},{2,1},{3,0},{4,7},{5,6},{6,5},{7,4},{8,11},{9,10},{10,... | collective-permute-start | bytes 393224 | tf_op jit(solution)/shard_map/ppermute | solution.py:350
  17.9 12.9 %collective-permute-start.6 = (bf16[128,512]{1,0:T(8,128)(2,1)S(1)}, bf16[128,512]{1,0:T(8,128)(2,1)S(1)}, u32[]{:S(2)}, u32[]{:S(2)}) collective-permute-start(bf16[128,512]{1,0:T(8,128)(2,1)S(1)} %get-tuple-element.82.refs_0_), channel_id=1, source_target_pairs={{0,2},{1,3},{2,0},{3,1},{4,6},{5,7},{6,4},{7,5},{8,10},{9,11},{10,... | collective-permute-start | bytes 393224 | tf_op jit(solution)/shard_map/ppermute | solution.py:350
  26.7 5.4 %collective-permute-start.3 = (bf16[128,256]{1,0:T(8,128)(2,1)S(1)}, bf16[128,256]{1,0:T(8,128)(2,1)S(1)}, u32[]{:S(2)}, u32[]{:S(2)}) collective-permute-start(bf16[128,256]{1,0:T(8,128)(2,1)S(1)} %get-tuple-element.70), channel_id=1, source_target_pairs={{0,2},{1,3},{2,0},{3,1},{4,6},{5,7},{6,4},{7,5},{8,10},{9,11},{10,... | collective-permute-start | bytes 196616 | tf_op jit(solution)/shard_map/ppermute | solution.py:350
  28.5 5.5 %collective-permute-start.4 = (bf16[128,256]{1,0:T(8,128)(2,1)S(1)}, bf16[128,256]{1,0:T(8,128)(2,1)S(1)}, u32[]{:S(2)}, u32[]{:S(2)}) collective-permute-start(bf16[128,256]{1,0:T(8,128)(2,1)S(1)} %get-tuple-element.71), channel_id=1, source_target_pairs={{0,3},{1,2},{2,1},{3,0},{4,7},{5,6},{6,5},{7,4},{8,11},{9,10},{10,... | collective-permute-start | bytes 196616 | tf_op jit(solution)/shard_map/ppermute | solution.py:350
  29.7 4.9 %collective-permute-start.5 = (bf16[128,256]{1,0:T(8,128)(2,1)S(1)}, bf16[128,256]{1,0:T(8,128)(2,1)S(1)}, u32[]{:S(2)}, u32[]{:S(2)}) collective-permute-start(bf16[128,256]{1,0:T(8,128)(2,1)S(1)} %get-tuple-element.72), channel_id=1, source_target_pairs={{0,1},{1,0},{2,3},{3,2},{4,5},{5,4},{6,7},{7,6},{8,9},{9,8},{10,11... | collective-permute-start | bytes 196616 | tf_op jit(solution)/shard_map/ppermute | solution.py:350
  34.8 4.3 %collective-permute-start.10 = (f32[2,128]{1,0:T(2,128)S(1)}, f32[2,128]{1,0:T(2,128)S(1)}, u32[]{:S(2)}, u32[]{:S(2)}) collective-permute-start(f32[2,128]{1,0:T(2,128)S(1)} %get-tuple-element.80.refs_0_), channel_id=1, source_target_pairs={{0,24},{8,16},{16,8},{24,0},{1,25},{9,17},{17,9},{25,1},{2,26},{10... | collective-permute-start | bytes 3080 | tf_op jit(solution)/shard_map/ppermute | solution.py:350
  34.9 4.3 %collective-permute-start.9 = (f32[2,128]{1,0:T(2,128)S(1)}, f32[2,128]{1,0:T(2,128)S(1)}, u32[]{:S(2)}, u32[]{:S(2)}) collective-permute-start(f32[2,128]{1,0:T(2,128)S(1)} %get-tuple-element.80.refs_0_), channel_id=1, source_target_pairs={{0,16},{8,24},{16,0},{24,8},{1,17},{9,25},{17,1},{25,9},{2,18},{10... | collective-permute-start | bytes 3080 | tf_op jit(solution)/shard_map/ppermute | solution.py:350
  36.4 2.7 %collective-permute-start.8 = (f32[2,128]{1,0:T(2,128)S(1)}, f32[2,128]{1,0:T(2,128)S(1)}, u32[]{:S(2)}, u32[]{:S(2)}) collective-permute-start(f32[2,128]{1,0:T(2,128)S(1)} %get-tuple-element.80.refs_0_), channel_id=1, source_target_pairs={{0,8},{8,0},{16,24},{24,16},{1,9},{9,1},{17,25},{25,17},{2,10},{10... | collective-permute-start | bytes 3080 | tf_op jit(solution)/shard_map/ppermute | solution.py:350
  36.7 9.4 %collective-permute-start.15 = (bf16[128,256]{1,0:T(8,128)(2,1)S(1)}, bf16[128,256]{1,0:T(8,128)(2,1)S(1)}, u32[]{:S(2)}, u32[]{:S(2)}) collective-permute-start(bf16[128,256]{1,0:T(8,128)(2,1)S(1)} %bitcast.11), channel_id=1, source_target_pairs={{0,4},{1,5},{2,6},{3,7},{4,0},{5,1},{6,2},{7,3},{8,12},{9,13},{10,... | collective-permute-start | bytes 196616 | tf_op jit(solution)/shard_map/ppermute | solution.py:350
  39.3 6.8 %collective-permute-start.14 = (bf16[128,256]{1,0:T(8,128)(2,1)S(1)}, bf16[128,256]{1,0:T(8,128)(2,1)S(1)}, u32[]{:S(2)}, u32[]{:S(2)}) collective-permute-start(bf16[128,256]{1,0:T(8,128)(2,1)S(1)} %shard_map.167.refs_4_), channel_id=1, source_target_pairs={{0,4},{1,5},{2,6},{3,7},{4,0},{5,1},{6,2},{7,3},{8,12},{9,13},{10,... | collective-permute-start | bytes 196616 | tf_op jit(solution)/shard_map/ppermute | solution.py:350
  41.1 7.0 %collective-permute-start.13 = (bf16[128,256]{1,0:T(8,128)(2,1)S(1)}, bf16[128,256]{1,0:T(8,128)(2,1)S(1)}, u32[]{:S(2)}, u32[]{:S(2)}) collective-permute-start(bf16[128,256]{1,0:T(8,128)(2,1)S(1)} %shard_map.167.refs_4_), channel_id=1, source_target_pairs={{0,3},{1,2},{2,1},{3,0},{4,7},{5,6},{6,5},{7,4},{8,11},{9,10},{10,... | collective-permute-start | bytes 196616 | tf_op jit(solution)/shard_map/ppermute | solution.py:350
  42.2 7.4 %collective-permute-start.12 = (bf16[128,256]{1,0:T(8,128)(2,1)S(1)}, bf16[128,256]{1,0:T(8,128)(2,1)S(1)}, u32[]{:S(2)}, u32[]{:S(2)}) collective-permute-start(bf16[128,256]{1,0:T(8,128)(2,1)S(1)} %shard_map.167.refs_4_), channel_id=1, source_target_pairs={{0,2},{1,3},{2,0},{3,1},{4,6},{5,7},{6,4},{7,5},{8,10},{9,11},{10,... | collective-permute-start | bytes 196616 | tf_op jit(solution)/shard_map/ppermute | solution.py:350
  43.1 6.6 %collective-permute-start.11 = (bf16[128,256]{1,0:T(8,128)(2,1)S(1)}, bf16[128,256]{1,0:T(8,128)(2,1)S(1)}, u32[]{:S(2)}, u32[]{:S(2)}) collective-permute-start(bf16[128,256]{1,0:T(8,128)(2,1)S(1)} %shard_map.167.refs_4_), channel_id=1, source_target_pairs={{0,1},{1,0},{2,3},{3,2},{4,5},{5,4},{6,7},{7,6},{8,9},{9,8},{10,11... | collective-permute-start | bytes 196616 | tf_op jit(solution)/shard_map/ppermute | solution.py:350
  46.1 7.4 %collective-permute-start.18 = (bf16[128,512]{1,0:T(8,128)(2,1)S(1)}, bf16[128,512]{1,0:T(8,128)(2,1)S(1)}, u32[]{:S(2)}, u32[]{:S(2)}) collective-permute-start(bf16[128,512]{1,0:T(8,128)(2,1)S(1)} %shard_map.170.refs_4_), channel_id=1, source_target_pairs={{0,3},{1,2},{2,1},{3,0},{4,7},{5,6},{6,5},{7,4},{8,11},{9,10},{10,... | collective-permute-start | bytes 393224 | tf_op jit(solution)/shard_map/ppermute | solution.py:350
  47.0 8.3 %collective-permute-start.17 = (bf16[128,512]{1,0:T(8,128)(2,1)S(1)}, bf16[128,512]{1,0:T(8,128)(2,1)S(1)}, u32[]{:S(2)}, u32[]{:S(2)}) collective-permute-start(bf16[128,512]{1,0:T(8,128)(2,1)S(1)} %shard_map.170.refs_4_), channel_id=1, source_target_pairs={{0,2},{1,3},{2,0},{3,1},{4,6},{5,7},{6,4},{7,5},{8,10},{9,11},{10,... | collective-permute-start | bytes 393224 | tf_op jit(solution)/shard_map/ppermute | solution.py:350
  48.1 7.3 %collective-permute-start.16 = (bf16[128,512]{1,0:T(8,128)(2,1)S(1)}, bf16[128,512]{1,0:T(8,128)(2,1)S(1)}, u32[]{:S(2)}, u32[]{:S(2)}) collective-permute-start(bf16[128,512]{1,0:T(8,128)(2,1)S(1)} %shard_map.170.refs_4_), channel_id=1, source_target_pairs={{0,1},{1,0},{2,3},{3,2},{4,5},{5,4},{6,7},{7,6},{8,9},{9,8},{10,11... | collective-permute-start | bytes 393224 | tf_op jit(solution)/shard_map/ppermute | solution.py:350
  50.5 7.7 %collective-permute-start.19 = (bf16[128,256]{1,0:T(8,128)(2,1)S(1)}, bf16[128,256]{1,0:T(8,128)(2,1)S(1)}, u32[]{:S(2)}, u32[]{:S(2)}) collective-permute-start(bf16[128,256]{1,0:T(8,128)(2,1)S(1)} %get-tuple-element.101), channel_id=1, source_target_pairs={{0,2},{1,3},{2,0},{3,1},{4,6},{5,7},{6,4},{7,5},{8,10},{9,11},{10,... | collective-permute-start | bytes 196616 | tf_op jit(solution)/shard_map/ppermute | solution.py:350
  50.6 7.7 %collective-permute-start.20 = (bf16[128,256]{1,0:T(8,128)(2,1)S(1)}, bf16[128,256]{1,0:T(8,128)(2,1)S(1)}, u32[]{:S(2)}, u32[]{:S(2)}) collective-permute-start(bf16[128,256]{1,0:T(8,128)(2,1)S(1)} %get-tuple-element.102), channel_id=1, source_target_pairs={{0,3},{1,2},{2,1},{3,0},{4,7},{5,6},{6,5},{7,4},{8,11},{9,10},{10,... | collective-permute-start | bytes 196616 | tf_op jit(solution)/shard_map/ppermute | solution.py:350
  53.4 5.0 %collective-permute-start.21 = (bf16[128,256]{1,0:T(8,128)(2,1)S(1)}, bf16[128,256]{1,0:T(8,128)(2,1)S(1)}, u32[]{:S(2)}, u32[]{:S(2)}) collective-permute-start(bf16[128,256]{1,0:T(8,128)(2,1)S(1)} %get-tuple-element.103), channel_id=1, source_target_pairs={{0,1},{1,0},{2,3},{3,2},{4,5},{5,4},{6,7},{7,6},{8,9},{9,8},{10,11... | collective-permute-start | bytes 196616 | tf_op jit(solution)/shard_map/ppermute | solution.py:350
  58.4 18.4 %collective-permute-start.22 = (bf16[672,128]{1,0:T(8,128)(2,1)S(1)}, bf16[672,128]{1,0:T(8,128)(2,1)S(1)}, u32[]{:S(2)}, u32[]{:S(2)}) collective-permute-start(bf16[672,128]{1,0:T(8,128)(2,1)S(1)} %get-tuple-element.108), channel_id=1, source_target_pairs={{0,1},{1,0},{2,3},{3,2},{4,5},{5,4},{6,7},{7,6},{8,9},{9,8},{10,11... | collective-permute-start | bytes 516104 | tf_op jit(solution)/shard_map/ppermute | solution.py:350
  59.7 17.1 %collective-permute-start.23 = (bf16[672,128]{1,0:T(8,128)(2,1)S(1)}, bf16[672,128]{1,0:T(8,128)(2,1)S(1)}, u32[]{:S(2)}, u32[]{:S(2)}) collective-permute-start(bf16[672,128]{1,0:T(8,128)(2,1)S(1)} %get-tuple-element.109), channel_id=1, source_target_pairs={{0,2},{1,3},{2,0},{3,1},{4,6},{5,7},{6,4},{7,5},{8,10},{9,11},{10,... | collective-permute-start | bytes 516104 | tf_op jit(solution)/shard_map/ppermute | solution.py:350
  60.1 16.7 %collective-permute-start.24 = (bf16[672,128]{1,0:T(8,128)(2,1)S(1)}, bf16[672,128]{1,0:T(8,128)(2,1)S(1)}, u32[]{:S(2)}, u32[]{:S(2)}) collective-permute-start(bf16[672,128]{1,0:T(8,128)(2,1)S(1)} %get-tuple-element.110), channel_id=1, source_target_pairs={{0,3},{1,2},{2,1},{3,0},{4,7},{5,6},{6,5},{7,4},{8,11},{9,10},{10,... | collective-permute-start | bytes 516104 | tf_op jit(solution)/shard_map/ppermute | solution.py:350
  61.9 7.0 %collective-permute-start.25 = (bf16[64,576]{1,0:T(8,128)(2,1)S(1)}, bf16[64,576]{1,0:T(8,128)(2,1)S(1)}, u32[]{:S(2)}, u32[]{:S(2)}) collective-permute-start(bf16[64,576]{1,0:T(8,128)(2,1)S(1)} %get-tuple-element.114), channel_id=1, source_target_pairs={{0,4},{1,5},{2,6},{3,7},{4,0},{5,1},{6,2},{7,3},{8,12},{9,13},{10,... | collective-permute-start | bytes 221192 | tf_op jit(solution)/shard_map/ppermute | solution.py:350
  63.3 9.0 %collective-permute-start.26 = (bf16[64,576]{1,0:T(8,128)(2,1)S(1)}, bf16[64,576]{1,0:T(8,128)(2,1)S(1)}, u32[]{:S(2)}, u32[]{:S(2)}) collective-permute-start(bf16[64,576]{1,0:T(8,128)(2,1)S(1)} %get-tuple-element.115), channel_id=1, source_target_pairs={{0,6},{1,7},{2,4},{3,5},{4,2},{5,3},{6,0},{7,1},{8,14},{9,15},{10,... | collective-permute-start | bytes 221192 | tf_op jit(solution)/shard_map/ppermute | solution.py:350
  72.3 4.5 %collective-permute-start.27 = (bf16[64,576]{1,0:T(8,128)(2,1)S(1)}, bf16[64,576]{1,0:T(8,128)(2,1)S(1)}, u32[]{:S(2)}, u32[]{:S(2)}) collective-permute-start(bf16[64,576]{1,0:T(8,128)(2,1)S(1)} %shard_map.173), channel_id=1, source_target_pairs={{0,1},{1,0},{2,3},{3,2},{4,5},{5,4},{6,7},{7,6},{8,9},{9,8},{10,11... | collective-permute-start | bytes 221192 | tf_op jit(solution)/shard_map/ppermute | solution.py:350

commit v15 on v14

--- a/solution.py
+++ b/solution.py
@@ -391,14 +391,15 @@
             24,
             flops=3 * mflop,
         )
+        *parts, queries = lax.optimization_barrier((*parts, queries))
         parts = [parts[0]] + [move(parts[d], d) for d in (*range(2, group), *range(1, min(2, group)))]
+        q_mirror = mirror(queries)
         *parts, kv_near = lax.optimization_barrier((*parts, kv_near))
         apply_out, sums = call(
             reduce_kernel, (arr((own, feat), F32), arr((2, own), F32)), (gg, *parts), 16
         )
-        sums, queries = lax.optimization_barrier((sums, queries))
         sums = [sums] + [move(sums, d, "head", head_n) for d in range(1, head_n)]
-        q_mirror = mirror(queries)
+        sums, q_mirror = lax.optimization_barrier((sums, q_mirror))
         (od,) = call(functools.partial(delta_kernel, head_n * feat), (block,), (apply_out, gg, *sums), 16)
         od_mirror = mirror(od)
         od_near = near_all(od)
@@ -452,6 +453,7 @@
             (arr((len(far) * padded(rows), 3 * slab), BF),),
             far_got,
             16,
+            flops=12 * mflop,
         )
         relayed = move(relayed, 1)
         out_tok = arr((1, own, feat), BF)
@@ -459,6 +461,7 @@
         grads_t = call(
             functools.partial(tokens_kernel, group), (out_tok,) * 3, (rate, tok, *grad_q, *near_got), 16
         )
+        relayed, grads_t = lax.optimization_barrier((relayed, grads_t))
         at = 2 * tiles(feat) * padded(own)
         grads_w = call(
             functools.partial(weights_kernel, group, tok_groups, slab, at),

time: 79.2 us -> 76.2 us (0.962)
  waiting for transfers between devices: 25.6 us -> 20.7 us
  starting transfers between devices: 41.1 us -> 43.2 us
    ppermute x28, waiting for transfers between devices: 25.6 us -> 20.7 us  [move(): return lax.ppermute(x, axis, [(i, i ^ dist) for i in range(size)])]
    ppermute x28, starting transfers between devices: 33.9 us -> 35.9 us  [move(): return lax.ppermute(x, axis, [(i, i ^ dist) for i in range(size)])]
  transfers between devices with their start and end apart: 29 -> 29, of which waited for: 15 -> 12; matrix products, arithmetic and copies ran while one was open for 0% -> 0% of each run, Pallas kernels for 7% -> 8%
where the time goes in v15:
time: 76.2 us; the launch traced here: 75.9 us
  starting transfers between devices  43.2 us (57%)
  waiting for transfers between devices  20.7 us (27%)
  Pallas kernels  9.76 us (13%)
  local copies, waits for them, and re-layouts  1.35 us (2%)
  between operations  0.84 us (1%)
    ppermute x28, starting transfers between devices, move(): return lax.ppermute(x, axis, [(i, i ^ dist) for i in range(size)])  35.9 us
    ppermute x28, waiting for transfers between devices, move(): return lax.ppermute(x, axis, [(i, i ^ dist) for i in range(size)])  20.7 us
    pallas_call x11, Pallas kernels, call(): pl.pallas_call(kernel, out_shape=outs, in_specs=[SMEM] * smem + [VMEM] *...  7.8 us
    all_to_all x1, starting transfers between devices, local(): lax.all_to_all(packed, 'seq', 0, 0, tiled=True)  7.26 us
    pallas_call x1, Pallas kernels, copying_call(): pl.pallas_call(kernel, out_shape=outs, in_specs=[pl.BlockSpec(memory_spac...  1.96 us
  transfers between devices with their start and end apart: 29, of which 12 were waited for; matrix products, arithmetic and copies ran while one was open for 0% of the time, Pallas kernels for 8%

profile of v15, /device:TPU:0, one launch (start us, length us, event | category | flops | bytes accessed | tf_op | source)
XLA Modules:
  0.0 75.9 jit_solution(7350270265980019918)
XLA Ops:
  0.7 2.0 %shard_map.163 = bf16[8,32,1152]{2,1,0:T(8,128)(2,1)} custom-call(bf16[1,32,768]{2,1,0:T(8,128)(2,1)} %refs_0_.1, bf16[1,32,768]{2,1,0:T(8,128)(2,1)} %refs_1_.1, bf16[1,32,768]{2,1,0:T(8,128)(2,1)} %refs_2_.1, bf16[1,32,768]{2,1,0:T(8,128)(2,1)} %refs_3_.1, bf16[1,32,768]{2,1,0:T(8,128)(2,1)} %refs_4_.1, bf16[1,32,768]{2,1,0:T(8,128)(2,1)} %refs_5_.1), custom_call_target="tpu_custom_call" | custom-call | tf_op jit(solution)/shard_map/pallas_call | solution.py:61
  2.6 7.3 %all-to-all-start = ((bf16[8,32,1152]{2,1,0:T(8,128)(2,1)}), bf16[8,32,1152]{2,1,0:T(8,128)(2,1)S(1)}, u32[]{:S(2)}, u32[]{:S(2)}) async-start(bf16[8,32,1152]{2,1,0:T(8,128)(2,1)} %shard_map.163), calls=%async_computation | async-start | bytes 1179648 | tf_op jit(solution)/shard_map/all_to_all | solution.py:373
  9.9 0.0 copy-start.4
  10.0 0.7 copy-done.4
  10.6 0.7 copy-done.5
  11.3 0.1 shard_map.164
  11.4 2.1 %collective-permute-start = (bf16[128,768]{1,0:T(8,128)(2,1)S(1)}, bf16[128,768]{1,0:T(8,128)(2,1)S(1)}, u32[]{:S(2)}, u32[]{:S(2)}) collective-permute-start(bf16[128,768]{1,0:T(8,128)(2,1)S(1)} %get-tuple-element.77), channel_id=1, source_target_pairs={{0,1},{1,0},{2,3},{3,2},{4,5},{5,4},{6,7},{7,6},{8,9},{9,8},{10,11... | collective-permute-start | bytes 589832 | tf_op jit(solution)/shard_map/ppermute | solution.py:350
  13.5 1.5 %collective-permute-start.7 = (bf16[128,512]{1,0:T(8,128)(2,1)S(1)}, bf16[128,512]{1,0:T(8,128)(2,1)S(1)}, u32[]{:S(2)}, u32[]{:S(2)}) collective-permute-start(bf16[128,512]{1,0:T(8,128)(2,1)S(1)} %get-tuple-element.101.refs_0_), channel_id=1, source_target_pairs={{0,3},{1,2},{2,1},{3,0},{4,7},{5,6},{6,5},{7,4},{8,11},{9,10},{10,... | collective-permute-start | bytes 393224 | tf_op jit(solution)/shard_map/ppermute | solution.py:350
  14.9 1.5 %collective-permute-start.2 = (bf16[128,256]{1,0:T(8,128)(2,1)S(1)}, bf16[128,256]{1,0:T(8,128)(2,1)S(1)}, u32[]{:S(2)}, u32[]{:S(2)}) collective-permute-start(bf16[128,256]{1,0:T(8,128)(2,1)S(1)} %bitcast.8), channel_id=1, source_target_pairs={{0,3},{1,2},{2,1},{3,0},{4,7},{5,6},{6,5},{7,4},{8,11},{9,10},{10,... | collective-permute-start | bytes 196616 | tf_op jit(solution)/shard_map/ppermute | solution.py:350
  16.4 1.5 %collective-permute-start.1 = (bf16[128,256]{1,0:T(8,128)(2,1)S(1)}, bf16[128,256]{1,0:T(8,128)(2,1)S(1)}, u32[]{:S(2)}, u32[]{:S(2)}) collective-permute-start(bf16[128,256]{1,0:T(8,128)(2,1)S(1)} %bitcast.9), channel_id=1, source_target_pairs={{0,2},{1,3},{2,0},{3,1},{4,6},{5,7},{6,4},{7,5},{8,10},{9,11},{10,... | collective-permute-start | bytes 196616 | tf_op jit(solution)/shard_map/ppermute | solution.py:350
  17.9 0.6 collective-permute-start.6
  18.4 9.5 %collective-permute-done.2.refs_3_ = bf16[128,256]{1,0:T(8,128)(2,1)S(1)} collective-permute-done((bf16[128,256]{1,0:T(8,128)(2,1)S(1)}, bf16[128,256]{1,0:T(8,128)(2,1)S(1)}, u32[]{:S(2)}, u32[]{:S(2)}) %collective-permute-start.2) | collective-permute-done | bytes 65568 | tf_op jit(solution)/shard_map/ppermute | solution.py:350
  27.9 0.0 collective-permute-done.1.refs_2_
  28.0 0.0 collective-permute-done.refs_1_
  28.0 0.8 %shard_map.165 = (bf16[128,256]{1,0:T(8,128)(2,1)S(1)}, bf16[128,256]{1,0:T(8,128)(2,1)S(1)}, bf16[128,256]{1,0:T(8,128)(2,1)S(1)}, bf16[128,256]{1,0:T(8,128)(2,1)S(1)}, bf16[256,576]{1,0:T(8,128)(2,1)S(1)}) custom-call(bf16[256,1152]{1,0:T(8,128)(2,1)S(1)} %bitcast.5, bf16[128,256]{1,0:T(8,128)(2,1)S(1)} %bitcast.10, ...), custom_call_target="tpu_custom_call" | custom-call | flops 150994944 | bytes 1540096 | tf_op jit(solution)/shard_map/pallas_call | solution.py:49
  28.7 1.3 %collective-permute-start.3 = (bf16[128,256]{1,0:T(8,128)(2,1)S(1)}, bf16[128,256]{1,0:T(8,128)(2,1)S(1)}, u32[]{:S(2)}, u32[]{:S(2)}) collective-permute-start(bf16[128,256]{1,0:T(8,128)(2,1)S(1)} %get-tuple-element.85), channel_id=1, source_target_pairs={{0,2},{1,3},{2,0},{3,1},{4,6},{5,7},{6,4},{7,5},{8,10},{9,11},{10,... | collective-permute-start | bytes 196616 | tf_op jit(solution)/shard_map/ppermute | solution.py:350
  30.1 2.2 %collective-permute-start.4 = (bf16[128,256]{1,0:T(8,128)(2,1)S(1)}, bf16[128,256]{1,0:T(8,128)(2,1)S(1)}, u32[]{:S(2)}, u32[]{:S(2)}) collective-permute-start(bf16[128,256]{1,0:T(8,128)(2,1)S(1)} %get-tuple-element.86), channel_id=1, source_target_pairs={{0,3},{1,2},{2,1},{3,0},{4,7},{5,6},{6,5},{7,4},{8,11},{9,10},{10,... | collective-permute-start | bytes 196616 | tf_op jit(solution)/shard_map/ppermute | solution.py:350
  32.2 0.1 collective-permute-start.5
  32.3 0.0 collective-permute-done.7.refs_3_
  32.3 3.3 %collective-permute-start.11 = (bf16[128,256]{1,0:T(8,128)(2,1)S(1)}, bf16[128,256]{1,0:T(8,128)(2,1)S(1)}, u32[]{:S(2)}, u32[]{:S(2)}) collective-permute-start(bf16[128,256]{1,0:T(8,128)(2,1)S(1)} %bitcast.11), channel_id=1, source_target_pairs={{0,4},{1,5},{2,6},{3,7},{4,0},{5,1},{6,2},{7,3},{8,12},{9,13},{10,... | collective-permute-start | bytes 196616 | tf_op jit(solution)/shard_map/ppermute | solution.py:350
  35.6 0.0 collective-permute-done.6.refs_2_
  35.6 0.0 collective-permute-done.3.refs_1_
  35.6 0.3 collective-permute-done.4.refs_2_
  35.9 0.7 collective-permute-done.5.refs_3_
  36.5 0.1 shard_map.166
  36.7 0.1 collective-permute-start.10
  36.8 1.6 %collective-permute-start.9 = (f32[2,128]{1,0:T(2,128)S(1)}, f32[2,128]{1,0:T(2,128)S(1)}, u32[]{:S(2)}, u32[]{:S(2)}) collective-permute-start(f32[2,128]{1,0:T(2,128)S(1)} %get-tuple-element.96.refs_0_), channel_id=1, source_target_pairs={{0,16},{8,24},{16,0},{24,8},{1,17},{9,25},{17,1},{25,9},{2,18},{10... | collective-permute-start | bytes 3080 | tf_op jit(solution)/shard_map/ppermute | solution.py:350
  38.4 0.3 collective-permute-start.8
  38.6 0.0 collective-permute-done.11.right
  38.6 1.1 %collective-permute-done.10.refs_3_ = f32[2,128]{1,0:T(2,128)S(1)} collective-permute-done((f32[2,128]{1,0:T(2,128)S(1)}, f32[2,128]{1,0:T(2,128)S(1)}, u32[]{:S(2)}, u32[]{:S(2)}) %collective-permute-start.10) | collective-permute-done | bytes 1056 | tf_op jit(solution)/shard_map/ppermute | solution.py:350
  39.8 0.7 collective-permute-done.9.refs_2_
  40.4 0.1 shard_map.167.refs_4_
  40.6 2.8 %collective-permute-start.15 = (bf16[128,256]{1,0:T(8,128)(2,1)S(1)}, bf16[128,256]{1,0:T(8,128)(2,1)S(1)}, u32[]{:S(2)}, u32[]{:S(2)}) collective-permute-start(bf16[128,256]{1,0:T(8,128)(2,1)S(1)} %shard_map.167.refs_4_), channel_id=1, source_target_pairs={{0,4},{1,5},{2,6},{3,7},{4,0},{5,1},{6,2},{7,3},{8,12},{9,13},{10,... | collective-permute-start | bytes 196616 | tf_op jit(solution)/shard_map/ppermute | solution.py:350
  43.3 1.3 %collective-permute-start.14 = (bf16[128,256]{1,0:T(8,128)(2,1)S(1)}, bf16[128,256]{1,0:T(8,128)(2,1)S(1)}, u32[]{:S(2)}, u32[]{:S(2)}) collective-permute-start(bf16[128,256]{1,0:T(8,128)(2,1)S(1)} %shard_map.167.refs_4_), channel_id=1, source_target_pairs={{0,3},{1,2},{2,1},{3,0},{4,7},{5,6},{6,5},{7,4},{8,11},{9,10},{10,... | collective-permute-start | bytes 196616 | tf_op jit(solution)/shard_map/ppermute | solution.py:350
  44.6 0.8 %collective-permute-start.13 = (bf16[128,256]{1,0:T(8,128)(2,1)S(1)}, bf16[128,256]{1,0:T(8,128)(2,1)S(1)}, u32[]{:S(2)}, u32[]{:S(2)}) collective-permute-start(bf16[128,256]{1,0:T(8,128)(2,1)S(1)} %shard_map.167.refs_4_), channel_id=1, source_target_pairs={{0,2},{1,3},{2,0},{3,1},{4,6},{5,7},{6,4},{7,5},{8,10},{9,11},{10,... | collective-permute-start | bytes 196616 | tf_op jit(solution)/shard_map/ppermute | solution.py:350
  45.4 1.5 %collective-permute-start.12 = (bf16[128,256]{1,0:T(8,128)(2,1)S(1)}, bf16[128,256]{1,0:T(8,128)(2,1)S(1)}, u32[]{:S(2)}, u32[]{:S(2)}) collective-permute-start(bf16[128,256]{1,0:T(8,128)(2,1)S(1)} %shard_map.167.refs_4_), channel_id=1, source_target_pairs={{0,1},{1,0},{2,3},{3,2},{4,5},{5,4},{6,7},{7,6},{8,9},{9,8},{10,11... | collective-permute-start | bytes 196616 | tf_op jit(solution)/shard_map/ppermute | solution.py:350
  46.8 0.1 pad_add_fusion.place
  46.9 1.1 %shard_map.169 = (f32[4,512,192]{2,1,0:T(8,128)S(1)}, bf16[3,512,192]{2,1,0:T(8,128)(2,1)S(1)}, f32[3,192]{1,0:T(4,128)S(1)}, f32[3,256,192]{2,1,0:T(8,128)S(1)}, f32[3,256,192]{2,1,0:T(8,128)S(1)}) custom-call(bf16[256,1152]{1,0:T(8,128)(2,1)S(1)} %bitcast.6, bf16[128,512]{1,0:T(8,128)(2,1)S(1)} %get-tuple-element.101.refs_0_, ...), custom_call_target="tpu_custom_call" | custom-call | flops 603979776 | bytes 4524288 | tf_op jit(solution)/shard_map/pallas_call | solution.py:49
  48.1 1.3 %collective-permute-start.18 = (bf16[128,512]{1,0:T(8,128)(2,1)S(1)}, bf16[128,512]{1,0:T(8,128)(2,1)S(1)}, u32[]{:S(2)}, u32[]{:S(2)}) collective-permute-start(bf16[128,512]{1,0:T(8,128)(2,1)S(1)} %shard_map.170.refs_4_), channel_id=1, source_target_pairs={{0,3},{1,2},{2,1},{3,0},{4,7},{5,6},{6,5},{7,4},{8,11},{9,10},{10,... | collective-permute-start | bytes 393224 | tf_op jit(solution)/shard_map/ppermute | solution.py:350
  49.4 0.8 %collective-permute-start.17 = (bf16[128,512]{1,0:T(8,128)(2,1)S(1)}, bf16[128,512]{1,0:T(8,128)(2,1)S(1)}, u32[]{:S(2)}, u32[]{:S(2)}) collective-permute-start(bf16[128,512]{1,0:T(8,128)(2,1)S(1)} %shard_map.170.refs_4_), channel_id=1, source_target_pairs={{0,2},{1,3},{2,0},{3,1},{4,6},{5,7},{6,4},{7,5},{8,10},{9,11},{10,... | collective-permute-start | bytes 393224 | tf_op jit(solution)/shard_map/ppermute | solution.py:350
  50.2 0.0 collective-permute-done.14.refs_7_
  50.2 1.5 %collective-permute-start.16 = (bf16[128,512]{1,0:T(8,128)(2,1)S(1)}, bf16[128,512]{1,0:T(8,128)(2,1)S(1)}, u32[]{:S(2)}, u32[]{:S(2)}) collective-permute-start(bf16[128,512]{1,0:T(8,128)(2,1)S(1)} %shard_map.170.refs_4_), channel_id=1, source_target_pairs={{0,1},{1,0},{2,3},{3,2},{4,5},{5,4},{6,7},{7,6},{8,9},{9,8},{10,11... | collective-permute-start | bytes 393224 | tf_op jit(solution)/shard_map/ppermute | solution.py:350
  51.6 0.8 %shard_map.168 = (bf16[128,256]{1,0:T(8,128)(2,1)S(1)}, bf16[128,256]{1,0:T(8,128)(2,1)S(1)}, bf16[128,256]{1,0:T(8,128)(2,1)S(1)}, bf16[128,256]{1,0:T(8,128)(2,1)S(1)}, f32[3,256,192]{2,1,0:T(8,128)S(1)}) custom-call(bf16[256,576]{1,0:T(8,128)(2,1)S(1)} %get-tuple-element.78.normed_ref, bf16[128,256]{1,0:T(8,128)(2,1)S(1)} %bitcast.12, ...), custom_call_target="tpu_custom_call" | custom-call | flops 3019898880 | bytes 1802240 | tf_op jit(solution)/shard_map/pallas_call | solution.py:49
  52.4 0.8 %collective-permute-start.19 = (bf16[128,256]{1,0:T(8,128)(2,1)S(1)}, bf16[128,256]{1,0:T(8,128)(2,1)S(1)}, u32[]{:S(2)}, u32[]{:S(2)}) collective-permute-start(bf16[128,256]{1,0:T(8,128)(2,1)S(1)} %get-tuple-element.119), channel_id=1, source_target_pairs={{0,2},{1,3},{2,0},{3,1},{4,6},{5,7},{6,4},{7,5},{8,10},{9,11},{10,... | collective-permute-start | bytes 196616 | tf_op jit(solution)/shard_map/ppermute | solution.py:350
  53.3 1.3 %collective-permute-start.20 = (bf16[128,256]{1,0:T(8,128)(2,1)S(1)}, bf16[128,256]{1,0:T(8,128)(2,1)S(1)}, u32[]{:S(2)}, u32[]{:S(2)}) collective-permute-start(bf16[128,256]{1,0:T(8,128)(2,1)S(1)} %get-tuple-element.120), channel_id=1, source_target_pairs={{0,3},{1,2},{2,1},{3,0},{4,7},{5,6},{6,5},{7,4},{8,11},{9,10},{10,... | collective-permute-start | bytes 196616 | tf_op jit(solution)/shard_map/ppermute | solution.py:350
  54.5 0.9 %collective-permute-done.18.refs_7_ = bf16[128,512]{1,0:T(8,128)(2,1)S(1)} collective-permute-done((bf16[128,512]{1,0:T(8,128)(2,1)S(1)}, bf16[128,512]{1,0:T(8,128)(2,1)S(1)}, u32[]{:S(2)}, u32[]{:S(2)}) %collective-permute-start.18) | collective-permute-done | bytes 131104 | tf_op jit(solution)/shard_map/ppermute | solution.py:350
  55.5 0.6 collective-permute-start.21
  56.0 1.0 %collective-permute-done.17.refs_6_ = bf16[128,512]{1,0:T(8,128)(2,1)S(1)} collective-permute-done((bf16[128,512]{1,0:T(8,128)(2,1)S(1)}, bf16[128,512]{1,0:T(8,128)(2,1)S(1)}, u32[]{:S(2)}, u32[]{:S(2)}) %collective-permute-start.17) | collective-permute-done | bytes 131104 | tf_op jit(solution)/shard_map/ppermute | solution.py:350
  57.1 0.9 %collective-permute-done.16.refs_5_ = bf16[128,512]{1,0:T(8,128)(2,1)S(1)} collective-permute-done((bf16[128,512]{1,0:T(8,128)(2,1)S(1)}, bf16[128,512]{1,0:T(8,128)(2,1)S(1)}, u32[]{:S(2)}, u32[]{:S(2)}) %collective-permute-start.16) | collective-permute-done | bytes 131104 | tf_op jit(solution)/shard_map/ppermute | solution.py:350
  58.0 2.6 %shard_map.171 = (bf16[128,512]{1,0:T(8,128)(2,1)S(1)}, bf16[32,576]{1,0:T(8,128)(2,1)S(1)}, bf16[672,128]{1,0:T(8,128)(2,1)S(1)}, bf16[672,128]{1,0:T(8,128)(2,...) custom-call(s32[3]{0:T(128)S(1)} %pad_add_fusion.place, ...), custom_call_target="tpu_custom_call" | custom-call | flops 6039797760 | bytes 6764812 | tf_op jit(solution)/shard_map/pallas_call | solution.py:49
  60.5 0.0 collective-permute-done.20.refs_2_
  60.5 1.1 %collective-permute-start.22 = (bf16[64,576]{1,0:T(8,128)(2,1)S(1)}, bf16[64,576]{1,0:T(8,128)(2,1)S(1)}, u32[]{:S(2)}, u32[]{:S(2)}) collective-permute-start(bf16[64,576]{1,0:T(8,128)(2,1)S(1)} %get-tuple-element.122), channel_id=1, source_target_pairs={{0,4},{1,5},{2,6},{3,7},{4,0},{5,1},{6,2},{7,3},{8,12},{9,13},{10,... | collective-permute-start | bytes 221192 | tf_op jit(solution)/shard_map/ppermute | solution.py:350
  61.6 2.1 %collective-permute-start.23 = (bf16[64,576]{1,0:T(8,128)(2,1)S(1)}, bf16[64,576]{1,0:T(8,128)(2,1)S(1)}, u32[]{:S(2)}, u32[]{:S(2)}) collective-permute-start(bf16[64,576]{1,0:T(8,128)(2,1)S(1)} %get-tuple-element.123), channel_id=1, source_target_pairs={{0,6},{1,7},{2,4},{3,5},{4,2},{5,3},{6,0},{7,1},{8,14},{9,15},{10,... | collective-permute-start | bytes 221192 | tf_op jit(solution)/shard_map/ppermute | solution.py:350
  63.7 1.1 %collective-permute-start.25 = (bf16[672,128]{1,0:T(8,128)(2,1)S(1)}, bf16[672,128]{1,0:T(8,128)(2,1)S(1)}, u32[]{:S(2)}, u32[]{:S(2)}) collective-permute-start(bf16[672,128]{1,0:T(8,128)(2,1)S(1)} %get-tuple-element.130), channel_id=1, source_target_pairs={{0,1},{1,0},{2,3},{3,2},{4,5},{5,4},{6,7},{7,6},{8,9},{9,8},{10,11... | collective-permute-start | bytes 516104 | tf_op jit(solution)/shard_map/ppermute | solution.py:350
  64.8 0.0 collective-permute-start.26
  64.8 2.4 %collective-permute-start.27 = (bf16[672,128]{1,0:T(8,128)(2,1)S(1)}, bf16[672,128]{1,0:T(8,128)(2,1)S(1)}, u32[]{:S(2)}, u32[]{:S(2)}) collective-permute-start(bf16[672,128]{1,0:T(8,128)(2,1)S(1)} %get-tuple-element.132), channel_id=1, source_target_pairs={{0,3},{1,2},{2,1},{3,0},{4,7},{5,6},{6,5},{7,4},{8,11},{9,10},{10,... | collective-permute-start | bytes 516104 | tf_op jit(solution)/shard_map/ppermute | solution.py:350
  67.2 1.6 %collective-permute-done.23.refs_1_.refs_4_ = bf16[64,576]{1,0:T(8,128)(2,1)S(1)} collective-permute-done((bf16[64,576]{1,0:T(8,128)(2,1)S(1)}, bf16[64,576]{1,0:T(8,128)(2,1)S(1)}, u32[]{:S(2)}, u32[]{:S(2)}) %collective-permute-start.23) | collective-permute-done | bytes 73760 | tf_op jit(solution)/shard_map/ppermute | solution.py:350
  68.8 1.0 %collective-permute-start.24 = (bf16[64,576]{1,0:T(8,128)(2,1)S(1)}, bf16[64,576]{1,0:T(8,128)(2,1)S(1)}, u32[]{:S(2)}, u32[]{:S(2)}) collective-permute-start(bf16[64,576]{1,0:T(8,128)(2,1)S(1)} %shard_map.172), channel_id=1, source_target_pairs={{0,1},{1,0},{2,3},{3,2},{4,5},{5,4},{6,7},{7,6},{8,9},{9,8},{10,11... | collective-permute-start | bytes 221192 | tf_op jit(solution)/shard_map/ppermute | solution.py:350
  69.9 1.9 %collective-permute-done.25.refs_4_.refs_0_ = bf16[672,128]{1,0:T(8,128)(2,1)S(1)} collective-permute-done((bf16[672,128]{1,0:T(8,128)(2,1)S(1)}, bf16[672,128]{1,0:T(8,128)(2,1)S(1)}, u32[]{:S(2)}, u32[]{:S(2)}) %collective-permute-start.25) | collective-permute-done | bytes 172064 | tf_op jit(solution)/shard_map/ppermute | solution.py:350
  71.7 0.2 collective-permute-done.26.refs_5_.refs_1_
  72.0 1.8 %collective-permute-done.27.refs_6_.refs_2_ = bf16[672,128]{1,0:T(8,128)(2,1)S(1)} collective-permute-done((bf16[672,128]{1,0:T(8,128)(2,1)S(1)}, bf16[672,128]{1,0:T(8,128)(2,1)S(1)}, u32[]{:S(2)}, u32[]{:S(2)}) %collective-permute-start.27) | collective-permute-done | bytes 172064 | tf_op jit(solution)/shard_map/ppermute | solution.py:350
  73.7 0.7 shard_map.173
  74.5 0.0 collective-permute-done.24.relayed
  74.5 1.4 %shard_map.174 = (f32[1,32,768]{2,1,0:T(8,128)}, f32[1,32,768]{2,1,0:T(8,128)}, f32[1,32,768]{2,1,0:T(8,128)}) custom-call(s32[3]{0:T(128)S(1)} %pad_add_fusion.place, bf16[64,576]{1,0:T(8,128)(2,1)S(1)} %collective-permute-done.24.relayed, bf16[32,576]{1,0:T(8,128)(2,1)S(1)} %get-tuple-element.140.inner, ...), custom_call_target="tpu_custom_call" | custom-call | bytes 1069068 | tf_op jit(solution)/shard_map/pallas_call | solution.py:49
  (19 shorter events, 0.1 us)
Async XLA Ops:
  0.6 9.3 %copy-start = (bf16[1,128,256]{2,1,0:T(8,128)(2,1)S(1)}, bf16[1,128,256]{2,1,0:T(8,128)(2,1)}, u32[]{:S(2)}) copy-start(bf16[1,128,256]{2,1,0:T(8,128)(2,1)} %q.1) | copy-start | bytes 196612
  0.6 9.3 %copy-start.3 = (bf16[1,128,256]{2,1,0:T(8,128)(2,1)S(1)}, bf16[1,128,256]{2,1,0:T(8,128)(2,1)}, u32[]{:S(2)}) copy-start(bf16[1,128,256]{2,1,0:T(8,128)(2,1)} %og.1) | copy-start | bytes 196612
  0.7 9.3 %copy-start.2 = (bf16[1,128,256]{2,1,0:T(8,128)(2,1)S(1)}, bf16[1,128,256]{2,1,0:T(8,128)(2,1)}, u32[]{:S(2)}) copy-start(bf16[1,128,256]{2,1,0:T(8,128)(2,1)} %v.1) | copy-start | bytes 196612
  0.7 9.3 %copy-start.1 = (bf16[1,128,256]{2,1,0:T(8,128)(2,1)S(1)}, bf16[1,128,256]{2,1,0:T(8,128)(2,1)}, u32[]{:S(2)}) copy-start(bf16[1,128,256]{2,1,0:T(8,128)(2,1)} %k.1) | copy-start | bytes 196612
  2.6 25.3 %all-to-all-start = ((bf16[8,32,1152]{2,1,0:T(8,128)(2,1)}), bf16[8,32,1152]{2,1,0:T(8,128)(2,1)S(1)}, u32[]{:S(2)}, u32[]{:S(2)}) async-start(bf16[8,32,1152]{2,1,0:T(8,128)(2,1)} %shard_map.163), calls=%async_computation | async-start | bytes 1179648 | tf_op jit(solution)/shard_map/all_to_all | solution.py:373
  9.9 0.7 copy-start.4
  10.6 0.7 copy-start.5
  11.4 16.6 %collective-permute-start = (bf16[128,768]{1,0:T(8,128)(2,1)S(1)}, bf16[128,768]{1,0:T(8,128)(2,1)S(1)}, u32[]{:S(2)}, u32[]{:S(2)}) collective-permute-start(bf16[128,768]{1,0:T(8,128)(2,1)S(1)} %get-tuple-element.77), channel_id=1, source_target_pairs={{0,1},{1,0},{2,3},{3,2},{4,5},{5,4},{6,7},{7,6},{8,9},{9,8},{10,11... | collective-permute-start | bytes 589832 | tf_op jit(solution)/shard_map/ppermute | solution.py:350
  13.5 18.8 %collective-permute-start.7 = (bf16[128,512]{1,0:T(8,128)(2,1)S(1)}, bf16[128,512]{1,0:T(8,128)(2,1)S(1)}, u32[]{:S(2)}, u32[]{:S(2)}) collective-permute-start(bf16[128,512]{1,0:T(8,128)(2,1)S(1)} %get-tuple-element.101.refs_0_), channel_id=1, source_target_pairs={{0,3},{1,2},{2,1},{3,0},{4,7},{5,6},{6,5},{7,4},{8,11},{9,10},{10,... | collective-permute-start | bytes 393224 | tf_op jit(solution)/shard_map/ppermute | solution.py:350
  14.9 13.0 %collective-permute-start.2 = (bf16[128,256]{1,0:T(8,128)(2,1)S(1)}, bf16[128,256]{1,0:T(8,128)(2,1)S(1)}, u32[]{:S(2)}, u32[]{:S(2)}) collective-permute-start(bf16[128,256]{1,0:T(8,128)(2,1)S(1)} %bitcast.8), channel_id=1, source_target_pairs={{0,3},{1,2},{2,1},{3,0},{4,7},{5,6},{6,5},{7,4},{8,11},{9,10},{10,... | collective-permute-start | bytes 196616 | tf_op jit(solution)/shard_map/ppermute | solution.py:350
  16.4 11.6 %collective-permute-start.1 = (bf16[128,256]{1,0:T(8,128)(2,1)S(1)}, bf16[128,256]{1,0:T(8,128)(2,1)S(1)}, u32[]{:S(2)}, u32[]{:S(2)}) collective-permute-start(bf16[128,256]{1,0:T(8,128)(2,1)S(1)} %bitcast.9), channel_id=1, source_target_pairs={{0,2},{1,3},{2,0},{3,1},{4,6},{5,7},{6,4},{7,5},{8,10},{9,11},{10,... | collective-permute-start | bytes 196616 | tf_op jit(solution)/shard_map/ppermute | solution.py:350
  17.9 17.7 %collective-permute-start.6 = (bf16[128,512]{1,0:T(8,128)(2,1)S(1)}, bf16[128,512]{1,0:T(8,128)(2,1)S(1)}, u32[]{:S(2)}, u32[]{:S(2)}) collective-permute-start(bf16[128,512]{1,0:T(8,128)(2,1)S(1)} %get-tuple-element.101.refs_0_), channel_id=1, source_target_pairs={{0,2},{1,3},{2,0},{3,1},{4,6},{5,7},{6,4},{7,5},{8,10},{9,11},{10,... | collective-permute-start | bytes 393224 | tf_op jit(solution)/shard_map/ppermute | solution.py:350
  28.7 6.8 %collective-permute-start.3 = (bf16[128,256]{1,0:T(8,128)(2,1)S(1)}, bf16[128,256]{1,0:T(8,128)(2,1)S(1)}, u32[]{:S(2)}, u32[]{:S(2)}) collective-permute-start(bf16[128,256]{1,0:T(8,128)(2,1)S(1)} %get-tuple-element.85), channel_id=1, source_target_pairs={{0,2},{1,3},{2,0},{3,1},{4,6},{5,7},{6,4},{7,5},{8,10},{9,11},{10,... | collective-permute-start | bytes 196616 | tf_op jit(solution)/shard_map/ppermute | solution.py:350
  30.1 5.8 %collective-permute-start.4 = (bf16[128,256]{1,0:T(8,128)(2,1)S(1)}, bf16[128,256]{1,0:T(8,128)(2,1)S(1)}, u32[]{:S(2)}, u32[]{:S(2)}) collective-permute-start(bf16[128,256]{1,0:T(8,128)(2,1)S(1)} %get-tuple-element.86), channel_id=1, source_target_pairs={{0,3},{1,2},{2,1},{3,0},{4,7},{5,6},{6,5},{7,4},{8,11},{9,10},{10,... | collective-permute-start | bytes 196616 | tf_op jit(solution)/shard_map/ppermute | solution.py:350
  32.2 4.3 %collective-permute-start.5 = (bf16[128,256]{1,0:T(8,128)(2,1)S(1)}, bf16[128,256]{1,0:T(8,128)(2,1)S(1)}, u32[]{:S(2)}, u32[]{:S(2)}) collective-permute-start(bf16[128,256]{1,0:T(8,128)(2,1)S(1)} %get-tuple-element.87), channel_id=1, source_target_pairs={{0,1},{1,0},{2,3},{3,2},{4,5},{5,4},{6,7},{7,6},{8,9},{9,8},{10,11... | collective-permute-start | bytes 196616 | tf_op jit(solution)/shard_map/ppermute | solution.py:350
  32.3 6.3 %collective-permute-start.11 = (bf16[128,256]{1,0:T(8,128)(2,1)S(1)}, bf16[128,256]{1,0:T(8,128)(2,1)S(1)}, u32[]{:S(2)}, u32[]{:S(2)}) collective-permute-start(bf16[128,256]{1,0:T(8,128)(2,1)S(1)} %bitcast.11), channel_id=1, source_target_pairs={{0,4},{1,5},{2,6},{3,7},{4,0},{5,1},{6,2},{7,3},{8,12},{9,13},{10,... | collective-permute-start | bytes 196616 | tf_op jit(solution)/shard_map/ppermute | solution.py:350
  36.7 3.1 %collective-permute-start.10 = (f32[2,128]{1,0:T(2,128)S(1)}, f32[2,128]{1,0:T(2,128)S(1)}, u32[]{:S(2)}, u32[]{:S(2)}) collective-permute-start(f32[2,128]{1,0:T(2,128)S(1)} %get-tuple-element.96.refs_0_), channel_id=1, source_target_pairs={{0,24},{8,16},{16,8},{24,0},{1,25},{9,17},{17,9},{25,1},{2,26},{10... | collective-permute-start | bytes 3080 | tf_op jit(solution)/shard_map/ppermute | solution.py:350
  36.8 3.6 %collective-permute-start.9 = (f32[2,128]{1,0:T(2,128)S(1)}, f32[2,128]{1,0:T(2,128)S(1)}, u32[]{:S(2)}, u32[]{:S(2)}) collective-permute-start(f32[2,128]{1,0:T(2,128)S(1)} %get-tuple-element.96.refs_0_), channel_id=1, source_target_pairs={{0,16},{8,24},{16,0},{24,8},{1,17},{9,25},{17,1},{25,9},{2,18},{10... | collective-permute-start | bytes 3080 | tf_op jit(solution)/shard_map/ppermute | solution.py:350
  38.4 2.0 %collective-permute-start.8 = (f32[2,128]{1,0:T(2,128)S(1)}, f32[2,128]{1,0:T(2,128)S(1)}, u32[]{:S(2)}, u32[]{:S(2)}) collective-permute-start(f32[2,128]{1,0:T(2,128)S(1)} %get-tuple-element.96.refs_0_), channel_id=1, source_target_pairs={{0,8},{8,0},{16,24},{24,16},{1,9},{9,1},{17,25},{25,17},{2,10},{10... | collective-permute-start | bytes 3080 | tf_op jit(solution)/shard_map/ppermute | solution.py:350
  40.6 7.5 %collective-permute-start.15 = (bf16[128,256]{1,0:T(8,128)(2,1)S(1)}, bf16[128,256]{1,0:T(8,128)(2,1)S(1)}, u32[]{:S(2)}, u32[]{:S(2)}) collective-permute-start(bf16[128,256]{1,0:T(8,128)(2,1)S(1)} %shard_map.167.refs_4_), channel_id=1, source_target_pairs={{0,4},{1,5},{2,6},{3,7},{4,0},{5,1},{6,2},{7,3},{8,12},{9,13},{10,... | collective-permute-start | bytes 196616 | tf_op jit(solution)/shard_map/ppermute | solution.py:350
  43.3 6.8 %collective-permute-start.14 = (bf16[128,256]{1,0:T(8,128)(2,1)S(1)}, bf16[128,256]{1,0:T(8,128)(2,1)S(1)}, u32[]{:S(2)}, u32[]{:S(2)}) collective-permute-start(bf16[128,256]{1,0:T(8,128)(2,1)S(1)} %shard_map.167.refs_4_), channel_id=1, source_target_pairs={{0,3},{1,2},{2,1},{3,0},{4,7},{5,6},{6,5},{7,4},{8,11},{9,10},{10,... | collective-permute-start | bytes 196616 | tf_op jit(solution)/shard_map/ppermute | solution.py:350
  44.6 7.0 %collective-permute-start.13 = (bf16[128,256]{1,0:T(8,128)(2,1)S(1)}, bf16[128,256]{1,0:T(8,128)(2,1)S(1)}, u32[]{:S(2)}, u32[]{:S(2)}) collective-permute-start(bf16[128,256]{1,0:T(8,128)(2,1)S(1)} %shard_map.167.refs_4_), channel_id=1, source_target_pairs={{0,2},{1,3},{2,0},{3,1},{4,6},{5,7},{6,4},{7,5},{8,10},{9,11},{10,... | collective-permute-start | bytes 196616 | tf_op jit(solution)/shard_map/ppermute | solution.py:350
  45.4 6.3 %collective-permute-start.12 = (bf16[128,256]{1,0:T(8,128)(2,1)S(1)}, bf16[128,256]{1,0:T(8,128)(2,1)S(1)}, u32[]{:S(2)}, u32[]{:S(2)}) collective-permute-start(bf16[128,256]{1,0:T(8,128)(2,1)S(1)} %shard_map.167.refs_4_), channel_id=1, source_target_pairs={{0,1},{1,0},{2,3},{3,2},{4,5},{5,4},{6,7},{7,6},{8,9},{9,8},{10,11... | collective-permute-start | bytes 196616 | tf_op jit(solution)/shard_map/ppermute | solution.py:350
  48.1 7.4 %collective-permute-start.18 = (bf16[128,512]{1,0:T(8,128)(2,1)S(1)}, bf16[128,512]{1,0:T(8,128)(2,1)S(1)}, u32[]{:S(2)}, u32[]{:S(2)}) collective-permute-start(bf16[128,512]{1,0:T(8,128)(2,1)S(1)} %shard_map.170.refs_4_), channel_id=1, source_target_pairs={{0,3},{1,2},{2,1},{3,0},{4,7},{5,6},{6,5},{7,4},{8,11},{9,10},{10,... | collective-permute-start | bytes 393224 | tf_op jit(solution)/shard_map/ppermute | solution.py:350
  49.4 7.7 %collective-permute-start.17 = (bf16[128,512]{1,0:T(8,128)(2,1)S(1)}, bf16[128,512]{1,0:T(8,128)(2,1)S(1)}, u32[]{:S(2)}, u32[]{:S(2)}) collective-permute-start(bf16[128,512]{1,0:T(8,128)(2,1)S(1)} %shard_map.170.refs_4_), channel_id=1, source_target_pairs={{0,2},{1,3},{2,0},{3,1},{4,6},{5,7},{6,4},{7,5},{8,10},{9,11},{10,... | collective-permute-start | bytes 393224 | tf_op jit(solution)/shard_map/ppermute | solution.py:350
  50.2 7.8 %collective-permute-start.16 = (bf16[128,512]{1,0:T(8,128)(2,1)S(1)}, bf16[128,512]{1,0:T(8,128)(2,1)S(1)}, u32[]{:S(2)}, u32[]{:S(2)}) collective-permute-start(bf16[128,512]{1,0:T(8,128)(2,1)S(1)} %shard_map.170.refs_4_), channel_id=1, source_target_pairs={{0,1},{1,0},{2,3},{3,2},{4,5},{5,4},{6,7},{7,6},{8,9},{9,8},{10,11... | collective-permute-start | bytes 393224 | tf_op jit(solution)/shard_map/ppermute | solution.py:350
  52.4 8.1 %collective-permute-start.19 = (bf16[128,256]{1,0:T(8,128)(2,1)S(1)}, bf16[128,256]{1,0:T(8,128)(2,1)S(1)}, u32[]{:S(2)}, u32[]{:S(2)}) collective-permute-start(bf16[128,256]{1,0:T(8,128)(2,1)S(1)} %get-tuple-element.119), channel_id=1, source_target_pairs={{0,2},{1,3},{2,0},{3,1},{4,6},{5,7},{6,4},{7,5},{8,10},{9,11},{10,... | collective-permute-start | bytes 196616 | tf_op jit(solution)/shard_map/ppermute | solution.py:350
  53.3 7.3 %collective-permute-start.20 = (bf16[128,256]{1,0:T(8,128)(2,1)S(1)}, bf16[128,256]{1,0:T(8,128)(2,1)S(1)}, u32[]{:S(2)}, u32[]{:S(2)}) collective-permute-start(bf16[128,256]{1,0:T(8,128)(2,1)S(1)} %get-tuple-element.120), channel_id=1, source_target_pairs={{0,3},{1,2},{2,1},{3,0},{4,7},{5,6},{6,5},{7,4},{8,11},{9,10},{10,... | collective-permute-start | bytes 196616 | tf_op jit(solution)/shard_map/ppermute | solution.py:350
  55.5 5.1 %collective-permute-start.21 = (bf16[128,256]{1,0:T(8,128)(2,1)S(1)}, bf16[128,256]{1,0:T(8,128)(2,1)S(1)}, u32[]{:S(2)}, u32[]{:S(2)}) collective-permute-start(bf16[128,256]{1,0:T(8,128)(2,1)S(1)} %get-tuple-element.121), channel_id=1, source_target_pairs={{0,1},{1,0},{2,3},{3,2},{4,5},{5,4},{6,7},{7,6},{8,9},{9,8},{10,11... | collective-permute-start | bytes 196616 | tf_op jit(solution)/shard_map/ppermute | solution.py:350
  60.5 6.7 %collective-permute-start.22 = (bf16[64,576]{1,0:T(8,128)(2,1)S(1)}, bf16[64,576]{1,0:T(8,128)(2,1)S(1)}, u32[]{:S(2)}, u32[]{:S(2)}) collective-permute-start(bf16[64,576]{1,0:T(8,128)(2,1)S(1)} %get-tuple-element.122), channel_id=1, source_target_pairs={{0,4},{1,5},{2,6},{3,7},{4,0},{5,1},{6,2},{7,3},{8,12},{9,13},{10,... | collective-permute-start | bytes 221192 | tf_op jit(solution)/shard_map/ppermute | solution.py:350
  61.6 7.2 %collective-permute-start.23 = (bf16[64,576]{1,0:T(8,128)(2,1)S(1)}, bf16[64,576]{1,0:T(8,128)(2,1)S(1)}, u32[]{:S(2)}, u32[]{:S(2)}) collective-permute-start(bf16[64,576]{1,0:T(8,128)(2,1)S(1)} %get-tuple-element.123), channel_id=1, source_target_pairs={{0,6},{1,7},{2,4},{3,5},{4,2},{5,3},{6,0},{7,1},{8,14},{9,15},{10,... | collective-permute-start | bytes 221192 | tf_op jit(solution)/shard_map/ppermute | solution.py:350
  63.7 8.0 %collective-permute-start.25 = (bf16[672,128]{1,0:T(8,128)(2,1)S(1)}, bf16[672,128]{1,0:T(8,128)(2,1)S(1)}, u32[]{:S(2)}, u32[]{:S(2)}) collective-permute-start(bf16[672,128]{1,0:T(8,128)(2,1)S(1)} %get-tuple-element.130), channel_id=1, source_target_pairs={{0,1},{1,0},{2,3},{3,2},{4,5},{5,4},{6,7},{7,6},{8,9},{9,8},{10,11... | collective-permute-start | bytes 516104 | tf_op jit(solution)/shard_map/ppermute | solution.py:350
  64.8 7.2 %collective-permute-start.26 = (bf16[672,128]{1,0:T(8,128)(2,1)S(1)}, bf16[672,128]{1,0:T(8,128)(2,1)S(1)}, u32[]{:S(2)}, u32[]{:S(2)}) collective-permute-start(bf16[672,128]{1,0:T(8,128)(2,1)S(1)} %get-tuple-element.131), channel_id=1, source_target_pairs={{0,2},{1,3},{2,0},{3,1},{4,6},{5,7},{6,4},{7,5},{8,10},{9,11},{10,... | collective-permute-start | bytes 516104 | tf_op jit(solution)/shard_map/ppermute | solution.py:350
  64.8 8.9 %collective-permute-start.27 = (bf16[672,128]{1,0:T(8,128)(2,1)S(1)}, bf16[672,128]{1,0:T(8,128)(2,1)S(1)}, u32[]{:S(2)}, u32[]{:S(2)}) collective-permute-start(bf16[672,128]{1,0:T(8,128)(2,1)S(1)} %get-tuple-element.132), channel_id=1, source_target_pairs={{0,3},{1,2},{2,1},{3,0},{4,7},{5,6},{6,5},{7,4},{8,11},{9,10},{10,... | collective-permute-start | bytes 516104 | tf_op jit(solution)/shard_map/ppermute | solution.py:350
  68.8 5.7 %collective-permute-start.24 = (bf16[64,576]{1,0:T(8,128)(2,1)S(1)}, bf16[64,576]{1,0:T(8,128)(2,1)S(1)}, u32[]{:S(2)}, u32[]{:S(2)}) collective-permute-start(bf16[64,576]{1,0:T(8,128)(2,1)S(1)} %shard_map.172), channel_id=1, source_target_pairs={{0,1},{1,0},{2,3},{3,2},{4,5},{5,4},{6,7},{7,6},{8,9},{9,8},{10,11... | collective-permute-start | bytes 221192 | tf_op jit(solution)/shard_map/ppermute | solution.py:350

commit v16 on v15

--- a/solution.py
+++ b/solution.py
@@ -72,14 +72,6 @@
     return jax.ShapeDtypeStruct(shape, dtype)
 
 
-def fetch(sources, buffers, sems):
-    copies = [pltpu.make_async_copy(s, b, sems.at[i]) for i, (s, b) in enumerate(zip(sources, buffers))]
-    for copy in copies:
-        copy.start()
-    for copy in copies:
-        copy.wait()
-
-
 def padded(rows):
     return -(-rows // 16) * 16
 
@@ -125,12 +117,15 @@
 
 def weight_pack_kernel(group, slab, *refs):
     args, (w_out, buf, sems) = refs[:6], refs[6:]
-    fetch(args, [buf.at[pl.ds(i, 1)] for i in range(6)], sems)
-    for j in range(group):
-        cols = pl.ds(j * slab, slab)
-        block = jnp.concatenate([buf[i, :, cols] for i in range(6)], axis=1)
-        for p in range(j, w_out.shape[0], group):
-            w_out[p] = block
+    copies = [pltpu.make_async_copy(args[i], buf.at[pl.ds(i, 1)], sems.at[i]) for i in range(6)]
+    for copy in copies:
+        copy.start()
+    for i, copy in enumerate(copies):
+        copy.wait()
+        for j in range(group):
+            block = buf[i, :, j * slab : (j + 1) * slab]
+            for p in range(j, w_out.shape[0], group):
+                w_out[p, :, i * slab : (i + 1) * slab] = block
 
 
 def columns(w, slab):
@@ -327,8 +322,9 @@
     gv[0] = (rate[...] * sums[1]).astype(BF)
 
 
-def weights_kernel(group, tok_groups, slab, at, place, relayed, inner, *refs):
-    blocks, (*outs, buf) = refs[:-4], refs[-4:]
+def final_kernel(group, tok_groups, slab, at, place, rate, tok, relayed, inner, *refs):
+    queries, blocks, outs, buf = refs[:group], refs[group:-7], refs[-7:-1], refs[-1]
+    tokens_kernel(group, rate, tok, *queries, *blocks[: group - 1], *outs[:3])
     _, rows, cols = buf.shape
     step = padded(rows)
     buf[0] = inner[...].astype(F32)
@@ -340,7 +336,7 @@
         buf[d ^ 1] += relayed[i * step : i * step + rows, :].astype(F32)
     total = [buf[place[1] ^ j] for j in range(group)]
     for i in range(3):
-        outs[i][0] = jnp.concatenate([t[:, i * slab : (i + 1) * slab] for t in total], axis=1)
+        outs[3 + i][0] = jnp.concatenate([t[:, i * slab : (i + 1) * slab] for t in total], axis=1)
 
 
 def make_local(seq_n, head_n, group):
@@ -458,20 +454,15 @@
         relayed = move(relayed, 1)
         out_tok = arr((1, own, feat), BF)
         grad_w = arr((1, rows, hidden), F32)
-        grads_t = call(
-            functools.partial(tokens_kernel, group), (out_tok,) * 3, (rate, tok, *grad_q, *near_got), 16
-        )
-        relayed, grads_t = lax.optimization_barrier((relayed, grads_t))
         at = 2 * tiles(feat) * padded(own)
-        grads_w = call(
-            functools.partial(weights_kernel, group, tok_groups, slab, at),
-            (grad_w,) * 3,
-            (place, relayed, inner, *near_got, *far_got),
+        return call(
+            functools.partial(final_kernel, group, tok_groups, slab, at),
+            (*(out_tok,) * 3, *(grad_w,) * 3),
+            (place, rate, tok, relayed, inner, *grad_q, *near_got, *far_got),
             16,
             smem=1,
             scratch=[pltpu.VMEM((group, rows, 3 * slab), F32)],
         )
-        return (*grads_t, *grads_w)
 
     return local
 

time: 76.2 us -> 76.7 us (level)
    pallas_call x11 -> x10, Pallas kernels: 7.8 us -> 7.33 us  [call(): pl.pallas_call(kernel, out_shape=outs, in_specs=[SMEM] * smem + [VMEM] *...]
  transfers between devices with their start and end apart: 29 -> 29, of which waited for: 12 -> 10; matrix products, arithmetic and copies ran while one was open for 0% -> 0% of each run, Pallas kernels for 8% -> 8%
where the time goes in v16:
time: 76.7 us; the launch traced here: 76.4 us
  starting transfers between devices  43.2 us (56%)
  waiting for transfers between devices  21.4 us (28%)
  Pallas kernels  9.52 us (12%)
  local copies, waits for them, and re-layouts  1.35 us (2%)
  between operations  0.84 us (1%)
    ppermute x28, starting transfers between devices, move(): return lax.ppermute(x, axis, [(i, i ^ dist) for i in range(size)])  35.9 us
    ppermute x28, waiting for transfers between devices, move(): return lax.ppermute(x, axis, [(i, i ^ dist) for i in range(size)])  21.4 us
    pallas_call x10, Pallas kernels, call(): pl.pallas_call(kernel, out_shape=outs, in_specs=[SMEM] * smem + [VMEM] *...  7.33 us
    all_to_all x1, starting transfers between devices, local(): lax.all_to_all(packed, 'seq', 0, 0, tiled=True)  7.26 us
    pallas_call x1, Pallas kernels, copying_call(): pl.pallas_call(kernel, out_shape=outs, in_specs=[pl.BlockSpec(memory_spac...  2.2 us
  transfers between devices with their start and end apart: 29, of which 10 were waited for; matrix products, arithmetic and copies ran while one was open for 0% of the time, Pallas kernels for 8%

profile of v16, /device:TPU:0, one launch (start us, length us, event | category | flops | bytes accessed | tf_op | source)
XLA Modules:
  0.0 76.4 jit_solution(14631198990609940829)
XLA Ops:
  0.7 2.2 %shard_map.164 = bf16[8,32,1152]{2,1,0:T(8,128)(2,1)} custom-call(bf16[1,32,768]{2,1,0:T(8,128)(2,1)} %refs_0_.1, bf16[1,32,768]{2,1,0:T(8,128)(2,1)} %refs_1_.1, bf16[1,32,768]{2,1,0:T(8,128)(2,1)} %refs_2_.1, bf16[1,32,768]{2,1,0:T(8,128)(2,1)} %refs_3_.1, bf16[1,32,768]{2,1,0:T(8,128)(2,1)} %refs_4_.1, bf16[1,32,768]{2,1,0:T(8,128)(2,1)} %refs_5_.1), custom_call_target="tpu_custom_call" | custom-call | tf_op jit(solution)/shard_map/pallas_call | solution.py:61
  2.9 7.3 %all-to-all-start = ((bf16[8,32,1152]{2,1,0:T(8,128)(2,1)}), bf16[8,32,1152]{2,1,0:T(8,128)(2,1)S(1)}, u32[]{:S(2)}, u32[]{:S(2)}) async-start(bf16[8,32,1152]{2,1,0:T(8,128)(2,1)} %shard_map.164), calls=%async_computation | async-start | bytes 1179648 | tf_op jit(solution)/shard_map/all_to_all | solution.py:369
  10.2 0.0 copy-start.4
  10.2 0.7 copy-done.4
  10.9 0.7 copy-done.5
  11.5 0.1 shard_map.163
  11.6 2.1 %collective-permute-start = (bf16[128,768]{1,0:T(8,128)(2,1)S(1)}, bf16[128,768]{1,0:T(8,128)(2,1)S(1)}, u32[]{:S(2)}, u32[]{:S(2)}) collective-permute-start(bf16[128,768]{1,0:T(8,128)(2,1)S(1)} %get-tuple-element.68), channel_id=1, source_target_pairs={{0,1},{1,0},{2,3},{3,2},{4,5},{5,4},{6,7},{7,6},{8,9},{9,8},{10,11... | collective-permute-start | bytes 589832 | tf_op jit(solution)/shard_map/ppermute | solution.py:346
  13.7 1.5 %collective-permute-start.7 = (bf16[128,512]{1,0:T(8,128)(2,1)S(1)}, bf16[128,512]{1,0:T(8,128)(2,1)S(1)}, u32[]{:S(2)}, u32[]{:S(2)}) collective-permute-start(bf16[128,512]{1,0:T(8,128)(2,1)S(1)} %get-tuple-element.92.refs_0_), channel_id=1, source_target_pairs={{0,3},{1,2},{2,1},{3,0},{4,7},{5,6},{6,5},{7,4},{8,11},{9,10},{10,... | collective-permute-start | bytes 393224 | tf_op jit(solution)/shard_map/ppermute | solution.py:346
  15.2 1.5 %collective-permute-start.2 = (bf16[128,256]{1,0:T(8,128)(2,1)S(1)}, bf16[128,256]{1,0:T(8,128)(2,1)S(1)}, u32[]{:S(2)}, u32[]{:S(2)}) collective-permute-start(bf16[128,256]{1,0:T(8,128)(2,1)S(1)} %bitcast.8), channel_id=1, source_target_pairs={{0,3},{1,2},{2,1},{3,0},{4,7},{5,6},{6,5},{7,4},{8,11},{9,10},{10,... | collective-permute-start | bytes 196616 | tf_op jit(solution)/shard_map/ppermute | solution.py:346
  16.6 1.5 %collective-permute-start.1 = (bf16[128,256]{1,0:T(8,128)(2,1)S(1)}, bf16[128,256]{1,0:T(8,128)(2,1)S(1)}, u32[]{:S(2)}, u32[]{:S(2)}) collective-permute-start(bf16[128,256]{1,0:T(8,128)(2,1)S(1)} %bitcast.9), channel_id=1, source_target_pairs={{0,2},{1,3},{2,0},{3,1},{4,6},{5,7},{6,4},{7,5},{8,10},{9,11},{10,... | collective-permute-start | bytes 196616 | tf_op jit(solution)/shard_map/ppermute | solution.py:346
  18.1 0.6 collective-permute-start.6
  18.7 9.5 %collective-permute-done.2.refs_3_ = bf16[128,256]{1,0:T(8,128)(2,1)S(1)} collective-permute-done((bf16[128,256]{1,0:T(8,128)(2,1)S(1)}, bf16[128,256]{1,0:T(8,128)(2,1)S(1)}, u32[]{:S(2)}, u32[]{:S(2)}) %collective-permute-start.2) | collective-permute-done | bytes 65568 | tf_op jit(solution)/shard_map/ppermute | solution.py:346
  28.2 0.0 collective-permute-done.1.refs_2_
  28.2 0.0 collective-permute-done.refs_1_
  28.2 0.0 all-to-all-done
  28.2 0.8 %shard_map.165 = (bf16[128,256]{1,0:T(8,128)(2,1)S(1)}, bf16[128,256]{1,0:T(8,128)(2,1)S(1)}, bf16[128,256]{1,0:T(8,128)(2,1)S(1)}, bf16[128,256]{1,0:T(8,128)(2,1)S(1)}, bf16[256,576]{1,0:T(8,128)(2,1)S(1)}) custom-call(bf16[256,1152]{1,0:T(8,128)(2,1)S(1)} %bitcast.5, bf16[128,256]{1,0:T(8,128)(2,1)S(1)} %bitcast.10, ...), custom_call_target="tpu_custom_call" | custom-call | flops 150994944 | bytes 1540096 | tf_op jit(solution)/shard_map/pallas_call | solution.py:49
  29.0 1.3 %collective-permute-start.3 = (bf16[128,256]{1,0:T(8,128)(2,1)S(1)}, bf16[128,256]{1,0:T(8,128)(2,1)S(1)}, u32[]{:S(2)}, u32[]{:S(2)}) collective-permute-start(bf16[128,256]{1,0:T(8,128)(2,1)S(1)} %get-tuple-element.76), channel_id=1, source_target_pairs={{0,2},{1,3},{2,0},{3,1},{4,6},{5,7},{6,4},{7,5},{8,10},{9,11},{10,... | collective-permute-start | bytes 196616 | tf_op jit(solution)/shard_map/ppermute | solution.py:346
  30.3 2.2 %collective-permute-start.4 = (bf16[128,256]{1,0:T(8,128)(2,1)S(1)}, bf16[128,256]{1,0:T(8,128)(2,1)S(1)}, u32[]{:S(2)}, u32[]{:S(2)}) collective-permute-start(bf16[128,256]{1,0:T(8,128)(2,1)S(1)} %get-tuple-element.77), channel_id=1, source_target_pairs={{0,3},{1,2},{2,1},{3,0},{4,7},{5,6},{6,5},{7,4},{8,11},{9,10},{10,... | collective-permute-start | bytes 196616 | tf_op jit(solution)/shard_map/ppermute | solution.py:346
  32.5 0.1 collective-permute-start.5
  32.5 0.0 collective-permute-done.7.refs_3_
  32.5 3.3 %collective-permute-start.11 = (bf16[128,256]{1,0:T(8,128)(2,1)S(1)}, bf16[128,256]{1,0:T(8,128)(2,1)S(1)}, u32[]{:S(2)}, u32[]{:S(2)}) collective-permute-start(bf16[128,256]{1,0:T(8,128)(2,1)S(1)} %bitcast.11), channel_id=1, source_target_pairs={{0,4},{1,5},{2,6},{3,7},{4,0},{5,1},{6,2},{7,3},{8,12},{9,13},{10,... | collective-permute-start | bytes 196616 | tf_op jit(solution)/shard_map/ppermute | solution.py:346
  35.8 0.0 collective-permute-done.6.refs_2_
  35.8 0.3 collective-permute-done.4.refs_2_
  36.1 0.7 collective-permute-done.5.refs_3_
  36.8 0.1 shard_map.166
  36.9 0.1 collective-permute-start.10
  37.0 1.6 %collective-permute-start.9 = (f32[2,128]{1,0:T(2,128)S(1)}, f32[2,128]{1,0:T(2,128)S(1)}, u32[]{:S(2)}, u32[]{:S(2)}) collective-permute-start(f32[2,128]{1,0:T(2,128)S(1)} %get-tuple-element.87.refs_0_), channel_id=1, source_target_pairs={{0,16},{8,24},{16,0},{24,8},{1,17},{9,25},{17,1},{25,9},{2,18},{10... | collective-permute-start | bytes 3080 | tf_op jit(solution)/shard_map/ppermute | solution.py:346
  38.6 0.3 collective-permute-start.8
  38.9 0.0 collective-permute-done.11.right
  38.9 1.1 %collective-permute-done.10.refs_3_ = f32[2,128]{1,0:T(2,128)S(1)} collective-permute-done((f32[2,128]{1,0:T(2,128)S(1)}, f32[2,128]{1,0:T(2,128)S(1)}, u32[]{:S(2)}, u32[]{:S(2)}) %collective-permute-start.10) | collective-permute-done | bytes 1056 | tf_op jit(solution)/shard_map/ppermute | solution.py:346
  40.0 0.7 collective-permute-done.9.refs_2_
  40.7 0.1 shard_map.167.refs_4_
  40.8 2.8 %collective-permute-start.15 = (bf16[128,256]{1,0:T(8,128)(2,1)S(1)}, bf16[128,256]{1,0:T(8,128)(2,1)S(1)}, u32[]{:S(2)}, u32[]{:S(2)}) collective-permute-start(bf16[128,256]{1,0:T(8,128)(2,1)S(1)} %shard_map.167.refs_4_), channel_id=1, source_target_pairs={{0,4},{1,5},{2,6},{3,7},{4,0},{5,1},{6,2},{7,3},{8,12},{9,13},{10,... | collective-permute-start | bytes 196616 | tf_op jit(solution)/shard_map/ppermute | solution.py:346
  43.6 1.3 %collective-permute-start.14 = (bf16[128,256]{1,0:T(8,128)(2,1)S(1)}, bf16[128,256]{1,0:T(8,128)(2,1)S(1)}, u32[]{:S(2)}, u32[]{:S(2)}) collective-permute-start(bf16[128,256]{1,0:T(8,128)(2,1)S(1)} %shard_map.167.refs_4_), channel_id=1, source_target_pairs={{0,3},{1,2},{2,1},{3,0},{4,7},{5,6},{6,5},{7,4},{8,11},{9,10},{10,... | collective-permute-start | bytes 196616 | tf_op jit(solution)/shard_map/ppermute | solution.py:346
  44.8 0.8 %collective-permute-start.13 = (bf16[128,256]{1,0:T(8,128)(2,1)S(1)}, bf16[128,256]{1,0:T(8,128)(2,1)S(1)}, u32[]{:S(2)}, u32[]{:S(2)}) collective-permute-start(bf16[128,256]{1,0:T(8,128)(2,1)S(1)} %shard_map.167.refs_4_), channel_id=1, source_target_pairs={{0,2},{1,3},{2,0},{3,1},{4,6},{5,7},{6,4},{7,5},{8,10},{9,11},{10,... | collective-permute-start | bytes 196616 | tf_op jit(solution)/shard_map/ppermute | solution.py:346
  45.6 1.5 %collective-permute-start.12 = (bf16[128,256]{1,0:T(8,128)(2,1)S(1)}, bf16[128,256]{1,0:T(8,128)(2,1)S(1)}, u32[]{:S(2)}, u32[]{:S(2)}) collective-permute-start(bf16[128,256]{1,0:T(8,128)(2,1)S(1)} %shard_map.167.refs_4_), channel_id=1, source_target_pairs={{0,1},{1,0},{2,3},{3,2},{4,5},{5,4},{6,7},{7,6},{8,9},{9,8},{10,11... | collective-permute-start | bytes 196616 | tf_op jit(solution)/shard_map/ppermute | solution.py:346
  47.1 0.1 pad_add_fusion.place
  47.1 1.1 %shard_map.169 = (f32[4,512,192]{2,1,0:T(8,128)S(1)}, bf16[3,512,192]{2,1,0:T(8,128)(2,1)S(1)}, f32[3,192]{1,0:T(4,128)S(1)}, f32[3,256,192]{2,1,0:T(8,128)S(1)}, f32[3,256,192]{2,1,0:T(8,128)S(1)}) custom-call(bf16[256,1152]{1,0:T(8,128)(2,1)S(1)} %bitcast.6, bf16[128,512]{1,0:T(8,128)(2,1)S(1)} %get-tuple-element.92.refs_0_, ...), custom_call_target="tpu_custom_call" | custom-call | flops 603979776 | bytes 4524288 | tf_op jit(solution)/shard_map/pallas_call | solution.py:49
  48.3 1.3 %collective-permute-start.18 = (bf16[128,512]{1,0:T(8,128)(2,1)S(1)}, bf16[128,512]{1,0:T(8,128)(2,1)S(1)}, u32[]{:S(2)}, u32[]{:S(2)}) collective-permute-start(bf16[128,512]{1,0:T(8,128)(2,1)S(1)} %shard_map.170.refs_4_), channel_id=1, source_target_pairs={{0,3},{1,2},{2,1},{3,0},{4,7},{5,6},{6,5},{7,4},{8,11},{9,10},{10,... | collective-permute-start | bytes 393224 | tf_op jit(solution)/shard_map/ppermute | solution.py:346
  49.6 0.8 %collective-permute-start.17 = (bf16[128,512]{1,0:T(8,128)(2,1)S(1)}, bf16[128,512]{1,0:T(8,128)(2,1)S(1)}, u32[]{:S(2)}, u32[]{:S(2)}) collective-permute-start(bf16[128,512]{1,0:T(8,128)(2,1)S(1)} %shard_map.170.refs_4_), channel_id=1, source_target_pairs={{0,2},{1,3},{2,0},{3,1},{4,6},{5,7},{6,4},{7,5},{8,10},{9,11},{10,... | collective-permute-start | bytes 393224 | tf_op jit(solution)/shard_map/ppermute | solution.py:346
  50.4 1.5 %collective-permute-start.16 = (bf16[128,512]{1,0:T(8,128)(2,1)S(1)}, bf16[128,512]{1,0:T(8,128)(2,1)S(1)}, u32[]{:S(2)}, u32[]{:S(2)}) collective-permute-start(bf16[128,512]{1,0:T(8,128)(2,1)S(1)} %shard_map.170.refs_4_), channel_id=1, source_target_pairs={{0,1},{1,0},{2,3},{3,2},{4,5},{5,4},{6,7},{7,6},{8,9},{9,8},{10,11... | collective-permute-start | bytes 393224 | tf_op jit(solution)/shard_map/ppermute | solution.py:346
  51.9 0.0 collective-permute-done.12.refs_5_
  51.9 0.8 %shard_map.168 = (bf16[128,256]{1,0:T(8,128)(2,1)S(1)}, bf16[128,256]{1,0:T(8,128)(2,1)S(1)}, bf16[128,256]{1,0:T(8,128)(2,1)S(1)}, bf16[128,256]{1,0:T(8,128)(2,1)S(1)}, f32[3,256,192]{2,1,0:T(8,128)S(1)}) custom-call(bf16[256,576]{1,0:T(8,128)(2,1)S(1)} %get-tuple-element.69.normed_ref, bf16[128,256]{1,0:T(8,128)(2,1)S(1)} %bitcast.12, ...), custom_call_target="tpu_custom_call" | custom-call | flops 3019898880 | bytes 1802240 | tf_op jit(solution)/shard_map/pallas_call | solution.py:49
  52.7 0.8 %collective-permute-start.19 = (bf16[128,256]{1,0:T(8,128)(2,1)S(1)}, bf16[128,256]{1,0:T(8,128)(2,1)S(1)}, u32[]{:S(2)}, u32[]{:S(2)}) collective-permute-start(bf16[128,256]{1,0:T(8,128)(2,1)S(1)} %get-tuple-element.111), channel_id=1, source_target_pairs={{0,2},{1,3},{2,0},{3,1},{4,6},{5,7},{6,4},{7,5},{8,10},{9,11},{10,... | collective-permute-start | bytes 196616 | tf_op jit(solution)/shard_map/ppermute | solution.py:346
  53.5 1.3 %collective-permute-start.20 = (bf16[128,256]{1,0:T(8,128)(2,1)S(1)}, bf16[128,256]{1,0:T(8,128)(2,1)S(1)}, u32[]{:S(2)}, u32[]{:S(2)}) collective-permute-start(bf16[128,256]{1,0:T(8,128)(2,1)S(1)} %get-tuple-element.112), channel_id=1, source_target_pairs={{0,3},{1,2},{2,1},{3,0},{4,7},{5,6},{6,5},{7,4},{8,11},{9,10},{10,... | collective-permute-start | bytes 196616 | tf_op jit(solution)/shard_map/ppermute | solution.py:346
  54.8 0.9 %collective-permute-done.18.refs_7_ = bf16[128,512]{1,0:T(8,128)(2,1)S(1)} collective-permute-done((bf16[128,512]{1,0:T(8,128)(2,1)S(1)}, bf16[128,512]{1,0:T(8,128)(2,1)S(1)}, u32[]{:S(2)}, u32[]{:S(2)}) %collective-permute-start.18) | collective-permute-done | bytes 131104 | tf_op jit(solution)/shard_map/ppermute | solution.py:346
  55.7 0.6 collective-permute-start.21
  56.3 1.0 %collective-permute-done.17.refs_6_ = bf16[128,512]{1,0:T(8,128)(2,1)S(1)} collective-permute-done((bf16[128,512]{1,0:T(8,128)(2,1)S(1)}, bf16[128,512]{1,0:T(8,128)(2,1)S(1)}, u32[]{:S(2)}, u32[]{:S(2)}) %collective-permute-start.17) | collective-permute-done | bytes 131104 | tf_op jit(solution)/shard_map/ppermute | solution.py:346
  57.3 0.9 %collective-permute-done.16.refs_5_ = bf16[128,512]{1,0:T(8,128)(2,1)S(1)} collective-permute-done((bf16[128,512]{1,0:T(8,128)(2,1)S(1)}, bf16[128,512]{1,0:T(8,128)(2,1)S(1)}, u32[]{:S(2)}, u32[]{:S(2)}) %collective-permute-start.16) | collective-permute-done | bytes 131104 | tf_op jit(solution)/shard_map/ppermute | solution.py:346
  58.2 2.8 %shard_map.171 = (bf16[128,512]{1,0:T(8,128)(2,1)S(1)}, bf16[32,576]{1,0:T(8,128)(2,1)S(1)}, bf16[672,128]{1,0:T(8,128)(2,1)S(1)}, bf16[672,128]{1,0:T(8,128)(2,...) custom-call(s32[3]{0:T(128)S(1)} %pad_add_fusion.place, ...), custom_call_target="tpu_custom_call" | custom-call | flops 6039797760 | bytes 6764812 | tf_op jit(solution)/shard_map/pallas_call | solution.py:49
  61.0 0.0 collective-permute-done.20.refs_2_
  61.0 0.0 collective-permute-done.21.refs_3_
  61.0 1.1 %collective-permute-start.22 = (bf16[64,576]{1,0:T(8,128)(2,1)S(1)}, bf16[64,576]{1,0:T(8,128)(2,1)S(1)}, u32[]{:S(2)}, u32[]{:S(2)}) collective-permute-start(bf16[64,576]{1,0:T(8,128)(2,1)S(1)} %get-tuple-element.114), channel_id=1, source_target_pairs={{0,4},{1,5},{2,6},{3,7},{4,0},{5,1},{6,2},{7,3},{8,12},{9,13},{10,... | collective-permute-start | bytes 221192 | tf_op jit(solution)/shard_map/ppermute | solution.py:346
  62.1 2.1 %collective-permute-start.23 = (bf16[64,576]{1,0:T(8,128)(2,1)S(1)}, bf16[64,576]{1,0:T(8,128)(2,1)S(1)}, u32[]{:S(2)}, u32[]{:S(2)}) collective-permute-start(bf16[64,576]{1,0:T(8,128)(2,1)S(1)} %get-tuple-element.115), channel_id=1, source_target_pairs={{0,6},{1,7},{2,4},{3,5},{4,2},{5,3},{6,0},{7,1},{8,14},{9,15},{10,... | collective-permute-start | bytes 221192 | tf_op jit(solution)/shard_map/ppermute | solution.py:346
  64.2 1.1 %collective-permute-start.25 = (bf16[672,128]{1,0:T(8,128)(2,1)S(1)}, bf16[672,128]{1,0:T(8,128)(2,1)S(1)}, u32[]{:S(2)}, u32[]{:S(2)}) collective-permute-start(bf16[672,128]{1,0:T(8,128)(2,1)S(1)} %get-tuple-element.121), channel_id=1, source_target_pairs={{0,1},{1,0},{2,3},{3,2},{4,5},{5,4},{6,7},{7,6},{8,9},{9,8},{10,11... | collective-permute-start | bytes 516104 | tf_op jit(solution)/shard_map/ppermute | solution.py:346
  65.2 0.0 collective-permute-start.26
  65.3 2.4 %collective-permute-start.27 = (bf16[672,128]{1,0:T(8,128)(2,1)S(1)}, bf16[672,128]{1,0:T(8,128)(2,1)S(1)}, u32[]{:S(2)}, u32[]{:S(2)}) collective-permute-start(bf16[672,128]{1,0:T(8,128)(2,1)S(1)} %get-tuple-element.123), channel_id=1, source_target_pairs={{0,3},{1,2},{2,1},{3,0},{4,7},{5,6},{6,5},{7,4},{8,11},{9,10},{10,... | collective-permute-start | bytes 516104 | tf_op jit(solution)/shard_map/ppermute | solution.py:346
  67.6 1.6 %collective-permute-done.23.refs_1_.refs_8_ = bf16[64,576]{1,0:T(8,128)(2,1)S(1)} collective-permute-done((bf16[64,576]{1,0:T(8,128)(2,1)S(1)}, bf16[64,576]{1,0:T(8,128)(2,1)S(1)}, u32[]{:S(2)}, u32[]{:S(2)}) %collective-permute-start.23) | collective-permute-done | bytes 73760 | tf_op jit(solution)/shard_map/ppermute | solution.py:346
  69.3 1.0 %collective-permute-start.24 = (bf16[64,576]{1,0:T(8,128)(2,1)S(1)}, bf16[64,576]{1,0:T(8,128)(2,1)S(1)}, u32[]{:S(2)}, u32[]{:S(2)}) collective-permute-start(bf16[64,576]{1,0:T(8,128)(2,1)S(1)} %shard_map.172), channel_id=1, source_target_pairs={{0,1},{1,0},{2,3},{3,2},{4,5},{5,4},{6,7},{7,6},{8,9},{9,8},{10,11... | collective-permute-start | bytes 221192 | tf_op jit(solution)/shard_map/ppermute | solution.py:346
  70.3 4.7 %collective-permute-done.24.relayed = bf16[64,576]{1,0:T(8,128)(2,1)S(1)} collective-permute-done((bf16[64,576]{1,0:T(8,128)(2,1)S(1)}, bf16[64,576]{1,0:T(8,128)(2,1)S(1)}, u32[]{:S(2)}, u32[]{:S(2)}) %collective-permute-start.24) | collective-permute-done | bytes 73760 | tf_op jit(solution)/shard_map/ppermute | solution.py:346
  74.9 0.0 collective-permute-done.25.refs_4_
  74.9 0.0 collective-permute-done.26.refs_5_
  74.9 0.0 collective-permute-done.27.refs_6_
  74.9 1.5 %shard_map.173 = (bf16[1,128,256]{2,1,0:T(8,128)(2,1)}, bf16[1,128,256]{2,1,0:T(8,128)(2,1)}, bf16[1,128,256]{2,1,0:T(8,128)(2,1)}, f32[1,32,768]{2,1,0:T(8,128)...) custom-call(s32[3]{0:T(128)S(1)} %pad_add_fusion.place, f32[128,256]{1,0:T(8,128)S(1)} %get-tuple-element.65.rate, ...), custom_call_target="tpu_custom_call" | custom-call | bytes 1789964 | tf_op jit(solution)/shard_map/pallas_call | solution.py:49
  (18 shorter events, 0.1 us)
Async XLA Ops:
  0.6 9.5 %copy-start = (bf16[1,128,256]{2,1,0:T(8,128)(2,1)S(1)}, bf16[1,128,256]{2,1,0:T(8,128)(2,1)}, u32[]{:S(2)}) copy-start(bf16[1,128,256]{2,1,0:T(8,128)(2,1)} %q.1) | copy-start | bytes 196612
  0.6 9.5 %copy-start.3 = (bf16[1,128,256]{2,1,0:T(8,128)(2,1)S(1)}, bf16[1,128,256]{2,1,0:T(8,128)(2,1)}, u32[]{:S(2)}) copy-start(bf16[1,128,256]{2,1,0:T(8,128)(2,1)} %og.1) | copy-start | bytes 196612
  0.7 9.5 %copy-start.2 = (bf16[1,128,256]{2,1,0:T(8,128)(2,1)S(1)}, bf16[1,128,256]{2,1,0:T(8,128)(2,1)}, u32[]{:S(2)}) copy-start(bf16[1,128,256]{2,1,0:T(8,128)(2,1)} %v.1) | copy-start | bytes 196612
  0.7 9.5 %copy-start.1 = (bf16[1,128,256]{2,1,0:T(8,128)(2,1)S(1)}, bf16[1,128,256]{2,1,0:T(8,128)(2,1)}, u32[]{:S(2)}) copy-start(bf16[1,128,256]{2,1,0:T(8,128)(2,1)} %k.1) | copy-start | bytes 196612
  2.9 25.3 %all-to-all-start = ((bf16[8,32,1152]{2,1,0:T(8,128)(2,1)}), bf16[8,32,1152]{2,1,0:T(8,128)(2,1)S(1)}, u32[]{:S(2)}, u32[]{:S(2)}) async-start(bf16[8,32,1152]{2,1,0:T(8,128)(2,1)} %shard_map.164), calls=%async_computation | async-start | bytes 1179648 | tf_op jit(solution)/shard_map/all_to_all | solution.py:369
  10.2 0.7 copy-start.4
  10.9 0.7 copy-start.5
  11.6 16.6 %collective-permute-start = (bf16[128,768]{1,0:T(8,128)(2,1)S(1)}, bf16[128,768]{1,0:T(8,128)(2,1)S(1)}, u32[]{:S(2)}, u32[]{:S(2)}) collective-permute-start(bf16[128,768]{1,0:T(8,128)(2,1)S(1)} %get-tuple-element.68), channel_id=1, source_target_pairs={{0,1},{1,0},{2,3},{3,2},{4,5},{5,4},{6,7},{7,6},{8,9},{9,8},{10,11... | collective-permute-start | bytes 589832 | tf_op jit(solution)/shard_map/ppermute | solution.py:346
  13.7 18.8 %collective-permute-start.7 = (bf16[128,512]{1,0:T(8,128)(2,1)S(1)}, bf16[128,512]{1,0:T(8,128)(2,1)S(1)}, u32[]{:S(2)}, u32[]{:S(2)}) collective-permute-start(bf16[128,512]{1,0:T(8,128)(2,1)S(1)} %get-tuple-element.92.refs_0_), channel_id=1, source_target_pairs={{0,3},{1,2},{2,1},{3,0},{4,7},{5,6},{6,5},{7,4},{8,11},{9,10},{10,... | collective-permute-start | bytes 393224 | tf_op jit(solution)/shard_map/ppermute | solution.py:346
  15.2 13.0 %collective-permute-start.2 = (bf16[128,256]{1,0:T(8,128)(2,1)S(1)}, bf16[128,256]{1,0:T(8,128)(2,1)S(1)}, u32[]{:S(2)}, u32[]{:S(2)}) collective-permute-start(bf16[128,256]{1,0:T(8,128)(2,1)S(1)} %bitcast.8), channel_id=1, source_target_pairs={{0,3},{1,2},{2,1},{3,0},{4,7},{5,6},{6,5},{7,4},{8,11},{9,10},{10,... | collective-permute-start | bytes 196616 | tf_op jit(solution)/shard_map/ppermute | solution.py:346
  16.6 11.6 %collective-permute-start.1 = (bf16[128,256]{1,0:T(8,128)(2,1)S(1)}, bf16[128,256]{1,0:T(8,128)(2,1)S(1)}, u32[]{:S(2)}, u32[]{:S(2)}) collective-permute-start(bf16[128,256]{1,0:T(8,128)(2,1)S(1)} %bitcast.9), channel_id=1, source_target_pairs={{0,2},{1,3},{2,0},{3,1},{4,6},{5,7},{6,4},{7,5},{8,10},{9,11},{10,... | collective-permute-start | bytes 196616 | tf_op jit(solution)/shard_map/ppermute | solution.py:346
  18.1 17.7 %collective-permute-start.6 = (bf16[128,512]{1,0:T(8,128)(2,1)S(1)}, bf16[128,512]{1,0:T(8,128)(2,1)S(1)}, u32[]{:S(2)}, u32[]{:S(2)}) collective-permute-start(bf16[128,512]{1,0:T(8,128)(2,1)S(1)} %get-tuple-element.92.refs_0_), channel_id=1, source_target_pairs={{0,2},{1,3},{2,0},{3,1},{4,6},{5,7},{6,4},{7,5},{8,10},{9,11},{10,... | collective-permute-start | bytes 393224 | tf_op jit(solution)/shard_map/ppermute | solution.py:346
  29.0 6.8 %collective-permute-start.3 = (bf16[128,256]{1,0:T(8,128)(2,1)S(1)}, bf16[128,256]{1,0:T(8,128)(2,1)S(1)}, u32[]{:S(2)}, u32[]{:S(2)}) collective-permute-start(bf16[128,256]{1,0:T(8,128)(2,1)S(1)} %get-tuple-element.76), channel_id=1, source_target_pairs={{0,2},{1,3},{2,0},{3,1},{4,6},{5,7},{6,4},{7,5},{8,10},{9,11},{10,... | collective-permute-start | bytes 196616 | tf_op jit(solution)/shard_map/ppermute | solution.py:346
  30.3 5.8 %collective-permute-start.4 = (bf16[128,256]{1,0:T(8,128)(2,1)S(1)}, bf16[128,256]{1,0:T(8,128)(2,1)S(1)}, u32[]{:S(2)}, u32[]{:S(2)}) collective-permute-start(bf16[128,256]{1,0:T(8,128)(2,1)S(1)} %get-tuple-element.77), channel_id=1, source_target_pairs={{0,3},{1,2},{2,1},{3,0},{4,7},{5,6},{6,5},{7,4},{8,11},{9,10},{10,... | collective-permute-start | bytes 196616 | tf_op jit(solution)/shard_map/ppermute | solution.py:346
  32.5 4.3 %collective-permute-start.5 = (bf16[128,256]{1,0:T(8,128)(2,1)S(1)}, bf16[128,256]{1,0:T(8,128)(2,1)S(1)}, u32[]{:S(2)}, u32[]{:S(2)}) collective-permute-start(bf16[128,256]{1,0:T(8,128)(2,1)S(1)} %get-tuple-element.78), channel_id=1, source_target_pairs={{0,1},{1,0},{2,3},{3,2},{4,5},{5,4},{6,7},{7,6},{8,9},{9,8},{10,11... | collective-permute-start | bytes 196616 | tf_op jit(solution)/shard_map/ppermute | solution.py:346
  32.5 6.3 %collective-permute-start.11 = (bf16[128,256]{1,0:T(8,128)(2,1)S(1)}, bf16[128,256]{1,0:T(8,128)(2,1)S(1)}, u32[]{:S(2)}, u32[]{:S(2)}) collective-permute-start(bf16[128,256]{1,0:T(8,128)(2,1)S(1)} %bitcast.11), channel_id=1, source_target_pairs={{0,4},{1,5},{2,6},{3,7},{4,0},{5,1},{6,2},{7,3},{8,12},{9,13},{10,... | collective-permute-start | bytes 196616 | tf_op jit(solution)/shard_map/ppermute | solution.py:346
  36.9 3.1 %collective-permute-start.10 = (f32[2,128]{1,0:T(2,128)S(1)}, f32[2,128]{1,0:T(2,128)S(1)}, u32[]{:S(2)}, u32[]{:S(2)}) collective-permute-start(f32[2,128]{1,0:T(2,128)S(1)} %get-tuple-element.87.refs_0_), channel_id=1, source_target_pairs={{0,24},{8,16},{16,8},{24,0},{1,25},{9,17},{17,9},{25,1},{2,26},{10... | collective-permute-start | bytes 3080 | tf_op jit(solution)/shard_map/ppermute | solution.py:346
  37.0 3.6 %collective-permute-start.9 = (f32[2,128]{1,0:T(2,128)S(1)}, f32[2,128]{1,0:T(2,128)S(1)}, u32[]{:S(2)}, u32[]{:S(2)}) collective-permute-start(f32[2,128]{1,0:T(2,128)S(1)} %get-tuple-element.87.refs_0_), channel_id=1, source_target_pairs={{0,16},{8,24},{16,0},{24,8},{1,17},{9,25},{17,1},{25,9},{2,18},{10... | collective-permute-start | bytes 3080 | tf_op jit(solution)/shard_map/ppermute | solution.py:346
  38.6 2.1 %collective-permute-start.8 = (f32[2,128]{1,0:T(2,128)S(1)}, f32[2,128]{1,0:T(2,128)S(1)}, u32[]{:S(2)}, u32[]{:S(2)}) collective-permute-start(f32[2,128]{1,0:T(2,128)S(1)} %get-tuple-element.87.refs_0_), channel_id=1, source_target_pairs={{0,8},{8,0},{16,24},{24,16},{1,9},{9,1},{17,25},{25,17},{2,10},{10... | collective-permute-start | bytes 3080 | tf_op jit(solution)/shard_map/ppermute | solution.py:346
  40.8 7.5 %collective-permute-start.15 = (bf16[128,256]{1,0:T(8,128)(2,1)S(1)}, bf16[128,256]{1,0:T(8,128)(2,1)S(1)}, u32[]{:S(2)}, u32[]{:S(2)}) collective-permute-start(bf16[128,256]{1,0:T(8,128)(2,1)S(1)} %shard_map.167.refs_4_), channel_id=1, source_target_pairs={{0,4},{1,5},{2,6},{3,7},{4,0},{5,1},{6,2},{7,3},{8,12},{9,13},{10,... | collective-permute-start | bytes 196616 | tf_op jit(solution)/shard_map/ppermute | solution.py:346
  43.6 6.8 %collective-permute-start.14 = (bf16[128,256]{1,0:T(8,128)(2,1)S(1)}, bf16[128,256]{1,0:T(8,128)(2,1)S(1)}, u32[]{:S(2)}, u32[]{:S(2)}) collective-permute-start(bf16[128,256]{1,0:T(8,128)(2,1)S(1)} %shard_map.167.refs_4_), channel_id=1, source_target_pairs={{0,3},{1,2},{2,1},{3,0},{4,7},{5,6},{6,5},{7,4},{8,11},{9,10},{10,... | collective-permute-start | bytes 196616 | tf_op jit(solution)/shard_map/ppermute | solution.py:346
  44.8 7.0 %collective-permute-start.13 = (bf16[128,256]{1,0:T(8,128)(2,1)S(1)}, bf16[128,256]{1,0:T(8,128)(2,1)S(1)}, u32[]{:S(2)}, u32[]{:S(2)}) collective-permute-start(bf16[128,256]{1,0:T(8,128)(2,1)S(1)} %shard_map.167.refs_4_), channel_id=1, source_target_pairs={{0,2},{1,3},{2,0},{3,1},{4,6},{5,7},{6,4},{7,5},{8,10},{9,11},{10,... | collective-permute-start | bytes 196616 | tf_op jit(solution)/shard_map/ppermute | solution.py:346
  45.6 6.3 %collective-permute-start.12 = (bf16[128,256]{1,0:T(8,128)(2,1)S(1)}, bf16[128,256]{1,0:T(8,128)(2,1)S(1)}, u32[]{:S(2)}, u32[]{:S(2)}) collective-permute-start(bf16[128,256]{1,0:T(8,128)(2,1)S(1)} %shard_map.167.refs_4_), channel_id=1, source_target_pairs={{0,1},{1,0},{2,3},{3,2},{4,5},{5,4},{6,7},{7,6},{8,9},{9,8},{10,11... | collective-permute-start | bytes 196616 | tf_op jit(solution)/shard_map/ppermute | solution.py:346
  48.3 7.4 %collective-permute-start.18 = (bf16[128,512]{1,0:T(8,128)(2,1)S(1)}, bf16[128,512]{1,0:T(8,128)(2,1)S(1)}, u32[]{:S(2)}, u32[]{:S(2)}) collective-permute-start(bf16[128,512]{1,0:T(8,128)(2,1)S(1)} %shard_map.170.refs_4_), channel_id=1, source_target_pairs={{0,3},{1,2},{2,1},{3,0},{4,7},{5,6},{6,5},{7,4},{8,11},{9,10},{10,... | collective-permute-start | bytes 393224 | tf_op jit(solution)/shard_map/ppermute | solution.py:346
  49.6 7.7 %collective-permute-start.17 = (bf16[128,512]{1,0:T(8,128)(2,1)S(1)}, bf16[128,512]{1,0:T(8,128)(2,1)S(1)}, u32[]{:S(2)}, u32[]{:S(2)}) collective-permute-start(bf16[128,512]{1,0:T(8,128)(2,1)S(1)} %shard_map.170.refs_4_), channel_id=1, source_target_pairs={{0,2},{1,3},{2,0},{3,1},{4,6},{5,7},{6,4},{7,5},{8,10},{9,11},{10,... | collective-permute-start | bytes 393224 | tf_op jit(solution)/shard_map/ppermute | solution.py:346
  50.4 7.8 %collective-permute-start.16 = (bf16[128,512]{1,0:T(8,128)(2,1)S(1)}, bf16[128,512]{1,0:T(8,128)(2,1)S(1)}, u32[]{:S(2)}, u32[]{:S(2)}) collective-permute-start(bf16[128,512]{1,0:T(8,128)(2,1)S(1)} %shard_map.170.refs_4_), channel_id=1, source_target_pairs={{0,1},{1,0},{2,3},{3,2},{4,5},{5,4},{6,7},{7,6},{8,9},{9,8},{10,11... | collective-permute-start | bytes 393224 | tf_op jit(solution)/shard_map/ppermute | solution.py:346
  52.7 8.3 %collective-permute-start.19 = (bf16[128,256]{1,0:T(8,128)(2,1)S(1)}, bf16[128,256]{1,0:T(8,128)(2,1)S(1)}, u32[]{:S(2)}, u32[]{:S(2)}) collective-permute-start(bf16[128,256]{1,0:T(8,128)(2,1)S(1)} %get-tuple-element.111), channel_id=1, source_target_pairs={{0,2},{1,3},{2,0},{3,1},{4,6},{5,7},{6,4},{7,5},{8,10},{9,11},{10,... | collective-permute-start | bytes 196616 | tf_op jit(solution)/shard_map/ppermute | solution.py:346
  53.5 7.5 %collective-permute-start.20 = (bf16[128,256]{1,0:T(8,128)(2,1)S(1)}, bf16[128,256]{1,0:T(8,128)(2,1)S(1)}, u32[]{:S(2)}, u32[]{:S(2)}) collective-permute-start(bf16[128,256]{1,0:T(8,128)(2,1)S(1)} %get-tuple-element.112), channel_id=1, source_target_pairs={{0,3},{1,2},{2,1},{3,0},{4,7},{5,6},{6,5},{7,4},{8,11},{9,10},{10,... | collective-permute-start | bytes 196616 | tf_op jit(solution)/shard_map/ppermute | solution.py:346
  55.7 5.3 %collective-permute-start.21 = (bf16[128,256]{1,0:T(8,128)(2,1)S(1)}, bf16[128,256]{1,0:T(8,128)(2,1)S(1)}, u32[]{:S(2)}, u32[]{:S(2)}) collective-permute-start(bf16[128,256]{1,0:T(8,128)(2,1)S(1)} %get-tuple-element.113), channel_id=1, source_target_pairs={{0,1},{1,0},{2,3},{3,2},{4,5},{5,4},{6,7},{7,6},{8,9},{9,8},{10,11... | collective-permute-start | bytes 196616 | tf_op jit(solution)/shard_map/ppermute | solution.py:346
  61.0 6.7 %collective-permute-start.22 = (bf16[64,576]{1,0:T(8,128)(2,1)S(1)}, bf16[64,576]{1,0:T(8,128)(2,1)S(1)}, u32[]{:S(2)}, u32[]{:S(2)}) collective-permute-start(bf16[64,576]{1,0:T(8,128)(2,1)S(1)} %get-tuple-element.114), channel_id=1, source_target_pairs={{0,4},{1,5},{2,6},{3,7},{4,0},{5,1},{6,2},{7,3},{8,12},{9,13},{10,... | collective-permute-start | bytes 221192 | tf_op jit(solution)/shard_map/ppermute | solution.py:346
  62.1 7.2 %collective-permute-start.23 = (bf16[64,576]{1,0:T(8,128)(2,1)S(1)}, bf16[64,576]{1,0:T(8,128)(2,1)S(1)}, u32[]{:S(2)}, u32[]{:S(2)}) collective-permute-start(bf16[64,576]{1,0:T(8,128)(2,1)S(1)} %get-tuple-element.115), channel_id=1, source_target_pairs={{0,6},{1,7},{2,4},{3,5},{4,2},{5,3},{6,0},{7,1},{8,14},{9,15},{10,... | collective-permute-start | bytes 221192 | tf_op jit(solution)/shard_map/ppermute | solution.py:346
  64.2 10.8 %collective-permute-start.25 = (bf16[672,128]{1,0:T(8,128)(2,1)S(1)}, bf16[672,128]{1,0:T(8,128)(2,1)S(1)}, u32[]{:S(2)}, u32[]{:S(2)}) collective-permute-start(bf16[672,128]{1,0:T(8,128)(2,1)S(1)} %get-tuple-element.121), channel_id=1, source_target_pairs={{0,1},{1,0},{2,3},{3,2},{4,5},{5,4},{6,7},{7,6},{8,9},{9,8},{10,11... | collective-permute-start | bytes 516104 | tf_op jit(solution)/shard_map/ppermute | solution.py:346
  65.2 9.7 %collective-permute-start.26 = (bf16[672,128]{1,0:T(8,128)(2,1)S(1)}, bf16[672,128]{1,0:T(8,128)(2,1)S(1)}, u32[]{:S(2)}, u32[]{:S(2)}) collective-permute-start(bf16[672,128]{1,0:T(8,128)(2,1)S(1)} %get-tuple-element.122), channel_id=1, source_target_pairs={{0,2},{1,3},{2,0},{3,1},{4,6},{5,7},{6,4},{7,5},{8,10},{9,11},{10,... | collective-permute-start | bytes 516104 | tf_op jit(solution)/shard_map/ppermute | solution.py:346
  65.3 9.7 %collective-permute-start.27 = (bf16[672,128]{1,0:T(8,128)(2,1)S(1)}, bf16[672,128]{1,0:T(8,128)(2,1)S(1)}, u32[]{:S(2)}, u32[]{:S(2)}) collective-permute-start(bf16[672,128]{1,0:T(8,128)(2,1)S(1)} %get-tuple-element.123), channel_id=1, source_target_pairs={{0,3},{1,2},{2,1},{3,0},{4,7},{5,6},{6,5},{7,4},{8,11},{9,10},{10,... | collective-permute-start | bytes 516104 | tf_op jit(solution)/shard_map/ppermute | solution.py:346
  69.3 5.7 %collective-permute-start.24 = (bf16[64,576]{1,0:T(8,128)(2,1)S(1)}, bf16[64,576]{1,0:T(8,128)(2,1)S(1)}, u32[]{:S(2)}, u32[]{:S(2)}) collective-permute-start(bf16[64,576]{1,0:T(8,128)(2,1)S(1)} %shard_map.172), channel_id=1, source_target_pairs={{0,1},{1,0},{2,3},{3,2},{4,5},{5,4},{6,7},{7,6},{8,9},{9,8},{10,11... | collective-permute-start | bytes 221192 | tf_op jit(solution)/shard_map/ppermute | solution.py:346

commit v17 on v15

--- a/solution.py
+++ b/solution.py
@@ -389,7 +389,7 @@
             (*(block,) * group, arr((seq_n * rows, 3 * slab), BF)),
             (wall, *q_near),
             24,
-            flops=3 * mflop,
+            flops=20 * mflop,
         )
         *parts, queries = lax.optimization_barrier((*parts, queries))
         parts = [parts[0]] + [move(parts[d], d) for d in (*range(2, group), *range(1, min(2, group)))]

time: 76.2 us -> 74.1 us (0.972)
  starting transfers between devices: 43.2 us -> 41.2 us
    ppermute x28, starting transfers between devices: 35.9 us -> 33.9 us  [move(): return lax.ppermute(x, axis, [(i, i ^ dist) for i in range(size)])]
  transfers between devices with their start and end apart: 29 -> 29, of which waited for: 12 -> 15; matrix products, arithmetic and copies ran while one was open for 0% -> 0% of each run, Pallas kernels for 8% -> 9%
where the time goes in v17:
time: 74.1 us; the launch traced here: 73.8 us
  starting transfers between devices  41.2 us (56%)
  waiting for transfers between devices  20.6 us (28%)
  Pallas kernels  9.76 us (13%)
  local copies, waits for them, and re-layouts  1.35 us (2%)
  between operations  0.84 us (1%)
    ppermute x28, starting transfers between devices, move(): return lax.ppermute(x, axis, [(i, i ^ dist) for i in range(size)])  33.9 us
    ppermute x28, waiting for transfers between devices, move(): return lax.ppermute(x, axis, [(i, i ^ dist) for i in range(size)])  20.6 us
    pallas_call x11, Pallas kernels, call(): pl.pallas_call(kernel, out_shape=outs, in_specs=[SMEM] * smem + [VMEM] *...  7.8 us
    all_to_all x1, starting transfers between devices, local(): lax.all_to_all(packed, 'seq', 0, 0, tiled=True)  7.26 us
    pallas_call x1, Pallas kernels, copying_call(): pl.pallas_call(kernel, out_shape=outs, in_specs=[pl.BlockSpec(memory_spac...  1.96 us
  transfers between devices with their start and end apart: 29, of which 15 were waited for; matrix products, arithmetic and copies ran while one was open for 0% of the time, Pallas kernels for 9%

profile of v17, /device:TPU:0, one launch (start us, length us, event | category | flops | bytes accessed | tf_op | source)
XLA Modules:
  0.0 73.8 jit_solution(15953023689201578434)
XLA Ops:
  0.7 2.0 %shard_map.163 = bf16[8,32,1152]{2,1,0:T(8,128)(2,1)} custom-call(bf16[1,32,768]{2,1,0:T(8,128)(2,1)} %refs_0_.1, bf16[1,32,768]{2,1,0:T(8,128)(2,1)} %refs_1_.1, bf16[1,32,768]{2,1,0:T(8,128)(2,1)} %refs_2_.1, bf16[1,32,768]{2,1,0:T(8,128)(2,1)} %refs_3_.1, bf16[1,32,768]{2,1,0:T(8,128)(2,1)} %refs_4_.1, bf16[1,32,768]{2,1,0:T(8,128)(2,1)} %refs_5_.1), custom_call_target="tpu_custom_call" | custom-call | tf_op jit(solution)/shard_map/pallas_call | solution.py:61
  2.6 7.3 %all-to-all-start = ((bf16[8,32,1152]{2,1,0:T(8,128)(2,1)}), bf16[8,32,1152]{2,1,0:T(8,128)(2,1)S(1)}, u32[]{:S(2)}, u32[]{:S(2)}) async-start(bf16[8,32,1152]{2,1,0:T(8,128)(2,1)} %shard_map.163), calls=%async_computation | async-start | bytes 1179648 | tf_op jit(solution)/shard_map/all_to_all | solution.py:373
  9.9 0.0 copy-start.4
  10.0 0.7 copy-done.4
  10.6 0.7 copy-done.5
  11.3 0.1 shard_map.164
  11.4 2.1 %collective-permute-start = (bf16[128,768]{1,0:T(8,128)(2,1)S(1)}, bf16[128,768]{1,0:T(8,128)(2,1)S(1)}, u32[]{:S(2)}, u32[]{:S(2)}) collective-permute-start(bf16[128,768]{1,0:T(8,128)(2,1)S(1)} %get-tuple-element.77), channel_id=1, source_target_pairs={{0,1},{1,0},{2,3},{3,2},{4,5},{5,4},{6,7},{7,6},{8,9},{9,8},{10,11... | collective-permute-start | bytes 589832 | tf_op jit(solution)/shard_map/ppermute | solution.py:350
  13.5 1.5 %collective-permute-start.2 = (bf16[128,256]{1,0:T(8,128)(2,1)S(1)}, bf16[128,256]{1,0:T(8,128)(2,1)S(1)}, u32[]{:S(2)}, u32[]{:S(2)}) collective-permute-start(bf16[128,256]{1,0:T(8,128)(2,1)S(1)} %bitcast.8), channel_id=1, source_target_pairs={{0,3},{1,2},{2,1},{3,0},{4,7},{5,6},{6,5},{7,4},{8,11},{9,10},{10,... | collective-permute-start | bytes 196616 | tf_op jit(solution)/shard_map/ppermute | solution.py:350
  14.9 0.1 collective-permute-start.1
  15.0 2.8 %collective-permute-start.7 = (bf16[128,512]{1,0:T(8,128)(2,1)S(1)}, bf16[128,512]{1,0:T(8,128)(2,1)S(1)}, u32[]{:S(2)}, u32[]{:S(2)}) collective-permute-start(bf16[128,512]{1,0:T(8,128)(2,1)S(1)} %get-tuple-element.101.refs_0_), channel_id=1, source_target_pairs={{0,3},{1,2},{2,1},{3,0},{4,7},{5,6},{6,5},{7,4},{8,11},{9,10},{10,... | collective-permute-start | bytes 393224 | tf_op jit(solution)/shard_map/ppermute | solution.py:350
  17.9 0.6 collective-permute-start.6
  18.4 4.8 %collective-permute-done.2.refs_3_ = bf16[128,256]{1,0:T(8,128)(2,1)S(1)} collective-permute-done((bf16[128,256]{1,0:T(8,128)(2,1)S(1)}, bf16[128,256]{1,0:T(8,128)(2,1)S(1)}, u32[]{:S(2)}, u32[]{:S(2)}) %collective-permute-start.2) | collective-permute-done | bytes 65568 | tf_op jit(solution)/shard_map/ppermute | solution.py:350
  23.3 0.4 collective-permute-done.1.refs_2_
  23.6 2.3 %collective-permute-done.refs_1_ = bf16[128,768]{1,0:T(8,128)(2,1)S(1)} collective-permute-done((bf16[128,768]{1,0:T(8,128)(2,1)S(1)}, bf16[128,768]{1,0:T(8,128)(2,1)S(1)}, u32[]{:S(2)}, u32[]{:S(2)}) %collective-permute-start) | collective-permute-done | bytes 196640 | tf_op jit(solution)/shard_map/ppermute | solution.py:350
  25.9 0.8 %shard_map.165 = (bf16[128,256]{1,0:T(8,128)(2,1)S(1)}, bf16[128,256]{1,0:T(8,128)(2,1)S(1)}, bf16[128,256]{1,0:T(8,128)(2,1)S(1)}, bf16[128,256]{1,0:T(8,128)(2,1)S(1)}, bf16[256,576]{1,0:T(8,128)(2,1)S(1)}) custom-call(bf16[256,1152]{1,0:T(8,128)(2,1)S(1)} %bitcast.5, bf16[128,256]{1,0:T(8,128)(2,1)S(1)} %bitcast.10, ...), custom_call_target="tpu_custom_call" | custom-call | flops 1006632960 | bytes 1540096 | tf_op jit(solution)/shard_map/pallas_call | solution.py:49
  26.7 1.8 %collective-permute-start.3 = (bf16[128,256]{1,0:T(8,128)(2,1)S(1)}, bf16[128,256]{1,0:T(8,128)(2,1)S(1)}, u32[]{:S(2)}, u32[]{:S(2)}) collective-permute-start(bf16[128,256]{1,0:T(8,128)(2,1)S(1)} %get-tuple-element.85), channel_id=1, source_target_pairs={{0,2},{1,3},{2,0},{3,1},{4,6},{5,7},{6,4},{7,5},{8,10},{9,11},{10,... | collective-permute-start | bytes 196616 | tf_op jit(solution)/shard_map/ppermute | solution.py:350
  28.5 1.1 %collective-permute-start.4 = (bf16[128,256]{1,0:T(8,128)(2,1)S(1)}, bf16[128,256]{1,0:T(8,128)(2,1)S(1)}, u32[]{:S(2)}, u32[]{:S(2)}) collective-permute-start(bf16[128,256]{1,0:T(8,128)(2,1)S(1)} %get-tuple-element.86), channel_id=1, source_target_pairs={{0,3},{1,2},{2,1},{3,0},{4,7},{5,6},{6,5},{7,4},{8,11},{9,10},{10,... | collective-permute-start | bytes 196616 | tf_op jit(solution)/shard_map/ppermute | solution.py:350
  29.7 0.6 collective-permute-start.5
  30.2 0.0 collective-permute-done.7.refs_3_
  30.3 2.5 %collective-permute-start.11 = (bf16[128,256]{1,0:T(8,128)(2,1)S(1)}, bf16[128,256]{1,0:T(8,128)(2,1)S(1)}, u32[]{:S(2)}, u32[]{:S(2)}) collective-permute-start(bf16[128,256]{1,0:T(8,128)(2,1)S(1)} %bitcast.11), channel_id=1, source_target_pairs={{0,4},{1,5},{2,6},{3,7},{4,0},{5,1},{6,2},{7,3},{8,12},{9,13},{10,... | collective-permute-start | bytes 196616 | tf_op jit(solution)/shard_map/ppermute | solution.py:350
  32.8 0.0 collective-permute-done.6.refs_2_
  32.8 0.0 collective-permute-done.3.refs_1_
  32.8 1.9 %collective-permute-done.4.refs_2_ = bf16[128,256]{1,0:T(8,128)(2,1)S(1)} collective-permute-done((bf16[128,256]{1,0:T(8,128)(2,1)S(1)}, bf16[128,256]{1,0:T(8,128)(2,1)S(1)}, u32[]{:S(2)}, u32[]{:S(2)}) %collective-permute-start.4) | collective-permute-done | bytes 65568 | tf_op jit(solution)/shard_map/ppermute | solution.py:350
  34.7 0.1 collective-permute-done.5.refs_3_
  34.8 0.1 shard_map.166
  35.0 0.1 collective-permute-start.10
  35.0 1.6 %collective-permute-start.9 = (f32[2,128]{1,0:T(2,128)S(1)}, f32[2,128]{1,0:T(2,128)S(1)}, u32[]{:S(2)}, u32[]{:S(2)}) collective-permute-start(f32[2,128]{1,0:T(2,128)S(1)} %get-tuple-element.96.refs_0_), channel_id=1, source_target_pairs={{0,16},{8,24},{16,0},{24,8},{1,17},{9,25},{17,1},{25,9},{2,18},{10... | collective-permute-start | bytes 3080 | tf_op jit(solution)/shard_map/ppermute | solution.py:350
  36.6 0.3 collective-permute-start.8
  36.9 0.0 collective-permute-done.11.right
  36.9 1.1 %collective-permute-done.10.refs_3_ = f32[2,128]{1,0:T(2,128)S(1)} collective-permute-done((f32[2,128]{1,0:T(2,128)S(1)}, f32[2,128]{1,0:T(2,128)S(1)}, u32[]{:S(2)}, u32[]{:S(2)}) %collective-permute-start.10) | collective-permute-done | bytes 1056 | tf_op jit(solution)/shard_map/ppermute | solution.py:350
  38.0 0.7 collective-permute-done.9.refs_2_
  38.7 0.0 collective-permute-done.8.refs_1_
  38.7 0.1 shard_map.167.refs_4_
  38.8 2.5 %collective-permute-start.15 = (bf16[128,256]{1,0:T(8,128)(2,1)S(1)}, bf16[128,256]{1,0:T(8,128)(2,1)S(1)}, u32[]{:S(2)}, u32[]{:S(2)}) collective-permute-start(bf16[128,256]{1,0:T(8,128)(2,1)S(1)} %shard_map.167.refs_4_), channel_id=1, source_target_pairs={{0,4},{1,5},{2,6},{3,7},{4,0},{5,1},{6,2},{7,3},{8,12},{9,13},{10,... | collective-permute-start | bytes 196616 | tf_op jit(solution)/shard_map/ppermute | solution.py:350
  41.3 0.9 %collective-permute-start.14 = (bf16[128,256]{1,0:T(8,128)(2,1)S(1)}, bf16[128,256]{1,0:T(8,128)(2,1)S(1)}, u32[]{:S(2)}, u32[]{:S(2)}) collective-permute-start(bf16[128,256]{1,0:T(8,128)(2,1)S(1)} %shard_map.167.refs_4_), channel_id=1, source_target_pairs={{0,3},{1,2},{2,1},{3,0},{4,7},{5,6},{6,5},{7,4},{8,11},{9,10},{10,... | collective-permute-start | bytes 196616 | tf_op jit(solution)/shard_map/ppermute | solution.py:350
  42.2 1.1 %collective-permute-start.13 = (bf16[128,256]{1,0:T(8,128)(2,1)S(1)}, bf16[128,256]{1,0:T(8,128)(2,1)S(1)}, u32[]{:S(2)}, u32[]{:S(2)}) collective-permute-start(bf16[128,256]{1,0:T(8,128)(2,1)S(1)} %shard_map.167.refs_4_), channel_id=1, source_target_pairs={{0,2},{1,3},{2,0},{3,1},{4,6},{5,7},{6,4},{7,5},{8,10},{9,11},{10,... | collective-permute-start | bytes 196616 | tf_op jit(solution)/shard_map/ppermute | solution.py:350
  43.3 1.5 %collective-permute-start.12 = (bf16[128,256]{1,0:T(8,128)(2,1)S(1)}, bf16[128,256]{1,0:T(8,128)(2,1)S(1)}, u32[]{:S(2)}, u32[]{:S(2)}) collective-permute-start(bf16[128,256]{1,0:T(8,128)(2,1)S(1)} %shard_map.167.refs_4_), channel_id=1, source_target_pairs={{0,1},{1,0},{2,3},{3,2},{4,5},{5,4},{6,7},{7,6},{8,9},{9,8},{10,11... | collective-permute-start | bytes 196616 | tf_op jit(solution)/shard_map/ppermute | solution.py:350
  44.8 0.1 pad_add_fusion.place
  44.9 1.1 %shard_map.169 = (f32[4,512,192]{2,1,0:T(8,128)S(1)}, bf16[3,512,192]{2,1,0:T(8,128)(2,1)S(1)}, f32[3,192]{1,0:T(4,128)S(1)}, f32[3,256,192]{2,1,0:T(8,128)S(1)}, f32[3,256,192]{2,1,0:T(8,128)S(1)}) custom-call(bf16[256,1152]{1,0:T(8,128)(2,1)S(1)} %bitcast.6, bf16[128,512]{1,0:T(8,128)(2,1)S(1)} %get-tuple-element.101.refs_0_, ...), custom_call_target="tpu_custom_call" | custom-call | flops 603979776 | bytes 4524288 | tf_op jit(solution)/shard_map/pallas_call | solution.py:49
  46.0 1.0 %collective-permute-start.18 = (bf16[128,512]{1,0:T(8,128)(2,1)S(1)}, bf16[128,512]{1,0:T(8,128)(2,1)S(1)}, u32[]{:S(2)}, u32[]{:S(2)}) collective-permute-start(bf16[128,512]{1,0:T(8,128)(2,1)S(1)} %shard_map.170.refs_4_), channel_id=1, source_target_pairs={{0,3},{1,2},{2,1},{3,0},{4,7},{5,6},{6,5},{7,4},{8,11},{9,10},{10,... | collective-permute-start | bytes 393224 | tf_op jit(solution)/shard_map/ppermute | solution.py:350
  47.0 1.1 %collective-permute-start.17 = (bf16[128,512]{1,0:T(8,128)(2,1)S(1)}, bf16[128,512]{1,0:T(8,128)(2,1)S(1)}, u32[]{:S(2)}, u32[]{:S(2)}) collective-permute-start(bf16[128,512]{1,0:T(8,128)(2,1)S(1)} %shard_map.170.refs_4_), channel_id=1, source_target_pairs={{0,2},{1,3},{2,0},{3,1},{4,6},{5,7},{6,4},{7,5},{8,10},{9,11},{10,... | collective-permute-start | bytes 393224 | tf_op jit(solution)/shard_map/ppermute | solution.py:350
  48.1 1.5 %collective-permute-start.16 = (bf16[128,512]{1,0:T(8,128)(2,1)S(1)}, bf16[128,512]{1,0:T(8,128)(2,1)S(1)}, u32[]{:S(2)}, u32[]{:S(2)}) collective-permute-start(bf16[128,512]{1,0:T(8,128)(2,1)S(1)} %shard_map.170.refs_4_), channel_id=1, source_target_pairs={{0,1},{1,0},{2,3},{3,2},{4,5},{5,4},{6,7},{7,6},{8,9},{9,8},{10,11... | collective-permute-start | bytes 393224 | tf_op jit(solution)/shard_map/ppermute | solution.py:350
  49.6 0.8 %shard_map.168 = (bf16[128,256]{1,0:T(8,128)(2,1)S(1)}, bf16[128,256]{1,0:T(8,128)(2,1)S(1)}, bf16[128,256]{1,0:T(8,128)(2,1)S(1)}, bf16[128,256]{1,0:T(8,128)(2,1)S(1)}, f32[3,256,192]{2,1,0:T(8,128)S(1)}) custom-call(bf16[256,576]{1,0:T(8,128)(2,1)S(1)} %get-tuple-element.78.normed_ref, bf16[128,256]{1,0:T(8,128)(2,1)S(1)} %bitcast.12, ...), custom_call_target="tpu_custom_call" | custom-call | flops 3019898880 | bytes 1802240 | tf_op jit(solution)/shard_map/pallas_call | solution.py:49
  50.4 0.4 collective-permute-start.19
  50.8 1.7 %collective-permute-start.20 = (bf16[128,256]{1,0:T(8,128)(2,1)S(1)}, bf16[128,256]{1,0:T(8,128)(2,1)S(1)}, u32[]{:S(2)}, u32[]{:S(2)}) collective-permute-start(bf16[128,256]{1,0:T(8,128)(2,1)S(1)} %get-tuple-element.120), channel_id=1, source_target_pairs={{0,3},{1,2},{2,1},{3,0},{4,7},{5,6},{6,5},{7,4},{8,11},{9,10},{10,... | collective-permute-start | bytes 196616 | tf_op jit(solution)/shard_map/ppermute | solution.py:350
  52.4 1.0 %collective-permute-done.18.refs_7_ = bf16[128,512]{1,0:T(8,128)(2,1)S(1)} collective-permute-done((bf16[128,512]{1,0:T(8,128)(2,1)S(1)}, bf16[128,512]{1,0:T(8,128)(2,1)S(1)}, u32[]{:S(2)}, u32[]{:S(2)}) %collective-permute-start.18) | collective-permute-done | bytes 131104 | tf_op jit(solution)/shard_map/ppermute | solution.py:350
  53.4 0.5 collective-permute-start.21
  54.0 1.2 %collective-permute-done.17.refs_6_ = bf16[128,512]{1,0:T(8,128)(2,1)S(1)} collective-permute-done((bf16[128,512]{1,0:T(8,128)(2,1)S(1)}, bf16[128,512]{1,0:T(8,128)(2,1)S(1)}, u32[]{:S(2)}, u32[]{:S(2)}) %collective-permute-start.17) | collective-permute-done | bytes 131104 | tf_op jit(solution)/shard_map/ppermute | solution.py:350
  55.2 0.8 %collective-permute-done.16.refs_5_ = bf16[128,512]{1,0:T(8,128)(2,1)S(1)} collective-permute-done((bf16[128,512]{1,0:T(8,128)(2,1)S(1)}, bf16[128,512]{1,0:T(8,128)(2,1)S(1)}, u32[]{:S(2)}, u32[]{:S(2)}) %collective-permute-start.16) | collective-permute-done | bytes 131104 | tf_op jit(solution)/shard_map/ppermute | solution.py:350
  56.0 2.6 %shard_map.171 = (bf16[128,512]{1,0:T(8,128)(2,1)S(1)}, bf16[32,576]{1,0:T(8,128)(2,1)S(1)}, bf16[672,128]{1,0:T(8,128)(2,1)S(1)}, bf16[672,128]{1,0:T(8,128)(2,...) custom-call(s32[3]{0:T(128)S(1)} %pad_add_fusion.place, ...), custom_call_target="tpu_custom_call" | custom-call | flops 6039797760 | bytes 6764812 | tf_op jit(solution)/shard_map/pallas_call | solution.py:49
  58.6 0.9 %collective-permute-start.22 = (bf16[64,576]{1,0:T(8,128)(2,1)S(1)}, bf16[64,576]{1,0:T(8,128)(2,1)S(1)}, u32[]{:S(2)}, u32[]{:S(2)}) collective-permute-start(bf16[64,576]{1,0:T(8,128)(2,1)S(1)} %get-tuple-element.122), channel_id=1, source_target_pairs={{0,4},{1,5},{2,6},{3,7},{4,0},{5,1},{6,2},{7,3},{8,12},{9,13},{10,... | collective-permute-start | bytes 221192 | tf_op jit(solution)/shard_map/ppermute | solution.py:350
  59.5 1.6 %collective-permute-start.23 = (bf16[64,576]{1,0:T(8,128)(2,1)S(1)}, bf16[64,576]{1,0:T(8,128)(2,1)S(1)}, u32[]{:S(2)}, u32[]{:S(2)}) collective-permute-start(bf16[64,576]{1,0:T(8,128)(2,1)S(1)} %get-tuple-element.123), channel_id=1, source_target_pairs={{0,6},{1,7},{2,4},{3,5},{4,2},{5,3},{6,0},{7,1},{8,14},{9,15},{10,... | collective-permute-start | bytes 221192 | tf_op jit(solution)/shard_map/ppermute | solution.py:350
  61.1 1.3 %collective-permute-start.25 = (bf16[672,128]{1,0:T(8,128)(2,1)S(1)}, bf16[672,128]{1,0:T(8,128)(2,1)S(1)}, u32[]{:S(2)}, u32[]{:S(2)}) collective-permute-start(bf16[672,128]{1,0:T(8,128)(2,1)S(1)} %get-tuple-element.130), channel_id=1, source_target_pairs={{0,1},{1,0},{2,3},{3,2},{4,5},{5,4},{6,7},{7,6},{8,9},{9,8},{10,11... | collective-permute-start | bytes 516104 | tf_op jit(solution)/shard_map/ppermute | solution.py:350
  62.4 0.3 collective-permute-start.26
  62.7 1.9 %collective-permute-start.27 = (bf16[672,128]{1,0:T(8,128)(2,1)S(1)}, bf16[672,128]{1,0:T(8,128)(2,1)S(1)}, u32[]{:S(2)}, u32[]{:S(2)}) collective-permute-start(bf16[672,128]{1,0:T(8,128)(2,1)S(1)} %get-tuple-element.132), channel_id=1, source_target_pairs={{0,3},{1,2},{2,1},{3,0},{4,7},{5,6},{6,5},{7,4},{8,11},{9,10},{10,... | collective-permute-start | bytes 516104 | tf_op jit(solution)/shard_map/ppermute | solution.py:350
  64.6 0.1 collective-permute-done.22.refs_0_.refs_3_
  64.7 2.0 %collective-permute-done.23.refs_1_.refs_4_ = bf16[64,576]{1,0:T(8,128)(2,1)S(1)} collective-permute-done((bf16[64,576]{1,0:T(8,128)(2,1)S(1)}, bf16[64,576]{1,0:T(8,128)(2,1)S(1)}, u32[]{:S(2)}, u32[]{:S(2)}) %collective-permute-start.23) | collective-permute-done | bytes 73760 | tf_op jit(solution)/shard_map/ppermute | solution.py:350
  66.7 0.8 %collective-permute-start.24 = (bf16[64,576]{1,0:T(8,128)(2,1)S(1)}, bf16[64,576]{1,0:T(8,128)(2,1)S(1)}, u32[]{:S(2)}, u32[]{:S(2)}) collective-permute-start(bf16[64,576]{1,0:T(8,128)(2,1)S(1)} %shard_map.172), channel_id=1, source_target_pairs={{0,1},{1,0},{2,3},{3,2},{4,5},{5,4},{6,7},{7,6},{8,9},{9,8},{10,11... | collective-permute-start | bytes 221192 | tf_op jit(solution)/shard_map/ppermute | solution.py:350
  67.5 1.7 %collective-permute-done.25.refs_4_.refs_0_ = bf16[672,128]{1,0:T(8,128)(2,1)S(1)} collective-permute-done((bf16[672,128]{1,0:T(8,128)(2,1)S(1)}, bf16[672,128]{1,0:T(8,128)(2,1)S(1)}, u32[]{:S(2)}, u32[]{:S(2)}) %collective-permute-start.25) | collective-permute-done | bytes 172064 | tf_op jit(solution)/shard_map/ppermute | solution.py:350
  69.2 0.2 collective-permute-done.26.refs_5_.refs_1_
  69.4 2.2 %collective-permute-done.27.refs_6_.refs_2_ = bf16[672,128]{1,0:T(8,128)(2,1)S(1)} collective-permute-done((bf16[672,128]{1,0:T(8,128)(2,1)S(1)}, bf16[672,128]{1,0:T(8,128)(2,1)S(1)}, u32[]{:S(2)}, u32[]{:S(2)}) %collective-permute-start.27) | collective-permute-done | bytes 172064 | tf_op jit(solution)/shard_map/ppermute | solution.py:350
  71.7 0.7 %shard_map.173 = (bf16[1,128,256]{2,1,0:T(8,128)(2,1)}, bf16[1,128,256]{2,1,0:T(8,128)(2,1)}, bf16[1,128,256]{2,1,0:T(8,128)(2,1)}) custom-call(f32[128,256]{1,0:T(8,128)S(1)} %get-tuple-element.124.rate, bf16[128,512]{1,0:T(8,128)(2,1)S(1)} %get-tuple-element.125.tok, bf16[128,256]{1,0:T(8,128)(2,1)S(1)} %get-tuple-element.126.refs_0_, ...), custom_call_target="tpu_custom_call" | custom-call | bytes 1236992 | tf_op jit(solution)/shard_map/pallas_call | solution.py:49
  72.4 0.0 collective-permute-done.24.relayed
  72.4 1.4 %shard_map.174 = (f32[1,32,768]{2,1,0:T(8,128)}, f32[1,32,768]{2,1,0:T(8,128)}, f32[1,32,768]{2,1,0:T(8,128)}) custom-call(s32[3]{0:T(128)S(1)} %pad_add_fusion.place, bf16[64,576]{1,0:T(8,128)(2,1)S(1)} %collective-permute-done.24.relayed, bf16[32,576]{1,0:T(8,128)(2,1)S(1)} %get-tuple-element.140.inner, ...), custom_call_target="tpu_custom_call" | custom-call | bytes 1069068 | tf_op jit(solution)/shard_map/pallas_call | solution.py:49
  (19 shorter events, 0.1 us)
Async XLA Ops:
  0.6 9.3 %copy-start.3 = (bf16[1,128,256]{2,1,0:T(8,128)(2,1)S(1)}, bf16[1,128,256]{2,1,0:T(8,128)(2,1)}, u32[]{:S(2)}) copy-start(bf16[1,128,256]{2,1,0:T(8,128)(2,1)} %q.1) | copy-start | bytes 196612
  0.6 9.3 %copy-start.2 = (bf16[1,128,256]{2,1,0:T(8,128)(2,1)S(1)}, bf16[1,128,256]{2,1,0:T(8,128)(2,1)}, u32[]{:S(2)}) copy-start(bf16[1,128,256]{2,1,0:T(8,128)(2,1)} %og.1) | copy-start | bytes 196612
  0.7 9.3 %copy-start.1 = (bf16[1,128,256]{2,1,0:T(8,128)(2,1)S(1)}, bf16[1,128,256]{2,1,0:T(8,128)(2,1)}, u32[]{:S(2)}) copy-start(bf16[1,128,256]{2,1,0:T(8,128)(2,1)} %v.1) | copy-start | bytes 196612
  0.7 9.3 %copy-start = (bf16[1,128,256]{2,1,0:T(8,128)(2,1)S(1)}, bf16[1,128,256]{2,1,0:T(8,128)(2,1)}, u32[]{:S(2)}) copy-start(bf16[1,128,256]{2,1,0:T(8,128)(2,1)} %k.1) | copy-start | bytes 196612
  2.6 23.3 %all-to-all-start = ((bf16[8,32,1152]{2,1,0:T(8,128)(2,1)}), bf16[8,32,1152]{2,1,0:T(8,128)(2,1)S(1)}, u32[]{:S(2)}, u32[]{:S(2)}) async-start(bf16[8,32,1152]{2,1,0:T(8,128)(2,1)} %shard_map.163), calls=%async_computation | async-start | bytes 1179648 | tf_op jit(solution)/shard_map/all_to_all | solution.py:373
  9.9 0.7 copy-start.4
  10.6 0.7 copy-start.5
  11.4 14.5 %collective-permute-start = (bf16[128,768]{1,0:T(8,128)(2,1)S(1)}, bf16[128,768]{1,0:T(8,128)(2,1)S(1)}, u32[]{:S(2)}, u32[]{:S(2)}) collective-permute-start(bf16[128,768]{1,0:T(8,128)(2,1)S(1)} %get-tuple-element.77), channel_id=1, source_target_pairs={{0,1},{1,0},{2,3},{3,2},{4,5},{5,4},{6,7},{7,6},{8,9},{9,8},{10,11... | collective-permute-start | bytes 589832 | tf_op jit(solution)/shard_map/ppermute | solution.py:350
  13.5 9.8 %collective-permute-start.2 = (bf16[128,256]{1,0:T(8,128)(2,1)S(1)}, bf16[128,256]{1,0:T(8,128)(2,1)S(1)}, u32[]{:S(2)}, u32[]{:S(2)}) collective-permute-start(bf16[128,256]{1,0:T(8,128)(2,1)S(1)} %bitcast.8), channel_id=1, source_target_pairs={{0,3},{1,2},{2,1},{3,0},{4,7},{5,6},{6,5},{7,4},{8,11},{9,10},{10,... | collective-permute-start | bytes 196616 | tf_op jit(solution)/shard_map/ppermute | solution.py:350
  14.9 8.7 %collective-permute-start.1 = (bf16[128,256]{1,0:T(8,128)(2,1)S(1)}, bf16[128,256]{1,0:T(8,128)(2,1)S(1)}, u32[]{:S(2)}, u32[]{:S(2)}) collective-permute-start(bf16[128,256]{1,0:T(8,128)(2,1)S(1)} %bitcast.9), channel_id=1, source_target_pairs={{0,2},{1,3},{2,0},{3,1},{4,6},{5,7},{6,4},{7,5},{8,10},{9,11},{10,... | collective-permute-start | bytes 196616 | tf_op jit(solution)/shard_map/ppermute | solution.py:350
  15.0 15.2 %collective-permute-start.7 = (bf16[128,512]{1,0:T(8,128)(2,1)S(1)}, bf16[128,512]{1,0:T(8,128)(2,1)S(1)}, u32[]{:S(2)}, u32[]{:S(2)}) collective-permute-start(bf16[128,512]{1,0:T(8,128)(2,1)S(1)} %get-tuple-element.101.refs_0_), channel_id=1, source_target_pairs={{0,3},{1,2},{2,1},{3,0},{4,7},{5,6},{6,5},{7,4},{8,11},{9,10},{10,... | collective-permute-start | bytes 393224 | tf_op jit(solution)/shard_map/ppermute | solution.py:350
  17.9 14.9 %collective-permute-start.6 = (bf16[128,512]{1,0:T(8,128)(2,1)S(1)}, bf16[128,512]{1,0:T(8,128)(2,1)S(1)}, u32[]{:S(2)}, u32[]{:S(2)}) collective-permute-start(bf16[128,512]{1,0:T(8,128)(2,1)S(1)} %get-tuple-element.101.refs_0_), channel_id=1, source_target_pairs={{0,2},{1,3},{2,0},{3,1},{4,6},{5,7},{6,4},{7,5},{8,10},{9,11},{10,... | collective-permute-start | bytes 393224 | tf_op jit(solution)/shard_map/ppermute | solution.py:350
  26.7 6.1 %collective-permute-start.3 = (bf16[128,256]{1,0:T(8,128)(2,1)S(1)}, bf16[128,256]{1,0:T(8,128)(2,1)S(1)}, u32[]{:S(2)}, u32[]{:S(2)}) collective-permute-start(bf16[128,256]{1,0:T(8,128)(2,1)S(1)} %get-tuple-element.85), channel_id=1, source_target_pairs={{0,2},{1,3},{2,0},{3,1},{4,6},{5,7},{6,4},{7,5},{8,10},{9,11},{10,... | collective-permute-start | bytes 196616 | tf_op jit(solution)/shard_map/ppermute | solution.py:350
  28.5 6.2 %collective-permute-start.4 = (bf16[128,256]{1,0:T(8,128)(2,1)S(1)}, bf16[128,256]{1,0:T(8,128)(2,1)S(1)}, u32[]{:S(2)}, u32[]{:S(2)}) collective-permute-start(bf16[128,256]{1,0:T(8,128)(2,1)S(1)} %get-tuple-element.86), channel_id=1, source_target_pairs={{0,3},{1,2},{2,1},{3,0},{4,7},{5,6},{6,5},{7,4},{8,11},{9,10},{10,... | collective-permute-start | bytes 196616 | tf_op jit(solution)/shard_map/ppermute | solution.py:350
  29.7 5.1 %collective-permute-start.5 = (bf16[128,256]{1,0:T(8,128)(2,1)S(1)}, bf16[128,256]{1,0:T(8,128)(2,1)S(1)}, u32[]{:S(2)}, u32[]{:S(2)}) collective-permute-start(bf16[128,256]{1,0:T(8,128)(2,1)S(1)} %get-tuple-element.87), channel_id=1, source_target_pairs={{0,1},{1,0},{2,3},{3,2},{4,5},{5,4},{6,7},{7,6},{8,9},{9,8},{10,11... | collective-permute-start | bytes 196616 | tf_op jit(solution)/shard_map/ppermute | solution.py:350
  30.3 6.6 %collective-permute-start.11 = (bf16[128,256]{1,0:T(8,128)(2,1)S(1)}, bf16[128,256]{1,0:T(8,128)(2,1)S(1)}, u32[]{:S(2)}, u32[]{:S(2)}) collective-permute-start(bf16[128,256]{1,0:T(8,128)(2,1)S(1)} %bitcast.11), channel_id=1, source_target_pairs={{0,4},{1,5},{2,6},{3,7},{4,0},{5,1},{6,2},{7,3},{8,12},{9,13},{10,... | collective-permute-start | bytes 196616 | tf_op jit(solution)/shard_map/ppermute | solution.py:350
  35.0 3.1 %collective-permute-start.10 = (f32[2,128]{1,0:T(2,128)S(1)}, f32[2,128]{1,0:T(2,128)S(1)}, u32[]{:S(2)}, u32[]{:S(2)}) collective-permute-start(f32[2,128]{1,0:T(2,128)S(1)} %get-tuple-element.96.refs_0_), channel_id=1, source_target_pairs={{0,24},{8,16},{16,8},{24,0},{1,25},{9,17},{17,9},{25,1},{2,26},{10... | collective-permute-start | bytes 3080 | tf_op jit(solution)/shard_map/ppermute | solution.py:350
  35.0 3.6 %collective-permute-start.9 = (f32[2,128]{1,0:T(2,128)S(1)}, f32[2,128]{1,0:T(2,128)S(1)}, u32[]{:S(2)}, u32[]{:S(2)}) collective-permute-start(f32[2,128]{1,0:T(2,128)S(1)} %get-tuple-element.96.refs_0_), channel_id=1, source_target_pairs={{0,16},{8,24},{16,0},{24,8},{1,17},{9,25},{17,1},{25,9},{2,18},{10... | collective-permute-start | bytes 3080 | tf_op jit(solution)/shard_map/ppermute | solution.py:350
  36.6 2.1 %collective-permute-start.8 = (f32[2,128]{1,0:T(2,128)S(1)}, f32[2,128]{1,0:T(2,128)S(1)}, u32[]{:S(2)}, u32[]{:S(2)}) collective-permute-start(f32[2,128]{1,0:T(2,128)S(1)} %get-tuple-element.96.refs_0_), channel_id=1, source_target_pairs={{0,8},{8,0},{16,24},{24,16},{1,9},{9,1},{17,25},{25,17},{2,10},{10... | collective-permute-start | bytes 3080 | tf_op jit(solution)/shard_map/ppermute | solution.py:350
  38.8 7.2 %collective-permute-start.15 = (bf16[128,256]{1,0:T(8,128)(2,1)S(1)}, bf16[128,256]{1,0:T(8,128)(2,1)S(1)}, u32[]{:S(2)}, u32[]{:S(2)}) collective-permute-start(bf16[128,256]{1,0:T(8,128)(2,1)S(1)} %shard_map.167.refs_4_), channel_id=1, source_target_pairs={{0,4},{1,5},{2,6},{3,7},{4,0},{5,1},{6,2},{7,3},{8,12},{9,13},{10,... | collective-permute-start | bytes 196616 | tf_op jit(solution)/shard_map/ppermute | solution.py:350
  41.3 6.8 %collective-permute-start.14 = (bf16[128,256]{1,0:T(8,128)(2,1)S(1)}, bf16[128,256]{1,0:T(8,128)(2,1)S(1)}, u32[]{:S(2)}, u32[]{:S(2)}) collective-permute-start(bf16[128,256]{1,0:T(8,128)(2,1)S(1)} %shard_map.167.refs_4_), channel_id=1, source_target_pairs={{0,3},{1,2},{2,1},{3,0},{4,7},{5,6},{6,5},{7,4},{8,11},{9,10},{10,... | collective-permute-start | bytes 196616 | tf_op jit(solution)/shard_map/ppermute | solution.py:350
  42.2 7.4 %collective-permute-start.13 = (bf16[128,256]{1,0:T(8,128)(2,1)S(1)}, bf16[128,256]{1,0:T(8,128)(2,1)S(1)}, u32[]{:S(2)}, u32[]{:S(2)}) collective-permute-start(bf16[128,256]{1,0:T(8,128)(2,1)S(1)} %shard_map.167.refs_4_), channel_id=1, source_target_pairs={{0,2},{1,3},{2,0},{3,1},{4,6},{5,7},{6,4},{7,5},{8,10},{9,11},{10,... | collective-permute-start | bytes 196616 | tf_op jit(solution)/shard_map/ppermute | solution.py:350
  43.3 6.3 %collective-permute-start.12 = (bf16[128,256]{1,0:T(8,128)(2,1)S(1)}, bf16[128,256]{1,0:T(8,128)(2,1)S(1)}, u32[]{:S(2)}, u32[]{:S(2)}) collective-permute-start(bf16[128,256]{1,0:T(8,128)(2,1)S(1)} %shard_map.167.refs_4_), channel_id=1, source_target_pairs={{0,1},{1,0},{2,3},{3,2},{4,5},{5,4},{6,7},{7,6},{8,9},{9,8},{10,11... | collective-permute-start | bytes 196616 | tf_op jit(solution)/shard_map/ppermute | solution.py:350
  46.0 7.4 %collective-permute-start.18 = (bf16[128,512]{1,0:T(8,128)(2,1)S(1)}, bf16[128,512]{1,0:T(8,128)(2,1)S(1)}, u32[]{:S(2)}, u32[]{:S(2)}) collective-permute-start(bf16[128,512]{1,0:T(8,128)(2,1)S(1)} %shard_map.170.refs_4_), channel_id=1, source_target_pairs={{0,3},{1,2},{2,1},{3,0},{4,7},{5,6},{6,5},{7,4},{8,11},{9,10},{10,... | collective-permute-start | bytes 393224 | tf_op jit(solution)/shard_map/ppermute | solution.py:350
  47.0 8.2 %collective-permute-start.17 = (bf16[128,512]{1,0:T(8,128)(2,1)S(1)}, bf16[128,512]{1,0:T(8,128)(2,1)S(1)}, u32[]{:S(2)}, u32[]{:S(2)}) collective-permute-start(bf16[128,512]{1,0:T(8,128)(2,1)S(1)} %shard_map.170.refs_4_), channel_id=1, source_target_pairs={{0,2},{1,3},{2,0},{3,1},{4,6},{5,7},{6,4},{7,5},{8,10},{9,11},{10,... | collective-permute-start | bytes 393224 | tf_op jit(solution)/shard_map/ppermute | solution.py:350
  48.1 8.0 %collective-permute-start.16 = (bf16[128,512]{1,0:T(8,128)(2,1)S(1)}, bf16[128,512]{1,0:T(8,128)(2,1)S(1)}, u32[]{:S(2)}, u32[]{:S(2)}) collective-permute-start(bf16[128,512]{1,0:T(8,128)(2,1)S(1)} %shard_map.170.refs_4_), channel_id=1, source_target_pairs={{0,1},{1,0},{2,3},{3,2},{4,5},{5,4},{6,7},{7,6},{8,9},{9,8},{10,11... | collective-permute-start | bytes 393224 | tf_op jit(solution)/shard_map/ppermute | solution.py:350
  50.4 8.2 %collective-permute-start.19 = (bf16[128,256]{1,0:T(8,128)(2,1)S(1)}, bf16[128,256]{1,0:T(8,128)(2,1)S(1)}, u32[]{:S(2)}, u32[]{:S(2)}) collective-permute-start(bf16[128,256]{1,0:T(8,128)(2,1)S(1)} %get-tuple-element.119), channel_id=1, source_target_pairs={{0,2},{1,3},{2,0},{3,1},{4,6},{5,7},{6,4},{7,5},{8,10},{9,11},{10,... | collective-permute-start | bytes 196616 | tf_op jit(solution)/shard_map/ppermute | solution.py:350
  50.8 7.8 %collective-permute-start.20 = (bf16[128,256]{1,0:T(8,128)(2,1)S(1)}, bf16[128,256]{1,0:T(8,128)(2,1)S(1)}, u32[]{:S(2)}, u32[]{:S(2)}) collective-permute-start(bf16[128,256]{1,0:T(8,128)(2,1)S(1)} %get-tuple-element.120), channel_id=1, source_target_pairs={{0,3},{1,2},{2,1},{3,0},{4,7},{5,6},{6,5},{7,4},{8,11},{9,10},{10,... | collective-permute-start | bytes 196616 | tf_op jit(solution)/shard_map/ppermute | solution.py:350
  53.4 5.2 %collective-permute-start.21 = (bf16[128,256]{1,0:T(8,128)(2,1)S(1)}, bf16[128,256]{1,0:T(8,128)(2,1)S(1)}, u32[]{:S(2)}, u32[]{:S(2)}) collective-permute-start(bf16[128,256]{1,0:T(8,128)(2,1)S(1)} %get-tuple-element.121), channel_id=1, source_target_pairs={{0,1},{1,0},{2,3},{3,2},{4,5},{5,4},{6,7},{7,6},{8,9},{9,8},{10,11... | collective-permute-start | bytes 196616 | tf_op jit(solution)/shard_map/ppermute | solution.py:350
  58.6 6.1 %collective-permute-start.22 = (bf16[64,576]{1,0:T(8,128)(2,1)S(1)}, bf16[64,576]{1,0:T(8,128)(2,1)S(1)}, u32[]{:S(2)}, u32[]{:S(2)}) collective-permute-start(bf16[64,576]{1,0:T(8,128)(2,1)S(1)} %get-tuple-element.122), channel_id=1, source_target_pairs={{0,4},{1,5},{2,6},{3,7},{4,0},{5,1},{6,2},{7,3},{8,12},{9,13},{10,... | collective-permute-start | bytes 221192 | tf_op jit(solution)/shard_map/ppermute | solution.py:350
  59.5 7.2 %collective-permute-start.23 = (bf16[64,576]{1,0:T(8,128)(2,1)S(1)}, bf16[64,576]{1,0:T(8,128)(2,1)S(1)}, u32[]{:S(2)}, u32[]{:S(2)}) collective-permute-start(bf16[64,576]{1,0:T(8,128)(2,1)S(1)} %get-tuple-element.123), channel_id=1, source_target_pairs={{0,6},{1,7},{2,4},{3,5},{4,2},{5,3},{6,0},{7,1},{8,14},{9,15},{10,... | collective-permute-start | bytes 221192 | tf_op jit(solution)/shard_map/ppermute | solution.py:350
  61.1 8.1 %collective-permute-start.25 = (bf16[672,128]{1,0:T(8,128)(2,1)S(1)}, bf16[672,128]{1,0:T(8,128)(2,1)S(1)}, u32[]{:S(2)}, u32[]{:S(2)}) collective-permute-start(bf16[672,128]{1,0:T(8,128)(2,1)S(1)} %get-tuple-element.130), channel_id=1, source_target_pairs={{0,1},{1,0},{2,3},{3,2},{4,5},{5,4},{6,7},{7,6},{8,9},{9,8},{10,11... | collective-permute-start | bytes 516104 | tf_op jit(solution)/shard_map/ppermute | solution.py:350
  62.4 7.0 %collective-permute-start.26 = (bf16[672,128]{1,0:T(8,128)(2,1)S(1)}, bf16[672,128]{1,0:T(8,128)(2,1)S(1)}, u32[]{:S(2)}, u32[]{:S(2)}) collective-permute-start(bf16[672,128]{1,0:T(8,128)(2,1)S(1)} %get-tuple-element.131), channel_id=1, source_target_pairs={{0,2},{1,3},{2,0},{3,1},{4,6},{5,7},{6,4},{7,5},{8,10},{9,11},{10,... | collective-permute-start | bytes 516104 | tf_op jit(solution)/shard_map/ppermute | solution.py:350
  62.7 8.9 %collective-permute-start.27 = (bf16[672,128]{1,0:T(8,128)(2,1)S(1)}, bf16[672,128]{1,0:T(8,128)(2,1)S(1)}, u32[]{:S(2)}, u32[]{:S(2)}) collective-permute-start(bf16[672,128]{1,0:T(8,128)(2,1)S(1)} %get-tuple-element.132), channel_id=1, source_target_pairs={{0,3},{1,2},{2,1},{3,0},{4,7},{5,6},{6,5},{7,4},{8,11},{9,10},{10,... | collective-permute-start | bytes 516104 | tf_op jit(solution)/shard_map/ppermute | solution.py:350
  66.7 5.7 %collective-permute-start.24 = (bf16[64,576]{1,0:T(8,128)(2,1)S(1)}, bf16[64,576]{1,0:T(8,128)(2,1)S(1)}, u32[]{:S(2)}, u32[]{:S(2)}) collective-permute-start(bf16[64,576]{1,0:T(8,128)(2,1)S(1)} %shard_map.172), channel_id=1, source_target_pairs={{0,1},{1,0},{2,3},{3,2},{4,5},{5,4},{6,7},{7,6},{8,9},{9,8},{10,11... | collective-permute-start | bytes 221192 | tf_op jit(solution)/shard_map/ppermute | solution.py:350

commit v18 on v17

--- a/solution.py
+++ b/solution.py
@@ -57,13 +57,20 @@
     )(*args)
 
 
-def copying_call(kernel, outs, args, buffers):
+def pack_weights(group, slab, args, seq_n):
+    _, rows, hidden = args[0].shape
+    hbm = pl.BlockSpec(memory_space=pltpu.HBM)
     return pl.pallas_call(
-        kernel,
-        out_shape=outs,
-        in_specs=[pl.BlockSpec(memory_space=pltpu.HBM)] * len(args),
-        out_specs=[VMEM] * len(outs),
-        scratch_shapes=[*buffers, pltpu.SemaphoreType.DMA((len(args),))],
+        functools.partial(weight_pack_kernel, group, slab),
+        out_shape=arr((seq_n, rows, 6 * slab), BF),
+        in_specs=[hbm] * len(args),
+        out_specs=hbm,
+        scratch_shapes=[
+            pltpu.VMEM((6, rows, hidden), BF),
+            pltpu.VMEM((group, rows, 6 * slab), BF),
+            pltpu.SemaphoreType.DMA((len(args),)),
+            pltpu.SemaphoreType.DMA((seq_n,)),
+        ],
         compiler_params=pltpu.CompilerParams(vmem_limit_bytes=56 << 20),
     )(*args)
 
@@ -124,13 +131,17 @@
 
 
 def weight_pack_kernel(group, slab, *refs):
-    args, (w_out, buf, sems) = refs[:6], refs[6:]
+    args, (w_out, buf, slabs, sems, out_sems) = refs[:6], refs[6:]
     fetch(args, [buf.at[pl.ds(i, 1)] for i in range(6)], sems)
+    copies = []
     for j in range(group):
         cols = pl.ds(j * slab, slab)
-        block = jnp.concatenate([buf[i, :, cols] for i in range(6)], axis=1)
+        slabs[j] = jnp.concatenate([buf[i, :, cols] for i in range(6)], axis=1)
         for p in range(j, w_out.shape[0], group):
-            w_out[p] = block
+            copies.append(pltpu.make_async_copy(slabs.at[j], w_out.at[p], out_sems.at[p]))
+            copies[-1].start()
+    for copy in copies:
+        copy.wait()
 
 
 def columns(w, slab):
@@ -350,7 +361,8 @@
         return lax.ppermute(x, axis, [(i, i ^ dist) for i in range(size)])
 
     def near_all(x):
-        return [x] + [move(x, d) for d in range(1, group)]
+        moved = {d: move(x, d) for d in reversed(range(1, group))}
+        return [x] + [moved[d] for d in range(1, group)]
 
     def mirror(x):
         return [move(x, e * group) for e in range(1, tok_groups)]
@@ -363,12 +375,7 @@
         me = lax.axis_index("seq")
         place = jnp.stack((lax.div(me, group), lax.rem(me, group), me)).astype(jnp.int32)
 
-        (packed,) = copying_call(
-            functools.partial(weight_pack_kernel, group, slab),
-            (arr((seq_n, rows, 6 * slab), BF),),
-            (gs, us, ds, gi, ui, di),
-            [pltpu.VMEM((6, rows, hidden), BF)],
-        )
+        packed = pack_weights(group, slab, (gs, us, ds, gi, ui, di), seq_n)
         packed, queries = lax.optimization_barrier((packed, q[0]))
         wall = lax.all_to_all(packed, "seq", 0, 0, tiled=True).reshape(seq_n * rows, 6 * slab)
         tokens, kv, gg, rate = call(

time: 74.1 us -> 74.1 us (level)
  no operation moved by 1% of the time
where the time goes in v18:
time: 74.1 us; the launch traced here: 73.8 us
  starting transfers between devices  41.2 us (56%)
  waiting for transfers between devices  20.6 us (28%)
  Pallas kernels  9.79 us (13%)
  local copies, waits for them, and re-layouts  1.35 us (2%)
  between operations  0.84 us (1%)
    ppermute x28, starting transfers between devices, move(): return lax.ppermute(x, axis, [(i, i ^ dist) for i in range(size)])  33.9 us
    ppermute x28, waiting for transfers between devices, move(): return lax.ppermute(x, axis, [(i, i ^ dist) for i in range(size)])  20.6 us
    pallas_call x11, Pallas kernels, call(): pl.pallas_call(kernel, out_shape=outs, in_specs=[SMEM] * smem + [VMEM] *...  7.8 us
    all_to_all x1, starting transfers between devices, local(): lax.all_to_all(packed, 'seq', 0, 0, tiled=True)  7.26 us
    pallas_call x1, Pallas kernels, pack_weights(): pl.pallas_call(functools.partial(weight_pack_kernel, group, slab), out_sh...  1.99 us
  transfers between devices with their start and end apart: 29, of which 15 were waited for; matrix products, arithmetic and copies ran while one was open for 0% of the time, Pallas kernels for 9%

profile of v18, /device:TPU:0, one launch (start us, length us, event | category | flops | bytes accessed | tf_op | source)
XLA Modules:
  0.0 73.8 jit_solution(14700595455184067306)
XLA Ops:
  0.7 2.0 %shard_map.163 = bf16[8,32,1152]{2,1,0:T(8,128)(2,1)} custom-call(bf16[1,32,768]{2,1,0:T(8,128)(2,1)} %refs_0_.1, bf16[1,32,768]{2,1,0:T(8,128)(2,1)} %refs_1_.1, bf16[1,32,768]{2,1,0:T(8,128)(2,1)} %refs_2_.1, bf16[1,32,768]{2,1,0:T(8,128)(2,1)} %refs_3_.1, bf16[1,32,768]{2,1,0:T(8,128)(2,1)} %refs_4_.1, bf16[1,32,768]{2,1,0:T(8,128)(2,1)} %refs_5_.1), custom_call_target="tpu_custom_call" | custom-call | tf_op jit(solution)/shard_map/pallas_call | solution.py:63
  2.7 7.3 %all-to-all-start = ((bf16[8,32,1152]{2,1,0:T(8,128)(2,1)}), bf16[8,32,1152]{2,1,0:T(8,128)(2,1)S(1)}, u32[]{:S(2)}, u32[]{:S(2)}) async-start(bf16[8,32,1152]{2,1,0:T(8,128)(2,1)} %shard_map.163), calls=%async_computation | async-start | bytes 1179648 | tf_op jit(solution)/shard_map/all_to_all | solution.py:380
  10.0 0.0 copy-start.4
  10.0 0.7 copy-done.4
  10.7 0.7 copy-done.5
  11.3 0.1 shard_map.164
  11.4 2.1 %collective-permute-start = (bf16[128,768]{1,0:T(8,128)(2,1)S(1)}, bf16[128,768]{1,0:T(8,128)(2,1)S(1)}, u32[]{:S(2)}, u32[]{:S(2)}) collective-permute-start(bf16[128,768]{1,0:T(8,128)(2,1)S(1)} %get-tuple-element.77), channel_id=1, source_target_pairs={{0,1},{1,0},{2,3},{3,2},{4,5},{5,4},{6,7},{7,6},{8,9},{9,8},{10,11... | collective-permute-start | bytes 589832 | tf_op jit(solution)/shard_map/ppermute | solution.py:361
  13.5 1.5 %collective-permute-start.2 = (bf16[128,256]{1,0:T(8,128)(2,1)S(1)}, bf16[128,256]{1,0:T(8,128)(2,1)S(1)}, u32[]{:S(2)}, u32[]{:S(2)}) collective-permute-start(bf16[128,256]{1,0:T(8,128)(2,1)S(1)} %bitcast.8), channel_id=1, source_target_pairs={{0,3},{1,2},{2,1},{3,0},{4,7},{5,6},{6,5},{7,4},{8,11},{9,10},{10,... | collective-permute-start | bytes 196616 | tf_op jit(solution)/shard_map/ppermute | solution.py:361
  15.0 0.1 collective-permute-start.1
  15.0 2.8 %collective-permute-start.7 = (bf16[128,512]{1,0:T(8,128)(2,1)S(1)}, bf16[128,512]{1,0:T(8,128)(2,1)S(1)}, u32[]{:S(2)}, u32[]{:S(2)}) collective-permute-start(bf16[128,512]{1,0:T(8,128)(2,1)S(1)} %get-tuple-element.101.refs_0_), channel_id=1, source_target_pairs={{0,3},{1,2},{2,1},{3,0},{4,7},{5,6},{6,5},{7,4},{8,11},{9,10},{10,... | collective-permute-start | bytes 393224 | tf_op jit(solution)/shard_map/ppermute | solution.py:361
  17.9 0.6 collective-permute-start.6
  18.5 4.8 %collective-permute-done.2.refs_3_ = bf16[128,256]{1,0:T(8,128)(2,1)S(1)} collective-permute-done((bf16[128,256]{1,0:T(8,128)(2,1)S(1)}, bf16[128,256]{1,0:T(8,128)(2,1)S(1)}, u32[]{:S(2)}, u32[]{:S(2)}) %collective-permute-start.2) | collective-permute-done | bytes 65568 | tf_op jit(solution)/shard_map/ppermute | solution.py:361
  23.3 0.4 collective-permute-done.1.refs_2_
  23.7 2.3 %collective-permute-done.refs_1_ = bf16[128,768]{1,0:T(8,128)(2,1)S(1)} collective-permute-done((bf16[128,768]{1,0:T(8,128)(2,1)S(1)}, bf16[128,768]{1,0:T(8,128)(2,1)S(1)}, u32[]{:S(2)}, u32[]{:S(2)}) %collective-permute-start) | collective-permute-done | bytes 196640 | tf_op jit(solution)/shard_map/ppermute | solution.py:361
  25.9 0.0 all-to-all-done
  25.9 0.8 %shard_map.165 = (bf16[128,256]{1,0:T(8,128)(2,1)S(1)}, bf16[128,256]{1,0:T(8,128)(2,1)S(1)}, bf16[128,256]{1,0:T(8,128)(2,1)S(1)}, bf16[128,256]{1,0:T(8,128)(2,1)S(1)}, bf16[256,576]{1,0:T(8,128)(2,1)S(1)}) custom-call(bf16[256,1152]{1,0:T(8,128)(2,1)S(1)} %bitcast.5, bf16[128,256]{1,0:T(8,128)(2,1)S(1)} %bitcast.10, ...), custom_call_target="tpu_custom_call" | custom-call | flops 1006632960 | bytes 1540096 | tf_op jit(solution)/shard_map/pallas_call | solution.py:49
  26.7 1.8 %collective-permute-start.3 = (bf16[128,256]{1,0:T(8,128)(2,1)S(1)}, bf16[128,256]{1,0:T(8,128)(2,1)S(1)}, u32[]{:S(2)}, u32[]{:S(2)}) collective-permute-start(bf16[128,256]{1,0:T(8,128)(2,1)S(1)} %get-tuple-element.85), channel_id=1, source_target_pairs={{0,2},{1,3},{2,0},{3,1},{4,6},{5,7},{6,4},{7,5},{8,10},{9,11},{10,... | collective-permute-start | bytes 196616 | tf_op jit(solution)/shard_map/ppermute | solution.py:361
  28.6 1.1 %collective-permute-start.4 = (bf16[128,256]{1,0:T(8,128)(2,1)S(1)}, bf16[128,256]{1,0:T(8,128)(2,1)S(1)}, u32[]{:S(2)}, u32[]{:S(2)}) collective-permute-start(bf16[128,256]{1,0:T(8,128)(2,1)S(1)} %get-tuple-element.86), channel_id=1, source_target_pairs={{0,3},{1,2},{2,1},{3,0},{4,7},{5,6},{6,5},{7,4},{8,11},{9,10},{10,... | collective-permute-start | bytes 196616 | tf_op jit(solution)/shard_map/ppermute | solution.py:361
  29.7 0.6 collective-permute-start.5
  30.3 0.0 collective-permute-done.7.refs_3_
  30.3 2.5 %collective-permute-start.11 = (bf16[128,256]{1,0:T(8,128)(2,1)S(1)}, bf16[128,256]{1,0:T(8,128)(2,1)S(1)}, u32[]{:S(2)}, u32[]{:S(2)}) collective-permute-start(bf16[128,256]{1,0:T(8,128)(2,1)S(1)} %bitcast.11), channel_id=1, source_target_pairs={{0,4},{1,5},{2,6},{3,7},{4,0},{5,1},{6,2},{7,3},{8,12},{9,13},{10,... | collective-permute-start | bytes 196616 | tf_op jit(solution)/shard_map/ppermute | solution.py:361
  32.8 0.0 collective-permute-done.3.refs_1_
  32.8 1.9 %collective-permute-done.4.refs_2_ = bf16[128,256]{1,0:T(8,128)(2,1)S(1)} collective-permute-done((bf16[128,256]{1,0:T(8,128)(2,1)S(1)}, bf16[128,256]{1,0:T(8,128)(2,1)S(1)}, u32[]{:S(2)}, u32[]{:S(2)}) %collective-permute-start.4) | collective-permute-done | bytes 65568 | tf_op jit(solution)/shard_map/ppermute | solution.py:361
  34.8 0.1 collective-permute-done.5.refs_3_
  34.8 0.1 shard_map.166
  35.0 0.1 collective-permute-start.10
  35.1 1.6 %collective-permute-start.9 = (f32[2,128]{1,0:T(2,128)S(1)}, f32[2,128]{1,0:T(2,128)S(1)}, u32[]{:S(2)}, u32[]{:S(2)}) collective-permute-start(f32[2,128]{1,0:T(2,128)S(1)} %get-tuple-element.96.refs_0_), channel_id=1, source_target_pairs={{0,16},{8,24},{16,0},{24,8},{1,17},{9,25},{17,1},{25,9},{2,18},{10... | collective-permute-start | bytes 3080 | tf_op jit(solution)/shard_map/ppermute | solution.py:361
  36.7 0.3 collective-permute-start.8
  36.9 0.0 collective-permute-done.11.right
  36.9 1.1 %collective-permute-done.10.refs_3_ = f32[2,128]{1,0:T(2,128)S(1)} collective-permute-done((f32[2,128]{1,0:T(2,128)S(1)}, f32[2,128]{1,0:T(2,128)S(1)}, u32[]{:S(2)}, u32[]{:S(2)}) %collective-permute-start.10) | collective-permute-done | bytes 1056 | tf_op jit(solution)/shard_map/ppermute | solution.py:361
  38.1 0.7 collective-permute-done.9.refs_2_
  38.7 0.1 shard_map.167.refs_4_
  38.8 2.5 %collective-permute-start.15 = (bf16[128,256]{1,0:T(8,128)(2,1)S(1)}, bf16[128,256]{1,0:T(8,128)(2,1)S(1)}, u32[]{:S(2)}, u32[]{:S(2)}) collective-permute-start(bf16[128,256]{1,0:T(8,128)(2,1)S(1)} %shard_map.167.refs_4_), channel_id=1, source_target_pairs={{0,4},{1,5},{2,6},{3,7},{4,0},{5,1},{6,2},{7,3},{8,12},{9,13},{10,... | collective-permute-start | bytes 196616 | tf_op jit(solution)/shard_map/ppermute | solution.py:361
  41.3 0.9 %collective-permute-start.14 = (bf16[128,256]{1,0:T(8,128)(2,1)S(1)}, bf16[128,256]{1,0:T(8,128)(2,1)S(1)}, u32[]{:S(2)}, u32[]{:S(2)}) collective-permute-start(bf16[128,256]{1,0:T(8,128)(2,1)S(1)} %shard_map.167.refs_4_), channel_id=1, source_target_pairs={{0,3},{1,2},{2,1},{3,0},{4,7},{5,6},{6,5},{7,4},{8,11},{9,10},{10,... | collective-permute-start | bytes 196616 | tf_op jit(solution)/shard_map/ppermute | solution.py:361
  42.2 1.1 %collective-permute-start.13 = (bf16[128,256]{1,0:T(8,128)(2,1)S(1)}, bf16[128,256]{1,0:T(8,128)(2,1)S(1)}, u32[]{:S(2)}, u32[]{:S(2)}) collective-permute-start(bf16[128,256]{1,0:T(8,128)(2,1)S(1)} %shard_map.167.refs_4_), channel_id=1, source_target_pairs={{0,2},{1,3},{2,0},{3,1},{4,6},{5,7},{6,4},{7,5},{8,10},{9,11},{10,... | collective-permute-start | bytes 196616 | tf_op jit(solution)/shard_map/ppermute | solution.py:361
  43.3 1.5 %collective-permute-start.12 = (bf16[128,256]{1,0:T(8,128)(2,1)S(1)}, bf16[128,256]{1,0:T(8,128)(2,1)S(1)}, u32[]{:S(2)}, u32[]{:S(2)}) collective-permute-start(bf16[128,256]{1,0:T(8,128)(2,1)S(1)} %shard_map.167.refs_4_), channel_id=1, source_target_pairs={{0,1},{1,0},{2,3},{3,2},{4,5},{5,4},{6,7},{7,6},{8,9},{9,8},{10,11... | collective-permute-start | bytes 196616 | tf_op jit(solution)/shard_map/ppermute | solution.py:361
  44.8 0.1 pad_add_fusion.place
  44.9 1.1 %shard_map.169 = (f32[4,512,192]{2,1,0:T(8,128)S(1)}, bf16[3,512,192]{2,1,0:T(8,128)(2,1)S(1)}, f32[3,192]{1,0:T(4,128)S(1)}, f32[3,256,192]{2,1,0:T(8,128)S(1)}, f32[3,256,192]{2,1,0:T(8,128)S(1)}) custom-call(bf16[256,1152]{1,0:T(8,128)(2,1)S(1)} %bitcast.6, bf16[128,512]{1,0:T(8,128)(2,1)S(1)} %get-tuple-element.101.refs_0_, ...), custom_call_target="tpu_custom_call" | custom-call | flops 603979776 | bytes 4524288 | tf_op jit(solution)/shard_map/pallas_call | solution.py:49
  46.0 1.0 %collective-permute-start.18 = (bf16[128,512]{1,0:T(8,128)(2,1)S(1)}, bf16[128,512]{1,0:T(8,128)(2,1)S(1)}, u32[]{:S(2)}, u32[]{:S(2)}) collective-permute-start(bf16[128,512]{1,0:T(8,128)(2,1)S(1)} %shard_map.170.refs_4_), channel_id=1, source_target_pairs={{0,3},{1,2},{2,1},{3,0},{4,7},{5,6},{6,5},{7,4},{8,11},{9,10},{10,... | collective-permute-start | bytes 393224 | tf_op jit(solution)/shard_map/ppermute | solution.py:361
  47.0 1.1 %collective-permute-start.17 = (bf16[128,512]{1,0:T(8,128)(2,1)S(1)}, bf16[128,512]{1,0:T(8,128)(2,1)S(1)}, u32[]{:S(2)}, u32[]{:S(2)}) collective-permute-start(bf16[128,512]{1,0:T(8,128)(2,1)S(1)} %shard_map.170.refs_4_), channel_id=1, source_target_pairs={{0,2},{1,3},{2,0},{3,1},{4,6},{5,7},{6,4},{7,5},{8,10},{9,11},{10,... | collective-permute-start | bytes 393224 | tf_op jit(solution)/shard_map/ppermute | solution.py:361
  48.1 0.0 collective-permute-done.14.refs_7_
  48.1 1.5 %collective-permute-start.16 = (bf16[128,512]{1,0:T(8,128)(2,1)S(1)}, bf16[128,512]{1,0:T(8,128)(2,1)S(1)}, u32[]{:S(2)}, u32[]{:S(2)}) collective-permute-start(bf16[128,512]{1,0:T(8,128)(2,1)S(1)} %shard_map.170.refs_4_), channel_id=1, source_target_pairs={{0,1},{1,0},{2,3},{3,2},{4,5},{5,4},{6,7},{7,6},{8,9},{9,8},{10,11... | collective-permute-start | bytes 393224 | tf_op jit(solution)/shard_map/ppermute | solution.py:361
  49.6 0.8 %shard_map.168 = (bf16[128,256]{1,0:T(8,128)(2,1)S(1)}, bf16[128,256]{1,0:T(8,128)(2,1)S(1)}, bf16[128,256]{1,0:T(8,128)(2,1)S(1)}, bf16[128,256]{1,0:T(8,128)(2,1)S(1)}, f32[3,256,192]{2,1,0:T(8,128)S(1)}) custom-call(bf16[256,576]{1,0:T(8,128)(2,1)S(1)} %get-tuple-element.78.normed_ref, bf16[128,256]{1,0:T(8,128)(2,1)S(1)} %bitcast.12, ...), custom_call_target="tpu_custom_call" | custom-call | flops 3019898880 | bytes 1802240 | tf_op jit(solution)/shard_map/pallas_call | solution.py:49
  50.4 0.4 collective-permute-start.19
  50.8 1.7 %collective-permute-start.20 = (bf16[128,256]{1,0:T(8,128)(2,1)S(1)}, bf16[128,256]{1,0:T(8,128)(2,1)S(1)}, u32[]{:S(2)}, u32[]{:S(2)}) collective-permute-start(bf16[128,256]{1,0:T(8,128)(2,1)S(1)} %get-tuple-element.120), channel_id=1, source_target_pairs={{0,3},{1,2},{2,1},{3,0},{4,7},{5,6},{6,5},{7,4},{8,11},{9,10},{10,... | collective-permute-start | bytes 196616 | tf_op jit(solution)/shard_map/ppermute | solution.py:361
  52.5 1.0 %collective-permute-done.18.refs_7_ = bf16[128,512]{1,0:T(8,128)(2,1)S(1)} collective-permute-done((bf16[128,512]{1,0:T(8,128)(2,1)S(1)}, bf16[128,512]{1,0:T(8,128)(2,1)S(1)}, u32[]{:S(2)}, u32[]{:S(2)}) %collective-permute-start.18) | collective-permute-done | bytes 131104 | tf_op jit(solution)/shard_map/ppermute | solution.py:361
  53.4 0.5 collective-permute-start.21
  54.0 1.2 %collective-permute-done.17.refs_6_ = bf16[128,512]{1,0:T(8,128)(2,1)S(1)} collective-permute-done((bf16[128,512]{1,0:T(8,128)(2,1)S(1)}, bf16[128,512]{1,0:T(8,128)(2,1)S(1)}, u32[]{:S(2)}, u32[]{:S(2)}) %collective-permute-start.17) | collective-permute-done | bytes 131104 | tf_op jit(solution)/shard_map/ppermute | solution.py:361
  55.2 0.8 %collective-permute-done.16.refs_5_ = bf16[128,512]{1,0:T(8,128)(2,1)S(1)} collective-permute-done((bf16[128,512]{1,0:T(8,128)(2,1)S(1)}, bf16[128,512]{1,0:T(8,128)(2,1)S(1)}, u32[]{:S(2)}, u32[]{:S(2)}) %collective-permute-start.16) | collective-permute-done | bytes 131104 | tf_op jit(solution)/shard_map/ppermute | solution.py:361
  56.1 2.6 %shard_map.171 = (bf16[128,512]{1,0:T(8,128)(2,1)S(1)}, bf16[32,576]{1,0:T(8,128)(2,1)S(1)}, bf16[672,128]{1,0:T(8,128)(2,1)S(1)}, bf16[672,128]{1,0:T(8,128)(2,...) custom-call(s32[3]{0:T(128)S(1)} %pad_add_fusion.place, ...), custom_call_target="tpu_custom_call" | custom-call | flops 6039797760 | bytes 6764812 | tf_op jit(solution)/shard_map/pallas_call | solution.py:49
  58.6 0.9 %collective-permute-start.22 = (bf16[64,576]{1,0:T(8,128)(2,1)S(1)}, bf16[64,576]{1,0:T(8,128)(2,1)S(1)}, u32[]{:S(2)}, u32[]{:S(2)}) collective-permute-start(bf16[64,576]{1,0:T(8,128)(2,1)S(1)} %get-tuple-element.122), channel_id=1, source_target_pairs={{0,4},{1,5},{2,6},{3,7},{4,0},{5,1},{6,2},{7,3},{8,12},{9,13},{10,... | collective-permute-start | bytes 221192 | tf_op jit(solution)/shard_map/ppermute | solution.py:361
  59.5 1.6 %collective-permute-start.23 = (bf16[64,576]{1,0:T(8,128)(2,1)S(1)}, bf16[64,576]{1,0:T(8,128)(2,1)S(1)}, u32[]{:S(2)}, u32[]{:S(2)}) collective-permute-start(bf16[64,576]{1,0:T(8,128)(2,1)S(1)} %get-tuple-element.123), channel_id=1, source_target_pairs={{0,6},{1,7},{2,4},{3,5},{4,2},{5,3},{6,0},{7,1},{8,14},{9,15},{10,... | collective-permute-start | bytes 221192 | tf_op jit(solution)/shard_map/ppermute | solution.py:361
  61.1 1.3 %collective-permute-start.25 = (bf16[672,128]{1,0:T(8,128)(2,1)S(1)}, bf16[672,128]{1,0:T(8,128)(2,1)S(1)}, u32[]{:S(2)}, u32[]{:S(2)}) collective-permute-start(bf16[672,128]{1,0:T(8,128)(2,1)S(1)} %get-tuple-element.130), channel_id=1, source_target_pairs={{0,1},{1,0},{2,3},{3,2},{4,5},{5,4},{6,7},{7,6},{8,9},{9,8},{10,11... | collective-permute-start | bytes 516104 | tf_op jit(solution)/shard_map/ppermute | solution.py:361
  62.4 0.3 collective-permute-start.26
  62.8 1.9 %collective-permute-start.27 = (bf16[672,128]{1,0:T(8,128)(2,1)S(1)}, bf16[672,128]{1,0:T(8,128)(2,1)S(1)}, u32[]{:S(2)}, u32[]{:S(2)}) collective-permute-start(bf16[672,128]{1,0:T(8,128)(2,1)S(1)} %get-tuple-element.132), channel_id=1, source_target_pairs={{0,3},{1,2},{2,1},{3,0},{4,7},{5,6},{6,5},{7,4},{8,11},{9,10},{10,... | collective-permute-start | bytes 516104 | tf_op jit(solution)/shard_map/ppermute | solution.py:361
  64.6 0.1 collective-permute-done.22.refs_0_.refs_3_
  64.7 2.0 %collective-permute-done.23.refs_1_.refs_4_ = bf16[64,576]{1,0:T(8,128)(2,1)S(1)} collective-permute-done((bf16[64,576]{1,0:T(8,128)(2,1)S(1)}, bf16[64,576]{1,0:T(8,128)(2,1)S(1)}, u32[]{:S(2)}, u32[]{:S(2)}) %collective-permute-start.23) | collective-permute-done | bytes 73760 | tf_op jit(solution)/shard_map/ppermute | solution.py:361
  66.7 0.8 %collective-permute-start.24 = (bf16[64,576]{1,0:T(8,128)(2,1)S(1)}, bf16[64,576]{1,0:T(8,128)(2,1)S(1)}, u32[]{:S(2)}, u32[]{:S(2)}) collective-permute-start(bf16[64,576]{1,0:T(8,128)(2,1)S(1)} %shard_map.172), channel_id=1, source_target_pairs={{0,1},{1,0},{2,3},{3,2},{4,5},{5,4},{6,7},{7,6},{8,9},{9,8},{10,11... | collective-permute-start | bytes 221192 | tf_op jit(solution)/shard_map/ppermute | solution.py:361
  67.6 1.7 %collective-permute-done.25.refs_4_.refs_0_ = bf16[672,128]{1,0:T(8,128)(2,1)S(1)} collective-permute-done((bf16[672,128]{1,0:T(8,128)(2,1)S(1)}, bf16[672,128]{1,0:T(8,128)(2,1)S(1)}, u32[]{:S(2)}, u32[]{:S(2)}) %collective-permute-start.25) | collective-permute-done | bytes 172064 | tf_op jit(solution)/shard_map/ppermute | solution.py:361
  69.2 0.2 collective-permute-done.26.refs_5_.refs_1_
  69.5 2.2 %collective-permute-done.27.refs_6_.refs_2_ = bf16[672,128]{1,0:T(8,128)(2,1)S(1)} collective-permute-done((bf16[672,128]{1,0:T(8,128)(2,1)S(1)}, bf16[672,128]{1,0:T(8,128)(2,1)S(1)}, u32[]{:S(2)}, u32[]{:S(2)}) %collective-permute-start.27) | collective-permute-done | bytes 172064 | tf_op jit(solution)/shard_map/ppermute | solution.py:361
  71.7 0.7 %shard_map.173 = (bf16[1,128,256]{2,1,0:T(8,128)(2,1)}, bf16[1,128,256]{2,1,0:T(8,128)(2,1)}, bf16[1,128,256]{2,1,0:T(8,128)(2,1)}) custom-call(f32[128,256]{1,0:T(8,128)S(1)} %get-tuple-element.124.rate, bf16[128,512]{1,0:T(8,128)(2,1)S(1)} %get-tuple-element.125.tok, bf16[128,256]{1,0:T(8,128)(2,1)S(1)} %get-tuple-element.126.refs_0_, ...), custom_call_target="tpu_custom_call" | custom-call | bytes 1236992 | tf_op jit(solution)/shard_map/pallas_call | solution.py:49
  72.4 0.0 collective-permute-done.24.relayed
  72.5 1.4 %shard_map.174 = (f32[1,32,768]{2,1,0:T(8,128)}, f32[1,32,768]{2,1,0:T(8,128)}, f32[1,32,768]{2,1,0:T(8,128)}) custom-call(s32[3]{0:T(128)S(1)} %pad_add_fusion.place, bf16[64,576]{1,0:T(8,128)(2,1)S(1)} %collective-permute-done.24.relayed, bf16[32,576]{1,0:T(8,128)(2,1)S(1)} %get-tuple-element.140.inner, ...), custom_call_target="tpu_custom_call" | custom-call | bytes 1069068 | tf_op jit(solution)/shard_map/pallas_call | solution.py:49
  (19 shorter events, 0.1 us)
Async XLA Ops:
  0.6 9.3 %copy-start.3 = (bf16[1,128,256]{2,1,0:T(8,128)(2,1)S(1)}, bf16[1,128,256]{2,1,0:T(8,128)(2,1)}, u32[]{:S(2)}) copy-start(bf16[1,128,256]{2,1,0:T(8,128)(2,1)} %q.1) | copy-start | bytes 196612
  0.6 9.3 %copy-start.2 = (bf16[1,128,256]{2,1,0:T(8,128)(2,1)S(1)}, bf16[1,128,256]{2,1,0:T(8,128)(2,1)}, u32[]{:S(2)}) copy-start(bf16[1,128,256]{2,1,0:T(8,128)(2,1)} %og.1) | copy-start | bytes 196612
  0.7 9.3 %copy-start.1 = (bf16[1,128,256]{2,1,0:T(8,128)(2,1)S(1)}, bf16[1,128,256]{2,1,0:T(8,128)(2,1)}, u32[]{:S(2)}) copy-start(bf16[1,128,256]{2,1,0:T(8,128)(2,1)} %v.1) | copy-start | bytes 196612
  0.7 9.3 %copy-start = (bf16[1,128,256]{2,1,0:T(8,128)(2,1)S(1)}, bf16[1,128,256]{2,1,0:T(8,128)(2,1)}, u32[]{:S(2)}) copy-start(bf16[1,128,256]{2,1,0:T(8,128)(2,1)} %k.1) | copy-start | bytes 196612
  2.7 23.3 %all-to-all-start = ((bf16[8,32,1152]{2,1,0:T(8,128)(2,1)}), bf16[8,32,1152]{2,1,0:T(8,128)(2,1)S(1)}, u32[]{:S(2)}, u32[]{:S(2)}) async-start(bf16[8,32,1152]{2,1,0:T(8,128)(2,1)} %shard_map.163), calls=%async_computation | async-start | bytes 1179648 | tf_op jit(solution)/shard_map/all_to_all | solution.py:380
  10.0 0.7 copy-start.4
  10.7 0.7 copy-start.5
  11.4 14.5 %collective-permute-start = (bf16[128,768]{1,0:T(8,128)(2,1)S(1)}, bf16[128,768]{1,0:T(8,128)(2,1)S(1)}, u32[]{:S(2)}, u32[]{:S(2)}) collective-permute-start(bf16[128,768]{1,0:T(8,128)(2,1)S(1)} %get-tuple-element.77), channel_id=1, source_target_pairs={{0,1},{1,0},{2,3},{3,2},{4,5},{5,4},{6,7},{7,6},{8,9},{9,8},{10,11... | collective-permute-start | bytes 589832 | tf_op jit(solution)/shard_map/ppermute | solution.py:361
  13.5 9.8 %collective-permute-start.2 = (bf16[128,256]{1,0:T(8,128)(2,1)S(1)}, bf16[128,256]{1,0:T(8,128)(2,1)S(1)}, u32[]{:S(2)}, u32[]{:S(2)}) collective-permute-start(bf16[128,256]{1,0:T(8,128)(2,1)S(1)} %bitcast.8), channel_id=1, source_target_pairs={{0,3},{1,2},{2,1},{3,0},{4,7},{5,6},{6,5},{7,4},{8,11},{9,10},{10,... | collective-permute-start | bytes 196616 | tf_op jit(solution)/shard_map/ppermute | solution.py:361
  15.0 8.7 %collective-permute-start.1 = (bf16[128,256]{1,0:T(8,128)(2,1)S(1)}, bf16[128,256]{1,0:T(8,128)(2,1)S(1)}, u32[]{:S(2)}, u32[]{:S(2)}) collective-permute-start(bf16[128,256]{1,0:T(8,128)(2,1)S(1)} %bitcast.9), channel_id=1, source_target_pairs={{0,2},{1,3},{2,0},{3,1},{4,6},{5,7},{6,4},{7,5},{8,10},{9,11},{10,... | collective-permute-start | bytes 196616 | tf_op jit(solution)/shard_map/ppermute | solution.py:361
  15.0 15.2 %collective-permute-start.7 = (bf16[128,512]{1,0:T(8,128)(2,1)S(1)}, bf16[128,512]{1,0:T(8,128)(2,1)S(1)}, u32[]{:S(2)}, u32[]{:S(2)}) collective-permute-start(bf16[128,512]{1,0:T(8,128)(2,1)S(1)} %get-tuple-element.101.refs_0_), channel_id=1, source_target_pairs={{0,3},{1,2},{2,1},{3,0},{4,7},{5,6},{6,5},{7,4},{8,11},{9,10},{10,... | collective-permute-start | bytes 393224 | tf_op jit(solution)/shard_map/ppermute | solution.py:361
  17.9 14.9 %collective-permute-start.6 = (bf16[128,512]{1,0:T(8,128)(2,1)S(1)}, bf16[128,512]{1,0:T(8,128)(2,1)S(1)}, u32[]{:S(2)}, u32[]{:S(2)}) collective-permute-start(bf16[128,512]{1,0:T(8,128)(2,1)S(1)} %get-tuple-element.101.refs_0_), channel_id=1, source_target_pairs={{0,2},{1,3},{2,0},{3,1},{4,6},{5,7},{6,4},{7,5},{8,10},{9,11},{10,... | collective-permute-start | bytes 393224 | tf_op jit(solution)/shard_map/ppermute | solution.py:361
  26.7 6.1 %collective-permute-start.3 = (bf16[128,256]{1,0:T(8,128)(2,1)S(1)}, bf16[128,256]{1,0:T(8,128)(2,1)S(1)}, u32[]{:S(2)}, u32[]{:S(2)}) collective-permute-start(bf16[128,256]{1,0:T(8,128)(2,1)S(1)} %get-tuple-element.85), channel_id=1, source_target_pairs={{0,2},{1,3},{2,0},{3,1},{4,6},{5,7},{6,4},{7,5},{8,10},{9,11},{10,... | collective-permute-start | bytes 196616 | tf_op jit(solution)/shard_map/ppermute | solution.py:361
  28.6 6.2 %collective-permute-start.4 = (bf16[128,256]{1,0:T(8,128)(2,1)S(1)}, bf16[128,256]{1,0:T(8,128)(2,1)S(1)}, u32[]{:S(2)}, u32[]{:S(2)}) collective-permute-start(bf16[128,256]{1,0:T(8,128)(2,1)S(1)} %get-tuple-element.86), channel_id=1, source_target_pairs={{0,3},{1,2},{2,1},{3,0},{4,7},{5,6},{6,5},{7,4},{8,11},{9,10},{10,... | collective-permute-start | bytes 196616 | tf_op jit(solution)/shard_map/ppermute | solution.py:361
  29.7 5.1 %collective-permute-start.5 = (bf16[128,256]{1,0:T(8,128)(2,1)S(1)}, bf16[128,256]{1,0:T(8,128)(2,1)S(1)}, u32[]{:S(2)}, u32[]{:S(2)}) collective-permute-start(bf16[128,256]{1,0:T(8,128)(2,1)S(1)} %get-tuple-element.87), channel_id=1, source_target_pairs={{0,1},{1,0},{2,3},{3,2},{4,5},{5,4},{6,7},{7,6},{8,9},{9,8},{10,11... | collective-permute-start | bytes 196616 | tf_op jit(solution)/shard_map/ppermute | solution.py:361
  30.3 6.6 %collective-permute-start.11 = (bf16[128,256]{1,0:T(8,128)(2,1)S(1)}, bf16[128,256]{1,0:T(8,128)(2,1)S(1)}, u32[]{:S(2)}, u32[]{:S(2)}) collective-permute-start(bf16[128,256]{1,0:T(8,128)(2,1)S(1)} %bitcast.11), channel_id=1, source_target_pairs={{0,4},{1,5},{2,6},{3,7},{4,0},{5,1},{6,2},{7,3},{8,12},{9,13},{10,... | collective-permute-start | bytes 196616 | tf_op jit(solution)/shard_map/ppermute | solution.py:361
  35.0 3.1 %collective-permute-start.10 = (f32[2,128]{1,0:T(2,128)S(1)}, f32[2,128]{1,0:T(2,128)S(1)}, u32[]{:S(2)}, u32[]{:S(2)}) collective-permute-start(f32[2,128]{1,0:T(2,128)S(1)} %get-tuple-element.96.refs_0_), channel_id=1, source_target_pairs={{0,24},{8,16},{16,8},{24,0},{1,25},{9,17},{17,9},{25,1},{2,26},{10... | collective-permute-start | bytes 3080 | tf_op jit(solution)/shard_map/ppermute | solution.py:361
  35.1 3.6 %collective-permute-start.9 = (f32[2,128]{1,0:T(2,128)S(1)}, f32[2,128]{1,0:T(2,128)S(1)}, u32[]{:S(2)}, u32[]{:S(2)}) collective-permute-start(f32[2,128]{1,0:T(2,128)S(1)} %get-tuple-element.96.refs_0_), channel_id=1, source_target_pairs={{0,16},{8,24},{16,0},{24,8},{1,17},{9,25},{17,1},{25,9},{2,18},{10... | collective-permute-start | bytes 3080 | tf_op jit(solution)/shard_map/ppermute | solution.py:361
  36.7 2.1 %collective-permute-start.8 = (f32[2,128]{1,0:T(2,128)S(1)}, f32[2,128]{1,0:T(2,128)S(1)}, u32[]{:S(2)}, u32[]{:S(2)}) collective-permute-start(f32[2,128]{1,0:T(2,128)S(1)} %get-tuple-element.96.refs_0_), channel_id=1, source_target_pairs={{0,8},{8,0},{16,24},{24,16},{1,9},{9,1},{17,25},{25,17},{2,10},{10... | collective-permute-start | bytes 3080 | tf_op jit(solution)/shard_map/ppermute | solution.py:361
  38.8 7.2 %collective-permute-start.15 = (bf16[128,256]{1,0:T(8,128)(2,1)S(1)}, bf16[128,256]{1,0:T(8,128)(2,1)S(1)}, u32[]{:S(2)}, u32[]{:S(2)}) collective-permute-start(bf16[128,256]{1,0:T(8,128)(2,1)S(1)} %shard_map.167.refs_4_), channel_id=1, source_target_pairs={{0,4},{1,5},{2,6},{3,7},{4,0},{5,1},{6,2},{7,3},{8,12},{9,13},{10,... | collective-permute-start | bytes 196616 | tf_op jit(solution)/shard_map/ppermute | solution.py:361
  41.3 6.8 %collective-permute-start.14 = (bf16[128,256]{1,0:T(8,128)(2,1)S(1)}, bf16[128,256]{1,0:T(8,128)(2,1)S(1)}, u32[]{:S(2)}, u32[]{:S(2)}) collective-permute-start(bf16[128,256]{1,0:T(8,128)(2,1)S(1)} %shard_map.167.refs_4_), channel_id=1, source_target_pairs={{0,3},{1,2},{2,1},{3,0},{4,7},{5,6},{6,5},{7,4},{8,11},{9,10},{10,... | collective-permute-start | bytes 196616 | tf_op jit(solution)/shard_map/ppermute | solution.py:361
  42.2 7.4 %collective-permute-start.13 = (bf16[128,256]{1,0:T(8,128)(2,1)S(1)}, bf16[128,256]{1,0:T(8,128)(2,1)S(1)}, u32[]{:S(2)}, u32[]{:S(2)}) collective-permute-start(bf16[128,256]{1,0:T(8,128)(2,1)S(1)} %shard_map.167.refs_4_), channel_id=1, source_target_pairs={{0,2},{1,3},{2,0},{3,1},{4,6},{5,7},{6,4},{7,5},{8,10},{9,11},{10,... | collective-permute-start | bytes 196616 | tf_op jit(solution)/shard_map/ppermute | solution.py:361
  43.3 6.3 %collective-permute-start.12 = (bf16[128,256]{1,0:T(8,128)(2,1)S(1)}, bf16[128,256]{1,0:T(8,128)(2,1)S(1)}, u32[]{:S(2)}, u32[]{:S(2)}) collective-permute-start(bf16[128,256]{1,0:T(8,128)(2,1)S(1)} %shard_map.167.refs_4_), channel_id=1, source_target_pairs={{0,1},{1,0},{2,3},{3,2},{4,5},{5,4},{6,7},{7,6},{8,9},{9,8},{10,11... | collective-permute-start | bytes 196616 | tf_op jit(solution)/shard_map/ppermute | solution.py:361
  46.0 7.4 %collective-permute-start.18 = (bf16[128,512]{1,0:T(8,128)(2,1)S(1)}, bf16[128,512]{1,0:T(8,128)(2,1)S(1)}, u32[]{:S(2)}, u32[]{:S(2)}) collective-permute-start(bf16[128,512]{1,0:T(8,128)(2,1)S(1)} %shard_map.170.refs_4_), channel_id=1, source_target_pairs={{0,3},{1,2},{2,1},{3,0},{4,7},{5,6},{6,5},{7,4},{8,11},{9,10},{10,... | collective-permute-start | bytes 393224 | tf_op jit(solution)/shard_map/ppermute | solution.py:361
  47.0 8.2 %collective-permute-start.17 = (bf16[128,512]{1,0:T(8,128)(2,1)S(1)}, bf16[128,512]{1,0:T(8,128)(2,1)S(1)}, u32[]{:S(2)}, u32[]{:S(2)}) collective-permute-start(bf16[128,512]{1,0:T(8,128)(2,1)S(1)} %shard_map.170.refs_4_), channel_id=1, source_target_pairs={{0,2},{1,3},{2,0},{3,1},{4,6},{5,7},{6,4},{7,5},{8,10},{9,11},{10,... | collective-permute-start | bytes 393224 | tf_op jit(solution)/shard_map/ppermute | solution.py:361
  48.1 8.0 %collective-permute-start.16 = (bf16[128,512]{1,0:T(8,128)(2,1)S(1)}, bf16[128,512]{1,0:T(8,128)(2,1)S(1)}, u32[]{:S(2)}, u32[]{:S(2)}) collective-permute-start(bf16[128,512]{1,0:T(8,128)(2,1)S(1)} %shard_map.170.refs_4_), channel_id=1, source_target_pairs={{0,1},{1,0},{2,3},{3,2},{4,5},{5,4},{6,7},{7,6},{8,9},{9,8},{10,11... | collective-permute-start | bytes 393224 | tf_op jit(solution)/shard_map/ppermute | solution.py:361
  50.4 8.2 %collective-permute-start.19 = (bf16[128,256]{1,0:T(8,128)(2,1)S(1)}, bf16[128,256]{1,0:T(8,128)(2,1)S(1)}, u32[]{:S(2)}, u32[]{:S(2)}) collective-permute-start(bf16[128,256]{1,0:T(8,128)(2,1)S(1)} %get-tuple-element.119), channel_id=1, source_target_pairs={{0,2},{1,3},{2,0},{3,1},{4,6},{5,7},{6,4},{7,5},{8,10},{9,11},{10,... | collective-permute-start | bytes 196616 | tf_op jit(solution)/shard_map/ppermute | solution.py:361
  50.8 7.8 %collective-permute-start.20 = (bf16[128,256]{1,0:T(8,128)(2,1)S(1)}, bf16[128,256]{1,0:T(8,128)(2,1)S(1)}, u32[]{:S(2)}, u32[]{:S(2)}) collective-permute-start(bf16[128,256]{1,0:T(8,128)(2,1)S(1)} %get-tuple-element.120), channel_id=1, source_target_pairs={{0,3},{1,2},{2,1},{3,0},{4,7},{5,6},{6,5},{7,4},{8,11},{9,10},{10,... | collective-permute-start | bytes 196616 | tf_op jit(solution)/shard_map/ppermute | solution.py:361
  53.4 5.2 %collective-permute-start.21 = (bf16[128,256]{1,0:T(8,128)(2,1)S(1)}, bf16[128,256]{1,0:T(8,128)(2,1)S(1)}, u32[]{:S(2)}, u32[]{:S(2)}) collective-permute-start(bf16[128,256]{1,0:T(8,128)(2,1)S(1)} %get-tuple-element.121), channel_id=1, source_target_pairs={{0,1},{1,0},{2,3},{3,2},{4,5},{5,4},{6,7},{7,6},{8,9},{9,8},{10,11... | collective-permute-start | bytes 196616 | tf_op jit(solution)/shard_map/ppermute | solution.py:361
  58.6 6.1 %collective-permute-start.22 = (bf16[64,576]{1,0:T(8,128)(2,1)S(1)}, bf16[64,576]{1,0:T(8,128)(2,1)S(1)}, u32[]{:S(2)}, u32[]{:S(2)}) collective-permute-start(bf16[64,576]{1,0:T(8,128)(2,1)S(1)} %get-tuple-element.122), channel_id=1, source_target_pairs={{0,4},{1,5},{2,6},{3,7},{4,0},{5,1},{6,2},{7,3},{8,12},{9,13},{10,... | collective-permute-start | bytes 221192 | tf_op jit(solution)/shard_map/ppermute | solution.py:361
  59.5 7.2 %collective-permute-start.23 = (bf16[64,576]{1,0:T(8,128)(2,1)S(1)}, bf16[64,576]{1,0:T(8,128)(2,1)S(1)}, u32[]{:S(2)}, u32[]{:S(2)}) collective-permute-start(bf16[64,576]{1,0:T(8,128)(2,1)S(1)} %get-tuple-element.123), channel_id=1, source_target_pairs={{0,6},{1,7},{2,4},{3,5},{4,2},{5,3},{6,0},{7,1},{8,14},{9,15},{10,... | collective-permute-start | bytes 221192 | tf_op jit(solution)/shard_map/ppermute | solution.py:361
  61.1 8.1 %collective-permute-start.25 = (bf16[672,128]{1,0:T(8,128)(2,1)S(1)}, bf16[672,128]{1,0:T(8,128)(2,1)S(1)}, u32[]{:S(2)}, u32[]{:S(2)}) collective-permute-start(bf16[672,128]{1,0:T(8,128)(2,1)S(1)} %get-tuple-element.130), channel_id=1, source_target_pairs={{0,1},{1,0},{2,3},{3,2},{4,5},{5,4},{6,7},{7,6},{8,9},{9,8},{10,11... | collective-permute-start | bytes 516104 | tf_op jit(solution)/shard_map/ppermute | solution.py:361
  62.4 7.0 %collective-permute-start.26 = (bf16[672,128]{1,0:T(8,128)(2,1)S(1)}, bf16[672,128]{1,0:T(8,128)(2,1)S(1)}, u32[]{:S(2)}, u32[]{:S(2)}) collective-permute-start(bf16[672,128]{1,0:T(8,128)(2,1)S(1)} %get-tuple-element.131), channel_id=1, source_target_pairs={{0,2},{1,3},{2,0},{3,1},{4,6},{5,7},{6,4},{7,5},{8,10},{9,11},{10,... | collective-permute-start | bytes 516104 | tf_op jit(solution)/shard_map/ppermute | solution.py:361
  62.8 8.9 %collective-permute-start.27 = (bf16[672,128]{1,0:T(8,128)(2,1)S(1)}, bf16[672,128]{1,0:T(8,128)(2,1)S(1)}, u32[]{:S(2)}, u32[]{:S(2)}) collective-permute-start(bf16[672,128]{1,0:T(8,128)(2,1)S(1)} %get-tuple-element.132), channel_id=1, source_target_pairs={{0,3},{1,2},{2,1},{3,0},{4,7},{5,6},{6,5},{7,4},{8,11},{9,10},{10,... | collective-permute-start | bytes 516104 | tf_op jit(solution)/shard_map/ppermute | solution.py:361
  66.7 5.7 %collective-permute-start.24 = (bf16[64,576]{1,0:T(8,128)(2,1)S(1)}, bf16[64,576]{1,0:T(8,128)(2,1)S(1)}, u32[]{:S(2)}, u32[]{:S(2)}) collective-permute-start(bf16[64,576]{1,0:T(8,128)(2,1)S(1)} %shard_map.172), channel_id=1, source_target_pairs={{0,1},{1,0},{2,3},{3,2},{4,5},{5,4},{6,7},{7,6},{8,9},{9,8},{10,11... | collective-permute-start | bytes 221192 | tf_op jit(solution)/shard_map/ppermute | solution.py:361

commit v19 on v17

--- a/solution.py
+++ b/solution.py
@@ -392,7 +392,7 @@
             flops=20 * mflop,
         )
         *parts, queries = lax.optimization_barrier((*parts, queries))
-        parts = [parts[0]] + [move(parts[d], d) for d in (*range(2, group), *range(1, min(2, group)))]
+        parts = [parts[0]] + [move(parts[d], d) for d in range(group - 1, 0, -1)]
         q_mirror = mirror(queries)
         *parts, kv_near = lax.optimization_barrier((*parts, kv_near))
         apply_out, sums = call(
@@ -425,7 +425,7 @@
         )
 
         q_block = (own, feat)
-        grad_q = [grad_q[0]] + [move(grad_q[d], d) for d in (*range(2, group), *range(1, min(2, group)))]
+        grad_q = [grad_q[0]] + [move(grad_q[d], d) for d in range(group - 1, 0, -1)]
         far = far_distances(group, tok_groups)
         tok, inner, *sends = call(
             functools.partial(backward_kernel, slab, group, tok_groups),
@@ -445,7 +445,7 @@
             ],
         )
         sends, grad_q = lax.optimization_barrier((sends, grad_q))
-        near_got = {d: move(sends[d - 1], d) for d in (*range(2, group), *range(1, min(2, group)))}
+        near_got = {d: move(sends[d - 1], d) for d in range(group - 1, 0, -1)}
         near_got = [near_got[d] for d in range(1, group)]
         far_got = [move(x, d) for x, d in zip(sends[group - 1 :], far)]
         (relayed,) = call(

time: 74.1 us -> 74.1 us (level)
  no operation moved by 1% of the time
where the time goes in v19:
time: 74.1 us; the launch traced here: 73.9 us
  starting transfers between devices  41.8 us (56%)
  waiting for transfers between devices  20 us (27%)
  Pallas kernels  9.76 us (13%)
  local copies, waits for them, and re-layouts  1.35 us (2%)
  between operations  0.84 us (1%)
    ppermute x28, starting transfers between devices, move(): return lax.ppermute(x, axis, [(i, i ^ dist) for i in range(size)])  34.6 us
    ppermute x28, waiting for transfers between devices, move(): return lax.ppermute(x, axis, [(i, i ^ dist) for i in range(size)])  20 us
    pallas_call x11, Pallas kernels, call(): pl.pallas_call(kernel, out_shape=outs, in_specs=[SMEM] * smem + [VMEM] *...  7.8 us
    all_to_all x1, starting transfers between devices, local(): lax.all_to_all(packed, 'seq', 0, 0, tiled=True)  7.26 us
    pallas_call x1, Pallas kernels, copying_call(): pl.pallas_call(kernel, out_shape=outs, in_specs=[pl.BlockSpec(memory_spac...  1.96 us
  transfers between devices with their start and end apart: 29, of which 15 were waited for; matrix products, arithmetic and copies ran while one was open for 0% of the time, Pallas kernels for 9%

profile of v19, /device:TPU:0, one launch (start us, length us, event | category | flops | bytes accessed | tf_op | source)
XLA Modules:
  0.0 73.9 jit_solution(3813583839418598680)
XLA Ops:
  0.7 2.0 %shard_map.163 = bf16[8,32,1152]{2,1,0:T(8,128)(2,1)} custom-call(bf16[1,32,768]{2,1,0:T(8,128)(2,1)} %refs_0_.1, bf16[1,32,768]{2,1,0:T(8,128)(2,1)} %refs_1_.1, bf16[1,32,768]{2,1,0:T(8,128)(2,1)} %refs_2_.1, bf16[1,32,768]{2,1,0:T(8,128)(2,1)} %refs_3_.1, bf16[1,32,768]{2,1,0:T(8,128)(2,1)} %refs_4_.1, bf16[1,32,768]{2,1,0:T(8,128)(2,1)} %refs_5_.1), custom_call_target="tpu_custom_call" | custom-call | tf_op jit(solution)/shard_map/pallas_call | solution.py:61
  2.6 7.3 %all-to-all-start = ((bf16[8,32,1152]{2,1,0:T(8,128)(2,1)}), bf16[8,32,1152]{2,1,0:T(8,128)(2,1)S(1)}, u32[]{:S(2)}, u32[]{:S(2)}) async-start(bf16[8,32,1152]{2,1,0:T(8,128)(2,1)} %shard_map.163), calls=%async_computation | async-start | bytes 1179648 | tf_op jit(solution)/shard_map/all_to_all | solution.py:373
  9.9 0.0 copy-start.4
  10.0 0.7 copy-done.4
  10.6 0.7 copy-done.5
  11.3 0.1 shard_map.164
  11.4 2.1 %collective-permute-start = (bf16[128,768]{1,0:T(8,128)(2,1)S(1)}, bf16[128,768]{1,0:T(8,128)(2,1)S(1)}, u32[]{:S(2)}, u32[]{:S(2)}) collective-permute-start(bf16[128,768]{1,0:T(8,128)(2,1)S(1)} %get-tuple-element.77), channel_id=1, source_target_pairs={{0,1},{1,0},{2,3},{3,2},{4,5},{5,4},{6,7},{7,6},{8,9},{9,8},{10,11... | collective-permute-start | bytes 589832 | tf_op jit(solution)/shard_map/ppermute | solution.py:350
  13.5 1.5 %collective-permute-start.2 = (bf16[128,256]{1,0:T(8,128)(2,1)S(1)}, bf16[128,256]{1,0:T(8,128)(2,1)S(1)}, u32[]{:S(2)}, u32[]{:S(2)}) collective-permute-start(bf16[128,256]{1,0:T(8,128)(2,1)S(1)} %bitcast.8), channel_id=1, source_target_pairs={{0,3},{1,2},{2,1},{3,0},{4,7},{5,6},{6,5},{7,4},{8,11},{9,10},{10,... | collective-permute-start | bytes 196616 | tf_op jit(solution)/shard_map/ppermute | solution.py:350
  14.9 0.1 collective-permute-start.1
  15.0 2.8 %collective-permute-start.7 = (bf16[128,512]{1,0:T(8,128)(2,1)S(1)}, bf16[128,512]{1,0:T(8,128)(2,1)S(1)}, u32[]{:S(2)}, u32[]{:S(2)}) collective-permute-start(bf16[128,512]{1,0:T(8,128)(2,1)S(1)} %get-tuple-element.101.refs_0_), channel_id=1, source_target_pairs={{0,3},{1,2},{2,1},{3,0},{4,7},{5,6},{6,5},{7,4},{8,11},{9,10},{10,... | collective-permute-start | bytes 393224 | tf_op jit(solution)/shard_map/ppermute | solution.py:350
  17.9 0.6 collective-permute-start.6
  18.4 4.8 %collective-permute-done.2.refs_3_ = bf16[128,256]{1,0:T(8,128)(2,1)S(1)} collective-permute-done((bf16[128,256]{1,0:T(8,128)(2,1)S(1)}, bf16[128,256]{1,0:T(8,128)(2,1)S(1)}, u32[]{:S(2)}, u32[]{:S(2)}) %collective-permute-start.2) | collective-permute-done | bytes 65568 | tf_op jit(solution)/shard_map/ppermute | solution.py:350
  23.3 0.4 collective-permute-done.1.refs_2_
  23.6 2.3 %collective-permute-done.refs_1_ = bf16[128,768]{1,0:T(8,128)(2,1)S(1)} collective-permute-done((bf16[128,768]{1,0:T(8,128)(2,1)S(1)}, bf16[128,768]{1,0:T(8,128)(2,1)S(1)}, u32[]{:S(2)}, u32[]{:S(2)}) %collective-permute-start) | collective-permute-done | bytes 196640 | tf_op jit(solution)/shard_map/ppermute | solution.py:350
  25.9 0.0 all-to-all-done
  25.9 0.8 %shard_map.165 = (bf16[128,256]{1,0:T(8,128)(2,1)S(1)}, bf16[128,256]{1,0:T(8,128)(2,1)S(1)}, bf16[128,256]{1,0:T(8,128)(2,1)S(1)}, bf16[128,256]{1,0:T(8,128)(2,1)S(1)}, bf16[256,576]{1,0:T(8,128)(2,1)S(1)}) custom-call(bf16[256,1152]{1,0:T(8,128)(2,1)S(1)} %bitcast.5, bf16[128,256]{1,0:T(8,128)(2,1)S(1)} %bitcast.10, ...), custom_call_target="tpu_custom_call" | custom-call | flops 1006632960 | bytes 1540096 | tf_op jit(solution)/shard_map/pallas_call | solution.py:49
  26.7 1.9 %collective-permute-start.3 = (bf16[128,256]{1,0:T(8,128)(2,1)S(1)}, bf16[128,256]{1,0:T(8,128)(2,1)S(1)}, u32[]{:S(2)}, u32[]{:S(2)}) collective-permute-start(bf16[128,256]{1,0:T(8,128)(2,1)S(1)} %get-tuple-element.85), channel_id=1, source_target_pairs={{0,3},{1,2},{2,1},{3,0},{4,7},{5,6},{6,5},{7,4},{8,11},{9,10},{10,... | collective-permute-start | bytes 196616 | tf_op jit(solution)/shard_map/ppermute | solution.py:350
  28.6 1.1 %collective-permute-start.4 = (bf16[128,256]{1,0:T(8,128)(2,1)S(1)}, bf16[128,256]{1,0:T(8,128)(2,1)S(1)}, u32[]{:S(2)}, u32[]{:S(2)}) collective-permute-start(bf16[128,256]{1,0:T(8,128)(2,1)S(1)} %get-tuple-element.86), channel_id=1, source_target_pairs={{0,2},{1,3},{2,0},{3,1},{4,6},{5,7},{6,4},{7,5},{8,10},{9,11},{10,... | collective-permute-start | bytes 196616 | tf_op jit(solution)/shard_map/ppermute | solution.py:350
  29.7 0.6 collective-permute-start.5
  30.3 2.5 %collective-permute-start.11 = (bf16[128,256]{1,0:T(8,128)(2,1)S(1)}, bf16[128,256]{1,0:T(8,128)(2,1)S(1)}, u32[]{:S(2)}, u32[]{:S(2)}) collective-permute-start(bf16[128,256]{1,0:T(8,128)(2,1)S(1)} %bitcast.11), channel_id=1, source_target_pairs={{0,4},{1,5},{2,6},{3,7},{4,0},{5,1},{6,2},{7,3},{8,12},{9,13},{10,... | collective-permute-start | bytes 196616 | tf_op jit(solution)/shard_map/ppermute | solution.py:350
  32.8 1.2 %collective-permute-done.3.refs_1_ = bf16[128,256]{1,0:T(8,128)(2,1)S(1)} collective-permute-done((bf16[128,256]{1,0:T(8,128)(2,1)S(1)}, bf16[128,256]{1,0:T(8,128)(2,1)S(1)}, u32[]{:S(2)}, u32[]{:S(2)}) %collective-permute-start.3) | collective-permute-done | bytes 65568 | tf_op jit(solution)/shard_map/ppermute | solution.py:350
  34.0 0.0 collective-permute-done.4.refs_2_
  34.0 0.4 collective-permute-done.5.refs_3_
  34.5 0.1 shard_map.166
  34.6 0.1 collective-permute-start.10
  34.7 1.6 %collective-permute-start.9 = (f32[2,128]{1,0:T(2,128)S(1)}, f32[2,128]{1,0:T(2,128)S(1)}, u32[]{:S(2)}, u32[]{:S(2)}) collective-permute-start(f32[2,128]{1,0:T(2,128)S(1)} %get-tuple-element.96.refs_0_), channel_id=1, source_target_pairs={{0,16},{8,24},{16,0},{24,8},{1,17},{9,25},{17,1},{25,9},{2,18},{10... | collective-permute-start | bytes 3080 | tf_op jit(solution)/shard_map/ppermute | solution.py:350
  36.3 0.3 collective-permute-start.8
  36.5 1.1 %collective-permute-done.10.refs_3_ = f32[2,128]{1,0:T(2,128)S(1)} collective-permute-done((f32[2,128]{1,0:T(2,128)S(1)}, f32[2,128]{1,0:T(2,128)S(1)}, u32[]{:S(2)}, u32[]{:S(2)}) %collective-permute-start.10) | collective-permute-done | bytes 1056 | tf_op jit(solution)/shard_map/ppermute | solution.py:350
  37.7 0.7 collective-permute-done.9.refs_2_
  38.3 0.0 collective-permute-done.8.refs_1_
  38.3 0.1 shard_map.167.refs_4_
  38.5 2.4 %collective-permute-start.15 = (bf16[128,256]{1,0:T(8,128)(2,1)S(1)}, bf16[128,256]{1,0:T(8,128)(2,1)S(1)}, u32[]{:S(2)}, u32[]{:S(2)}) collective-permute-start(bf16[128,256]{1,0:T(8,128)(2,1)S(1)} %shard_map.167.refs_4_), channel_id=1, source_target_pairs={{0,4},{1,5},{2,6},{3,7},{4,0},{5,1},{6,2},{7,3},{8,12},{9,13},{10,... | collective-permute-start | bytes 196616 | tf_op jit(solution)/shard_map/ppermute | solution.py:350
  40.9 0.7 collective-permute-start.14
  41.6 1.6 %collective-permute-start.13 = (bf16[128,256]{1,0:T(8,128)(2,1)S(1)}, bf16[128,256]{1,0:T(8,128)(2,1)S(1)}, u32[]{:S(2)}, u32[]{:S(2)}) collective-permute-start(bf16[128,256]{1,0:T(8,128)(2,1)S(1)} %shard_map.167.refs_4_), channel_id=1, source_target_pairs={{0,2},{1,3},{2,0},{3,1},{4,6},{5,7},{6,4},{7,5},{8,10},{9,11},{10,... | collective-permute-start | bytes 196616 | tf_op jit(solution)/shard_map/ppermute | solution.py:350
  43.1 1.2 %collective-permute-start.12 = (bf16[128,256]{1,0:T(8,128)(2,1)S(1)}, bf16[128,256]{1,0:T(8,128)(2,1)S(1)}, u32[]{:S(2)}, u32[]{:S(2)}) collective-permute-start(bf16[128,256]{1,0:T(8,128)(2,1)S(1)} %shard_map.167.refs_4_), channel_id=1, source_target_pairs={{0,1},{1,0},{2,3},{3,2},{4,5},{5,4},{6,7},{7,6},{8,9},{9,8},{10,11... | collective-permute-start | bytes 196616 | tf_op jit(solution)/shard_map/ppermute | solution.py:350
  44.4 0.1 pad_add_fusion.place
  44.4 1.1 %shard_map.169 = (f32[4,512,192]{2,1,0:T(8,128)S(1)}, bf16[3,512,192]{2,1,0:T(8,128)(2,1)S(1)}, f32[3,192]{1,0:T(4,128)S(1)}, f32[3,256,192]{2,1,0:T(8,128)S(1)}, f32[3,256,192]{2,1,0:T(8,128)S(1)}) custom-call(bf16[256,1152]{1,0:T(8,128)(2,1)S(1)} %bitcast.6, bf16[128,512]{1,0:T(8,128)(2,1)S(1)} %get-tuple-element.101.refs_0_, ...), custom_call_target="tpu_custom_call" | custom-call | flops 603979776 | bytes 4524288 | tf_op jit(solution)/shard_map/pallas_call | solution.py:49
  45.6 0.0 collective-permute-done.15.left
  45.6 0.8 %collective-permute-start.18 = (bf16[128,512]{1,0:T(8,128)(2,1)S(1)}, bf16[128,512]{1,0:T(8,128)(2,1)S(1)}, u32[]{:S(2)}, u32[]{:S(2)}) collective-permute-start(bf16[128,512]{1,0:T(8,128)(2,1)S(1)} %shard_map.170.refs_4_), channel_id=1, source_target_pairs={{0,3},{1,2},{2,1},{3,0},{4,7},{5,6},{6,5},{7,4},{8,11},{9,10},{10,... | collective-permute-start | bytes 393224 | tf_op jit(solution)/shard_map/ppermute | solution.py:350
  46.4 1.6 %collective-permute-start.17 = (bf16[128,512]{1,0:T(8,128)(2,1)S(1)}, bf16[128,512]{1,0:T(8,128)(2,1)S(1)}, u32[]{:S(2)}, u32[]{:S(2)}) collective-permute-start(bf16[128,512]{1,0:T(8,128)(2,1)S(1)} %shard_map.170.refs_4_), channel_id=1, source_target_pairs={{0,2},{1,3},{2,0},{3,1},{4,6},{5,7},{6,4},{7,5},{8,10},{9,11},{10,... | collective-permute-start | bytes 393224 | tf_op jit(solution)/shard_map/ppermute | solution.py:350
  47.9 0.0 collective-permute-done.14.refs_7_
  47.9 1.2 %collective-permute-start.16 = (bf16[128,512]{1,0:T(8,128)(2,1)S(1)}, bf16[128,512]{1,0:T(8,128)(2,1)S(1)}, u32[]{:S(2)}, u32[]{:S(2)}) collective-permute-start(bf16[128,512]{1,0:T(8,128)(2,1)S(1)} %shard_map.170.refs_4_), channel_id=1, source_target_pairs={{0,1},{1,0},{2,3},{3,2},{4,5},{5,4},{6,7},{7,6},{8,9},{9,8},{10,11... | collective-permute-start | bytes 393224 | tf_op jit(solution)/shard_map/ppermute | solution.py:350
  49.2 0.8 %shard_map.168 = (bf16[128,256]{1,0:T(8,128)(2,1)S(1)}, bf16[128,256]{1,0:T(8,128)(2,1)S(1)}, bf16[128,256]{1,0:T(8,128)(2,1)S(1)}, bf16[128,256]{1,0:T(8,128)(2,1)S(1)}, f32[3,256,192]{2,1,0:T(8,128)S(1)}) custom-call(bf16[256,576]{1,0:T(8,128)(2,1)S(1)} %get-tuple-element.78.normed_ref, bf16[128,256]{1,0:T(8,128)(2,1)S(1)} %bitcast.12, ...), custom_call_target="tpu_custom_call" | custom-call | flops 3019898880 | bytes 1802240 | tf_op jit(solution)/shard_map/pallas_call | solution.py:49
  50.0 0.8 %collective-permute-start.19 = (bf16[128,256]{1,0:T(8,128)(2,1)S(1)}, bf16[128,256]{1,0:T(8,128)(2,1)S(1)}, u32[]{:S(2)}, u32[]{:S(2)}) collective-permute-start(bf16[128,256]{1,0:T(8,128)(2,1)S(1)} %get-tuple-element.119), channel_id=1, source_target_pairs={{0,3},{1,2},{2,1},{3,0},{4,7},{5,6},{6,5},{7,4},{8,11},{9,10},{10,... | collective-permute-start | bytes 196616 | tf_op jit(solution)/shard_map/ppermute | solution.py:350
  50.8 1.6 %collective-permute-start.20 = (bf16[128,256]{1,0:T(8,128)(2,1)S(1)}, bf16[128,256]{1,0:T(8,128)(2,1)S(1)}, u32[]{:S(2)}, u32[]{:S(2)}) collective-permute-start(bf16[128,256]{1,0:T(8,128)(2,1)S(1)} %get-tuple-element.120), channel_id=1, source_target_pairs={{0,2},{1,3},{2,0},{3,1},{4,6},{5,7},{6,4},{7,5},{8,10},{9,11},{10,... | collective-permute-start | bytes 196616 | tf_op jit(solution)/shard_map/ppermute | solution.py:350
  52.3 0.7 collective-permute-done.18.refs_7_
  53.0 0.9 %collective-permute-start.21 = (bf16[128,256]{1,0:T(8,128)(2,1)S(1)}, bf16[128,256]{1,0:T(8,128)(2,1)S(1)}, u32[]{:S(2)}, u32[]{:S(2)}) collective-permute-start(bf16[128,256]{1,0:T(8,128)(2,1)S(1)} %get-tuple-element.121), channel_id=1, source_target_pairs={{0,1},{1,0},{2,3},{3,2},{4,5},{5,4},{6,7},{7,6},{8,9},{9,8},{10,11... | collective-permute-start | bytes 196616 | tf_op jit(solution)/shard_map/ppermute | solution.py:350
  53.9 0.9 %collective-permute-done.17.refs_6_ = bf16[128,512]{1,0:T(8,128)(2,1)S(1)} collective-permute-done((bf16[128,512]{1,0:T(8,128)(2,1)S(1)}, bf16[128,512]{1,0:T(8,128)(2,1)S(1)}, u32[]{:S(2)}, u32[]{:S(2)}) %collective-permute-start.17) | collective-permute-done | bytes 131104 | tf_op jit(solution)/shard_map/ppermute | solution.py:350
  54.8 0.9 %collective-permute-done.16.refs_5_ = bf16[128,512]{1,0:T(8,128)(2,1)S(1)} collective-permute-done((bf16[128,512]{1,0:T(8,128)(2,1)S(1)}, bf16[128,512]{1,0:T(8,128)(2,1)S(1)}, u32[]{:S(2)}, u32[]{:S(2)}) %collective-permute-start.16) | collective-permute-done | bytes 131104 | tf_op jit(solution)/shard_map/ppermute | solution.py:350
  55.7 2.6 %shard_map.171 = (bf16[128,512]{1,0:T(8,128)(2,1)S(1)}, bf16[32,576]{1,0:T(8,128)(2,1)S(1)}, bf16[672,128]{1,0:T(8,128)(2,1)S(1)}, bf16[672,128]{1,0:T(8,128)(2,...) custom-call(s32[3]{0:T(128)S(1)} %pad_add_fusion.place, ...), custom_call_target="tpu_custom_call" | custom-call | flops 6039797760 | bytes 6764812 | tf_op jit(solution)/shard_map/pallas_call | solution.py:49
  58.3 0.8 %collective-permute-start.22 = (bf16[64,576]{1,0:T(8,128)(2,1)S(1)}, bf16[64,576]{1,0:T(8,128)(2,1)S(1)}, u32[]{:S(2)}, u32[]{:S(2)}) collective-permute-start(bf16[64,576]{1,0:T(8,128)(2,1)S(1)} %get-tuple-element.122), channel_id=1, source_target_pairs={{0,4},{1,5},{2,6},{3,7},{4,0},{5,1},{6,2},{7,3},{8,12},{9,13},{10,... | collective-permute-start | bytes 221192 | tf_op jit(solution)/shard_map/ppermute | solution.py:350
  59.1 1.8 %collective-permute-start.23 = (bf16[64,576]{1,0:T(8,128)(2,1)S(1)}, bf16[64,576]{1,0:T(8,128)(2,1)S(1)}, u32[]{:S(2)}, u32[]{:S(2)}) collective-permute-start(bf16[64,576]{1,0:T(8,128)(2,1)S(1)} %get-tuple-element.123), channel_id=1, source_target_pairs={{0,6},{1,7},{2,4},{3,5},{4,2},{5,3},{6,0},{7,1},{8,14},{9,15},{10,... | collective-permute-start | bytes 221192 | tf_op jit(solution)/shard_map/ppermute | solution.py:350
  60.9 0.9 %collective-permute-start.25 = (bf16[672,128]{1,0:T(8,128)(2,1)S(1)}, bf16[672,128]{1,0:T(8,128)(2,1)S(1)}, u32[]{:S(2)}, u32[]{:S(2)}) collective-permute-start(bf16[672,128]{1,0:T(8,128)(2,1)S(1)} %get-tuple-element.130), channel_id=1, source_target_pairs={{0,1},{1,0},{2,3},{3,2},{4,5},{5,4},{6,7},{7,6},{8,9},{9,8},{10,11... | collective-permute-start | bytes 516104 | tf_op jit(solution)/shard_map/ppermute | solution.py:350
  61.8 0.7 %collective-permute-start.26 = (bf16[672,128]{1,0:T(8,128)(2,1)S(1)}, bf16[672,128]{1,0:T(8,128)(2,1)S(1)}, u32[]{:S(2)}, u32[]{:S(2)}) collective-permute-start(bf16[672,128]{1,0:T(8,128)(2,1)S(1)} %get-tuple-element.131), channel_id=1, source_target_pairs={{0,2},{1,3},{2,0},{3,1},{4,6},{5,7},{6,4},{7,5},{8,10},{9,11},{10,... | collective-permute-start | bytes 516104 | tf_op jit(solution)/shard_map/ppermute | solution.py:350
  62.5 1.8 %collective-permute-start.27 = (bf16[672,128]{1,0:T(8,128)(2,1)S(1)}, bf16[672,128]{1,0:T(8,128)(2,1)S(1)}, u32[]{:S(2)}, u32[]{:S(2)}) collective-permute-start(bf16[672,128]{1,0:T(8,128)(2,1)S(1)} %get-tuple-element.132), channel_id=1, source_target_pairs={{0,3},{1,2},{2,1},{3,0},{4,7},{5,6},{6,5},{7,4},{8,11},{9,10},{10,... | collective-permute-start | bytes 516104 | tf_op jit(solution)/shard_map/ppermute | solution.py:350
  64.3 0.9 %collective-permute-done.22.refs_0_.refs_3_ = bf16[64,576]{1,0:T(8,128)(2,1)S(1)} collective-permute-done((bf16[64,576]{1,0:T(8,128)(2,1)S(1)}, bf16[64,576]{1,0:T(8,128)(2,1)S(1)}, u32[]{:S(2)}, u32[]{:S(2)}) %collective-permute-start.22) | collective-permute-done | bytes 73760 | tf_op jit(solution)/shard_map/ppermute | solution.py:350
  65.3 1.0 %collective-permute-done.23.refs_1_.refs_4_ = bf16[64,576]{1,0:T(8,128)(2,1)S(1)} collective-permute-done((bf16[64,576]{1,0:T(8,128)(2,1)S(1)}, bf16[64,576]{1,0:T(8,128)(2,1)S(1)}, u32[]{:S(2)}, u32[]{:S(2)}) %collective-permute-start.23) | collective-permute-done | bytes 73760 | tf_op jit(solution)/shard_map/ppermute | solution.py:350
  66.3 0.9 %collective-permute-start.24 = (bf16[64,576]{1,0:T(8,128)(2,1)S(1)}, bf16[64,576]{1,0:T(8,128)(2,1)S(1)}, u32[]{:S(2)}, u32[]{:S(2)}) collective-permute-start(bf16[64,576]{1,0:T(8,128)(2,1)S(1)} %shard_map.172), channel_id=1, source_target_pairs={{0,1},{1,0},{2,3},{3,2},{4,5},{5,4},{6,7},{7,6},{8,9},{9,8},{10,11... | collective-permute-start | bytes 221192 | tf_op jit(solution)/shard_map/ppermute | solution.py:350
  67.2 1.3 %collective-permute-done.25.refs_4_.refs_0_ = bf16[672,128]{1,0:T(8,128)(2,1)S(1)} collective-permute-done((bf16[672,128]{1,0:T(8,128)(2,1)S(1)}, bf16[672,128]{1,0:T(8,128)(2,1)S(1)}, u32[]{:S(2)}, u32[]{:S(2)}) %collective-permute-start.25) | collective-permute-done | bytes 172064 | tf_op jit(solution)/shard_map/ppermute | solution.py:350
  68.4 1.2 %collective-permute-done.26.refs_5_.refs_1_ = bf16[672,128]{1,0:T(8,128)(2,1)S(1)} collective-permute-done((bf16[672,128]{1,0:T(8,128)(2,1)S(1)}, bf16[672,128]{1,0:T(8,128)(2,1)S(1)}, u32[]{:S(2)}, u32[]{:S(2)}) %collective-permute-start.26) | collective-permute-done | bytes 172064 | tf_op jit(solution)/shard_map/ppermute | solution.py:350
  69.6 2.1 %collective-permute-done.27.refs_6_.refs_2_ = bf16[672,128]{1,0:T(8,128)(2,1)S(1)} collective-permute-done((bf16[672,128]{1,0:T(8,128)(2,1)S(1)}, bf16[672,128]{1,0:T(8,128)(2,1)S(1)}, u32[]{:S(2)}, u32[]{:S(2)}) %collective-permute-start.27) | collective-permute-done | bytes 172064 | tf_op jit(solution)/shard_map/ppermute | solution.py:350
  71.7 0.7 %shard_map.173 = (bf16[1,128,256]{2,1,0:T(8,128)(2,1)}, bf16[1,128,256]{2,1,0:T(8,128)(2,1)}, bf16[1,128,256]{2,1,0:T(8,128)(2,1)}) custom-call(f32[128,256]{1,0:T(8,128)S(1)} %get-tuple-element.124.rate, bf16[128,512]{1,0:T(8,128)(2,1)S(1)} %get-tuple-element.125.tok, bf16[128,256]{1,0:T(8,128)(2,1)S(1)} %get-tuple-element.126.refs_0_, ...), custom_call_target="tpu_custom_call" | custom-call | bytes 1236992 | tf_op jit(solution)/shard_map/pallas_call | solution.py:49
  72.5 0.0 collective-permute-done.24.relayed
  72.5 1.4 %shard_map.174 = (f32[1,32,768]{2,1,0:T(8,128)}, f32[1,32,768]{2,1,0:T(8,128)}, f32[1,32,768]{2,1,0:T(8,128)}) custom-call(s32[3]{0:T(128)S(1)} %pad_add_fusion.place, bf16[64,576]{1,0:T(8,128)(2,1)S(1)} %collective-permute-done.24.relayed, bf16[32,576]{1,0:T(8,128)(2,1)S(1)} %get-tuple-element.140.inner, ...), custom_call_target="tpu_custom_call" | custom-call | bytes 1069068 | tf_op jit(solution)/shard_map/pallas_call | solution.py:49
  (19 shorter events, 0.1 us)
Async XLA Ops:
  0.6 9.3 %copy-start.3 = (bf16[1,128,256]{2,1,0:T(8,128)(2,1)S(1)}, bf16[1,128,256]{2,1,0:T(8,128)(2,1)}, u32[]{:S(2)}) copy-start(bf16[1,128,256]{2,1,0:T(8,128)(2,1)} %q.1) | copy-start | bytes 196612
  0.6 9.3 %copy-start.2 = (bf16[1,128,256]{2,1,0:T(8,128)(2,1)S(1)}, bf16[1,128,256]{2,1,0:T(8,128)(2,1)}, u32[]{:S(2)}) copy-start(bf16[1,128,256]{2,1,0:T(8,128)(2,1)} %og.1) | copy-start | bytes 196612
  0.7 9.3 %copy-start.1 = (bf16[1,128,256]{2,1,0:T(8,128)(2,1)S(1)}, bf16[1,128,256]{2,1,0:T(8,128)(2,1)}, u32[]{:S(2)}) copy-start(bf16[1,128,256]{2,1,0:T(8,128)(2,1)} %v.1) | copy-start | bytes 196612
  0.7 9.3 %copy-start = (bf16[1,128,256]{2,1,0:T(8,128)(2,1)S(1)}, bf16[1,128,256]{2,1,0:T(8,128)(2,1)}, u32[]{:S(2)}) copy-start(bf16[1,128,256]{2,1,0:T(8,128)(2,1)} %k.1) | copy-start | bytes 196612
  2.6 23.3 %all-to-all-start = ((bf16[8,32,1152]{2,1,0:T(8,128)(2,1)}), bf16[8,32,1152]{2,1,0:T(8,128)(2,1)S(1)}, u32[]{:S(2)}, u32[]{:S(2)}) async-start(bf16[8,32,1152]{2,1,0:T(8,128)(2,1)} %shard_map.163), calls=%async_computation | async-start | bytes 1179648 | tf_op jit(solution)/shard_map/all_to_all | solution.py:373
  9.9 0.7 copy-start.4
  10.6 0.7 copy-start.5
  11.4 14.5 %collective-permute-start = (bf16[128,768]{1,0:T(8,128)(2,1)S(1)}, bf16[128,768]{1,0:T(8,128)(2,1)S(1)}, u32[]{:S(2)}, u32[]{:S(2)}) collective-permute-start(bf16[128,768]{1,0:T(8,128)(2,1)S(1)} %get-tuple-element.77), channel_id=1, source_target_pairs={{0,1},{1,0},{2,3},{3,2},{4,5},{5,4},{6,7},{7,6},{8,9},{9,8},{10,11... | collective-permute-start | bytes 589832 | tf_op jit(solution)/shard_map/ppermute | solution.py:350
  13.5 9.8 %collective-permute-start.2 = (bf16[128,256]{1,0:T(8,128)(2,1)S(1)}, bf16[128,256]{1,0:T(8,128)(2,1)S(1)}, u32[]{:S(2)}, u32[]{:S(2)}) collective-permute-start(bf16[128,256]{1,0:T(8,128)(2,1)S(1)} %bitcast.8), channel_id=1, source_target_pairs={{0,3},{1,2},{2,1},{3,0},{4,7},{5,6},{6,5},{7,4},{8,11},{9,10},{10,... | collective-permute-start | bytes 196616 | tf_op jit(solution)/shard_map/ppermute | solution.py:350
  14.9 8.7 %collective-permute-start.1 = (bf16[128,256]{1,0:T(8,128)(2,1)S(1)}, bf16[128,256]{1,0:T(8,128)(2,1)S(1)}, u32[]{:S(2)}, u32[]{:S(2)}) collective-permute-start(bf16[128,256]{1,0:T(8,128)(2,1)S(1)} %bitcast.9), channel_id=1, source_target_pairs={{0,2},{1,3},{2,0},{3,1},{4,6},{5,7},{6,4},{7,5},{8,10},{9,11},{10,... | collective-permute-start | bytes 196616 | tf_op jit(solution)/shard_map/ppermute | solution.py:350
  15.0 15.2 %collective-permute-start.7 = (bf16[128,512]{1,0:T(8,128)(2,1)S(1)}, bf16[128,512]{1,0:T(8,128)(2,1)S(1)}, u32[]{:S(2)}, u32[]{:S(2)}) collective-permute-start(bf16[128,512]{1,0:T(8,128)(2,1)S(1)} %get-tuple-element.101.refs_0_), channel_id=1, source_target_pairs={{0,3},{1,2},{2,1},{3,0},{4,7},{5,6},{6,5},{7,4},{8,11},{9,10},{10,... | collective-permute-start | bytes 393224 | tf_op jit(solution)/shard_map/ppermute | solution.py:350
  17.9 14.9 %collective-permute-start.6 = (bf16[128,512]{1,0:T(8,128)(2,1)S(1)}, bf16[128,512]{1,0:T(8,128)(2,1)S(1)}, u32[]{:S(2)}, u32[]{:S(2)}) collective-permute-start(bf16[128,512]{1,0:T(8,128)(2,1)S(1)} %get-tuple-element.101.refs_0_), channel_id=1, source_target_pairs={{0,2},{1,3},{2,0},{3,1},{4,6},{5,7},{6,4},{7,5},{8,10},{9,11},{10,... | collective-permute-start | bytes 393224 | tf_op jit(solution)/shard_map/ppermute | solution.py:350
  26.7 7.3 %collective-permute-start.3 = (bf16[128,256]{1,0:T(8,128)(2,1)S(1)}, bf16[128,256]{1,0:T(8,128)(2,1)S(1)}, u32[]{:S(2)}, u32[]{:S(2)}) collective-permute-start(bf16[128,256]{1,0:T(8,128)(2,1)S(1)} %get-tuple-element.85), channel_id=1, source_target_pairs={{0,3},{1,2},{2,1},{3,0},{4,7},{5,6},{6,5},{7,4},{8,11},{9,10},{10,... | collective-permute-start | bytes 196616 | tf_op jit(solution)/shard_map/ppermute | solution.py:350
  28.6 5.5 %collective-permute-start.4 = (bf16[128,256]{1,0:T(8,128)(2,1)S(1)}, bf16[128,256]{1,0:T(8,128)(2,1)S(1)}, u32[]{:S(2)}, u32[]{:S(2)}) collective-permute-start(bf16[128,256]{1,0:T(8,128)(2,1)S(1)} %get-tuple-element.86), channel_id=1, source_target_pairs={{0,2},{1,3},{2,0},{3,1},{4,6},{5,7},{6,4},{7,5},{8,10},{9,11},{10,... | collective-permute-start | bytes 196616 | tf_op jit(solution)/shard_map/ppermute | solution.py:350
  29.7 4.8 %collective-permute-start.5 = (bf16[128,256]{1,0:T(8,128)(2,1)S(1)}, bf16[128,256]{1,0:T(8,128)(2,1)S(1)}, u32[]{:S(2)}, u32[]{:S(2)}) collective-permute-start(bf16[128,256]{1,0:T(8,128)(2,1)S(1)} %get-tuple-element.87), channel_id=1, source_target_pairs={{0,1},{1,0},{2,3},{3,2},{4,5},{5,4},{6,7},{7,6},{8,9},{9,8},{10,11... | collective-permute-start | bytes 196616 | tf_op jit(solution)/shard_map/ppermute | solution.py:350
  30.3 6.3 %collective-permute-start.11 = (bf16[128,256]{1,0:T(8,128)(2,1)S(1)}, bf16[128,256]{1,0:T(8,128)(2,1)S(1)}, u32[]{:S(2)}, u32[]{:S(2)}) collective-permute-start(bf16[128,256]{1,0:T(8,128)(2,1)S(1)} %bitcast.11), channel_id=1, source_target_pairs={{0,4},{1,5},{2,6},{3,7},{4,0},{5,1},{6,2},{7,3},{8,12},{9,13},{10,... | collective-permute-start | bytes 196616 | tf_op jit(solution)/shard_map/ppermute | solution.py:350
  34.6 3.1 %collective-permute-start.10 = (f32[2,128]{1,0:T(2,128)S(1)}, f32[2,128]{1,0:T(2,128)S(1)}, u32[]{:S(2)}, u32[]{:S(2)}) collective-permute-start(f32[2,128]{1,0:T(2,128)S(1)} %get-tuple-element.96.refs_0_), channel_id=1, source_target_pairs={{0,24},{8,16},{16,8},{24,0},{1,25},{9,17},{17,9},{25,1},{2,26},{10... | collective-permute-start | bytes 3080 | tf_op jit(solution)/shard_map/ppermute | solution.py:350
  34.7 3.6 %collective-permute-start.9 = (f32[2,128]{1,0:T(2,128)S(1)}, f32[2,128]{1,0:T(2,128)S(1)}, u32[]{:S(2)}, u32[]{:S(2)}) collective-permute-start(f32[2,128]{1,0:T(2,128)S(1)} %get-tuple-element.96.refs_0_), channel_id=1, source_target_pairs={{0,16},{8,24},{16,0},{24,8},{1,17},{9,25},{17,1},{25,9},{2,18},{10... | collective-permute-start | bytes 3080 | tf_op jit(solution)/shard_map/ppermute | solution.py:350
  36.3 2.1 %collective-permute-start.8 = (f32[2,128]{1,0:T(2,128)S(1)}, f32[2,128]{1,0:T(2,128)S(1)}, u32[]{:S(2)}, u32[]{:S(2)}) collective-permute-start(f32[2,128]{1,0:T(2,128)S(1)} %get-tuple-element.96.refs_0_), channel_id=1, source_target_pairs={{0,8},{8,0},{16,24},{24,16},{1,9},{9,1},{17,25},{25,17},{2,10},{10... | collective-permute-start | bytes 3080 | tf_op jit(solution)/shard_map/ppermute | solution.py:350
  38.5 7.1 %collective-permute-start.15 = (bf16[128,256]{1,0:T(8,128)(2,1)S(1)}, bf16[128,256]{1,0:T(8,128)(2,1)S(1)}, u32[]{:S(2)}, u32[]{:S(2)}) collective-permute-start(bf16[128,256]{1,0:T(8,128)(2,1)S(1)} %shard_map.167.refs_4_), channel_id=1, source_target_pairs={{0,4},{1,5},{2,6},{3,7},{4,0},{5,1},{6,2},{7,3},{8,12},{9,13},{10,... | collective-permute-start | bytes 196616 | tf_op jit(solution)/shard_map/ppermute | solution.py:350
  40.9 7.0 %collective-permute-start.14 = (bf16[128,256]{1,0:T(8,128)(2,1)S(1)}, bf16[128,256]{1,0:T(8,128)(2,1)S(1)}, u32[]{:S(2)}, u32[]{:S(2)}) collective-permute-start(bf16[128,256]{1,0:T(8,128)(2,1)S(1)} %shard_map.167.refs_4_), channel_id=1, source_target_pairs={{0,3},{1,2},{2,1},{3,0},{4,7},{5,6},{6,5},{7,4},{8,11},{9,10},{10,... | collective-permute-start | bytes 196616 | tf_op jit(solution)/shard_map/ppermute | solution.py:350
  41.6 7.6 %collective-permute-start.13 = (bf16[128,256]{1,0:T(8,128)(2,1)S(1)}, bf16[128,256]{1,0:T(8,128)(2,1)S(1)}, u32[]{:S(2)}, u32[]{:S(2)}) collective-permute-start(bf16[128,256]{1,0:T(8,128)(2,1)S(1)} %shard_map.167.refs_4_), channel_id=1, source_target_pairs={{0,2},{1,3},{2,0},{3,1},{4,6},{5,7},{6,4},{7,5},{8,10},{9,11},{10,... | collective-permute-start | bytes 196616 | tf_op jit(solution)/shard_map/ppermute | solution.py:350
  43.1 6.0 %collective-permute-start.12 = (bf16[128,256]{1,0:T(8,128)(2,1)S(1)}, bf16[128,256]{1,0:T(8,128)(2,1)S(1)}, u32[]{:S(2)}, u32[]{:S(2)}) collective-permute-start(bf16[128,256]{1,0:T(8,128)(2,1)S(1)} %shard_map.167.refs_4_), channel_id=1, source_target_pairs={{0,1},{1,0},{2,3},{3,2},{4,5},{5,4},{6,7},{7,6},{8,9},{9,8},{10,11... | collective-permute-start | bytes 196616 | tf_op jit(solution)/shard_map/ppermute | solution.py:350
  45.6 7.4 %collective-permute-start.18 = (bf16[128,512]{1,0:T(8,128)(2,1)S(1)}, bf16[128,512]{1,0:T(8,128)(2,1)S(1)}, u32[]{:S(2)}, u32[]{:S(2)}) collective-permute-start(bf16[128,512]{1,0:T(8,128)(2,1)S(1)} %shard_map.170.refs_4_), channel_id=1, source_target_pairs={{0,3},{1,2},{2,1},{3,0},{4,7},{5,6},{6,5},{7,4},{8,11},{9,10},{10,... | collective-permute-start | bytes 393224 | tf_op jit(solution)/shard_map/ppermute | solution.py:350
  46.4 8.5 %collective-permute-start.17 = (bf16[128,512]{1,0:T(8,128)(2,1)S(1)}, bf16[128,512]{1,0:T(8,128)(2,1)S(1)}, u32[]{:S(2)}, u32[]{:S(2)}) collective-permute-start(bf16[128,512]{1,0:T(8,128)(2,1)S(1)} %shard_map.170.refs_4_), channel_id=1, source_target_pairs={{0,2},{1,3},{2,0},{3,1},{4,6},{5,7},{6,4},{7,5},{8,10},{9,11},{10,... | collective-permute-start | bytes 393224 | tf_op jit(solution)/shard_map/ppermute | solution.py:350
  47.9 7.8 %collective-permute-start.16 = (bf16[128,512]{1,0:T(8,128)(2,1)S(1)}, bf16[128,512]{1,0:T(8,128)(2,1)S(1)}, u32[]{:S(2)}, u32[]{:S(2)}) collective-permute-start(bf16[128,512]{1,0:T(8,128)(2,1)S(1)} %shard_map.170.refs_4_), channel_id=1, source_target_pairs={{0,1},{1,0},{2,3},{3,2},{4,5},{5,4},{6,7},{7,6},{8,9},{9,8},{10,11... | collective-permute-start | bytes 393224 | tf_op jit(solution)/shard_map/ppermute | solution.py:350
  50.0 8.3 %collective-permute-start.19 = (bf16[128,256]{1,0:T(8,128)(2,1)S(1)}, bf16[128,256]{1,0:T(8,128)(2,1)S(1)}, u32[]{:S(2)}, u32[]{:S(2)}) collective-permute-start(bf16[128,256]{1,0:T(8,128)(2,1)S(1)} %get-tuple-element.119), channel_id=1, source_target_pairs={{0,3},{1,2},{2,1},{3,0},{4,7},{5,6},{6,5},{7,4},{8,11},{9,10},{10,... | collective-permute-start | bytes 196616 | tf_op jit(solution)/shard_map/ppermute | solution.py:350
  50.8 7.6 %collective-permute-start.20 = (bf16[128,256]{1,0:T(8,128)(2,1)S(1)}, bf16[128,256]{1,0:T(8,128)(2,1)S(1)}, u32[]{:S(2)}, u32[]{:S(2)}) collective-permute-start(bf16[128,256]{1,0:T(8,128)(2,1)S(1)} %get-tuple-element.120), channel_id=1, source_target_pairs={{0,2},{1,3},{2,0},{3,1},{4,6},{5,7},{6,4},{7,5},{8,10},{9,11},{10,... | collective-permute-start | bytes 196616 | tf_op jit(solution)/shard_map/ppermute | solution.py:350
  53.0 5.3 %collective-permute-start.21 = (bf16[128,256]{1,0:T(8,128)(2,1)S(1)}, bf16[128,256]{1,0:T(8,128)(2,1)S(1)}, u32[]{:S(2)}, u32[]{:S(2)}) collective-permute-start(bf16[128,256]{1,0:T(8,128)(2,1)S(1)} %get-tuple-element.121), channel_id=1, source_target_pairs={{0,1},{1,0},{2,3},{3,2},{4,5},{5,4},{6,7},{7,6},{8,9},{9,8},{10,11... | collective-permute-start | bytes 196616 | tf_op jit(solution)/shard_map/ppermute | solution.py:350
  58.3 7.0 %collective-permute-start.22 = (bf16[64,576]{1,0:T(8,128)(2,1)S(1)}, bf16[64,576]{1,0:T(8,128)(2,1)S(1)}, u32[]{:S(2)}, u32[]{:S(2)}) collective-permute-start(bf16[64,576]{1,0:T(8,128)(2,1)S(1)} %get-tuple-element.122), channel_id=1, source_target_pairs={{0,4},{1,5},{2,6},{3,7},{4,0},{5,1},{6,2},{7,3},{8,12},{9,13},{10,... | collective-permute-start | bytes 221192 | tf_op jit(solution)/shard_map/ppermute | solution.py:350
  59.1 7.2 %collective-permute-start.23 = (bf16[64,576]{1,0:T(8,128)(2,1)S(1)}, bf16[64,576]{1,0:T(8,128)(2,1)S(1)}, u32[]{:S(2)}, u32[]{:S(2)}) collective-permute-start(bf16[64,576]{1,0:T(8,128)(2,1)S(1)} %get-tuple-element.123), channel_id=1, source_target_pairs={{0,6},{1,7},{2,4},{3,5},{4,2},{5,3},{6,0},{7,1},{8,14},{9,15},{10,... | collective-permute-start | bytes 221192 | tf_op jit(solution)/shard_map/ppermute | solution.py:350
  60.9 7.5 %collective-permute-start.25 = (bf16[672,128]{1,0:T(8,128)(2,1)S(1)}, bf16[672,128]{1,0:T(8,128)(2,1)S(1)}, u32[]{:S(2)}, u32[]{:S(2)}) collective-permute-start(bf16[672,128]{1,0:T(8,128)(2,1)S(1)} %get-tuple-element.130), channel_id=1, source_target_pairs={{0,1},{1,0},{2,3},{3,2},{4,5},{5,4},{6,7},{7,6},{8,9},{9,8},{10,11... | collective-permute-start | bytes 516104 | tf_op jit(solution)/shard_map/ppermute | solution.py:350
  61.8 7.8 %collective-permute-start.26 = (bf16[672,128]{1,0:T(8,128)(2,1)S(1)}, bf16[672,128]{1,0:T(8,128)(2,1)S(1)}, u32[]{:S(2)}, u32[]{:S(2)}) collective-permute-start(bf16[672,128]{1,0:T(8,128)(2,1)S(1)} %get-tuple-element.131), channel_id=1, source_target_pairs={{0,2},{1,3},{2,0},{3,1},{4,6},{5,7},{6,4},{7,5},{8,10},{9,11},{10,... | collective-permute-start | bytes 516104 | tf_op jit(solution)/shard_map/ppermute | solution.py:350
  62.5 9.2 %collective-permute-start.27 = (bf16[672,128]{1,0:T(8,128)(2,1)S(1)}, bf16[672,128]{1,0:T(8,128)(2,1)S(1)}, u32[]{:S(2)}, u32[]{:S(2)}) collective-permute-start(bf16[672,128]{1,0:T(8,128)(2,1)S(1)} %get-tuple-element.132), channel_id=1, source_target_pairs={{0,3},{1,2},{2,1},{3,0},{4,7},{5,6},{6,5},{7,4},{8,11},{9,10},{10,... | collective-permute-start | bytes 516104 | tf_op jit(solution)/shard_map/ppermute | solution.py:350
  66.3 6.2 %collective-permute-start.24 = (bf16[64,576]{1,0:T(8,128)(2,1)S(1)}, bf16[64,576]{1,0:T(8,128)(2,1)S(1)}, u32[]{:S(2)}, u32[]{:S(2)}) collective-permute-start(bf16[64,576]{1,0:T(8,128)(2,1)S(1)} %shard_map.172), channel_id=1, source_target_pairs={{0,1},{1,0},{2,3},{3,2},{4,5},{5,4},{6,7},{7,6},{8,9},{9,8},{10,11... | collective-permute-start | bytes 221192 | tf_op jit(solution)/shard_map/ppermute | solution.py:350
